TPU v7x, 32 devices: a whole 2x2x4 slice. The times are simulated.
32 devices in a mesh: segment: 4 (over x, core), seq: 4 (over z), tp: 2 (over y).
Axes of the slice: x: 2, y: 2, z: 4, core: 2. Of those that a mesh axis runs over, the one named last changes fastest.
Arguments:
- pairs: bfloat16 [4, 1024, 2, 2048], P('segment', ('seq', 'tp')), may hold values from -4 to 4
- queries: bfloat16 [4, 1536, 2048], P('segment', None, ('seq', 'tp')), may hold values from -24 to 24
- upstream: bfloat16 [4, 1536, 2048], P('segment', None, ('seq', 'tp')), may hold values from -6 to 6
Outputs:
- context: bfloat16 [4, 1536, 2048], P('segment', None, ('seq', 'tp'))
- grad_query: bfloat16 [4, 1536, 2048], P('segment', None, ('seq', 'tp'))
- grad_pairs: bfloat16 [4, 1024, 2, 2048], P('segment', ('seq', 'tp'))
All inputs are finite; a program needn't handle non-finite values.
Results may differ from a plain program's by a relative error of at most 0.011.
Values may be sent and summed in bfloat16 or wider, within the bound.
No kernel may reach another device: no remote copies, remote signals or barrier semaphores. Data moves between devices by JAX's collectives and lax.ppermute only.
A program may use at most 128 MiB of HBM per device.

v0:
```python
import jax
import jax.numpy as jnp
from jax import lax
from jax.sharding import PartitionSpec as P

HEAD = 128


def passed_along(block, axis, distance):
    devices = range(lax.axis_size(axis))
    route = [((i - distance) % len(devices), i) for i in devices]
    return lax.ppermute(block, axis, route)


def spread_heads(pairs):
    rows = pairs.shape[1]
    width = pairs.shape[3]
    seq_count = lax.axis_size("seq")
    tp_count = lax.axis_size("tp")
    local = width // (seq_count * tp_count)
    shaped = pairs.reshape(1, rows, 2, seq_count * tp_count, local)
    moved = lax.all_to_all(shaped, ("seq", "tp"), split_axis=3, concat_axis=0, tiled=True)
    return moved.reshape(seq_count * tp_count * rows, 2, local)


def collect_rows(grads):
    seq_count = lax.axis_size("seq")
    tp_count = lax.axis_size("tp")
    groups = seq_count * tp_count
    rows = grads.shape[0] // groups
    local = grads.shape[2]
    shaped = grads.reshape(groups, rows, 2, 1, local)
    moved = lax.all_to_all(shaped, ("seq", "tp"), split_axis=0, concat_axis=3, tiled=True)
    return moved.reshape(1, rows, 2, groups * local)


def attend(head_pairs, query_rows, grad_rows):
    enc_len = head_pairs.shape[0]
    local = head_pairs.shape[2]
    num_heads = local // HEAD
    dec_len = query_rows.shape[0]
    block = min(512, dec_len)
    count = dec_len // block
    factor = HEAD ** (-0.5)
    keys_all = head_pairs[:, 0, :].reshape(enc_len, num_heads, HEAD)
    values_all = head_pairs[:, 1, :].reshape(enc_len, num_heads, HEAD)
    query_blocks = query_rows.reshape(count, block, num_heads, HEAD)
    grad_blocks = grad_rows.reshape(count, block, num_heads, HEAD)

    def step(carry, inputs):
        grad_keys, grad_values = carry
        query_block, grad_block = inputs
        scores = (
            jnp.einsum("bhd,shd->hbs", query_block, keys_all, preferred_element_type=jnp.float32)
            * factor
        )
        row_max = jnp.max(scores, axis=2, keepdims=True)
        raised = jnp.exp(scores - row_max)
        weights = raised / jnp.sum(raised, axis=2, keepdims=True)
        weights_low = weights.astype(jnp.bfloat16)
        full_context = jnp.einsum(
            "hbs,shd->bhd", weights_low, values_all, preferred_element_type=jnp.float32
        )
        row_dot = jnp.sum(grad_block.astype(jnp.float32) * full_context, axis=2)
        grad_weights = jnp.einsum(
            "bhd,shd->hbs", grad_block, values_all, preferred_element_type=jnp.float32
        )
        grad_scores = (weights * (grad_weights - row_dot.T[:, :, None]) * factor).astype(
            jnp.bfloat16
        )
        grad_q = jnp.einsum(
            "hbs,shd->bhd", grad_scores, keys_all, preferred_element_type=jnp.float32
        )
        grad_keys = grad_keys + jnp.einsum(
            "hbs,bhd->shd", grad_scores, query_block, preferred_element_type=jnp.float32
        )
        grad_values = grad_values + jnp.einsum(
            "hbs,bhd->shd", weights_low, grad_block, preferred_element_type=jnp.float32
        )
        return (
            (grad_keys, grad_values),
            (full_context.astype(jnp.bfloat16), grad_q.astype(jnp.bfloat16)),
        )

    zeros_start = jnp.zeros((enc_len, num_heads, HEAD), jnp.float32)
    (grad_keys, grad_values), (context, grad_query) = lax.scan(
        step, (zeros_start, zeros_start), (query_blocks, grad_blocks)
    )
    grad_pairs = (
        jnp.stack([grad_keys, grad_values], axis=1).astype(jnp.bfloat16).reshape(enc_len, 2, local)
    )
    return (context.reshape(dec_len, local), grad_query.reshape(dec_len, local), grad_pairs)


def shards(pairs, queries, upstream):
    arrived = passed_along(pairs, "segment", 1)
    head_pairs = spread_heads(arrived)
    context, grad_query, head_grads = attend(head_pairs, queries[0], upstream[0])
    grad_pairs = passed_along(collect_rows(head_grads), "segment", -1)
    return (context[None], grad_query[None], grad_pairs)


def solution(mesh):
    return jax.shard_map(
        shards,
        mesh=mesh,
        in_specs=(
            P("segment", ("seq", "tp"), None, None),
            P("segment", None, ("seq", "tp")),
            P("segment", None, ("seq", "tp")),
        ),
        out_specs=(
            P("segment", None, ("seq", "tp")),
            P("segment", None, ("seq", "tp")),
            P("segment", ("seq", "tp"), None, None),
        ),
        check_vma=False,
    )
```

profile of v0, /device:TPU:0, one launch (start us, length us, event | category | flops | bytes accessed | tf_op | source)
XLA Modules:
  0.0 148.9 jit_solution(3335942665295852914)
XLA Ops:
  0.6 2.5 %copy.43 = bf16[1,128,2,2048]{1,3,2,0:T(8,128)(2,1)S(1)} copy(bf16[1,128,2,2048]{3,2,1,0:T(2,128)(2,1)} %param.5) | data formatting | bytes 2097152 | tf_op args[0]
  3.2 0.5 collective-permute-start
  3.7 14.4 %collective-permute-done = bf16[1,128,2,2048]{1,3,2,0:T(8,128)(2,1)S(1)} collective-permute-done((bf16[1,128,2,2048]{1,3,2,0:T(8,128)(2,1)S(1)}, bf16[1,128,2,2048]{1,3,2,0:T(8,128)(2,1)S(1)}, u32[]{:S(2)}, u32[]{:S(2)}) %collective-permute-start) | collective-permute-done | bytes 1048608 | tf_op jit(solution)/shard_map/ppermute | solution.py:12
  18.1 1.0 copy.44
  19.1 6.6 %all-to-all-start = ((bf16[1,128,2,8,256]{1,4,2,0,3:T(8,128)(2,1)}), bf16[1,128,2,8,256]{1,4,2,0,3:T(8,128)(2,1)}, u32[]{:S(2)}, u32[]{:S(2)}) async-start(bf16[1,128,2,8,256]{1,4,2,0,3:T(8,128)(2,1)} %copy.44), calls=%async_computation | async-start | bytes 2097152 | tf_op jit(solution)/shard_map/all_to_all | solution.py:22
  25.8 2.0 %reshape_squeeze.12 = bf16[3,512,2,128]{3,2,1,0:T(2,128)(2,1)S(1)} reshape(bf16[1,1536,256]{2,1,0:T(8,128)(2,1)} %param.6) | data formatting | bytes 1572864 | tf_op jit(solution)/shard_map/reshape;squeeze | solution.py:47
  27.8 2.7 %reshape_squeeze.14 = bf16[3,512,2,128]{3,2,1,0:T(2,128)(2,1)} reshape(bf16[1,1536,256]{2,1,0:T(8,128)(2,1)} %param.7) | data formatting | bytes 1572864 | tf_op jit(solution)/shard_map/reshape;squeeze | solution.py:48
  30.6 20.6 %all-to-all-done = bf16[1,128,2,8,256]{1,4,2,0,3:T(8,128)(2,1)} async-done(((bf16[1,128,2,8,256]{1,4,2,0,3:T(8,128)(2,1)}), bf16[1,128,2,8,256]{1,4,2,0,3:T(8,128)(2,1)}, u32[]{:S(2)}, u32[]{:S(2)}) %all-to-all-start) | async-done | bytes 1048608 | tf_op jit(solution)/shard_map/all_to_all | solution.py:22
  51.2 2.9 %copy.45 = bf16[8,1,128,2,1,256]{2,0,5,3,4,1:T(8,128)(2,1)} copy(bf16[8,1,128,2,1,256]{2,5,3,0,4,1:T(8,128)(2,1)} %bitcast.2) | data formatting | bytes 2097152 | tf_op jit(solution)/shard_map/all_to_all | solution.py:22
  54.0 2.3 %reshape.54 = bf16[1024,2,256]{0,2,1:T(8,128)(2,1)} reshape(bf16[8,1,128,2,1,256]{2,0,5,3,4,1:T(8,128)(2,1)} %copy.45) | data formatting | bytes 2097152 | tf_op jit(solution)/shard_map/reshape | solution.py:23
  56.3 2.1 %fusion.14 = (bf16[1024,1,256]{0,2,1:T(8,128)(2,1)}, bf16[1024,1,256]{0,2,1:T(8,128)(2,1)S(1)}) fusion(bf16[1024,2,256]{0,2,1:T(8,128)(2,1)} %reshape.54), kind=kLoop, calls=%fused_computation.28 | loop fusion | bytes 2097152 | tf_op jit(solution)/shard_map/slice | solution.py:46
  58.4 1.0 copy.47
  59.4 43.2 %while.17 = (s32[]{:T(128)}, f32[1024,2,128]{0,2,1:T(8,128)S(1)}, f32[1024,2,128]{0,2,1:T(8,128)S(1)}, bf16[3,512,2,128]{3,2,1,0:T(2,128)(2,1)}, bf16[3,512,2,12...) while((s32[]{:T(128)}, f32[1024,2,128]{0,2,1:T(8,128)S(1)}, ...), condition=%wide.region_4.5_spmd.clone, body=%wide.region_0.4_spmd.clone.sunk | while | flops 1622802432 | bytes 56381660 | solution.py:86
  59.4 1.1 constant_dynamic-slice_fusion.4
  60.5 0.2 constant_dynamic-slice_fusion.5
  60.7 4.4 %fusion.45 = (f32[2,512]{1,0:T(2,128)S(1)}, f32[2,512,1024]{2,1,0:T(8,128)}) fusion(bf16[1024,2,128]{2,0,1:T(8,128)(2,1)} %get-tuple-element.238, bf16[1,512,2,128]{3,2,1,0:T(2,128)(2,1)S(1)} %constant_dynamic-slice_fusion.5), kind=kOutput, calls=%fused_computation.27.clone.1 | convolution fusion | flops 271582208 | bytes 4984832 | tf_op jit(solution)/shard_map/while/body/eval_jaxpr/sub | solution.py:58
  65.1 2.7 %fusion.46 = bf16[2,512,1024]{2,1,0:T(8,128)(2,1)S(1)} fusion(f32[2,512,1024]{2,1,0:T(8,128)} %get-tuple-element.204, f32[2,512]{1,0:T(2,128)S(1)} %get-tuple-element.205), kind=kLoop, calls=%fused_computation.7.clone.1 | loop fusion | flops 2097152 | bytes 6295552 | tf_op jit(solution)/shard_map/while/body/eval_jaxpr/convert_element_type | solution.py:60
  67.9 0.0 copy-done.3
  67.9 0.8 convert_bitcast_fusion.2
  68.7 0.6 fusion.48
  69.4 0.7 copy-done
  70.1 0.9 multiply_convert_fusion.2
  71.0 0.1 copy-done.2
  71.1 0.7 fusion.49
  71.8 0.6 fusion.47
  72.5 1.3 copy_dynamic-update-slice_fusion.3
  73.8 1.1 constant_dynamic-slice_fusion.4
  74.9 0.2 constant_dynamic-slice_fusion.5
  75.1 4.4 %fusion.45 = (f32[2,512]{1,0:T(2,128)S(1)}, f32[2,512,1024]{2,1,0:T(8,128)}) fusion(bf16[1024,2,128]{2,0,1:T(8,128)(2,1)} %get-tuple-element.238, bf16[1,512,2,128]{3,2,1,0:T(2,128)(2,1)S(1)} %constant_dynamic-slice_fusion.5), kind=kOutput, calls=%fused_computation.27.clone.1 | convolution fusion | flops 271582208 | bytes 4984832 | tf_op jit(solution)/shard_map/while/body/eval_jaxpr/sub | solution.py:58
  79.5 2.7 %fusion.46 = bf16[2,512,1024]{2,1,0:T(8,128)(2,1)S(1)} fusion(f32[2,512,1024]{2,1,0:T(8,128)} %get-tuple-element.204, f32[2,512]{1,0:T(2,128)S(1)} %get-tuple-element.205), kind=kLoop, calls=%fused_computation.7.clone.1 | loop fusion | flops 2097152 | bytes 6295552 | tf_op jit(solution)/shard_map/while/body/eval_jaxpr/convert_element_type | solution.py:60
  82.2 0.8 convert_bitcast_fusion.2
  83.1 0.6 fusion.48
  83.7 0.7 copy-done
  84.4 0.9 multiply_convert_fusion.2
  85.3 0.1 copy-done.2
  85.5 0.7 fusion.49
  86.2 0.6 fusion.47
  86.8 1.4 copy_dynamic-update-slice_fusion.3
  88.2 1.1 constant_dynamic-slice_fusion.4
  89.3 0.2 constant_dynamic-slice_fusion.5
  89.5 4.4 %fusion.45 = (f32[2,512]{1,0:T(2,128)S(1)}, f32[2,512,1024]{2,1,0:T(8,128)}) fusion(bf16[1024,2,128]{2,0,1:T(8,128)(2,1)} %get-tuple-element.238, bf16[1,512,2,128]{3,2,1,0:T(2,128)(2,1)S(1)} %constant_dynamic-slice_fusion.5), kind=kOutput, calls=%fused_computation.27.clone.1 | convolution fusion | flops 271582208 | bytes 4984832 | tf_op jit(solution)/shard_map/while/body/eval_jaxpr/sub | solution.py:58
  93.9 2.7 %fusion.46 = bf16[2,512,1024]{2,1,0:T(8,128)(2,1)S(1)} fusion(f32[2,512,1024]{2,1,0:T(8,128)} %get-tuple-element.204, f32[2,512]{1,0:T(2,128)S(1)} %get-tuple-element.205), kind=kLoop, calls=%fused_computation.7.clone.1 | loop fusion | flops 2097152 | bytes 6295552 | tf_op jit(solution)/shard_map/while/body/eval_jaxpr/convert_element_type | solution.py:60
  96.7 0.8 convert_bitcast_fusion.2
  97.5 0.6 fusion.48
  98.1 0.7 copy-done
  98.8 0.9 multiply_convert_fusion.2
  99.8 0.1 copy-done.2
  99.9 0.7 fusion.49
  100.6 0.6 fusion.47
  101.2 1.4 copy_dynamic-update-slice_fusion.3
  102.6 0.1 convert.8
  102.7 0.1 copy.64
  102.8 0.1 convert.9
  102.8 0.1 copy.65
  102.9 0.0 copy-start.1
  103.0 0.1 pad_maximum_fusion
  103.1 1.5 copy.51
  104.6 29.1 %all_to_all.30 = bf16[8,128,2,1,256]{4,2,1,3,0:T(2,128)(2,1)S(1)} all-to-all(bf16[8,128,2,1,256]{4,2,1,3,0:T(2,128)(2,1)S(1)} %copy.51), channel_id=1, replica_groups=mesh['segment'=4,'seq'=4,'tp'=2] {'seq','tp'}, dimensions={0} | all-to-all | bytes 2097152 | tf_op jit(solution)/shard_map/all_to_all | solution.py:33
  133.6 0.9 copy.52
  134.5 0.1 collective-permute-start.1
  134.6 1.4 broadcast_in_dim_reshape.7
  136.0 3.1 %broadcast_in_dim_reshape.6 = bf16[1,1536,256]{2,1,0:T(8,128)(2,1)} reshape(bf16[3,512,2,128]{3,2,1,0:T(2,128)(2,1)} %get-tuple-element.53) | data formatting | bytes 1572864 | tf_op jit(solution)/shard_map/broadcast_in_dim;reshape | solution.py:100
  139.1 7.8 %collective-permute-done.1 = bf16[1,128,2,2048]{1,3,2,0:T(8,128)(2,1)S(1)} collective-permute-done((bf16[1,128,2,2048]{1,3,2,0:T(8,128)(2,1)S(1)}, bf16[1,128,2,2048]{1,3,2,0:T(8,128)(2,1)S(1)}, u32[]{:S(2)}, u32[]{:S(2)}) %collective-permute-start.1) | collective-permute-done | bytes 1048608 | tf_op jit(solution)/shard_map/ppermute | solution.py:12
  146.9 2.0 %copy.53 = bf16[1,128,2,2048]{3,2,1,0:T(2,128)(2,1)} copy(bf16[1,128,2,2048]{1,3,2,0:T(8,128)(2,1)S(1)} %collective-permute-done.1) | data formatting | bytes 2097152
  (16 shorter events, 0.0 us)
Async XLA Ops:
  3.2 14.9 %collective-permute-start = (bf16[1,128,2,2048]{1,3,2,0:T(8,128)(2,1)S(1)}, bf16[1,128,2,2048]{1,3,2,0:T(8,128)(2,1)S(1)}, u32[]{:S(2)}, u32[]{:S(2)}) collective-permute-start(bf16[1,128,2,2048]{1,3,2,0:T(8,128)(2,1)S(1)} %copy.43), channel_id=1, source_target_pairs={{24,0},{0,8},{8,16},{16,24},{25,1},{1,9},{9,17},{17,25},{26,2},{2,... | collective-permute-start | bytes 3145736 | tf_op jit(solution)/shard_map/ppermute | solution.py:12
  19.1 32.0 %all-to-all-start = ((bf16[1,128,2,8,256]{1,4,2,0,3:T(8,128)(2,1)}), bf16[1,128,2,8,256]{1,4,2,0,3:T(8,128)(2,1)}, u32[]{:S(2)}, u32[]{:S(2)}) async-start(bf16[1,128,2,8,256]{1,4,2,0,3:T(8,128)(2,1)} %copy.44), calls=%async_computation | async-start | bytes 2097152 | tf_op jit(solution)/shard_map/all_to_all | solution.py:22
  65.1 2.7 %copy-start.3 = (bf16[1024,2,128]{0,2,1:T(8,128)(2,1)S(1)}, bf16[1024,2,128]{0,2,1:T(8,128)(2,1)}, u32[]{:S(2)}) copy-start(bf16[1024,2,128]{0,2,1:T(8,128)(2,1)} %get-tuple-element.240) | copy-start | bytes 1572868 | tf_op jit(solution)/shard_map/while
  67.9 2.2 %copy-start = (f32[2,512,1024]{2,1,0:T(8,128)S(1)}, f32[2,512,1024]{2,1,0:T(8,128)}, u32[]{:S(2)}) copy-start(f32[2,512,1024]{2,1,0:T(8,128)} %get-tuple-element.204) | copy-start | bytes 12582916 | tf_op jit(solution)/shard_map/while
  70.1 1.0 copy-start.2
  79.5 2.7 %copy-start.3 = (bf16[1024,2,128]{0,2,1:T(8,128)(2,1)S(1)}, bf16[1024,2,128]{0,2,1:T(8,128)(2,1)}, u32[]{:S(2)}) copy-start(bf16[1024,2,128]{0,2,1:T(8,128)(2,1)} %get-tuple-element.240) | copy-start | bytes 1572868 | tf_op jit(solution)/shard_map/while
  82.2 2.2 %copy-start = (f32[2,512,1024]{2,1,0:T(8,128)S(1)}, f32[2,512,1024]{2,1,0:T(8,128)}, u32[]{:S(2)}) copy-start(f32[2,512,1024]{2,1,0:T(8,128)} %get-tuple-element.204) | copy-start | bytes 12582916 | tf_op jit(solution)/shard_map/while
  84.4 1.0 copy-start.2
  93.9 2.7 %copy-start.3 = (bf16[1024,2,128]{0,2,1:T(8,128)(2,1)S(1)}, bf16[1024,2,128]{0,2,1:T(8,128)(2,1)}, u32[]{:S(2)}) copy-start(bf16[1024,2,128]{0,2,1:T(8,128)(2,1)} %get-tuple-element.240) | copy-start | bytes 1572868 | tf_op jit(solution)/shard_map/while
  96.6 2.2 %copy-start = (f32[2,512,1024]{2,1,0:T(8,128)S(1)}, f32[2,512,1024]{2,1,0:T(8,128)}, u32[]{:S(2)}) copy-start(f32[2,512,1024]{2,1,0:T(8,128)} %get-tuple-element.204) | copy-start | bytes 12582916 | tf_op jit(solution)/shard_map/while
  98.8 1.0 copy-start.2
  102.9 31.6 %copy-start.1 = (bf16[3,512,2,128]{3,2,1,0:T(2,128)(2,1)S(1)}, bf16[3,512,2,128]{3,2,1,0:T(2,128)(2,1)}, u32[]{:S(2)}) copy-start(bf16[3,512,2,128]{3,2,1,0:T(2,128)(2,1)} %get-tuple-element.54) | copy-start | bytes 2359300
  134.5 12.4 %collective-permute-start.1 = (bf16[1,128,2,2048]{1,3,2,0:T(8,128)(2,1)S(1)}, bf16[1,128,2,2048]{1,3,2,0:T(8,128)(2,1)S(1)}, u32[]{:S(2)}, u32[]{:S(2)}) collective-permute-start(bf16[1,128,2,2048]{1,3,2,0:T(8,128)(2,1)S(1)} %bitcast.115), channel_id=1, source_target_pairs={{8,0},{16,8},{24,16},{0,24},{9,1},{17,9},{25,17},{1,25},{10,2},{18... | collective-permute-start | bytes 3145736 | tf_op jit(solution)/shard_map/ppermute | solution.py:12
where the time goes:
time: 150 us; the launch traced here: 149 us
  waiting for transfers between devices  42.8 us (29%)
  local copies, waits for them, and re-layouts  36.1 us (24%)
  blocking collectives  29.1 us (19%)
  matrix products  24.3 us (16%)
  other arithmetic  8.43 us (6%)
  starting transfers between devices  7.21 us (5%)
    all_to_all x1, blocking collectives, collect_rows(): lax.all_to_all(shaped, ('seq', 'tp'), split_axis=0, concat_axis=3, tiled=...  29.1 us
    ppermute x2, waiting for transfers between devices, passed_along(): return lax.ppermute(block, axis, route)  22.2 us
    all_to_all x1, waiting for transfers between devices, spread_heads(): lax.all_to_all(shaped, ('seq', 'tp'), split_axis=3, concat_axis=0, tiled=...  20.6 us
    sub x3, matrix products, step(): raised = jnp.exp(scores - row_max)  13.1 us
    convert_element_type x3, other arithmetic, step(): weights_low = weights.astype(jnp.bfloat16)  8.19 us
    all_to_all x1, starting transfers between devices, spread_heads(): lax.all_to_all(shaped, ('seq', 'tp'), split_axis=3, concat_axis=0, tiled=...  6.64 us
    unnamed x7, local copies, waits for them, and re-layouts  5.75 us
    another operation x2, local copies, waits for them, and re-layouts, shards(): return (context[None], grad_query[None], grad_pairs)  4.51 us
  transfers between devices with their start and end apart: 3, of which 3 were waited for; matrix products, arithmetic and copies ran while one was open for 6% of the time, Pallas kernels for 0%

commit v1 on v0

--- a/solution.py
+++ b/solution.py
@@ -4,34 +4,38 @@
 from jax.sharding import PartitionSpec as P
 
 HEAD = 128
+AXES = ("segment", "seq", "tp")
 
 
-def passed_along(block, axis, distance):
-    devices = range(lax.axis_size(axis))
-    route = [((i - distance) % len(devices), i) for i in devices]
-    return lax.ppermute(block, axis, route)
+def offsets():
+    seq_count = lax.axis_size("seq")
+    tp_count = lax.axis_size("tp")
+    pairs = [(dz, dy) for dz in range(seq_count) for dy in range(tp_count)]
+    middle = seq_count / 2
+    return sorted(pairs, key=lambda o: (abs(o[0] - middle), -o[1]))
 
 
-def spread_heads(pairs):
-    rows = pairs.shape[1]
-    width = pairs.shape[3]
+def group_at(offset):
     seq_count = lax.axis_size("seq")
     tp_count = lax.axis_size("tp")
-    local = width // (seq_count * tp_count)
-    shaped = pairs.reshape(1, rows, 2, seq_count * tp_count, local)
-    moved = lax.all_to_all(shaped, ("seq", "tp"), split_axis=3, concat_axis=0, tiled=True)
-    return moved.reshape(seq_count * tp_count * rows, 2, local)
+    z = lax.rem(lax.axis_index("seq") + offset[0], seq_count)
+    y = lax.rem(lax.axis_index("tp") + offset[1], tp_count)
+    return z * tp_count + y
 
 
-def collect_rows(grads):
-    seq_count = lax.axis_size("seq")
-    tp_count = lax.axis_size("tp")
-    groups = seq_count * tp_count
-    rows = grads.shape[0] // groups
-    local = grads.shape[2]
-    shaped = grads.reshape(groups, rows, 2, 1, local)
-    moved = lax.all_to_all(shaped, ("seq", "tp"), split_axis=0, concat_axis=3, tiled=True)
-    return moved.reshape(1, rows, 2, groups * local)
+def route(offset, back):
+    segments, seq_count, tp_count = (lax.axis_size(a) for a in AXES)
+    hops = []
+    for s in range(segments):
+        for z in range(seq_count):
+            for y in range(tp_count):
+                source = (s * seq_count + z) * tp_count + y
+                s_to = (s + 1) % segments
+                z_to = (z + offset[0]) % seq_count
+                y_to = (y + offset[1]) % tp_count
+                target = (s_to * seq_count + z_to) * tp_count + y_to
+                hops.append((target, source) if back else (source, target))
+    return hops
 
 
 def attend(head_pairs, query_rows, grad_rows):
@@ -93,11 +97,24 @@
 
 
 def shards(pairs, queries, upstream):
-    arrived = passed_along(pairs, "segment", 1)
-    head_pairs = spread_heads(arrived)
+    groups = lax.axis_size("seq") * lax.axis_size("tp")
+    rows, _, width = pairs.shape[1:]
+    local = width // groups
+    order = offsets()
+    by_group = pairs.reshape(rows, 2, groups, local)
+    arrived = []
+    for offset in order:
+        block = lax.dynamic_index_in_dim(by_group, group_at(offset), axis=2, keepdims=False)
+        arrived.append(lax.ppermute(block, AXES, route(offset, False)))
+    head_pairs = jnp.concatenate(arrived, axis=0)
     context, grad_query, head_grads = attend(head_pairs, queries[0], upstream[0])
-    grad_pairs = passed_along(collect_rows(head_grads), "segment", -1)
-    return (context[None], grad_query[None], grad_pairs)
+    grad_pairs = jnp.zeros((rows, 2, groups, local), pairs.dtype)
+    for i, offset in enumerate(order):
+        block = lax.ppermute(head_grads[i * rows : (i + 1) * rows], AXES, route(offset, True))
+        grad_pairs = lax.dynamic_update_index_in_dim(
+            grad_pairs, block, group_at(offset), axis=2
+        )
+    return (context[None], grad_query[None], grad_pairs.reshape(1, rows, 2, width))
 
 
 def solution(mesh):

time: 150 us -> 157 us (1.047); the launches traced: 149 us -> 154 us
  waiting for transfers between devices: 42.8 us -> 11.9 us
  local copies, waits for them, and re-layouts: 36.1 us -> 65.6 us
  blocking collectives: 29.1 us -> 0 us
  starting transfers between devices: 7.21 us -> 27.2 us
  matrix products: 24.3 us -> 37.1 us
  other arithmetic: 8.43 us -> 10.4 us
    all_to_all x1 -> x0, blocking collectives: 29.1 us -> none  [collect_rows(): lax.all_to_all(shaped, ('seq', 'tp'), split_axis=0, concat_axis=3, tiled=...]
    ppermute x2 -> x16, starting transfers between devices: 0.56 us -> 27.2 us  [the longest x8 15 us: shards(): arrived.append(lax.ppermute(block, AXES, route(offset, False)))]
    dynamic_update_slice x0 -> x8, local copies, waits for them, and re-layouts: none -> 26.5 us  [shards(): lax.dynamic_update_index_in_dim(grad_pairs, block, group_at(offset), axis=2)]
    all_to_all x1 -> x0, waiting for transfers between devices: 20.6 us -> none  [spread_heads(): lax.all_to_all(shaped, ('seq', 'tp'), split_axis=3, concat_axis=0, tiled=...]
    ppermute x2 -> x16, waiting for transfers between devices: 22.2 us -> 11.9 us  [the longest x8 6.12 us: shards(): lax.ppermute(head_grads[i * rows:(i + 1) * rows], AXES, route(offset, True))]
    all_to_all x1 -> x0, starting transfers between devices: 6.64 us -> none  [spread_heads(): lax.all_to_all(shaped, ('seq', 'tp'), split_axis=3, concat_axis=0, tiled=...]
    dot_general x3, matrix products: 1.93 us -> 6.91 us  [step(): jnp.einsum('hbs,bhd->shd', weights_low, grad_block, preferred_element_typ...]
    dot_general x3, matrix products: 1.92 us -> 6.78 us  [step(): jnp.einsum('hbs,bhd->shd', grad_scores, query_block, preferred_element_ty...]
  transfers between devices with their start and end apart: 3 -> 16, of which waited for: 3 -> 7; matrix products, arithmetic and copies ran while one was open for 6% -> 11% of each run, Pallas kernels for 0% -> 0%
where the time goes in v1:
time: 157 us; the launch traced here: 154 us
  local copies, waits for them, and re-layouts  65.6 us (42%)
  matrix products  37.1 us (24%)
  starting transfers between devices  27.2 us (17%)
  waiting for transfers between devices  11.9 us (8%)
  other arithmetic  10.4 us (7%)
    dynamic_update_slice x8, local copies, waits for them, and re-layouts, shards(): lax.dynamic_update_index_in_dim(grad_pairs, block, group_at(offset), axis=2)  26.5 us
    ppermute x8, starting transfers between devices, shards(): arrived.append(lax.ppermute(block, AXES, route(offset, False)))  15 us
    sub x3, matrix products, step(): raised = jnp.exp(scores - row_max)  13.1 us
    ppermute x8, starting transfers between devices, shards(): lax.ppermute(head_grads[i * rows:(i + 1) * rows], AXES, route(offset, True))  12.2 us
    convert_element_type x3, other arithmetic, step(): weights_low = weights.astype(jnp.bfloat16)  8.6 us
    dot_general x3, matrix products, step(): jnp.einsum('hbs,bhd->shd', weights_low, grad_block, preferred_element_typ...  6.91 us
    dynamic_slice x6, local copies, waits for them, and re-layouts, attend(): lax.scan(step, (zeros_start, zeros_start), (query_blocks, grad_blocks))  6.81 us
    dot_general x3, matrix products, step(): jnp.einsum('hbs,bhd->shd', grad_scores, query_block, preferred_element_ty...  6.78 us
  transfers between devices with their start and end apart: 16, of which 7 were waited for; matrix products, arithmetic and copies ran while one was open for 11% of the time, Pallas kernels for 0%

profile of v1, /device:TPU:0, one launch (start us, length us, event | category | flops | bytes accessed | tf_op | source)
XLA Modules:
  0.0 153.6 jit_solution(10324391789619858285)
XLA Ops:
  0.7 1.7 %reshape.24 = bf16[128,2,8,256]{3,2,1,0:T(8,128)(2,1)S(1)} reshape(bf16[1,128,2,2048]{3,2,1,0:T(2,128)(2,1)} %param.5) | data formatting | bytes 2097152 | tf_op jit(solution)/shard_map/reshape | solution.py:104
  2.5 2.4 %constant_dynamic-slice_fusion.2 = (bf16[128,2,1,256]{3,2,1,0:T(2,128)(2,1)S(1)}, bf16[128,2,1,256]{3,2,1,0:T(2,128)(2,1)S(1)}, bf16[128,2,1,256]{3,2,1,0:T(2,12...) fusion(bf16[128,2,8,256]{3,2,1,0:T(8,128)(2,1)S(1)} %reshape.24, ...), kind=kLoop, calls=%fused_computation.58 | loop fusion | bytes 2097184 | tf_op jit(solution)/shard_map/jit(dynamic_index_in_dim)/dynamic_slice | solution.py:107
  5.1 4.5 %collective-permute-start = (bf16[128,2,256]{0,2,1:T(8,128)(2,1)S(1)}, bf16[128,2,256]{0,2,1:T(8,128)(2,1)}, u32[]{:S(2)}, u32[]{:S(2)}) collective-permute-start(bf16[128,2,256]{0,2,1:T(8,128)(2,1)S(1)} %bitcast.139), channel_id=1, source_target_pairs={{0,13},{1,12},{2,15},{3,14},{4,9},{5,8},{6,11},{7,10},{8,21},{9,20... | collective-permute-start | bytes 393224 | tf_op jit(solution)/shard_map/ppermute | solution.py:108
  9.8 1.6 %collective-permute-start.1 = (bf16[128,2,256]{0,2,1:T(8,128)(2,1)S(1)}, bf16[128,2,256]{0,2,1:T(8,128)(2,1)}, u32[]{:S(2)}, u32[]{:S(2)}) collective-permute-start(bf16[128,2,256]{0,2,1:T(8,128)(2,1)S(1)} %bitcast.136), channel_id=1, source_target_pairs={{0,12},{1,13},{2,14},{3,15},{4,8},{5,9},{6,10},{7,11},{8,20},{9,21... | collective-permute-start | bytes 393224 | tf_op jit(solution)/shard_map/ppermute | solution.py:108
  11.6 1.3 collective-permute-start.2
  13.0 3.2 %collective-permute-start.3 = (bf16[128,2,256]{0,2,1:T(8,128)(2,1)S(1)}, bf16[128,2,256]{0,2,1:T(8,128)(2,1)}, u32[]{:S(2)}, u32[]{:S(2)}) collective-permute-start(bf16[128,2,256]{0,2,1:T(8,128)(2,1)S(1)} %bitcast.129), channel_id=1, source_target_pairs={{0,15},{1,14},{2,9},{3,8},{4,11},{5,10},{6,13},{7,12},{8,23},{9,22... | collective-permute-start | bytes 393224 | tf_op jit(solution)/shard_map/ppermute | solution.py:108
  17.1 2.7 %reshape_squeeze.12 = bf16[3,512,2,128]{3,2,1,0:T(2,128)(2,1)} reshape(bf16[1,1536,256]{2,1,0:T(8,128)(2,1)} %param.6) | data formatting | bytes 1572864 | tf_op jit(solution)/shard_map/reshape;squeeze | solution.py:51
  19.8 1.1 reshape_squeeze.14
  20.9 1.8 %collective-permute-done = bf16[128,2,256]{0,2,1:T(8,128)(2,1)} collective-permute-done((bf16[128,2,256]{0,2,1:T(8,128)(2,1)S(1)}, bf16[128,2,256]{0,2,1:T(8,128)(2,1)}, u32[]{:S(2)}, u32[]{:S(2)}) %collective-permute-start) | collective-permute-done | bytes 131104 | tf_op jit(solution)/shard_map/ppermute | solution.py:108
  22.7 2.6 %collective-permute-start.5 = (bf16[128,2,256]{0,2,1:T(8,128)(2,1)S(1)}, bf16[128,2,256]{0,2,1:T(8,128)(2,1)S(1)}, u32[]{:S(2)}, u32[]{:S(2)}) collective-permute-start(bf16[128,2,256]{0,2,1:T(8,128)(2,1)S(1)} %bitcast.131), channel_id=1, source_target_pairs={{0,14},{1,15},{2,8},{3,9},{4,10},{5,11},{6,12},{7,13},{8,22},{9,23... | collective-permute-start | bytes 393224 | tf_op jit(solution)/shard_map/ppermute | solution.py:108
  25.3 0.9 constant_dynamic-update-slice_fusion.7
  26.2 3.1 %collective-permute-done.1 = bf16[128,2,256]{0,2,1:T(8,128)(2,1)} collective-permute-done((bf16[128,2,256]{0,2,1:T(8,128)(2,1)S(1)}, bf16[128,2,256]{0,2,1:T(8,128)(2,1)}, u32[]{:S(2)}, u32[]{:S(2)}) %collective-permute-start.1) | collective-permute-done | bytes 131104 | tf_op jit(solution)/shard_map/ppermute | solution.py:108
  29.4 0.9 constant_dynamic-update-slice_fusion.6
  30.3 1.7 %collective-permute-start.7 = (bf16[128,2,256]{0,2,1:T(8,128)(2,1)S(1)}, bf16[128,2,256]{0,2,1:T(8,128)(2,1)S(1)}, u32[]{:S(2)}, u32[]{:S(2)}) collective-permute-start(bf16[128,2,256]{0,2,1:T(8,128)(2,1)S(1)} %bitcast.125), channel_id=1, source_target_pairs={{0,8},{1,9},{2,10},{3,11},{4,12},{5,13},{6,14},{7,15},{8,16},{9,17... | collective-permute-start | bytes 393224 | tf_op jit(solution)/shard_map/ppermute | solution.py:108
  32.0 0.9 constant_dynamic-update-slice_fusion.5
  33.0 0.9 constant_dynamic-update-slice_fusion.4
  35.0 0.9 fusion.21
  35.9 1.0 copy.41
  36.9 60.8 %while.17 = (s32[]{:T(128)}, f32[1024,2,128]{0,2,1:T(8,128)S(1)}, f32[1024,2,128]{0,2,1:T(8,128)}, bf16[3,512,2,128]{3,2,1,0:T(2,128)(2,1)}, bf16[3,512,2,128]{3...) while((s32[]{:T(128)}, f32[1024,2,128]{0,2,1:T(8,128)S(1)}, ...), condition=%wide.region_4.5_spmd.clone, body=%wide.region_0.4_spmd.clone.sunk | while | flops 1622802432 | bytes 64770824 | solution.py:90
  36.9 1.1 constant_dynamic-slice_fusion.13
  38.0 4.4 %fusion.52 = (f32[2,512]{1,0:T(2,128)S(1)}, f32[2,512,1024]{2,1,0:T(8,128)}) fusion(bf16[1024,2,128]{2,0,1:T(8,128)(2,1)} %get-tuple-element.235, bf16[1,512,2,128]{3,2,1,0:T(2,128)(2,1)S(1)} %constant_dynamic-slice_fusion.13), kind=kOutput, calls=%fused_computation.66.clone.1 | convolution fusion | flops 271582208 | bytes 4984832 | tf_op jit(solution)/shard_map/while/body/eval_jaxpr/sub | solution.py:62
  42.4 2.9 %fusion.53 = bf16[2,512,1024]{2,1,0:T(8,128)(2,1)S(1)} fusion(f32[2,512,1024]{2,1,0:T(8,128)} %get-tuple-element.201, f32[2,512]{1,0:T(2,128)S(1)} %get-tuple-element.202), kind=kLoop, calls=%fused_computation.7.clone.1 | loop fusion | flops 2097152 | bytes 6295552 | tf_op jit(solution)/shard_map/while/body/eval_jaxpr/convert_element_type | solution.py:64
  45.3 1.1 constant_dynamic-slice_fusion.12
  47.3 0.9 multiply_convert_fusion.2
  48.2 1.3 copy-done.1
  49.5 1.7 %fusion.56 = bf16[1,512,2,128]{3,1,2,0:T(8,128)(2,1)S(1)} fusion(bf16[2,512,1024]{2,1,0:T(8,128)(2,1)S(1)} %multiply_convert_fusion.2, bf16[1024,2,128]{2,0,1:T(8,128)(2,1)} %get-tuple-element.235), kind=kOutput, calls=%fused_computation.14.clone.1 | convolution fusion | flops 268566528 | bytes 2883584 | tf_op jit(solution)/shard_map/while/body/eval_jaxpr/hbs,shd->bhd/dot_general | solution.py:75
  51.2 1.3 copy_dynamic-update-slice_fusion.3
  52.6 2.3 %fusion.54 = f32[1024,2,128]{0,2,1:T(8,128)S(1)} fusion(bf16[2,512,1024]{2,1,0:T(8,128)(2,1)} %copy-done.1, f32[1024,2,128]{0,2,1:T(8,128)S(1)} %get-tuple-element.219, pred[]{:T(512)S(6)} %compare.9, bf16[1,512,2,128]{3,2,1,0:T(2,128)(2,1)S(1)} %constant_dynamic-slice_fusion.13), kind=kOutput, calls=%fused_computation.10.clone.1 | convolution fusion | flops 268959744 | bytes 4456449 | tf_op jit(solution)/shard_map/while/body/eval_jaxpr/hbs,bhd->shd/dot_general | solution.py:78
  54.9 1.5 fusion.55
  56.3 1.1 constant_dynamic-slice_fusion.13
  57.5 4.4 %fusion.52 = (f32[2,512]{1,0:T(2,128)S(1)}, f32[2,512,1024]{2,1,0:T(8,128)}) fusion(bf16[1024,2,128]{2,0,1:T(8,128)(2,1)} %get-tuple-element.235, bf16[1,512,2,128]{3,2,1,0:T(2,128)(2,1)S(1)} %constant_dynamic-slice_fusion.13), kind=kOutput, calls=%fused_computation.66.clone.1 | convolution fusion | flops 271582208 | bytes 4984832 | tf_op jit(solution)/shard_map/while/body/eval_jaxpr/sub | solution.py:62
  61.9 2.9 %fusion.53 = bf16[2,512,1024]{2,1,0:T(8,128)(2,1)S(1)} fusion(f32[2,512,1024]{2,1,0:T(8,128)} %get-tuple-element.201, f32[2,512]{1,0:T(2,128)S(1)} %get-tuple-element.202), kind=kLoop, calls=%fused_computation.7.clone.1 | loop fusion | flops 2097152 | bytes 6295552 | tf_op jit(solution)/shard_map/while/body/eval_jaxpr/convert_element_type | solution.py:64
  64.7 1.1 constant_dynamic-slice_fusion.12
  67.6 1.3 copy-done.1
  68.9 1.7 %fusion.56 = bf16[1,512,2,128]{3,1,2,0:T(8,128)(2,1)S(1)} fusion(bf16[2,512,1024]{2,1,0:T(8,128)(2,1)S(1)} %multiply_convert_fusion.2, bf16[1024,2,128]{2,0,1:T(8,128)(2,1)} %get-tuple-element.235), kind=kOutput, calls=%fused_computation.14.clone.1 | convolution fusion | flops 268566528 | bytes 2883584 | tf_op jit(solution)/shard_map/while/body/eval_jaxpr/hbs,shd->bhd/dot_general | solution.py:75
  70.7 1.3 copy_dynamic-update-slice_fusion.3
  72.0 2.3 %fusion.54 = f32[1024,2,128]{0,2,1:T(8,128)S(1)} fusion(bf16[2,512,1024]{2,1,0:T(8,128)(2,1)} %copy-done.1, f32[1024,2,128]{0,2,1:T(8,128)S(1)} %get-tuple-element.219, pred[]{:T(512)S(6)} %compare.9, bf16[1,512,2,128]{3,2,1,0:T(2,128)(2,1)S(1)} %constant_dynamic-slice_fusion.13), kind=kOutput, calls=%fused_computation.10.clone.1 | convolution fusion | flops 268959744 | bytes 4456449 | tf_op jit(solution)/shard_map/while/body/eval_jaxpr/hbs,bhd->shd/dot_general | solution.py:78
  74.3 2.7 %fusion.55 = f32[1024,2,128]{0,2,1:T(8,128)} fusion(bf16[2,512,1024]{2,1,0:T(8,128)(2,1)S(1)} %fusion.53, f32[1024,2,128]{0,2,1:T(8,128)} %get-tuple-element.220, pred[]{:T(512)S(6)} %compare.9, bf16[1,512,2,128]{3,2,1,0:T(2,128)(2,1)S(1)} %copy-done.3), kind=kOutput, calls=%fused_computation.11.clone.1 | convolution fusion | flops 268959744 | bytes 4456449 | tf_op jit(solution)/shard_map/while/body/eval_jaxpr/hbs,bhd->shd/dot_general | solution.py:81
  77.0 1.1 constant_dynamic-slice_fusion.13
  78.2 4.4 %fusion.52 = (f32[2,512]{1,0:T(2,128)S(1)}, f32[2,512,1024]{2,1,0:T(8,128)}) fusion(bf16[1024,2,128]{2,0,1:T(8,128)(2,1)} %get-tuple-element.235, bf16[1,512,2,128]{3,2,1,0:T(2,128)(2,1)S(1)} %constant_dynamic-slice_fusion.13), kind=kOutput, calls=%fused_computation.66.clone.1 | convolution fusion | flops 271582208 | bytes 4984832 | tf_op jit(solution)/shard_map/while/body/eval_jaxpr/sub | solution.py:62
  82.5 2.9 %fusion.53 = bf16[2,512,1024]{2,1,0:T(8,128)(2,1)S(1)} fusion(f32[2,512,1024]{2,1,0:T(8,128)} %get-tuple-element.201, f32[2,512]{1,0:T(2,128)S(1)} %get-tuple-element.202), kind=kLoop, calls=%fused_computation.7.clone.1 | loop fusion | flops 2097152 | bytes 6295552 | tf_op jit(solution)/shard_map/while/body/eval_jaxpr/convert_element_type | solution.py:64
  85.4 1.1 constant_dynamic-slice_fusion.12
  88.3 1.3 copy-done.1
  89.6 1.7 %fusion.56 = bf16[1,512,2,128]{3,1,2,0:T(8,128)(2,1)S(1)} fusion(bf16[2,512,1024]{2,1,0:T(8,128)(2,1)S(1)} %multiply_convert_fusion.2, bf16[1024,2,128]{2,0,1:T(8,128)(2,1)} %get-tuple-element.235), kind=kOutput, calls=%fused_computation.14.clone.1 | convolution fusion | flops 268566528 | bytes 2883584 | tf_op jit(solution)/shard_map/while/body/eval_jaxpr/hbs,shd->bhd/dot_general | solution.py:75
  91.4 1.3 copy_dynamic-update-slice_fusion.3
  92.7 2.3 %fusion.54 = f32[1024,2,128]{0,2,1:T(8,128)S(1)} fusion(bf16[2,512,1024]{2,1,0:T(8,128)(2,1)} %copy-done.1, f32[1024,2,128]{0,2,1:T(8,128)S(1)} %get-tuple-element.219, pred[]{:T(512)S(6)} %compare.9, bf16[1,512,2,128]{3,2,1,0:T(2,128)(2,1)S(1)} %constant_dynamic-slice_fusion.13), kind=kOutput, calls=%fused_computation.10.clone.1 | convolution fusion | flops 268959744 | bytes 4456449 | tf_op jit(solution)/shard_map/while/body/eval_jaxpr/hbs,bhd->shd/dot_general | solution.py:78
  95.0 2.7 %fusion.55 = f32[1024,2,128]{0,2,1:T(8,128)} fusion(bf16[2,512,1024]{2,1,0:T(8,128)(2,1)S(1)} %fusion.53, f32[1024,2,128]{0,2,1:T(8,128)} %get-tuple-element.220, pred[]{:T(512)S(6)} %compare.9, bf16[1,512,2,128]{3,2,1,0:T(2,128)(2,1)S(1)} %copy-done.3), kind=kOutput, calls=%fused_computation.11.clone.1 | convolution fusion | flops 268959744 | bytes 4456449 | tf_op jit(solution)/shard_map/while/body/eval_jaxpr/hbs,bhd->shd/dot_general | solution.py:81
  97.7 1.5 convert_bitcast_fusion.1
  99.6 4.0 %collective-permute-start.8 = (bf16[128,2,256]{2,0,1:T(8,128)(2,1)S(1)}, bf16[128,2,256]{2,0,1:T(8,128)(2,1)S(1)}, u32[]{:S(2)}, u32[]{:S(2)}) collective-permute-start(bf16[128,2,256]{2,0,1:T(8,128)(2,1)S(1)} %copy.65), channel_id=1, source_target_pairs={{13,0},{12,1},{15,2},{14,3},{9,4},{8,5},{11,6},{10,7},{21,8},{20,9... | collective-permute-start | bytes 393224 | tf_op jit(solution)/shard_map/ppermute | solution.py:113
  105.9 2.2 %collective-permute-start.11 = (bf16[128,2,256]{2,0,1:T(8,128)(2,1)}, bf16[128,2,256]{2,0,1:T(8,128)(2,1)S(1)}, u32[]{:S(2)}, u32[]{:S(2)}) collective-permute-start(bf16[128,2,256]{2,0,1:T(8,128)(2,1)} %copy.68), channel_id=1, source_target_pairs={{15,0},{14,1},{9,2},{8,3},{11,4},{10,5},{13,6},{12,7},{23,8},{22,9... | collective-permute-start | bytes 393224 | tf_op jit(solution)/shard_map/ppermute | solution.py:113
  108.9 2.4 %collective-permute-start.12 = (bf16[128,2,256]{2,0,1:T(8,128)(2,1)}, bf16[128,2,256]{2,0,1:T(8,128)(2,1)S(1)}, u32[]{:S(2)}, u32[]{:S(2)}) collective-permute-start(bf16[128,2,256]{2,0,1:T(8,128)(2,1)} %copy.69), channel_id=1, source_target_pairs={{10,0},{11,1},{12,2},{13,3},{14,4},{15,5},{8,6},{9,7},{18,8},{19,9... | collective-permute-start | bytes 393224 | tf_op jit(solution)/shard_map/ppermute | solution.py:113
  112.8 5.4 %collective-permute-done.9 = bf16[128,2,256]{2,0,1:T(8,128)(2,1)S(1)} collective-permute-done((bf16[128,2,256]{2,0,1:T(8,128)(2,1)S(1)}, bf16[128,2,256]{2,0,1:T(8,128)(2,1)S(1)}, u32[]{:S(2)}, u32[]{:S(2)}) %collective-permute-start.9) | collective-permute-done | bytes 131104 | tf_op jit(solution)/shard_map/ppermute | solution.py:113
  118.2 2.3 %collective-permute-start.14 = (bf16[128,2,256]{2,0,1:T(8,128)(2,1)S(1)}, bf16[128,2,256]{2,0,1:T(8,128)(2,1)S(1)}, u32[]{:S(2)}, u32[]{:S(2)}) collective-permute-start(bf16[128,2,256]{2,0,1:T(8,128)(2,1)S(1)} %copy.71), channel_id=1, source_target_pairs={{9,0},{8,1},{11,2},{10,3},{13,4},{12,5},{15,6},{14,7},{17,8},{16,9... | collective-permute-start | bytes 393224 | tf_op jit(solution)/shard_map/ppermute | solution.py:113
  121.3 1.4 broadcast_in_dim_reshape.6
  122.7 1.4 broadcast_in_dim_reshape.7
  126.0 3.3 %dynamic_update_slice.32 = bf16[128,2,8,256]{3,2,1,0:T(8,128)(2,1)S(1)} dynamic-update-slice(bf16[128,2,8,256]{3,2,1,0:T(8,128)(2,1)S(1)} %broadcast_in_dim.42, bf16[128,2,1,256]{3,2,1,0:T(2,128)(2,1)S(1)} %copy.46, s32[]{:T(128)} %constant.79.clone.1, s32[]{:T(128)} %constant.79.clone.1, s32[]{:T(128)S(6)} %select_n.34, s32[]{:T(128)} %constant.79.clone.1) | dynamic-update-slice | bytes 262148 | tf_op jit(solution)/shard_map/jit(dynamic_update_index_in_dim)/dynamic_update_slice | solution.py:114
  129.3 3.3 %dynamic_update_slice.33 = bf16[128,2,8,256]{3,2,1,0:T(8,128)(2,1)S(1)} dynamic-update-slice(bf16[128,2,8,256]{3,2,1,0:T(8,128)(2,1)S(1)} %dynamic_update_slice.32, bf16[128,2,1,256]{3,2,1,0:T(2,128)(2,1)S(1)} %copy.48, s32[]{:T(128)} %constant.79.clone.1, s32[]{:T(128)} %constant.79.clone.1, s32[]{:T(128)S(6)} %select_n.35, s32[]{:T(128)} %constant.79.clone.1) | dynamic-update-slice | bytes 262148 | tf_op jit(solution)/shard_map/jit(dynamic_update_index_in_dim)/dynamic_update_slice | solution.py:114
  132.6 3.3 %dynamic_update_slice.34 = bf16[128,2,8,256]{3,2,1,0:T(8,128)(2,1)S(1)} dynamic-update-slice(bf16[128,2,8,256]{3,2,1,0:T(8,128)(2,1)S(1)} %dynamic_update_slice.33, bf16[128,2,1,256]{3,2,1,0:T(2,128)(2,1)S(1)} %copy.50, s32[]{:T(128)} %constant.79.clone.1, s32[]{:T(128)} %constant.79.clone.1, s32[]{:T(128)S(6)} %select_n.36, s32[]{:T(128)} %constant.79.clone.1) | dynamic-update-slice | bytes 262148 | tf_op jit(solution)/shard_map/jit(dynamic_update_index_in_dim)/dynamic_update_slice | solution.py:114
  135.9 3.3 %dynamic_update_slice.35 = bf16[128,2,8,256]{3,2,1,0:T(8,128)(2,1)S(1)} dynamic-update-slice(bf16[128,2,8,256]{3,2,1,0:T(8,128)(2,1)S(1)} %dynamic_update_slice.34, bf16[128,2,1,256]{3,2,1,0:T(2,128)(2,1)S(1)} %copy.52, s32[]{:T(128)} %constant.79.clone.1, s32[]{:T(128)} %constant.79.clone.1, s32[]{:T(128)S(6)} %select_n.37, s32[]{:T(128)} %constant.79.clone.1) | dynamic-update-slice | bytes 262148 | tf_op jit(solution)/shard_map/jit(dynamic_update_index_in_dim)/dynamic_update_slice | solution.py:114
  139.2 3.3 %dynamic_update_slice.36 = bf16[128,2,8,256]{3,2,1,0:T(8,128)(2,1)S(1)} dynamic-update-slice(bf16[128,2,8,256]{3,2,1,0:T(8,128)(2,1)S(1)} %dynamic_update_slice.35, bf16[128,2,1,256]{3,2,1,0:T(2,128)(2,1)S(1)} %copy.54, s32[]{:T(128)} %constant.79.clone.1, s32[]{:T(128)} %constant.79.clone.1, s32[]{:T(128)S(6)} %select_n.38, s32[]{:T(128)} %constant.79.clone.1) | dynamic-update-slice | bytes 262148 | tf_op jit(solution)/shard_map/jit(dynamic_update_index_in_dim)/dynamic_update_slice | solution.py:114
  142.6 3.3 %dynamic_update_slice.37 = bf16[128,2,8,256]{3,2,1,0:T(8,128)(2,1)S(1)} dynamic-update-slice(bf16[128,2,8,256]{3,2,1,0:T(8,128)(2,1)S(1)} %dynamic_update_slice.36, bf16[128,2,1,256]{3,2,1,0:T(2,128)(2,1)S(1)} %copy.56, s32[]{:T(128)} %constant.79.clone.1, s32[]{:T(128)} %constant.79.clone.1, s32[]{:T(128)S(6)} %select_n.39, s32[]{:T(128)} %constant.79.clone.1) | dynamic-update-slice | bytes 262148 | tf_op jit(solution)/shard_map/jit(dynamic_update_index_in_dim)/dynamic_update_slice | solution.py:114
  145.9 3.3 %dynamic_update_slice.38 = bf16[128,2,8,256]{3,2,1,0:T(8,128)(2,1)S(1)} dynamic-update-slice(bf16[128,2,8,256]{3,2,1,0:T(8,128)(2,1)S(1)} %dynamic_update_slice.37, bf16[128,2,1,256]{3,2,1,0:T(2,128)(2,1)S(1)} %copy.58, s32[]{:T(128)} %constant.79.clone.1, s32[]{:T(128)} %constant.79.clone.1, s32[]{:T(128)S(6)} %select_n.40, s32[]{:T(128)} %constant.79.clone.1) | dynamic-update-slice | bytes 262148 | tf_op jit(solution)/shard_map/jit(dynamic_update_index_in_dim)/dynamic_update_slice | solution.py:114
  149.2 3.3 %dynamic_update_slice.39 = bf16[128,2,8,256]{3,2,1,0:T(8,128)(2,1)S(1)} dynamic-update-slice(bf16[128,2,8,256]{3,2,1,0:T(8,128)(2,1)S(1)} %dynamic_update_slice.38, bf16[128,2,1,256]{3,2,1,0:T(2,128)(2,1)S(1)} %copy.60, s32[]{:T(128)} %constant.79.clone.1, s32[]{:T(128)} %constant.79.clone.1, s32[]{:T(128)S(6)} %select_n.41, s32[]{:T(128)} %constant.79.clone.1) | dynamic-update-slice | bytes 262148 | tf_op jit(solution)/shard_map/jit(dynamic_update_index_in_dim)/dynamic_update_slice | solution.py:114
  152.5 1.1 reshape.25
  (91 shorter events, 14.3 us)
Async XLA Ops:
  4.9 14.9 %copy-start.4 = (bf16[1,1536,256]{2,1,0:T(8,128)(2,1)S(1)}, bf16[1,1536,256]{2,1,0:T(8,128)(2,1)}, u32[]{:S(2)}) copy-start(bf16[1,1536,256]{2,1,0:T(8,128)(2,1)} %param.7) | copy-start | bytes 2359300
  5.1 17.6 %collective-permute-start = (bf16[128,2,256]{0,2,1:T(8,128)(2,1)S(1)}, bf16[128,2,256]{0,2,1:T(8,128)(2,1)}, u32[]{:S(2)}, u32[]{:S(2)}) collective-permute-start(bf16[128,2,256]{0,2,1:T(8,128)(2,1)S(1)} %bitcast.139), channel_id=1, source_target_pairs={{0,13},{1,12},{2,15},{3,14},{4,9},{5,8},{6,11},{7,10},{8,21},{9,20... | collective-permute-start | bytes 393224 | tf_op jit(solution)/shard_map/ppermute | solution.py:108
  9.8 19.6 %collective-permute-start.1 = (bf16[128,2,256]{0,2,1:T(8,128)(2,1)S(1)}, bf16[128,2,256]{0,2,1:T(8,128)(2,1)}, u32[]{:S(2)}, u32[]{:S(2)}) collective-permute-start(bf16[128,2,256]{0,2,1:T(8,128)(2,1)S(1)} %bitcast.136), channel_id=1, source_target_pairs={{0,12},{1,13},{2,14},{3,15},{4,8},{5,9},{6,10},{7,11},{8,20},{9,21... | collective-permute-start | bytes 393224 | tf_op jit(solution)/shard_map/ppermute | solution.py:108
  11.6 18.8 %collective-permute-start.2 = (bf16[128,2,256]{0,2,1:T(8,128)(2,1)S(1)}, bf16[128,2,256]{0,2,1:T(8,128)(2,1)}, u32[]{:S(2)}, u32[]{:S(2)}) collective-permute-start(bf16[128,2,256]{0,2,1:T(8,128)(2,1)S(1)} %bitcast.135), channel_id=1, source_target_pairs={{0,11},{1,10},{2,13},{3,12},{4,15},{5,14},{6,9},{7,8},{8,19},{9,18... | collective-permute-start | bytes 393224 | tf_op jit(solution)/shard_map/ppermute | solution.py:108
  13.0 20.0 %collective-permute-start.3 = (bf16[128,2,256]{0,2,1:T(8,128)(2,1)S(1)}, bf16[128,2,256]{0,2,1:T(8,128)(2,1)}, u32[]{:S(2)}, u32[]{:S(2)}) collective-permute-start(bf16[128,2,256]{0,2,1:T(8,128)(2,1)S(1)} %bitcast.129), channel_id=1, source_target_pairs={{0,15},{1,14},{2,9},{3,8},{4,11},{5,10},{6,13},{7,12},{8,23},{9,22... | collective-permute-start | bytes 393224 | tf_op jit(solution)/shard_map/ppermute | solution.py:108
  16.4 17.5 %collective-permute-start.4 = (bf16[128,2,256]{0,2,1:T(8,128)(2,1)S(1)}, bf16[128,2,256]{0,2,1:T(8,128)(2,1)S(1)}, u32[]{:S(2)}, u32[]{:S(2)}) collective-permute-start(bf16[128,2,256]{0,2,1:T(8,128)(2,1)S(1)} %bitcast.128), channel_id=1, source_target_pairs={{0,10},{1,11},{2,12},{3,13},{4,14},{5,15},{6,8},{7,9},{8,18},{9,19... | collective-permute-start | bytes 393224 | tf_op jit(solution)/shard_map/ppermute | solution.py:108
  22.7 11.3 %collective-permute-start.5 = (bf16[128,2,256]{0,2,1:T(8,128)(2,1)S(1)}, bf16[128,2,256]{0,2,1:T(8,128)(2,1)S(1)}, u32[]{:S(2)}, u32[]{:S(2)}) collective-permute-start(bf16[128,2,256]{0,2,1:T(8,128)(2,1)S(1)} %bitcast.131), channel_id=1, source_target_pairs={{0,14},{1,15},{2,8},{3,9},{4,10},{5,11},{6,12},{7,13},{8,22},{9,23... | collective-permute-start | bytes 393224 | tf_op jit(solution)/shard_map/ppermute | solution.py:108
  29.4 5.3 %collective-permute-start.6 = (bf16[128,2,256]{0,2,1:T(8,128)(2,1)S(1)}, bf16[128,2,256]{0,2,1:T(8,128)(2,1)S(1)}, u32[]{:S(2)}, u32[]{:S(2)}) collective-permute-start(bf16[128,2,256]{0,2,1:T(8,128)(2,1)S(1)} %bitcast.127), channel_id=1, source_target_pairs={{0,9},{1,8},{2,11},{3,10},{4,13},{5,12},{6,15},{7,14},{8,17},{9,16... | collective-permute-start | bytes 393224 | tf_op jit(solution)/shard_map/ppermute | solution.py:108
  30.3 4.6 %collective-permute-start.7 = (bf16[128,2,256]{0,2,1:T(8,128)(2,1)S(1)}, bf16[128,2,256]{0,2,1:T(8,128)(2,1)S(1)}, u32[]{:S(2)}, u32[]{:S(2)}) collective-permute-start(bf16[128,2,256]{0,2,1:T(8,128)(2,1)S(1)} %bitcast.125), channel_id=1, source_target_pairs={{0,8},{1,9},{2,10},{3,11},{4,12},{5,13},{6,14},{7,15},{8,16},{9,17... | collective-permute-start | bytes 393224 | tf_op jit(solution)/shard_map/ppermute | solution.py:108
  42.4 4.0 %copy-start.7 = (bf16[1024,2,128]{0,2,1:T(8,128)(2,1)S(1)}, bf16[1024,2,128]{0,2,1:T(8,128)(2,1)}, u32[]{:S(2)}) copy-start(bf16[1024,2,128]{0,2,1:T(8,128)(2,1)} %get-tuple-element.237) | copy-start | bytes 1572868 | tf_op jit(solution)/shard_map/while
  42.4 4.9 %copy-start = (f32[2,512,1024]{2,1,0:T(8,128)S(1)}, f32[2,512,1024]{2,1,0:T(8,128)}, u32[]{:S(2)}) copy-start(f32[2,512,1024]{2,1,0:T(8,128)} %get-tuple-element.201) | copy-start | bytes 12582916 | tf_op jit(solution)/shard_map/while
  46.4 1.7 %copy-start.2 = (bf16[1,512,2,128]{3,2,1,0:T(2,128)(2,1)}, bf16[1,512,2,128]{3,2,1,0:T(2,128)(2,1)S(1)}, u32[]{:S(2)}) copy-start(bf16[1,512,2,128]{3,2,1,0:T(2,128)(2,1)S(1)} %constant_dynamic-slice_fusion.12) | copy-start | bytes 786436 | tf_op jit(solution)/shard_map/while
  48.2 1.3 copy-start.1
  52.6 2.3 %copy-start.3 = (bf16[1,512,2,128]{3,2,1,0:T(2,128)(2,1)S(1)}, bf16[1,512,2,128]{3,2,1,0:T(2,128)(2,1)}, u32[]{:S(2)}) copy-start(bf16[1,512,2,128]{3,2,1,0:T(2,128)(2,1)} %copy-done.2) | copy-start | bytes 786436 | tf_op jit(solution)/shard_map/while
  61.8 4.0 %copy-start.7 = (bf16[1024,2,128]{0,2,1:T(8,128)(2,1)S(1)}, bf16[1024,2,128]{0,2,1:T(8,128)(2,1)}, u32[]{:S(2)}) copy-start(bf16[1024,2,128]{0,2,1:T(8,128)(2,1)} %get-tuple-element.237) | copy-start | bytes 1572868 | tf_op jit(solution)/shard_map/while
  61.9 4.9 %copy-start = (f32[2,512,1024]{2,1,0:T(8,128)S(1)}, f32[2,512,1024]{2,1,0:T(8,128)}, u32[]{:S(2)}) copy-start(f32[2,512,1024]{2,1,0:T(8,128)} %get-tuple-element.201) | copy-start | bytes 12582916 | tf_op jit(solution)/shard_map/while
  65.9 1.7 %copy-start.2 = (bf16[1,512,2,128]{3,2,1,0:T(2,128)(2,1)}, bf16[1,512,2,128]{3,2,1,0:T(2,128)(2,1)S(1)}, u32[]{:S(2)}) copy-start(bf16[1,512,2,128]{3,2,1,0:T(2,128)(2,1)S(1)} %constant_dynamic-slice_fusion.12) | copy-start | bytes 786436 | tf_op jit(solution)/shard_map/while
  67.6 1.3 copy-start.1
  72.0 2.3 %copy-start.3 = (bf16[1,512,2,128]{3,2,1,0:T(2,128)(2,1)S(1)}, bf16[1,512,2,128]{3,2,1,0:T(2,128)(2,1)}, u32[]{:S(2)}) copy-start(bf16[1,512,2,128]{3,2,1,0:T(2,128)(2,1)} %copy-done.2) | copy-start | bytes 786436 | tf_op jit(solution)/shard_map/while
  82.5 4.0 %copy-start.7 = (bf16[1024,2,128]{0,2,1:T(8,128)(2,1)S(1)}, bf16[1024,2,128]{0,2,1:T(8,128)(2,1)}, u32[]{:S(2)}) copy-start(bf16[1024,2,128]{0,2,1:T(8,128)(2,1)} %get-tuple-element.237) | copy-start | bytes 1572868 | tf_op jit(solution)/shard_map/while
  82.5 4.9 %copy-start = (f32[2,512,1024]{2,1,0:T(8,128)S(1)}, f32[2,512,1024]{2,1,0:T(8,128)}, u32[]{:S(2)}) copy-start(f32[2,512,1024]{2,1,0:T(8,128)} %get-tuple-element.201) | copy-start | bytes 12582916 | tf_op jit(solution)/shard_map/while
  86.5 1.7 %copy-start.2 = (bf16[1,512,2,128]{3,2,1,0:T(2,128)(2,1)}, bf16[1,512,2,128]{3,2,1,0:T(2,128)(2,1)S(1)}, u32[]{:S(2)}) copy-start(bf16[1,512,2,128]{3,2,1,0:T(2,128)(2,1)S(1)} %constant_dynamic-slice_fusion.12) | copy-start | bytes 786436 | tf_op jit(solution)/shard_map/while
  88.3 1.3 copy-start.1
  92.7 2.3 %copy-start.3 = (bf16[1,512,2,128]{3,2,1,0:T(2,128)(2,1)S(1)}, bf16[1,512,2,128]{3,2,1,0:T(2,128)(2,1)}, u32[]{:S(2)}) copy-start(bf16[1,512,2,128]{3,2,1,0:T(2,128)(2,1)} %copy-done.2) | copy-start | bytes 786436 | tf_op jit(solution)/shard_map/while
  97.7 23.6 %copy-start.5 = (bf16[3,512,2,128]{3,2,1,0:T(2,128)(2,1)S(1)}, bf16[3,512,2,128]{3,2,1,0:T(2,128)(2,1)}, u32[]{:S(2)}) copy-start(bf16[3,512,2,128]{3,2,1,0:T(2,128)(2,1)} %get-tuple-element.53) | copy-start | bytes 2359300
  97.7 25.0 %copy-start.6 = (bf16[3,512,2,128]{3,2,1,0:T(2,128)(2,1)S(1)}, bf16[3,512,2,128]{3,2,1,0:T(2,128)(2,1)}, u32[]{:S(2)}) copy-start(bf16[3,512,2,128]{3,2,1,0:T(2,128)(2,1)} %get-tuple-element.54) | copy-start | bytes 2359300
  99.6 13.2 %collective-permute-start.8 = (bf16[128,2,256]{2,0,1:T(8,128)(2,1)S(1)}, bf16[128,2,256]{2,0,1:T(8,128)(2,1)S(1)}, u32[]{:S(2)}, u32[]{:S(2)}) collective-permute-start(bf16[128,2,256]{2,0,1:T(8,128)(2,1)S(1)} %copy.65), channel_id=1, source_target_pairs={{13,0},{12,1},{15,2},{14,3},{9,4},{8,5},{11,6},{10,7},{21,8},{20,9... | collective-permute-start | bytes 393224 | tf_op jit(solution)/shard_map/ppermute | solution.py:113
  103.7 14.5 %collective-permute-start.9 = (bf16[128,2,256]{2,0,1:T(8,128)(2,1)S(1)}, bf16[128,2,256]{2,0,1:T(8,128)(2,1)S(1)}, u32[]{:S(2)}, u32[]{:S(2)}) collective-permute-start(bf16[128,2,256]{2,0,1:T(8,128)(2,1)S(1)} %copy.66), channel_id=1, source_target_pairs={{12,0},{13,1},{14,2},{15,3},{8,4},{9,5},{10,6},{11,7},{20,8},{21,9... | collective-permute-start | bytes 393224 | tf_op jit(solution)/shard_map/ppermute | solution.py:113
  104.6 16.7 %collective-permute-start.10 = (bf16[128,2,256]{2,0,1:T(8,128)(2,1)S(1)}, bf16[128,2,256]{2,0,1:T(8,128)(2,1)S(1)}, u32[]{:S(2)}, u32[]{:S(2)}) collective-permute-start(bf16[128,2,256]{2,0,1:T(8,128)(2,1)S(1)} %copy.67), channel_id=1, source_target_pairs={{11,0},{10,1},{13,2},{12,3},{15,4},{14,5},{9,6},{8,7},{19,8},{18,9... | collective-permute-start | bytes 393224 | tf_op jit(solution)/shard_map/ppermute | solution.py:113
  105.9 18.8 %collective-permute-start.11 = (bf16[128,2,256]{2,0,1:T(8,128)(2,1)}, bf16[128,2,256]{2,0,1:T(8,128)(2,1)S(1)}, u32[]{:S(2)}, u32[]{:S(2)}) collective-permute-start(bf16[128,2,256]{2,0,1:T(8,128)(2,1)} %copy.68), channel_id=1, source_target_pairs={{15,0},{14,1},{9,2},{8,3},{11,4},{10,5},{13,6},{12,7},{23,8},{22,9... | collective-permute-start | bytes 393224 | tf_op jit(solution)/shard_map/ppermute | solution.py:113
  108.9 16.1 %collective-permute-start.12 = (bf16[128,2,256]{2,0,1:T(8,128)(2,1)}, bf16[128,2,256]{2,0,1:T(8,128)(2,1)S(1)}, u32[]{:S(2)}, u32[]{:S(2)}) collective-permute-start(bf16[128,2,256]{2,0,1:T(8,128)(2,1)} %copy.69), channel_id=1, source_target_pairs={{10,0},{11,1},{12,2},{13,3},{14,4},{15,5},{8,6},{9,7},{18,8},{19,9... | collective-permute-start | bytes 393224 | tf_op jit(solution)/shard_map/ppermute | solution.py:113
  112.8 12.3 %collective-permute-start.13 = (bf16[128,2,256]{2,0,1:T(8,128)(2,1)}, bf16[128,2,256]{2,0,1:T(8,128)(2,1)S(1)}, u32[]{:S(2)}, u32[]{:S(2)}) collective-permute-start(bf16[128,2,256]{2,0,1:T(8,128)(2,1)} %copy.70), channel_id=1, source_target_pairs={{14,0},{15,1},{8,2},{9,3},{10,4},{11,5},{12,6},{13,7},{22,8},{23,9... | collective-permute-start | bytes 393224 | tf_op jit(solution)/shard_map/ppermute | solution.py:113
  118.2 7.1 %collective-permute-start.14 = (bf16[128,2,256]{2,0,1:T(8,128)(2,1)S(1)}, bf16[128,2,256]{2,0,1:T(8,128)(2,1)S(1)}, u32[]{:S(2)}, u32[]{:S(2)}) collective-permute-start(bf16[128,2,256]{2,0,1:T(8,128)(2,1)S(1)} %copy.71), channel_id=1, source_target_pairs={{9,0},{8,1},{11,2},{10,3},{13,4},{12,5},{15,6},{14,7},{17,8},{16,9... | collective-permute-start | bytes 393224 | tf_op jit(solution)/shard_map/ppermute | solution.py:113
  121.3 4.4 %collective-permute-start.15 = (bf16[128,2,256]{2,0,1:T(8,128)(2,1)}, bf16[128,2,256]{2,0,1:T(8,128)(2,1)S(1)}, u32[]{:S(2)}, u32[]{:S(2)}) collective-permute-start(bf16[128,2,256]{2,0,1:T(8,128)(2,1)} %copy.72), channel_id=1, source_target_pairs={{8,0},{9,1},{10,2},{11,3},{12,4},{13,5},{14,6},{15,7},{16,8},{17,9... | collective-permute-start | bytes 393224 | tf_op jit(solution)/shard_map/ppermute | solution.py:113

commit v2 on v1

v2 whole, which is shorter than its diff:
```python
import functools

import jax
import jax.numpy as jnp
from jax import lax
from jax.experimental import pallas as pl
from jax.experimental.pallas import tpu as pltpu
from jax.sharding import PartitionSpec as P

HEAD = 128
AXES = ("segment", "seq", "tp")
LOG2E = 1.4426950408889634
MIB = 1 << 20


def offsets():
    seq_count = lax.axis_size("seq")
    tp_count = lax.axis_size("tp")
    pairs = [(dz, dy) for dz in range(seq_count) for dy in range(tp_count)]
    middle = seq_count / 2
    return sorted(pairs, key=lambda o: (abs(o[0] - middle), -o[1]))


def group_at(offset):
    seq_count = lax.axis_size("seq")
    tp_count = lax.axis_size("tp")
    z = lax.rem(lax.axis_index("seq") + offset[0], seq_count)
    y = lax.rem(lax.axis_index("tp") + offset[1], tp_count)
    return z * tp_count + y


def route(offset, back):
    segments, seq_count, tp_count = (lax.axis_size(a) for a in AXES)
    hops = []
    for s in range(segments):
        for z in range(seq_count):
            for y in range(tp_count):
                source = (s * seq_count + z) * tp_count + y
                s_to = (s + 1) % segments
                z_to = (z + offset[0]) % seq_count
                y_to = (y + offset[1]) % tp_count
                target = (s_to * seq_count + z_to) * tp_count + y_to
                hops.append((target, source) if back else (source, target))
    return hops


def pack(pairs, order, heads):
    _, rows, _, width = pairs.shape
    local = heads * HEAD

    def kernel(pairs_ref, *refs):
        outs, sem = refs[:-1], refs[-1]
        copies = []
        for i, offset in enumerate(order):
            base = group_at(offset) * local
            for h in range(heads):
                column = pl.multiple_of(base + h * HEAD, HEAD)
                copy = pltpu.make_async_copy(
                    pairs_ref.at[0, :, :, pl.ds(column, HEAD)], outs[i].at[h], sem.at[i, h]
                )
                copy.start()
                copies.append(copy)
        for copy in copies:
            copy.wait()

    return pl.pallas_call(
        kernel,
        out_shape=[jax.ShapeDtypeStruct((heads, rows, 2, HEAD), pairs.dtype)] * len(order),
        in_specs=[pl.BlockSpec(memory_space=pl.ANY)],
        out_specs=[pl.BlockSpec(memory_space=pl.ANY)] * len(order),
        scratch_shapes=[pltpu.SemaphoreType.DMA((len(order), heads))],
        name="pack",
    )(pairs)


def unpack(blocks, order, width):
    heads, rows, _, _ = blocks[0].shape
    local = heads * HEAD

    def kernel(*refs):
        ins, out, sem = refs[: len(order)], refs[len(order)], refs[-1]
        copies = []
        for i, offset in enumerate(order):
            base = group_at(offset) * local
            for h in range(heads):
                column = pl.multiple_of(base + h * HEAD, HEAD)
                copy = pltpu.make_async_copy(
                    ins[i].at[h], out.at[0, :, :, pl.ds(column, HEAD)], sem.at[i, h]
                )
                copy.start()
                copies.append(copy)
        for copy in copies:
            copy.wait()

    return pl.pallas_call(
        kernel,
        out_shape=jax.ShapeDtypeStruct((1, rows, 2, width), blocks[0].dtype),
        in_specs=[pl.BlockSpec(memory_space=pl.ANY)] * len(order),
        out_specs=pl.BlockSpec(memory_space=pl.ANY),
        scratch_shapes=[pltpu.SemaphoreType.DMA((len(order), heads))],
        name="unpack",
    )(*blocks)


def dot(a, b, contract=((1,), (0,))):
    return lax.dot_general(a, b, (contract, ((), ())), preferred_element_type=jnp.float32)


NT = ((1,), (1,))


def splitter(rows):
    to = lax.broadcasted_iota(jnp.int32, (2 * rows, 2 * rows), 0)
    source = lax.broadcasted_iota(jnp.int32, (2 * rows, 2 * rows), 1)
    wanted = jnp.where(to < rows, 2 * to, 2 * (to - rows) + 1)
    return jnp.where(source == wanted, 1.0, 0.0).astype(jnp.bfloat16)


def joiner(rows):
    to = lax.broadcasted_iota(jnp.int32, (2 * rows, 2 * rows), 0)
    source = lax.broadcasted_iota(jnp.int32, (2 * rows, 2 * rows), 1)
    wanted = jnp.where(source < rows, 2 * source, 2 * (source - rows) + 1)
    return jnp.where(to == wanted, 1.0, 0.0).astype(jnp.bfloat16)


def attend_kernel(count, steps, sub, *refs):
    chunks = refs[:count]
    q_ref, g_ref, ctx_ref, gq_ref = refs[count : count + 4]
    outs = refs[count + 4 : 2 * count + 4]
    k_ref, v_ref, kt_ref, vt_ref, gk_ref, gv_ref = refs[2 * count + 4 :]
    rows = chunks[0].shape[1] // 2
    factor = HEAD**-0.5
    step = pl.program_id(1)

    @pl.when(step == 0)
    def _():
        split = splitter(rows)
        for i in range(count):
            both = dot(split, chunks[i][0])
            here = slice(i * rows, (i + 1) * rows)
            k_ref[here, :] = both[:rows].astype(jnp.bfloat16)
            v_ref[here, :] = both[rows:].astype(jnp.bfloat16)
            kt_ref[:, here] = both[:rows].T.astype(jnp.bfloat16)
            vt_ref[:HEAD, here] = both[rows:].T.astype(jnp.bfloat16)
        vt_ref[HEAD:, :] = jnp.ones((vt_ref.shape[0] - HEAD, vt_ref.shape[1]), jnp.bfloat16)
        gk_ref[...] = jnp.zeros_like(gk_ref)
        gv_ref[...] = jnp.zeros_like(gv_ref)

    for j in range(q_ref.shape[1] // sub):
        here = slice(j * sub, (j + 1) * sub)
        qt = q_ref[0, here, :].astype(jnp.float32).T
        gt = g_ref[0, here, :].astype(jnp.float32).T
        scores = dot(k_ref[...], qt.astype(jnp.bfloat16))
        top = jnp.max(scores, axis=0, keepdims=True)
        raised = jnp.exp2((scores - top) * (factor * LOG2E))
        raised_low = raised.astype(jnp.bfloat16)
        summed = dot(vt_ref[...], raised_low)
        scale = 1.0 / summed[HEAD : HEAD + 1, :]
        context = summed[:HEAD, :] * scale
        row_dot = jnp.sum(gt * context, axis=0, keepdims=True)
        grad_weights = dot(v_ref[...], gt.astype(jnp.bfloat16))
        grad_scores = (raised * (grad_weights - row_dot)).astype(jnp.bfloat16)
        ctx_ref[0, here, :] = context.T.astype(jnp.bfloat16)
        grad_q = dot(kt_ref[...], grad_scores) * (scale * factor)
        gq_ref[0, here, :] = grad_q.T.astype(jnp.bfloat16)
        gk_ref[...] += dot(grad_scores, (qt * (scale * factor)).astype(jnp.bfloat16), NT)
        gv_ref[...] += dot(raised_low, (gt * scale).astype(jnp.bfloat16), NT)

    @pl.when(step == steps - 1)
    def _():
        join = joiner(rows)
        for i in range(count):
            here = slice(i * rows, (i + 1) * rows)
            both = jnp.concatenate([gk_ref[here, :], gv_ref[here, :]], axis=0)
            outs[i][0] = dot(join, both.astype(jnp.bfloat16)).astype(jnp.bfloat16)


def attend(chunks, queries, upstream):
    heads, pair_rows, _ = chunks[0].shape
    count = len(chunks)
    enc_len = count * pair_rows // 2
    dec_len = queries.shape[1]
    block = 512 if dec_len % 512 == 0 else dec_len
    sub = 256 if block % 256 == 0 else block
    steps = dec_len // block
    chunk_spec = pl.BlockSpec((1, pair_rows, HEAD), lambda h, i: (h, 0, 0))
    row_spec = pl.BlockSpec((1, block, HEAD), lambda h, i: (0, i, h))
    rows_shape = jax.ShapeDtypeStruct(queries.shape, queries.dtype)
    results = pl.pallas_call(
        functools.partial(attend_kernel, count, steps, sub),
        grid=(heads, steps),
        out_shape=[rows_shape, rows_shape]
        + [jax.ShapeDtypeStruct(c.shape, c.dtype) for c in chunks],
        in_specs=[chunk_spec] * count + [row_spec] * 2,
        out_specs=[row_spec] * 2 + [chunk_spec] * count,
        scratch_shapes=[
            pltpu.VMEM((enc_len, HEAD), jnp.bfloat16),
            pltpu.VMEM((enc_len, HEAD), jnp.bfloat16),
            pltpu.VMEM((HEAD, enc_len), jnp.bfloat16),
            pltpu.VMEM((HEAD + 16, enc_len), jnp.bfloat16),
            pltpu.VMEM((enc_len, HEAD), jnp.float32),
            pltpu.VMEM((enc_len, HEAD), jnp.float32),
        ],
        compiler_params=pltpu.CompilerParams(vmem_limit_bytes=48 * MIB),
        cost_estimate=pl.CostEstimate(
            flops=heads * 12 * enc_len * dec_len * HEAD,
            bytes_accessed=heads * HEAD * (8 * enc_len + 8 * dec_len),
            transcendentals=heads * enc_len * dec_len,
        ),
        name="attend",
    )(*chunks, queries, upstream)
    return results[0], results[1], results[2:]


def shards(pairs, queries, upstream):
    _, rows, _, width = pairs.shape
    heads = queries.shape[2] // HEAD
    order = offsets()
    arrived = []
    for offset, block in zip(order, pack(pairs, order, heads)):
        block = block.reshape(heads, 2 * rows, HEAD)
        arrived.append(lax.ppermute(block, AXES, route(offset, False)))
    context, grad_query, grads = attend(arrived, queries, upstream)
    returned = []
    for offset, block in zip(order, grads):
        block = lax.ppermute(block, AXES, route(offset, True))
        returned.append(block.reshape(heads, rows, 2, HEAD))
    return context, grad_query, unpack(returned, order, width)


def solution(mesh):
    return jax.shard_map(
        shards,
        mesh=mesh,
        in_specs=(
            P("segment", ("seq", "tp"), None, None),
            P("segment", None, ("seq", "tp")),
            P("segment", None, ("seq", "tp")),
        ),
        out_specs=(
            P("segment", None, ("seq", "tp")),
            P("segment", None, ("seq", "tp")),
            P("segment", ("seq", "tp"), None, None),
        ),
        check_vma=False,
    )
```

time: 157 us -> 146 us (0.930); the launches traced: 154 us -> 146 us
  Pallas kernels: 0 us -> 86.4 us
  local copies, waits for them, and re-layouts: 65.6 us -> 1.77 us
  matrix products: 37.1 us -> 0 us
  waiting for transfers between devices: 11.9 us -> 25.6 us
  other arithmetic: 10.4 us -> 0 us
  starting transfers between devices: 27.2 us -> 31 us
    pallas_call x0 -> x3, Pallas kernels: none -> 86.4 us  [the longest x1 33 us: pack(): pl.pallas_call(kernel, out_shape=[jax.ShapeDtypeStruct((heads, rows, 2, H...]
    dynamic_update_slice x11 -> x0, local copies, waits for them, and re-layouts: 30.5 us -> none  [the longest x8 26.5 us: shards(): lax.dynamic_update_index_in_dim(grad_pairs, block, group_at(offset), axis=2)]
    dot_general x15 -> x0, matrix products: 24.1 us -> none  [the longest x3 6.91 us: step(): jnp.einsum('hbs,bhd->shd', weights_low, grad_block, preferred_element_typ...]
    sub x3 -> x0, matrix products: 13.1 us -> none  [step(): raised = jnp.exp(scores - row_max)]
    ppermute x8, waiting for transfers between devices: 5.82 us -> 15.8 us  [shards(): arrived.append(lax.ppermute(block, AXES, route(offset, False)))]
    dynamic_slice x7 -> x0, local copies, waits for them, and re-layouts: 9.25 us -> none  [the longest x6 6.81 us: attend(): lax.scan(step, (zeros_start, zeros_start), (query_blocks, grad_blocks))]
    convert_element_type x3 -> x0, other arithmetic: 8.6 us -> none  [step(): weights_low = weights.astype(jnp.bfloat16)]
    another operation x4 -> x0, local copies, waits for them, and re-layouts: 6.53 us -> none  [the longest x1 2.71 us: attend(): query_blocks = query_rows.reshape(count, block, num_heads, HEAD)]
  transfers between devices with their start and end apart: 16 -> 16, of which waited for: 7 -> 9; matrix products, arithmetic and copies ran while one was open for 11% -> 0% of each run, Pallas kernels for 0% -> 0%
where the time goes in v2:
time: 146 us
  Pallas kernels  86.4 us (59%)
  starting transfers between devices  31 us (21%)
  waiting for transfers between devices  25.6 us (18%)
  local copies, waits for them, and re-layouts  1.77 us (1%)
    pallas_call x1, Pallas kernels, pack(): pl.pallas_call(kernel, out_shape=[jax.ShapeDtypeStruct((heads, rows, 2, H...  33 us
    pallas_call x1, Pallas kernels, unpack(): pl.pallas_call(kernel, out_shape=jax.ShapeDtypeStruct((1, rows, 2, width)...  33 us
    pallas_call x1, Pallas kernels, attend(): pl.pallas_call(functools.partial(attend_kernel, count, steps, sub), grid=...  20.4 us
    ppermute x8, starting transfers between devices, shards(): block = lax.ppermute(block, AXES, route(offset, True))  17.2 us
    ppermute x8, waiting for transfers between devices, shards(): arrived.append(lax.ppermute(block, AXES, route(offset, False)))  15.8 us
    ppermute x8, starting transfers between devices, shards(): arrived.append(lax.ppermute(block, AXES, route(offset, False)))  13.8 us
    ppermute x8, waiting for transfers between devices, shards(): block = lax.ppermute(block, AXES, route(offset, True))  9.84 us
  transfers between devices with their start and end apart: 16, of which 9 were waited for; matrix products, arithmetic and copies ran while one was open for 0% of the time, Pallas kernels for 0%

profile of v2, /device:TPU:0, one launch (start us, length us, event | category | flops | bytes accessed | tf_op | source)
XLA Modules:
  0.0 145.5 jit_solution(17552387244718111999)
XLA Ops:
  0.6 0.0 copy-start
  0.6 33.0 %pack.1 = (bf16[2,128,2,128]{3,2,1,0:T(2,128)(2,1)}, bf16[2,128,2,128]{3,2,1,0:T(2,128)(2,1)}, bf16[2,128,2,128]{3,2,1,0:T(2,128)(2,1)}, bf16[2,128,2,128]{3,2,1...) custom-call(bf16[1,128,2,2048]{3,2,1,0:T(2,128)(2,1)} %pairs_ref.1), custom_call_target="tpu_custom_call" | custom-call | tf_op jit(solution)/shard_map/pack/pallas_call | solution.py:66
  33.7 3.5 %collective-permute-start.1 = (bf16[2,256,128]{2,1,0:T(8,128)(2,1)}, bf16[2,256,128]{2,1,0:T(8,128)(2,1)S(1)}, u32[]{:S(2)}, u32[]{:S(2)}) collective-permute-start(bf16[2,256,128]{2,1,0:T(8,128)(2,1)} %bitcast.31), channel_id=1, source_target_pairs={{0,12},{1,13},{2,14},{3,15},{4,8},{5,9},{6,10},{7,11},{8,20},{9,21... | collective-permute-start | bytes 393224 | tf_op jit(solution)/shard_map/ppermute | solution.py:222
  37.2 2.5 %collective-permute-start = (bf16[2,256,128]{2,1,0:T(8,128)(2,1)}, bf16[2,256,128]{2,1,0:T(8,128)(2,1)S(1)}, u32[]{:S(2)}, u32[]{:S(2)}) collective-permute-start(bf16[2,256,128]{2,1,0:T(8,128)(2,1)} %bitcast.30), channel_id=1, source_target_pairs={{0,13},{1,12},{2,15},{3,14},{4,9},{5,8},{6,11},{7,10},{8,21},{9,20... | collective-permute-start | bytes 393224 | tf_op jit(solution)/shard_map/ppermute | solution.py:222
  39.7 1.2 collective-permute-start.2
  40.9 3.2 %collective-permute-start.3 = (bf16[2,256,128]{2,1,0:T(8,128)(2,1)}, bf16[2,256,128]{2,1,0:T(8,128)(2,1)S(1)}, u32[]{:S(2)}, u32[]{:S(2)}) collective-permute-start(bf16[2,256,128]{2,1,0:T(8,128)(2,1)} %bitcast.28), channel_id=1, source_target_pairs={{0,15},{1,14},{2,9},{3,8},{4,11},{5,10},{6,13},{7,12},{8,23},{9,22... | collective-permute-start | bytes 393224 | tf_op jit(solution)/shard_map/ppermute | solution.py:222
  44.1 0.0 collective-permute-start.4
  44.1 5.4 %collective-permute-done.1.refs_1_ = bf16[2,256,128]{2,1,0:T(8,128)(2,1)S(1)} collective-permute-done((bf16[2,256,128]{2,1,0:T(8,128)(2,1)}, bf16[2,256,128]{2,1,0:T(8,128)(2,1)S(1)}, u32[]{:S(2)}, u32[]{:S(2)}) %collective-permute-start.1) | collective-permute-done | bytes 131104 | tf_op jit(solution)/shard_map/ppermute | solution.py:222
  49.5 1.6 %collective-permute-start.5 = (bf16[2,256,128]{2,1,0:T(8,128)(2,1)}, bf16[2,256,128]{2,1,0:T(8,128)(2,1)S(1)}, u32[]{:S(2)}, u32[]{:S(2)}) collective-permute-start(bf16[2,256,128]{2,1,0:T(8,128)(2,1)} %bitcast.26), channel_id=1, source_target_pairs={{0,14},{1,15},{2,8},{3,9},{4,10},{5,11},{6,12},{7,13},{8,22},{9,23... | collective-permute-start | bytes 393224 | tf_op jit(solution)/shard_map/ppermute | solution.py:222
  51.1 6.7 %collective-permute-done.refs_0_ = bf16[2,256,128]{2,1,0:T(8,128)(2,1)S(1)} collective-permute-done((bf16[2,256,128]{2,1,0:T(8,128)(2,1)}, bf16[2,256,128]{2,1,0:T(8,128)(2,1)S(1)}, u32[]{:S(2)}, u32[]{:S(2)}) %collective-permute-start) | collective-permute-done | bytes 131104 | tf_op jit(solution)/shard_map/ppermute | solution.py:222
  57.8 0.0 collective-permute-start.6
  57.8 0.0 collective-permute-done.2.refs_2_
  57.8 1.8 %collective-permute-start.7 = (bf16[2,256,128]{2,1,0:T(8,128)(2,1)}, bf16[2,256,128]{2,1,0:T(8,128)(2,1)S(1)}, u32[]{:S(2)}, u32[]{:S(2)}) collective-permute-start(bf16[2,256,128]{2,1,0:T(8,128)(2,1)} %bitcast.24), channel_id=1, source_target_pairs={{0,8},{1,9},{2,10},{3,11},{4,12},{5,13},{6,14},{7,15},{8,16},{9,17... | collective-permute-start | bytes 393224 | tf_op jit(solution)/shard_map/ppermute | solution.py:222
  59.6 0.0 collective-permute-done.3.refs_3_
  59.6 0.0 collective-permute-done.4.refs_4_
  59.6 1.2 collective-permute-done.5.refs_5_
  60.8 2.5 %collective-permute-done.6.refs_6_ = bf16[2,256,128]{2,1,0:T(8,128)(2,1)S(1)} collective-permute-done((bf16[2,256,128]{2,1,0:T(8,128)(2,1)}, bf16[2,256,128]{2,1,0:T(8,128)(2,1)S(1)}, u32[]{:S(2)}, u32[]{:S(2)}) %collective-permute-start.6) | collective-permute-done | bytes 131104 | tf_op jit(solution)/shard_map/ppermute | solution.py:222
  63.3 0.0 collective-permute-done.7.refs_7_
  63.3 0.0 copy-done
  63.3 0.0 copy-start.1
  63.3 1.1 copy-done.1
  64.5 20.4 %attend.1 = (bf16[1,1536,256]{2,1,0:T(8,128)(2,1)}, bf16[1,1536,256]{2,1,0:T(8,128)(2,1)}, bf16[2,256,128]{2,1,0:T(8,128)(2,1)S(1)}, bf16[2,256,128]{2,1,0:T(8,1...) custom-call(bf16[2,256,128]{2,1,0:T(8,128)(2,1)S(1)} %collective-per, ...), custom_call_target="tpu_custom_call" | custom-call | flops 4831838208 | bytes 5242880 | tf_op jit(solution)/shard_map/attend/pallas_call | solution.py:189
  84.8 3.9 %collective-permute-start.8 = (bf16[2,256,128]{2,1,0:T(8,128)(2,1)S(1)}, bf16[2,256,128]{2,1,0:T(8,128)(2,1)S(1)}, u32[]{:S(2)}, u32[]{:S(2)}) collective-permute-start(bf16[2,256,128]{2,1,0:T(8,128)(2,1)S(1)} %get-tuple-element.31), channel_id=1, source_target_pairs={{13,0},{12,1},{15,2},{14,3},{9,4},{8,5},{11,6},{10,7},{21,8},{20,9... | collective-permute-start | bytes 393224 | tf_op jit(solution)/shard_map/ppermute | solution.py:226
  88.7 1.4 collective-permute-start.9
  90.2 0.5 collective-permute-start.10
  90.7 1.7 %collective-permute-start.11 = (bf16[2,256,128]{2,1,0:T(8,128)(2,1)S(1)}, bf16[2,256,128]{2,1,0:T(8,128)(2,1)S(1)}, u32[]{:S(2)}, u32[]{:S(2)}) collective-permute-start(bf16[2,256,128]{2,1,0:T(8,128)(2,1)S(1)} %get-tuple-element.34), channel_id=1, source_target_pairs={{15,0},{14,1},{9,2},{8,3},{11,4},{10,5},{13,6},{12,7},{23,8},{22,9... | collective-permute-start | bytes 393224 | tf_op jit(solution)/shard_map/ppermute | solution.py:226
  92.4 2.8 %collective-permute-start.12 = (bf16[2,256,128]{2,1,0:T(8,128)(2,1)S(1)}, bf16[2,256,128]{2,1,0:T(8,128)(2,1)S(1)}, u32[]{:S(2)}, u32[]{:S(2)}) collective-permute-start(bf16[2,256,128]{2,1,0:T(8,128)(2,1)S(1)} %get-tuple-element.35), channel_id=1, source_target_pairs={{10,0},{11,1},{12,2},{13,3},{14,4},{15,5},{8,6},{9,7},{18,8},{19,9... | collective-permute-start | bytes 393224 | tf_op jit(solution)/shard_map/ppermute | solution.py:226
  95.2 3.0 %collective-permute-done.8 = bf16[2,256,128]{2,1,0:T(8,128)(2,1)S(1)} collective-permute-done((bf16[2,256,128]{2,1,0:T(8,128)(2,1)S(1)}, bf16[2,256,128]{2,1,0:T(8,128)(2,1)S(1)}, u32[]{:S(2)}, u32[]{:S(2)}) %collective-permute-start.8) | collective-permute-done | bytes 131104 | tf_op jit(solution)/shard_map/ppermute | solution.py:226
  98.2 0.0 copy-start.2
  98.2 1.5 %collective-permute-start.13 = (bf16[2,256,128]{2,1,0:T(8,128)(2,1)S(1)}, bf16[2,256,128]{2,1,0:T(8,128)(2,1)S(1)}, u32[]{:S(2)}, u32[]{:S(2)}) collective-permute-start(bf16[2,256,128]{2,1,0:T(8,128)(2,1)S(1)} %get-tuple-element.36), channel_id=1, source_target_pairs={{14,0},{15,1},{8,2},{9,3},{10,4},{11,5},{12,6},{13,7},{22,8},{23,9... | collective-permute-start | bytes 393224 | tf_op jit(solution)/shard_map/ppermute | solution.py:226
  99.7 3.9 %collective-permute-done.9 = bf16[2,256,128]{2,1,0:T(8,128)(2,1)S(1)} collective-permute-done((bf16[2,256,128]{2,1,0:T(8,128)(2,1)S(1)}, bf16[2,256,128]{2,1,0:T(8,128)(2,1)S(1)}, u32[]{:S(2)}, u32[]{:S(2)}) %collective-permute-start.9) | collective-permute-done | bytes 131104 | tf_op jit(solution)/shard_map/ppermute | solution.py:226
  103.7 0.0 copy-start.3
  103.7 4.3 %collective-permute-start.14 = (bf16[2,256,128]{2,1,0:T(8,128)(2,1)S(1)}, bf16[2,256,128]{2,1,0:T(8,128)(2,1)S(1)}, u32[]{:S(2)}, u32[]{:S(2)}) collective-permute-start(bf16[2,256,128]{2,1,0:T(8,128)(2,1)S(1)} %get-tuple-element.37), channel_id=1, source_target_pairs={{9,0},{8,1},{11,2},{10,3},{13,4},{12,5},{15,6},{14,7},{17,8},{16,9... | collective-permute-start | bytes 393224 | tf_op jit(solution)/shard_map/ppermute | solution.py:226
  108.0 0.0 collective-permute-done.10
  108.0 0.0 copy-start.4
  108.0 0.9 collective-permute-start.15
  108.9 0.0 collective-permute-done.11
  108.9 0.0 copy-start.5
  108.9 0.4 collective-permute-done.12
  109.3 0.0 copy-start.6
  109.3 0.0 collective-permute-done.13
  109.3 0.0 copy-start.7
  109.4 1.2 collective-permute-done.14
  110.5 0.0 copy-start.8
  110.5 1.4 collective-permute-done.15
  111.9 0.0 copy-start.9
  111.9 0.0 copy-done.2
  111.9 0.0 copy-done.3
  111.9 0.0 copy-done.4
  111.9 0.0 copy-done.5
  111.9 0.0 copy-done.6
  111.9 0.0 copy-done.7
  111.9 0.0 copy-done.8
  111.9 0.6 copy-done.9
  112.5 33.0 %unpack.1 = bf16[1,128,2,2048]{3,2,1,0:T(2,128)(2,1)} custom-call(bf16[2,128,2,128]{3,2,1,0:T(2,128)(2,1)} %bitcast.16, bf16[2,128,2,128]{3,2,1,0:T(2,128)(2,1)} %bitcast.17, bf16[2,128,2,128]{3,2,1,0:T(2,128)(2,1)} %bitcast.18, bf16[2,128,2,128]{3,2,1,0:T(2,128)(2,1)} %bitcast.19, bf16[2,128,2,128]{3,2,1,0:T(2,128)(2,1)} %bitcast.20, ...), custom_call_target="tpu_custom_call" | custom-call | tf_op jit(solution)/shard_map/unpack/pallas_call | solution.py:95
Async XLA Ops:
  0.6 62.7 %copy-start = (bf16[1,1536,256]{2,1,0:T(8,128)(2,1)S(1)}, bf16[1,1536,256]{2,1,0:T(8,128)(2,1)}, u32[]{:S(2)}) copy-start(bf16[1,1536,256]{2,1,0:T(8,128)(2,1)} %refs_8_.1) | copy-start | bytes 2359300
  33.7 15.8 %collective-permute-start.1 = (bf16[2,256,128]{2,1,0:T(8,128)(2,1)}, bf16[2,256,128]{2,1,0:T(8,128)(2,1)S(1)}, u32[]{:S(2)}, u32[]{:S(2)}) collective-permute-start(bf16[2,256,128]{2,1,0:T(8,128)(2,1)} %bitcast.31), channel_id=1, source_target_pairs={{0,12},{1,13},{2,14},{3,15},{4,8},{5,9},{6,10},{7,11},{8,20},{9,21... | collective-permute-start | bytes 393224 | tf_op jit(solution)/shard_map/ppermute | solution.py:222
  37.2 20.6 %collective-permute-start = (bf16[2,256,128]{2,1,0:T(8,128)(2,1)}, bf16[2,256,128]{2,1,0:T(8,128)(2,1)S(1)}, u32[]{:S(2)}, u32[]{:S(2)}) collective-permute-start(bf16[2,256,128]{2,1,0:T(8,128)(2,1)} %bitcast.30), channel_id=1, source_target_pairs={{0,13},{1,12},{2,15},{3,14},{4,9},{5,8},{6,11},{7,10},{8,21},{9,20... | collective-permute-start | bytes 393224 | tf_op jit(solution)/shard_map/ppermute | solution.py:222
  39.7 18.1 %collective-permute-start.2 = (bf16[2,256,128]{2,1,0:T(8,128)(2,1)}, bf16[2,256,128]{2,1,0:T(8,128)(2,1)S(1)}, u32[]{:S(2)}, u32[]{:S(2)}) collective-permute-start(bf16[2,256,128]{2,1,0:T(8,128)(2,1)} %bitcast.29), channel_id=1, source_target_pairs={{0,11},{1,10},{2,13},{3,12},{4,15},{5,14},{6,9},{7,8},{8,19},{9,18... | collective-permute-start | bytes 393224 | tf_op jit(solution)/shard_map/ppermute | solution.py:222
  40.9 18.7 %collective-permute-start.3 = (bf16[2,256,128]{2,1,0:T(8,128)(2,1)}, bf16[2,256,128]{2,1,0:T(8,128)(2,1)S(1)}, u32[]{:S(2)}, u32[]{:S(2)}) collective-permute-start(bf16[2,256,128]{2,1,0:T(8,128)(2,1)} %bitcast.28), channel_id=1, source_target_pairs={{0,15},{1,14},{2,9},{3,8},{4,11},{5,10},{6,13},{7,12},{8,23},{9,22... | collective-permute-start | bytes 393224 | tf_op jit(solution)/shard_map/ppermute | solution.py:222
  44.1 15.5 %collective-permute-start.4 = (bf16[2,256,128]{2,1,0:T(8,128)(2,1)}, bf16[2,256,128]{2,1,0:T(8,128)(2,1)S(1)}, u32[]{:S(2)}, u32[]{:S(2)}) collective-permute-start(bf16[2,256,128]{2,1,0:T(8,128)(2,1)} %bitcast.27), channel_id=1, source_target_pairs={{0,10},{1,11},{2,12},{3,13},{4,14},{5,15},{6,8},{7,9},{8,18},{9,19... | collective-permute-start | bytes 393224 | tf_op jit(solution)/shard_map/ppermute | solution.py:222
  49.5 11.3 %collective-permute-start.5 = (bf16[2,256,128]{2,1,0:T(8,128)(2,1)}, bf16[2,256,128]{2,1,0:T(8,128)(2,1)S(1)}, u32[]{:S(2)}, u32[]{:S(2)}) collective-permute-start(bf16[2,256,128]{2,1,0:T(8,128)(2,1)} %bitcast.26), channel_id=1, source_target_pairs={{0,14},{1,15},{2,8},{3,9},{4,10},{5,11},{6,12},{7,13},{8,22},{9,23... | collective-permute-start | bytes 393224 | tf_op jit(solution)/shard_map/ppermute | solution.py:222
  57.8 5.5 %collective-permute-start.6 = (bf16[2,256,128]{2,1,0:T(8,128)(2,1)}, bf16[2,256,128]{2,1,0:T(8,128)(2,1)S(1)}, u32[]{:S(2)}, u32[]{:S(2)}) collective-permute-start(bf16[2,256,128]{2,1,0:T(8,128)(2,1)} %bitcast.25), channel_id=1, source_target_pairs={{0,9},{1,8},{2,11},{3,10},{4,13},{5,12},{6,15},{7,14},{8,17},{9,16... | collective-permute-start | bytes 393224 | tf_op jit(solution)/shard_map/ppermute | solution.py:222
  57.8 5.5 %collective-permute-start.7 = (bf16[2,256,128]{2,1,0:T(8,128)(2,1)}, bf16[2,256,128]{2,1,0:T(8,128)(2,1)S(1)}, u32[]{:S(2)}, u32[]{:S(2)}) collective-permute-start(bf16[2,256,128]{2,1,0:T(8,128)(2,1)} %bitcast.24), channel_id=1, source_target_pairs={{0,8},{1,9},{2,10},{3,11},{4,12},{5,13},{6,14},{7,15},{8,16},{9,17... | collective-permute-start | bytes 393224 | tf_op jit(solution)/shard_map/ppermute | solution.py:222
  63.3 1.1 copy-start.1
  84.8 13.3 %collective-permute-start.8 = (bf16[2,256,128]{2,1,0:T(8,128)(2,1)S(1)}, bf16[2,256,128]{2,1,0:T(8,128)(2,1)S(1)}, u32[]{:S(2)}, u32[]{:S(2)}) collective-permute-start(bf16[2,256,128]{2,1,0:T(8,128)(2,1)S(1)} %get-tuple-element.31), channel_id=1, source_target_pairs={{13,0},{12,1},{15,2},{14,3},{9,4},{8,5},{11,6},{10,7},{21,8},{20,9... | collective-permute-start | bytes 393224 | tf_op jit(solution)/shard_map/ppermute | solution.py:226
  88.7 14.9 %collective-permute-start.9 = (bf16[2,256,128]{2,1,0:T(8,128)(2,1)S(1)}, bf16[2,256,128]{2,1,0:T(8,128)(2,1)S(1)}, u32[]{:S(2)}, u32[]{:S(2)}) collective-permute-start(bf16[2,256,128]{2,1,0:T(8,128)(2,1)S(1)} %get-tuple-element.32), channel_id=1, source_target_pairs={{12,0},{13,1},{14,2},{15,3},{8,4},{9,5},{10,6},{11,7},{20,8},{21,9... | collective-permute-start | bytes 393224 | tf_op jit(solution)/shard_map/ppermute | solution.py:226
  90.2 17.8 %collective-permute-start.10 = (bf16[2,256,128]{2,1,0:T(8,128)(2,1)S(1)}, bf16[2,256,128]{2,1,0:T(8,128)(2,1)S(1)}, u32[]{:S(2)}, u32[]{:S(2)}) collective-permute-start(bf16[2,256,128]{2,1,0:T(8,128)(2,1)S(1)} %get-tuple-element.33), channel_id=1, source_target_pairs={{11,0},{10,1},{13,2},{12,3},{15,4},{14,5},{9,6},{8,7},{19,8},{18,9... | collective-permute-start | bytes 393224 | tf_op jit(solution)/shard_map/ppermute | solution.py:226
  90.7 18.2 %collective-permute-start.11 = (bf16[2,256,128]{2,1,0:T(8,128)(2,1)S(1)}, bf16[2,256,128]{2,1,0:T(8,128)(2,1)S(1)}, u32[]{:S(2)}, u32[]{:S(2)}) collective-permute-start(bf16[2,256,128]{2,1,0:T(8,128)(2,1)S(1)} %get-tuple-element.34), channel_id=1, source_target_pairs={{15,0},{14,1},{9,2},{8,3},{11,4},{10,5},{13,6},{12,7},{23,8},{22,9... | collective-permute-start | bytes 393224 | tf_op jit(solution)/shard_map/ppermute | solution.py:226
  92.4 16.9 %collective-permute-start.12 = (bf16[2,256,128]{2,1,0:T(8,128)(2,1)S(1)}, bf16[2,256,128]{2,1,0:T(8,128)(2,1)S(1)}, u32[]{:S(2)}, u32[]{:S(2)}) collective-permute-start(bf16[2,256,128]{2,1,0:T(8,128)(2,1)S(1)} %get-tuple-element.35), channel_id=1, source_target_pairs={{10,0},{11,1},{12,2},{13,3},{14,4},{15,5},{8,6},{9,7},{18,8},{19,9... | collective-permute-start | bytes 393224 | tf_op jit(solution)/shard_map/ppermute | solution.py:226
  98.2 13.7 %copy-start.2 = (bf16[2,256,128]{2,1,0:T(8,128)(2,1)}, bf16[2,256,128]{2,1,0:T(8,128)(2,1)S(1)}, u32[]{:S(2)}) copy-start(bf16[2,256,128]{2,1,0:T(8,128)(2,1)S(1)} %collective-permute-done.8) | copy-start | bytes 393220
  98.2 11.2 %collective-permute-start.13 = (bf16[2,256,128]{2,1,0:T(8,128)(2,1)S(1)}, bf16[2,256,128]{2,1,0:T(8,128)(2,1)S(1)}, u32[]{:S(2)}, u32[]{:S(2)}) collective-permute-start(bf16[2,256,128]{2,1,0:T(8,128)(2,1)S(1)} %get-tuple-element.36), channel_id=1, source_target_pairs={{14,0},{15,1},{8,2},{9,3},{10,4},{11,5},{12,6},{13,7},{22,8},{23,9... | collective-permute-start | bytes 393224 | tf_op jit(solution)/shard_map/ppermute | solution.py:226
  103.7 8.2 %copy-start.3 = (bf16[2,256,128]{2,1,0:T(8,128)(2,1)}, bf16[2,256,128]{2,1,0:T(8,128)(2,1)S(1)}, u32[]{:S(2)}) copy-start(bf16[2,256,128]{2,1,0:T(8,128)(2,1)S(1)} %collective-permute-done.9) | copy-start | bytes 393220
  103.7 6.9 %collective-permute-start.14 = (bf16[2,256,128]{2,1,0:T(8,128)(2,1)S(1)}, bf16[2,256,128]{2,1,0:T(8,128)(2,1)S(1)}, u32[]{:S(2)}, u32[]{:S(2)}) collective-permute-start(bf16[2,256,128]{2,1,0:T(8,128)(2,1)S(1)} %get-tuple-element.37), channel_id=1, source_target_pairs={{9,0},{8,1},{11,2},{10,3},{13,4},{12,5},{15,6},{14,7},{17,8},{16,9... | collective-permute-start | bytes 393224 | tf_op jit(solution)/shard_map/ppermute | solution.py:226
  108.0 3.9 %copy-start.4 = (bf16[2,256,128]{2,1,0:T(8,128)(2,1)}, bf16[2,256,128]{2,1,0:T(8,128)(2,1)S(1)}, u32[]{:S(2)}) copy-start(bf16[2,256,128]{2,1,0:T(8,128)(2,1)S(1)} %collective-permute-done.10) | copy-start | bytes 393220
  108.0 3.9 %collective-permute-start.15 = (bf16[2,256,128]{2,1,0:T(8,128)(2,1)S(1)}, bf16[2,256,128]{2,1,0:T(8,128)(2,1)S(1)}, u32[]{:S(2)}, u32[]{:S(2)}) collective-permute-start(bf16[2,256,128]{2,1,0:T(8,128)(2,1)S(1)} %get-tuple-element.38), channel_id=1, source_target_pairs={{8,0},{9,1},{10,2},{11,3},{12,4},{13,5},{14,6},{15,7},{16,8},{17,9... | collective-permute-start | bytes 393224 | tf_op jit(solution)/shard_map/ppermute | solution.py:226
  108.9 3.0 %copy-start.5 = (bf16[2,256,128]{2,1,0:T(8,128)(2,1)}, bf16[2,256,128]{2,1,0:T(8,128)(2,1)S(1)}, u32[]{:S(2)}) copy-start(bf16[2,256,128]{2,1,0:T(8,128)(2,1)S(1)} %collective-permute-done.11) | copy-start | bytes 393220
  109.3 2.6 %copy-start.6 = (bf16[2,256,128]{2,1,0:T(8,128)(2,1)}, bf16[2,256,128]{2,1,0:T(8,128)(2,1)S(1)}, u32[]{:S(2)}) copy-start(bf16[2,256,128]{2,1,0:T(8,128)(2,1)S(1)} %collective-permute-done.12) | copy-start | bytes 393220
  109.3 2.6 %copy-start.7 = (bf16[2,256,128]{2,1,0:T(8,128)(2,1)}, bf16[2,256,128]{2,1,0:T(8,128)(2,1)S(1)}, u32[]{:S(2)}) copy-start(bf16[2,256,128]{2,1,0:T(8,128)(2,1)S(1)} %collective-permute-done.13) | copy-start | bytes 393220
  110.5 1.4 copy-start.8
  111.9 0.7 copy-start.9

commit v3 on v2

--- a/solution.py
+++ b/solution.py
@@ -48,27 +48,19 @@
     _, rows, _, width = pairs.shape
     local = heads * HEAD
 
-    def kernel(pairs_ref, *refs):
-        outs, sem = refs[:-1], refs[-1]
-        copies = []
+    def kernel(pairs_ref, *outs):
         for i, offset in enumerate(order):
             base = group_at(offset) * local
             for h in range(heads):
                 column = pl.multiple_of(base + h * HEAD, HEAD)
-                copy = pltpu.make_async_copy(
-                    pairs_ref.at[0, :, :, pl.ds(column, HEAD)], outs[i].at[h], sem.at[i, h]
-                )
-                copy.start()
-                copies.append(copy)
-        for copy in copies:
-            copy.wait()
+                outs[i][h] = pairs_ref[0, :, :, pl.ds(column, HEAD)]
 
     return pl.pallas_call(
         kernel,
         out_shape=[jax.ShapeDtypeStruct((heads, rows, 2, HEAD), pairs.dtype)] * len(order),
-        in_specs=[pl.BlockSpec(memory_space=pl.ANY)],
-        out_specs=[pl.BlockSpec(memory_space=pl.ANY)] * len(order),
-        scratch_shapes=[pltpu.SemaphoreType.DMA((len(order), heads))],
+        in_specs=[pl.BlockSpec(memory_space=pltpu.VMEM)],
+        out_specs=[pl.BlockSpec(memory_space=pltpu.VMEM)] * len(order),
+        compiler_params=pltpu.CompilerParams(vmem_limit_bytes=32 * MIB),
         name="pack",
     )(pairs)
 
@@ -78,26 +70,19 @@
     local = heads * HEAD
 
     def kernel(*refs):
-        ins, out, sem = refs[: len(order)], refs[len(order)], refs[-1]
-        copies = []
+        ins, out = refs[: len(order)], refs[len(order)]
         for i, offset in enumerate(order):
             base = group_at(offset) * local
             for h in range(heads):
                 column = pl.multiple_of(base + h * HEAD, HEAD)
-                copy = pltpu.make_async_copy(
-                    ins[i].at[h], out.at[0, :, :, pl.ds(column, HEAD)], sem.at[i, h]
-                )
-                copy.start()
-                copies.append(copy)
-        for copy in copies:
-            copy.wait()
+                out[0, :, :, pl.ds(column, HEAD)] = ins[i][h]
 
     return pl.pallas_call(
         kernel,
         out_shape=jax.ShapeDtypeStruct((1, rows, 2, width), blocks[0].dtype),
-        in_specs=[pl.BlockSpec(memory_space=pl.ANY)] * len(order),
-        out_specs=pl.BlockSpec(memory_space=pl.ANY),
-        scratch_shapes=[pltpu.SemaphoreType.DMA((len(order), heads))],
+        in_specs=[pl.BlockSpec(memory_space=pltpu.VMEM)] * len(order),
+        out_specs=pl.BlockSpec(memory_space=pltpu.VMEM),
+        compiler_params=pltpu.CompilerParams(vmem_limit_bytes=32 * MIB),
         name="unpack",
     )(*blocks)
 

time: 146 us -> 82.3 us (0.56)
  Pallas kernels: 86.4 us -> 22.8 us
    pallas_call x1, Pallas kernels: 33 us -> 0.73 us  [pack(): pl.pallas_call(kernel, out_shape=[jax.ShapeDtypeStruct((heads, rows, 2, H...]
    pallas_call x1, Pallas kernels: 33 us -> 1.7 us  [unpack(): pl.pallas_call(kernel, out_shape=jax.ShapeDtypeStruct((1, rows, 2, width)...]
where the time goes in v3:
time: 82.3 us; the launch traced here: 81.8 us
  starting transfers between devices  30.5 us (37%)
  waiting for transfers between devices  25.4 us (31%)
  Pallas kernels  22.8 us (28%)
  local copies, waits for them, and re-layouts  2.36 us (3%)
    pallas_call x1, Pallas kernels, attend(): pl.pallas_call(functools.partial(attend_kernel, count, steps, sub), grid=...  20.4 us
    ppermute x8, starting transfers between devices, shards(): block = lax.ppermute(block, AXES, route(offset, True))  16.7 us
    ppermute x8, waiting for transfers between devices, shards(): arrived.append(lax.ppermute(block, AXES, route(offset, False)))  15.4 us
    ppermute x8, starting transfers between devices, shards(): arrived.append(lax.ppermute(block, AXES, route(offset, False)))  13.8 us
    ppermute x8, waiting for transfers between devices, shards(): block = lax.ppermute(block, AXES, route(offset, True))  10 us
    unnamed x6, local copies, waits for them, and re-layouts  2.36 us
    pallas_call x1, Pallas kernels, unpack(): pl.pallas_call(kernel, out_shape=jax.ShapeDtypeStruct((1, rows, 2, width)...  1.7 us
  transfers between devices with their start and end apart: 16, of which 9 were waited for; matrix products, arithmetic and copies ran while one was open for 0% of the time, Pallas kernels for 0%

profile of v3, /device:TPU:0, one launch (start us, length us, event | category | flops | bytes accessed | tf_op | source)
XLA Modules:
  0.0 81.8 jit_solution(397114440673329956)
XLA Ops:
  0.6 0.0 copy-start
  0.6 1.2 %copy-done = bf16[1,128,2,2048]{3,2,1,0:T(2,128)(2,1)S(1)} copy-done((bf16[1,128,2,2048]{3,2,1,0:T(2,128)(2,1)S(1)}, bf16[1,128,2,2048]{3,2,1,0:T(2,128)(2,1)}, u32[]{:S(2)}) %copy-start) | copy-done | bytes 1048600
  1.9 0.0 copy-start.1
  1.9 0.7 pack.1
  2.6 3.5 %collective-permute-start.1 = (bf16[2,256,128]{2,1,0:T(8,128)(2,1)S(1)}, bf16[2,256,128]{2,1,0:T(8,128)(2,1)S(1)}, u32[]{:S(2)}, u32[]{:S(2)}) collective-permute-start(bf16[2,256,128]{2,1,0:T(8,128)(2,1)S(1)} %bitcast.31), channel_id=1, source_target_pairs={{0,12},{1,13},{2,14},{3,15},{4,8},{5,9},{6,10},{7,11},{8,20},{9,21... | collective-permute-start | bytes 393224 | tf_op jit(solution)/shard_map/ppermute | solution.py:207
  6.1 2.5 %collective-permute-start = (bf16[2,256,128]{2,1,0:T(8,128)(2,1)S(1)}, bf16[2,256,128]{2,1,0:T(8,128)(2,1)S(1)}, u32[]{:S(2)}, u32[]{:S(2)}) collective-permute-start(bf16[2,256,128]{2,1,0:T(8,128)(2,1)S(1)} %bitcast.30), channel_id=1, source_target_pairs={{0,13},{1,12},{2,15},{3,14},{4,9},{5,8},{6,11},{7,10},{8,21},{9,20... | collective-permute-start | bytes 393224 | tf_op jit(solution)/shard_map/ppermute | solution.py:207
  8.6 1.2 %collective-permute-start.2 = (bf16[2,256,128]{2,1,0:T(8,128)(2,1)S(1)}, bf16[2,256,128]{2,1,0:T(8,128)(2,1)S(1)}, u32[]{:S(2)}, u32[]{:S(2)}) collective-permute-start(bf16[2,256,128]{2,1,0:T(8,128)(2,1)S(1)} %bitcast.29), channel_id=1, source_target_pairs={{0,11},{1,10},{2,13},{3,12},{4,15},{5,14},{6,9},{7,8},{8,19},{9,18... | collective-permute-start | bytes 393224 | tf_op jit(solution)/shard_map/ppermute | solution.py:207
  9.9 3.2 %collective-permute-start.3 = (bf16[2,256,128]{2,1,0:T(8,128)(2,1)S(1)}, bf16[2,256,128]{2,1,0:T(8,128)(2,1)S(1)}, u32[]{:S(2)}, u32[]{:S(2)}) collective-permute-start(bf16[2,256,128]{2,1,0:T(8,128)(2,1)S(1)} %bitcast.28), channel_id=1, source_target_pairs={{0,15},{1,14},{2,9},{3,8},{4,11},{5,10},{6,13},{7,12},{8,23},{9,22... | collective-permute-start | bytes 393224 | tf_op jit(solution)/shard_map/ppermute | solution.py:207
  13.0 0.0 collective-permute-start.4
  13.0 5.2 %collective-permute-done.1.refs_1_ = bf16[2,256,128]{2,1,0:T(8,128)(2,1)S(1)} collective-permute-done((bf16[2,256,128]{2,1,0:T(8,128)(2,1)S(1)}, bf16[2,256,128]{2,1,0:T(8,128)(2,1)S(1)}, u32[]{:S(2)}, u32[]{:S(2)}) %collective-permute-start.1) | collective-permute-done | bytes 131104 | tf_op jit(solution)/shard_map/ppermute | solution.py:207
  18.2 1.6 %collective-permute-start.5 = (bf16[2,256,128]{2,1,0:T(8,128)(2,1)S(1)}, bf16[2,256,128]{2,1,0:T(8,128)(2,1)S(1)}, u32[]{:S(2)}, u32[]{:S(2)}) collective-permute-start(bf16[2,256,128]{2,1,0:T(8,128)(2,1)S(1)} %bitcast.26), channel_id=1, source_target_pairs={{0,14},{1,15},{2,8},{3,9},{4,10},{5,11},{6,12},{7,13},{8,22},{9,23... | collective-permute-start | bytes 393224 | tf_op jit(solution)/shard_map/ppermute | solution.py:207
  19.8 6.7 %collective-permute-done.refs_0_ = bf16[2,256,128]{2,1,0:T(8,128)(2,1)S(1)} collective-permute-done((bf16[2,256,128]{2,1,0:T(8,128)(2,1)S(1)}, bf16[2,256,128]{2,1,0:T(8,128)(2,1)S(1)}, u32[]{:S(2)}, u32[]{:S(2)}) %collective-permute-start) | collective-permute-done | bytes 131104 | tf_op jit(solution)/shard_map/ppermute | solution.py:207
  26.5 0.0 collective-permute-start.6
  26.5 0.0 collective-permute-done.2.refs_2_
  26.5 1.8 %collective-permute-start.7 = (bf16[2,256,128]{2,1,0:T(8,128)(2,1)S(1)}, bf16[2,256,128]{2,1,0:T(8,128)(2,1)S(1)}, u32[]{:S(2)}, u32[]{:S(2)}) collective-permute-start(bf16[2,256,128]{2,1,0:T(8,128)(2,1)S(1)} %bitcast.24), channel_id=1, source_target_pairs={{0,8},{1,9},{2,10},{3,11},{4,12},{5,13},{6,14},{7,15},{8,16},{9,17... | collective-permute-start | bytes 393224 | tf_op jit(solution)/shard_map/ppermute | solution.py:207
  28.3 0.0 collective-permute-done.3.refs_3_
  28.3 0.0 collective-permute-done.4.refs_4_
  28.3 1.2 %collective-permute-done.5.refs_5_ = bf16[2,256,128]{2,1,0:T(8,128)(2,1)S(1)} collective-permute-done((bf16[2,256,128]{2,1,0:T(8,128)(2,1)S(1)}, bf16[2,256,128]{2,1,0:T(8,128)(2,1)S(1)}, u32[]{:S(2)}, u32[]{:S(2)}) %collective-permute-start.5) | collective-permute-done | bytes 131104 | tf_op jit(solution)/shard_map/ppermute | solution.py:207
  29.5 2.3 %collective-permute-done.6.refs_6_ = bf16[2,256,128]{2,1,0:T(8,128)(2,1)S(1)} collective-permute-done((bf16[2,256,128]{2,1,0:T(8,128)(2,1)S(1)}, bf16[2,256,128]{2,1,0:T(8,128)(2,1)S(1)}, u32[]{:S(2)}, u32[]{:S(2)}) %collective-permute-start.6) | collective-permute-done | bytes 131104 | tf_op jit(solution)/shard_map/ppermute | solution.py:207
  31.8 0.0 collective-permute-done.7.refs_7_
  31.8 0.0 copy-done.1
  31.8 0.0 copy-start.2
  31.8 1.1 %copy-done.2 = bf16[1,1536,256]{2,1,0:T(8,128)(2,1)S(1)} copy-done((bf16[1,1536,256]{2,1,0:T(8,128)(2,1)S(1)}, bf16[1,1536,256]{2,1,0:T(8,128)(2,1)}, u32[]{:S(2)}) %copy-start.2) | copy-done | bytes 786456
  33.0 20.4 %attend.1 = (bf16[1,1536,256]{2,1,0:T(8,128)(2,1)}, bf16[1,1536,256]{2,1,0:T(8,128)(2,1)}, bf16[2,256,128]{2,1,0:T(8,128)(2,1)S(1)}, bf16[2,256,128]{2,1,0:T(8,1...) custom-call(bf16[2,256,128]{2,1,0:T(8,128)(2,1)S(1)} %collective-per, ...), custom_call_target="tpu_custom_call" | custom-call | flops 4831838208 | bytes 5242880 | tf_op jit(solution)/shard_map/attend/pallas_call | solution.py:174
  53.4 3.8 %collective-permute-start.8 = (bf16[2,256,128]{2,1,0:T(8,128)(2,1)S(1)}, bf16[2,256,128]{2,1,0:T(8,128)(2,1)S(1)}, u32[]{:S(2)}, u32[]{:S(2)}) collective-permute-start(bf16[2,256,128]{2,1,0:T(8,128)(2,1)S(1)} %get-tuple-element.31), channel_id=1, source_target_pairs={{13,0},{12,1},{15,2},{14,3},{9,4},{8,5},{11,6},{10,7},{21,8},{20,9... | collective-permute-start | bytes 393224 | tf_op jit(solution)/shard_map/ppermute | solution.py:211
  57.1 1.5 %collective-permute-start.9 = (bf16[2,256,128]{2,1,0:T(8,128)(2,1)S(1)}, bf16[2,256,128]{2,1,0:T(8,128)(2,1)S(1)}, u32[]{:S(2)}, u32[]{:S(2)}) collective-permute-start(bf16[2,256,128]{2,1,0:T(8,128)(2,1)S(1)} %get-tuple-element.32), channel_id=1, source_target_pairs={{12,0},{13,1},{14,2},{15,3},{8,4},{9,5},{10,6},{11,7},{20,8},{21,9... | collective-permute-start | bytes 393224 | tf_op jit(solution)/shard_map/ppermute | solution.py:211
  58.7 0.4 collective-permute-start.10
  59.1 1.8 %collective-permute-start.11 = (bf16[2,256,128]{2,1,0:T(8,128)(2,1)S(1)}, bf16[2,256,128]{2,1,0:T(8,128)(2,1)S(1)}, u32[]{:S(2)}, u32[]{:S(2)}) collective-permute-start(bf16[2,256,128]{2,1,0:T(8,128)(2,1)S(1)} %get-tuple-element.34), channel_id=1, source_target_pairs={{15,0},{14,1},{9,2},{8,3},{11,4},{10,5},{13,6},{12,7},{23,8},{22,9... | collective-permute-start | bytes 393224 | tf_op jit(solution)/shard_map/ppermute | solution.py:211
  60.9 2.8 %collective-permute-start.12 = (bf16[2,256,128]{2,1,0:T(8,128)(2,1)S(1)}, bf16[2,256,128]{2,1,0:T(8,128)(2,1)S(1)}, u32[]{:S(2)}, u32[]{:S(2)}) collective-permute-start(bf16[2,256,128]{2,1,0:T(8,128)(2,1)S(1)} %get-tuple-element.35), channel_id=1, source_target_pairs={{10,0},{11,1},{12,2},{13,3},{14,4},{15,5},{8,6},{9,7},{18,8},{19,9... | collective-permute-start | bytes 393224 | tf_op jit(solution)/shard_map/ppermute | solution.py:211
  63.7 3.0 %collective-permute-done.8 = bf16[2,256,128]{2,1,0:T(8,128)(2,1)S(1)} collective-permute-done((bf16[2,256,128]{2,1,0:T(8,128)(2,1)S(1)}, bf16[2,256,128]{2,1,0:T(8,128)(2,1)S(1)}, u32[]{:S(2)}, u32[]{:S(2)}) %collective-permute-start.8) | collective-permute-done | bytes 131104 | tf_op jit(solution)/shard_map/ppermute | solution.py:211
  66.7 1.3 %collective-permute-start.13 = (bf16[2,256,128]{2,1,0:T(8,128)(2,1)S(1)}, bf16[2,256,128]{2,1,0:T(8,128)(2,1)S(1)}, u32[]{:S(2)}, u32[]{:S(2)}) collective-permute-start(bf16[2,256,128]{2,1,0:T(8,128)(2,1)S(1)} %get-tuple-element.36), channel_id=1, source_target_pairs={{14,0},{15,1},{8,2},{9,3},{10,4},{11,5},{12,6},{13,7},{22,8},{23,9... | collective-permute-start | bytes 393224 | tf_op jit(solution)/shard_map/ppermute | solution.py:211
  68.1 4.5 %collective-permute-done.9 = bf16[2,256,128]{2,1,0:T(8,128)(2,1)S(1)} collective-permute-done((bf16[2,256,128]{2,1,0:T(8,128)(2,1)S(1)}, bf16[2,256,128]{2,1,0:T(8,128)(2,1)S(1)}, u32[]{:S(2)}, u32[]{:S(2)}) %collective-permute-start.9) | collective-permute-done | bytes 131104 | tf_op jit(solution)/shard_map/ppermute | solution.py:211
  72.5 1.4 %collective-permute-start.14 = (bf16[2,256,128]{2,1,0:T(8,128)(2,1)S(1)}, bf16[2,256,128]{2,1,0:T(8,128)(2,1)S(1)}, u32[]{:S(2)}, u32[]{:S(2)}) collective-permute-start(bf16[2,256,128]{2,1,0:T(8,128)(2,1)S(1)} %get-tuple-element.37), channel_id=1, source_target_pairs={{9,0},{8,1},{11,2},{10,3},{13,4},{12,5},{15,6},{14,7},{17,8},{16,9... | collective-permute-start | bytes 393224 | tf_op jit(solution)/shard_map/ppermute | solution.py:211
  73.9 0.0 collective-permute-done.10
  73.9 3.7 %collective-permute-start.15 = (bf16[2,256,128]{2,1,0:T(8,128)(2,1)S(1)}, bf16[2,256,128]{2,1,0:T(8,128)(2,1)S(1)}, u32[]{:S(2)}, u32[]{:S(2)}) collective-permute-start(bf16[2,256,128]{2,1,0:T(8,128)(2,1)S(1)} %get-tuple-element.38), channel_id=1, source_target_pairs={{8,0},{9,1},{10,2},{11,3},{12,4},{13,5},{14,6},{15,7},{16,8},{17,9... | collective-permute-start | bytes 393224 | tf_op jit(solution)/shard_map/ppermute | solution.py:211
  77.6 0.0 collective-permute-done.11
  77.6 0.3 collective-permute-done.12
  77.9 0.0 collective-permute-done.13
  77.9 0.4 collective-permute-done.14
  78.3 1.8 %collective-permute-done.15 = bf16[2,256,128]{2,1,0:T(8,128)(2,1)S(1)} collective-permute-done((bf16[2,256,128]{2,1,0:T(8,128)(2,1)S(1)}, bf16[2,256,128]{2,1,0:T(8,128)(2,1)S(1)}, u32[]{:S(2)}, u32[]{:S(2)}) %collective-permute-start.15) | collective-permute-done | bytes 131104 | tf_op jit(solution)/shard_map/ppermute | solution.py:211
  80.1 1.7 %unpack.1 = bf16[1,128,2,2048]{3,2,1,0:T(2,128)(2,1)} custom-call(bf16[2,128,2,128]{3,2,1,0:T(2,128)(2,1)S(1)} %bitcast.16, bf16[2,128,2,128]{3,2,1,0:T(2,128)(2,1)S(1)} %bitcast.17, bf16[2,128,2,128]{3,2,1,0:T(2,128)(2,1)S(1)} %bitcast.18, bf16[2,128,2,128]{3,2,1,0:T(2,128)(2,1)S(1)} %bitcast.19, bf16[2,128,2,128]{3,2,1,0:T(2,128)(2,1)S(1)} %bitcast.20, ...), custom_call_target="tpu_custom_call" | custom-call | tf_op jit(solution)/shard_map/unpack/pallas_call | solution.py:80
Async XLA Ops:
  0.6 1.2 %copy-start = (bf16[1,128,2,2048]{3,2,1,0:T(2,128)(2,1)S(1)}, bf16[1,128,2,2048]{3,2,1,0:T(2,128)(2,1)}, u32[]{:S(2)}) copy-start(bf16[1,128,2,2048]{3,2,1,0:T(2,128)(2,1)} %pairs_ref.1) | copy-start | bytes 3145732
  1.9 30.0 %copy-start.1 = (bf16[1,1536,256]{2,1,0:T(8,128)(2,1)S(1)}, bf16[1,1536,256]{2,1,0:T(8,128)(2,1)}, u32[]{:S(2)}) copy-start(bf16[1,1536,256]{2,1,0:T(8,128)(2,1)} %refs_8_.1) | copy-start | bytes 2359300
  2.6 15.6 %collective-permute-start.1 = (bf16[2,256,128]{2,1,0:T(8,128)(2,1)S(1)}, bf16[2,256,128]{2,1,0:T(8,128)(2,1)S(1)}, u32[]{:S(2)}, u32[]{:S(2)}) collective-permute-start(bf16[2,256,128]{2,1,0:T(8,128)(2,1)S(1)} %bitcast.31), channel_id=1, source_target_pairs={{0,12},{1,13},{2,14},{3,15},{4,8},{5,9},{6,10},{7,11},{8,20},{9,21... | collective-permute-start | bytes 393224 | tf_op jit(solution)/shard_map/ppermute | solution.py:207
  6.1 20.4 %collective-permute-start = (bf16[2,256,128]{2,1,0:T(8,128)(2,1)S(1)}, bf16[2,256,128]{2,1,0:T(8,128)(2,1)S(1)}, u32[]{:S(2)}, u32[]{:S(2)}) collective-permute-start(bf16[2,256,128]{2,1,0:T(8,128)(2,1)S(1)} %bitcast.30), channel_id=1, source_target_pairs={{0,13},{1,12},{2,15},{3,14},{4,9},{5,8},{6,11},{7,10},{8,21},{9,20... | collective-permute-start | bytes 393224 | tf_op jit(solution)/shard_map/ppermute | solution.py:207
  8.6 17.9 %collective-permute-start.2 = (bf16[2,256,128]{2,1,0:T(8,128)(2,1)S(1)}, bf16[2,256,128]{2,1,0:T(8,128)(2,1)S(1)}, u32[]{:S(2)}, u32[]{:S(2)}) collective-permute-start(bf16[2,256,128]{2,1,0:T(8,128)(2,1)S(1)} %bitcast.29), channel_id=1, source_target_pairs={{0,11},{1,10},{2,13},{3,12},{4,15},{5,14},{6,9},{7,8},{8,19},{9,18... | collective-permute-start | bytes 393224 | tf_op jit(solution)/shard_map/ppermute | solution.py:207
  9.9 18.5 %collective-permute-start.3 = (bf16[2,256,128]{2,1,0:T(8,128)(2,1)S(1)}, bf16[2,256,128]{2,1,0:T(8,128)(2,1)S(1)}, u32[]{:S(2)}, u32[]{:S(2)}) collective-permute-start(bf16[2,256,128]{2,1,0:T(8,128)(2,1)S(1)} %bitcast.28), channel_id=1, source_target_pairs={{0,15},{1,14},{2,9},{3,8},{4,11},{5,10},{6,13},{7,12},{8,23},{9,22... | collective-permute-start | bytes 393224 | tf_op jit(solution)/shard_map/ppermute | solution.py:207
  13.0 15.3 %collective-permute-start.4 = (bf16[2,256,128]{2,1,0:T(8,128)(2,1)S(1)}, bf16[2,256,128]{2,1,0:T(8,128)(2,1)S(1)}, u32[]{:S(2)}, u32[]{:S(2)}) collective-permute-start(bf16[2,256,128]{2,1,0:T(8,128)(2,1)S(1)} %bitcast.27), channel_id=1, source_target_pairs={{0,10},{1,11},{2,12},{3,13},{4,14},{5,15},{6,8},{7,9},{8,18},{9,19... | collective-permute-start | bytes 393224 | tf_op jit(solution)/shard_map/ppermute | solution.py:207
  18.2 11.3 %collective-permute-start.5 = (bf16[2,256,128]{2,1,0:T(8,128)(2,1)S(1)}, bf16[2,256,128]{2,1,0:T(8,128)(2,1)S(1)}, u32[]{:S(2)}, u32[]{:S(2)}) collective-permute-start(bf16[2,256,128]{2,1,0:T(8,128)(2,1)S(1)} %bitcast.26), channel_id=1, source_target_pairs={{0,14},{1,15},{2,8},{3,9},{4,10},{5,11},{6,12},{7,13},{8,22},{9,23... | collective-permute-start | bytes 393224 | tf_op jit(solution)/shard_map/ppermute | solution.py:207
  26.5 5.3 %collective-permute-start.6 = (bf16[2,256,128]{2,1,0:T(8,128)(2,1)S(1)}, bf16[2,256,128]{2,1,0:T(8,128)(2,1)S(1)}, u32[]{:S(2)}, u32[]{:S(2)}) collective-permute-start(bf16[2,256,128]{2,1,0:T(8,128)(2,1)S(1)} %bitcast.25), channel_id=1, source_target_pairs={{0,9},{1,8},{2,11},{3,10},{4,13},{5,12},{6,15},{7,14},{8,17},{9,16... | collective-permute-start | bytes 393224 | tf_op jit(solution)/shard_map/ppermute | solution.py:207
  26.5 5.3 %collective-permute-start.7 = (bf16[2,256,128]{2,1,0:T(8,128)(2,1)S(1)}, bf16[2,256,128]{2,1,0:T(8,128)(2,1)S(1)}, u32[]{:S(2)}, u32[]{:S(2)}) collective-permute-start(bf16[2,256,128]{2,1,0:T(8,128)(2,1)S(1)} %bitcast.24), channel_id=1, source_target_pairs={{0,8},{1,9},{2,10},{3,11},{4,12},{5,13},{6,14},{7,15},{8,16},{9,17... | collective-permute-start | bytes 393224 | tf_op jit(solution)/shard_map/ppermute | solution.py:207
  31.8 1.1 %copy-start.2 = (bf16[1,1536,256]{2,1,0:T(8,128)(2,1)S(1)}, bf16[1,1536,256]{2,1,0:T(8,128)(2,1)}, u32[]{:S(2)}) copy-start(bf16[1,1536,256]{2,1,0:T(8,128)(2,1)} %refs_9_.1) | copy-start | bytes 2359300
  53.4 13.4 %collective-permute-start.8 = (bf16[2,256,128]{2,1,0:T(8,128)(2,1)S(1)}, bf16[2,256,128]{2,1,0:T(8,128)(2,1)S(1)}, u32[]{:S(2)}, u32[]{:S(2)}) collective-permute-start(bf16[2,256,128]{2,1,0:T(8,128)(2,1)S(1)} %get-tuple-element.31), channel_id=1, source_target_pairs={{13,0},{12,1},{15,2},{14,3},{9,4},{8,5},{11,6},{10,7},{21,8},{20,9... | collective-permute-start | bytes 393224 | tf_op jit(solution)/shard_map/ppermute | solution.py:211
  57.1 15.4 %collective-permute-start.9 = (bf16[2,256,128]{2,1,0:T(8,128)(2,1)S(1)}, bf16[2,256,128]{2,1,0:T(8,128)(2,1)S(1)}, u32[]{:S(2)}, u32[]{:S(2)}) collective-permute-start(bf16[2,256,128]{2,1,0:T(8,128)(2,1)S(1)} %get-tuple-element.32), channel_id=1, source_target_pairs={{12,0},{13,1},{14,2},{15,3},{8,4},{9,5},{10,6},{11,7},{20,8},{21,9... | collective-permute-start | bytes 393224 | tf_op jit(solution)/shard_map/ppermute | solution.py:211
  58.7 15.2 %collective-permute-start.10 = (bf16[2,256,128]{2,1,0:T(8,128)(2,1)S(1)}, bf16[2,256,128]{2,1,0:T(8,128)(2,1)S(1)}, u32[]{:S(2)}, u32[]{:S(2)}) collective-permute-start(bf16[2,256,128]{2,1,0:T(8,128)(2,1)S(1)} %get-tuple-element.33), channel_id=1, source_target_pairs={{11,0},{10,1},{13,2},{12,3},{15,4},{14,5},{9,6},{8,7},{19,8},{18,9... | collective-permute-start | bytes 393224 | tf_op jit(solution)/shard_map/ppermute | solution.py:211
  59.1 18.5 %collective-permute-start.11 = (bf16[2,256,128]{2,1,0:T(8,128)(2,1)S(1)}, bf16[2,256,128]{2,1,0:T(8,128)(2,1)S(1)}, u32[]{:S(2)}, u32[]{:S(2)}) collective-permute-start(bf16[2,256,128]{2,1,0:T(8,128)(2,1)S(1)} %get-tuple-element.34), channel_id=1, source_target_pairs={{15,0},{14,1},{9,2},{8,3},{11,4},{10,5},{13,6},{12,7},{23,8},{22,9... | collective-permute-start | bytes 393224 | tf_op jit(solution)/shard_map/ppermute | solution.py:211
  60.9 17.0 %collective-permute-start.12 = (bf16[2,256,128]{2,1,0:T(8,128)(2,1)S(1)}, bf16[2,256,128]{2,1,0:T(8,128)(2,1)S(1)}, u32[]{:S(2)}, u32[]{:S(2)}) collective-permute-start(bf16[2,256,128]{2,1,0:T(8,128)(2,1)S(1)} %get-tuple-element.35), channel_id=1, source_target_pairs={{10,0},{11,1},{12,2},{13,3},{14,4},{15,5},{8,6},{9,7},{18,8},{19,9... | collective-permute-start | bytes 393224 | tf_op jit(solution)/shard_map/ppermute | solution.py:211
  66.7 11.2 %collective-permute-start.13 = (bf16[2,256,128]{2,1,0:T(8,128)(2,1)S(1)}, bf16[2,256,128]{2,1,0:T(8,128)(2,1)S(1)}, u32[]{:S(2)}, u32[]{:S(2)}) collective-permute-start(bf16[2,256,128]{2,1,0:T(8,128)(2,1)S(1)} %get-tuple-element.36), channel_id=1, source_target_pairs={{14,0},{15,1},{8,2},{9,3},{10,4},{11,5},{12,6},{13,7},{22,8},{23,9... | collective-permute-start | bytes 393224 | tf_op jit(solution)/shard_map/ppermute | solution.py:211
  72.5 5.8 %collective-permute-start.14 = (bf16[2,256,128]{2,1,0:T(8,128)(2,1)S(1)}, bf16[2,256,128]{2,1,0:T(8,128)(2,1)S(1)}, u32[]{:S(2)}, u32[]{:S(2)}) collective-permute-start(bf16[2,256,128]{2,1,0:T(8,128)(2,1)S(1)} %get-tuple-element.37), channel_id=1, source_target_pairs={{9,0},{8,1},{11,2},{10,3},{13,4},{12,5},{15,6},{14,7},{17,8},{16,9... | collective-permute-start | bytes 393224 | tf_op jit(solution)/shard_map/ppermute | solution.py:211
  73.9 6.2 %collective-permute-start.15 = (bf16[2,256,128]{2,1,0:T(8,128)(2,1)S(1)}, bf16[2,256,128]{2,1,0:T(8,128)(2,1)S(1)}, u32[]{:S(2)}, u32[]{:S(2)}) collective-permute-start(bf16[2,256,128]{2,1,0:T(8,128)(2,1)S(1)} %get-tuple-element.38), channel_id=1, source_target_pairs={{8,0},{9,1},{10,2},{11,3},{12,4},{13,5},{14,6},{15,7},{16,8},{17,9... | collective-permute-start | bytes 393224 | tf_op jit(solution)/shard_map/ppermute | solution.py:211

commit v4 on v1

v4 whole, which is shorter than its diff:
```python
import functools

import jax
import jax.numpy as jnp
from jax import lax
from jax.experimental import pallas as pl
from jax.experimental.pallas import tpu as pltpu
from jax.sharding import PartitionSpec as P

HEAD = 128
AXES = ("segment", "seq", "tp")
FACTOR = HEAD**-0.5
EXPONENT = FACTOR * 1.4426950408889634
MIB = 1 << 20
NT = ((1,), (1,))
ANY = pl.BlockSpec(memory_space=pl.ANY)
VMEM = pl.BlockSpec(memory_space=pltpu.VMEM)


def offsets():
    seq_count = lax.axis_size("seq")
    tp_count = lax.axis_size("tp")
    near = [(0, dy) for dy in reversed(range(tp_count))]
    order = [(dz, dy) for dz in range(1, seq_count) for dy in reversed(range(tp_count))]
    order.sort(key=lambda o: -abs(o[0] - seq_count / 2))
    for i, offset in enumerate(near):
        order.insert(3 + 2 * i, offset)
    return order


def group_at(offset):
    seq_count = lax.axis_size("seq")
    tp_count = lax.axis_size("tp")
    z = lax.rem(lax.axis_index("seq") + offset[0], seq_count)
    y = lax.rem(lax.axis_index("tp") + offset[1], tp_count)
    return z * tp_count + y


def route(offset, back):
    segments, seq_count, tp_count = (lax.axis_size(a) for a in AXES)
    hops = []
    for s in range(segments):
        for z in range(seq_count):
            for y in range(tp_count):
                source = (s * seq_count + z) * tp_count + y
                s_to = (s + 1) % segments
                z_to = (z + offset[0]) % seq_count
                y_to = (y + offset[1]) % tp_count
                target = (s_to * seq_count + z_to) * tp_count + y_to
                hops.append((target, source) if back else (source, target))
    return hops


def params(enc_len):
    return pltpu.CompilerParams(vmem_limit_bytes=(12 + enc_len * 36 // 4096) * MIB)


def pack(pairs, order, heads):
    _, rows, _, width = pairs.shape
    local = heads * HEAD

    def kernel(pairs_ref, *outs):
        @pl.loop(0, rows // 16)
        def _(r):
            here = pl.ds(pl.multiple_of(r * 16, 16), 16)
            for i, offset in enumerate(order):
                base = group_at(offset) * local
                for h in range(heads):
                    column = pl.multiple_of(base + h * HEAD, HEAD)
                    outs[i][h, here] = pairs_ref[0, here, :, pl.ds(column, HEAD)]

    return pl.pallas_call(
        kernel,
        out_shape=[jax.ShapeDtypeStruct((heads, rows, 2, HEAD), pairs.dtype)] * len(order),
        in_specs=[VMEM],
        out_specs=[VMEM] * len(order),
        compiler_params=pltpu.CompilerParams(vmem_limit_bytes=24 * MIB),
        name="pack",
    )(pairs)


def unpack(blocks, order, width):
    heads, rows, _, _ = blocks[0].shape
    local = heads * HEAD

    def kernel(*refs):
        ins, out = refs[: len(order)], refs[len(order)]

        @pl.loop(0, rows // 16)
        def _(r):
            here = pl.ds(pl.multiple_of(r * 16, 16), 16)
            for i, offset in enumerate(order):
                base = group_at(offset) * local
                for h in range(heads):
                    column = pl.multiple_of(base + h * HEAD, HEAD)
                    out[0, here, :, pl.ds(column, HEAD)] = ins[i][h, here]

    return pl.pallas_call(
        kernel,
        out_shape=jax.ShapeDtypeStruct((1, rows, 2, width), blocks[0].dtype),
        in_specs=[VMEM] * len(order),
        out_specs=VMEM,
        compiler_params=pltpu.CompilerParams(vmem_limit_bytes=24 * MIB),
        name="unpack",
    )(*blocks)


def turned(rows):
    _, tokens, local = rows.shape
    heads = local // HEAD
    tile = 256 if tokens % 256 == 0 else tokens

    def kernel(rows_ref, out_ref):
        for h in range(heads):
            for j in range(tokens // tile):
                here = slice(j * tile, (j + 1) * tile)
                block = rows_ref[0, here, h * HEAD : (h + 1) * HEAD]
                out_ref[h, :, here] = block.astype(jnp.float32).T.astype(rows.dtype)

    return pl.pallas_call(
        kernel,
        out_shape=jax.ShapeDtypeStruct((heads, HEAD, tokens), rows.dtype),
        in_specs=[VMEM],
        out_specs=VMEM,
        compiler_params=pltpu.CompilerParams(vmem_limit_bytes=16 * MIB),
        name="turned",
    )(rows)


def dot(a, b, contract=((1,), (0,))):
    return lax.dot_general(a, b, (contract, ((), ())), preferred_element_type=jnp.float32)


def shuffle(rows, join):
    to = lax.broadcasted_iota(jnp.int32, (2 * rows, 2 * rows), 1 if join else 0)
    source = lax.broadcasted_iota(jnp.int32, (2 * rows, 2 * rows), 0 if join else 1)
    wanted = jnp.where(to < rows, 2 * to, 2 * (to - rows) + 1)
    return jnp.where(source == wanted, 1.0, 0.0).astype(jnp.bfloat16)


def split_chunks(chunks, h, rows, k_ref=None, v_ref=None, kt_ref=None, vt_ref=None):
    split = shuffle(rows, False)
    for i, chunk in enumerate(chunks):
        both = dot(split, chunk[h])
        here = slice(i * rows, (i + 1) * rows)
        keys, values = both[:rows], both[rows:]
        if k_ref is not None:
            k_ref[h, here, :] = keys.astype(jnp.bfloat16)
        if v_ref is not None:
            v_ref[h, here, :] = values.astype(jnp.bfloat16)
        if kt_ref is not None:
            kt_ref[h, :, here] = keys.T.astype(jnp.bfloat16)
        if vt_ref is not None:
            vt_ref[h, :HEAD, here] = values.T.astype(jnp.bfloat16)
    if vt_ref is not None:
        tail = (vt_ref.shape[1] - HEAD, vt_ref.shape[2])
        vt_ref[h, HEAD:, :] = jnp.ones(tail, jnp.bfloat16)


def join_chunks(outs, h, rows, gk_ref, gv_ref):
    join = shuffle(rows, True)
    for i, out in enumerate(outs):
        here = slice(i * rows, (i + 1) * rows)
        both = jnp.concatenate([gk_ref[h, here, :], gv_ref[h, here, :]], axis=0)
        out[h] = dot(join, both.astype(jnp.bfloat16)).astype(jnp.bfloat16)


def raise_scores(keys, qt, values_t, before):
    scores = dot(keys, qt)
    top = jnp.max(scores, axis=0, keepdims=True)
    if before is not None:
        top = jnp.maximum(top, before[0])
    raised = jnp.exp2((scores - top) * EXPONENT)
    low = raised.astype(jnp.bfloat16)
    summed = dot(values_t, low)
    total, context = summed[HEAD : HEAD + 1], summed[:HEAD]
    if before is not None:
        shrink = jnp.exp2((before[0] - top) * EXPONENT)
        total = total + before[1] * shrink
        context = context + before[2] * shrink
    return raised, low, top, total, context


def forward_kernel(count, first, tile, *refs):
    chunks, refs = refs[:count], refs[count:]
    qt_ref, refs = refs[0], refs[1:]
    if not first:
        stats_in, context_in, refs = refs[0], refs[1], refs[2:]
    stats_ref, context_ref, low_ref, k_ref, vt_ref = refs
    heads, pair_rows, _ = chunks[0].shape
    for h in range(heads):
        split_chunks(chunks, h, pair_rows // 2, k_ref=k_ref, vt_ref=vt_ref)

    @pl.loop(0, qt_ref.shape[2] // tile)
    def _(j):
        here = pl.ds(pl.multiple_of(j * tile, tile), tile)
        for h in range(heads):
            before = None
            if not first:
                before = (stats_in[h, 0:1, here], stats_in[h, 1:2, here], context_in[h, :, here])
            _, low, top, total, context = raise_scores(
                k_ref[h], qt_ref[h, :, here], vt_ref[h], before
            )
            low_ref[h, :, here] = low
            stats_ref[h, 0:1, here] = top
            stats_ref[h, 1:2, here] = total
            context_ref[h, :, here] = context


def gradients(raised, low, shrunk, stats, h, here, refs):
    qt_ref, gt_ref, v_ref, kt_ref, gk_ref, gv_ref = refs
    scale, row_dot = stats
    qt = qt_ref[h, :, here].astype(jnp.float32)
    gt = gt_ref[h, :, here]
    grad_weights = dot(v_ref[h], gt)
    grad_scores = (raised * (grad_weights - row_dot)).astype(jnp.bfloat16)
    scale = scale if shrunk is None else scale * shrunk
    grad_q = dot(kt_ref[h], grad_scores) * (scale * FACTOR)
    gk_ref[h] += dot(grad_scores, (qt * (scale * FACTOR)).astype(jnp.bfloat16), NT)
    gv_ref[h] += dot(low, (gt.astype(jnp.float32) * scale).astype(jnp.bfloat16), NT)
    return grad_q


def turn_kernel(count, tile, *refs):
    chunks, refs = refs[:count], refs[count:]
    qt_ref, gt_ref, stats_in, context_in = refs[:4]
    stats_ref, context_ref, grad_q_ref = refs[4:7]
    outs, refs = refs[7 : 7 + count], refs[7 + count :]
    k_ref, v_ref, kt_ref, vt_ref, gk_ref, gv_ref = refs
    heads, pair_rows, _ = chunks[0].shape
    rows = pair_rows // 2
    for h in range(heads):
        split_chunks(chunks, h, rows, k_ref, v_ref, kt_ref, vt_ref)
    gk_ref[...] = jnp.zeros_like(gk_ref)
    gv_ref[...] = jnp.zeros_like(gv_ref)

    @pl.loop(0, qt_ref.shape[2] // tile)
    def _(j):
        here = pl.ds(pl.multiple_of(j * tile, tile), tile)
        for h in range(heads):
            before = (stats_in[h, 0:1, here], stats_in[h, 1:2, here], context_in[h, :, here])
            raised, low, top, total, context = raise_scores(
                k_ref[h], qt_ref[h, :, here], vt_ref[h], before
            )
            scale = 1.0 / total
            context = context * scale
            row_dot = jnp.sum(
                gt_ref[h, :, here].astype(jnp.float32) * context, axis=0, keepdims=True
            )
            context_ref[h, :, here] = context
            stats_ref[h, 0:1, here] = top
            stats_ref[h, 1:2, here] = scale
            stats_ref[h, 2:3, here] = row_dot
            grad_q_ref[h, :, here] = gradients(
                raised,
                low,
                None,
                (scale, row_dot),
                h,
                here,
                (qt_ref, gt_ref, v_ref, kt_ref, gk_ref, gv_ref),
            )

    for h in range(heads):
        join_chunks(outs, h, rows, gk_ref, gv_ref)


def backward_kernel(back, count, ready, last, tile, *refs):
    chunks, refs = refs[back : back + count], refs[back + count :]
    qt_ref, gt_ref, low_ref, stats_then, stats_ref, grad_q_in = refs[:6]
    refs = refs[6:]
    if ready:
        ready_ref, refs = refs[0], refs[1:]
    if ready or last:
        rows_ref, refs = refs[0], refs[1:]
    if not last:
        grad_q_ref, refs = refs[0], refs[1:]
    outs, refs = refs[:count], refs[count:]
    v_ref, kt_ref, gk_ref, gv_ref = refs
    heads, pair_rows, _ = chunks[0].shape
    rows = pair_rows // 2
    for h in range(heads):
        split_chunks(chunks, h, rows, v_ref=v_ref, kt_ref=kt_ref)
    gk_ref[...] = jnp.zeros_like(gk_ref)
    gv_ref[...] = jnp.zeros_like(gv_ref)

    @pl.loop(0, qt_ref.shape[2] // tile)
    def _(j):
        here = pl.ds(pl.multiple_of(j * tile, tile), tile)
        for h in range(heads):
            columns = slice(h * HEAD, (h + 1) * HEAD)
            low = low_ref[h, :, here]
            top, scale, row_dot = (stats_ref[h, i : i + 1, here] for i in range(3))
            shrunk = jnp.exp2((stats_then[h, 0:1, here] - top) * EXPONENT)
            grad_q = grad_q_in[h, :, here] + gradients(
                low.astype(jnp.float32),
                low,
                shrunk,
                (scale, row_dot),
                h,
                here,
                (qt_ref, gt_ref, v_ref, kt_ref, gk_ref, gv_ref),
            )
            if last:
                rows_ref[0, here, columns] = grad_q.T.astype(rows_ref.dtype)
            else:
                grad_q_ref[h, :, here] = grad_q
            if ready:
                rows_ref[0, here, columns] = ready_ref[h, :, here].T.astype(rows_ref.dtype)

    for h in range(heads):
        join_chunks(outs, h, rows, gk_ref, gv_ref)


def cost(heads, rows, tokens, matmuls):
    return pl.CostEstimate(
        flops=2 * matmuls * heads * rows * tokens * HEAD,
        bytes_accessed=heads * (rows + tokens) * HEAD * 8,
        transcendentals=heads * rows * tokens,
    )


def attend(arrived, queries, upstream, send_back):
    heads, pair_rows, _ = arrived[0].shape
    rows = pair_rows // 2
    enc_len = len(arrived) * rows
    tokens = queries.shape[1]
    tile = 256 if tokens % 256 == 0 else tokens
    qt, gt = turned(queries), turned(upstream)
    stats_shape = jax.ShapeDtypeStruct((heads, 8, tokens), jnp.float32)
    wide_shape = jax.ShapeDtypeStruct((heads, HEAD, tokens), jnp.float32)
    rows_shape = jax.ShapeDtypeStruct(queries.shape, queries.dtype)
    compiler_params = params(enc_len)
    turn_at = len(arrived) - len(arrived) // 4
    half = (turn_at + 1) // 2

    def natural(count):
        return pltpu.VMEM((heads, count * rows, HEAD), jnp.bfloat16)

    def across(count, extra=0):
        return pltpu.VMEM((heads, HEAD + extra, count * rows), jnp.bfloat16)

    def sums(count):
        return pltpu.VMEM((heads, count * rows, HEAD), jnp.float32)

    def shapes_of(group):
        return [jax.ShapeDtypeStruct(c.shape, c.dtype) for c in group]

    state, parts = [], []
    for begin, end in ((0, half), (half, turn_at)):
        group, count = arrived[begin:end], end - begin
        low_shape = jax.ShapeDtypeStruct((heads, count * rows, tokens), jnp.bfloat16)
        stats, context, low = pl.pallas_call(
            functools.partial(forward_kernel, count, not state, tile),
            out_shape=[stats_shape, wide_shape, low_shape],
            in_specs=[VMEM] * (count + 1 + len(state)),
            out_specs=[VMEM] * 3,
            scratch_shapes=[natural(count), across(count, 16)],
            compiler_params=compiler_params,
            cost_estimate=cost(heads, count * rows, tokens, 2),
            name="forward",
        )(*group, qt, *state)
        state = [stats, context]
        parts.insert(0, (begin, count, low, stats))

    group, count = arrived[turn_at:], len(arrived) - turn_at
    final, context, grad_q, *grads = pl.pallas_call(
        functools.partial(turn_kernel, count, tile),
        out_shape=[stats_shape, wide_shape, wide_shape] + shapes_of(group),
        in_specs=[VMEM] * (count + 4),
        out_specs=[VMEM] * (count + 3),
        scratch_shapes=[natural(count), natural(count), across(count), across(count, 16)]
        + [sums(count)] * 2,
        compiler_params=compiler_params,
        cost_estimate=cost(heads, count * rows, tokens, 6),
        name="turn",
    )(*group, qt, gt, *state)
    returned = [send_back(turn_at, grads)]

    for i, (begin, count, low, then) in enumerate(parts):
        group = arrived[begin : begin + count]
        ready, last = i == 0, i == len(parts) - 1
        back = returned[i - 1] if i >= 1 else []
        extra = [rows_shape] * (ready or last) + [wide_shape] * (not last)
        outs = pl.pallas_call(
            functools.partial(backward_kernel, len(back), count, ready, last, tile),
            out_shape=extra + shapes_of(group),
            in_specs=[ANY] * len(back) + [VMEM] * (count + 6 + ready),
            out_specs=[VMEM] * (len(extra) + count),
            scratch_shapes=[natural(count), across(count)] + [sums(count)] * 2,
            compiler_params=compiler_params,
            cost_estimate=cost(heads, count * rows, tokens, 4),
            name="backward",
        )(*back, *group, qt, gt, low, then, final, grad_q, *([context] if ready else []))
        if ready:
            context_rows = outs[0]
        if last:
            grad_query = outs[0]
        else:
            grad_q = outs[len(extra) - 1]
        returned.append(send_back(begin, outs[len(extra) :]))
    return context_rows, grad_query, returned


def shards(pairs, queries, upstream):
    _, rows, _, width = pairs.shape
    heads = queries.shape[2] // HEAD
    order = offsets()
    arrived = []
    for offset, block in zip(order, pack(pairs, order, heads)):
        block = block.reshape(heads, 2 * rows, HEAD)
        arrived.append(lax.ppermute(block, AXES, route(offset, False)))
    homes = []

    def send_back(begin, blocks):
        there = order[begin : begin + len(blocks)]
        homes.extend(there)
        return [lax.ppermute(b, AXES, route(o, True)) for o, b in zip(there, blocks)]

    context, grad_query, parts = attend(arrived, queries, upstream, send_back)
    returned = [b.reshape(heads, rows, 2, HEAD) for part in parts for b in part]
    return context, grad_query, unpack(returned, homes, width)


def solution(mesh):
    return jax.shard_map(
        shards,
        mesh=mesh,
        in_specs=(
            P("segment", ("seq", "tp"), None, None),
            P("segment", None, ("seq", "tp")),
            P("segment", None, ("seq", "tp")),
        ),
        out_specs=(
            P("segment", None, ("seq", "tp")),
            P("segment", None, ("seq", "tp")),
            P("segment", ("seq", "tp"), None, None),
        ),
        check_vma=False,
    )
```

time: 157 us -> 79.6 us (0.51); the launches traced: 154 us -> 79.4 us
  local copies, waits for them, and re-layouts: 65.6 us -> 1.23 us
  matrix products: 37.1 us -> 0 us
  Pallas kernels: 0 us -> 36 us
  other arithmetic: 10.4 us -> 0 us
  starting transfers between devices: 27.2 us -> 31.2 us
  waiting for transfers between devices: 11.9 us -> 10.2 us
    pallas_call x0 -> x9, Pallas kernels: none -> 36 us  [the longest x2 13 us: attend(): pl.pallas_call(functools.partial(backward_kernel, len(back), count, ready...]
    dynamic_update_slice x11 -> x0, local copies, waits for them, and re-layouts: 30.5 us -> none  [the longest x8 26.5 us: shards(): lax.dynamic_update_index_in_dim(grad_pairs, block, group_at(offset), axis=2)]
    dot_general x15 -> x0, matrix products: 24.1 us -> none  [the longest x3 6.91 us: step(): jnp.einsum('hbs,bhd->shd', weights_low, grad_block, preferred_element_typ...]
    sub x3 -> x0, matrix products: 13.1 us -> none  [step(): raised = jnp.exp(scores - row_max)]
    dynamic_slice x7 -> x0, local copies, waits for them, and re-layouts: 9.25 us -> none  [the longest x6 6.81 us: attend(): lax.scan(step, (zeros_start, zeros_start), (query_blocks, grad_blocks))]
    convert_element_type x3 -> x0, other arithmetic: 8.6 us -> none  [step(): weights_low = weights.astype(jnp.bfloat16)]
    another operation x4 -> x0, local copies, waits for them, and re-layouts: 6.53 us -> none  [the longest x1 2.71 us: attend(): query_blocks = query_rows.reshape(count, block, num_heads, HEAD)]
    unnamed x22 -> x6, local copies, waits for them, and re-layouts: 6.32 us -> 1.23 us
  transfers between devices with their start and end apart: 16 -> 16, of which waited for: 7 -> 6; matrix products, arithmetic and copies ran while one was open for 11% -> 0% of each run, Pallas kernels for 0% -> 31%
where the time goes in v4:
time: 79.6 us; the launch traced here: 79.4 us
  Pallas kernels  36 us (45%)
  starting transfers between devices  31.2 us (39%)
  waiting for transfers between devices  10.2 us (13%)
  local copies, waits for them, and re-layouts  1.23 us (2%)
    ppermute x8, starting transfers between devices, shards(): arrived.append(lax.ppermute(block, AXES, route(offset, False)))  17.4 us
    ppermute x8, starting transfers between devices, send_back(): lax.ppermute(b, AXES, route(o, True))  13.9 us
    pallas_call x2, Pallas kernels, attend(): pl.pallas_call(functools.partial(backward_kernel, len(back), count, ready...  13 us
    pallas_call x2, Pallas kernels, attend(): pl.pallas_call(functools.partial(forward_kernel, count, not state, tile),...  11.1 us
    pallas_call x1, Pallas kernels, attend(): pl.pallas_call(functools.partial(turn_kernel, count, tile), out_shape=[st...  8.62 us
    ppermute x8, waiting for transfers between devices, send_back(): lax.ppermute(b, AXES, route(o, True))  7.11 us
    ppermute x8, waiting for transfers between devices, shards(): arrived.append(lax.ppermute(block, AXES, route(offset, False)))  3.04 us
    pallas_call x1, Pallas kernels, unpack(): pl.pallas_call(kernel, out_shape=jax.ShapeDtypeStruct((1, rows, 2, width)...  1.79 us
  transfers between devices with their start and end apart: 16, of which 6 were waited for; matrix products, arithmetic and copies ran while one was open for 0% of the time, Pallas kernels for 31%

profile of v4, /device:TPU:0, one launch (start us, length us, event | category | flops | bytes accessed | tf_op | source)
XLA Modules:
  0.0 79.4 jit_solution(17198427109795902346)
XLA Ops:
  0.6 0.0 copy-start
  0.6 1.2 %copy-done = bf16[1,128,2,2048]{3,2,1,0:T(2,128)(2,1)S(1)} copy-done((bf16[1,128,2,2048]{3,2,1,0:T(2,128)(2,1)S(1)}, bf16[1,128,2,2048]{3,2,1,0:T(2,128)(2,1)}, u32[]{:S(2)}) %copy-start) | copy-done | bytes 1048600
  1.9 0.0 copy-start.1
  1.9 0.0 copy-start.2
  1.9 1.0 %pack.1 = (bf16[2,128,2,128]{3,2,1,0:T(2,128)(2,1)S(1)}, bf16[2,128,2,128]{3,2,1,0:T(2,128)(2,1)S(1)}, bf16[2,128,2,128]{3,2,1,0:T(2,128)(2,1)S(1)}, bf16[2,128,...) custom-call(bf16[1,128,2,2048]{3,2,1,0:T(2,128)(2,1)S(1)} %copy-done), custom_call_target="tpu_custom_call" | custom-call | tf_op jit(solution)/shard_map/pack/pallas_call | solution.py:72
  2.8 3.5 %collective-permute-start.3 = (bf16[2,256,128]{2,1,0:T(8,128)(2,1)S(1)}, bf16[2,256,128]{2,1,0:T(8,128)(2,1)S(1)}, u32[]{:S(2)}, u32[]{:S(2)}) collective-permute-start(bf16[2,256,128]{2,1,0:T(8,128)(2,1)S(1)} %bitcast.31), channel_id=1, source_target_pairs={{0,11},{1,10},{2,13},{3,12},{4,15},{5,14},{6,9},{7,8},{8,19},{9,18... | collective-permute-start | bytes 393224 | tf_op jit(solution)/shard_map/ppermute | solution.py:412
  6.3 2.8 %collective-permute-start.4 = (bf16[2,256,128]{2,1,0:T(8,128)(2,1)S(1)}, bf16[2,256,128]{2,1,0:T(8,128)(2,1)S(1)}, u32[]{:S(2)}, u32[]{:S(2)}) collective-permute-start(bf16[2,256,128]{2,1,0:T(8,128)(2,1)S(1)} %bitcast.30), channel_id=1, source_target_pairs={{0,10},{1,11},{2,12},{3,13},{4,14},{5,15},{6,8},{7,9},{8,18},{9,19... | collective-permute-start | bytes 393224 | tf_op jit(solution)/shard_map/ppermute | solution.py:412
  9.1 1.6 %collective-permute-start.5 = (bf16[2,256,128]{2,1,0:T(8,128)(2,1)S(1)}, bf16[2,256,128]{2,1,0:T(8,128)(2,1)S(1)}, u32[]{:S(2)}, u32[]{:S(2)}) collective-permute-start(bf16[2,256,128]{2,1,0:T(8,128)(2,1)S(1)} %bitcast.29), channel_id=1, source_target_pairs={{0,15},{1,14},{2,9},{3,8},{4,11},{5,10},{6,13},{7,12},{8,23},{9,22... | collective-permute-start | bytes 393224 | tf_op jit(solution)/shard_map/ppermute | solution.py:412
  10.7 0.3 collective-permute-start.1
  11.1 1.7 %collective-permute-start = (bf16[2,256,128]{2,1,0:T(8,128)(2,1)S(1)}, bf16[2,256,128]{2,1,0:T(8,128)(2,1)S(1)}, u32[]{:S(2)}, u32[]{:S(2)}) collective-permute-start(bf16[2,256,128]{2,1,0:T(8,128)(2,1)S(1)} %bitcast.27), channel_id=1, source_target_pairs={{0,9},{1,8},{2,11},{3,10},{4,13},{5,12},{6,15},{7,14},{8,17},{9,16... | collective-permute-start | bytes 393224 | tf_op jit(solution)/shard_map/ppermute | solution.py:412
  12.7 0.4 collective-permute-done.3.refs_0_.refs_2_
  13.1 0.9 %collective-permute-start.2 = (bf16[2,256,128]{2,1,0:T(8,128)(2,1)S(1)}, bf16[2,256,128]{2,1,0:T(8,128)(2,1)S(1)}, u32[]{:S(2)}, u32[]{:S(2)}) collective-permute-start(bf16[2,256,128]{2,1,0:T(8,128)(2,1)S(1)} %bitcast.26), channel_id=1, source_target_pairs={{0,8},{1,9},{2,10},{3,11},{4,12},{5,13},{6,14},{7,15},{8,16},{9,17... | collective-permute-start | bytes 393224 | tf_op jit(solution)/shard_map/ppermute | solution.py:412
  14.0 2.7 %collective-permute-done.4.refs_1_.refs_3_ = bf16[2,256,128]{2,1,0:T(8,128)(2,1)S(1)} collective-permute-done((bf16[2,256,128]{2,1,0:T(8,128)(2,1)S(1)}, bf16[2,256,128]{2,1,0:T(8,128)(2,1)S(1)}, u32[]{:S(2)}, u32[]{:S(2)}) %collective-permute-start.4) | collective-permute-done | bytes 131104 | tf_op jit(solution)/shard_map/ppermute | solution.py:412
  16.7 5.1 %collective-permute-start.6 = (bf16[2,256,128]{2,1,0:T(8,128)(2,1)S(1)}, bf16[2,256,128]{2,1,0:T(8,128)(2,1)S(1)}, u32[]{:S(2)}, u32[]{:S(2)}) collective-permute-start(bf16[2,256,128]{2,1,0:T(8,128)(2,1)S(1)} %bitcast.25), channel_id=1, source_target_pairs={{0,13},{1,12},{2,15},{3,14},{4,9},{5,8},{6,11},{7,10},{8,21},{9,20... | collective-permute-start | bytes 393224 | tf_op jit(solution)/shard_map/ppermute | solution.py:412
  21.8 0.0 collective-permute-done.5.refs_2_.refs_4_
  21.8 1.5 %collective-permute-start.7 = (bf16[2,256,128]{2,1,0:T(8,128)(2,1)S(1)}, bf16[2,256,128]{2,1,0:T(8,128)(2,1)S(1)}, u32[]{:S(2)}, u32[]{:S(2)}) collective-permute-start(bf16[2,256,128]{2,1,0:T(8,128)(2,1)S(1)} %bitcast.24), channel_id=1, source_target_pairs={{0,12},{1,13},{2,14},{3,15},{4,8},{5,9},{6,10},{7,11},{8,20},{9,21... | collective-permute-start | bytes 393224 | tf_op jit(solution)/shard_map/ppermute | solution.py:412
  23.3 0.0 copy-done.1
  23.3 0.3 turned.2.refs_3_.refs_2_.refs_5_
  23.5 0.0 copy-done.2
  23.5 0.3 turned.3.refs_3_.refs_4_.refs_6_
  23.8 5.5 %forward.2 = (f32[2,8,1536]{2,1,0:T(8,128)S(1)}, f32[2,128,1536]{2,1,0:T(8,128)S(1)}, bf16[2,384,1536]{2,1,0:T(8,128)(2,1)S(1)}) custom-call(bf16[2,256,128]{2,1,0:T(8,128)(2,1)S(1)} %collective-permute-done.3.refs_0_.refs_2_, bf16[2,256,128]{2,1,0:T(8,128)(2,1)S(1)} %collective-permute-done.4.refs_1_.refs_3_, ...), custom_call_target="tpu_custom_call" | custom-call | flops 603979776 | bytes 3932160 | tf_op jit(solution)/shard_map/forward/pallas_call | solution.py:353
  29.3 0.0 collective-permute-done.1.refs_1_
  29.3 0.0 collective-permute-done.refs_0_
  29.4 0.0 collective-permute-done.2.refs_2_
  29.4 5.6 %forward.3 = (f32[2,8,1536]{2,1,0:T(8,128)S(1)}, f32[2,128,1536]{2,1,0:T(8,128)S(1)}, bf16[2,384,1536]{2,1,0:T(8,128)(2,1)S(1)}) custom-call(bf16[2,256,128]{2,1,0:T(8,128)(2,1)S(1)} %collective-permute-done.refs_0_, bf16[2,256,128]{2,1,0:T(8,128)(2,1)S(1)} %collective-permute-done.1.refs_1_, bf16[2,256,128]{2,1,0:T(8,128)(2,1)S(1)} %collective-permute-done.2.refs_2_, ...), custom_call_target="tpu_custom_call" | custom-call | flops 603979776 | bytes 3932160 | tf_op jit(solution)/shard_map/forward/pallas_call | solution.py:353
  34.9 0.0 collective-permute-done.6.refs_0_
  35.0 0.0 collective-permute-done.7.refs_1_
  35.0 8.6 %turn.1 = (f32[2,8,1536]{2,1,0:T(8,128)S(1)}, f32[2,128,1536]{2,1,0:T(8,128)S(1)}, f32[2,128,1536]{2,1,0:T(8,128)S(1)}, bf16[2,256,128]{2,1,0:T(8,128)(2,1)S(1)}, bf16[2,256,128]{2,1,0:T(8,128)(2,1)S(1)}) custom-call(bf16[2,256,128]{2,1,0:T(8,128)(2,1)S(1)} %collective-permute-done.6.refs_0_, bf16[2,256,128]{2,1,0:T(8,128)(2,1)S(1)} %collective-permute-done.7.refs_1_, ...), custom_call_target="tpu_custom_call" | custom-call | flops 1207959552 | bytes 3670016 | tf_op jit(solution)/shard_map/turn/pallas_call | solution.py:367
  43.6 4.5 %collective-permute-start.8 = (bf16[2,256,128]{2,1,0:T(8,128)(2,1)S(1)}, bf16[2,256,128]{2,1,0:T(8,128)(2,1)S(1)}, u32[]{:S(2)}, u32[]{:S(2)}) collective-permute-start(bf16[2,256,128]{2,1,0:T(8,128)(2,1)S(1)} %get-tuple-element.48), channel_id=1, source_target_pairs={{13,0},{12,1},{15,2},{14,3},{9,4},{8,5},{11,6},{10,7},{21,8},{20,9... | collective-permute-start | bytes 393224 | tf_op jit(solution)/shard_map/ppermute | solution.py:418
  48.1 1.1 %collective-permute-start.9 = (bf16[2,256,128]{2,1,0:T(8,128)(2,1)S(1)}, bf16[2,256,128]{2,1,0:T(8,128)(2,1)S(1)}, u32[]{:S(2)}, u32[]{:S(2)}) collective-permute-start(bf16[2,256,128]{2,1,0:T(8,128)(2,1)S(1)} %get-tuple-element.49), channel_id=1, source_target_pairs={{12,0},{13,1},{14,2},{15,3},{8,4},{9,5},{10,6},{11,7},{20,8},{21,9... | collective-permute-start | bytes 393224 | tf_op jit(solution)/shard_map/ppermute | solution.py:418
  49.2 6.5 %backward.2 = (bf16[1,1536,256]{2,1,0:T(8,128)(2,1)}, f32[2,128,1536]{2,1,0:T(8,128)S(1)}, bf16[2,256,128]{2,1,0:T(8,128)(2,1)S(1)}, bf16[2,256,128]{2,1,0:T(8,128)(2,1)S(1)}, bf16[2,256,128]{2,1,0:T(8,128)(2,1)S(1)}) custom-call(bf16[2,256,128]{2,1,0:T(8,128)(2,1)S(1)} %collective-permute-done.refs_0_, ...), custom_call_target="tpu_custom_call" | custom-call | flops 1207959552 | bytes 3932160 | tf_op jit(solution)/shard_map/backward/pallas_call | solution.py:385
  55.7 0.0 collective-permute-start.10
  55.7 0.3 collective-permute-start.11
  56.0 1.5 %collective-permute-start.12 = (bf16[2,256,128]{2,1,0:T(8,128)(2,1)S(1)}, bf16[2,256,128]{2,1,0:T(8,128)(2,1)S(1)}, u32[]{:S(2)}, u32[]{:S(2)}) collective-permute-start(bf16[2,256,128]{2,1,0:T(8,128)(2,1)S(1)} %get-tuple-element.55), channel_id=1, source_target_pairs={{8,0},{9,1},{10,2},{11,3},{12,4},{13,5},{14,6},{15,7},{16,8},{17,9... | collective-permute-start | bytes 393224 | tf_op jit(solution)/shard_map/ppermute | solution.py:418
  57.5 0.0 collective-permute-done.8.refs_0_
  57.5 0.5 collective-permute-done.9.refs_1_
  58.0 6.5 %backward.3 = (bf16[1,1536,256]{2,1,0:T(8,128)(2,1)}, bf16[2,256,128]{2,1,0:T(8,128)(2,1)S(1)}, bf16[2,256,128]{2,1,0:T(8,128)(2,1)S(1)}, bf16[2,256,128]{2,1,0:T(8,128)(2,1)S(1)}) custom-call(bf16[2,256,128]{2,1,0:T(8,128)(2,1)S(1)} %collective-permute-done.8.refs_0_, bf16[2,256,128]{2,1,0:T(8,128)(2,1)S(1)} %collective-permute-done.9.refs_1_, ...), custom_call_target="tpu_custom_call" | custom-call | flops 1207959552 | bytes 3932160 | tf_op jit(solution)/shard_map/backward/pallas_call | solution.py:385
  64.5 3.7 %collective-permute-start.13 = (bf16[2,256,128]{2,1,0:T(8,128)(2,1)S(1)}, bf16[2,256,128]{2,1,0:T(8,128)(2,1)S(1)}, u32[]{:S(2)}, u32[]{:S(2)}) collective-permute-start(bf16[2,256,128]{2,1,0:T(8,128)(2,1)S(1)} %get-tuple-element.56), channel_id=1, source_target_pairs={{11,0},{10,1},{13,2},{12,3},{15,4},{14,5},{9,6},{8,7},{19,8},{18,9... | collective-permute-start | bytes 393224 | tf_op jit(solution)/shard_map/ppermute | solution.py:418
  68.3 0.4 collective-permute-start.14
  68.7 0.0 collective-permute-done.10
  68.7 2.3 %collective-permute-start.15 = (bf16[2,256,128]{2,1,0:T(8,128)(2,1)S(1)}, bf16[2,256,128]{2,1,0:T(8,128)(2,1)S(1)}, u32[]{:S(2)}, u32[]{:S(2)}) collective-permute-start(bf16[2,256,128]{2,1,0:T(8,128)(2,1)S(1)} %get-tuple-element.58), channel_id=1, source_target_pairs={{15,0},{14,1},{9,2},{8,3},{11,4},{10,5},{13,6},{12,7},{23,8},{22,9... | collective-permute-start | bytes 393224 | tf_op jit(solution)/shard_map/ppermute | solution.py:418
  71.0 0.0 collective-permute-done.11
  71.0 0.0 collective-permute-done.12
  71.0 1.2 %collective-permute-done.13 = bf16[2,256,128]{2,1,0:T(8,128)(2,1)S(1)} collective-permute-done((bf16[2,256,128]{2,1,0:T(8,128)(2,1)S(1)}, bf16[2,256,128]{2,1,0:T(8,128)(2,1)S(1)}, u32[]{:S(2)}, u32[]{:S(2)}) %collective-permute-start.13) | collective-permute-done | bytes 131104 | tf_op jit(solution)/shard_map/ppermute | solution.py:418
  72.1 2.8 %collective-permute-done.14 = bf16[2,256,128]{2,1,0:T(8,128)(2,1)S(1)} collective-permute-done((bf16[2,256,128]{2,1,0:T(8,128)(2,1)S(1)}, bf16[2,256,128]{2,1,0:T(8,128)(2,1)S(1)}, u32[]{:S(2)}, u32[]{:S(2)}) %collective-permute-start.14) | collective-permute-done | bytes 131104 | tf_op jit(solution)/shard_map/ppermute | solution.py:418
  74.9 2.7 %collective-permute-done.15 = bf16[2,256,128]{2,1,0:T(8,128)(2,1)S(1)} collective-permute-done((bf16[2,256,128]{2,1,0:T(8,128)(2,1)S(1)}, bf16[2,256,128]{2,1,0:T(8,128)(2,1)S(1)}, u32[]{:S(2)}, u32[]{:S(2)}) %collective-permute-start.15) | collective-permute-done | bytes 131104 | tf_op jit(solution)/shard_map/ppermute | solution.py:418
  77.6 1.8 %unpack.1 = bf16[1,128,2,2048]{3,2,1,0:T(2,128)(2,1)} custom-call(bf16[2,128,2,128]{3,2,1,0:T(2,128)(2,1)S(1)} %bitcast.16, bf16[2,128,2,128]{3,2,1,0:T(2,128)(2,1)S(1)} %bitcast.17, bf16[2,128,2,128]{3,2,1,0:T(2,128)(2,1)S(1)} %bitcast.18, bf16[2,128,2,128]{3,2,1,0:T(2,128)(2,1)S(1)} %bitcast.19, bf16[2,128,2,128]{3,2,1,0:T(2,128)(2,1)S(1)} %bitcast.20, ...), custom_call_target="tpu_custom_call" | custom-call | tf_op jit(solution)/shard_map/unpack/pallas_call | solution.py:98
Async XLA Ops:
  0.6 1.2 %copy-start = (bf16[1,128,2,2048]{3,2,1,0:T(2,128)(2,1)S(1)}, bf16[1,128,2,2048]{3,2,1,0:T(2,128)(2,1)}, u32[]{:S(2)}) copy-start(bf16[1,128,2,2048]{3,2,1,0:T(2,128)(2,1)} %pairs_ref.1) | copy-start | bytes 3145732
  1.9 21.4 %copy-start.1 = (bf16[1,1536,256]{2,1,0:T(8,128)(2,1)S(1)}, bf16[1,1536,256]{2,1,0:T(8,128)(2,1)}, u32[]{:S(2)}) copy-start(bf16[1,1536,256]{2,1,0:T(8,128)(2,1)} %rows_ref.2) | copy-start | bytes 2359300
  1.9 21.7 %copy-start.2 = (bf16[1,1536,256]{2,1,0:T(8,128)(2,1)S(1)}, bf16[1,1536,256]{2,1,0:T(8,128)(2,1)}, u32[]{:S(2)}) copy-start(bf16[1,1536,256]{2,1,0:T(8,128)(2,1)} %rows_ref.3) | copy-start | bytes 2359300
  2.8 10.3 %collective-permute-start.3 = (bf16[2,256,128]{2,1,0:T(8,128)(2,1)S(1)}, bf16[2,256,128]{2,1,0:T(8,128)(2,1)S(1)}, u32[]{:S(2)}, u32[]{:S(2)}) collective-permute-start(bf16[2,256,128]{2,1,0:T(8,128)(2,1)S(1)} %bitcast.31), channel_id=1, source_target_pairs={{0,11},{1,10},{2,13},{3,12},{4,15},{5,14},{6,9},{7,8},{8,19},{9,18... | collective-permute-start | bytes 393224 | tf_op jit(solution)/shard_map/ppermute | solution.py:412
  6.3 10.3 %collective-permute-start.4 = (bf16[2,256,128]{2,1,0:T(8,128)(2,1)S(1)}, bf16[2,256,128]{2,1,0:T(8,128)(2,1)S(1)}, u32[]{:S(2)}, u32[]{:S(2)}) collective-permute-start(bf16[2,256,128]{2,1,0:T(8,128)(2,1)S(1)} %bitcast.30), channel_id=1, source_target_pairs={{0,10},{1,11},{2,12},{3,13},{4,14},{5,15},{6,8},{7,9},{8,18},{9,19... | collective-permute-start | bytes 393224 | tf_op jit(solution)/shard_map/ppermute | solution.py:412
  9.1 12.7 %collective-permute-start.5 = (bf16[2,256,128]{2,1,0:T(8,128)(2,1)S(1)}, bf16[2,256,128]{2,1,0:T(8,128)(2,1)S(1)}, u32[]{:S(2)}, u32[]{:S(2)}) collective-permute-start(bf16[2,256,128]{2,1,0:T(8,128)(2,1)S(1)} %bitcast.29), channel_id=1, source_target_pairs={{0,15},{1,14},{2,9},{3,8},{4,11},{5,10},{6,13},{7,12},{8,23},{9,22... | collective-permute-start | bytes 393224 | tf_op jit(solution)/shard_map/ppermute | solution.py:412
  10.7 18.6 %collective-permute-start.1 = (bf16[2,256,128]{2,1,0:T(8,128)(2,1)S(1)}, bf16[2,256,128]{2,1,0:T(8,128)(2,1)S(1)}, u32[]{:S(2)}, u32[]{:S(2)}) collective-permute-start(bf16[2,256,128]{2,1,0:T(8,128)(2,1)S(1)} %bitcast.28), channel_id=1, source_target_pairs={{0,14},{1,15},{2,8},{3,9},{4,10},{5,11},{6,12},{7,13},{8,22},{9,23... | collective-permute-start | bytes 393224 | tf_op jit(solution)/shard_map/ppermute | solution.py:412
  11.1 18.3 %collective-permute-start = (bf16[2,256,128]{2,1,0:T(8,128)(2,1)S(1)}, bf16[2,256,128]{2,1,0:T(8,128)(2,1)S(1)}, u32[]{:S(2)}, u32[]{:S(2)}) collective-permute-start(bf16[2,256,128]{2,1,0:T(8,128)(2,1)S(1)} %bitcast.27), channel_id=1, source_target_pairs={{0,9},{1,8},{2,11},{3,10},{4,13},{5,12},{6,15},{7,14},{8,17},{9,16... | collective-permute-start | bytes 393224 | tf_op jit(solution)/shard_map/ppermute | solution.py:412
  13.1 16.3 %collective-permute-start.2 = (bf16[2,256,128]{2,1,0:T(8,128)(2,1)S(1)}, bf16[2,256,128]{2,1,0:T(8,128)(2,1)S(1)}, u32[]{:S(2)}, u32[]{:S(2)}) collective-permute-start(bf16[2,256,128]{2,1,0:T(8,128)(2,1)S(1)} %bitcast.26), channel_id=1, source_target_pairs={{0,8},{1,9},{2,10},{3,11},{4,12},{5,13},{6,14},{7,15},{8,16},{9,17... | collective-permute-start | bytes 393224 | tf_op jit(solution)/shard_map/ppermute | solution.py:412
  16.7 18.3 %collective-permute-start.6 = (bf16[2,256,128]{2,1,0:T(8,128)(2,1)S(1)}, bf16[2,256,128]{2,1,0:T(8,128)(2,1)S(1)}, u32[]{:S(2)}, u32[]{:S(2)}) collective-permute-start(bf16[2,256,128]{2,1,0:T(8,128)(2,1)S(1)} %bitcast.25), channel_id=1, source_target_pairs={{0,13},{1,12},{2,15},{3,14},{4,9},{5,8},{6,11},{7,10},{8,21},{9,20... | collective-permute-start | bytes 393224 | tf_op jit(solution)/shard_map/ppermute | solution.py:412
  21.8 13.2 %collective-permute-start.7 = (bf16[2,256,128]{2,1,0:T(8,128)(2,1)S(1)}, bf16[2,256,128]{2,1,0:T(8,128)(2,1)S(1)}, u32[]{:S(2)}, u32[]{:S(2)}) collective-permute-start(bf16[2,256,128]{2,1,0:T(8,128)(2,1)S(1)} %bitcast.24), channel_id=1, source_target_pairs={{0,12},{1,13},{2,14},{3,15},{4,8},{5,9},{6,10},{7,11},{8,20},{9,21... | collective-permute-start | bytes 393224 | tf_op jit(solution)/shard_map/ppermute | solution.py:412
  43.6 13.9 %collective-permute-start.8 = (bf16[2,256,128]{2,1,0:T(8,128)(2,1)S(1)}, bf16[2,256,128]{2,1,0:T(8,128)(2,1)S(1)}, u32[]{:S(2)}, u32[]{:S(2)}) collective-permute-start(bf16[2,256,128]{2,1,0:T(8,128)(2,1)S(1)} %get-tuple-element.48), channel_id=1, source_target_pairs={{13,0},{12,1},{15,2},{14,3},{9,4},{8,5},{11,6},{10,7},{21,8},{20,9... | collective-permute-start | bytes 393224 | tf_op jit(solution)/shard_map/ppermute | solution.py:418
  48.1 9.9 %collective-permute-start.9 = (bf16[2,256,128]{2,1,0:T(8,128)(2,1)S(1)}, bf16[2,256,128]{2,1,0:T(8,128)(2,1)S(1)}, u32[]{:S(2)}, u32[]{:S(2)}) collective-permute-start(bf16[2,256,128]{2,1,0:T(8,128)(2,1)S(1)} %get-tuple-element.49), channel_id=1, source_target_pairs={{12,0},{13,1},{14,2},{15,3},{8,4},{9,5},{10,6},{11,7},{20,8},{21,9... | collective-permute-start | bytes 393224 | tf_op jit(solution)/shard_map/ppermute | solution.py:418
  55.7 13.0 %collective-permute-start.10 = (bf16[2,256,128]{2,1,0:T(8,128)(2,1)S(1)}, bf16[2,256,128]{2,1,0:T(8,128)(2,1)S(1)}, u32[]{:S(2)}, u32[]{:S(2)}) collective-permute-start(bf16[2,256,128]{2,1,0:T(8,128)(2,1)S(1)} %get-tuple-element.53), channel_id=1, source_target_pairs={{9,0},{8,1},{11,2},{10,3},{13,4},{12,5},{15,6},{14,7},{17,8},{16,9... | collective-permute-start | bytes 393224 | tf_op jit(solution)/shard_map/ppermute | solution.py:418
  55.7 15.3 %collective-permute-start.11 = (bf16[2,256,128]{2,1,0:T(8,128)(2,1)S(1)}, bf16[2,256,128]{2,1,0:T(8,128)(2,1)S(1)}, u32[]{:S(2)}, u32[]{:S(2)}) collective-permute-start(bf16[2,256,128]{2,1,0:T(8,128)(2,1)S(1)} %get-tuple-element.54), channel_id=1, source_target_pairs={{14,0},{15,1},{8,2},{9,3},{10,4},{11,5},{12,6},{13,7},{22,8},{23,9... | collective-permute-start | bytes 393224 | tf_op jit(solution)/shard_map/ppermute | solution.py:418
  56.0 15.0 %collective-permute-start.12 = (bf16[2,256,128]{2,1,0:T(8,128)(2,1)S(1)}, bf16[2,256,128]{2,1,0:T(8,128)(2,1)S(1)}, u32[]{:S(2)}, u32[]{:S(2)}) collective-permute-start(bf16[2,256,128]{2,1,0:T(8,128)(2,1)S(1)} %get-tuple-element.55), channel_id=1, source_target_pairs={{8,0},{9,1},{10,2},{11,3},{12,4},{13,5},{14,6},{15,7},{16,8},{17,9... | collective-permute-start | bytes 393224 | tf_op jit(solution)/shard_map/ppermute | solution.py:418
  64.5 7.6 %collective-permute-start.13 = (bf16[2,256,128]{2,1,0:T(8,128)(2,1)S(1)}, bf16[2,256,128]{2,1,0:T(8,128)(2,1)S(1)}, u32[]{:S(2)}, u32[]{:S(2)}) collective-permute-start(bf16[2,256,128]{2,1,0:T(8,128)(2,1)S(1)} %get-tuple-element.56), channel_id=1, source_target_pairs={{11,0},{10,1},{13,2},{12,3},{15,4},{14,5},{9,6},{8,7},{19,8},{18,9... | collective-permute-start | bytes 393224 | tf_op jit(solution)/shard_map/ppermute | solution.py:418
  68.3 6.7 %collective-permute-start.14 = (bf16[2,256,128]{2,1,0:T(8,128)(2,1)S(1)}, bf16[2,256,128]{2,1,0:T(8,128)(2,1)S(1)}, u32[]{:S(2)}, u32[]{:S(2)}) collective-permute-start(bf16[2,256,128]{2,1,0:T(8,128)(2,1)S(1)} %get-tuple-element.57), channel_id=1, source_target_pairs={{10,0},{11,1},{12,2},{13,3},{14,4},{15,5},{8,6},{9,7},{18,8},{19,9... | collective-permute-start | bytes 393224 | tf_op jit(solution)/shard_map/ppermute | solution.py:418
  68.7 8.9 %collective-permute-start.15 = (bf16[2,256,128]{2,1,0:T(8,128)(2,1)S(1)}, bf16[2,256,128]{2,1,0:T(8,128)(2,1)S(1)}, u32[]{:S(2)}, u32[]{:S(2)}) collective-permute-start(bf16[2,256,128]{2,1,0:T(8,128)(2,1)S(1)} %get-tuple-element.58), channel_id=1, source_target_pairs={{15,0},{14,1},{9,2},{8,3},{11,4},{10,5},{13,6},{12,7},{23,8},{22,9... | collective-permute-start | bytes 393224 | tf_op jit(solution)/shard_map/ppermute | solution.py:418

commit v5 on v4

--- a/solution.py
+++ b/solution.py
@@ -125,6 +125,28 @@
         compiler_params=pltpu.CompilerParams(vmem_limit_bytes=16 * MIB),
         name="turned",
     )(rows)
+
+
+def tiles(count):
+    def run(body):
+        if count <= 2:
+            for j in range(count):
+                body(j)
+        else:
+            pl.loop(0, count)(body)
+
+    return run
+
+
+def tokens_of(j, tile):
+    return pl.ds(j * tile if isinstance(j, int) else pl.multiple_of(j * tile, tile), tile)
+
+
+def tile_of(rows, tokens):
+    for parts in range(1, tokens // 256 + 1):
+        if tokens % (256 * parts) == 0 and rows * (tokens // parts) * 4 <= 5 * MIB // 4:
+            return tokens // parts
+    return 256 if tokens % 256 == 0 else tokens
 
 
 def dot(a, b, contract=((1,), (0,))):
@@ -191,9 +213,9 @@
     for h in range(heads):
         split_chunks(chunks, h, pair_rows // 2, k_ref=k_ref, vt_ref=vt_ref)
 
-    @pl.loop(0, qt_ref.shape[2] // tile)
+    @tiles(qt_ref.shape[2] // tile)
     def _(j):
-        here = pl.ds(pl.multiple_of(j * tile, tile), tile)
+        here = tokens_of(j, tile)
         for h in range(heads):
             before = None
             if not first:
@@ -234,9 +256,9 @@
     gk_ref[...] = jnp.zeros_like(gk_ref)
     gv_ref[...] = jnp.zeros_like(gv_ref)
 
-    @pl.loop(0, qt_ref.shape[2] // tile)
+    @tiles(qt_ref.shape[2] // tile)
     def _(j):
-        here = pl.ds(pl.multiple_of(j * tile, tile), tile)
+        here = tokens_of(j, tile)
         for h in range(heads):
             before = (stats_in[h, 0:1, here], stats_in[h, 1:2, here], context_in[h, :, here])
             raised, low, top, total, context = raise_scores(
@@ -284,9 +306,9 @@
     gk_ref[...] = jnp.zeros_like(gk_ref)
     gv_ref[...] = jnp.zeros_like(gv_ref)
 
-    @pl.loop(0, qt_ref.shape[2] // tile)
+    @tiles(qt_ref.shape[2] // tile)
     def _(j):
-        here = pl.ds(pl.multiple_of(j * tile, tile), tile)
+        here = tokens_of(j, tile)
         for h in range(heads):
             columns = slice(h * HEAD, (h + 1) * HEAD)
             low = low_ref[h, :, here]
@@ -325,7 +347,6 @@
     rows = pair_rows // 2
     enc_len = len(arrived) * rows
     tokens = queries.shape[1]
-    tile = 256 if tokens % 256 == 0 else tokens
     qt, gt = turned(queries), turned(upstream)
     stats_shape = jax.ShapeDtypeStruct((heads, 8, tokens), jnp.float32)
     wide_shape = jax.ShapeDtypeStruct((heads, HEAD, tokens), jnp.float32)
@@ -351,7 +372,7 @@
         group, count = arrived[begin:end], end - begin
         low_shape = jax.ShapeDtypeStruct((heads, count * rows, tokens), jnp.bfloat16)
         stats, context, low = pl.pallas_call(
-            functools.partial(forward_kernel, count, not state, tile),
+            functools.partial(forward_kernel, count, not state, tile_of(count * rows, tokens)),
             out_shape=[stats_shape, wide_shape, low_shape],
             in_specs=[VMEM] * (count + 1 + len(state)),
             out_specs=[VMEM] * 3,
@@ -365,7 +386,7 @@
 
     group, count = arrived[turn_at:], len(arrived) - turn_at
     final, context, grad_q, *grads = pl.pallas_call(
-        functools.partial(turn_kernel, count, tile),
+        functools.partial(turn_kernel, count, tile_of(count * rows, tokens)),
         out_shape=[stats_shape, wide_shape, wide_shape] + shapes_of(group),
         in_specs=[VMEM] * (count + 4),
         out_specs=[VMEM] * (count + 3),
@@ -383,7 +404,9 @@
         back = returned[i - 1] if i >= 1 else []
         extra = [rows_shape] * (ready or last) + [wide_shape] * (not last)
         outs = pl.pallas_call(
-            functools.partial(backward_kernel, len(back), count, ready, last, tile),
+            functools.partial(
+                backward_kernel, len(back), count, ready, last, tile_of(count * rows, tokens)
+            ),
             out_shape=extra + shapes_of(group),
             in_specs=[ANY] * len(back) + [VMEM] * (count + 6 + ready),
             out_specs=[VMEM] * (len(extra) + count),

time: 79.6 us -> 71.1 us (0.89)
  Pallas kernels: 36 us -> 20.3 us
  waiting for transfers between devices: 10.2 us -> 21.3 us
  starting transfers between devices: 31.2 us -> 26.9 us
    pallas_call x3, Pallas kernels: 19.7 us -> 9.09 us  [the longest x2 5.09 us: attend(): pl.pallas_call(functools.partial(forward_kernel, count, not state, tile_o...]
    ppermute x8, waiting for transfers between devices: 7.11 us -> 13.7 us  [send_back(): lax.ppermute(b, AXES, route(o, True))]
    pallas_call x2, Pallas kernels: 13 us -> 7.94 us  [attend(): pl.pallas_call(functools.partial(backward_kernel, len(back), count, ready...]
    ppermute x8, waiting for transfers between devices: 3.04 us -> 7.53 us  [shards(): arrived.append(lax.ppermute(block, AXES, route(offset, False)))]
    ppermute x8, starting transfers between devices: 13.9 us -> 9.5 us  [send_back(): lax.ppermute(b, AXES, route(o, True))]
  transfers between devices with their start and end apart: 16 -> 16, of which waited for: 6 -> 9; matrix products, arithmetic and copies ran while one was open for 0% -> 0% of each run, Pallas kernels for 31% -> 19%
where the time goes in v5:
time: 71.1 us; the launch traced here: 70.4 us
  starting transfers between devices  26.9 us (38%)
  waiting for transfers between devices  21.3 us (30%)
  Pallas kernels  20.3 us (29%)
  local copies, waits for them, and re-layouts  1.23 us (2%)
  between operations  0.74 us (1%)
    ppermute x8, starting transfers between devices, shards(): arrived.append(lax.ppermute(block, AXES, route(offset, False)))  17.4 us
    ppermute x8, waiting for transfers between devices, send_back(): lax.ppermute(b, AXES, route(o, True))  13.7 us
    ppermute x8, starting transfers between devices, send_back(): lax.ppermute(b, AXES, route(o, True))  9.5 us
    pallas_call x2, Pallas kernels, attend(): pl.pallas_call(functools.partial(backward_kernel, len(back), count, ready...  7.94 us
    ppermute x8, waiting for transfers between devices, shards(): arrived.append(lax.ppermute(block, AXES, route(offset, False)))  7.53 us
    pallas_call x2, Pallas kernels, attend(): pl.pallas_call(functools.partial(forward_kernel, count, not state, tile_o...  5.09 us
    pallas_call x1, Pallas kernels, attend(): pl.pallas_call(functools.partial(turn_kernel, count, tile_of(count * rows...  4 us
    pallas_call x1, Pallas kernels, unpack(): pl.pallas_call(kernel, out_shape=jax.ShapeDtypeStruct((1, rows, 2, width)...  1.79 us
  transfers between devices with their start and end apart: 16, of which 9 were waited for; matrix products, arithmetic and copies ran while one was open for 0% of the time, Pallas kernels for 19%

profile of v5, /device:TPU:0, one launch (start us, length us, event | category | flops | bytes accessed | tf_op | source)
XLA Modules:
  0.0 70.4 jit_solution(6834604878575545492)
XLA Ops:
  0.6 0.0 copy-start
  0.6 1.2 %copy-done = bf16[1,128,2,2048]{3,2,1,0:T(2,128)(2,1)S(1)} copy-done((bf16[1,128,2,2048]{3,2,1,0:T(2,128)(2,1)S(1)}, bf16[1,128,2,2048]{3,2,1,0:T(2,128)(2,1)}, u32[]{:S(2)}) %copy-start) | copy-done | bytes 1048600
  1.9 0.0 copy-start.1
  1.9 0.0 copy-start.2
  1.9 1.0 %pack.1 = (bf16[2,128,2,128]{3,2,1,0:T(2,128)(2,1)S(1)}, bf16[2,128,2,128]{3,2,1,0:T(2,128)(2,1)S(1)}, bf16[2,128,2,128]{3,2,1,0:T(2,128)(2,1)S(1)}, bf16[2,128,...) custom-call(bf16[1,128,2,2048]{3,2,1,0:T(2,128)(2,1)S(1)} %copy-done), custom_call_target="tpu_custom_call" | custom-call | tf_op jit(solution)/shard_map/pack/pallas_call | solution.py:72
  2.8 3.5 %collective-permute-start.3 = (bf16[2,256,128]{2,1,0:T(8,128)(2,1)S(1)}, bf16[2,256,128]{2,1,0:T(8,128)(2,1)S(1)}, u32[]{:S(2)}, u32[]{:S(2)}) collective-permute-start(bf16[2,256,128]{2,1,0:T(8,128)(2,1)S(1)} %bitcast.31), channel_id=1, source_target_pairs={{0,11},{1,10},{2,13},{3,12},{4,15},{5,14},{6,9},{7,8},{8,19},{9,18... | collective-permute-start | bytes 393224 | tf_op jit(solution)/shard_map/ppermute | solution.py:435
  6.3 2.8 %collective-permute-start.4 = (bf16[2,256,128]{2,1,0:T(8,128)(2,1)S(1)}, bf16[2,256,128]{2,1,0:T(8,128)(2,1)S(1)}, u32[]{:S(2)}, u32[]{:S(2)}) collective-permute-start(bf16[2,256,128]{2,1,0:T(8,128)(2,1)S(1)} %bitcast.30), channel_id=1, source_target_pairs={{0,10},{1,11},{2,12},{3,13},{4,14},{5,15},{6,8},{7,9},{8,18},{9,19... | collective-permute-start | bytes 393224 | tf_op jit(solution)/shard_map/ppermute | solution.py:435
  9.1 1.6 %collective-permute-start.5 = (bf16[2,256,128]{2,1,0:T(8,128)(2,1)S(1)}, bf16[2,256,128]{2,1,0:T(8,128)(2,1)S(1)}, u32[]{:S(2)}, u32[]{:S(2)}) collective-permute-start(bf16[2,256,128]{2,1,0:T(8,128)(2,1)S(1)} %bitcast.29), channel_id=1, source_target_pairs={{0,15},{1,14},{2,9},{3,8},{4,11},{5,10},{6,13},{7,12},{8,23},{9,22... | collective-permute-start | bytes 393224 | tf_op jit(solution)/shard_map/ppermute | solution.py:435
  10.7 0.3 collective-permute-start.1
  11.1 1.7 %collective-permute-start = (bf16[2,256,128]{2,1,0:T(8,128)(2,1)S(1)}, bf16[2,256,128]{2,1,0:T(8,128)(2,1)S(1)}, u32[]{:S(2)}, u32[]{:S(2)}) collective-permute-start(bf16[2,256,128]{2,1,0:T(8,128)(2,1)S(1)} %bitcast.27), channel_id=1, source_target_pairs={{0,9},{1,8},{2,11},{3,10},{4,13},{5,12},{6,15},{7,14},{8,17},{9,16... | collective-permute-start | bytes 393224 | tf_op jit(solution)/shard_map/ppermute | solution.py:435
  12.7 0.4 collective-permute-done.3.refs_0_.refs_2_
  13.1 0.9 %collective-permute-start.2 = (bf16[2,256,128]{2,1,0:T(8,128)(2,1)S(1)}, bf16[2,256,128]{2,1,0:T(8,128)(2,1)S(1)}, u32[]{:S(2)}, u32[]{:S(2)}) collective-permute-start(bf16[2,256,128]{2,1,0:T(8,128)(2,1)S(1)} %bitcast.26), channel_id=1, source_target_pairs={{0,8},{1,9},{2,10},{3,11},{4,12},{5,13},{6,14},{7,15},{8,16},{9,17... | collective-permute-start | bytes 393224 | tf_op jit(solution)/shard_map/ppermute | solution.py:435
  14.0 2.7 %collective-permute-done.4.refs_1_.refs_3_ = bf16[2,256,128]{2,1,0:T(8,128)(2,1)S(1)} collective-permute-done((bf16[2,256,128]{2,1,0:T(8,128)(2,1)S(1)}, bf16[2,256,128]{2,1,0:T(8,128)(2,1)S(1)}, u32[]{:S(2)}, u32[]{:S(2)}) %collective-permute-start.4) | collective-permute-done | bytes 131104 | tf_op jit(solution)/shard_map/ppermute | solution.py:435
  16.7 5.1 %collective-permute-start.6 = (bf16[2,256,128]{2,1,0:T(8,128)(2,1)S(1)}, bf16[2,256,128]{2,1,0:T(8,128)(2,1)S(1)}, u32[]{:S(2)}, u32[]{:S(2)}) collective-permute-start(bf16[2,256,128]{2,1,0:T(8,128)(2,1)S(1)} %bitcast.25), channel_id=1, source_target_pairs={{0,13},{1,12},{2,15},{3,14},{4,9},{5,8},{6,11},{7,10},{8,21},{9,20... | collective-permute-start | bytes 393224 | tf_op jit(solution)/shard_map/ppermute | solution.py:435
  21.8 0.0 collective-permute-done.5.refs_2_.refs_4_
  21.8 1.5 %collective-permute-start.7 = (bf16[2,256,128]{2,1,0:T(8,128)(2,1)S(1)}, bf16[2,256,128]{2,1,0:T(8,128)(2,1)S(1)}, u32[]{:S(2)}, u32[]{:S(2)}) collective-permute-start(bf16[2,256,128]{2,1,0:T(8,128)(2,1)S(1)} %bitcast.24), channel_id=1, source_target_pairs={{0,12},{1,13},{2,14},{3,15},{4,8},{5,9},{6,10},{7,11},{8,20},{9,21... | collective-permute-start | bytes 393224 | tf_op jit(solution)/shard_map/ppermute | solution.py:435
  23.3 0.0 copy-done.1
  23.3 0.3 turned.2.refs_3_.refs_2_.refs_5_
  23.5 0.0 copy-done.2
  23.5 0.3 turned.3.refs_3_.refs_4_.refs_6_
  23.8 2.6 %forward.2 = (f32[2,8,1536]{2,1,0:T(8,128)S(1)}, f32[2,128,1536]{2,1,0:T(8,128)S(1)}, bf16[2,384,1536]{2,1,0:T(8,128)(2,1)S(1)}) custom-call(bf16[2,256,128]{2,1,0:T(8,128)(2,1)S(1)} %collective-permute-done.3.refs_0_.refs_2_, bf16[2,256,128]{2,1,0:T(8,128)(2,1)S(1)} %collective-permute-done.4.refs_1_.refs_3_, ...), custom_call_target="tpu_custom_call" | custom-call | flops 603979776 | bytes 3932160 | tf_op jit(solution)/shard_map/forward/pallas_call | solution.py:374
  26.4 0.0 collective-permute-done.1.refs_1_
  26.4 0.0 collective-permute-done.refs_0_
  26.4 0.0 collective-permute-done.2.refs_2_
  26.4 2.5 %forward.3 = (f32[2,8,1536]{2,1,0:T(8,128)S(1)}, f32[2,128,1536]{2,1,0:T(8,128)S(1)}, bf16[2,384,1536]{2,1,0:T(8,128)(2,1)S(1)}) custom-call(bf16[2,256,128]{2,1,0:T(8,128)(2,1)S(1)} %collective-permute-done.refs_0_, bf16[2,256,128]{2,1,0:T(8,128)(2,1)S(1)} %collective-permute-done.1.refs_1_, bf16[2,256,128]{2,1,0:T(8,128)(2,1)S(1)} %collective-permute-done.2.refs_2_, ...), custom_call_target="tpu_custom_call" | custom-call | flops 603979776 | bytes 3932160 | tf_op jit(solution)/shard_map/forward/pallas_call | solution.py:374
  29.0 1.0 %collective-permute-done.6.refs_0_ = bf16[2,256,128]{2,1,0:T(8,128)(2,1)S(1)} collective-permute-done((bf16[2,256,128]{2,1,0:T(8,128)(2,1)S(1)}, bf16[2,256,128]{2,1,0:T(8,128)(2,1)S(1)}, u32[]{:S(2)}, u32[]{:S(2)}) %collective-permute-start.6) | collective-permute-done | bytes 131104 | tf_op jit(solution)/shard_map/ppermute | solution.py:435
  29.9 3.5 %collective-permute-done.7.refs_1_ = bf16[2,256,128]{2,1,0:T(8,128)(2,1)S(1)} collective-permute-done((bf16[2,256,128]{2,1,0:T(8,128)(2,1)S(1)}, bf16[2,256,128]{2,1,0:T(8,128)(2,1)S(1)}, u32[]{:S(2)}, u32[]{:S(2)}) %collective-permute-start.7) | collective-permute-done | bytes 131104 | tf_op jit(solution)/shard_map/ppermute | solution.py:435
  33.5 4.0 %turn.1 = (f32[2,8,1536]{2,1,0:T(8,128)S(1)}, f32[2,128,1536]{2,1,0:T(8,128)S(1)}, f32[2,128,1536]{2,1,0:T(8,128)S(1)}, bf16[2,256,128]{2,1,0:T(8,128)(2,1)S(1)}, bf16[2,256,128]{2,1,0:T(8,128)(2,1)S(1)}) custom-call(bf16[2,256,128]{2,1,0:T(8,128)(2,1)S(1)} %collective-permute-done.6.refs_0_, bf16[2,256,128]{2,1,0:T(8,128)(2,1)S(1)} %collective-permute-done.7.refs_1_, ...), custom_call_target="tpu_custom_call" | custom-call | flops 1207959552 | bytes 3670016 | tf_op jit(solution)/shard_map/turn/pallas_call | solution.py:388
  37.5 0.1 collective-permute-start.8
  37.5 3.0 %collective-permute-start.9 = (bf16[2,256,128]{2,1,0:T(8,128)(2,1)S(1)}, bf16[2,256,128]{2,1,0:T(8,128)(2,1)S(1)}, u32[]{:S(2)}, u32[]{:S(2)}) collective-permute-start(bf16[2,256,128]{2,1,0:T(8,128)(2,1)S(1)} %get-tuple-element.49), channel_id=1, source_target_pairs={{12,0},{13,1},{14,2},{15,3},{8,4},{9,5},{10,6},{11,7},{20,8},{21,9... | collective-permute-start | bytes 393224 | tf_op jit(solution)/shard_map/ppermute | solution.py:441
  40.5 4.0 %backward.2 = (bf16[1,1536,256]{2,1,0:T(8,128)(2,1)}, f32[2,128,1536]{2,1,0:T(8,128)S(1)}, bf16[2,256,128]{2,1,0:T(8,128)(2,1)S(1)}, bf16[2,256,128]{2,1,0:T(8,128)(2,1)S(1)}, bf16[2,256,128]{2,1,0:T(8,128)(2,1)S(1)}) custom-call(bf16[2,256,128]{2,1,0:T(8,128)(2,1)S(1)} %collective-permute-done.refs_0_, ...), custom_call_target="tpu_custom_call" | custom-call | flops 1207959552 | bytes 3932160 | tf_op jit(solution)/shard_map/backward/pallas_call | solution.py:406
  44.5 0.0 collective-permute-start.10
  44.5 0.0 collective-permute-start.11
  44.5 3.3 %collective-permute-start.12 = (bf16[2,256,128]{2,1,0:T(8,128)(2,1)S(1)}, bf16[2,256,128]{2,1,0:T(8,128)(2,1)S(1)}, u32[]{:S(2)}, u32[]{:S(2)}) collective-permute-start(bf16[2,256,128]{2,1,0:T(8,128)(2,1)S(1)} %get-tuple-element.55), channel_id=1, source_target_pairs={{8,0},{9,1},{10,2},{11,3},{12,4},{13,5},{14,6},{15,7},{16,8},{17,9... | collective-permute-start | bytes 393224 | tf_op jit(solution)/shard_map/ppermute | solution.py:441
  47.9 1.3 %collective-permute-done.8.refs_0_ = bf16[2,256,128]{2,1,0:T(8,128)(2,1)S(1)} collective-permute-done((bf16[2,256,128]{2,1,0:T(8,128)(2,1)S(1)}, bf16[2,256,128]{2,1,0:T(8,128)(2,1)S(1)}, u32[]{:S(2)}, u32[]{:S(2)}) %collective-permute-start.8) | collective-permute-done | bytes 131104 | tf_op jit(solution)/shard_map/ppermute | solution.py:441
  49.2 5.0 %collective-permute-done.9.refs_1_ = bf16[2,256,128]{2,1,0:T(8,128)(2,1)S(1)} collective-permute-done((bf16[2,256,128]{2,1,0:T(8,128)(2,1)S(1)}, bf16[2,256,128]{2,1,0:T(8,128)(2,1)S(1)}, u32[]{:S(2)}, u32[]{:S(2)}) %collective-permute-start.9) | collective-permute-done | bytes 131104 | tf_op jit(solution)/shard_map/ppermute | solution.py:441
  54.2 3.9 %backward.3 = (bf16[1,1536,256]{2,1,0:T(8,128)(2,1)}, bf16[2,256,128]{2,1,0:T(8,128)(2,1)S(1)}, bf16[2,256,128]{2,1,0:T(8,128)(2,1)S(1)}, bf16[2,256,128]{2,1,0:T(8,128)(2,1)S(1)}) custom-call(bf16[2,256,128]{2,1,0:T(8,128)(2,1)S(1)} %collective-permute-done.8.refs_0_, bf16[2,256,128]{2,1,0:T(8,128)(2,1)S(1)} %collective-permute-done.9.refs_1_, ...), custom_call_target="tpu_custom_call" | custom-call | flops 1207959552 | bytes 3932160 | tf_op jit(solution)/shard_map/backward/pallas_call | solution.py:406
  58.2 0.0 collective-permute-start.13
  58.2 0.0 collective-permute-start.14
  58.2 0.0 collective-permute-done.10
  58.2 3.1 %collective-permute-start.15 = (bf16[2,256,128]{2,1,0:T(8,128)(2,1)S(1)}, bf16[2,256,128]{2,1,0:T(8,128)(2,1)S(1)}, u32[]{:S(2)}, u32[]{:S(2)}) collective-permute-start(bf16[2,256,128]{2,1,0:T(8,128)(2,1)S(1)} %get-tuple-element.58), channel_id=1, source_target_pairs={{15,0},{14,1},{9,2},{8,3},{11,4},{10,5},{13,6},{12,7},{23,8},{22,9... | collective-permute-start | bytes 393224 | tf_op jit(solution)/shard_map/ppermute | solution.py:441
  61.3 0.0 collective-permute-done.11
  61.3 0.0 collective-permute-done.12
  61.3 2.8 %collective-permute-done.13 = bf16[2,256,128]{2,1,0:T(8,128)(2,1)S(1)} collective-permute-done((bf16[2,256,128]{2,1,0:T(8,128)(2,1)S(1)}, bf16[2,256,128]{2,1,0:T(8,128)(2,1)S(1)}, u32[]{:S(2)}, u32[]{:S(2)}) %collective-permute-start.13) | collective-permute-done | bytes 131104 | tf_op jit(solution)/shard_map/ppermute | solution.py:441
  64.1 0.7 %collective-permute-done.14 = bf16[2,256,128]{2,1,0:T(8,128)(2,1)S(1)} collective-permute-done((bf16[2,256,128]{2,1,0:T(8,128)(2,1)S(1)}, bf16[2,256,128]{2,1,0:T(8,128)(2,1)S(1)}, u32[]{:S(2)}, u32[]{:S(2)}) %collective-permute-start.14) | collective-permute-done | bytes 131104 | tf_op jit(solution)/shard_map/ppermute | solution.py:441
  64.9 3.8 %collective-permute-done.15 = bf16[2,256,128]{2,1,0:T(8,128)(2,1)S(1)} collective-permute-done((bf16[2,256,128]{2,1,0:T(8,128)(2,1)S(1)}, bf16[2,256,128]{2,1,0:T(8,128)(2,1)S(1)}, u32[]{:S(2)}, u32[]{:S(2)}) %collective-permute-start.15) | collective-permute-done | bytes 131104 | tf_op jit(solution)/shard_map/ppermute | solution.py:441
  68.6 1.8 %unpack.1 = bf16[1,128,2,2048]{3,2,1,0:T(2,128)(2,1)} custom-call(bf16[2,128,2,128]{3,2,1,0:T(2,128)(2,1)S(1)} %bitcast.16, bf16[2,128,2,128]{3,2,1,0:T(2,128)(2,1)S(1)} %bitcast.17, bf16[2,128,2,128]{3,2,1,0:T(2,128)(2,1)S(1)} %bitcast.18, bf16[2,128,2,128]{3,2,1,0:T(2,128)(2,1)S(1)} %bitcast.19, bf16[2,128,2,128]{3,2,1,0:T(2,128)(2,1)S(1)} %bitcast.20, ...), custom_call_target="tpu_custom_call" | custom-call | tf_op jit(solution)/shard_map/unpack/pallas_call | solution.py:98
Async XLA Ops:
  0.6 1.2 %copy-start = (bf16[1,128,2,2048]{3,2,1,0:T(2,128)(2,1)S(1)}, bf16[1,128,2,2048]{3,2,1,0:T(2,128)(2,1)}, u32[]{:S(2)}) copy-start(bf16[1,128,2,2048]{3,2,1,0:T(2,128)(2,1)} %pairs_ref.1) | copy-start | bytes 3145732
  1.9 21.4 %copy-start.1 = (bf16[1,1536,256]{2,1,0:T(8,128)(2,1)S(1)}, bf16[1,1536,256]{2,1,0:T(8,128)(2,1)}, u32[]{:S(2)}) copy-start(bf16[1,1536,256]{2,1,0:T(8,128)(2,1)} %rows_ref.2) | copy-start | bytes 2359300
  1.9 21.7 %copy-start.2 = (bf16[1,1536,256]{2,1,0:T(8,128)(2,1)S(1)}, bf16[1,1536,256]{2,1,0:T(8,128)(2,1)}, u32[]{:S(2)}) copy-start(bf16[1,1536,256]{2,1,0:T(8,128)(2,1)} %rows_ref.3) | copy-start | bytes 2359300
  2.8 10.3 %collective-permute-start.3 = (bf16[2,256,128]{2,1,0:T(8,128)(2,1)S(1)}, bf16[2,256,128]{2,1,0:T(8,128)(2,1)S(1)}, u32[]{:S(2)}, u32[]{:S(2)}) collective-permute-start(bf16[2,256,128]{2,1,0:T(8,128)(2,1)S(1)} %bitcast.31), channel_id=1, source_target_pairs={{0,11},{1,10},{2,13},{3,12},{4,15},{5,14},{6,9},{7,8},{8,19},{9,18... | collective-permute-start | bytes 393224 | tf_op jit(solution)/shard_map/ppermute | solution.py:435
  6.3 10.3 %collective-permute-start.4 = (bf16[2,256,128]{2,1,0:T(8,128)(2,1)S(1)}, bf16[2,256,128]{2,1,0:T(8,128)(2,1)S(1)}, u32[]{:S(2)}, u32[]{:S(2)}) collective-permute-start(bf16[2,256,128]{2,1,0:T(8,128)(2,1)S(1)} %bitcast.30), channel_id=1, source_target_pairs={{0,10},{1,11},{2,12},{3,13},{4,14},{5,15},{6,8},{7,9},{8,18},{9,19... | collective-permute-start | bytes 393224 | tf_op jit(solution)/shard_map/ppermute | solution.py:435
  9.1 12.7 %collective-permute-start.5 = (bf16[2,256,128]{2,1,0:T(8,128)(2,1)S(1)}, bf16[2,256,128]{2,1,0:T(8,128)(2,1)S(1)}, u32[]{:S(2)}, u32[]{:S(2)}) collective-permute-start(bf16[2,256,128]{2,1,0:T(8,128)(2,1)S(1)} %bitcast.29), channel_id=1, source_target_pairs={{0,15},{1,14},{2,9},{3,8},{4,11},{5,10},{6,13},{7,12},{8,23},{9,22... | collective-permute-start | bytes 393224 | tf_op jit(solution)/shard_map/ppermute | solution.py:435
  10.7 15.7 %collective-permute-start.1 = (bf16[2,256,128]{2,1,0:T(8,128)(2,1)S(1)}, bf16[2,256,128]{2,1,0:T(8,128)(2,1)S(1)}, u32[]{:S(2)}, u32[]{:S(2)}) collective-permute-start(bf16[2,256,128]{2,1,0:T(8,128)(2,1)S(1)} %bitcast.28), channel_id=1, source_target_pairs={{0,14},{1,15},{2,8},{3,9},{4,10},{5,11},{6,12},{7,13},{8,22},{9,23... | collective-permute-start | bytes 393224 | tf_op jit(solution)/shard_map/ppermute | solution.py:435
  11.1 15.3 %collective-permute-start = (bf16[2,256,128]{2,1,0:T(8,128)(2,1)S(1)}, bf16[2,256,128]{2,1,0:T(8,128)(2,1)S(1)}, u32[]{:S(2)}, u32[]{:S(2)}) collective-permute-start(bf16[2,256,128]{2,1,0:T(8,128)(2,1)S(1)} %bitcast.27), channel_id=1, source_target_pairs={{0,9},{1,8},{2,11},{3,10},{4,13},{5,12},{6,15},{7,14},{8,17},{9,16... | collective-permute-start | bytes 393224 | tf_op jit(solution)/shard_map/ppermute | solution.py:435
  13.1 13.3 %collective-permute-start.2 = (bf16[2,256,128]{2,1,0:T(8,128)(2,1)S(1)}, bf16[2,256,128]{2,1,0:T(8,128)(2,1)S(1)}, u32[]{:S(2)}, u32[]{:S(2)}) collective-permute-start(bf16[2,256,128]{2,1,0:T(8,128)(2,1)S(1)} %bitcast.26), channel_id=1, source_target_pairs={{0,8},{1,9},{2,10},{3,11},{4,12},{5,13},{6,14},{7,15},{8,16},{9,17... | collective-permute-start | bytes 393224 | tf_op jit(solution)/shard_map/ppermute | solution.py:435
  16.7 13.3 %collective-permute-start.6 = (bf16[2,256,128]{2,1,0:T(8,128)(2,1)S(1)}, bf16[2,256,128]{2,1,0:T(8,128)(2,1)S(1)}, u32[]{:S(2)}, u32[]{:S(2)}) collective-permute-start(bf16[2,256,128]{2,1,0:T(8,128)(2,1)S(1)} %bitcast.25), channel_id=1, source_target_pairs={{0,13},{1,12},{2,15},{3,14},{4,9},{5,8},{6,11},{7,10},{8,21},{9,20... | collective-permute-start | bytes 393224 | tf_op jit(solution)/shard_map/ppermute | solution.py:435
  21.8 11.7 %collective-permute-start.7 = (bf16[2,256,128]{2,1,0:T(8,128)(2,1)S(1)}, bf16[2,256,128]{2,1,0:T(8,128)(2,1)S(1)}, u32[]{:S(2)}, u32[]{:S(2)}) collective-permute-start(bf16[2,256,128]{2,1,0:T(8,128)(2,1)S(1)} %bitcast.24), channel_id=1, source_target_pairs={{0,12},{1,13},{2,14},{3,15},{4,8},{5,9},{6,10},{7,11},{8,20},{9,21... | collective-permute-start | bytes 393224 | tf_op jit(solution)/shard_map/ppermute | solution.py:435
  37.5 11.7 %collective-permute-start.8 = (bf16[2,256,128]{2,1,0:T(8,128)(2,1)S(1)}, bf16[2,256,128]{2,1,0:T(8,128)(2,1)S(1)}, u32[]{:S(2)}, u32[]{:S(2)}) collective-permute-start(bf16[2,256,128]{2,1,0:T(8,128)(2,1)S(1)} %get-tuple-element.48), channel_id=1, source_target_pairs={{13,0},{12,1},{15,2},{14,3},{9,4},{8,5},{11,6},{10,7},{21,8},{20,9... | collective-permute-start | bytes 393224 | tf_op jit(solution)/shard_map/ppermute | solution.py:441
  37.5 16.7 %collective-permute-start.9 = (bf16[2,256,128]{2,1,0:T(8,128)(2,1)S(1)}, bf16[2,256,128]{2,1,0:T(8,128)(2,1)S(1)}, u32[]{:S(2)}, u32[]{:S(2)}) collective-permute-start(bf16[2,256,128]{2,1,0:T(8,128)(2,1)S(1)} %get-tuple-element.49), channel_id=1, source_target_pairs={{12,0},{13,1},{14,2},{15,3},{8,4},{9,5},{10,6},{11,7},{20,8},{21,9... | collective-permute-start | bytes 393224 | tf_op jit(solution)/shard_map/ppermute | solution.py:441
  44.5 13.7 %collective-permute-start.10 = (bf16[2,256,128]{2,1,0:T(8,128)(2,1)S(1)}, bf16[2,256,128]{2,1,0:T(8,128)(2,1)S(1)}, u32[]{:S(2)}, u32[]{:S(2)}) collective-permute-start(bf16[2,256,128]{2,1,0:T(8,128)(2,1)S(1)} %get-tuple-element.53), channel_id=1, source_target_pairs={{9,0},{8,1},{11,2},{10,3},{13,4},{12,5},{15,6},{14,7},{17,8},{16,9... | collective-permute-start | bytes 393224 | tf_op jit(solution)/shard_map/ppermute | solution.py:441
  44.5 16.8 %collective-permute-start.11 = (bf16[2,256,128]{2,1,0:T(8,128)(2,1)S(1)}, bf16[2,256,128]{2,1,0:T(8,128)(2,1)S(1)}, u32[]{:S(2)}, u32[]{:S(2)}) collective-permute-start(bf16[2,256,128]{2,1,0:T(8,128)(2,1)S(1)} %get-tuple-element.54), channel_id=1, source_target_pairs={{14,0},{15,1},{8,2},{9,3},{10,4},{11,5},{12,6},{13,7},{22,8},{23,9... | collective-permute-start | bytes 393224 | tf_op jit(solution)/shard_map/ppermute | solution.py:441
  44.5 16.8 %collective-permute-start.12 = (bf16[2,256,128]{2,1,0:T(8,128)(2,1)S(1)}, bf16[2,256,128]{2,1,0:T(8,128)(2,1)S(1)}, u32[]{:S(2)}, u32[]{:S(2)}) collective-permute-start(bf16[2,256,128]{2,1,0:T(8,128)(2,1)S(1)} %get-tuple-element.55), channel_id=1, source_target_pairs={{8,0},{9,1},{10,2},{11,3},{12,4},{13,5},{14,6},{15,7},{16,8},{17,9... | collective-permute-start | bytes 393224 | tf_op jit(solution)/shard_map/ppermute | solution.py:441
  58.2 6.0 %collective-permute-start.13 = (bf16[2,256,128]{2,1,0:T(8,128)(2,1)S(1)}, bf16[2,256,128]{2,1,0:T(8,128)(2,1)S(1)}, u32[]{:S(2)}, u32[]{:S(2)}) collective-permute-start(bf16[2,256,128]{2,1,0:T(8,128)(2,1)S(1)} %get-tuple-element.56), channel_id=1, source_target_pairs={{11,0},{10,1},{13,2},{12,3},{15,4},{14,5},{9,6},{8,7},{19,8},{18,9... | collective-permute-start | bytes 393224 | tf_op jit(solution)/shard_map/ppermute | solution.py:441
  58.2 6.7 %collective-permute-start.14 = (bf16[2,256,128]{2,1,0:T(8,128)(2,1)S(1)}, bf16[2,256,128]{2,1,0:T(8,128)(2,1)S(1)}, u32[]{:S(2)}, u32[]{:S(2)}) collective-permute-start(bf16[2,256,128]{2,1,0:T(8,128)(2,1)S(1)} %get-tuple-element.57), channel_id=1, source_target_pairs={{10,0},{11,1},{12,2},{13,3},{14,4},{15,5},{8,6},{9,7},{18,8},{19,9... | collective-permute-start | bytes 393224 | tf_op jit(solution)/shard_map/ppermute | solution.py:441
  58.2 10.4 %collective-permute-start.15 = (bf16[2,256,128]{2,1,0:T(8,128)(2,1)S(1)}, bf16[2,256,128]{2,1,0:T(8,128)(2,1)S(1)}, u32[]{:S(2)}, u32[]{:S(2)}) collective-permute-start(bf16[2,256,128]{2,1,0:T(8,128)(2,1)S(1)} %get-tuple-element.58), channel_id=1, source_target_pairs={{15,0},{14,1},{9,2},{8,3},{11,4},{10,5},{13,6},{12,7},{23,8},{22,9... | collective-permute-start | bytes 393224 | tf_op jit(solution)/shard_map/ppermute | solution.py:441

commit v6 on v5

--- a/solution.py
+++ b/solution.py
@@ -22,9 +22,10 @@
     tp_count = lax.axis_size("tp")
     near = [(0, dy) for dy in reversed(range(tp_count))]
     order = [(dz, dy) for dz in range(1, seq_count) for dy in reversed(range(tp_count))]
-    order.sort(key=lambda o: -abs(o[0] - seq_count / 2))
+    order.sort(key=lambda o: abs(o[0] - seq_count / 2))
+    last = len(order) - 1
     for i, offset in enumerate(near):
-        order.insert(3 + 2 * i, offset)
+        order.insert(last + 2 * i, offset)
     return order
 
 
@@ -200,7 +201,7 @@
         shrink = jnp.exp2((before[0] - top) * EXPONENT)
         total = total + before[1] * shrink
         context = context + before[2] * shrink
-    return raised, low, top, total, context
+    return low, top, total, context
 
 
 def forward_kernel(count, first, tile, *refs):
@@ -220,7 +221,7 @@
             before = None
             if not first:
                 before = (stats_in[h, 0:1, here], stats_in[h, 1:2, here], context_in[h, :, here])
-            _, low, top, total, context = raise_scores(
+            low, top, total, context = raise_scores(
                 k_ref[h], qt_ref[h, :, here], vt_ref[h], before
             )
             low_ref[h, :, here] = low
@@ -229,30 +230,30 @@
             context_ref[h, :, here] = context
 
 
-def gradients(raised, low, shrunk, stats, h, here, refs):
+def gradients(low, scale, row_dot, h, here, refs):
     qt_ref, gt_ref, v_ref, kt_ref, gk_ref, gv_ref = refs
-    scale, row_dot = stats
     qt = qt_ref[h, :, here].astype(jnp.float32)
     gt = gt_ref[h, :, here]
     grad_weights = dot(v_ref[h], gt)
-    grad_scores = (raised * (grad_weights - row_dot)).astype(jnp.bfloat16)
-    scale = scale if shrunk is None else scale * shrunk
+    grad_scores = (low.astype(jnp.float32) * (grad_weights - row_dot)).astype(jnp.bfloat16)
     grad_q = dot(kt_ref[h], grad_scores) * (scale * FACTOR)
     gk_ref[h] += dot(grad_scores, (qt * (scale * FACTOR)).astype(jnp.bfloat16), NT)
     gv_ref[h] += dot(low, (gt.astype(jnp.float32) * scale).astype(jnp.bfloat16), NT)
     return grad_q
 
 
-def turn_kernel(count, tile, *refs):
+def turn_kernel(count, others, tile, *refs):
     chunks, refs = refs[:count], refs[count:]
-    qt_ref, gt_ref, stats_in, context_in = refs[:4]
-    stats_ref, context_ref, grad_q_ref = refs[4:7]
-    outs, refs = refs[7 : 7 + count], refs[7 + count :]
-    k_ref, v_ref, kt_ref, vt_ref, gk_ref, gv_ref = refs
+    far_chunks, refs = refs[:others], refs[others:]
+    qt_ref, gt_ref, stats_in, context_in, far_low_ref, far_stats = refs[:6]
+    stats_ref, context_ref, low_ref, grad_q_ref = refs[6:10]
+    outs, refs = refs[10 : 10 + others], refs[10 + others :]
+    k_ref, vt_ref, v_ref, kt_ref, gk_ref, gv_ref = refs
     heads, pair_rows, _ = chunks[0].shape
     rows = pair_rows // 2
     for h in range(heads):
-        split_chunks(chunks, h, rows, k_ref, v_ref, kt_ref, vt_ref)
+        split_chunks(chunks, h, rows, k_ref=k_ref, vt_ref=vt_ref)
+        split_chunks(far_chunks, h, rows, v_ref=v_ref, kt_ref=kt_ref)
     gk_ref[...] = jnp.zeros_like(gk_ref)
     gv_ref[...] = jnp.zeros_like(gv_ref)
 
@@ -261,7 +262,7 @@
         here = tokens_of(j, tile)
         for h in range(heads):
             before = (stats_in[h, 0:1, here], stats_in[h, 1:2, here], context_in[h, :, here])
-            raised, low, top, total, context = raise_scores(
+            low, top, total, context = raise_scores(
                 k_ref[h], qt_ref[h, :, here], vt_ref[h], before
             )
             scale = 1.0 / total
@@ -269,15 +270,16 @@
             row_dot = jnp.sum(
                 gt_ref[h, :, here].astype(jnp.float32) * context, axis=0, keepdims=True
             )
+            low_ref[h, :, here] = low
             context_ref[h, :, here] = context
             stats_ref[h, 0:1, here] = top
             stats_ref[h, 1:2, here] = scale
             stats_ref[h, 2:3, here] = row_dot
+            shrunk = jnp.exp2((far_stats[h, 0:1, here] - top) * EXPONENT)
             grad_q_ref[h, :, here] = gradients(
-                raised,
-                low,
-                None,
-                (scale, row_dot),
+                far_low_ref[h, :, here],
+                scale * shrunk,
+                row_dot,
                 h,
                 here,
                 (qt_ref, gt_ref, v_ref, kt_ref, gk_ref, gv_ref),
@@ -287,16 +289,13 @@
         join_chunks(outs, h, rows, gk_ref, gv_ref)
 
 
-def backward_kernel(back, count, ready, last, tile, *refs):
+def backward_kernel(back, count, first, tile, *refs):
     chunks, refs = refs[back : back + count], refs[back + count :]
     qt_ref, gt_ref, low_ref, stats_then, stats_ref, grad_q_in = refs[:6]
-    refs = refs[6:]
-    if ready:
-        ready_ref, refs = refs[0], refs[1:]
-    if ready or last:
-        rows_ref, refs = refs[0], refs[1:]
-    if not last:
-        grad_q_ref, refs = refs[0], refs[1:]
+    if first:
+        ready_ref, rows_ref, grad_q_ref, refs = refs[6], refs[7], refs[8], refs[9:]
+    else:
+        rows_ref, refs = refs[6], refs[7:]
     outs, refs = refs[:count], refs[count:]
     v_ref, kt_ref, gk_ref, gv_ref = refs
     heads, pair_rows, _ = chunks[0].shape
@@ -311,24 +310,20 @@
         here = tokens_of(j, tile)
         for h in range(heads):
             columns = slice(h * HEAD, (h + 1) * HEAD)
-            low = low_ref[h, :, here]
             top, scale, row_dot = (stats_ref[h, i : i + 1, here] for i in range(3))
             shrunk = jnp.exp2((stats_then[h, 0:1, here] - top) * EXPONENT)
             grad_q = grad_q_in[h, :, here] + gradients(
-                low.astype(jnp.float32),
-                low,
-                shrunk,
-                (scale, row_dot),
+                low_ref[h, :, here],
+                scale * shrunk,
+                row_dot,
                 h,
                 here,
                 (qt_ref, gt_ref, v_ref, kt_ref, gk_ref, gv_ref),
             )
-            if last:
-                rows_ref[0, here, columns] = grad_q.T.astype(rows_ref.dtype)
-            else:
+            if first:
                 grad_q_ref[h, :, here] = grad_q
-            if ready:
-                rows_ref[0, here, columns] = ready_ref[h, :, here].T.astype(rows_ref.dtype)
+                grad_q = ready_ref[h, :, here]
+            rows_ref[0, here, columns] = grad_q.T.astype(rows_ref.dtype)
 
     for h in range(heads):
         join_chunks(outs, h, rows, gk_ref, gv_ref)
@@ -352,8 +347,8 @@
     wide_shape = jax.ShapeDtypeStruct((heads, HEAD, tokens), jnp.float32)
     rows_shape = jax.ShapeDtypeStruct(queries.shape, queries.dtype)
     compiler_params = params(enc_len)
-    turn_at = len(arrived) - len(arrived) // 4
-    half = (turn_at + 1) // 2
+    quarter = max(1, len(arrived) // 4)
+    cuts = [0, quarter, len(arrived) - quarter, len(arrived)]
 
     def natural(count):
         return pltpu.VMEM((heads, count * rows, HEAD), jnp.bfloat16)
@@ -364,16 +359,18 @@
     def sums(count):
         return pltpu.VMEM((heads, count * rows, HEAD), jnp.float32)
 
+    def low_of(count):
+        return jax.ShapeDtypeStruct((heads, count * rows, tokens), jnp.bfloat16)
+
     def shapes_of(group):
         return [jax.ShapeDtypeStruct(c.shape, c.dtype) for c in group]
 
-    state, parts = [], []
-    for begin, end in ((0, half), (half, turn_at)):
+    state, kept = [], []
+    for begin, end in zip(cuts[:2], cuts[1:3]):
         group, count = arrived[begin:end], end - begin
-        low_shape = jax.ShapeDtypeStruct((heads, count * rows, tokens), jnp.bfloat16)
         stats, context, low = pl.pallas_call(
             functools.partial(forward_kernel, count, not state, tile_of(count * rows, tokens)),
-            out_shape=[stats_shape, wide_shape, low_shape],
+            out_shape=[stats_shape, wide_shape, low_of(count)],
             in_specs=[VMEM] * (count + 1 + len(state)),
             out_specs=[VMEM] * 3,
             scratch_shapes=[natural(count), across(count, 16)],
@@ -382,46 +379,46 @@
             name="forward",
         )(*group, qt, *state)
         state = [stats, context]
-        parts.insert(0, (begin, count, low, stats))
-
-    group, count = arrived[turn_at:], len(arrived) - turn_at
-    final, context, grad_q, *grads = pl.pallas_call(
-        functools.partial(turn_kernel, count, tile_of(count * rows, tokens)),
-        out_shape=[stats_shape, wide_shape, wide_shape] + shapes_of(group),
-        in_specs=[VMEM] * (count + 4),
-        out_specs=[VMEM] * (count + 3),
-        scratch_shapes=[natural(count), natural(count), across(count), across(count, 16)]
-        + [sums(count)] * 2,
+        kept.append((low, stats))
+
+    far, group = arrived[: cuts[1]], arrived[cuts[2] :]
+    others, count = len(far), len(group)
+    final, context, low, grad_q, *grads = pl.pallas_call(
+        functools.partial(turn_kernel, count, others, tile_of(count * rows, tokens)),
+        out_shape=[stats_shape, wide_shape, low_of(count), wide_shape] + shapes_of(far),
+        in_specs=[VMEM] * (count + others + 6),
+        out_specs=[VMEM] * (others + 4),
+        scratch_shapes=[natural(count), across(count, 16), natural(others), across(others)]
+        + [sums(others)] * 2,
         compiler_params=compiler_params,
         cost_estimate=cost(heads, count * rows, tokens, 6),
         name="turn",
-    )(*group, qt, gt, *state)
-    returned = [send_back(turn_at, grads)]
-
-    for i, (begin, count, low, then) in enumerate(parts):
-        group = arrived[begin : begin + count]
-        ready, last = i == 0, i == len(parts) - 1
-        back = returned[i - 1] if i >= 1 else []
-        extra = [rows_shape] * (ready or last) + [wide_shape] * (not last)
+    )(*group, *far, qt, gt, *state, *kept[0])
+    kept.append((low, final))
+    returned = [send_back(0, grads)]
+
+    for i, (begin, end) in enumerate(zip(cuts[1:3], cuts[2:])):
+        group, count = arrived[begin:end], end - begin
+        first = i == 0
+        back = [] if first else returned[0]
+        shapes = [rows_shape, wide_shape] if first else [rows_shape]
         outs = pl.pallas_call(
             functools.partial(
-                backward_kernel, len(back), count, ready, last, tile_of(count * rows, tokens)
+                backward_kernel, len(back), count, first, tile_of(count * rows, tokens)
             ),
-            out_shape=extra + shapes_of(group),
-            in_specs=[ANY] * len(back) + [VMEM] * (count + 6 + ready),
-            out_specs=[VMEM] * (len(extra) + count),
+            out_shape=shapes + shapes_of(group),
+            in_specs=[ANY] * len(back) + [VMEM] * (count + 6 + first),
+            out_specs=[VMEM] * (len(shapes) + count),
             scratch_shapes=[natural(count), across(count)] + [sums(count)] * 2,
             compiler_params=compiler_params,
             cost_estimate=cost(heads, count * rows, tokens, 4),
             name="backward",
-        )(*back, *group, qt, gt, low, then, final, grad_q, *([context] if ready else []))
-        if ready:
-            context_rows = outs[0]
-        if last:
+        )(*back, *group, qt, gt, *kept[i + 1], final, grad_q, *([context] if first else []))
+        if first:
+            context_rows, grad_q = outs[:2]
+        else:
             grad_query = outs[0]
-        else:
-            grad_q = outs[len(extra) - 1]
-        returned.append(send_back(begin, outs[len(extra) :]))
+        returned.append(send_back(begin, outs[len(shapes) :]))
     return context_rows, grad_query, returned
 
 

time: 71.1 us -> 68.2 us (0.959)
  the two profiles are of different devices: /device:TPU:0 before, /device:TPU:1 now
where the time goes in v6:
time: 68.2 us; the launch traced here: 68.1 us
  starting transfers between devices  29.7 us (44%)
  Pallas kernels  21.9 us (32%)
  waiting for transfers between devices  14.6 us (21%)
  local copies, waits for them, and re-layouts  1.23 us (2%)
  between operations  0.75 us (1%)
    ppermute x8, starting transfers between devices, shards(): arrived.append(lax.ppermute(block, AXES, route(offset, False)))  15.8 us
    ppermute x8, starting transfers between devices, send_back(): lax.ppermute(b, AXES, route(o, True))  13.9 us
    ppermute x8, waiting for transfers between devices, shards(): arrived.append(lax.ppermute(block, AXES, route(offset, False)))  9.15 us
    pallas_call x2, Pallas kernels, attend(): pl.pallas_call(functools.partial(backward_kernel, len(back), count, first...  8.68 us
    pallas_call x2, Pallas kernels, attend(): pl.pallas_call(functools.partial(forward_kernel, count, not state, tile_o...  5.69 us
    ppermute x8, waiting for transfers between devices, send_back(): lax.ppermute(b, AXES, route(o, True))  5.44 us
    pallas_call x1, Pallas kernels, attend(): pl.pallas_call(functools.partial(turn_kernel, count, others, tile_of(coun...  4.22 us
    pallas_call x1, Pallas kernels, unpack(): pl.pallas_call(kernel, out_shape=jax.ShapeDtypeStruct((1, rows, 2, width)...  1.78 us
  transfers between devices with their start and end apart: 16, of which 6 were waited for; matrix products, arithmetic and copies ran while one was open for 0% of the time, Pallas kernels for 22%

profile of v6, /device:TPU:1, one launch (start us, length us, event | category | flops | bytes accessed | tf_op | source)
XLA Modules:
  0.0 68.1 jit_solution(7217249188796439460)
XLA Ops:
  0.6 0.0 copy-start
  0.6 1.2 %copy-done = bf16[1,128,2,2048]{3,2,1,0:T(2,128)(2,1)S(1)} copy-done((bf16[1,128,2,2048]{3,2,1,0:T(2,128)(2,1)S(1)}, bf16[1,128,2,2048]{3,2,1,0:T(2,128)(2,1)}, u32[]{:S(2)}) %copy-start) | copy-done | bytes 1048600
  1.9 0.0 copy-start.1
  1.9 0.0 copy-start.2
  1.9 1.0 %pack.1 = (bf16[2,128,2,128]{3,2,1,0:T(2,128)(2,1)S(1)}, bf16[2,128,2,128]{3,2,1,0:T(2,128)(2,1)S(1)}, bf16[2,128,2,128]{3,2,1,0:T(2,128)(2,1)S(1)}, bf16[2,128,...) custom-call(bf16[1,128,2,2048]{3,2,1,0:T(2,128)(2,1)S(1)} %copy-done), custom_call_target="tpu_custom_call" | custom-call | tf_op jit(solution)/shard_map/pack/pallas_call | solution.py:73
  2.8 3.7 %collective-permute-start.1 = (bf16[2,256,128]{2,1,0:T(8,128)(2,1)S(1)}, bf16[2,256,128]{2,1,0:T(8,128)(2,1)S(1)}, u32[]{:S(2)}, u32[]{:S(2)}) collective-permute-start(bf16[2,256,128]{2,1,0:T(8,128)(2,1)S(1)} %bitcast.31), channel_id=1, source_target_pairs={{0,10},{1,11},{2,12},{3,13},{4,14},{5,15},{6,8},{7,9},{8,18},{9,19... | collective-permute-start | bytes 393224 | tf_op jit(solution)/shard_map/ppermute | solution.py:432
  6.5 3.0 %collective-permute-start.4 = (bf16[2,256,128]{2,1,0:T(8,128)(2,1)S(1)}, bf16[2,256,128]{2,1,0:T(8,128)(2,1)S(1)}, u32[]{:S(2)}, u32[]{:S(2)}) collective-permute-start(bf16[2,256,128]{2,1,0:T(8,128)(2,1)S(1)} %bitcast.30), channel_id=1, source_target_pairs={{0,13},{1,12},{2,15},{3,14},{4,9},{5,8},{6,11},{7,10},{8,21},{9,20... | collective-permute-start | bytes 393224 | tf_op jit(solution)/shard_map/ppermute | solution.py:432
  9.5 0.6 collective-permute-start.5
  10.1 1.0 %collective-permute-start = (bf16[2,256,128]{2,1,0:T(8,128)(2,1)S(1)}, bf16[2,256,128]{2,1,0:T(8,128)(2,1)S(1)}, u32[]{:S(2)}, u32[]{:S(2)}) collective-permute-start(bf16[2,256,128]{2,1,0:T(8,128)(2,1)S(1)} %bitcast.28), channel_id=1, source_target_pairs={{0,11},{1,10},{2,13},{3,12},{4,15},{5,14},{6,9},{7,8},{8,19},{9,18... | collective-permute-start | bytes 393224 | tf_op jit(solution)/shard_map/ppermute | solution.py:432
  11.0 4.4 %collective-permute-start.2 = (bf16[2,256,128]{2,1,0:T(8,128)(2,1)S(1)}, bf16[2,256,128]{2,1,0:T(8,128)(2,1)S(1)}, u32[]{:S(2)}, u32[]{:S(2)}) collective-permute-start(bf16[2,256,128]{2,1,0:T(8,128)(2,1)S(1)} %bitcast.27), channel_id=1, source_target_pairs={{0,15},{1,14},{2,9},{3,8},{4,11},{5,10},{6,13},{7,12},{8,23},{9,22... | collective-permute-start | bytes 393224 | tf_op jit(solution)/shard_map/ppermute | solution.py:432
  15.4 0.0 collective-permute-done.1.refs_1_
  15.4 0.2 collective-permute-start.3
  15.7 9.1 %collective-permute-done.4.refs_0_.refs_2_ = bf16[2,256,128]{2,1,0:T(8,128)(2,1)S(1)} collective-permute-done((bf16[2,256,128]{2,1,0:T(8,128)(2,1)S(1)}, bf16[2,256,128]{2,1,0:T(8,128)(2,1)S(1)}, u32[]{:S(2)}, u32[]{:S(2)}) %collective-permute-start.4) | collective-permute-done | bytes 131104 | tf_op jit(solution)/shard_map/ppermute | solution.py:432
  24.8 2.1 %collective-permute-start.6 = (bf16[2,256,128]{2,1,0:T(8,128)(2,1)S(1)}, bf16[2,256,128]{2,1,0:T(8,128)(2,1)S(1)}, u32[]{:S(2)}, u32[]{:S(2)}) collective-permute-start(bf16[2,256,128]{2,1,0:T(8,128)(2,1)S(1)} %bitcast.25), channel_id=1, source_target_pairs={{0,14},{1,15},{2,8},{3,9},{4,10},{5,11},{6,12},{7,13},{8,22},{9,23... | collective-permute-start | bytes 393224 | tf_op jit(solution)/shard_map/ppermute | solution.py:432
  26.9 0.0 collective-permute-done.5.refs_1_.refs_3_
  26.9 0.9 %collective-permute-start.7 = (bf16[2,256,128]{2,1,0:T(8,128)(2,1)S(1)}, bf16[2,256,128]{2,1,0:T(8,128)(2,1)S(1)}, u32[]{:S(2)}, u32[]{:S(2)}) collective-permute-start(bf16[2,256,128]{2,1,0:T(8,128)(2,1)S(1)} %bitcast.24), channel_id=1, source_target_pairs={{0,8},{1,9},{2,10},{3,11},{4,12},{5,13},{6,14},{7,15},{8,16},{9,17... | collective-permute-start | bytes 393224 | tf_op jit(solution)/shard_map/ppermute | solution.py:432
  27.8 0.0 copy-done.1
  27.8 0.3 turned.2.refs_2_.refs_4_
  28.0 0.0 copy-done.2
  28.0 0.3 turned.3.refs_5_
  28.3 1.8 %forward.2 = (f32[2,8,1536]{2,1,0:T(8,128)S(1)}, f32[2,128,1536]{2,1,0:T(8,128)S(1)}, bf16[2,256,1536]{2,1,0:T(8,128)(2,1)S(1)}) custom-call(bf16[2,256,128]{2,1,0:T(8,128)(2,1)S(1)} %collective-permute-done.4.refs_0_.refs_2_, bf16[2,256,128]{2,1,0:T(8,128)(2,1)S(1)} %collective-permute-done.5.refs_1_.refs_3_, bf16[2,128,1536]{2,1,0:T(8,128)(2,1)S(1)} %turned.2.refs_2_.refs_4_), custom_call_target="tpu_custom_call" | custom-call | flops 402653184 | bytes 3670016 | tf_op jit(solution)/shard_map/forward/pallas_call | solution.py:371
  30.2 0.0 collective-permute-done.refs_0_
  30.2 0.0 collective-permute-done.2.refs_2_
  30.2 0.0 collective-permute-done.3.refs_3_
  30.2 3.9 %forward.3 = (f32[2,8,1536]{2,1,0:T(8,128)S(1)}, f32[2,128,1536]{2,1,0:T(8,128)S(1)}, bf16[2,512,1536]{2,1,0:T(8,128)(2,1)S(1)}) custom-call(bf16[2,256,128]{2,1,0:T(8,128)(2,1)S(1)} %collective-permute-done.refs_0_, bf16[2,256,128]{2,1,0:T(8,128)(2,1)S(1)} %collective-permute-done.1.refs_1_, bf16[2,256,128]{2,1,0:T(8,128)(2,1)S(1)} %collective-permute-done.2.refs_2_, ...), custom_call_target="tpu_custom_call" | custom-call | flops 805306368 | bytes 4194304 | tf_op jit(solution)/shard_map/forward/pallas_call | solution.py:371
  34.1 0.0 collective-permute-done.6.refs_0_.refs_2_
  34.1 0.0 collective-permute-done.7.refs_1_.refs_3_
  34.1 4.2 %turn.1 = (f32[2,8,1536]{2,1,0:T(8,128)S(1)}, f32[2,128,1536]{2,1,0:T(8,128)S(1)}, bf16[2,256,1536]{2,1,0:T(8,128)(2,1)S(1)}, f32[2,128,1536]{2,1,0:T(8,128)S(1)...) custom-call(bf16[2,256,128]{2,1,0:T(8,128)(2,1)S(1)} %collective-permute-done.6.refs_0_.refs_2_, ...), custom_call_target="tpu_custom_call" | custom-call | flops 1207959552 | bytes 3670016 | tf_op jit(solution)/shard_map/turn/pallas_call | solution.py:386
  38.3 3.7 %collective-permute-start.8 = (bf16[2,256,128]{2,1,0:T(8,128)(2,1)S(1)}, bf16[2,256,128]{2,1,0:T(8,128)(2,1)S(1)}, u32[]{:S(2)}, u32[]{:S(2)}) collective-permute-start(bf16[2,256,128]{2,1,0:T(8,128)(2,1)S(1)} %get-tuple-element.50), channel_id=1, source_target_pairs={{13,0},{12,1},{15,2},{14,3},{9,4},{8,5},{11,6},{10,7},{21,8},{20,9... | collective-permute-start | bytes 393224 | tf_op jit(solution)/shard_map/ppermute | solution.py:438
  42.0 0.2 collective-permute-start.9
  42.2 5.4 %backward.2 = (bf16[1,1536,256]{2,1,0:T(8,128)(2,1)}, f32[2,128,1536]{2,1,0:T(8,128)S(1)}, bf16[2,256,128]{2,1,0:T(8,128)(2,1)S(1)}, bf16[2,256,128]{2,1,0:T(8,1...) custom-call(bf16[2,256,128]{2,1,0:T(8,128)(2,1)S(1)} %collective-permute-done.refs_0_, ...), custom_call_target="tpu_custom_call" | custom-call | flops 1610612736 | bytes 4194304 | tf_op jit(solution)/shard_map/backward/pallas_call | solution.py:405
  47.7 0.0 collective-permute-start.10
  47.7 4.2 %collective-permute-start.11 = (bf16[2,256,128]{2,1,0:T(8,128)(2,1)S(1)}, bf16[2,256,128]{2,1,0:T(8,128)(2,1)S(1)}, u32[]{:S(2)}, u32[]{:S(2)}) collective-permute-start(bf16[2,256,128]{2,1,0:T(8,128)(2,1)S(1)} %get-tuple-element.56), channel_id=1, source_target_pairs={{10,0},{11,1},{12,2},{13,3},{14,4},{15,5},{8,6},{9,7},{18,8},{19,9... | collective-permute-start | bytes 393224 | tf_op jit(solution)/shard_map/ppermute | solution.py:438
  51.9 0.0 collective-permute-start.12
  51.9 0.1 collective-permute-done.8.refs_0_
  52.0 1.7 %collective-permute-start.13 = (bf16[2,256,128]{2,1,0:T(8,128)(2,1)S(1)}, bf16[2,256,128]{2,1,0:T(8,128)(2,1)S(1)}, u32[]{:S(2)}, u32[]{:S(2)}) collective-permute-start(bf16[2,256,128]{2,1,0:T(8,128)(2,1)S(1)} %get-tuple-element.58), channel_id=1, source_target_pairs={{9,0},{8,1},{11,2},{10,3},{13,4},{12,5},{15,6},{14,7},{17,8},{16,9... | collective-permute-start | bytes 393224 | tf_op jit(solution)/shard_map/ppermute | solution.py:438
  53.6 0.9 %collective-permute-done.9.refs_1_ = bf16[2,256,128]{2,1,0:T(8,128)(2,1)S(1)} collective-permute-done((bf16[2,256,128]{2,1,0:T(8,128)(2,1)S(1)}, bf16[2,256,128]{2,1,0:T(8,128)(2,1)S(1)}, u32[]{:S(2)}, u32[]{:S(2)}) %collective-permute-start.9) | collective-permute-done | bytes 131104 | tf_op jit(solution)/shard_map/ppermute | solution.py:438
  54.6 3.2 %backward.3 = (bf16[1,1536,256]{2,1,0:T(8,128)(2,1)}, bf16[2,256,128]{2,1,0:T(8,128)(2,1)S(1)}, bf16[2,256,128]{2,1,0:T(8,128)(2,1)S(1)}) custom-call(bf16[2,256,128]{2,1,0:T(8,128)(2,1)S(1)} %collective-permute-done.8.refs_0_, bf16[2,256,128]{2,1,0:T(8,128)(2,1)S(1)} %collective-permute-done.9.refs_1_, ...), custom_call_target="tpu_custom_call" | custom-call | flops 805306368 | bytes 3670016 | tf_op jit(solution)/shard_map/backward/pallas_call | solution.py:405
  57.8 4.1 %collective-permute-start.14 = (bf16[2,256,128]{2,1,0:T(8,128)(2,1)S(1)}, bf16[2,256,128]{2,1,0:T(8,128)(2,1)S(1)}, u32[]{:S(2)}, u32[]{:S(2)}) collective-permute-start(bf16[2,256,128]{2,1,0:T(8,128)(2,1)S(1)} %get-tuple-element.59), channel_id=1, source_target_pairs={{14,0},{15,1},{8,2},{9,3},{10,4},{11,5},{12,6},{13,7},{22,8},{23,9... | collective-permute-start | bytes 393224 | tf_op jit(solution)/shard_map/ppermute | solution.py:438
  61.8 0.0 collective-permute-done.10
  61.9 0.0 collective-permute-start.15
  61.9 0.0 collective-permute-done.11
  61.9 0.6 collective-permute-done.12
  62.4 0.0 collective-permute-done.13
  62.4 2.5 %collective-permute-done.14 = bf16[2,256,128]{2,1,0:T(8,128)(2,1)S(1)} collective-permute-done((bf16[2,256,128]{2,1,0:T(8,128)(2,1)S(1)}, bf16[2,256,128]{2,1,0:T(8,128)(2,1)S(1)}, u32[]{:S(2)}, u32[]{:S(2)}) %collective-permute-start.14) | collective-permute-done | bytes 131104 | tf_op jit(solution)/shard_map/ppermute | solution.py:438
  64.9 1.4 %collective-permute-done.15 = bf16[2,256,128]{2,1,0:T(8,128)(2,1)S(1)} collective-permute-done((bf16[2,256,128]{2,1,0:T(8,128)(2,1)S(1)}, bf16[2,256,128]{2,1,0:T(8,128)(2,1)S(1)}, u32[]{:S(2)}, u32[]{:S(2)}) %collective-permute-start.15) | collective-permute-done | bytes 131104 | tf_op jit(solution)/shard_map/ppermute | solution.py:438
  66.3 1.8 %unpack.1 = bf16[1,128,2,2048]{3,2,1,0:T(2,128)(2,1)} custom-call(bf16[2,128,2,128]{3,2,1,0:T(2,128)(2,1)S(1)} %bitcast.16, bf16[2,128,2,128]{3,2,1,0:T(2,128)(2,1)S(1)} %bitcast.17, bf16[2,128,2,128]{3,2,1,0:T(2,128)(2,1)S(1)} %bitcast.18, bf16[2,128,2,128]{3,2,1,0:T(2,128)(2,1)S(1)} %bitcast.19, bf16[2,128,2,128]{3,2,1,0:T(2,128)(2,1)S(1)} %bitcast.20, ...), custom_call_target="tpu_custom_call" | custom-call | tf_op jit(solution)/shard_map/unpack/pallas_call | solution.py:99
Async XLA Ops:
  0.6 1.2 %copy-start = (bf16[1,128,2,2048]{3,2,1,0:T(2,128)(2,1)S(1)}, bf16[1,128,2,2048]{3,2,1,0:T(2,128)(2,1)}, u32[]{:S(2)}) copy-start(bf16[1,128,2,2048]{3,2,1,0:T(2,128)(2,1)} %pairs_ref.1) | copy-start | bytes 3145732
  1.9 25.9 %copy-start.1 = (bf16[1,1536,256]{2,1,0:T(8,128)(2,1)S(1)}, bf16[1,1536,256]{2,1,0:T(8,128)(2,1)}, u32[]{:S(2)}) copy-start(bf16[1,1536,256]{2,1,0:T(8,128)(2,1)} %rows_ref.2) | copy-start | bytes 2359300
  1.9 26.2 %copy-start.2 = (bf16[1,1536,256]{2,1,0:T(8,128)(2,1)S(1)}, bf16[1,1536,256]{2,1,0:T(8,128)(2,1)}, u32[]{:S(2)}) copy-start(bf16[1,1536,256]{2,1,0:T(8,128)(2,1)} %rows_ref.3) | copy-start | bytes 2359300
  2.8 12.6 %collective-permute-start.1 = (bf16[2,256,128]{2,1,0:T(8,128)(2,1)S(1)}, bf16[2,256,128]{2,1,0:T(8,128)(2,1)S(1)}, u32[]{:S(2)}, u32[]{:S(2)}) collective-permute-start(bf16[2,256,128]{2,1,0:T(8,128)(2,1)S(1)} %bitcast.31), channel_id=1, source_target_pairs={{0,10},{1,11},{2,12},{3,13},{4,14},{5,15},{6,8},{7,9},{8,18},{9,19... | collective-permute-start | bytes 393224 | tf_op jit(solution)/shard_map/ppermute | solution.py:432
  6.5 18.3 %collective-permute-start.4 = (bf16[2,256,128]{2,1,0:T(8,128)(2,1)S(1)}, bf16[2,256,128]{2,1,0:T(8,128)(2,1)S(1)}, u32[]{:S(2)}, u32[]{:S(2)}) collective-permute-start(bf16[2,256,128]{2,1,0:T(8,128)(2,1)S(1)} %bitcast.30), channel_id=1, source_target_pairs={{0,13},{1,12},{2,15},{3,14},{4,9},{5,8},{6,11},{7,10},{8,21},{9,20... | collective-permute-start | bytes 393224 | tf_op jit(solution)/shard_map/ppermute | solution.py:432
  9.5 17.4 %collective-permute-start.5 = (bf16[2,256,128]{2,1,0:T(8,128)(2,1)S(1)}, bf16[2,256,128]{2,1,0:T(8,128)(2,1)S(1)}, u32[]{:S(2)}, u32[]{:S(2)}) collective-permute-start(bf16[2,256,128]{2,1,0:T(8,128)(2,1)S(1)} %bitcast.29), channel_id=1, source_target_pairs={{0,12},{1,13},{2,14},{3,15},{4,8},{5,9},{6,10},{7,11},{8,20},{9,21... | collective-permute-start | bytes 393224 | tf_op jit(solution)/shard_map/ppermute | solution.py:432
  10.1 20.1 %collective-permute-start = (bf16[2,256,128]{2,1,0:T(8,128)(2,1)S(1)}, bf16[2,256,128]{2,1,0:T(8,128)(2,1)S(1)}, u32[]{:S(2)}, u32[]{:S(2)}) collective-permute-start(bf16[2,256,128]{2,1,0:T(8,128)(2,1)S(1)} %bitcast.28), channel_id=1, source_target_pairs={{0,11},{1,10},{2,13},{3,12},{4,15},{5,14},{6,9},{7,8},{8,19},{9,18... | collective-permute-start | bytes 393224 | tf_op jit(solution)/shard_map/ppermute | solution.py:432
  11.0 19.1 %collective-permute-start.2 = (bf16[2,256,128]{2,1,0:T(8,128)(2,1)S(1)}, bf16[2,256,128]{2,1,0:T(8,128)(2,1)S(1)}, u32[]{:S(2)}, u32[]{:S(2)}) collective-permute-start(bf16[2,256,128]{2,1,0:T(8,128)(2,1)S(1)} %bitcast.27), channel_id=1, source_target_pairs={{0,15},{1,14},{2,9},{3,8},{4,11},{5,10},{6,13},{7,12},{8,23},{9,22... | collective-permute-start | bytes 393224 | tf_op jit(solution)/shard_map/ppermute | solution.py:432
  15.4 14.7 %collective-permute-start.3 = (bf16[2,256,128]{2,1,0:T(8,128)(2,1)S(1)}, bf16[2,256,128]{2,1,0:T(8,128)(2,1)S(1)}, u32[]{:S(2)}, u32[]{:S(2)}) collective-permute-start(bf16[2,256,128]{2,1,0:T(8,128)(2,1)S(1)} %bitcast.26), channel_id=1, source_target_pairs={{0,9},{1,8},{2,11},{3,10},{4,13},{5,12},{6,15},{7,14},{8,17},{9,16... | collective-permute-start | bytes 393224 | tf_op jit(solution)/shard_map/ppermute | solution.py:432
  24.8 9.3 %collective-permute-start.6 = (bf16[2,256,128]{2,1,0:T(8,128)(2,1)S(1)}, bf16[2,256,128]{2,1,0:T(8,128)(2,1)S(1)}, u32[]{:S(2)}, u32[]{:S(2)}) collective-permute-start(bf16[2,256,128]{2,1,0:T(8,128)(2,1)S(1)} %bitcast.25), channel_id=1, source_target_pairs={{0,14},{1,15},{2,8},{3,9},{4,10},{5,11},{6,12},{7,13},{8,22},{9,23... | collective-permute-start | bytes 393224 | tf_op jit(solution)/shard_map/ppermute | solution.py:432
  26.9 7.2 %collective-permute-start.7 = (bf16[2,256,128]{2,1,0:T(8,128)(2,1)S(1)}, bf16[2,256,128]{2,1,0:T(8,128)(2,1)S(1)}, u32[]{:S(2)}, u32[]{:S(2)}) collective-permute-start(bf16[2,256,128]{2,1,0:T(8,128)(2,1)S(1)} %bitcast.24), channel_id=1, source_target_pairs={{0,8},{1,9},{2,10},{3,11},{4,12},{5,13},{6,14},{7,15},{8,16},{9,17... | collective-permute-start | bytes 393224 | tf_op jit(solution)/shard_map/ppermute | solution.py:432
  38.3 13.7 %collective-permute-start.8 = (bf16[2,256,128]{2,1,0:T(8,128)(2,1)S(1)}, bf16[2,256,128]{2,1,0:T(8,128)(2,1)S(1)}, u32[]{:S(2)}, u32[]{:S(2)}) collective-permute-start(bf16[2,256,128]{2,1,0:T(8,128)(2,1)S(1)} %get-tuple-element.50), channel_id=1, source_target_pairs={{13,0},{12,1},{15,2},{14,3},{9,4},{8,5},{11,6},{10,7},{21,8},{20,9... | collective-permute-start | bytes 393224 | tf_op jit(solution)/shard_map/ppermute | solution.py:438
  42.0 12.6 %collective-permute-start.9 = (bf16[2,256,128]{2,1,0:T(8,128)(2,1)S(1)}, bf16[2,256,128]{2,1,0:T(8,128)(2,1)S(1)}, u32[]{:S(2)}, u32[]{:S(2)}) collective-permute-start(bf16[2,256,128]{2,1,0:T(8,128)(2,1)S(1)} %get-tuple-element.51), channel_id=1, source_target_pairs={{12,0},{13,1},{14,2},{15,3},{8,4},{9,5},{10,6},{11,7},{20,8},{21,9... | collective-permute-start | bytes 393224 | tf_op jit(solution)/shard_map/ppermute | solution.py:438
  47.7 14.2 %collective-permute-start.10 = (bf16[2,256,128]{2,1,0:T(8,128)(2,1)S(1)}, bf16[2,256,128]{2,1,0:T(8,128)(2,1)S(1)}, u32[]{:S(2)}, u32[]{:S(2)}) collective-permute-start(bf16[2,256,128]{2,1,0:T(8,128)(2,1)S(1)} %get-tuple-element.55), channel_id=1, source_target_pairs={{11,0},{10,1},{13,2},{12,3},{15,4},{14,5},{9,6},{8,7},{19,8},{18,9... | collective-permute-start | bytes 393224 | tf_op jit(solution)/shard_map/ppermute | solution.py:438
  47.7 14.2 %collective-permute-start.11 = (bf16[2,256,128]{2,1,0:T(8,128)(2,1)S(1)}, bf16[2,256,128]{2,1,0:T(8,128)(2,1)S(1)}, u32[]{:S(2)}, u32[]{:S(2)}) collective-permute-start(bf16[2,256,128]{2,1,0:T(8,128)(2,1)S(1)} %get-tuple-element.56), channel_id=1, source_target_pairs={{10,0},{11,1},{12,2},{13,3},{14,4},{15,5},{8,6},{9,7},{18,8},{19,9... | collective-permute-start | bytes 393224 | tf_op jit(solution)/shard_map/ppermute | solution.py:438
  51.9 10.5 %collective-permute-start.12 = (bf16[2,256,128]{2,1,0:T(8,128)(2,1)S(1)}, bf16[2,256,128]{2,1,0:T(8,128)(2,1)S(1)}, u32[]{:S(2)}, u32[]{:S(2)}) collective-permute-start(bf16[2,256,128]{2,1,0:T(8,128)(2,1)S(1)} %get-tuple-element.57), channel_id=1, source_target_pairs={{15,0},{14,1},{9,2},{8,3},{11,4},{10,5},{13,6},{12,7},{23,8},{22,9... | collective-permute-start | bytes 393224 | tf_op jit(solution)/shard_map/ppermute | solution.py:438
  52.0 10.5 %collective-permute-start.13 = (bf16[2,256,128]{2,1,0:T(8,128)(2,1)S(1)}, bf16[2,256,128]{2,1,0:T(8,128)(2,1)S(1)}, u32[]{:S(2)}, u32[]{:S(2)}) collective-permute-start(bf16[2,256,128]{2,1,0:T(8,128)(2,1)S(1)} %get-tuple-element.58), channel_id=1, source_target_pairs={{9,0},{8,1},{11,2},{10,3},{13,4},{12,5},{15,6},{14,7},{17,8},{16,9... | collective-permute-start | bytes 393224 | tf_op jit(solution)/shard_map/ppermute | solution.py:438
  57.8 7.1 %collective-permute-start.14 = (bf16[2,256,128]{2,1,0:T(8,128)(2,1)S(1)}, bf16[2,256,128]{2,1,0:T(8,128)(2,1)S(1)}, u32[]{:S(2)}, u32[]{:S(2)}) collective-permute-start(bf16[2,256,128]{2,1,0:T(8,128)(2,1)S(1)} %get-tuple-element.59), channel_id=1, source_target_pairs={{14,0},{15,1},{8,2},{9,3},{10,4},{11,5},{12,6},{13,7},{22,8},{23,9... | collective-permute-start | bytes 393224 | tf_op jit(solution)/shard_map/ppermute | solution.py:438
  61.9 4.4 %collective-permute-start.15 = (bf16[2,256,128]{2,1,0:T(8,128)(2,1)S(1)}, bf16[2,256,128]{2,1,0:T(8,128)(2,1)S(1)}, u32[]{:S(2)}, u32[]{:S(2)}) collective-permute-start(bf16[2,256,128]{2,1,0:T(8,128)(2,1)S(1)} %get-tuple-element.60), channel_id=1, source_target_pairs={{8,0},{9,1},{10,2},{11,3},{12,4},{13,5},{14,6},{15,7},{16,8},{17,9... | collective-permute-start | bytes 393224 | tf_op jit(solution)/shard_map/ppermute | solution.py:438

commit v7 on v6

--- a/solution.py
+++ b/solution.py
@@ -21,12 +21,11 @@
     seq_count = lax.axis_size("seq")
     tp_count = lax.axis_size("tp")
     near = [(0, dy) for dy in reversed(range(tp_count))]
-    order = [(dz, dy) for dz in range(1, seq_count) for dy in reversed(range(tp_count))]
-    order.sort(key=lambda o: abs(o[0] - seq_count / 2))
-    last = len(order) - 1
-    for i, offset in enumerate(near):
-        order.insert(last + 2 * i, offset)
-    return order
+    far = [(dz, dy) for dz in range(1, seq_count) for dy in reversed(range(tp_count))]
+    far.sort(key=lambda o: -abs(o[0] - seq_count / 2))
+    quarter = max(1, (len(near) + len(far)) // 4)
+    half = 2 * quarter - 1
+    return far[:1] + near[:1] + far[1:half] + far[-quarter:] + far[half:-quarter] + near[1:]
 
 
 def group_at(offset):
@@ -289,21 +288,26 @@
         join_chunks(outs, h, rows, gk_ref, gv_ref)
 
 
-def backward_kernel(back, count, first, tile, *refs):
-    chunks, refs = refs[back : back + count], refs[back + count :]
-    qt_ref, gt_ref, low_ref, stats_then, stats_ref, grad_q_in = refs[:6]
+def backward_kernel(back, counts, first, tile, *refs):
+    refs = refs[back:]
+    groups = []
+    for count in counts:
+        groups.append((refs[:count], refs[count], refs[count + 1]))
+        refs = refs[count + 2 :]
+    qt_ref, gt_ref, stats_ref, grad_q_in = refs[:4]
     if first:
-        ready_ref, rows_ref, grad_q_ref, refs = refs[6], refs[7], refs[8], refs[9:]
+        ready_ref, rows_ref, grad_q_ref, refs = refs[4], refs[5], refs[6], refs[7:]
     else:
-        rows_ref, refs = refs[6], refs[7:]
-    outs, refs = refs[:count], refs[count:]
-    v_ref, kt_ref, gk_ref, gv_ref = refs
-    heads, pair_rows, _ = chunks[0].shape
+        rows_ref, refs = refs[4], refs[5:]
+    outs, refs = refs[: sum(counts)], refs[sum(counts) :]
+    scratch = [refs[i : i + 4] for i in range(0, len(refs), 4)]
+    heads, pair_rows, _ = groups[0][0][0].shape
     rows = pair_rows // 2
-    for h in range(heads):
-        split_chunks(chunks, h, rows, v_ref=v_ref, kt_ref=kt_ref)
-    gk_ref[...] = jnp.zeros_like(gk_ref)
-    gv_ref[...] = jnp.zeros_like(gv_ref)
+    for (chunks, _, _), (v_ref, kt_ref, gk_ref, gv_ref) in zip(groups, scratch):
+        for h in range(heads):
+            split_chunks(chunks, h, rows, v_ref=v_ref, kt_ref=kt_ref)
+        gk_ref[...] = jnp.zeros_like(gk_ref)
+        gv_ref[...] = jnp.zeros_like(gv_ref)
 
     @tiles(qt_ref.shape[2] // tile)
     def _(j):
@@ -311,22 +315,21 @@
         for h in range(heads):
             columns = slice(h * HEAD, (h + 1) * HEAD)
             top, scale, row_dot = (stats_ref[h, i : i + 1, here] for i in range(3))
-            shrunk = jnp.exp2((stats_then[h, 0:1, here] - top) * EXPONENT)
-            grad_q = grad_q_in[h, :, here] + gradients(
-                low_ref[h, :, here],
-                scale * shrunk,
-                row_dot,
-                h,
-                here,
-                (qt_ref, gt_ref, v_ref, kt_ref, gk_ref, gv_ref),
-            )
+            grad_q = grad_q_in[h, :, here]
+            for (_, low_ref, then_ref), own in zip(groups, scratch):
+                shrunk = jnp.exp2((then_ref[h, 0:1, here] - top) * EXPONENT)
+                grad_q = grad_q + gradients(
+                    low_ref[h, :, here], scale * shrunk, row_dot, h, here, (qt_ref, gt_ref, *own)
+                )
             if first:
                 grad_q_ref[h, :, here] = grad_q
                 grad_q = ready_ref[h, :, here]
             rows_ref[0, here, columns] = grad_q.T.astype(rows_ref.dtype)
 
-    for h in range(heads):
-        join_chunks(outs, h, rows, gk_ref, gv_ref)
+    for count, (_, _, gk_ref, gv_ref) in zip(counts, scratch):
+        for h in range(heads):
+            join_chunks(outs[:count], h, rows, gk_ref, gv_ref)
+        outs = outs[count:]
 
 
 def cost(heads, rows, tokens, matmuls):
@@ -348,7 +351,8 @@
     rows_shape = jax.ShapeDtypeStruct(queries.shape, queries.dtype)
     compiler_params = params(enc_len)
     quarter = max(1, len(arrived) // 4)
-    cuts = [0, quarter, len(arrived) - quarter, len(arrived)]
+    cuts = [0, quarter, 2 * quarter, 3 * quarter, len(arrived)]
+    groups = [arrived[a:b] for a, b in zip(cuts[:-1], cuts[1:])]
 
     def natural(count):
         return pltpu.VMEM((heads, count * rows, HEAD), jnp.bfloat16)
@@ -366,8 +370,8 @@
         return [jax.ShapeDtypeStruct(c.shape, c.dtype) for c in group]
 
     state, kept = [], []
-    for begin, end in zip(cuts[:2], cuts[1:3]):
-        group, count = arrived[begin:end], end - begin
+    for group in groups[:-1]:
+        count = len(group)
         stats, context, low = pl.pallas_call(
             functools.partial(forward_kernel, count, not state, tile_of(count * rows, tokens)),
             out_shape=[stats_shape, wide_shape, low_of(count)],
@@ -381,7 +385,7 @@
         state = [stats, context]
         kept.append((low, stats))
 
-    far, group = arrived[: cuts[1]], arrived[cuts[2] :]
+    far, group = groups[-2], groups[-1]
     others, count = len(far), len(group)
     final, context, low, grad_q, *grads = pl.pallas_call(
         functools.partial(turn_kernel, count, others, tile_of(count * rows, tokens)),
@@ -393,32 +397,41 @@
         compiler_params=compiler_params,
         cost_estimate=cost(heads, count * rows, tokens, 6),
         name="turn",
-    )(*group, *far, qt, gt, *state, *kept[0])
+    )(*group, *far, qt, gt, *state, *kept[-1])
     kept.append((low, final))
-    returned = [send_back(0, grads)]
-
-    for i, (begin, end) in enumerate(zip(cuts[1:3], cuts[2:])):
-        group, count = arrived[begin:end], end - begin
-        first = i == 0
+    returned = [send_back(cuts[-3], grads)]
+
+    for first, part in ((True, [1, 3]), (False, [0])):
+        counts = [len(groups[i]) for i in part]
         back = [] if first else returned[0]
+        operands = []
+        for i in part:
+            operands += [*groups[i], *kept[i]]
         shapes = [rows_shape, wide_shape] if first else [rows_shape]
         outs = pl.pallas_call(
             functools.partial(
-                backward_kernel, len(back), count, first, tile_of(count * rows, tokens)
+                backward_kernel, len(back), counts, first, tile_of(max(counts) * rows, tokens)
             ),
-            out_shape=shapes + shapes_of(group),
-            in_specs=[ANY] * len(back) + [VMEM] * (count + 6 + first),
-            out_specs=[VMEM] * (len(shapes) + count),
-            scratch_shapes=[natural(count), across(count)] + [sums(count)] * 2,
+            out_shape=shapes + shapes_of(sum((groups[i] for i in part), [])),
+            in_specs=[ANY] * len(back) + [VMEM] * (len(operands) + 4 + first),
+            out_specs=[VMEM] * (len(shapes) + sum(counts)),
+            scratch_shapes=[
+                shape
+                for count in counts
+                for shape in (natural(count), across(count), sums(count), sums(count))
+            ],
             compiler_params=compiler_params,
-            cost_estimate=cost(heads, count * rows, tokens, 4),
+            cost_estimate=cost(heads, sum(counts) * rows, tokens, 4),
             name="backward",
-        )(*back, *group, qt, gt, *kept[i + 1], final, grad_q, *([context] if first else []))
+        )(*back, *operands, qt, gt, final, grad_q, *([context] if first else []))
         if first:
             context_rows, grad_q = outs[:2]
         else:
             grad_query = outs[0]
-        returned.append(send_back(begin, outs[len(shapes) :]))
+        blocks = list(outs[len(shapes) :])
+        for i in part:
+            returned.append(send_back(cuts[i], blocks[: len(groups[i])]))
+            blocks = blocks[len(groups[i]) :]
     return context_rows, grad_query, returned
 
 

time: 68.2 us -> 69.3 us (1.016)
  the two profiles are of different devices: /device:TPU:1 before, /device:TPU:0 now
where the time goes in v7:
time: 69.3 us; the launch traced here: 67.9 us
  starting transfers between devices  28.4 us (41%)
  Pallas kernels  21.5 us (31%)
  waiting for transfers between devices  16 us (23%)
  local copies, waits for them, and re-layouts  1.23 us (2%)
  between operations  0.75 us (1%)
    ppermute x8, starting transfers between devices, shards(): arrived.append(lax.ppermute(block, AXES, route(offset, False)))  15.6 us
    ppermute x8, starting transfers between devices, send_back(): lax.ppermute(b, AXES, route(o, True))  12.8 us
    pallas_call x2, Pallas kernels, attend(): pl.pallas_call(functools.partial(backward_kernel, len(back), counts, firs...  8.54 us
    ppermute x8, waiting for transfers between devices, shards(): arrived.append(lax.ppermute(block, AXES, route(offset, False)))  8.31 us
    ppermute x8, waiting for transfers between devices, send_back(): lax.ppermute(b, AXES, route(o, True))  7.68 us
    pallas_call x3, Pallas kernels, attend(): pl.pallas_call(functools.partial(forward_kernel, count, not state, tile_o...  5.51 us
    pallas_call x1, Pallas kernels, attend(): pl.pallas_call(functools.partial(turn_kernel, count, others, tile_of(coun...  4.22 us
    pallas_call x1, Pallas kernels, unpack(): pl.pallas_call(kernel, out_shape=jax.ShapeDtypeStruct((1, rows, 2, width)...  1.78 us
  transfers between devices with their start and end apart: 16, of which 7 were waited for; matrix products, arithmetic and copies ran while one was open for 0% of the time, Pallas kernels for 21%

profile of v7, /device:TPU:0, one launch (start us, length us, event | category | flops | bytes accessed | tf_op | source)
XLA Modules:
  0.0 67.9 jit_solution(10151679435501478707)
XLA Ops:
  0.6 0.0 copy-start
  0.6 1.2 %copy-done = bf16[1,128,2,2048]{3,2,1,0:T(2,128)(2,1)S(1)} copy-done((bf16[1,128,2,2048]{3,2,1,0:T(2,128)(2,1)S(1)}, bf16[1,128,2,2048]{3,2,1,0:T(2,128)(2,1)}, u32[]{:S(2)}) %copy-start) | copy-done | bytes 1048600
  1.9 0.0 copy-start.1
  1.9 0.0 copy-start.2
  1.9 0.9 %pack.1 = (bf16[2,128,2,128]{3,2,1,0:T(2,128)(2,1)S(1)}, bf16[2,128,2,128]{3,2,1,0:T(2,128)(2,1)S(1)}, bf16[2,128,2,128]{3,2,1,0:T(2,128)(2,1)S(1)}, bf16[2,128,...) custom-call(bf16[1,128,2,2048]{3,2,1,0:T(2,128)(2,1)S(1)} %copy-done), custom_call_target="tpu_custom_call" | custom-call | tf_op jit(solution)/shard_map/pack/pallas_call | solution.py:72
  2.8 5.5 %collective-permute-start.1 = (bf16[2,256,128]{2,1,0:T(8,128)(2,1)S(1)}, bf16[2,256,128]{2,1,0:T(8,128)(2,1)S(1)}, u32[]{:S(2)}, u32[]{:S(2)}) collective-permute-start(bf16[2,256,128]{2,1,0:T(8,128)(2,1)S(1)} %bitcast.31), channel_id=1, source_target_pairs={{0,15},{1,14},{2,9},{3,8},{4,11},{5,10},{6,13},{7,12},{8,23},{9,22... | collective-permute-start | bytes 393224 | tf_op jit(solution)/shard_map/ppermute | solution.py:445
  8.3 0.0 collective-permute-start.2
  8.3 1.7 %collective-permute-start.3 = (bf16[2,256,128]{2,1,0:T(8,128)(2,1)S(1)}, bf16[2,256,128]{2,1,0:T(8,128)(2,1)S(1)}, u32[]{:S(2)}, u32[]{:S(2)}) collective-permute-start(bf16[2,256,128]{2,1,0:T(8,128)(2,1)S(1)} %bitcast.29), channel_id=1, source_target_pairs={{0,9},{1,8},{2,11},{3,10},{4,13},{5,12},{6,15},{7,14},{8,17},{9,16... | collective-permute-start | bytes 393224 | tf_op jit(solution)/shard_map/ppermute | solution.py:445
  10.0 0.6 collective-permute-start
  10.7 3.8 %collective-permute-start.6 = (bf16[2,256,128]{2,1,0:T(8,128)(2,1)S(1)}, bf16[2,256,128]{2,1,0:T(8,128)(2,1)S(1)}, u32[]{:S(2)}, u32[]{:S(2)}) collective-permute-start(bf16[2,256,128]{2,1,0:T(8,128)(2,1)S(1)} %bitcast.27), channel_id=1, source_target_pairs={{0,13},{1,12},{2,15},{3,14},{4,9},{5,8},{6,11},{7,10},{8,21},{9,20... | collective-permute-start | bytes 393224 | tf_op jit(solution)/shard_map/ppermute | solution.py:445
  14.5 0.0 collective-permute-done.1.refs_1_
  14.5 0.0 collective-permute-start.7
  14.5 2.5 %collective-permute-done.2.refs_0_.refs_2_ = bf16[2,256,128]{2,1,0:T(8,128)(2,1)S(1)} collective-permute-done((bf16[2,256,128]{2,1,0:T(8,128)(2,1)S(1)}, bf16[2,256,128]{2,1,0:T(8,128)(2,1)S(1)}, u32[]{:S(2)}, u32[]{:S(2)}) %collective-permute-start.2) | collective-permute-done | bytes 131104 | tf_op jit(solution)/shard_map/ppermute | solution.py:445
  17.0 2.4 %collective-permute-start.4 = (bf16[2,256,128]{2,1,0:T(8,128)(2,1)S(1)}, bf16[2,256,128]{2,1,0:T(8,128)(2,1)S(1)}, u32[]{:S(2)}, u32[]{:S(2)}) collective-permute-start(bf16[2,256,128]{2,1,0:T(8,128)(2,1)S(1)} %bitcast.25), channel_id=1, source_target_pairs={{0,14},{1,15},{2,8},{3,9},{4,10},{5,11},{6,12},{7,13},{8,22},{9,23... | collective-permute-start | bytes 393224 | tf_op jit(solution)/shard_map/ppermute | solution.py:445
  19.4 0.0 collective-permute-done.3.refs_1_.refs_3_
  19.4 1.5 %collective-permute-start.5 = (bf16[2,256,128]{2,1,0:T(8,128)(2,1)S(1)}, bf16[2,256,128]{2,1,0:T(8,128)(2,1)S(1)}, u32[]{:S(2)}, u32[]{:S(2)}) collective-permute-start(bf16[2,256,128]{2,1,0:T(8,128)(2,1)S(1)} %bitcast.24), channel_id=1, source_target_pairs={{0,8},{1,9},{2,10},{3,11},{4,12},{5,13},{6,14},{7,15},{8,16},{9,17... | collective-permute-start | bytes 393224 | tf_op jit(solution)/shard_map/ppermute | solution.py:445
  20.9 0.0 copy-done.1
  20.9 0.3 turned.2.refs_2_.refs_4_.refs_8_.refs_6_
  21.2 0.0 copy-done.2
  21.2 0.3 turned.3.refs_5_.refs_9_.refs_7_
  21.5 1.8 %forward.3 = (f32[2,8,1536]{2,1,0:T(8,128)S(1)}, f32[2,128,1536]{2,1,0:T(8,128)S(1)}, bf16[2,256,1536]{2,1,0:T(8,128)(2,1)S(1)}) custom-call(bf16[2,256,128]{2,1,0:T(8,128)(2,1)S(1)} %collective-permute-done.2.refs_0_.refs_2_, bf16[2,256,128]{2,1,0:T(8,128)(2,1)S(1)} %collective-permute-done.3.refs_1_.refs_3_, ...), custom_call_target="tpu_custom_call" | custom-call | flops 402653184 | bytes 3670016 | tf_op jit(solution)/shard_map/forward/pallas_call | solution.py:375
  23.3 0.0 collective-permute-done.refs_0_
  23.3 1.8 %forward.4 = (f32[2,8,1536]{2,1,0:T(8,128)S(1)}, f32[2,128,1536]{2,1,0:T(8,128)S(1)}, bf16[2,256,1536]{2,1,0:T(8,128)(2,1)S(1)}) custom-call(bf16[2,256,128]{2,1,0:T(8,128)(2,1)S(1)} %collective-permute-done.refs_0_, bf16[2,256,128]{2,1,0:T(8,128)(2,1)S(1)} %collective-permute-done.1.refs_1_, ...), custom_call_target="tpu_custom_call" | custom-call | flops 402653184 | bytes 3670016 | tf_op jit(solution)/shard_map/forward/pallas_call | solution.py:375
  25.2 3.7 %collective-permute-done.6.refs_0_.refs_2_ = bf16[2,256,128]{2,1,0:T(8,128)(2,1)S(1)} collective-permute-done((bf16[2,256,128]{2,1,0:T(8,128)(2,1)S(1)}, bf16[2,256,128]{2,1,0:T(8,128)(2,1)S(1)}, u32[]{:S(2)}, u32[]{:S(2)}) %collective-permute-start.6) | collective-permute-done | bytes 131104 | tf_op jit(solution)/shard_map/ppermute | solution.py:445
  28.9 2.2 %collective-permute-done.7.refs_1_.refs_3_ = bf16[2,256,128]{2,1,0:T(8,128)(2,1)S(1)} collective-permute-done((bf16[2,256,128]{2,1,0:T(8,128)(2,1)S(1)}, bf16[2,256,128]{2,1,0:T(8,128)(2,1)S(1)}, u32[]{:S(2)}, u32[]{:S(2)}) %collective-permute-start.7) | collective-permute-done | bytes 131104 | tf_op jit(solution)/shard_map/ppermute | solution.py:445
  31.0 1.8 %forward.5 = (f32[2,8,1536]{2,1,0:T(8,128)S(1)}, f32[2,128,1536]{2,1,0:T(8,128)S(1)}, bf16[2,256,1536]{2,1,0:T(8,128)(2,1)S(1)}) custom-call(bf16[2,256,128]{2,1,0:T(8,128)(2,1)S(1)} %collective-permute-done.6.refs_0_.refs_2_, bf16[2,256,128]{2,1,0:T(8,128)(2,1)S(1)} %collective-permute-done.7.refs_1_.refs_3_, ...), custom_call_target="tpu_custom_call" | custom-call | flops 402653184 | bytes 3670016 | tf_op jit(solution)/shard_map/forward/pallas_call | solution.py:375
  32.9 0.0 collective-permute-done.4.refs_0_.refs_4_
  32.9 0.0 collective-permute-done.5.refs_1_.refs_5_
  32.9 4.2 %turn.1 = (f32[2,8,1536]{2,1,0:T(8,128)S(1)}, f32[2,128,1536]{2,1,0:T(8,128)S(1)}, bf16[2,256,1536]{2,1,0:T(8,128)(2,1)S(1)}, f32[2,128,1536]{2,1,0:T(8,128)S(1)...) custom-call(bf16[2,256,128]{2,1,0:T(8,128)(2,1)S(1)} %collective-permute-done.4.refs_0_.refs_4_, ...), custom_call_target="tpu_custom_call" | custom-call | flops 1207959552 | bytes 3670016 | tf_op jit(solution)/shard_map/turn/pallas_call | solution.py:390
  37.1 0.9 %collective-permute-start.8 = (bf16[2,256,128]{2,1,0:T(8,128)(2,1)S(1)}, bf16[2,256,128]{2,1,0:T(8,128)(2,1)S(1)}, u32[]{:S(2)}, u32[]{:S(2)}) collective-permute-start(bf16[2,256,128]{2,1,0:T(8,128)(2,1)S(1)} %get-tuple-element.56), channel_id=1, source_target_pairs={{13,0},{12,1},{15,2},{14,3},{9,4},{8,5},{11,6},{10,7},{21,8},{20,9... | collective-permute-start | bytes 393224 | tf_op jit(solution)/shard_map/ppermute | solution.py:451
  38.0 3.4 %collective-permute-start.9 = (bf16[2,256,128]{2,1,0:T(8,128)(2,1)S(1)}, bf16[2,256,128]{2,1,0:T(8,128)(2,1)S(1)}, u32[]{:S(2)}, u32[]{:S(2)}) collective-permute-start(bf16[2,256,128]{2,1,0:T(8,128)(2,1)S(1)} %get-tuple-element.57), channel_id=1, source_target_pairs={{12,0},{13,1},{14,2},{15,3},{8,4},{9,5},{10,6},{11,7},{20,8},{21,9... | collective-permute-start | bytes 393224 | tf_op jit(solution)/shard_map/ppermute | solution.py:451
  41.5 5.3 %backward.2 = (bf16[1,1536,256]{2,1,0:T(8,128)(2,1)}, f32[2,128,1536]{2,1,0:T(8,128)S(1)}, bf16[2,256,128]{2,1,0:T(8,128)(2,1)S(1)}, bf16[2,256,128]{2,1,0:T(8,1...) custom-call(bf16[2,256,128]{2,1,0:T(8,128)(2,1)S(1)} %collective-permute-done.refs_0_, ...), custom_call_target="tpu_custom_call" | custom-call | flops 1610612736 | bytes 4194304 | tf_op jit(solution)/shard_map/backward/pallas_call | solution.py:411
  46.8 3.6 %collective-permute-start.10 = (bf16[2,256,128]{2,1,0:T(8,128)(2,1)S(1)}, bf16[2,256,128]{2,1,0:T(8,128)(2,1)S(1)}, u32[]{:S(2)}, u32[]{:S(2)}) collective-permute-start(bf16[2,256,128]{2,1,0:T(8,128)(2,1)S(1)} %get-tuple-element.61), channel_id=1, source_target_pairs={{10,0},{11,1},{12,2},{13,3},{14,4},{15,5},{8,6},{9,7},{18,8},{19,9... | collective-permute-start | bytes 393224 | tf_op jit(solution)/shard_map/ppermute | solution.py:451
  50.4 0.0 collective-permute-start.11
  50.4 0.0 collective-permute-start.12
  50.4 0.0 collective-permute-done.8.refs_0_
  50.4 1.4 %collective-permute-start.13 = (bf16[2,256,128]{2,1,0:T(8,128)(2,1)S(1)}, bf16[2,256,128]{2,1,0:T(8,128)(2,1)S(1)}, u32[]{:S(2)}, u32[]{:S(2)}) collective-permute-start(bf16[2,256,128]{2,1,0:T(8,128)(2,1)S(1)} %get-tuple-element.64), channel_id=1, source_target_pairs={{8,0},{9,1},{10,2},{11,3},{12,4},{13,5},{14,6},{15,7},{16,8},{17,9... | collective-permute-start | bytes 393224 | tf_op jit(solution)/shard_map/ppermute | solution.py:451
  51.7 0.9 %collective-permute-done.9.refs_1_ = bf16[2,256,128]{2,1,0:T(8,128)(2,1)S(1)} collective-permute-done((bf16[2,256,128]{2,1,0:T(8,128)(2,1)S(1)}, bf16[2,256,128]{2,1,0:T(8,128)(2,1)S(1)}, u32[]{:S(2)}, u32[]{:S(2)}) %collective-permute-start.9) | collective-permute-done | bytes 131104 | tf_op jit(solution)/shard_map/ppermute | solution.py:451
  52.7 3.2 %backward.3 = (bf16[1,1536,256]{2,1,0:T(8,128)(2,1)}, bf16[2,256,128]{2,1,0:T(8,128)(2,1)S(1)}, bf16[2,256,128]{2,1,0:T(8,128)(2,1)S(1)}) custom-call(bf16[2,256,128]{2,1,0:T(8,128)(2,1)S(1)} %collective-permute-done.8.refs_0_, bf16[2,256,128]{2,1,0:T(8,128)(2,1)S(1)} %collective-permute-done.9.refs_1_, ...), custom_call_target="tpu_custom_call" | custom-call | flops 805306368 | bytes 3670016 | tf_op jit(solution)/shard_map/backward/pallas_call | solution.py:411
  55.9 3.5 %collective-permute-start.14 = (bf16[2,256,128]{2,1,0:T(8,128)(2,1)S(1)}, bf16[2,256,128]{2,1,0:T(8,128)(2,1)S(1)}, u32[]{:S(2)}, u32[]{:S(2)}) collective-permute-start(bf16[2,256,128]{2,1,0:T(8,128)(2,1)S(1)} %get-tuple-element.65), channel_id=1, source_target_pairs={{11,0},{10,1},{13,2},{12,3},{15,4},{14,5},{9,6},{8,7},{19,8},{18,9... | collective-permute-start | bytes 393224 | tf_op jit(solution)/shard_map/ppermute | solution.py:451
  59.4 2.0 %collective-permute-done.10 = bf16[2,256,128]{2,1,0:T(8,128)(2,1)S(1)} collective-permute-done((bf16[2,256,128]{2,1,0:T(8,128)(2,1)S(1)}, bf16[2,256,128]{2,1,0:T(8,128)(2,1)S(1)}, u32[]{:S(2)}, u32[]{:S(2)}) %collective-permute-start.10) | collective-permute-done | bytes 131104 | tf_op jit(solution)/shard_map/ppermute | solution.py:451
  61.4 0.0 collective-permute-start.15
  61.4 0.0 collective-permute-done.11
  61.4 0.0 collective-permute-done.12
  61.4 0.0 collective-permute-done.13
  61.4 3.0 %collective-permute-done.14 = bf16[2,256,128]{2,1,0:T(8,128)(2,1)S(1)} collective-permute-done((bf16[2,256,128]{2,1,0:T(8,128)(2,1)S(1)}, bf16[2,256,128]{2,1,0:T(8,128)(2,1)S(1)}, u32[]{:S(2)}, u32[]{:S(2)}) %collective-permute-start.14) | collective-permute-done | bytes 131104 | tf_op jit(solution)/shard_map/ppermute | solution.py:451
  64.4 1.8 %collective-permute-done.15 = bf16[2,256,128]{2,1,0:T(8,128)(2,1)S(1)} collective-permute-done((bf16[2,256,128]{2,1,0:T(8,128)(2,1)S(1)}, bf16[2,256,128]{2,1,0:T(8,128)(2,1)S(1)}, u32[]{:S(2)}, u32[]{:S(2)}) %collective-permute-start.15) | collective-permute-done | bytes 131104 | tf_op jit(solution)/shard_map/ppermute | solution.py:451
  66.1 1.8 %unpack.1 = bf16[1,128,2,2048]{3,2,1,0:T(2,128)(2,1)} custom-call(bf16[2,128,2,128]{3,2,1,0:T(2,128)(2,1)S(1)} %bitcast.16, bf16[2,128,2,128]{3,2,1,0:T(2,128)(2,1)S(1)} %bitcast.17, bf16[2,128,2,128]{3,2,1,0:T(2,128)(2,1)S(1)} %bitcast.18, bf16[2,128,2,128]{3,2,1,0:T(2,128)(2,1)S(1)} %bitcast.19, bf16[2,128,2,128]{3,2,1,0:T(2,128)(2,1)S(1)} %bitcast.20, ...), custom_call_target="tpu_custom_call" | custom-call | tf_op jit(solution)/shard_map/unpack/pallas_call | solution.py:98
Async XLA Ops:
  0.6 1.2 %copy-start = (bf16[1,128,2,2048]{3,2,1,0:T(2,128)(2,1)S(1)}, bf16[1,128,2,2048]{3,2,1,0:T(2,128)(2,1)}, u32[]{:S(2)}) copy-start(bf16[1,128,2,2048]{3,2,1,0:T(2,128)(2,1)} %pairs_ref.1) | copy-start | bytes 3145732
  1.9 19.1 %copy-start.1 = (bf16[1,1536,256]{2,1,0:T(8,128)(2,1)S(1)}, bf16[1,1536,256]{2,1,0:T(8,128)(2,1)}, u32[]{:S(2)}) copy-start(bf16[1,1536,256]{2,1,0:T(8,128)(2,1)} %rows_ref.2) | copy-start | bytes 2359300
  1.9 19.4 %copy-start.2 = (bf16[1,1536,256]{2,1,0:T(8,128)(2,1)S(1)}, bf16[1,1536,256]{2,1,0:T(8,128)(2,1)}, u32[]{:S(2)}) copy-start(bf16[1,1536,256]{2,1,0:T(8,128)(2,1)} %rows_ref.3) | copy-start | bytes 2359300
  2.8 11.7 %collective-permute-start.1 = (bf16[2,256,128]{2,1,0:T(8,128)(2,1)S(1)}, bf16[2,256,128]{2,1,0:T(8,128)(2,1)S(1)}, u32[]{:S(2)}, u32[]{:S(2)}) collective-permute-start(bf16[2,256,128]{2,1,0:T(8,128)(2,1)S(1)} %bitcast.31), channel_id=1, source_target_pairs={{0,15},{1,14},{2,9},{3,8},{4,11},{5,10},{6,13},{7,12},{8,23},{9,22... | collective-permute-start | bytes 393224 | tf_op jit(solution)/shard_map/ppermute | solution.py:445
  8.3 8.7 %collective-permute-start.2 = (bf16[2,256,128]{2,1,0:T(8,128)(2,1)S(1)}, bf16[2,256,128]{2,1,0:T(8,128)(2,1)S(1)}, u32[]{:S(2)}, u32[]{:S(2)}) collective-permute-start(bf16[2,256,128]{2,1,0:T(8,128)(2,1)S(1)} %bitcast.30), channel_id=1, source_target_pairs={{0,11},{1,10},{2,13},{3,12},{4,15},{5,14},{6,9},{7,8},{8,19},{9,18... | collective-permute-start | bytes 393224 | tf_op jit(solution)/shard_map/ppermute | solution.py:445
  8.3 11.1 %collective-permute-start.3 = (bf16[2,256,128]{2,1,0:T(8,128)(2,1)S(1)}, bf16[2,256,128]{2,1,0:T(8,128)(2,1)S(1)}, u32[]{:S(2)}, u32[]{:S(2)}) collective-permute-start(bf16[2,256,128]{2,1,0:T(8,128)(2,1)S(1)} %bitcast.29), channel_id=1, source_target_pairs={{0,9},{1,8},{2,11},{3,10},{4,13},{5,12},{6,15},{7,14},{8,17},{9,16... | collective-permute-start | bytes 393224 | tf_op jit(solution)/shard_map/ppermute | solution.py:445
  10.0 13.3 %collective-permute-start = (bf16[2,256,128]{2,1,0:T(8,128)(2,1)S(1)}, bf16[2,256,128]{2,1,0:T(8,128)(2,1)S(1)}, u32[]{:S(2)}, u32[]{:S(2)}) collective-permute-start(bf16[2,256,128]{2,1,0:T(8,128)(2,1)S(1)} %bitcast.28), channel_id=1, source_target_pairs={{0,10},{1,11},{2,12},{3,13},{4,14},{5,15},{6,8},{7,9},{8,18},{9,19... | collective-permute-start | bytes 393224 | tf_op jit(solution)/shard_map/ppermute | solution.py:445
  10.7 18.2 %collective-permute-start.6 = (bf16[2,256,128]{2,1,0:T(8,128)(2,1)S(1)}, bf16[2,256,128]{2,1,0:T(8,128)(2,1)S(1)}, u32[]{:S(2)}, u32[]{:S(2)}) collective-permute-start(bf16[2,256,128]{2,1,0:T(8,128)(2,1)S(1)} %bitcast.27), channel_id=1, source_target_pairs={{0,13},{1,12},{2,15},{3,14},{4,9},{5,8},{6,11},{7,10},{8,21},{9,20... | collective-permute-start | bytes 393224 | tf_op jit(solution)/shard_map/ppermute | solution.py:445
  14.5 16.5 %collective-permute-start.7 = (bf16[2,256,128]{2,1,0:T(8,128)(2,1)S(1)}, bf16[2,256,128]{2,1,0:T(8,128)(2,1)S(1)}, u32[]{:S(2)}, u32[]{:S(2)}) collective-permute-start(bf16[2,256,128]{2,1,0:T(8,128)(2,1)S(1)} %bitcast.26), channel_id=1, source_target_pairs={{0,12},{1,13},{2,14},{3,15},{4,8},{5,9},{6,10},{7,11},{8,20},{9,21... | collective-permute-start | bytes 393224 | tf_op jit(solution)/shard_map/ppermute | solution.py:445
  17.0 15.9 %collective-permute-start.4 = (bf16[2,256,128]{2,1,0:T(8,128)(2,1)S(1)}, bf16[2,256,128]{2,1,0:T(8,128)(2,1)S(1)}, u32[]{:S(2)}, u32[]{:S(2)}) collective-permute-start(bf16[2,256,128]{2,1,0:T(8,128)(2,1)S(1)} %bitcast.25), channel_id=1, source_target_pairs={{0,14},{1,15},{2,8},{3,9},{4,10},{5,11},{6,12},{7,13},{8,22},{9,23... | collective-permute-start | bytes 393224 | tf_op jit(solution)/shard_map/ppermute | solution.py:445
  19.4 13.4 %collective-permute-start.5 = (bf16[2,256,128]{2,1,0:T(8,128)(2,1)S(1)}, bf16[2,256,128]{2,1,0:T(8,128)(2,1)S(1)}, u32[]{:S(2)}, u32[]{:S(2)}) collective-permute-start(bf16[2,256,128]{2,1,0:T(8,128)(2,1)S(1)} %bitcast.24), channel_id=1, source_target_pairs={{0,8},{1,9},{2,10},{3,11},{4,12},{5,13},{6,14},{7,15},{8,16},{9,17... | collective-permute-start | bytes 393224 | tf_op jit(solution)/shard_map/ppermute | solution.py:445
  37.1 13.3 %collective-permute-start.8 = (bf16[2,256,128]{2,1,0:T(8,128)(2,1)S(1)}, bf16[2,256,128]{2,1,0:T(8,128)(2,1)S(1)}, u32[]{:S(2)}, u32[]{:S(2)}) collective-permute-start(bf16[2,256,128]{2,1,0:T(8,128)(2,1)S(1)} %get-tuple-element.56), channel_id=1, source_target_pairs={{13,0},{12,1},{15,2},{14,3},{9,4},{8,5},{11,6},{10,7},{21,8},{20,9... | collective-permute-start | bytes 393224 | tf_op jit(solution)/shard_map/ppermute | solution.py:451
  38.0 14.7 %collective-permute-start.9 = (bf16[2,256,128]{2,1,0:T(8,128)(2,1)S(1)}, bf16[2,256,128]{2,1,0:T(8,128)(2,1)S(1)}, u32[]{:S(2)}, u32[]{:S(2)}) collective-permute-start(bf16[2,256,128]{2,1,0:T(8,128)(2,1)S(1)} %get-tuple-element.57), channel_id=1, source_target_pairs={{12,0},{13,1},{14,2},{15,3},{8,4},{9,5},{10,6},{11,7},{20,8},{21,9... | collective-permute-start | bytes 393224 | tf_op jit(solution)/shard_map/ppermute | solution.py:451
  46.8 14.6 %collective-permute-start.10 = (bf16[2,256,128]{2,1,0:T(8,128)(2,1)S(1)}, bf16[2,256,128]{2,1,0:T(8,128)(2,1)S(1)}, u32[]{:S(2)}, u32[]{:S(2)}) collective-permute-start(bf16[2,256,128]{2,1,0:T(8,128)(2,1)S(1)} %get-tuple-element.61), channel_id=1, source_target_pairs={{10,0},{11,1},{12,2},{13,3},{14,4},{15,5},{8,6},{9,7},{18,8},{19,9... | collective-permute-start | bytes 393224 | tf_op jit(solution)/shard_map/ppermute | solution.py:451
  50.4 11.0 %collective-permute-start.11 = (bf16[2,256,128]{2,1,0:T(8,128)(2,1)S(1)}, bf16[2,256,128]{2,1,0:T(8,128)(2,1)S(1)}, u32[]{:S(2)}, u32[]{:S(2)}) collective-permute-start(bf16[2,256,128]{2,1,0:T(8,128)(2,1)S(1)} %get-tuple-element.62), channel_id=1, source_target_pairs={{15,0},{14,1},{9,2},{8,3},{11,4},{10,5},{13,6},{12,7},{23,8},{22,9... | collective-permute-start | bytes 393224 | tf_op jit(solution)/shard_map/ppermute | solution.py:451
  50.4 11.0 %collective-permute-start.12 = (bf16[2,256,128]{2,1,0:T(8,128)(2,1)S(1)}, bf16[2,256,128]{2,1,0:T(8,128)(2,1)S(1)}, u32[]{:S(2)}, u32[]{:S(2)}) collective-permute-start(bf16[2,256,128]{2,1,0:T(8,128)(2,1)S(1)} %get-tuple-element.63), channel_id=1, source_target_pairs={{14,0},{15,1},{8,2},{9,3},{10,4},{11,5},{12,6},{13,7},{22,8},{23,9... | collective-permute-start | bytes 393224 | tf_op jit(solution)/shard_map/ppermute | solution.py:451
  50.4 11.0 %collective-permute-start.13 = (bf16[2,256,128]{2,1,0:T(8,128)(2,1)S(1)}, bf16[2,256,128]{2,1,0:T(8,128)(2,1)S(1)}, u32[]{:S(2)}, u32[]{:S(2)}) collective-permute-start(bf16[2,256,128]{2,1,0:T(8,128)(2,1)S(1)} %get-tuple-element.64), channel_id=1, source_target_pairs={{8,0},{9,1},{10,2},{11,3},{12,4},{13,5},{14,6},{15,7},{16,8},{17,9... | collective-permute-start | bytes 393224 | tf_op jit(solution)/shard_map/ppermute | solution.py:451
  55.9 8.5 %collective-permute-start.14 = (bf16[2,256,128]{2,1,0:T(8,128)(2,1)S(1)}, bf16[2,256,128]{2,1,0:T(8,128)(2,1)S(1)}, u32[]{:S(2)}, u32[]{:S(2)}) collective-permute-start(bf16[2,256,128]{2,1,0:T(8,128)(2,1)S(1)} %get-tuple-element.65), channel_id=1, source_target_pairs={{11,0},{10,1},{13,2},{12,3},{15,4},{14,5},{9,6},{8,7},{19,8},{18,9... | collective-permute-start | bytes 393224 | tf_op jit(solution)/shard_map/ppermute | solution.py:451
  61.4 4.8 %collective-permute-start.15 = (bf16[2,256,128]{2,1,0:T(8,128)(2,1)S(1)}, bf16[2,256,128]{2,1,0:T(8,128)(2,1)S(1)}, u32[]{:S(2)}, u32[]{:S(2)}) collective-permute-start(bf16[2,256,128]{2,1,0:T(8,128)(2,1)S(1)} %get-tuple-element.66), channel_id=1, source_target_pairs={{9,0},{8,1},{11,2},{10,3},{13,4},{12,5},{15,6},{14,7},{17,8},{16,9... | collective-permute-start | bytes 393224 | tf_op jit(solution)/shard_map/ppermute | solution.py:451

commit v8 on v7

v8 whole, which is shorter than its diff:
```python
import functools

import jax
import jax.numpy as jnp
from jax import lax
from jax.experimental import pallas as pl
from jax.experimental.pallas import tpu as pltpu
from jax.sharding import PartitionSpec as P

HEAD = 128
AXES = ("segment", "seq", "tp")
FACTOR = HEAD**-0.5
EXPONENT = FACTOR * 1.4426950408889634
MIB = 1 << 20
NT = ((1,), (1,))
ANY = pl.BlockSpec(memory_space=pl.ANY)
HBM = pl.BlockSpec(memory_space=pltpu.HBM)
VMEM = pl.BlockSpec(memory_space=pltpu.VMEM)


def offsets():
    seq_count = lax.axis_size("seq")
    tp_count = lax.axis_size("tp")
    near = [(0, dy) for dy in reversed(range(tp_count))]
    far = [(dz, dy) for dz in range(1, seq_count) for dy in reversed(range(tp_count))]
    far.sort(key=lambda o: -abs(o[0] - seq_count / 2))
    quarter = max(1, (len(near) + len(far)) // 4)
    return far[:1] + near[:1] + far[1:-quarter] + near[1:] + far[-quarter:]


def group_at(offset):
    seq_count = lax.axis_size("seq")
    tp_count = lax.axis_size("tp")
    z = lax.rem(lax.axis_index("seq") + offset[0], seq_count)
    y = lax.rem(lax.axis_index("tp") + offset[1], tp_count)
    return z * tp_count + y


def route(offset, back):
    segments, seq_count, tp_count = (lax.axis_size(a) for a in AXES)
    hops = []
    for s in range(segments):
        for z in range(seq_count):
            for y in range(tp_count):
                source = (s * seq_count + z) * tp_count + y
                s_to = (s + 1) % segments
                z_to = (z + offset[0]) % seq_count
                y_to = (y + offset[1]) % tp_count
                target = (s_to * seq_count + z_to) * tp_count + y_to
                hops.append((target, source) if back else (source, target))
    return hops


def params(enc_len):
    return pltpu.CompilerParams(vmem_limit_bytes=(12 + enc_len * 36 // 4096) * MIB)


def pack(pairs, pieces):
    _, rows, _, width = pairs.shape
    groups = lax.axis_size("seq") * lax.axis_size("tp")
    local = width // groups

    def kernel(pairs_ref, *outs):
        @pl.loop(0, rows // 16)
        def _(r):
            here = pl.ds(pl.multiple_of(r * 16, 16), 16)
            for out, (offset, head, count) in zip(outs, pieces):
                base = group_at(offset) * local + head * HEAD
                for h in range(count):
                    column = pl.multiple_of(base + h * HEAD, HEAD)
                    out[h, here] = pairs_ref[0, here, :, pl.ds(column, HEAD)]

    return pl.pallas_call(
        kernel,
        out_shape=[
            jax.ShapeDtypeStruct((count, rows, 2, HEAD), pairs.dtype) for _, _, count in pieces
        ],
        in_specs=[VMEM],
        out_specs=[VMEM] * len(pieces),
        compiler_params=pltpu.CompilerParams(vmem_limit_bytes=24 * MIB),
        name="pack",
    )(pairs)


def unpack(blocks, pieces, width):
    _, rows, _, _ = blocks[0].shape
    groups = lax.axis_size("seq") * lax.axis_size("tp")
    local = width // groups
    parts = 4 if rows % 64 == 0 else 1
    size = rows // parts

    def kernel(*refs):
        ins, out, held, sem = refs[: len(pieces)], refs[len(pieces)], refs[-2], refs[-1]

        def store(r):
            here = pl.ds(pl.multiple_of(r * size, size), size)
            return pltpu.make_async_copy(held.at[here], out.at[0, here], sem.at[r])

        @pl.loop(0, parts)
        def _(r):
            here = pl.ds(pl.multiple_of(r * size, size), size)
            for block, (offset, head, count) in zip(ins, pieces):
                base = group_at(offset) * local + head * HEAD
                for h in range(count):
                    column = pl.multiple_of(base + h * HEAD, HEAD)
                    held[here, :, pl.ds(column, HEAD)] = block[h, here]
            store(r).start()

        for r in range(parts):
            store(r).wait()

    return pl.pallas_call(
        kernel,
        out_shape=jax.ShapeDtypeStruct((1, rows, 2, width), blocks[0].dtype),
        in_specs=[VMEM] * len(pieces),
        out_specs=HBM,
        scratch_shapes=[
            pltpu.VMEM((rows, 2, width), blocks[0].dtype),
            pltpu.SemaphoreType.DMA((parts,)),
        ],
        compiler_params=pltpu.CompilerParams(vmem_limit_bytes=24 * MIB),
        name="unpack",
    )(*blocks)


def turned(rows):
    _, tokens, local = rows.shape
    heads = local // HEAD
    tile = 256 if tokens % 256 == 0 else tokens

    def kernel(rows_ref, out_ref):
        for h in range(heads):
            for j in range(tokens // tile):
                here = slice(j * tile, (j + 1) * tile)
                block = rows_ref[0, here, h * HEAD : (h + 1) * HEAD]
                out_ref[h, :, here] = block.astype(jnp.float32).T.astype(rows.dtype)

    return pl.pallas_call(
        kernel,
        out_shape=jax.ShapeDtypeStruct((heads, HEAD, tokens), rows.dtype),
        in_specs=[VMEM],
        out_specs=VMEM,
        compiler_params=pltpu.CompilerParams(vmem_limit_bytes=16 * MIB),
        name="turned",
    )(rows)


def tiles(count):
    def run(body):
        if count <= 2:
            for j in range(count):
                body(j)
        else:
            pl.loop(0, count)(body)

    return run


def tokens_of(j, tile):
    return pl.ds(j * tile if isinstance(j, int) else pl.multiple_of(j * tile, tile), tile)


def tile_of(rows, tokens):
    for parts in range(1, tokens // 256 + 1):
        if tokens % (256 * parts) == 0 and rows * (tokens // parts) * 4 <= 5 * MIB // 4:
            return tokens // parts
    return 256 if tokens % 256 == 0 else tokens


def dot(a, b, contract=((1,), (0,))):
    return lax.dot_general(a, b, (contract, ((), ())), preferred_element_type=jnp.float32)


def shuffle(rows, join):
    to = lax.broadcasted_iota(jnp.int32, (2 * rows, 2 * rows), 1 if join else 0)
    source = lax.broadcasted_iota(jnp.int32, (2 * rows, 2 * rows), 0 if join else 1)
    wanted = jnp.where(to < rows, 2 * to, 2 * (to - rows) + 1)
    return jnp.where(source == wanted, 1.0, 0.0).astype(jnp.bfloat16)


def split_chunks(chunks, h, rows, k_ref=None, v_ref=None, kt_ref=None, vt_ref=None):
    split = shuffle(rows, False)
    for i, chunk in enumerate(chunks):
        both = dot(split, chunk[h])
        here = slice(i * rows, (i + 1) * rows)
        keys, values = both[:rows], both[rows:]
        if k_ref is not None:
            k_ref[h, here, :] = keys.astype(jnp.bfloat16)
        if v_ref is not None:
            v_ref[h, here, :] = values.astype(jnp.bfloat16)
        if kt_ref is not None:
            kt_ref[h, :, here] = keys.T.astype(jnp.bfloat16)
        if vt_ref is not None:
            vt_ref[h, :HEAD, here] = values.T.astype(jnp.bfloat16)
    if vt_ref is not None:
        tail = (vt_ref.shape[1] - HEAD, vt_ref.shape[2])
        vt_ref[h, HEAD:, :] = jnp.ones(tail, jnp.bfloat16)


def join_chunks(outs, h, rows, gk_ref, gv_ref):
    join = shuffle(rows, True)
    for i, out in enumerate(outs):
        here = slice(i * rows, (i + 1) * rows)
        both = jnp.concatenate([gk_ref[h, here, :], gv_ref[h, here, :]], axis=0)
        out[h] = dot(join, both.astype(jnp.bfloat16)).astype(jnp.bfloat16)


def raise_scores(keys, qt, values_t, before):
    scores = dot(keys, qt)
    top = jnp.max(scores, axis=0, keepdims=True)
    if before is not None:
        top = jnp.maximum(top, before[0])
    raised = jnp.exp2((scores - top) * EXPONENT)
    low = raised.astype(jnp.bfloat16)
    summed = dot(values_t, low)
    total, context = summed[HEAD : HEAD + 1], summed[:HEAD]
    if before is not None:
        shrink = jnp.exp2((before[0] - top) * EXPONENT)
        total = total + before[1] * shrink
        context = context + before[2] * shrink
    return raised, low, top, total, context


def forward_kernel(count, first, tile, *refs):
    chunks, refs = refs[:count], refs[count:]
    qt_ref, refs = refs[0], refs[1:]
    if not first:
        stats_in, context_in, refs = refs[0], refs[1], refs[2:]
    stats_ref, context_ref, low_ref, k_ref, vt_ref = refs
    heads, pair_rows, _ = chunks[0].shape
    for h in range(heads):
        split_chunks(chunks, h, pair_rows // 2, k_ref=k_ref, vt_ref=vt_ref)

    @tiles(qt_ref.shape[2] // tile)
    def _(j):
        here = tokens_of(j, tile)
        for h in range(heads):
            before = None
            if not first:
                before = (stats_in[h, 0:1, here], stats_in[h, 1:2, here], context_in[h, :, here])
            _, low, top, total, context = raise_scores(
                k_ref[h], qt_ref[h, :, here], vt_ref[h], before
            )
            low_ref[h, :, here] = low
            stats_ref[h, 0:1, here] = top
            stats_ref[h, 1:2, here] = total
            context_ref[h, :, here] = context


def gradients(raised, low, scale, row_dot, qt, gt, refs, h):
    v_ref, kt_ref, gk_ref, gv_ref = refs
    grad_weights = dot(v_ref[h], gt)
    grad_scores = (raised * (grad_weights - row_dot)).astype(jnp.bfloat16)
    grad_q = dot(kt_ref[h], grad_scores) * (scale * FACTOR)
    scaled = (qt.astype(jnp.float32) * (scale * FACTOR)).astype(jnp.bfloat16)
    gk_ref[h] += dot(grad_scores, scaled, NT)
    gv_ref[h] += dot(low, (gt.astype(jnp.float32) * scale).astype(jnp.bfloat16), NT)
    return grad_q


def turn_kernel(count, head, tile, *refs):
    chunks, refs = refs[:count], refs[count:]
    qt_ref, gt_ref, stats_in, context_in = refs[:4]
    stats_ref, context_ref, grad_q_ref = refs[4:7]
    outs, refs = refs[7 : 7 + count], refs[7 + count :]
    k_ref, vt_ref, v_ref, kt_ref, gk_ref, gv_ref = refs
    rows = chunks[0].shape[1] // 2
    split_chunks(chunks, 0, rows, k_ref, v_ref, kt_ref, vt_ref)
    gk_ref[...] = jnp.zeros_like(gk_ref)
    gv_ref[...] = jnp.zeros_like(gv_ref)

    @tiles(qt_ref.shape[2] // tile)
    def _(j):
        here = tokens_of(j, tile)
        qt, gt = qt_ref[head, :, here], gt_ref[head, :, here]
        before = (
            stats_in[head, 0:1, here],
            stats_in[head, 1:2, here],
            context_in[head, :, here],
        )
        raised, low, top, total, context = raise_scores(k_ref[0], qt, vt_ref[0], before)
        scale = 1.0 / total
        context = context * scale
        row_dot = jnp.sum(gt.astype(jnp.float32) * context, axis=0, keepdims=True)
        context_ref[0, :, here] = context
        stats_ref[0, 0:1, here] = top
        stats_ref[0, 1:2, here] = scale
        stats_ref[0, 2:3, here] = row_dot
        grad_q_ref[0, :, here] = gradients(
            raised, low, scale, row_dot, qt, gt, (v_ref, kt_ref, gk_ref, gv_ref), 0
        )

    join_chunks(outs, 0, rows, gk_ref, gv_ref)


def backward_kernel(back, counts, heads, first, tile, *refs):
    refs = refs[back:]
    groups = []
    for count in counts:
        groups.append((refs[:count], refs[count], refs[count + 1]))
        refs = refs[count + 2 :]
    qt_ref, gt_ref, refs = refs[0], refs[1], refs[2:]
    final, grads_in, refs = refs[:heads], refs[heads : 2 * heads], refs[2 * heads :]
    if first:
        ready, rows_ref, grads_out, refs = (
            refs[:heads],
            refs[heads],
            refs[heads + 1 : 2 * heads + 1],
            refs[2 * heads + 1 :],
        )
    else:
        rows_ref, refs = refs[0], refs[1:]
    outs, refs = refs[: sum(counts)], refs[sum(counts) :]
    scratch = [refs[i : i + 4] for i in range(0, len(refs), 4)]
    rows = groups[0][0][0].shape[1] // 2
    for (chunks, _, _), (v_ref, kt_ref, gk_ref, gv_ref) in zip(groups, scratch):
        for h in range(heads):
            split_chunks(chunks, h, rows, v_ref=v_ref, kt_ref=kt_ref)
        gk_ref[...] = jnp.zeros_like(gk_ref)
        gv_ref[...] = jnp.zeros_like(gv_ref)

    @tiles(qt_ref.shape[2] // tile)
    def _(j):
        here = tokens_of(j, tile)
        for h in range(heads):
            columns = slice(h * HEAD, (h + 1) * HEAD)
            qt, gt = qt_ref[h, :, here], gt_ref[h, :, here]
            top, scale, row_dot = (final[h][0, i : i + 1, here] for i in range(3))
            grad_q = grads_in[h][0, :, here]
            for (_, low_ref, then_ref), own in zip(groups, scratch):
                shrunk = jnp.exp2((then_ref[h, 0:1, here] - top) * EXPONENT)
                low = low_ref[h, :, here]
                raised = low.astype(jnp.float32)
                grad_q = grad_q + gradients(
                    raised, low, scale * shrunk, row_dot, qt, gt, own, h
                )
            if first:
                grads_out[h][0, :, here] = grad_q
                grad_q = ready[h][0, :, here]
            rows_ref[0, here, columns] = grad_q.T.astype(rows_ref.dtype)

    for count, (_, _, gk_ref, gv_ref) in zip(counts, scratch):
        for h in range(heads):
            join_chunks(outs[:count], h, rows, gk_ref, gv_ref)
        outs = outs[count:]


def cost(heads, rows, tokens, matmuls):
    return pl.CostEstimate(
        flops=2 * matmuls * heads * rows * tokens * HEAD,
        bytes_accessed=heads * (rows + tokens) * HEAD * 8,
        transcendentals=heads * rows * tokens,
    )


def attend(groups, last, queries, upstream, send_back):
    heads, pair_rows, _ = groups[0][0].shape
    rows = pair_rows // 2
    enc_len = (sum(len(g) for g in groups) + len(last[0])) * rows
    tokens = queries.shape[1]
    qt, gt = turned(queries), turned(upstream)
    stats_shape = jax.ShapeDtypeStruct((heads, 8, tokens), jnp.float32)
    wide_shape = jax.ShapeDtypeStruct((heads, HEAD, tokens), jnp.float32)
    stats_one = jax.ShapeDtypeStruct((1, 8, tokens), jnp.float32)
    wide_one = jax.ShapeDtypeStruct((1, HEAD, tokens), jnp.float32)
    rows_shape = jax.ShapeDtypeStruct(queries.shape, queries.dtype)
    compiler_params = params(enc_len)

    def natural(heads, count):
        return pltpu.VMEM((heads, count * rows, HEAD), jnp.bfloat16)

    def across(heads, count, extra=0):
        return pltpu.VMEM((heads, HEAD + extra, count * rows), jnp.bfloat16)

    def sums(heads, count):
        return pltpu.VMEM((heads, count * rows, HEAD), jnp.float32)

    def shapes_of(group):
        return [jax.ShapeDtypeStruct(c.shape, c.dtype) for c in group]

    state, kept = [], []
    for group in groups:
        count = len(group)
        low_shape = jax.ShapeDtypeStruct((heads, count * rows, tokens), jnp.bfloat16)
        stats, context, low = pl.pallas_call(
            functools.partial(forward_kernel, count, not state, tile_of(count * rows, tokens)),
            out_shape=[stats_shape, wide_shape, low_shape],
            in_specs=[VMEM] * (count + 1 + len(state)),
            out_specs=[VMEM] * 3,
            scratch_shapes=[natural(heads, count), across(heads, count, 16)],
            compiler_params=compiler_params,
            cost_estimate=cost(heads, count * rows, tokens, 2),
            name="forward",
        )(*group, qt, *state)
        state = [stats, context]
        kept.append((low, stats))

    final, contexts, grads_q, returned = [], [], [], []
    for h, group in enumerate(last):
        count = len(group)
        stats, context, grad_q, *grads = pl.pallas_call(
            functools.partial(turn_kernel, count, h, tile_of(count * rows, tokens)),
            out_shape=[stats_one, wide_one, wide_one] + shapes_of(group),
            in_specs=[VMEM] * (count + 4),
            out_specs=[VMEM] * (count + 3),
            scratch_shapes=[natural(1, count), across(1, count, 16)]
            + [natural(1, count), across(1, count)]
            + [sums(1, count)] * 2,
            compiler_params=compiler_params,
            cost_estimate=cost(1, count * rows, tokens, 6),
            name="turn",
        )(*group, qt, gt, *state)
        final.append(stats)
        contexts.append(context)
        grads_q.append(grad_q)
        returned.append(send_back(len(groups), h, grads))

    for part in (list(range(1, len(groups))), [0]):
        first = part[0] > 0
        counts = [len(groups[i]) for i in part]
        back = [] if first else sum(returned, [])
        operands = []
        for i in part:
            operands += [*groups[i], *kept[i]]
        operands += [qt, gt, *final, *grads_q, *(contexts if first else [])]
        shapes = [rows_shape] + ([wide_one] * heads if first else [])
        outs = pl.pallas_call(
            functools.partial(
                backward_kernel,
                len(back),
                counts,
                heads,
                first,
                tile_of(max(counts) * rows, tokens),
            ),
            out_shape=shapes + shapes_of(sum((groups[i] for i in part), [])),
            in_specs=[ANY] * len(back) + [VMEM] * len(operands),
            out_specs=[VMEM] * (len(shapes) + sum(counts)),
            scratch_shapes=[
                shape
                for count in counts
                for shape in (
                    natural(heads, count),
                    across(heads, count),
                    sums(heads, count),
                    sums(heads, count),
                )
            ],
            compiler_params=compiler_params,
            cost_estimate=cost(heads, sum(counts) * rows, tokens, 4),
            name="backward",
        )(*back, *operands)
        if first:
            context_rows, grads_q = outs[0], outs[1 : 1 + heads]
        else:
            grad_query = outs[0]
        blocks = list(outs[len(shapes) :])
        for i in part:
            send_back(i, 0, blocks[: len(groups[i])])
            blocks = blocks[len(groups[i]) :]
    return context_rows, grad_query


def shards(pairs, queries, upstream):
    _, rows, _, width = pairs.shape
    heads = queries.shape[2] // HEAD
    order = offsets()
    quarter = max(1, len(order) // 4)
    cuts = [0, quarter, 2 * quarter, len(order) - quarter, len(order)]
    whole = [[(o, 0, heads) for o in order[a:b]] for a, b in zip(cuts[:-2], cuts[1:-1])]
    single = [[(o, h, 1) for o in order[cuts[-2] :]] for h in range(heads)]
    pieces = sum(whole + single, [])
    blocks = []
    for piece, block in zip(pieces, pack(pairs, pieces)):
        block = block.reshape(-1, 2 * rows, HEAD)
        blocks.append(lax.ppermute(block, AXES, route(piece[0], False)))
    arrived = []
    for group in whole + single:
        arrived.append(blocks[: len(group)])
        blocks = blocks[len(group) :]
    homes, returned = [], []

    def send_back(index, head, grads):
        sent = (whole + single)[index + head]
        back = [lax.ppermute(g, AXES, route(p[0], True)) for p, g in zip(sent, grads)]
        homes.extend(sent)
        returned.extend(b.reshape(-1, rows, 2, HEAD) for b in back)
        return back

    context, grad_query = attend(
        arrived[: len(whole)], arrived[len(whole) :], queries, upstream, send_back
    )
    return context, grad_query, unpack(returned, homes, width)


def solution(mesh):
    return jax.shard_map(
        shards,
        mesh=mesh,
        in_specs=(
            P("segment", ("seq", "tp"), None, None),
            P("segment", None, ("seq", "tp")),
            P("segment", None, ("seq", "tp")),
        ),
        out_specs=(
            P("segment", None, ("seq", "tp")),
            P("segment", None, ("seq", "tp")),
            P("segment", ("seq", "tp"), None, None),
        ),
        check_vma=False,
    )
```

time: 69.3 us -> 69 us (level); the launches traced: 67.9 us -> 68.8 us
  starting transfers between devices: 28.4 us -> 37.5 us
  waiting for transfers between devices: 16 us -> 7.61 us
    ppermute x16 -> x20, starting transfers between devices: 28.4 us -> 37.5 us  [the longest x10 20.1 us: shards(): blocks.append(lax.ppermute(block, AXES, route(piece[0], False)))]
    ppermute x16 -> x20, waiting for transfers between devices: 16 us -> 7.61 us  [the longest x10 6.73 us: send_back(): lax.ppermute(g, AXES, route(p[0], True))]
    pallas_call x4 -> x5, Pallas kernels: 13.7 us -> 14 us  [the longest x2 8.54 us: attend(): pl.pallas_call(functools.partial(backward_kernel, len(back), counts, head...]
  transfers between devices with their start and end apart: 16 -> 20, of which waited for: 7 -> 4; matrix products, arithmetic and copies ran while one was open for 0% -> 0% of each run, Pallas kernels for 21% -> 28%
where the time goes in v8:
time: 69 us; the launch traced here: 68.8 us
  starting transfers between devices  37.5 us (54%)
  Pallas kernels  21.6 us (31%)
  waiting for transfers between devices  7.61 us (11%)
  local copies, waits for them, and re-layouts  1.23 us (2%)
  between operations  0.91 us (1%)
    ppermute x10, starting transfers between devices, shards(): blocks.append(lax.ppermute(block, AXES, route(piece[0], False)))  20.1 us
    ppermute x10, starting transfers between devices, send_back(): lax.ppermute(g, AXES, route(p[0], True))  17.4 us
    pallas_call x2, Pallas kernels, attend(): pl.pallas_call(functools.partial(backward_kernel, len(back), counts, head...  8.54 us
    ppermute x10, waiting for transfers between devices, send_back(): lax.ppermute(g, AXES, route(p[0], True))  6.73 us
    pallas_call x3, Pallas kernels, attend(): pl.pallas_call(functools.partial(forward_kernel, count, not state, tile_o...  5.5 us
    pallas_call x2, Pallas kernels, attend(): pl.pallas_call(functools.partial(turn_kernel, count, h, tile_of(count * r...  4.5 us
    pallas_call x1, Pallas kernels, unpack(): pl.pallas_call(kernel, out_shape=jax.ShapeDtypeStruct((1, rows, 2, width)...  1.51 us
  transfers between devices with their start and end apart: 20, of which 4 were waited for; matrix products, arithmetic and copies ran while one was open for 0% of the time, Pallas kernels for 28%

profile of v8, /device:TPU:0, one launch (start us, length us, event | category | flops | bytes accessed | tf_op | source)
XLA Modules:
  0.0 68.8 jit_solution(6306043691600544936)
XLA Ops:
  0.6 0.0 copy-start
  0.6 1.2 %copy-done = bf16[1,128,2,2048]{3,2,1,0:T(2,128)(2,1)S(1)} copy-done((bf16[1,128,2,2048]{3,2,1,0:T(2,128)(2,1)S(1)}, bf16[1,128,2,2048]{3,2,1,0:T(2,128)(2,1)}, u32[]{:S(2)}) %copy-start) | copy-done | bytes 1048600
  1.9 0.0 copy-start.1
  1.9 0.0 copy-start.2
  1.9 1.0 %pack.1 = (bf16[2,128,2,128]{3,2,1,0:T(2,128)(2,1)S(1)}, bf16[2,128,2,128]{3,2,1,0:T(2,128)(2,1)S(1)}, bf16[2,128,2,128]{3,2,1,0:T(2,128)(2,1)S(1)}, bf16[2,128,...) custom-call(bf16[1,128,2,2048]{3,2,1,0:T(2,128)(2,1)S(1)} %copy-done), custom_call_target="tpu_custom_call" | custom-call | tf_op jit(solution)/shard_map/pack/pallas_call | solution.py:73
  2.8 3.5 %collective-permute-start.2 = (bf16[2,256,128]{2,1,0:T(8,128)(2,1)S(1)}, bf16[2,256,128]{2,1,0:T(8,128)(2,1)S(1)}, u32[]{:S(2)}, u32[]{:S(2)}) collective-permute-start(bf16[2,256,128]{2,1,0:T(8,128)(2,1)S(1)} %bitcast.35), channel_id=1, source_target_pairs={{0,11},{1,10},{2,13},{3,12},{4,15},{5,14},{6,9},{7,8},{8,19},{9,18... | collective-permute-start | bytes 393224 | tf_op jit(solution)/shard_map/ppermute | solution.py:476
  6.3 1.7 %collective-permute-start.3 = (bf16[2,256,128]{2,1,0:T(8,128)(2,1)S(1)}, bf16[2,256,128]{2,1,0:T(8,128)(2,1)S(1)}, u32[]{:S(2)}, u32[]{:S(2)}) collective-permute-start(bf16[2,256,128]{2,1,0:T(8,128)(2,1)S(1)} %bitcast.34), channel_id=1, source_target_pairs={{0,9},{1,8},{2,11},{3,10},{4,13},{5,12},{6,15},{7,14},{8,17},{9,16... | collective-permute-start | bytes 393224 | tf_op jit(solution)/shard_map/ppermute | solution.py:476
  8.0 2.6 %collective-permute-start.1 = (bf16[2,256,128]{2,1,0:T(8,128)(2,1)S(1)}, bf16[2,256,128]{2,1,0:T(8,128)(2,1)S(1)}, u32[]{:S(2)}, u32[]{:S(2)}) collective-permute-start(bf16[2,256,128]{2,1,0:T(8,128)(2,1)S(1)} %bitcast.33), channel_id=1, source_target_pairs={{0,15},{1,14},{2,9},{3,8},{4,11},{5,10},{6,13},{7,12},{8,23},{9,22... | collective-permute-start | bytes 393224 | tf_op jit(solution)/shard_map/ppermute | solution.py:476
  10.7 0.0 collective-permute-start
  10.7 3.5 %collective-permute-start.4 = (bf16[2,256,128]{2,1,0:T(8,128)(2,1)S(1)}, bf16[2,256,128]{2,1,0:T(8,128)(2,1)S(1)}, u32[]{:S(2)}, u32[]{:S(2)}) collective-permute-start(bf16[2,256,128]{2,1,0:T(8,128)(2,1)S(1)} %bitcast.31), channel_id=1, source_target_pairs={{0,14},{1,15},{2,8},{3,9},{4,10},{5,11},{6,12},{7,13},{8,22},{9,23... | collective-permute-start | bytes 393224 | tf_op jit(solution)/shard_map/ppermute | solution.py:476
  14.2 0.0 collective-permute-done.2.refs_0_.refs_4_
  14.2 1.6 %collective-permute-start.5 = (bf16[2,256,128]{2,1,0:T(8,128)(2,1)S(1)}, bf16[2,256,128]{2,1,0:T(8,128)(2,1)S(1)}, u32[]{:S(2)}, u32[]{:S(2)}) collective-permute-start(bf16[2,256,128]{2,1,0:T(8,128)(2,1)S(1)} %bitcast.30), channel_id=1, source_target_pairs={{0,8},{1,9},{2,10},{3,11},{4,12},{5,13},{6,14},{7,15},{8,16},{9,17... | collective-permute-start | bytes 393224 | tf_op jit(solution)/shard_map/ppermute | solution.py:476
  15.8 0.0 copy-done.1
  15.8 0.3 turned.2.refs_2_.refs_8_
  16.1 0.0 copy-done.2
  16.1 0.3 turned.3.refs_3_.refs_9_
  16.4 0.9 %collective-permute-done.3.refs_1_.refs_5_ = bf16[2,256,128]{2,1,0:T(8,128)(2,1)S(1)} collective-permute-done((bf16[2,256,128]{2,1,0:T(8,128)(2,1)S(1)}, bf16[2,256,128]{2,1,0:T(8,128)(2,1)S(1)}, u32[]{:S(2)}, u32[]{:S(2)}) %collective-permute-start.3) | collective-permute-done | bytes 131104 | tf_op jit(solution)/shard_map/ppermute | solution.py:476
  17.2 2.7 %collective-permute-start.6 = (bf16[1,256,128]{2,1,0:T(8,128)(2,1)S(1)}, bf16[1,256,128]{2,1,0:T(8,128)(2,1)S(1)}, u32[]{:S(2)}, u32[]{:S(2)}) collective-permute-start(bf16[1,256,128]{2,1,0:T(8,128)(2,1)S(1)} %bitcast.39), channel_id=1, source_target_pairs={{0,13},{1,12},{2,15},{3,14},{4,9},{5,8},{6,11},{7,10},{8,21},{9,20... | collective-permute-start | bytes 196616 | tf_op jit(solution)/shard_map/ppermute | solution.py:476
  19.9 1.8 %forward.3 = (f32[2,8,1536]{2,1,0:T(8,128)S(1)}, f32[2,128,1536]{2,1,0:T(8,128)S(1)}, bf16[2,256,1536]{2,1,0:T(8,128)(2,1)S(1)}) custom-call(bf16[2,256,128]{2,1,0:T(8,128)(2,1)S(1)} %collective-permute-done.2.refs_0_.refs_4_, bf16[2,256,128]{2,1,0:T(8,128)(2,1)S(1)} %collective-permute-done.3.refs_1_.refs_5_, bf16[2,128,1536]{2,1,0:T(8,128)(2,1)S(1)} %turned.2.refs_2_.refs_8_), custom_call_target="tpu_custom_call" | custom-call | flops 402653184 | bytes 3670016 | tf_op jit(solution)/shard_map/forward/pallas_call | solution.py:385
  21.7 0.0 collective-permute-done.1.refs_1_
  21.8 1.2 %collective-permute-start.7 = (bf16[1,256,128]{2,1,0:T(8,128)(2,1)S(1)}, bf16[1,256,128]{2,1,0:T(8,128)(2,1)S(1)}, u32[]{:S(2)}, u32[]{:S(2)}) collective-permute-start(bf16[1,256,128]{2,1,0:T(8,128)(2,1)S(1)} %bitcast.38), channel_id=1, source_target_pairs={{0,12},{1,13},{2,14},{3,15},{4,8},{5,9},{6,10},{7,11},{8,20},{9,21... | collective-permute-start | bytes 196616 | tf_op jit(solution)/shard_map/ppermute | solution.py:476
  23.0 0.0 collective-permute-done.refs_0_
  23.0 2.8 %collective-permute-start.8 = (bf16[1,256,128]{2,1,0:T(8,128)(2,1)S(1)}, bf16[1,256,128]{2,1,0:T(8,128)(2,1)S(1)}, u32[]{:S(2)}, u32[]{:S(2)}) collective-permute-start(bf16[1,256,128]{2,1,0:T(8,128)(2,1)S(1)} %bitcast.37), channel_id=1, source_target_pairs={{0,13},{1,12},{2,15},{3,14},{4,9},{5,8},{6,11},{7,10},{8,21},{9,20... | collective-permute-start | bytes 196616 | tf_op jit(solution)/shard_map/ppermute | solution.py:476
  25.8 1.8 %forward.4 = (f32[2,8,1536]{2,1,0:T(8,128)S(1)}, f32[2,128,1536]{2,1,0:T(8,128)S(1)}, bf16[2,256,1536]{2,1,0:T(8,128)(2,1)S(1)}) custom-call(bf16[2,256,128]{2,1,0:T(8,128)(2,1)S(1)} %collective-permute-done.refs_0_, bf16[2,256,128]{2,1,0:T(8,128)(2,1)S(1)} %collective-permute-done.1.refs_1_, bf16[2,128,1536]{2,1,0:T(8,128)(2,1)S(1)} %turned.2.refs_2_.refs_8_, ...), custom_call_target="tpu_custom_call" | custom-call | flops 402653184 | bytes 3670016 | tf_op jit(solution)/shard_map/forward/pallas_call | solution.py:385
  27.6 0.0 collective-permute-done.4.refs_0_.refs_4_
  27.6 0.5 collective-permute-start.9
  28.1 0.0 collective-permute-done.5.refs_1_.refs_5_
  28.1 1.8 %forward.5 = (f32[2,8,1536]{2,1,0:T(8,128)S(1)}, f32[2,128,1536]{2,1,0:T(8,128)S(1)}, bf16[2,256,1536]{2,1,0:T(8,128)(2,1)S(1)}) custom-call(bf16[2,256,128]{2,1,0:T(8,128)(2,1)S(1)} %collective-permute-done.4.refs_0_.refs_4_, bf16[2,256,128]{2,1,0:T(8,128)(2,1)S(1)} %collective-permute-done.5.refs_1_.refs_5_, ...), custom_call_target="tpu_custom_call" | custom-call | flops 402653184 | bytes 3670016 | tf_op jit(solution)/shard_map/forward/pallas_call | solution.py:385
  29.9 0.0 collective-permute-done.6.refs_0_
  30.0 0.0 collective-permute-done.7.refs_1_
  30.0 2.3 %turn.2 = (f32[1,8,1536]{2,1,0:T(8,128)S(1)}, f32[1,128,1536]{2,1,0:T(8,128)S(1)}, f32[1,128,1536]{2,1,0:T(8,128)S(1)}, bf16[1,256,128]{2,1,0:T(8,128)(2,1)S(1)}, bf16[1,256,128]{2,1,0:T(8,128)(2,1)S(1)}) custom-call(bf16[1,256,128]{2,1,0:T(8,128)(2,1)S(1)} %collective-permute-done.6.refs_0_, bf16[1,256,128]{2,1,0:T(8,128)(2,1)S(1)} %collective-permute-done.7.refs_1_, ...), custom_call_target="tpu_custom_call" | custom-call | flops 603979776 | bytes 1835008 | tf_op jit(solution)/shard_map/turn/pallas_call | solution.py:401
  32.2 4.1 %collective-permute-start.10 = (bf16[1,256,128]{2,1,0:T(8,128)(2,1)S(1)}, bf16[1,256,128]{2,1,0:T(8,128)(2,1)S(1)}, u32[]{:S(2)}, u32[]{:S(2)}) collective-permute-start(bf16[1,256,128]{2,1,0:T(8,128)(2,1)S(1)} %get-tuple-element.67), channel_id=1, source_target_pairs={{13,0},{12,1},{15,2},{14,3},{9,4},{8,5},{11,6},{10,7},{21,8},{20,9... | collective-permute-start | bytes 196616 | tf_op jit(solution)/shard_map/ppermute | solution.py:485
  36.4 0.6 collective-permute-start.11
  37.0 0.0 collective-permute-done.8.refs_0_
  37.0 0.0 collective-permute-done.9.refs_1_
  37.0 2.2 %turn.3 = (f32[1,8,1536]{2,1,0:T(8,128)S(1)}, f32[1,128,1536]{2,1,0:T(8,128)S(1)}, f32[1,128,1536]{2,1,0:T(8,128)S(1)}, bf16[1,256,128]{2,1,0:T(8,128)(2,1)S(1)}, bf16[1,256,128]{2,1,0:T(8,128)(2,1)S(1)}) custom-call(bf16[1,256,128]{2,1,0:T(8,128)(2,1)S(1)} %collective-permute-done.8.refs_0_, bf16[1,256,128]{2,1,0:T(8,128)(2,1)S(1)} %collective-permute-done.9.refs_1_, ...), custom_call_target="tpu_custom_call" | custom-call | flops 603979776 | bytes 1835008 | tf_op jit(solution)/shard_map/turn/pallas_call | solution.py:401
  39.2 1.5 %collective-permute-start.12 = (bf16[1,256,128]{2,1,0:T(8,128)(2,1)S(1)}, bf16[1,256,128]{2,1,0:T(8,128)(2,1)S(1)}, u32[]{:S(2)}, u32[]{:S(2)}) collective-permute-start(bf16[1,256,128]{2,1,0:T(8,128)(2,1)S(1)} %get-tuple-element.69), channel_id=1, source_target_pairs={{13,0},{12,1},{15,2},{14,3},{9,4},{8,5},{11,6},{10,7},{21,8},{20,9... | collective-permute-start | bytes 196616 | tf_op jit(solution)/shard_map/ppermute | solution.py:485
  40.8 0.9 %collective-permute-start.13 = (bf16[1,256,128]{2,1,0:T(8,128)(2,1)S(1)}, bf16[1,256,128]{2,1,0:T(8,128)(2,1)S(1)}, u32[]{:S(2)}, u32[]{:S(2)}) collective-permute-start(bf16[1,256,128]{2,1,0:T(8,128)(2,1)S(1)} %get-tuple-element.70), channel_id=1, source_target_pairs={{12,0},{13,1},{14,2},{15,3},{8,4},{9,5},{10,6},{11,7},{20,8},{21,9... | collective-permute-start | bytes 196616 | tf_op jit(solution)/shard_map/ppermute | solution.py:485
  41.7 5.3 %backward.2 = (bf16[1,1536,256]{2,1,0:T(8,128)(2,1)}, f32[1,128,1536]{2,1,0:T(8,128)S(1)}, f32[1,128,1536]{2,1,0:T(8,128)S(1)}, bf16[2,256,128]{2,1,0:T(8,128)(2...) custom-call(bf16[2,256,128]{2,1,0:T(8,128)(2,1)S(1)} %collective-permu, ...), custom_call_target="tpu_custom_call" | custom-call | flops 1610612736 | bytes 4194304 | tf_op jit(solution)/shard_map/backward/pallas_call | solution.py:427
  47.0 4.0 %collective-permute-start.14 = (bf16[2,256,128]{2,1,0:T(8,128)(2,1)S(1)}, bf16[2,256,128]{2,1,0:T(8,128)(2,1)S(1)}, u32[]{:S(2)}, u32[]{:S(2)}) collective-permute-start(bf16[2,256,128]{2,1,0:T(8,128)(2,1)S(1)} %get-tuple-element.75), channel_id=1, source_target_pairs={{10,0},{11,1},{12,2},{13,3},{14,4},{15,5},{8,6},{9,7},{18,8},{19,9... | collective-permute-start | bytes 393224 | tf_op jit(solution)/shard_map/ppermute | solution.py:485
  50.9 0.0 collective-permute-done.10.refs_0_
  51.0 0.0 collective-permute-start.15
  51.0 0.0 collective-permute-done.11.refs_1_
  51.0 0.4 collective-permute-start.16
  51.4 0.0 collective-permute-done.12.refs_2_
  51.4 0.2 collective-permute-start.17
  51.6 0.0 collective-permute-done.13.refs_3_
  51.6 3.2 %backward.3 = (bf16[1,1536,256]{2,1,0:T(8,128)(2,1)}, bf16[2,256,128]{2,1,0:T(8,128)(2,1)S(1)}, bf16[2,256,128]{2,1,0:T(8,128)(2,1)S(1)}) custom-call(bf16[1,256,128]{2,1,0:T(8,128)(2,1)S(1)} %collective-permute-done.10.refs_0_, bf16[1,256,128]{2,1,0:T(8,128)(2,1)S(1)} %collective-permute-done.11.refs_1_, ...), custom_call_target="tpu_custom_call" | custom-call | flops 805306368 | bytes 3670016 | tf_op jit(solution)/shard_map/backward/pallas_call | solution.py:427
  54.8 4.9 %collective-permute-start.18 = (bf16[2,256,128]{2,1,0:T(8,128)(2,1)S(1)}, bf16[2,256,128]{2,1,0:T(8,128)(2,1)S(1)}, u32[]{:S(2)}, u32[]{:S(2)}) collective-permute-start(bf16[2,256,128]{2,1,0:T(8,128)(2,1)S(1)} %get-tuple-element.79), channel_id=1, source_target_pairs={{11,0},{10,1},{13,2},{12,3},{15,4},{14,5},{9,6},{8,7},{19,8},{18,9... | collective-permute-start | bytes 393224 | tf_op jit(solution)/shard_map/ppermute | solution.py:485
  59.7 0.0 collective-permute-done.14
  59.7 0.7 %collective-permute-start.19 = (bf16[2,256,128]{2,1,0:T(8,128)(2,1)S(1)}, bf16[2,256,128]{2,1,0:T(8,128)(2,1)S(1)}, u32[]{:S(2)}, u32[]{:S(2)}) collective-permute-start(bf16[2,256,128]{2,1,0:T(8,128)(2,1)S(1)} %get-tuple-element.80), channel_id=1, source_target_pairs={{9,0},{8,1},{11,2},{10,3},{13,4},{12,5},{15,6},{14,7},{17,8},{16,9... | collective-permute-start | bytes 393224 | tf_op jit(solution)/shard_map/ppermute | solution.py:485
  60.4 0.0 collective-permute-done.15
  60.4 0.6 collective-permute-done.16
  61.0 0.0 collective-permute-done.17
  61.0 3.9 %collective-permute-done.18 = bf16[2,256,128]{2,1,0:T(8,128)(2,1)S(1)} collective-permute-done((bf16[2,256,128]{2,1,0:T(8,128)(2,1)S(1)}, bf16[2,256,128]{2,1,0:T(8,128)(2,1)S(1)}, u32[]{:S(2)}, u32[]{:S(2)}) %collective-permute-start.18) | collective-permute-done | bytes 131104 | tf_op jit(solution)/shard_map/ppermute | solution.py:485
  64.9 2.3 %collective-permute-done.19 = bf16[2,256,128]{2,1,0:T(8,128)(2,1)S(1)} collective-permute-done((bf16[2,256,128]{2,1,0:T(8,128)(2,1)S(1)}, bf16[2,256,128]{2,1,0:T(8,128)(2,1)S(1)}, u32[]{:S(2)}, u32[]{:S(2)}) %collective-permute-start.19) | collective-permute-done | bytes 131104 | tf_op jit(solution)/shard_map/ppermute | solution.py:485
  67.2 1.5 %unpack.1 = bf16[1,128,2,2048]{3,2,1,0:T(2,128)(2,1)} custom-call(bf16[1,128,2,128]{3,2,1,0:T(2,128)(2,1)S(1)} %bitcast.20, bf16[1,128,2,128]{3,2,1,0:T(2,128)(2,1)S(1)} %bitcast.21, bf16[1,128,2,128]{3,2,1,0:T(2,128)(2,1)S(1)} %bitcast.22, bf16[1,128,2,128]{3,2,1,0:T(2,128)(2,1)S(1)} %bitcast.23, bf16[2,128,2,128]{3,2,1,0:T(2,128)(2,1)S(1)} %bitcast.24, ...), custom_call_target="tpu_custom_call" | custom-call | tf_op jit(solution)/shard_map/unpack/pallas_call | solution.py:112
Async XLA Ops:
  0.6 1.2 %copy-start = (bf16[1,128,2,2048]{3,2,1,0:T(2,128)(2,1)S(1)}, bf16[1,128,2,2048]{3,2,1,0:T(2,128)(2,1)}, u32[]{:S(2)}) copy-start(bf16[1,128,2,2048]{3,2,1,0:T(2,128)(2,1)} %pairs_ref.1) | copy-start | bytes 3145732
  1.9 13.9 %copy-start.1 = (bf16[1,1536,256]{2,1,0:T(8,128)(2,1)S(1)}, bf16[1,1536,256]{2,1,0:T(8,128)(2,1)}, u32[]{:S(2)}) copy-start(bf16[1,1536,256]{2,1,0:T(8,128)(2,1)} %rows_ref.2) | copy-start | bytes 2359300
  1.9 14.2 %copy-start.2 = (bf16[1,1536,256]{2,1,0:T(8,128)(2,1)S(1)}, bf16[1,1536,256]{2,1,0:T(8,128)(2,1)}, u32[]{:S(2)}) copy-start(bf16[1,1536,256]{2,1,0:T(8,128)(2,1)} %rows_ref.3) | copy-start | bytes 2359300
  2.8 11.3 %collective-permute-start.2 = (bf16[2,256,128]{2,1,0:T(8,128)(2,1)S(1)}, bf16[2,256,128]{2,1,0:T(8,128)(2,1)S(1)}, u32[]{:S(2)}, u32[]{:S(2)}) collective-permute-start(bf16[2,256,128]{2,1,0:T(8,128)(2,1)S(1)} %bitcast.35), channel_id=1, source_target_pairs={{0,11},{1,10},{2,13},{3,12},{4,15},{5,14},{6,9},{7,8},{8,19},{9,18... | collective-permute-start | bytes 393224 | tf_op jit(solution)/shard_map/ppermute | solution.py:476
  6.3 10.9 %collective-permute-start.3 = (bf16[2,256,128]{2,1,0:T(8,128)(2,1)S(1)}, bf16[2,256,128]{2,1,0:T(8,128)(2,1)S(1)}, u32[]{:S(2)}, u32[]{:S(2)}) collective-permute-start(bf16[2,256,128]{2,1,0:T(8,128)(2,1)S(1)} %bitcast.34), channel_id=1, source_target_pairs={{0,9},{1,8},{2,11},{3,10},{4,13},{5,12},{6,15},{7,14},{8,17},{9,16... | collective-permute-start | bytes 393224 | tf_op jit(solution)/shard_map/ppermute | solution.py:476
  8.0 13.7 %collective-permute-start.1 = (bf16[2,256,128]{2,1,0:T(8,128)(2,1)S(1)}, bf16[2,256,128]{2,1,0:T(8,128)(2,1)S(1)}, u32[]{:S(2)}, u32[]{:S(2)}) collective-permute-start(bf16[2,256,128]{2,1,0:T(8,128)(2,1)S(1)} %bitcast.33), channel_id=1, source_target_pairs={{0,15},{1,14},{2,9},{3,8},{4,11},{5,10},{6,13},{7,12},{8,23},{9,22... | collective-permute-start | bytes 393224 | tf_op jit(solution)/shard_map/ppermute | solution.py:476
  10.7 12.3 %collective-permute-start = (bf16[2,256,128]{2,1,0:T(8,128)(2,1)S(1)}, bf16[2,256,128]{2,1,0:T(8,128)(2,1)S(1)}, u32[]{:S(2)}, u32[]{:S(2)}) collective-permute-start(bf16[2,256,128]{2,1,0:T(8,128)(2,1)S(1)} %bitcast.32), channel_id=1, source_target_pairs={{0,10},{1,11},{2,12},{3,13},{4,14},{5,15},{6,8},{7,9},{8,18},{9,19... | collective-permute-start | bytes 393224 | tf_op jit(solution)/shard_map/ppermute | solution.py:476
  10.7 16.9 %collective-permute-start.4 = (bf16[2,256,128]{2,1,0:T(8,128)(2,1)S(1)}, bf16[2,256,128]{2,1,0:T(8,128)(2,1)S(1)}, u32[]{:S(2)}, u32[]{:S(2)}) collective-permute-start(bf16[2,256,128]{2,1,0:T(8,128)(2,1)S(1)} %bitcast.31), channel_id=1, source_target_pairs={{0,14},{1,15},{2,8},{3,9},{4,10},{5,11},{6,12},{7,13},{8,22},{9,23... | collective-permute-start | bytes 393224 | tf_op jit(solution)/shard_map/ppermute | solution.py:476
  14.2 13.9 %collective-permute-start.5 = (bf16[2,256,128]{2,1,0:T(8,128)(2,1)S(1)}, bf16[2,256,128]{2,1,0:T(8,128)(2,1)S(1)}, u32[]{:S(2)}, u32[]{:S(2)}) collective-permute-start(bf16[2,256,128]{2,1,0:T(8,128)(2,1)S(1)} %bitcast.30), channel_id=1, source_target_pairs={{0,8},{1,9},{2,10},{3,11},{4,12},{5,13},{6,14},{7,15},{8,16},{9,17... | collective-permute-start | bytes 393224 | tf_op jit(solution)/shard_map/ppermute | solution.py:476
  17.2 12.7 %collective-permute-start.6 = (bf16[1,256,128]{2,1,0:T(8,128)(2,1)S(1)}, bf16[1,256,128]{2,1,0:T(8,128)(2,1)S(1)}, u32[]{:S(2)}, u32[]{:S(2)}) collective-permute-start(bf16[1,256,128]{2,1,0:T(8,128)(2,1)S(1)} %bitcast.39), channel_id=1, source_target_pairs={{0,13},{1,12},{2,15},{3,14},{4,9},{5,8},{6,11},{7,10},{8,21},{9,20... | collective-permute-start | bytes 196616 | tf_op jit(solution)/shard_map/ppermute | solution.py:476
  21.8 8.2 %collective-permute-start.7 = (bf16[1,256,128]{2,1,0:T(8,128)(2,1)S(1)}, bf16[1,256,128]{2,1,0:T(8,128)(2,1)S(1)}, u32[]{:S(2)}, u32[]{:S(2)}) collective-permute-start(bf16[1,256,128]{2,1,0:T(8,128)(2,1)S(1)} %bitcast.38), channel_id=1, source_target_pairs={{0,12},{1,13},{2,14},{3,15},{4,8},{5,9},{6,10},{7,11},{8,20},{9,21... | collective-permute-start | bytes 196616 | tf_op jit(solution)/shard_map/ppermute | solution.py:476
  23.0 14.0 %collective-permute-start.8 = (bf16[1,256,128]{2,1,0:T(8,128)(2,1)S(1)}, bf16[1,256,128]{2,1,0:T(8,128)(2,1)S(1)}, u32[]{:S(2)}, u32[]{:S(2)}) collective-permute-start(bf16[1,256,128]{2,1,0:T(8,128)(2,1)S(1)} %bitcast.37), channel_id=1, source_target_pairs={{0,13},{1,12},{2,15},{3,14},{4,9},{5,8},{6,11},{7,10},{8,21},{9,20... | collective-permute-start | bytes 196616 | tf_op jit(solution)/shard_map/ppermute | solution.py:476
  27.6 9.4 %collective-permute-start.9 = (bf16[1,256,128]{2,1,0:T(8,128)(2,1)S(1)}, bf16[1,256,128]{2,1,0:T(8,128)(2,1)S(1)}, u32[]{:S(2)}, u32[]{:S(2)}) collective-permute-start(bf16[1,256,128]{2,1,0:T(8,128)(2,1)S(1)} %bitcast.36), channel_id=1, source_target_pairs={{0,12},{1,13},{2,14},{3,15},{4,8},{5,9},{6,10},{7,11},{8,20},{9,21... | collective-permute-start | bytes 196616 | tf_op jit(solution)/shard_map/ppermute | solution.py:476
  32.2 18.7 %collective-permute-start.10 = (bf16[1,256,128]{2,1,0:T(8,128)(2,1)S(1)}, bf16[1,256,128]{2,1,0:T(8,128)(2,1)S(1)}, u32[]{:S(2)}, u32[]{:S(2)}) collective-permute-start(bf16[1,256,128]{2,1,0:T(8,128)(2,1)S(1)} %get-tuple-element.67), channel_id=1, source_target_pairs={{13,0},{12,1},{15,2},{14,3},{9,4},{8,5},{11,6},{10,7},{21,8},{20,9... | collective-permute-start | bytes 196616 | tf_op jit(solution)/shard_map/ppermute | solution.py:485
  36.4 14.6 %collective-permute-start.11 = (bf16[1,256,128]{2,1,0:T(8,128)(2,1)S(1)}, bf16[1,256,128]{2,1,0:T(8,128)(2,1)S(1)}, u32[]{:S(2)}, u32[]{:S(2)}) collective-permute-start(bf16[1,256,128]{2,1,0:T(8,128)(2,1)S(1)} %get-tuple-element.68), channel_id=1, source_target_pairs={{12,0},{13,1},{14,2},{15,3},{8,4},{9,5},{10,6},{11,7},{20,8},{21,9... | collective-permute-start | bytes 196616 | tf_op jit(solution)/shard_map/ppermute | solution.py:485
  39.2 12.1 %collective-permute-start.12 = (bf16[1,256,128]{2,1,0:T(8,128)(2,1)S(1)}, bf16[1,256,128]{2,1,0:T(8,128)(2,1)S(1)}, u32[]{:S(2)}, u32[]{:S(2)}) collective-permute-start(bf16[1,256,128]{2,1,0:T(8,128)(2,1)S(1)} %get-tuple-element.69), channel_id=1, source_target_pairs={{13,0},{12,1},{15,2},{14,3},{9,4},{8,5},{11,6},{10,7},{21,8},{20,9... | collective-permute-start | bytes 196616 | tf_op jit(solution)/shard_map/ppermute | solution.py:485
  40.8 10.8 %collective-permute-start.13 = (bf16[1,256,128]{2,1,0:T(8,128)(2,1)S(1)}, bf16[1,256,128]{2,1,0:T(8,128)(2,1)S(1)}, u32[]{:S(2)}, u32[]{:S(2)}) collective-permute-start(bf16[1,256,128]{2,1,0:T(8,128)(2,1)S(1)} %get-tuple-element.70), channel_id=1, source_target_pairs={{12,0},{13,1},{14,2},{15,3},{8,4},{9,5},{10,6},{11,7},{20,8},{21,9... | collective-permute-start | bytes 196616 | tf_op jit(solution)/shard_map/ppermute | solution.py:485
  47.0 12.7 %collective-permute-start.14 = (bf16[2,256,128]{2,1,0:T(8,128)(2,1)S(1)}, bf16[2,256,128]{2,1,0:T(8,128)(2,1)S(1)}, u32[]{:S(2)}, u32[]{:S(2)}) collective-permute-start(bf16[2,256,128]{2,1,0:T(8,128)(2,1)S(1)} %get-tuple-element.75), channel_id=1, source_target_pairs={{10,0},{11,1},{12,2},{13,3},{14,4},{15,5},{8,6},{9,7},{18,8},{19,9... | collective-permute-start | bytes 393224 | tf_op jit(solution)/shard_map/ppermute | solution.py:485
  51.0 9.5 %collective-permute-start.15 = (bf16[2,256,128]{2,1,0:T(8,128)(2,1)S(1)}, bf16[2,256,128]{2,1,0:T(8,128)(2,1)S(1)}, u32[]{:S(2)}, u32[]{:S(2)}) collective-permute-start(bf16[2,256,128]{2,1,0:T(8,128)(2,1)S(1)} %get-tuple-element.76), channel_id=1, source_target_pairs={{15,0},{14,1},{9,2},{8,3},{11,4},{10,5},{13,6},{12,7},{23,8},{22,9... | collective-permute-start | bytes 393224 | tf_op jit(solution)/shard_map/ppermute | solution.py:485
  51.0 10.0 %collective-permute-start.16 = (bf16[2,256,128]{2,1,0:T(8,128)(2,1)S(1)}, bf16[2,256,128]{2,1,0:T(8,128)(2,1)S(1)}, u32[]{:S(2)}, u32[]{:S(2)}) collective-permute-start(bf16[2,256,128]{2,1,0:T(8,128)(2,1)S(1)} %get-tuple-element.77), channel_id=1, source_target_pairs={{14,0},{15,1},{8,2},{9,3},{10,4},{11,5},{12,6},{13,7},{22,8},{23,9... | collective-permute-start | bytes 393224 | tf_op jit(solution)/shard_map/ppermute | solution.py:485
  51.4 9.7 %collective-permute-start.17 = (bf16[2,256,128]{2,1,0:T(8,128)(2,1)S(1)}, bf16[2,256,128]{2,1,0:T(8,128)(2,1)S(1)}, u32[]{:S(2)}, u32[]{:S(2)}) collective-permute-start(bf16[2,256,128]{2,1,0:T(8,128)(2,1)S(1)} %get-tuple-element.78), channel_id=1, source_target_pairs={{8,0},{9,1},{10,2},{11,3},{12,4},{13,5},{14,6},{15,7},{16,8},{17,9... | collective-permute-start | bytes 393224 | tf_op jit(solution)/shard_map/ppermute | solution.py:485
  54.8 10.1 %collective-permute-start.18 = (bf16[2,256,128]{2,1,0:T(8,128)(2,1)S(1)}, bf16[2,256,128]{2,1,0:T(8,128)(2,1)S(1)}, u32[]{:S(2)}, u32[]{:S(2)}) collective-permute-start(bf16[2,256,128]{2,1,0:T(8,128)(2,1)S(1)} %get-tuple-element.79), channel_id=1, source_target_pairs={{11,0},{10,1},{13,2},{12,3},{15,4},{14,5},{9,6},{8,7},{19,8},{18,9... | collective-permute-start | bytes 393224 | tf_op jit(solution)/shard_map/ppermute | solution.py:485
  59.7 7.4 %collective-permute-start.19 = (bf16[2,256,128]{2,1,0:T(8,128)(2,1)S(1)}, bf16[2,256,128]{2,1,0:T(8,128)(2,1)S(1)}, u32[]{:S(2)}, u32[]{:S(2)}) collective-permute-start(bf16[2,256,128]{2,1,0:T(8,128)(2,1)S(1)} %get-tuple-element.80), channel_id=1, source_target_pairs={{9,0},{8,1},{11,2},{10,3},{13,4},{12,5},{15,6},{14,7},{17,8},{16,9... | collective-permute-start | bytes 393224 | tf_op jit(solution)/shard_map/ppermute | solution.py:485

commit v9 on v0

v9 whole, which is shorter than its diff:
```python
import functools

import jax
import jax.numpy as jnp
from jax import lax
from jax.experimental import pallas as pl
from jax.experimental.pallas import tpu as pltpu
from jax.sharding import PartitionSpec as P

HEAD = 128
FACTOR = HEAD**-0.5
EXPONENT = FACTOR * 1.4426950408889634
MIB = 1 << 20
NT = ((1,), (1,))
HBM = pl.BlockSpec(memory_space=pltpu.HBM)
VMEM = pl.BlockSpec(memory_space=pltpu.VMEM)


def passed_along(block, distance):
    count = lax.axis_size("segment")
    return lax.ppermute(block, "segment", [((i - distance) % count, i) for i in range(count)])


def swapped(blocks):
    return lax.all_to_all(blocks, ("seq", "tp"), split_axis=0, concat_axis=0, tiled=True)


def pack(pairs, groups, heads):
    _, rows, _, width = pairs.shape

    def kernel(pairs_ref, *outs):
        @pl.loop(0, rows // 16)
        def _(r):
            here = pl.ds(pl.multiple_of(r * 16, 16), 16)
            for g in range(groups):
                for h, out in enumerate(outs):
                    column = (g * heads + h) * HEAD
                    out[g, here] = pairs_ref[0, here, :, column : column + HEAD]

    return pl.pallas_call(
        kernel,
        out_shape=[jax.ShapeDtypeStruct((groups, rows, 2, HEAD), pairs.dtype)] * heads,
        in_specs=[VMEM],
        out_specs=[VMEM] * heads,
        compiler_params=pltpu.CompilerParams(vmem_limit_bytes=24 * MIB),
        name="pack",
    )(pairs)


def unpack(blocks, width):
    heads = len(blocks)
    groups, rows, _, _ = blocks[0].shape
    parts = 4 if rows % 64 == 0 else 1
    size = rows // parts

    def kernel(*refs):
        ins, out, held, sem = refs[:heads], refs[heads], refs[-2], refs[-1]

        def store(r):
            here = pl.ds(pl.multiple_of(r * size, size), size)
            return pltpu.make_async_copy(held.at[here], out.at[0, here], sem.at[r])

        @pl.loop(0, parts)
        def _(r):
            here = pl.ds(pl.multiple_of(r * size, size), size)
            for g in range(groups):
                for h, block in enumerate(ins):
                    column = (g * heads + h) * HEAD
                    held[here, :, column : column + HEAD] = block[g, here]
            store(r).start()

        for r in range(parts):
            store(r).wait()

    return pl.pallas_call(
        kernel,
        out_shape=jax.ShapeDtypeStruct((1, rows, 2, width), blocks[0].dtype),
        in_specs=[VMEM] * heads,
        out_specs=HBM,
        scratch_shapes=[
            pltpu.VMEM((rows, 2, width), blocks[0].dtype),
            pltpu.SemaphoreType.DMA((parts,)),
        ],
        compiler_params=pltpu.CompilerParams(vmem_limit_bytes=24 * MIB),
        name="unpack",
    )(*blocks)


def turned(arrays, head):
    _, tokens, _ = arrays[0].shape
    tile = 256 if tokens % 256 == 0 else tokens
    columns = slice(head * HEAD, (head + 1) * HEAD)

    def kernel(*refs):
        out = refs[-1]
        for i, ref in enumerate(refs[:-1]):
            for j in range(tokens // tile):
                here = slice(j * tile, (j + 1) * tile)
                block = ref[0, here, columns].astype(jnp.float32)
                out[i, :, here] = block.T.astype(out.dtype)

    return pl.pallas_call(
        kernel,
        out_shape=jax.ShapeDtypeStruct((len(arrays), HEAD, tokens), arrays[0].dtype),
        in_specs=[VMEM] * len(arrays),
        out_specs=VMEM,
        compiler_params=pltpu.CompilerParams(vmem_limit_bytes=16 * MIB),
        name="turned",
    )(*arrays)


def turned_back(per_head):
    count, _, tokens = per_head[0].shape
    heads = len(per_head)
    tile = 256 if tokens % 256 == 0 else tokens

    def kernel(*refs):
        ins, outs = refs[:heads], refs[heads:]
        for i, out in enumerate(outs):
            for h, block in enumerate(ins):
                for j in range(tokens // tile):
                    here = slice(j * tile, (j + 1) * tile)
                    rows = block[i, :, here].astype(jnp.float32).T
                    out[0, here, h * HEAD : (h + 1) * HEAD] = rows.astype(out.dtype)

    shape = jax.ShapeDtypeStruct((1, tokens, heads * HEAD), per_head[0].dtype)
    return pl.pallas_call(
        kernel,
        out_shape=[shape] * count,
        in_specs=[VMEM] * heads,
        out_specs=[VMEM] * count,
        compiler_params=pltpu.CompilerParams(vmem_limit_bytes=16 * MIB),
        name="turned_back",
    )(*per_head)


def tiles(count):
    def run(body):
        if count <= 3:
            for j in range(count):
                body(j)
        else:
            pl.loop(0, count)(body)

    return run


def tokens_of(j, tile):
    return pl.ds(j * tile if isinstance(j, int) else pl.multiple_of(j * tile, tile), tile)


def tile_of(rows, tokens):
    for parts in range(1, tokens // 256 + 1):
        if tokens % (256 * parts) == 0 and rows * (tokens // parts) * 4 <= 2 * MIB:
            return tokens // parts
    return 256 if tokens % 256 == 0 else tokens


def dot(a, b, contract=((1,), (0,))):
    return lax.dot_general(a, b, (contract, ((), ())), preferred_element_type=jnp.float32)


def shuffle(rows, join):
    to = lax.broadcasted_iota(jnp.int32, (2 * rows, 2 * rows), 1 if join else 0)
    source = lax.broadcasted_iota(jnp.int32, (2 * rows, 2 * rows), 0 if join else 1)
    wanted = jnp.where(to < rows, 2 * to, 2 * (to - rows) + 1)
    return jnp.where(source == wanted, 1.0, 0.0).astype(jnp.bfloat16)


def attend_kernel(tile, pairs_ref, tokens_ref, result_ref, grads_ref, *scratch):
    k_ref, v_ref, kt_ref, vt_ref, gk_ref, gv_ref = scratch
    groups, pair_rows, _ = pairs_ref.shape
    rows = pair_rows // 2
    split = shuffle(rows, False)
    for g in range(groups):
        both = dot(split, pairs_ref[g])
        here = slice(g * rows, (g + 1) * rows)
        keys, values = both[:rows], both[rows:]
        k_ref[here, :] = keys.astype(jnp.bfloat16)
        v_ref[here, :] = values.astype(jnp.bfloat16)
        kt_ref[:, here] = keys.T.astype(jnp.bfloat16)
        vt_ref[:HEAD, here] = values.T.astype(jnp.bfloat16)
    vt_ref[HEAD:, :] = jnp.ones((vt_ref.shape[0] - HEAD, vt_ref.shape[1]), jnp.bfloat16)
    gk_ref[...] = jnp.zeros_like(gk_ref)
    gv_ref[...] = jnp.zeros_like(gv_ref)

    @tiles(tokens_ref.shape[2] // tile)
    def _(j):
        here = tokens_of(j, tile)
        qt, gt = tokens_ref[0, :, here], tokens_ref[1, :, here]
        scores = dot(k_ref[...], qt)
        grad_weights = dot(v_ref[...], gt)
        top = jnp.max(scores, axis=0, keepdims=True)
        raised = jnp.exp2((scores - top) * EXPONENT)
        low = raised.astype(jnp.bfloat16)
        summed = dot(vt_ref[...], low)
        scale = 1.0 / summed[HEAD : HEAD + 1]
        context = summed[:HEAD] * scale
        row_dot = jnp.sum(gt.astype(jnp.float32) * context, axis=0, keepdims=True)
        result_ref[0, :, here] = context.astype(jnp.bfloat16)
        grad_scores = (raised * (grad_weights - row_dot)).astype(jnp.bfloat16)
        grad_q = dot(kt_ref[...], grad_scores) * (scale * FACTOR)
        result_ref[1, :, here] = grad_q.astype(jnp.bfloat16)
        scaled = (qt.astype(jnp.float32) * (scale * FACTOR)).astype(jnp.bfloat16)
        gk_ref[...] += dot(grad_scores, scaled, NT)
        gv_ref[...] += dot(low, (gt.astype(jnp.float32) * scale).astype(jnp.bfloat16), NT)

    join = shuffle(rows, True)
    for g in range(groups):
        here = slice(g * rows, (g + 1) * rows)
        both = jnp.concatenate([gk_ref[here, :], gv_ref[here, :]], axis=0)
        grads_ref[g] = dot(join, both.astype(jnp.bfloat16)).astype(jnp.bfloat16)


def attend(pairs, both):
    groups, pair_rows, _ = pairs.shape
    enc_len = groups * pair_rows // 2
    tokens = both.shape[2]
    return pl.pallas_call(
        functools.partial(attend_kernel, tile_of(enc_len, tokens)),
        out_shape=[
            jax.ShapeDtypeStruct(both.shape, both.dtype),
            jax.ShapeDtypeStruct(pairs.shape, pairs.dtype),
        ],
        in_specs=[VMEM] * 2,
        out_specs=[VMEM] * 2,
        scratch_shapes=[
            pltpu.VMEM((enc_len, HEAD), jnp.bfloat16),
            pltpu.VMEM((enc_len, HEAD), jnp.bfloat16),
            pltpu.VMEM((HEAD, enc_len), jnp.bfloat16),
            pltpu.VMEM((HEAD + 16, enc_len), jnp.bfloat16),
            pltpu.VMEM((enc_len, HEAD), jnp.float32),
            pltpu.VMEM((enc_len, HEAD), jnp.float32),
        ],
        compiler_params=pltpu.CompilerParams(vmem_limit_bytes=(16 + enc_len * 32 // 4096) * MIB),
        cost_estimate=pl.CostEstimate(
            flops=12 * enc_len * tokens * HEAD,
            bytes_accessed=HEAD * (8 * enc_len + 8 * tokens),
            transcendentals=enc_len * tokens,
        ),
        name="attend",
    )(pairs, both)


def shards(pairs, queries, upstream):
    _, rows, _, width = pairs.shape
    groups = lax.axis_size("seq") * lax.axis_size("tp")
    heads = queries.shape[2] // HEAD
    arrived = []
    for h, block in enumerate(pack(pairs, groups, heads)):
        both = passed_along(turned([queries, upstream], h), -1)
        arrived.append((swapped(block.reshape(groups, 2 * rows, HEAD)), both))
    results, grads = [], []
    for block, both in arrived:
        result, grad = attend(block, both)
        grads.append(swapped(grad).reshape(groups, rows, 2, HEAD))
        results.append(passed_along(result, 1))
    context, grad_query = turned_back(results)
    return context, grad_query, unpack(grads, width)


def solution(mesh):
    return jax.shard_map(
        shards,
        mesh=mesh,
        in_specs=(
            P("segment", ("seq", "tp"), None, None),
            P("segment", None, ("seq", "tp")),
            P("segment", None, ("seq", "tp")),
        ),
        out_specs=(
            P("segment", None, ("seq", "tp")),
            P("segment", None, ("seq", "tp")),
            P("segment", ("seq", "tp"), None, None),
        ),
        check_vma=False,
    )
```

time: 150 us -> 90.1 us (0.60)
  local copies, waits for them, and re-layouts: 36.1 us -> 2.42 us
  blocking collectives: 29.1 us -> 0 us
  matrix products: 24.3 us -> 0 us
  Pallas kernels: 0 us -> 22.5 us
  starting transfers between devices: 7.21 us -> 21.5 us
  other arithmetic: 8.43 us -> 0 us
    all_to_all x1 -> x0, blocking collectives: 29.1 us -> none  [collect_rows(): lax.all_to_all(shaped, ('seq', 'tp'), split_axis=0, concat_axis=3, tiled=...]
    pallas_call x0 -> x7, Pallas kernels: none -> 22.5 us  [the longest x2 17.2 us: attend(): pl.pallas_call(functools.partial(attend_kernel, tile_of(enc_len, tokens))...]
    sub x3 -> x0, matrix products: 13.1 us -> none  [step(): raised = jnp.exp(scores - row_max)]
    all_to_all x1 -> x4, starting transfers between devices: 6.64 us -> 18.9 us  [swapped(): lax.all_to_all(blocks, ('seq', 'tp'), split_axis=0, concat_axis=0, tiled=...]
    dot_general x15 -> x0, matrix products: 11.2 us -> none  [the longest x3 2.75 us: step(): jnp.einsum('bhd,shd->hbs', grad_block, values_all, preferred_element_type...]
    another operation x5 -> x0, local copies, waits for them, and re-layouts: 10.7 us -> none  [the longest x2 4.51 us: shards(): return (context[None], grad_query[None], grad_pairs)]
    convert_element_type x3 -> x0, other arithmetic: 8.19 us -> none  [step(): weights_low = weights.astype(jnp.bfloat16)]
    dynamic_update_slice x3 -> x0, local copies, waits for them, and re-layouts: 4.05 us -> none  [attend(): lax.scan(step, (zeros_start, zeros_start), (query_blocks, grad_blocks))]
  transfers between devices with their start and end apart: 3 -> 8, of which waited for: 3 -> 5; matrix products, arithmetic and copies ran while one was open for 6% -> 0% of each run, Pallas kernels for 0% -> 22%
where the time goes in v9:
time: 90.1 us; the launch traced here: 89.5 us
  waiting for transfers between devices  42.2 us (47%)
  Pallas kernels  22.5 us (25%)
  starting transfers between devices  21.5 us (24%)
  local copies, waits for them, and re-layouts  2.42 us (3%)
    all_to_all x4, waiting for transfers between devices, swapped(): lax.all_to_all(blocks, ('seq', 'tp'), split_axis=0, concat_axis=0, tiled=...  23.9 us
    all_to_all x4, starting transfers between devices, swapped(): lax.all_to_all(blocks, ('seq', 'tp'), split_axis=0, concat_axis=0, tiled=...  18.9 us
    ppermute x4, waiting for transfers between devices, passed_along(): lax.ppermute(block, 'segment', [((i - distance) % count, i) for i in rang...  18.2 us
    pallas_call x2, Pallas kernels, attend(): pl.pallas_call(functools.partial(attend_kernel, tile_of(enc_len, tokens))...  17.2 us
    ppermute x4, starting transfers between devices, passed_along(): lax.ppermute(block, 'segment', [((i - distance) % count, i) for i in rang...  2.66 us
    unnamed x10, local copies, waits for them, and re-layouts  2.42 us
  transfers between devices with their start and end apart: 8, of which 5 were waited for; matrix products, arithmetic and copies ran while one was open for 0% of the time, Pallas kernels for 22%

profile of v9, /device:TPU:0, one launch (start us, length us, event | category | flops | bytes accessed | tf_op | source)
XLA Modules:
  0.0 89.5 jit_solution(13797626033689632442)
XLA Ops:
  0.6 0.0 copy-start.2
  0.6 1.2 %copy-done.2 = bf16[1,128,2,2048]{3,2,1,0:T(2,128)(2,1)S(1)} copy-done((bf16[1,128,2,2048]{3,2,1,0:T(2,128)(2,1)S(1)}, bf16[1,128,2,2048]{3,2,1,0:T(2,128)(2,1)}, u32[]{:S(2)}) %copy-start.2) | copy-done | bytes 1048600
  1.9 0.0 copy-start.1
  1.9 1.7 %pack.1 = (bf16[8,128,2,128]{3,2,1,0:T(2,128)(2,1)}, bf16[8,128,2,128]{3,2,1,0:T(2,128)(2,1)}) custom-call(bf16[1,128,2,2048]{3,2,1,0:T(2,128)(2,1)S(1)} %copy-done.2), custom_call_target="tpu_custom_call" | custom-call | tf_op jit(solution)/shard_map/pack/pallas_call | solution.py:40
  3.6 0.0 copy-start
  3.6 7.4 %all-to-all-start.1 = ((bf16[8,256,128]{2,1,0:T(8,128)(2,1)}), bf16[8,256,128]{2,1,0:T(8,128)(2,1)S(1)}, u32[]{:S(2)}, u32[]{:S(2)}) async-start(bf16[8,256,128]{2,1,0:T(8,128)(2,1)} %bitcast.1), calls=%async_computation.1 | async-start | bytes 1048576 | tf_op jit(solution)/shard_map/all_to_all | solution.py:25
  11.0 0.0 copy-done.1
  11.0 0.0 copy-done
  11.0 0.3 turned.3
  11.3 0.7 collective-permute-start.2
  12.0 13.5 %all-to-all-done.1.pairs_ref = bf16[8,256,128]{2,1,0:T(8,128)(2,1)S(1)} async-done(((bf16[8,256,128]{2,1,0:T(8,128)(2,1)}), bf16[8,256,128]{2,1,0:T(8,128)(2,1)S(1)}, u32[]{:S(2)}, u32[]{:S(2)}) %all-to-all-start.1) | async-done | bytes 524320 | tf_op jit(solution)/shard_map/all_to_all | solution.py:25
  25.5 0.0 copy-start.3
  25.5 0.8 copy-done.3
  26.3 4.1 %all-to-all-start = ((bf16[8,256,128]{2,1,0:T(8,128)(2,1)}), bf16[8,256,128]{2,1,0:T(8,128)(2,1)}, u32[]{:S(2)}, u32[]{:S(2)}) async-start(bf16[8,256,128]{2,1,0:T(8,128)(2,1)} %bitcast), calls=%async_computation | async-start | bytes 1048576 | tf_op jit(solution)/shard_map/all_to_all | solution.py:25
  30.4 0.0 copy-start.4
  30.4 0.3 turned.2
  30.7 0.4 collective-permute-start
  31.1 0.0 collective-permute-done.2.tokens_ref
  31.1 0.4 copy-done.4
  31.5 8.7 %attend.3 = (bf16[2,128,1536]{2,1,0:T(8,128)(2,1)S(1)}, bf16[8,256,128]{2,1,0:T(8,128)(2,1)}) custom-call(bf16[8,256,128]{2,1,0:T(8,128)(2,1)S(1)} %copy-done.4, bf16[2,128,1536]{2,1,0:T(8,128)(2,1)} %collective-permute-done.2.tokens_ref), custom_call_target="tpu_custom_call" | custom-call | flops 2415919104 | bytes 2621440 | tf_op jit(solution)/shard_map/attend/pallas_call | solution.py:219
  40.1 4.6 %all-to-all-done.pairs_ref = bf16[8,256,128]{2,1,0:T(8,128)(2,1)} async-done(((bf16[8,256,128]{2,1,0:T(8,128)(2,1)}), bf16[8,256,128]{2,1,0:T(8,128)(2,1)}, u32[]{:S(2)}, u32[]{:S(2)}) %all-to-all-start) | async-done | bytes 524320 | tf_op jit(solution)/shard_map/all_to_all | solution.py:25
  44.7 3.7 %all-to-all-start.3 = ((bf16[8,256,128]{2,1,0:T(8,128)(2,1)}), bf16[8,256,128]{2,1,0:T(8,128)(2,1)S(1)}, u32[]{:S(2)}, u32[]{:S(2)}) async-start(bf16[8,256,128]{2,1,0:T(8,128)(2,1)} %get-tuple-element.18), calls=%async_computation.3 | async-start | bytes 1048576 | tf_op jit(solution)/shard_map/all_to_all | solution.py:25
  48.4 0.0 collective-permute-done.tokens_ref
  48.4 8.6 %attend.2 = (bf16[2,128,1536]{2,1,0:T(8,128)(2,1)S(1)}, bf16[8,256,128]{2,1,0:T(8,128)(2,1)}) custom-call(bf16[8,256,128]{2,1,0:T(8,128)(2,1)} %all-to-all-done.pairs_ref, bf16[2,128,1536]{2,1,0:T(8,128)(2,1)S(1)} %collective-permute-done.tokens_ref), custom_call_target="tpu_custom_call" | custom-call | flops 2415919104 | bytes 2621440 | tf_op jit(solution)/shard_map/attend/pallas_call | solution.py:219
  57.0 5.9 %all-to-all-done.3 = bf16[8,256,128]{2,1,0:T(8,128)(2,1)S(1)} async-done(((bf16[8,256,128]{2,1,0:T(8,128)(2,1)}), bf16[8,256,128]{2,1,0:T(8,128)(2,1)S(1)}, u32[]{:S(2)}, u32[]{:S(2)}) %all-to-all-start.3) | async-done | bytes 524320 | tf_op jit(solution)/shard_map/all_to_all | solution.py:25
  62.9 3.6 %all-to-all-start.2 = ((bf16[8,256,128]{2,1,0:T(8,128)(2,1)}), bf16[8,256,128]{2,1,0:T(8,128)(2,1)S(1)}, u32[]{:S(2)}, u32[]{:S(2)}) async-start(bf16[8,256,128]{2,1,0:T(8,128)(2,1)} %get-tuple-element.17), calls=%async_computation.2 | async-start | bytes 1048576 | tf_op jit(solution)/shard_map/all_to_all | solution.py:25
  66.5 0.0 collective-permute-start.1
  66.5 1.6 %collective-permute-start.3 = (bf16[2,128,1536]{2,1,0:T(8,128)(2,1)S(1)}, bf16[2,128,1536]{2,1,0:T(8,128)(2,1)S(1)}, u32[]{:S(2)}, u32[]{:S(2)}) collective-permute-start(bf16[2,128,1536]{2,1,0:T(8,128)(2,1)S(1)} %get-tuple-element.14), channel_id=1, source_target_pairs={{24,0},{0,8},{8,16},{16,24},{25,1},{1,9},{9,17},{17,25},{26,2},{2,... | collective-permute-start | bytes 2359304 | tf_op jit(solution)/shard_map/ppermute | solution.py:21
  68.1 9.8 %collective-permute-done.1.refs_0_ = bf16[2,128,1536]{2,1,0:T(8,128)(2,1)S(1)} collective-permute-done((bf16[2,128,1536]{2,1,0:T(8,128)(2,1)S(1)}, bf16[2,128,1536]{2,1,0:T(8,128)(2,1)S(1)}, u32[]{:S(2)}, u32[]{:S(2)}) %collective-permute-start.1) | collective-permute-done | bytes 786464 | tf_op jit(solution)/shard_map/ppermute | solution.py:21
  77.9 8.4 %collective-permute-done.3.refs_1_ = bf16[2,128,1536]{2,1,0:T(8,128)(2,1)S(1)} collective-permute-done((bf16[2,128,1536]{2,1,0:T(8,128)(2,1)S(1)}, bf16[2,128,1536]{2,1,0:T(8,128)(2,1)S(1)}, u32[]{:S(2)}, u32[]{:S(2)}) %collective-permute-start.3) | collective-permute-done | bytes 786464 | tf_op jit(solution)/shard_map/ppermute | solution.py:21
  86.3 1.5 %turned_back.1 = (bf16[1,1536,256]{2,1,0:T(8,128)(2,1)}, bf16[1,1536,256]{2,1,0:T(8,128)(2,1)}) custom-call(bf16[2,128,1536]{2,1,0:T(8,128)(2,1)S(1)} %collective-permute-done.1.refs_0_, bf16[2,128,1536]{2,1,0:T(8,128)(2,1)S(1)} %collective-permute-done.3.refs_1_), custom_call_target="tpu_custom_call" | custom-call | tf_op jit(solution)/shard_map/turned_back/pallas_call | solution.py:127
  87.9 0.0 all-to-all-done.2
  87.9 1.5 %unpack.1 = bf16[1,128,2,2048]{3,2,1,0:T(2,128)(2,1)} custom-call(bf16[8,128,2,128]{3,2,1,0:T(2,128)(2,1)S(1)} %bitcast.5, bf16[8,128,2,128]{3,2,1,0:T(2,128)(2,1)S(1)} %bitcast.4), custom_call_target="tpu_custom_call" | custom-call | tf_op jit(solution)/shard_map/unpack/pallas_call | solution.py:75
Async XLA Ops:
  0.6 1.2 %copy-start.2 = (bf16[1,128,2,2048]{3,2,1,0:T(2,128)(2,1)S(1)}, bf16[1,128,2,2048]{3,2,1,0:T(2,128)(2,1)}, u32[]{:S(2)}) copy-start(bf16[1,128,2,2048]{3,2,1,0:T(2,128)(2,1)} %pairs_ref.1) | copy-start | bytes 3145732
  1.9 9.1 %copy-start.1 = (bf16[1,1536,256]{2,1,0:T(8,128)(2,1)S(1)}, bf16[1,1536,256]{2,1,0:T(8,128)(2,1)}, u32[]{:S(2)}) copy-start(bf16[1,1536,256]{2,1,0:T(8,128)(2,1)} %refs_1_.3) | copy-start | bytes 2359300
  3.6 7.4 %copy-start = (bf16[1,1536,256]{2,1,0:T(8,128)(2,1)S(1)}, bf16[1,1536,256]{2,1,0:T(8,128)(2,1)}, u32[]{:S(2)}) copy-start(bf16[1,1536,256]{2,1,0:T(8,128)(2,1)} %refs_0_.3) | copy-start | bytes 2359300
  3.6 21.9 %all-to-all-start.1 = ((bf16[8,256,128]{2,1,0:T(8,128)(2,1)}), bf16[8,256,128]{2,1,0:T(8,128)(2,1)S(1)}, u32[]{:S(2)}, u32[]{:S(2)}) async-start(bf16[8,256,128]{2,1,0:T(8,128)(2,1)} %bitcast.1), calls=%async_computation.1 | async-start | bytes 1048576 | tf_op jit(solution)/shard_map/all_to_all | solution.py:25
  11.3 19.8 %collective-permute-start.2 = (bf16[2,128,1536]{2,1,0:T(8,128)(2,1)S(1)}, bf16[2,128,1536]{2,1,0:T(8,128)(2,1)}, u32[]{:S(2)}, u32[]{:S(2)}) collective-permute-start(bf16[2,128,1536]{2,1,0:T(8,128)(2,1)S(1)} %turned.3), channel_id=1, source_target_pairs={{8,0},{16,8},{24,16},{0,24},{9,1},{17,9},{25,17},{1,25},{10,2},{18... | collective-permute-start | bytes 2359304 | tf_op jit(solution)/shard_map/ppermute | solution.py:21
  25.5 0.8 copy-start.3
  26.3 18.4 %all-to-all-start = ((bf16[8,256,128]{2,1,0:T(8,128)(2,1)}), bf16[8,256,128]{2,1,0:T(8,128)(2,1)}, u32[]{:S(2)}, u32[]{:S(2)}) async-start(bf16[8,256,128]{2,1,0:T(8,128)(2,1)} %bitcast), calls=%async_computation | async-start | bytes 1048576 | tf_op jit(solution)/shard_map/all_to_all | solution.py:25
  30.4 1.0 %copy-start.4 = (bf16[8,256,128]{2,1,0:T(8,128)(2,1)S(1)}, bf16[8,256,128]{2,1,0:T(8,128)(2,1)}, u32[]{:S(2)}) copy-start(bf16[8,256,128]{2,1,0:T(8,128)(2,1)} %copy-done.3) | copy-start | bytes 1572868
  30.7 17.7 %collective-permute-start = (bf16[2,128,1536]{2,1,0:T(8,128)(2,1)S(1)}, bf16[2,128,1536]{2,1,0:T(8,128)(2,1)S(1)}, u32[]{:S(2)}, u32[]{:S(2)}) collective-permute-start(bf16[2,128,1536]{2,1,0:T(8,128)(2,1)S(1)} %turned.2), channel_id=1, source_target_pairs={{8,0},{16,8},{24,16},{0,24},{9,1},{17,9},{25,17},{1,25},{10,2},{18... | collective-permute-start | bytes 2359304 | tf_op jit(solution)/shard_map/ppermute | solution.py:21
  44.7 18.1 %all-to-all-start.3 = ((bf16[8,256,128]{2,1,0:T(8,128)(2,1)}), bf16[8,256,128]{2,1,0:T(8,128)(2,1)S(1)}, u32[]{:S(2)}, u32[]{:S(2)}) async-start(bf16[8,256,128]{2,1,0:T(8,128)(2,1)} %get-tuple-element.18), calls=%async_computation.3 | async-start | bytes 1048576 | tf_op jit(solution)/shard_map/all_to_all | solution.py:25
  62.9 25.0 %all-to-all-start.2 = ((bf16[8,256,128]{2,1,0:T(8,128)(2,1)}), bf16[8,256,128]{2,1,0:T(8,128)(2,1)S(1)}, u32[]{:S(2)}, u32[]{:S(2)}) async-start(bf16[8,256,128]{2,1,0:T(8,128)(2,1)} %get-tuple-element.17), calls=%async_computation.2 | async-start | bytes 1048576 | tf_op jit(solution)/shard_map/all_to_all | solution.py:25
  66.5 11.4 %collective-permute-start.1 = (bf16[2,128,1536]{2,1,0:T(8,128)(2,1)S(1)}, bf16[2,128,1536]{2,1,0:T(8,128)(2,1)S(1)}, u32[]{:S(2)}, u32[]{:S(2)}) collective-permute-start(bf16[2,128,1536]{2,1,0:T(8,128)(2,1)S(1)} %get-tuple-element.12), channel_id=1, source_target_pairs={{24,0},{0,8},{8,16},{16,24},{25,1},{1,9},{9,17},{17,25},{26,2},{2,... | collective-permute-start | bytes 2359304 | tf_op jit(solution)/shard_map/ppermute | solution.py:21
  66.5 19.8 %collective-permute-start.3 = (bf16[2,128,1536]{2,1,0:T(8,128)(2,1)S(1)}, bf16[2,128,1536]{2,1,0:T(8,128)(2,1)S(1)}, u32[]{:S(2)}, u32[]{:S(2)}) collective-permute-start(bf16[2,128,1536]{2,1,0:T(8,128)(2,1)S(1)} %get-tuple-element.14), channel_id=1, source_target_pairs={{24,0},{0,8},{8,16},{16,24},{25,1},{1,9},{9,17},{17,25},{26,2},{2,... | collective-permute-start | bytes 2359304 | tf_op jit(solution)/shard_map/ppermute | solution.py:21

commit v10 on v5

--- a/solution.py
+++ b/solution.py
@@ -14,25 +14,31 @@
 MIB = 1 << 20
 NT = ((1,), (1,))
 ANY = pl.BlockSpec(memory_space=pl.ANY)
+HBM = pl.BlockSpec(memory_space=pltpu.HBM)
 VMEM = pl.BlockSpec(memory_space=pltpu.VMEM)
 
 
-def offsets():
+def partner(index, distance, count):
+    if count & (count - 1):
+        return (index + distance) % count
+    return index ^ distance
+
+
+def offset_groups():
     seq_count = lax.axis_size("seq")
     tp_count = lax.axis_size("tp")
-    near = [(0, dy) for dy in reversed(range(tp_count))]
-    order = [(dz, dy) for dz in range(1, seq_count) for dy in reversed(range(tp_count))]
-    order.sort(key=lambda o: -abs(o[0] - seq_count / 2))
-    for i, offset in enumerate(near):
-        order.insert(3 + 2 * i, offset)
-    return order
+    middle = seq_count // 2
+    far = [(dz, dy) for dy in reversed(range(tp_count)) for dz in range(middle, seq_count)]
+    near = [(dz, dy) for dy in reversed(range(tp_count)) for dz in reversed(range(middle))]
+    f, n = max(1, len(far) // 4), len(near) // 2
+    return [far[:f] + near[:n], far[f : 2 * f] + near[n:] + far[2 * f : -f], far[-f:]]
 
 
 def group_at(offset):
     seq_count = lax.axis_size("seq")
     tp_count = lax.axis_size("tp")
-    z = lax.rem(lax.axis_index("seq") + offset[0], seq_count)
-    y = lax.rem(lax.axis_index("tp") + offset[1], tp_count)
+    z = partner(lax.axis_index("seq"), offset[0], seq_count)
+    y = partner(lax.axis_index("tp"), offset[1], tp_count)
     return z * tp_count + y
 
 
@@ -44,8 +50,8 @@
             for y in range(tp_count):
                 source = (s * seq_count + z) * tp_count + y
                 s_to = (s + 1) % segments
-                z_to = (z + offset[0]) % seq_count
-                y_to = (y + offset[1]) % tp_count
+                z_to = partner(z, offset[0], seq_count)
+                y_to = partner(y, offset[1], tp_count)
                 target = (s_to * seq_count + z_to) * tp_count + y_to
                 hops.append((target, source) if back else (source, target))
     return hops
@@ -63,11 +69,11 @@
         @pl.loop(0, rows // 16)
         def _(r):
             here = pl.ds(pl.multiple_of(r * 16, 16), 16)
-            for i, offset in enumerate(order):
+            for out, offset in zip(outs, order):
                 base = group_at(offset) * local
                 for h in range(heads):
                     column = pl.multiple_of(base + h * HEAD, HEAD)
-                    outs[i][h, here] = pairs_ref[0, here, :, pl.ds(column, HEAD)]
+                    out[h, here] = pairs_ref[0, here, :, pl.ds(column, HEAD)]
 
     return pl.pallas_call(
         kernel,
@@ -82,24 +88,38 @@
 def unpack(blocks, order, width):
     heads, rows, _, _ = blocks[0].shape
     local = heads * HEAD
+    parts = 4 if rows % 64 == 0 else 1
+    size = rows // parts
 
     def kernel(*refs):
-        ins, out = refs[: len(order)], refs[len(order)]
-
-        @pl.loop(0, rows // 16)
+        ins, out, held, sem = refs[: len(order)], refs[len(order)], refs[-2], refs[-1]
+
+        def store(r):
+            here = pl.ds(pl.multiple_of(r * size, size), size)
+            return pltpu.make_async_copy(held.at[here], out.at[0, here], sem.at[r])
+
+        @pl.loop(0, parts)
         def _(r):
-            here = pl.ds(pl.multiple_of(r * 16, 16), 16)
-            for i, offset in enumerate(order):
+            here = pl.ds(pl.multiple_of(r * size, size), size)
+            for block, offset in zip(ins, order):
                 base = group_at(offset) * local
                 for h in range(heads):
                     column = pl.multiple_of(base + h * HEAD, HEAD)
-                    out[0, here, :, pl.ds(column, HEAD)] = ins[i][h, here]
+                    held[here, :, pl.ds(column, HEAD)] = block[h, here]
+            store(r).start()
+
+        for r in range(parts):
+            store(r).wait()
 
     return pl.pallas_call(
         kernel,
         out_shape=jax.ShapeDtypeStruct((1, rows, 2, width), blocks[0].dtype),
         in_specs=[VMEM] * len(order),
-        out_specs=VMEM,
+        out_specs=HBM,
+        scratch_shapes=[
+            pltpu.VMEM((rows, 2, width), blocks[0].dtype),
+            pltpu.SemaphoreType.DMA((parts,)),
+        ],
         compiler_params=pltpu.CompilerParams(vmem_limit_bytes=24 * MIB),
         name="unpack",
     )(*blocks)
@@ -229,16 +249,13 @@
             context_ref[h, :, here] = context
 
 
-def gradients(raised, low, shrunk, stats, h, here, refs):
-    qt_ref, gt_ref, v_ref, kt_ref, gk_ref, gv_ref = refs
-    scale, row_dot = stats
-    qt = qt_ref[h, :, here].astype(jnp.float32)
-    gt = gt_ref[h, :, here]
+def gradients(raised, low, scale, row_dot, qt, gt, refs, h):
+    v_ref, kt_ref, gk_ref, gv_ref = refs
     grad_weights = dot(v_ref[h], gt)
     grad_scores = (raised * (grad_weights - row_dot)).astype(jnp.bfloat16)
-    scale = scale if shrunk is None else scale * shrunk
     grad_q = dot(kt_ref[h], grad_scores) * (scale * FACTOR)
-    gk_ref[h] += dot(grad_scores, (qt * (scale * FACTOR)).astype(jnp.bfloat16), NT)
+    scaled = (qt.astype(jnp.float32) * (scale * FACTOR)).astype(jnp.bfloat16)
+    gk_ref[h] += dot(grad_scores, scaled, NT)
     gv_ref[h] += dot(low, (gt.astype(jnp.float32) * scale).astype(jnp.bfloat16), NT)
     return grad_q
 
@@ -248,7 +265,7 @@
     qt_ref, gt_ref, stats_in, context_in = refs[:4]
     stats_ref, context_ref, grad_q_ref = refs[4:7]
     outs, refs = refs[7 : 7 + count], refs[7 + count :]
-    k_ref, v_ref, kt_ref, vt_ref, gk_ref, gv_ref = refs
+    k_ref, vt_ref, v_ref, kt_ref, gk_ref, gv_ref = refs
     heads, pair_rows, _ = chunks[0].shape
     rows = pair_rows // 2
     for h in range(heads):
@@ -260,40 +277,32 @@
     def _(j):
         here = tokens_of(j, tile)
         for h in range(heads):
+            qt, gt = qt_ref[h, :, here], gt_ref[h, :, here]
             before = (stats_in[h, 0:1, here], stats_in[h, 1:2, here], context_in[h, :, here])
-            raised, low, top, total, context = raise_scores(
-                k_ref[h], qt_ref[h, :, here], vt_ref[h], before
-            )
+            raised, low, top, total, context = raise_scores(k_ref[h], qt, vt_ref[h], before)
             scale = 1.0 / total
             context = context * scale
-            row_dot = jnp.sum(
-                gt_ref[h, :, here].astype(jnp.float32) * context, axis=0, keepdims=True
-            )
+            row_dot = jnp.sum(gt.astype(jnp.float32) * context, axis=0, keepdims=True)
             context_ref[h, :, here] = context
             stats_ref[h, 0:1, here] = top
             stats_ref[h, 1:2, here] = scale
             stats_ref[h, 2:3, here] = row_dot
             grad_q_ref[h, :, here] = gradients(
-                raised,
-                low,
-                None,
-                (scale, row_dot),
-                h,
-                here,
-                (qt_ref, gt_ref, v_ref, kt_ref, gk_ref, gv_ref),
+                raised, low, scale, row_dot, qt, gt, (v_ref, kt_ref, gk_ref, gv_ref), h
             )
 
     for h in range(heads):
         join_chunks(outs, h, rows, gk_ref, gv_ref)
 
 
-def backward_kernel(back, count, ready, last, tile, *refs):
-    chunks, refs = refs[back : back + count], refs[back + count :]
-    qt_ref, gt_ref, low_ref, stats_then, stats_ref, grad_q_in = refs[:6]
+def backward_kernel(back, count, first, last, tile, *refs):
+    refs = refs[back:]
+    chunks, refs = refs[:count], refs[count:]
+    low_ref, then_ref, qt_ref, gt_ref, stats_ref, grad_q_in = refs[:6]
     refs = refs[6:]
-    if ready:
+    if first:
         ready_ref, refs = refs[0], refs[1:]
-    if ready or last:
+    if first or last:
         rows_ref, refs = refs[0], refs[1:]
     if not last:
         grad_q_ref, refs = refs[0], refs[1:]
@@ -311,23 +320,19 @@
         here = tokens_of(j, tile)
         for h in range(heads):
             columns = slice(h * HEAD, (h + 1) * HEAD)
+            qt, gt = qt_ref[h, :, here], gt_ref[h, :, here]
+            top, scale, row_dot = (stats_ref[h, i : i + 1, here] for i in range(3))
+            shrunk = jnp.exp2((then_ref[h, 0:1, here] - top) * EXPONENT)
             low = low_ref[h, :, here]
-            top, scale, row_dot = (stats_ref[h, i : i + 1, here] for i in range(3))
-            shrunk = jnp.exp2((stats_then[h, 0:1, here] - top) * EXPONENT)
+            raised = low.astype(jnp.float32)
             grad_q = grad_q_in[h, :, here] + gradients(
-                low.astype(jnp.float32),
-                low,
-                shrunk,
-                (scale, row_dot),
-                h,
-                here,
-                (qt_ref, gt_ref, v_ref, kt_ref, gk_ref, gv_ref),
+                raised, low, scale * shrunk, row_dot, qt, gt, refs, h
             )
             if last:
                 rows_ref[0, here, columns] = grad_q.T.astype(rows_ref.dtype)
             else:
                 grad_q_ref[h, :, here] = grad_q
-            if ready:
+            if first:
                 rows_ref[0, here, columns] = ready_ref[h, :, here].T.astype(rows_ref.dtype)
 
     for h in range(heads):
@@ -342,18 +347,16 @@
     )
 
 
-def attend(arrived, queries, upstream, send_back):
-    heads, pair_rows, _ = arrived[0].shape
+def attend(groups, queries, upstream, send_back):
+    heads, pair_rows, _ = groups[0][0].shape
     rows = pair_rows // 2
-    enc_len = len(arrived) * rows
+    enc_len = sum(len(g) for g in groups) * rows
     tokens = queries.shape[1]
     qt, gt = turned(queries), turned(upstream)
     stats_shape = jax.ShapeDtypeStruct((heads, 8, tokens), jnp.float32)
     wide_shape = jax.ShapeDtypeStruct((heads, HEAD, tokens), jnp.float32)
     rows_shape = jax.ShapeDtypeStruct(queries.shape, queries.dtype)
     compiler_params = params(enc_len)
-    turn_at = len(arrived) - len(arrived) // 4
-    half = (turn_at + 1) // 2
 
     def natural(count):
         return pltpu.VMEM((heads, count * rows, HEAD), jnp.bfloat16)
@@ -367,9 +370,10 @@
     def shapes_of(group):
         return [jax.ShapeDtypeStruct(c.shape, c.dtype) for c in group]
 
-    state, parts = [], []
-    for begin, end in ((0, half), (half, turn_at)):
-        group, count = arrived[begin:end], end - begin
+    waits = {1: [], 0: [0]}
+    state, kept = [], []
+    for group in groups[:-1]:
+        count = len(group)
         low_shape = jax.ShapeDtypeStruct((heads, count * rows, tokens), jnp.bfloat16)
         stats, context, low = pl.pallas_call(
             functools.partial(forward_kernel, count, not state, tile_of(count * rows, tokens)),
@@ -382,66 +386,72 @@
             name="forward",
         )(*group, qt, *state)
         state = [stats, context]
-        parts.insert(0, (begin, count, low, stats))
-
-    group, count = arrived[turn_at:], len(arrived) - turn_at
+        kept.append((low, stats))
+
+    group, count = groups[-1], len(groups[-1])
     final, context, grad_q, *grads = pl.pallas_call(
         functools.partial(turn_kernel, count, tile_of(count * rows, tokens)),
         out_shape=[stats_shape, wide_shape, wide_shape] + shapes_of(group),
         in_specs=[VMEM] * (count + 4),
         out_specs=[VMEM] * (count + 3),
-        scratch_shapes=[natural(count), natural(count), across(count), across(count, 16)]
+        scratch_shapes=[natural(count), across(count, 16), natural(count), across(count)]
         + [sums(count)] * 2,
         compiler_params=compiler_params,
         cost_estimate=cost(heads, count * rows, tokens, 6),
         name="turn",
     )(*group, qt, gt, *state)
-    returned = [send_back(turn_at, grads)]
-
-    for i, (begin, count, low, then) in enumerate(parts):
-        group = arrived[begin : begin + count]
-        ready, last = i == 0, i == len(parts) - 1
-        back = returned[i - 1] if i >= 1 else []
-        extra = [rows_shape] * (ready or last) + [wide_shape] * (not last)
+    returned = [send_back(len(groups) - 1, grads)]
+
+    for i in reversed(range(len(groups) - 1)):
+        group, count = groups[i], len(groups[i])
+        first, last = i == len(groups) - 2, i == 0
+        back = sum((returned[k] for k in waits[i]), [])
+        operands = [*group, *kept[i], qt, gt, final, grad_q, *([context] if first else [])]
+        shapes = [rows_shape] * (first or last) + [wide_shape] * (not last)
         outs = pl.pallas_call(
             functools.partial(
-                backward_kernel, len(back), count, ready, last, tile_of(count * rows, tokens)
+                backward_kernel, len(back), count, first, last, tile_of(count * rows, tokens)
             ),
-            out_shape=extra + shapes_of(group),
-            in_specs=[ANY] * len(back) + [VMEM] * (count + 6 + ready),
-            out_specs=[VMEM] * (len(extra) + count),
-            scratch_shapes=[natural(count), across(count)] + [sums(count)] * 2,
+            out_shape=shapes + shapes_of(group),
+            in_specs=[ANY] * len(back) + [VMEM] * len(operands),
+            out_specs=[VMEM] * (len(shapes) + count),
+            scratch_shapes=[natural(count), across(count), sums(count), sums(count)],
             compiler_params=compiler_params,
             cost_estimate=cost(heads, count * rows, tokens, 4),
             name="backward",
-        )(*back, *group, qt, gt, low, then, final, grad_q, *([context] if ready else []))
-        if ready:
+        )(*back, *operands)
+        if first:
             context_rows = outs[0]
         if last:
             grad_query = outs[0]
         else:
-            grad_q = outs[len(extra) - 1]
-        returned.append(send_back(begin, outs[len(extra) :]))
-    return context_rows, grad_query, returned
+            grad_q = outs[len(shapes) - 1]
+        returned.append(send_back(i, outs[len(shapes) :]))
+    return context_rows, grad_query
 
 
 def shards(pairs, queries, upstream):
     _, rows, _, width = pairs.shape
     heads = queries.shape[2] // HEAD
-    order = offsets()
-    arrived = []
+    offsets = offset_groups()
+    order = sum(offsets, [])
+    blocks = []
     for offset, block in zip(order, pack(pairs, order, heads)):
         block = block.reshape(heads, 2 * rows, HEAD)
-        arrived.append(lax.ppermute(block, AXES, route(offset, False)))
-    homes = []
-
-    def send_back(begin, blocks):
-        there = order[begin : begin + len(blocks)]
-        homes.extend(there)
-        return [lax.ppermute(b, AXES, route(o, True)) for o, b in zip(there, blocks)]
-
-    context, grad_query, parts = attend(arrived, queries, upstream, send_back)
-    returned = [b.reshape(heads, rows, 2, HEAD) for part in parts for b in part]
+        blocks.append(lax.ppermute(block, AXES, route(offset, False)))
+    groups = []
+    for group in offsets:
+        groups.append(blocks[: len(group)])
+        blocks = blocks[len(group) :]
+    homes, returned = [], []
+
+    def send_back(i, grads):
+        back = [lax.ppermute(g, AXES, route(o, True)) for o, g in zip(offsets[i], grads)]
+        homes.extend(offsets[i])
+        returned.extend(b.reshape(heads, rows, 2, HEAD) for b in back)
+        return back
+
+    context, grad_query = attend(groups, queries, upstream, send_back)
     return context, grad_query, unpack(returned, homes, width)
 
 

time: 71.1 us -> 69.5 us (0.977)
  waiting for transfers between devices: 21.3 us -> 18.3 us
  Pallas kernels: 20.3 us -> 21.3 us
    ppermute x16, waiting for transfers between devices: 21.3 us -> 18.3 us  [the longest x8 10.4 us: shards(): blocks.append(lax.ppermute(block, AXES, route(offset, False)))]
    pallas_call x2, Pallas kernels: 7.94 us -> 9.39 us  [attend(): pl.pallas_call(functools.partial(backward_kernel, len(back), count, first...]
    pallas_call x1, Pallas kernels: 4 us -> 2.57 us  [attend(): pl.pallas_call(functools.partial(turn_kernel, count, tile_of(count * rows...]
    pallas_call x2, Pallas kernels: 5.09 us -> 6.4 us  [attend(): pl.pallas_call(functools.partial(forward_kernel, count, not state, tile_o...]
    ppermute x16, starting transfers between devices: 26.9 us -> 27.6 us  [the longest x8 14.4 us: shards(): blocks.append(lax.ppermute(block, AXES, route(offset, False)))]
  transfers between devices with their start and end apart: 16 -> 16, of which waited for: 9 -> 5; matrix products, arithmetic and copies ran while one was open for 0% -> 0% of each run, Pallas kernels for 19% -> 24%
where the time goes in v10:
time: 69.5 us; the launch traced here: 69.4 us
  starting transfers between devices  27.6 us (40%)
  Pallas kernels  21.3 us (31%)
  waiting for transfers between devices  18.3 us (26%)
  local copies, waits for them, and re-layouts  1.23 us (2%)
  between operations  0.9 us (1%)
    ppermute x8, starting transfers between devices, shards(): blocks.append(lax.ppermute(block, AXES, route(offset, False)))  14.4 us
    ppermute x8, starting transfers between devices, send_back(): lax.ppermute(g, AXES, route(o, True))  13.3 us
    ppermute x8, waiting for transfers between devices, shards(): blocks.append(lax.ppermute(block, AXES, route(offset, False)))  10.4 us
    pallas_call x2, Pallas kernels, attend(): pl.pallas_call(functools.partial(backward_kernel, len(back), count, first...  9.39 us
    ppermute x8, waiting for transfers between devices, send_back(): lax.ppermute(g, AXES, route(o, True))  7.84 us
    pallas_call x2, Pallas kernels, attend(): pl.pallas_call(functools.partial(forward_kernel, count, not state, tile_o...  6.4 us
    pallas_call x1, Pallas kernels, attend(): pl.pallas_call(functools.partial(turn_kernel, count, tile_of(count * rows...  2.57 us
    pallas_call x1, Pallas kernels, unpack(): pl.pallas_call(kernel, out_shape=jax.ShapeDtypeStruct((1, rows, 2, width)...  1.51 us
  transfers between devices with their start and end apart: 16, of which 5 were waited for; matrix products, arithmetic and copies ran while one was open for 0% of the time, Pallas kernels for 24%

profile of v10, /device:TPU:0, one launch (start us, length us, event | category | flops | bytes accessed | tf_op | source)
XLA Modules:
  0.0 69.4 jit_solution(15694954462238232547)
XLA Ops:
  0.6 0.0 copy-start
  0.6 1.2 %copy-done = bf16[1,128,2,2048]{3,2,1,0:T(2,128)(2,1)S(1)} copy-done((bf16[1,128,2,2048]{3,2,1,0:T(2,128)(2,1)S(1)}, bf16[1,128,2,2048]{3,2,1,0:T(2,128)(2,1)}, u32[]{:S(2)}) %copy-start) | copy-done | bytes 1048600
  1.9 0.0 copy-start.1
  1.9 0.0 copy-start.2
  1.9 0.9 %pack.1 = (bf16[2,128,2,128]{3,2,1,0:T(2,128)(2,1)S(1)}, bf16[2,128,2,128]{3,2,1,0:T(2,128)(2,1)S(1)}, bf16[2,128,2,128]{3,2,1,0:T(2,128)(2,1)S(1)}, bf16[2,128,...) custom-call(bf16[1,128,2,2048]{3,2,1,0:T(2,128)(2,1)S(1)} %copy-done), custom_call_target="tpu_custom_call" | custom-call | tf_op jit(solution)/shard_map/pack/pallas_call | solution.py:78
  2.8 4.5 %collective-permute-start.4 = (bf16[2,256,128]{2,1,0:T(8,128)(2,1)S(1)}, bf16[2,256,128]{2,1,0:T(8,128)(2,1)S(1)}, u32[]{:S(2)}, u32[]{:S(2)}) collective-permute-start(bf16[2,256,128]{2,1,0:T(8,128)(2,1)S(1)} %bitcast.31), channel_id=1, source_target_pairs={{0,13},{1,12},{2,15},{3,14},{4,9},{5,8},{6,11},{7,10},{8,21},{9,20... | collective-permute-start | bytes 393224 | tf_op jit(solution)/shard_map/ppermute | solution.py:441
  7.2 2.7 %collective-permute-start.5 = (bf16[2,256,128]{2,1,0:T(8,128)(2,1)S(1)}, bf16[2,256,128]{2,1,0:T(8,128)(2,1)S(1)}, u32[]{:S(2)}, u32[]{:S(2)}) collective-permute-start(bf16[2,256,128]{2,1,0:T(8,128)(2,1)S(1)} %bitcast.30), channel_id=1, source_target_pairs={{0,11},{1,10},{2,9},{3,8},{4,15},{5,14},{6,13},{7,12},{8,19},{9,18... | collective-permute-start | bytes 393224 | tf_op jit(solution)/shard_map/ppermute | solution.py:441
  10.0 1.0 %collective-permute-start.6 = (bf16[2,256,128]{2,1,0:T(8,128)(2,1)S(1)}, bf16[2,256,128]{2,1,0:T(8,128)(2,1)S(1)}, u32[]{:S(2)}, u32[]{:S(2)}) collective-permute-start(bf16[2,256,128]{2,1,0:T(8,128)(2,1)S(1)} %bitcast.29), channel_id=1, source_target_pairs={{0,9},{1,8},{2,11},{3,10},{4,13},{5,12},{6,15},{7,14},{8,17},{9,16... | collective-permute-start | bytes 393224 | tf_op jit(solution)/shard_map/ppermute | solution.py:441
  10.9 0.7 %collective-permute-start.1 = (bf16[2,256,128]{2,1,0:T(8,128)(2,1)S(1)}, bf16[2,256,128]{2,1,0:T(8,128)(2,1)S(1)}, u32[]{:S(2)}, u32[]{:S(2)}) collective-permute-start(bf16[2,256,128]{2,1,0:T(8,128)(2,1)S(1)} %bitcast.28), channel_id=1, source_target_pairs={{0,10},{1,11},{2,8},{3,9},{4,14},{5,15},{6,12},{7,13},{8,18},{9,19... | collective-permute-start | bytes 393224 | tf_op jit(solution)/shard_map/ppermute | solution.py:441
  11.6 1.1 %collective-permute-start = (bf16[2,256,128]{2,1,0:T(8,128)(2,1)S(1)}, bf16[2,256,128]{2,1,0:T(8,128)(2,1)S(1)}, u32[]{:S(2)}, u32[]{:S(2)}) collective-permute-start(bf16[2,256,128]{2,1,0:T(8,128)(2,1)S(1)} %bitcast.27), channel_id=1, source_target_pairs={{0,15},{1,14},{2,13},{3,12},{4,11},{5,10},{6,9},{7,8},{8,23},{9,22... | collective-permute-start | bytes 393224 | tf_op jit(solution)/shard_map/ppermute | solution.py:441
  12.7 2.0 %collective-permute-done.4.refs_0_.refs_1_ = bf16[2,256,128]{2,1,0:T(8,128)(2,1)S(1)} collective-permute-done((bf16[2,256,128]{2,1,0:T(8,128)(2,1)S(1)}, bf16[2,256,128]{2,1,0:T(8,128)(2,1)S(1)}, u32[]{:S(2)}, u32[]{:S(2)}) %collective-permute-start.4) | collective-permute-done | bytes 131104 | tf_op jit(solution)/shard_map/ppermute | solution.py:441
  14.7 0.0 collective-permute-start.2
  14.7 1.5 %collective-permute-done.5.refs_1_.refs_2_ = bf16[2,256,128]{2,1,0:T(8,128)(2,1)S(1)} collective-permute-done((bf16[2,256,128]{2,1,0:T(8,128)(2,1)S(1)}, bf16[2,256,128]{2,1,0:T(8,128)(2,1)S(1)}, u32[]{:S(2)}, u32[]{:S(2)}) %collective-permute-start.5) | collective-permute-done | bytes 131104 | tf_op jit(solution)/shard_map/ppermute | solution.py:441
  16.2 1.1 %collective-permute-start.3 = (bf16[2,256,128]{2,1,0:T(8,128)(2,1)S(1)}, bf16[2,256,128]{2,1,0:T(8,128)(2,1)S(1)}, u32[]{:S(2)}, u32[]{:S(2)}) collective-permute-start(bf16[2,256,128]{2,1,0:T(8,128)(2,1)S(1)} %bitcast.25), channel_id=1, source_target_pairs={{0,12},{1,13},{2,14},{3,15},{4,8},{5,9},{6,10},{7,11},{8,20},{9,21... | collective-permute-start | bytes 393224 | tf_op jit(solution)/shard_map/ppermute | solution.py:441
  17.2 0.0 copy-done.1
  17.2 0.3 turned.2.refs_3_.refs_4_.refs_1_.refs_6_
  17.5 0.0 copy-done.2
  17.5 0.3 turned.3.refs_2_.refs_7_
  17.8 0.0 collective-permute-done.6.refs_2_.refs_3_
  17.8 3.3 %collective-permute-start.7 = (bf16[2,256,128]{2,1,0:T(8,128)(2,1)S(1)}, bf16[2,256,128]{2,1,0:T(8,128)(2,1)S(1)}, u32[]{:S(2)}, u32[]{:S(2)}) collective-permute-start(bf16[2,256,128]{2,1,0:T(8,128)(2,1)S(1)} %bitcast.24), channel_id=1, source_target_pairs={{0,14},{1,15},{2,12},{3,13},{4,10},{5,11},{6,8},{7,9},{8,22},{9,23... | collective-permute-start | bytes 393224 | tf_op jit(solution)/shard_map/ppermute | solution.py:441
  21.2 2.5 %forward.2 = (f32[2,8,1536]{2,1,0:T(8,128)S(1)}, f32[2,128,1536]{2,1,0:T(8,128)S(1)}, bf16[2,384,1536]{2,1,0:T(8,128)(2,1)S(1)}) custom-call(bf16[2,256,128]{2,1,0:T(8,128)(2,1)S(1)} %collective-permute-done.4.refs_0_.refs_1_, bf16[2,256,128]{2,1,0:T(8,128)(2,1)S(1)} %collective-permute-done.5.refs_1_.refs_2_, ...), custom_call_target="tpu_custom_call" | custom-call | flops 603979776 | bytes 3932160 | tf_op jit(solution)/shard_map/forward/pallas_call | solution.py:378
  23.7 0.0 collective-permute-done.1.refs_1_
  23.7 0.0 collective-permute-done.refs_0_
  23.7 0.0 collective-permute-done.2.refs_2_
  23.7 7.0 %collective-permute-done.3.refs_3_ = bf16[2,256,128]{2,1,0:T(8,128)(2,1)S(1)} collective-permute-done((bf16[2,256,128]{2,1,0:T(8,128)(2,1)S(1)}, bf16[2,256,128]{2,1,0:T(8,128)(2,1)S(1)}, u32[]{:S(2)}, u32[]{:S(2)}) %collective-permute-start.3) | collective-permute-done | bytes 131104 | tf_op jit(solution)/shard_map/ppermute | solution.py:441
  30.7 3.9 %forward.3 = (f32[2,8,1536]{2,1,0:T(8,128)S(1)}, f32[2,128,1536]{2,1,0:T(8,128)S(1)}, bf16[2,512,1536]{2,1,0:T(8,128)(2,1)S(1)}) custom-call(bf16[2,256,128]{2,1,0:T(8,128)(2,1)S(1)} %collective-permute-done.refs_0_, bf16[2,256,128]{2,1,0:T(8,128)(2,1)S(1)} %collective-permute-done.1.refs_1_, bf16[2,256,128]{2,1,0:T(8,128)(2,1)S(1)} %collective-permute-done.2.refs_2_, ...), custom_call_target="tpu_custom_call" | custom-call | flops 805306368 | bytes 4194304 | tf_op jit(solution)/shard_map/forward/pallas_call | solution.py:378
  34.6 0.0 collective-permute-done.7.refs_0_
  34.6 2.6 %turn.1 = (f32[2,8,1536]{2,1,0:T(8,128)S(1)}, f32[2,128,1536]{2,1,0:T(8,128)S(1)}, f32[2,128,1536]{2,1,0:T(8,128)S(1)}, bf16[2,256,128]{2,1,0:T(8,128)(2,1)S(1)}) custom-call(bf16[2,256,128]{2,1,0:T(8,128)(2,1)S(1)} %collective-permute-done.7.refs_0_, bf16[2,128,1536]{2,1,0:T(8,128)(2,1)S(1)} %turned.2.refs_3_.refs_4_.refs_1_.refs_6_, ...), custom_call_target="tpu_custom_call" | custom-call | flops 603979776 | bytes 3407872 | tf_op jit(solution)/shard_map/turn/pallas_call | solution.py:392
  37.2 2.2 %collective-permute-start.8 = (bf16[2,256,128]{2,1,0:T(8,128)(2,1)S(1)}, bf16[2,256,128]{2,1,0:T(8,128)(2,1)S(1)}, u32[]{:S(2)}, u32[]{:S(2)}) collective-permute-start(bf16[2,256,128]{2,1,0:T(8,128)(2,1)S(1)} %get-tuple-element.48), channel_id=1, source_target_pairs={{14,0},{15,1},{12,2},{13,3},{10,4},{11,5},{8,6},{9,7},{22,8},{23,9... | collective-permute-start | bytes 393224 | tf_op jit(solution)/shard_map/ppermute | solution.py:449
  39.4 5.4 %backward.2 = (bf16[1,1536,256]{2,1,0:T(8,128)(2,1)}, f32[2,128,1536]{2,1,0:T(8,128)S(1)}, bf16[2,256,128]{2,1,0:T(8,128)(2,1)S(1)}, bf16[2,256,128]{2,1,0:T(8,1...) custom-call(bf16[2,256,128]{2,1,0:T(8,128)(2,1)S(1)} %collective-permute-done.refs_0_, ...), custom_call_target="tpu_custom_call" | custom-call | flops 1610612736 | bytes 4194304 | tf_op jit(solution)/shard_map/backward/pallas_call | solution.py:411
  44.8 3.2 %collective-permute-start.9 = (bf16[2,256,128]{2,1,0:T(8,128)(2,1)S(1)}, bf16[2,256,128]{2,1,0:T(8,128)(2,1)S(1)}, u32[]{:S(2)}, u32[]{:S(2)}) collective-permute-start(bf16[2,256,128]{2,1,0:T(8,128)(2,1)S(1)} %get-tuple-element.52), channel_id=1, source_target_pairs={{15,0},{14,1},{13,2},{12,3},{11,4},{10,5},{9,6},{8,7},{23,8},{22,9... | collective-permute-start | bytes 393224 | tf_op jit(solution)/shard_map/ppermute | solution.py:449
  48.0 0.0 collective-permute-start.10
  48.0 0.0 collective-permute-start.11
  48.1 1.9 %collective-permute-start.12 = (bf16[2,256,128]{2,1,0:T(8,128)(2,1)S(1)}, bf16[2,256,128]{2,1,0:T(8,128)(2,1)S(1)}, u32[]{:S(2)}, u32[]{:S(2)}) collective-permute-start(bf16[2,256,128]{2,1,0:T(8,128)(2,1)S(1)} %get-tuple-element.55), channel_id=1, source_target_pairs={{12,0},{13,1},{14,2},{15,3},{8,4},{9,5},{10,6},{11,7},{20,8},{21,9... | collective-permute-start | bytes 393224 | tf_op jit(solution)/shard_map/ppermute | solution.py:449
  49.9 0.0 collective-permute-done.8.refs_0_
  49.9 3.9 %backward.3 = (bf16[1,1536,256]{2,1,0:T(8,128)(2,1)}, bf16[2,256,128]{2,1,0:T(8,128)(2,1)S(1)}, bf16[2,256,128]{2,1,0:T(8,128)(2,1)S(1)}, bf16[2,256,128]{2,1,0:T(8,128)(2,1)S(1)}) custom-call(bf16[2,256,128]{2,1,0:T(8,128)(2,1)S(1)} %collective-permute-done.8.refs_0_, bf16[2,256,128]{2,1,0:T(8,128)(2,1)S(1)} %collective-permute-done.4.refs_0_.refs_1_, ...), custom_call_target="tpu_custom_call" | custom-call | flops 1207959552 | bytes 3932160 | tf_op jit(solution)/shard_map/backward/pallas_call | solution.py:411
  53.9 1.2 %collective-permute-start.13 = (bf16[2,256,128]{2,1,0:T(8,128)(2,1)S(1)}, bf16[2,256,128]{2,1,0:T(8,128)(2,1)S(1)}, u32[]{:S(2)}, u32[]{:S(2)}) collective-permute-start(bf16[2,256,128]{2,1,0:T(8,128)(2,1)S(1)} %get-tuple-element.56), channel_id=1, source_target_pairs={{13,0},{12,1},{15,2},{14,3},{9,4},{8,5},{11,6},{10,7},{21,8},{20,9... | collective-permute-start | bytes 393224 | tf_op jit(solution)/shard_map/ppermute | solution.py:449
  55.1 0.0 collective-permute-done.9
  55.1 3.1 %collective-permute-start.14 = (bf16[2,256,128]{2,1,0:T(8,128)(2,1)S(1)}, bf16[2,256,128]{2,1,0:T(8,128)(2,1)S(1)}, u32[]{:S(2)}, u32[]{:S(2)}) collective-permute-start(bf16[2,256,128]{2,1,0:T(8,128)(2,1)S(1)} %get-tuple-element.57), channel_id=1, source_target_pairs={{11,0},{10,1},{9,2},{8,3},{15,4},{14,5},{13,6},{12,7},{19,8},{18,9... | collective-permute-start | bytes 393224 | tf_op jit(solution)/shard_map/ppermute | solution.py:449
  58.2 0.0 collective-permute-done.10
  58.2 1.7 %collective-permute-start.15 = (bf16[2,256,128]{2,1,0:T(8,128)(2,1)S(1)}, bf16[2,256,128]{2,1,0:T(8,128)(2,1)S(1)}, u32[]{:S(2)}, u32[]{:S(2)}) collective-permute-start(bf16[2,256,128]{2,1,0:T(8,128)(2,1)S(1)} %get-tuple-element.58), channel_id=1, source_target_pairs={{9,0},{8,1},{11,2},{10,3},{13,4},{12,5},{15,6},{14,7},{17,8},{16,9... | collective-permute-start | bytes 393224 | tf_op jit(solution)/shard_map/ppermute | solution.py:449
  59.9 0.0 collective-permute-done.11
  59.9 0.0 collective-permute-done.12
  59.9 5.4 %collective-permute-done.13 = bf16[2,256,128]{2,1,0:T(8,128)(2,1)S(1)} collective-permute-done((bf16[2,256,128]{2,1,0:T(8,128)(2,1)S(1)}, bf16[2,256,128]{2,1,0:T(8,128)(2,1)S(1)}, u32[]{:S(2)}, u32[]{:S(2)}) %collective-permute-start.13) | collective-permute-done | bytes 131104 | tf_op jit(solution)/shard_map/ppermute | solution.py:449
  65.3 0.0 collective-permute-done.14
  65.3 2.4 %collective-permute-done.15 = bf16[2,256,128]{2,1,0:T(8,128)(2,1)S(1)} collective-permute-done((bf16[2,256,128]{2,1,0:T(8,128)(2,1)S(1)}, bf16[2,256,128]{2,1,0:T(8,128)(2,1)S(1)}, u32[]{:S(2)}, u32[]{:S(2)}) %collective-permute-start.15) | collective-permute-done | bytes 131104 | tf_op jit(solution)/shard_map/ppermute | solution.py:449
  67.7 1.5 %unpack.1 = bf16[1,128,2,2048]{3,2,1,0:T(2,128)(2,1)} custom-call(bf16[2,128,2,128]{3,2,1,0:T(2,128)(2,1)S(1)} %bitcast.16, bf16[2,128,2,128]{3,2,1,0:T(2,128)(2,1)S(1)} %bitcast.17, bf16[2,128,2,128]{3,2,1,0:T(2,128)(2,1)S(1)} %bitcast.18, bf16[2,128,2,128]{3,2,1,0:T(2,128)(2,1)S(1)} %bitcast.19, bf16[2,128,2,128]{3,2,1,0:T(2,128)(2,1)S(1)} %bitcast.20, ...), custom_call_target="tpu_custom_call" | custom-call | tf_op jit(solution)/shard_map/unpack/pallas_call | solution.py:114
Async XLA Ops:
  0.6 1.2 %copy-start = (bf16[1,128,2,2048]{3,2,1,0:T(2,128)(2,1)S(1)}, bf16[1,128,2,2048]{3,2,1,0:T(2,128)(2,1)}, u32[]{:S(2)}) copy-start(bf16[1,128,2,2048]{3,2,1,0:T(2,128)(2,1)} %pairs_ref.1) | copy-start | bytes 3145732
  1.9 15.4 %copy-start.1 = (bf16[1,1536,256]{2,1,0:T(8,128)(2,1)S(1)}, bf16[1,1536,256]{2,1,0:T(8,128)(2,1)}, u32[]{:S(2)}) copy-start(bf16[1,1536,256]{2,1,0:T(8,128)(2,1)} %rows_ref.2) | copy-start | bytes 2359300
  1.9 15.7 %copy-start.2 = (bf16[1,1536,256]{2,1,0:T(8,128)(2,1)S(1)}, bf16[1,1536,256]{2,1,0:T(8,128)(2,1)}, u32[]{:S(2)}) copy-start(bf16[1,1536,256]{2,1,0:T(8,128)(2,1)} %rows_ref.3) | copy-start | bytes 2359300
  2.8 11.9 %collective-permute-start.4 = (bf16[2,256,128]{2,1,0:T(8,128)(2,1)S(1)}, bf16[2,256,128]{2,1,0:T(8,128)(2,1)S(1)}, u32[]{:S(2)}, u32[]{:S(2)}) collective-permute-start(bf16[2,256,128]{2,1,0:T(8,128)(2,1)S(1)} %bitcast.31), channel_id=1, source_target_pairs={{0,13},{1,12},{2,15},{3,14},{4,9},{5,8},{6,11},{7,10},{8,21},{9,20... | collective-permute-start | bytes 393224 | tf_op jit(solution)/shard_map/ppermute | solution.py:441
  7.2 8.9 %collective-permute-start.5 = (bf16[2,256,128]{2,1,0:T(8,128)(2,1)S(1)}, bf16[2,256,128]{2,1,0:T(8,128)(2,1)S(1)}, u32[]{:S(2)}, u32[]{:S(2)}) collective-permute-start(bf16[2,256,128]{2,1,0:T(8,128)(2,1)S(1)} %bitcast.30), channel_id=1, source_target_pairs={{0,11},{1,10},{2,9},{3,8},{4,15},{5,14},{6,13},{7,12},{8,19},{9,18... | collective-permute-start | bytes 393224 | tf_op jit(solution)/shard_map/ppermute | solution.py:441
  10.0 7.8 %collective-permute-start.6 = (bf16[2,256,128]{2,1,0:T(8,128)(2,1)S(1)}, bf16[2,256,128]{2,1,0:T(8,128)(2,1)S(1)}, u32[]{:S(2)}, u32[]{:S(2)}) collective-permute-start(bf16[2,256,128]{2,1,0:T(8,128)(2,1)S(1)} %bitcast.29), channel_id=1, source_target_pairs={{0,9},{1,8},{2,11},{3,10},{4,13},{5,12},{6,15},{7,14},{8,17},{9,16... | collective-permute-start | bytes 393224 | tf_op jit(solution)/shard_map/ppermute | solution.py:441
  10.9 12.8 %collective-permute-start.1 = (bf16[2,256,128]{2,1,0:T(8,128)(2,1)S(1)}, bf16[2,256,128]{2,1,0:T(8,128)(2,1)S(1)}, u32[]{:S(2)}, u32[]{:S(2)}) collective-permute-start(bf16[2,256,128]{2,1,0:T(8,128)(2,1)S(1)} %bitcast.28), channel_id=1, source_target_pairs={{0,10},{1,11},{2,8},{3,9},{4,14},{5,15},{6,12},{7,13},{8,18},{9,19... | collective-permute-start | bytes 393224 | tf_op jit(solution)/shard_map/ppermute | solution.py:441
  11.6 12.1 %collective-permute-start = (bf16[2,256,128]{2,1,0:T(8,128)(2,1)S(1)}, bf16[2,256,128]{2,1,0:T(8,128)(2,1)S(1)}, u32[]{:S(2)}, u32[]{:S(2)}) collective-permute-start(bf16[2,256,128]{2,1,0:T(8,128)(2,1)S(1)} %bitcast.27), channel_id=1, source_target_pairs={{0,15},{1,14},{2,13},{3,12},{4,11},{5,10},{6,9},{7,8},{8,23},{9,22... | collective-permute-start | bytes 393224 | tf_op jit(solution)/shard_map/ppermute | solution.py:441
  14.7 9.1 %collective-permute-start.2 = (bf16[2,256,128]{2,1,0:T(8,128)(2,1)S(1)}, bf16[2,256,128]{2,1,0:T(8,128)(2,1)S(1)}, u32[]{:S(2)}, u32[]{:S(2)}) collective-permute-start(bf16[2,256,128]{2,1,0:T(8,128)(2,1)S(1)} %bitcast.26), channel_id=1, source_target_pairs={{0,8},{1,9},{2,10},{3,11},{4,12},{5,13},{6,14},{7,15},{8,16},{9,17... | collective-permute-start | bytes 393224 | tf_op jit(solution)/shard_map/ppermute | solution.py:441
  16.2 14.6 %collective-permute-start.3 = (bf16[2,256,128]{2,1,0:T(8,128)(2,1)S(1)}, bf16[2,256,128]{2,1,0:T(8,128)(2,1)S(1)}, u32[]{:S(2)}, u32[]{:S(2)}) collective-permute-start(bf16[2,256,128]{2,1,0:T(8,128)(2,1)S(1)} %bitcast.25), channel_id=1, source_target_pairs={{0,12},{1,13},{2,14},{3,15},{4,8},{5,9},{6,10},{7,11},{8,20},{9,21... | collective-permute-start | bytes 393224 | tf_op jit(solution)/shard_map/ppermute | solution.py:441
  17.8 16.8 %collective-permute-start.7 = (bf16[2,256,128]{2,1,0:T(8,128)(2,1)S(1)}, bf16[2,256,128]{2,1,0:T(8,128)(2,1)S(1)}, u32[]{:S(2)}, u32[]{:S(2)}) collective-permute-start(bf16[2,256,128]{2,1,0:T(8,128)(2,1)S(1)} %bitcast.24), channel_id=1, source_target_pairs={{0,14},{1,15},{2,12},{3,13},{4,10},{5,11},{6,8},{7,9},{8,22},{9,23... | collective-permute-start | bytes 393224 | tf_op jit(solution)/shard_map/ppermute | solution.py:441
  37.2 12.7 %collective-permute-start.8 = (bf16[2,256,128]{2,1,0:T(8,128)(2,1)S(1)}, bf16[2,256,128]{2,1,0:T(8,128)(2,1)S(1)}, u32[]{:S(2)}, u32[]{:S(2)}) collective-permute-start(bf16[2,256,128]{2,1,0:T(8,128)(2,1)S(1)} %get-tuple-element.48), channel_id=1, source_target_pairs={{14,0},{15,1},{12,2},{13,3},{10,4},{11,5},{8,6},{9,7},{22,8},{23,9... | collective-permute-start | bytes 393224 | tf_op jit(solution)/shard_map/ppermute | solution.py:449
  44.8 10.3 %collective-permute-start.9 = (bf16[2,256,128]{2,1,0:T(8,128)(2,1)S(1)}, bf16[2,256,128]{2,1,0:T(8,128)(2,1)S(1)}, u32[]{:S(2)}, u32[]{:S(2)}) collective-permute-start(bf16[2,256,128]{2,1,0:T(8,128)(2,1)S(1)} %get-tuple-element.52), channel_id=1, source_target_pairs={{15,0},{14,1},{13,2},{12,3},{11,4},{10,5},{9,6},{8,7},{23,8},{22,9... | collective-permute-start | bytes 393224 | tf_op jit(solution)/shard_map/ppermute | solution.py:449
  48.0 10.2 %collective-permute-start.10 = (bf16[2,256,128]{2,1,0:T(8,128)(2,1)S(1)}, bf16[2,256,128]{2,1,0:T(8,128)(2,1)S(1)}, u32[]{:S(2)}, u32[]{:S(2)}) collective-permute-start(bf16[2,256,128]{2,1,0:T(8,128)(2,1)S(1)} %get-tuple-element.53), channel_id=1, source_target_pairs={{10,0},{11,1},{8,2},{9,3},{14,4},{15,5},{12,6},{13,7},{18,8},{19,9... | collective-permute-start | bytes 393224 | tf_op jit(solution)/shard_map/ppermute | solution.py:449
  48.0 11.8 %collective-permute-start.11 = (bf16[2,256,128]{2,1,0:T(8,128)(2,1)S(1)}, bf16[2,256,128]{2,1,0:T(8,128)(2,1)S(1)}, u32[]{:S(2)}, u32[]{:S(2)}) collective-permute-start(bf16[2,256,128]{2,1,0:T(8,128)(2,1)S(1)} %get-tuple-element.54), channel_id=1, source_target_pairs={{8,0},{9,1},{10,2},{11,3},{12,4},{13,5},{14,6},{15,7},{16,8},{17,9... | collective-permute-start | bytes 393224 | tf_op jit(solution)/shard_map/ppermute | solution.py:449
  48.1 11.8 %collective-permute-start.12 = (bf16[2,256,128]{2,1,0:T(8,128)(2,1)S(1)}, bf16[2,256,128]{2,1,0:T(8,128)(2,1)S(1)}, u32[]{:S(2)}, u32[]{:S(2)}) collective-permute-start(bf16[2,256,128]{2,1,0:T(8,128)(2,1)S(1)} %get-tuple-element.55), channel_id=1, source_target_pairs={{12,0},{13,1},{14,2},{15,3},{8,4},{9,5},{10,6},{11,7},{20,8},{21,9... | collective-permute-start | bytes 393224 | tf_op jit(solution)/shard_map/ppermute | solution.py:449
  53.9 11.4 %collective-permute-start.13 = (bf16[2,256,128]{2,1,0:T(8,128)(2,1)S(1)}, bf16[2,256,128]{2,1,0:T(8,128)(2,1)S(1)}, u32[]{:S(2)}, u32[]{:S(2)}) collective-permute-start(bf16[2,256,128]{2,1,0:T(8,128)(2,1)S(1)} %get-tuple-element.56), channel_id=1, source_target_pairs={{13,0},{12,1},{15,2},{14,3},{9,4},{8,5},{11,6},{10,7},{21,8},{20,9... | collective-permute-start | bytes 393224 | tf_op jit(solution)/shard_map/ppermute | solution.py:449
  55.1 10.2 %collective-permute-start.14 = (bf16[2,256,128]{2,1,0:T(8,128)(2,1)S(1)}, bf16[2,256,128]{2,1,0:T(8,128)(2,1)S(1)}, u32[]{:S(2)}, u32[]{:S(2)}) collective-permute-start(bf16[2,256,128]{2,1,0:T(8,128)(2,1)S(1)} %get-tuple-element.57), channel_id=1, source_target_pairs={{11,0},{10,1},{9,2},{8,3},{15,4},{14,5},{13,6},{12,7},{19,8},{18,9... | collective-permute-start | bytes 393224 | tf_op jit(solution)/shard_map/ppermute | solution.py:449
  58.2 9.5 %collective-permute-start.15 = (bf16[2,256,128]{2,1,0:T(8,128)(2,1)S(1)}, bf16[2,256,128]{2,1,0:T(8,128)(2,1)S(1)}, u32[]{:S(2)}, u32[]{:S(2)}) collective-permute-start(bf16[2,256,128]{2,1,0:T(8,128)(2,1)S(1)} %get-tuple-element.58), channel_id=1, source_target_pairs={{9,0},{8,1},{11,2},{10,3},{13,4},{12,5},{15,6},{14,7},{17,8},{16,9... | collective-permute-start | bytes 393224 | tf_op jit(solution)/shard_map/ppermute | solution.py:449

commit v11 on v10

--- a/solution.py
+++ b/solution.py
@@ -19,26 +19,25 @@
 
 
 def partner(index, distance, count):
-    if count & (count - 1):
-        return (index + distance) % count
-    return index ^ distance
+    turned_round = (index & 1) * (count // 2) if count % 4 == 0 and distance % (count // 2) == 0 else 0
+    total = index + distance + turned_round
+    return total % count if isinstance(total, int) else lax.rem(total, count)
 
 
 def offset_groups():
     seq_count = lax.axis_size("seq")
     tp_count = lax.axis_size("tp")
-    middle = seq_count // 2
-    far = [(dz, dy) for dy in reversed(range(tp_count)) for dz in range(middle, seq_count)]
-    near = [(dz, dy) for dy in reversed(range(tp_count)) for dz in reversed(range(middle))]
-    f, n = max(1, len(far) // 4), len(near) // 2
-    return [far[:f] + near[:n], far[f : 2 * f] + near[n:] + far[2 * f : -f], far[-f:]]
+    order = [(dz, dy) for dz in range(seq_count) for dy in reversed(range(tp_count))]
+    count = len(order)
+    cuts = [0, count * 3 // 8, count * 3 // 4, count]
+    return [order[a:b] for a, b in zip(cuts[:-1], cuts[1:])]
 
 
 def group_at(offset):
     seq_count = lax.axis_size("seq")
     tp_count = lax.axis_size("tp")
     z = partner(lax.axis_index("seq"), offset[0], seq_count)
-    y = partner(lax.axis_index("tp"), offset[1], tp_count)
+    y = lax.rem(lax.axis_index("tp") + offset[1], tp_count)
     return z * tp_count + y
 
 
@@ -51,7 +50,7 @@
                 source = (s * seq_count + z) * tp_count + y
                 s_to = (s + 1) % segments
                 z_to = partner(z, offset[0], seq_count)
-                y_to = partner(y, offset[1], tp_count)
+                y_to = (y + offset[1]) % tp_count
                 target = (s_to * seq_count + z_to) * tp_count + y_to
                 hops.append((target, source) if back else (source, target))
     return hops

time: 69.5 us -> 70.7 us (1.017)
  the two profiles are of different devices: /device:TPU:0 before, /device:TPU:21 now
where the time goes in v11:
time: 70.7 us; the launch traced here: 70.5 us
  starting transfers between devices  31.5 us (45%)
  Pallas kernels  20.1 us (28%)
  waiting for transfers between devices  16.8 us (24%)
  local copies, waits for them, and re-layouts  1.23 us (2%)
  between operations  0.92 us (1%)
    ppermute x8, starting transfers between devices, send_back(): lax.ppermute(g, AXES, route(o, True))  18 us
    ppermute x8, starting transfers between devices, shards(): blocks.append(lax.ppermute(block, AXES, route(offset, False)))  13.5 us
    ppermute x8, waiting for transfers between devices, shards(): blocks.append(lax.ppermute(block, AXES, route(offset, False)))  9.22 us
    pallas_call x2, Pallas kernels, attend(): pl.pallas_call(functools.partial(backward_kernel, len(back), count, first...  7.94 us
    ppermute x8, waiting for transfers between devices, send_back(): lax.ppermute(g, AXES, route(o, True))  7.56 us
    pallas_call x2, Pallas kernels, attend(): pl.pallas_call(functools.partial(forward_kernel, count, not state, tile_o...  5.09 us
    pallas_call x1, Pallas kernels, attend(): pl.pallas_call(functools.partial(turn_kernel, count, tile_of(count * rows...  4.01 us
    pallas_call x1, Pallas kernels, unpack(): pl.pallas_call(kernel, out_shape=jax.ShapeDtypeStruct((1, rows, 2, width)...  1.51 us
  transfers between devices with their start and end apart: 16, of which 5 were waited for; matrix products, arithmetic and copies ran while one was open for 0% of the time, Pallas kernels for 19%

profile of v11, /device:TPU:21, one launch (start us, length us, event | category | flops | bytes accessed | tf_op | source)
XLA Modules:
  0.0 70.5 jit_solution(16707230519313416286)
XLA Ops:
  0.6 0.0 copy-start
  0.6 1.2 %copy-done = bf16[1,128,2,2048]{3,2,1,0:T(2,128)(2,1)S(1)} copy-done((bf16[1,128,2,2048]{3,2,1,0:T(2,128)(2,1)S(1)}, bf16[1,128,2,2048]{3,2,1,0:T(2,128)(2,1)}, u32[]{:S(2)}) %copy-start) | copy-done | bytes 1048600
  1.9 0.0 copy-start.1
  1.9 0.0 copy-start.2
  1.9 1.0 %pack.1 = (bf16[2,128,2,128]{3,2,1,0:T(2,128)(2,1)S(1)}, bf16[2,128,2,128]{3,2,1,0:T(2,128)(2,1)S(1)}, bf16[2,128,2,128]{3,2,1,0:T(2,128)(2,1)S(1)}, bf16[2,128,...) custom-call(bf16[1,128,2,2048]{3,2,1,0:T(2,128)(2,1)S(1)} %copy-done), custom_call_target="tpu_custom_call" | custom-call | tf_op jit(solution)/shard_map/pack/pallas_call | solution.py:77
  2.8 1.8 %collective-permute-start.3 = (bf16[2,256,128]{2,1,0:T(8,128)(2,1)S(1)}, bf16[2,256,128]{2,1,0:T(8,128)(2,1)S(1)}, u32[]{:S(2)}, u32[]{:S(2)}) collective-permute-start(bf16[2,256,128]{2,1,0:T(8,128)(2,1)S(1)} %bitcast.31), channel_id=1, source_target_pairs={{0,9},{1,8},{2,15},{3,14},{4,13},{5,12},{6,11},{7,10},{8,17},{9,16... | collective-permute-start | bytes 393224 | tf_op jit(solution)/shard_map/ppermute | solution.py:440
  4.6 0.1 collective-permute-start.4
  4.7 4.5 %collective-permute-start.5 = (bf16[2,256,128]{2,1,0:T(8,128)(2,1)S(1)}, bf16[2,256,128]{2,1,0:T(8,128)(2,1)S(1)}, u32[]{:S(2)}, u32[]{:S(2)}) collective-permute-start(bf16[2,256,128]{2,1,0:T(8,128)(2,1)S(1)} %bitcast.29), channel_id=1, source_target_pairs={{0,11},{1,10},{2,13},{3,12},{4,15},{5,14},{6,9},{7,8},{8,19},{9,18... | collective-permute-start | bytes 393224 | tf_op jit(solution)/shard_map/ppermute | solution.py:440
  9.2 0.1 collective-permute-start.1
  9.3 0.0 collective-permute-start
  9.3 0.0 collective-permute-done.3.refs_0_.refs_2_
  9.3 3.5 %collective-permute-start.2 = (bf16[2,256,128]{2,1,0:T(8,128)(2,1)S(1)}, bf16[2,256,128]{2,1,0:T(8,128)(2,1)S(1)}, u32[]{:S(2)}, u32[]{:S(2)}) collective-permute-start(bf16[2,256,128]{2,1,0:T(8,128)(2,1)S(1)} %bitcast.26), channel_id=1, source_target_pairs={{0,12},{1,13},{2,10},{3,11},{4,8},{5,9},{6,14},{7,15},{8,20},{9,21... | collective-permute-start | bytes 393224 | tf_op jit(solution)/shard_map/ppermute | solution.py:440
  12.7 0.0 collective-permute-done.4.refs_1_.refs_3_
  12.7 3.5 %collective-permute-start.6 = (bf16[2,256,128]{2,1,0:T(8,128)(2,1)S(1)}, bf16[2,256,128]{2,1,0:T(8,128)(2,1)S(1)}, u32[]{:S(2)}, u32[]{:S(2)}) collective-permute-start(bf16[2,256,128]{2,1,0:T(8,128)(2,1)S(1)} %bitcast.25), channel_id=1, source_target_pairs={{0,15},{1,14},{2,9},{3,8},{4,11},{5,10},{6,13},{7,12},{8,23},{9,22... | collective-permute-start | bytes 393224 | tf_op jit(solution)/shard_map/ppermute | solution.py:440
  16.3 2.8 %collective-permute-done.5.refs_2_.refs_4_ = bf16[2,256,128]{2,1,0:T(8,128)(2,1)S(1)} collective-permute-done((bf16[2,256,128]{2,1,0:T(8,128)(2,1)S(1)}, bf16[2,256,128]{2,1,0:T(8,128)(2,1)S(1)}, u32[]{:S(2)}, u32[]{:S(2)}) %collective-permute-start.5) | collective-permute-done | bytes 131104 | tf_op jit(solution)/shard_map/ppermute | solution.py:440
  19.0 0.1 collective-permute-start.7
  19.1 0.0 copy-done.1
  19.1 0.3 turned.2.refs_3_.refs_2_.refs_5_.refs_7_
  19.4 0.0 copy-done.2
  19.4 0.3 turned.3.refs_3_.refs_6_.refs_8_
  19.7 2.6 %forward.2 = (f32[2,8,1536]{2,1,0:T(8,128)S(1)}, f32[2,128,1536]{2,1,0:T(8,128)S(1)}, bf16[2,384,1536]{2,1,0:T(8,128)(2,1)S(1)}) custom-call(bf16[2,256,128]{2,1,0:T(8,128)(2,1)S(1)} %collective-permute-done.3.refs_0_.refs_2_, bf16[2,256,128]{2,1,0:T(8,128)(2,1)S(1)} %collective-permute-done.4.refs_1_.refs_3_, ...), custom_call_target="tpu_custom_call" | custom-call | flops 603979776 | bytes 3932160 | tf_op jit(solution)/shard_map/forward/pallas_call | solution.py:377
  22.3 0.0 collective-permute-done.1.refs_1_
  22.3 6.4 %collective-permute-done.refs_0_ = bf16[2,256,128]{2,1,0:T(8,128)(2,1)S(1)} collective-permute-done((bf16[2,256,128]{2,1,0:T(8,128)(2,1)S(1)}, bf16[2,256,128]{2,1,0:T(8,128)(2,1)S(1)}, u32[]{:S(2)}, u32[]{:S(2)}) %collective-permute-start) | collective-permute-done | bytes 131104 | tf_op jit(solution)/shard_map/ppermute | solution.py:440
  28.7 0.0 collective-permute-done.2.refs_2_
  28.7 2.5 %forward.3 = (f32[2,8,1536]{2,1,0:T(8,128)S(1)}, f32[2,128,1536]{2,1,0:T(8,128)S(1)}, bf16[2,384,1536]{2,1,0:T(8,128)(2,1)S(1)}) custom-call(bf16[2,256,128]{2,1,0:T(8,128)(2,1)S(1)} %collective-permute-done.refs_0_, bf16[2,256,128]{2,1,0:T(8,128)(2,1)S(1)} %collective-permute-done.1.refs_1_, bf16[2,256,128]{2,1,0:T(8,128)(2,1)S(1)} %collective-permute-done.2.refs_2_, ...), custom_call_target="tpu_custom_call" | custom-call | flops 603979776 | bytes 3932160 | tf_op jit(solution)/shard_map/forward/pallas_call | solution.py:377
  31.3 0.0 collective-permute-done.6.refs_0_
  31.3 0.0 collective-permute-done.7.refs_1_
  31.3 4.0 %turn.1 = (f32[2,8,1536]{2,1,0:T(8,128)S(1)}, f32[2,128,1536]{2,1,0:T(8,128)S(1)}, f32[2,128,1536]{2,1,0:T(8,128)S(1)}, bf16[2,256,128]{2,1,0:T(8,128)(2,1)S(1)}, bf16[2,256,128]{2,1,0:T(8,128)(2,1)S(1)}) custom-call(bf16[2,256,128]{2,1,0:T(8,128)(2,1)S(1)} %collective-permute-done.6.refs_0_, bf16[2,256,128]{2,1,0:T(8,128)(2,1)S(1)} %collective-permute-done.7.refs_1_, ...), custom_call_target="tpu_custom_call" | custom-call | flops 1207959552 | bytes 3670016 | tf_op jit(solution)/shard_map/turn/pallas_call | solution.py:391
  35.3 0.1 collective-permute-start.8
  35.4 2.6 %collective-permute-start.9 = (bf16[2,256,128]{2,1,0:T(8,128)(2,1)S(1)}, bf16[2,256,128]{2,1,0:T(8,128)(2,1)S(1)}, u32[]{:S(2)}, u32[]{:S(2)}) collective-permute-start(bf16[2,256,128]{2,1,0:T(8,128)(2,1)S(1)} %get-tuple-element.49), channel_id=1, source_target_pairs={{14,0},{15,1},{8,2},{9,3},{10,4},{11,5},{12,6},{13,7},{22,8},{23,9... | collective-permute-start | bytes 393224 | tf_op jit(solution)/shard_map/ppermute | solution.py:448
  37.9 4.0 %backward.2 = (bf16[1,1536,256]{2,1,0:T(8,128)(2,1)}, f32[2,128,1536]{2,1,0:T(8,128)S(1)}, bf16[2,256,128]{2,1,0:T(8,128)(2,1)S(1)}, bf16[2,256,128]{2,1,0:T(8,128)(2,1)S(1)}, bf16[2,256,128]{2,1,0:T(8,128)(2,1)S(1)}) custom-call(bf16[2,256,128]{2,1,0:T(8,128)(2,1)S(1)} %collective-permute-done.refs_0_, ...), custom_call_target="tpu_custom_call" | custom-call | flops 1207959552 | bytes 3932160 | tf_op jit(solution)/shard_map/backward/pallas_call | solution.py:410
  41.9 2.6 %collective-permute-start.10 = (bf16[2,256,128]{2,1,0:T(8,128)(2,1)S(1)}, bf16[2,256,128]{2,1,0:T(8,128)(2,1)S(1)}, u32[]{:S(2)}, u32[]{:S(2)}) collective-permute-start(bf16[2,256,128]{2,1,0:T(8,128)(2,1)S(1)} %get-tuple-element.53), channel_id=1, source_target_pairs={{10,0},{11,1},{12,2},{13,3},{14,4},{15,5},{8,6},{9,7},{18,8},{19,9... | collective-permute-start | bytes 393224 | tf_op jit(solution)/shard_map/ppermute | solution.py:448
  44.5 3.4 %collective-permute-start.11 = (bf16[2,256,128]{2,1,0:T(8,128)(2,1)S(1)}, bf16[2,256,128]{2,1,0:T(8,128)(2,1)S(1)}, u32[]{:S(2)}, u32[]{:S(2)}) collective-permute-start(bf16[2,256,128]{2,1,0:T(8,128)(2,1)S(1)} %get-tuple-element.54), channel_id=1, source_target_pairs={{13,0},{12,1},{11,2},{10,3},{9,4},{8,5},{15,6},{14,7},{21,8},{20,9... | collective-permute-start | bytes 393224 | tf_op jit(solution)/shard_map/ppermute | solution.py:448
  47.9 0.0 collective-permute-start.12
  47.9 0.0 collective-permute-done.8.refs_0_
  47.9 0.0 collective-permute-done.9.refs_1_
  47.9 4.0 %backward.3 = (bf16[1,1536,256]{2,1,0:T(8,128)(2,1)}, bf16[2,256,128]{2,1,0:T(8,128)(2,1)S(1)}, bf16[2,256,128]{2,1,0:T(8,128)(2,1)S(1)}, bf16[2,256,128]{2,1,0:T(8,128)(2,1)S(1)}) custom-call(bf16[2,256,128]{2,1,0:T(8,128)(2,1)S(1)} %collective-permute-done.8.refs_0_, bf16[2,256,128]{2,1,0:T(8,128)(2,1)S(1)} %collective-permute-done.9.refs_1_, ...), custom_call_target="tpu_custom_call" | custom-call | flops 1207959552 | bytes 3932160 | tf_op jit(solution)/shard_map/backward/pallas_call | solution.py:410
  51.9 9.4 %collective-permute-start.13 = (bf16[2,256,128]{2,1,0:T(8,128)(2,1)S(1)}, bf16[2,256,128]{2,1,0:T(8,128)(2,1)S(1)}, u32[]{:S(2)}, u32[]{:S(2)}) collective-permute-start(bf16[2,256,128]{2,1,0:T(8,128)(2,1)S(1)} %get-tuple-element.56), channel_id=1, source_target_pairs={{9,0},{8,1},{15,2},{14,3},{13,4},{12,5},{11,6},{10,7},{17,8},{16,9... | collective-permute-start | bytes 393224 | tf_op jit(solution)/shard_map/ppermute | solution.py:448
  61.3 0.0 collective-permute-start.14
  61.3 0.0 collective-permute-done.10
  61.3 0.0 collective-permute-start.15
  61.3 0.0 collective-permute-done.11
  61.3 0.0 collective-permute-done.12
  61.3 3.3 %collective-permute-done.13 = bf16[2,256,128]{2,1,0:T(8,128)(2,1)S(1)} collective-permute-done((bf16[2,256,128]{2,1,0:T(8,128)(2,1)S(1)}, bf16[2,256,128]{2,1,0:T(8,128)(2,1)S(1)}, u32[]{:S(2)}, u32[]{:S(2)}) %collective-permute-start.13) | collective-permute-done | bytes 131104 | tf_op jit(solution)/shard_map/ppermute | solution.py:448
  64.6 2.5 %collective-permute-done.14 = bf16[2,256,128]{2,1,0:T(8,128)(2,1)S(1)} collective-permute-done((bf16[2,256,128]{2,1,0:T(8,128)(2,1)S(1)}, bf16[2,256,128]{2,1,0:T(8,128)(2,1)S(1)}, u32[]{:S(2)}, u32[]{:S(2)}) %collective-permute-start.14) | collective-permute-done | bytes 131104 | tf_op jit(solution)/shard_map/ppermute | solution.py:448
  67.1 1.8 %collective-permute-done.15 = bf16[2,256,128]{2,1,0:T(8,128)(2,1)S(1)} collective-permute-done((bf16[2,256,128]{2,1,0:T(8,128)(2,1)S(1)}, bf16[2,256,128]{2,1,0:T(8,128)(2,1)S(1)}, u32[]{:S(2)}, u32[]{:S(2)}) %collective-permute-start.15) | collective-permute-done | bytes 131104 | tf_op jit(solution)/shard_map/ppermute | solution.py:448
  68.8 1.5 %unpack.1 = bf16[1,128,2,2048]{3,2,1,0:T(2,128)(2,1)} custom-call(bf16[2,128,2,128]{3,2,1,0:T(2,128)(2,1)S(1)} %bitcast.16, bf16[2,128,2,128]{3,2,1,0:T(2,128)(2,1)S(1)} %bitcast.17, bf16[2,128,2,128]{3,2,1,0:T(2,128)(2,1)S(1)} %bitcast.18, bf16[2,128,2,128]{3,2,1,0:T(2,128)(2,1)S(1)} %bitcast.19, bf16[2,128,2,128]{3,2,1,0:T(2,128)(2,1)S(1)} %bitcast.20, ...), custom_call_target="tpu_custom_call" | custom-call | tf_op jit(solution)/shard_map/unpack/pallas_call | solution.py:113
Async XLA Ops:
  0.6 1.2 %copy-start = (bf16[1,128,2,2048]{3,2,1,0:T(2,128)(2,1)S(1)}, bf16[1,128,2,2048]{3,2,1,0:T(2,128)(2,1)}, u32[]{:S(2)}) copy-start(bf16[1,128,2,2048]{3,2,1,0:T(2,128)(2,1)} %pairs_ref.1) | copy-start | bytes 3145732
  1.9 17.3 %copy-start.1 = (bf16[1,1536,256]{2,1,0:T(8,128)(2,1)S(1)}, bf16[1,1536,256]{2,1,0:T(8,128)(2,1)}, u32[]{:S(2)}) copy-start(bf16[1,1536,256]{2,1,0:T(8,128)(2,1)} %rows_ref.2) | copy-start | bytes 2359300
  1.9 17.6 %copy-start.2 = (bf16[1,1536,256]{2,1,0:T(8,128)(2,1)S(1)}, bf16[1,1536,256]{2,1,0:T(8,128)(2,1)}, u32[]{:S(2)}) copy-start(bf16[1,1536,256]{2,1,0:T(8,128)(2,1)} %rows_ref.3) | copy-start | bytes 2359300
  2.8 6.4 %collective-permute-start.3 = (bf16[2,256,128]{2,1,0:T(8,128)(2,1)S(1)}, bf16[2,256,128]{2,1,0:T(8,128)(2,1)S(1)}, u32[]{:S(2)}, u32[]{:S(2)}) collective-permute-start(bf16[2,256,128]{2,1,0:T(8,128)(2,1)S(1)} %bitcast.31), channel_id=1, source_target_pairs={{0,9},{1,8},{2,15},{3,14},{4,13},{5,12},{6,11},{7,10},{8,17},{9,16... | collective-permute-start | bytes 393224 | tf_op jit(solution)/shard_map/ppermute | solution.py:440
  4.6 8.1 %collective-permute-start.4 = (bf16[2,256,128]{2,1,0:T(8,128)(2,1)S(1)}, bf16[2,256,128]{2,1,0:T(8,128)(2,1)S(1)}, u32[]{:S(2)}, u32[]{:S(2)}) collective-permute-start(bf16[2,256,128]{2,1,0:T(8,128)(2,1)S(1)} %bitcast.30), channel_id=1, source_target_pairs={{0,8},{1,9},{2,14},{3,15},{4,12},{5,13},{6,10},{7,11},{8,16},{9,17... | collective-permute-start | bytes 393224 | tf_op jit(solution)/shard_map/ppermute | solution.py:440
  4.7 14.3 %collective-permute-start.5 = (bf16[2,256,128]{2,1,0:T(8,128)(2,1)S(1)}, bf16[2,256,128]{2,1,0:T(8,128)(2,1)S(1)}, u32[]{:S(2)}, u32[]{:S(2)}) collective-permute-start(bf16[2,256,128]{2,1,0:T(8,128)(2,1)S(1)} %bitcast.29), channel_id=1, source_target_pairs={{0,11},{1,10},{2,13},{3,12},{4,15},{5,14},{6,9},{7,8},{8,19},{9,18... | collective-permute-start | bytes 393224 | tf_op jit(solution)/shard_map/ppermute | solution.py:440
  9.2 13.1 %collective-permute-start.1 = (bf16[2,256,128]{2,1,0:T(8,128)(2,1)S(1)}, bf16[2,256,128]{2,1,0:T(8,128)(2,1)S(1)}, u32[]{:S(2)}, u32[]{:S(2)}) collective-permute-start(bf16[2,256,128]{2,1,0:T(8,128)(2,1)S(1)} %bitcast.28), channel_id=1, source_target_pairs={{0,13},{1,12},{2,11},{3,10},{4,9},{5,8},{6,15},{7,14},{8,21},{9,20... | collective-permute-start | bytes 393224 | tf_op jit(solution)/shard_map/ppermute | solution.py:440
  9.3 19.4 %collective-permute-start = (bf16[2,256,128]{2,1,0:T(8,128)(2,1)S(1)}, bf16[2,256,128]{2,1,0:T(8,128)(2,1)S(1)}, u32[]{:S(2)}, u32[]{:S(2)}) collective-permute-start(bf16[2,256,128]{2,1,0:T(8,128)(2,1)S(1)} %bitcast.27), channel_id=1, source_target_pairs={{0,10},{1,11},{2,12},{3,13},{4,14},{5,15},{6,8},{7,9},{8,18},{9,19... | collective-permute-start | bytes 393224 | tf_op jit(solution)/shard_map/ppermute | solution.py:440
  9.3 19.4 %collective-permute-start.2 = (bf16[2,256,128]{2,1,0:T(8,128)(2,1)S(1)}, bf16[2,256,128]{2,1,0:T(8,128)(2,1)S(1)}, u32[]{:S(2)}, u32[]{:S(2)}) collective-permute-start(bf16[2,256,128]{2,1,0:T(8,128)(2,1)S(1)} %bitcast.26), channel_id=1, source_target_pairs={{0,12},{1,13},{2,10},{3,11},{4,8},{5,9},{6,14},{7,15},{8,20},{9,21... | collective-permute-start | bytes 393224 | tf_op jit(solution)/shard_map/ppermute | solution.py:440
  12.7 18.5 %collective-permute-start.6 = (bf16[2,256,128]{2,1,0:T(8,128)(2,1)S(1)}, bf16[2,256,128]{2,1,0:T(8,128)(2,1)S(1)}, u32[]{:S(2)}, u32[]{:S(2)}) collective-permute-start(bf16[2,256,128]{2,1,0:T(8,128)(2,1)S(1)} %bitcast.25), channel_id=1, source_target_pairs={{0,15},{1,14},{2,9},{3,8},{4,11},{5,10},{6,13},{7,12},{8,23},{9,22... | collective-permute-start | bytes 393224 | tf_op jit(solution)/shard_map/ppermute | solution.py:440
  19.0 12.2 %collective-permute-start.7 = (bf16[2,256,128]{2,1,0:T(8,128)(2,1)S(1)}, bf16[2,256,128]{2,1,0:T(8,128)(2,1)S(1)}, u32[]{:S(2)}, u32[]{:S(2)}) collective-permute-start(bf16[2,256,128]{2,1,0:T(8,128)(2,1)S(1)} %bitcast.24), channel_id=1, source_target_pairs={{0,14},{1,15},{2,8},{3,9},{4,10},{5,11},{6,12},{7,13},{8,22},{9,23... | collective-permute-start | bytes 393224 | tf_op jit(solution)/shard_map/ppermute | solution.py:440
  35.3 12.6 %collective-permute-start.8 = (bf16[2,256,128]{2,1,0:T(8,128)(2,1)S(1)}, bf16[2,256,128]{2,1,0:T(8,128)(2,1)S(1)}, u32[]{:S(2)}, u32[]{:S(2)}) collective-permute-start(bf16[2,256,128]{2,1,0:T(8,128)(2,1)S(1)} %get-tuple-element.48), channel_id=1, source_target_pairs={{15,0},{14,1},{9,2},{8,3},{11,4},{10,5},{13,6},{12,7},{23,8},{22,9... | collective-permute-start | bytes 393224 | tf_op jit(solution)/shard_map/ppermute | solution.py:448
  35.4 12.5 %collective-permute-start.9 = (bf16[2,256,128]{2,1,0:T(8,128)(2,1)S(1)}, bf16[2,256,128]{2,1,0:T(8,128)(2,1)S(1)}, u32[]{:S(2)}, u32[]{:S(2)}) collective-permute-start(bf16[2,256,128]{2,1,0:T(8,128)(2,1)S(1)} %get-tuple-element.49), channel_id=1, source_target_pairs={{14,0},{15,1},{8,2},{9,3},{10,4},{11,5},{12,6},{13,7},{22,8},{23,9... | collective-permute-start | bytes 393224 | tf_op jit(solution)/shard_map/ppermute | solution.py:448
  41.9 19.3 %collective-permute-start.10 = (bf16[2,256,128]{2,1,0:T(8,128)(2,1)S(1)}, bf16[2,256,128]{2,1,0:T(8,128)(2,1)S(1)}, u32[]{:S(2)}, u32[]{:S(2)}) collective-permute-start(bf16[2,256,128]{2,1,0:T(8,128)(2,1)S(1)} %get-tuple-element.53), channel_id=1, source_target_pairs={{10,0},{11,1},{12,2},{13,3},{14,4},{15,5},{8,6},{9,7},{18,8},{19,9... | collective-permute-start | bytes 393224 | tf_op jit(solution)/shard_map/ppermute | solution.py:448
  44.5 16.8 %collective-permute-start.11 = (bf16[2,256,128]{2,1,0:T(8,128)(2,1)S(1)}, bf16[2,256,128]{2,1,0:T(8,128)(2,1)S(1)}, u32[]{:S(2)}, u32[]{:S(2)}) collective-permute-start(bf16[2,256,128]{2,1,0:T(8,128)(2,1)S(1)} %get-tuple-element.54), channel_id=1, source_target_pairs={{13,0},{12,1},{11,2},{10,3},{9,4},{8,5},{15,6},{14,7},{21,8},{20,9... | collective-permute-start | bytes 393224 | tf_op jit(solution)/shard_map/ppermute | solution.py:448
  47.9 13.4 %collective-permute-start.12 = (bf16[2,256,128]{2,1,0:T(8,128)(2,1)S(1)}, bf16[2,256,128]{2,1,0:T(8,128)(2,1)S(1)}, u32[]{:S(2)}, u32[]{:S(2)}) collective-permute-start(bf16[2,256,128]{2,1,0:T(8,128)(2,1)S(1)} %get-tuple-element.55), channel_id=1, source_target_pairs={{12,0},{13,1},{10,2},{11,3},{8,4},{9,5},{14,6},{15,7},{20,8},{21,9... | collective-permute-start | bytes 393224 | tf_op jit(solution)/shard_map/ppermute | solution.py:448
  51.9 12.7 %collective-permute-start.13 = (bf16[2,256,128]{2,1,0:T(8,128)(2,1)S(1)}, bf16[2,256,128]{2,1,0:T(8,128)(2,1)S(1)}, u32[]{:S(2)}, u32[]{:S(2)}) collective-permute-start(bf16[2,256,128]{2,1,0:T(8,128)(2,1)S(1)} %get-tuple-element.56), channel_id=1, source_target_pairs={{9,0},{8,1},{15,2},{14,3},{13,4},{12,5},{11,6},{10,7},{17,8},{16,9... | collective-permute-start | bytes 393224 | tf_op jit(solution)/shard_map/ppermute | solution.py:448
  61.3 5.8 %collective-permute-start.14 = (bf16[2,256,128]{2,1,0:T(8,128)(2,1)S(1)}, bf16[2,256,128]{2,1,0:T(8,128)(2,1)S(1)}, u32[]{:S(2)}, u32[]{:S(2)}) collective-permute-start(bf16[2,256,128]{2,1,0:T(8,128)(2,1)S(1)} %get-tuple-element.57), channel_id=1, source_target_pairs={{8,0},{9,1},{14,2},{15,3},{12,4},{13,5},{10,6},{11,7},{16,8},{17,9... | collective-permute-start | bytes 393224 | tf_op jit(solution)/shard_map/ppermute | solution.py:448
  61.3 7.6 %collective-permute-start.15 = (bf16[2,256,128]{2,1,0:T(8,128)(2,1)S(1)}, bf16[2,256,128]{2,1,0:T(8,128)(2,1)S(1)}, u32[]{:S(2)}, u32[]{:S(2)}) collective-permute-start(bf16[2,256,128]{2,1,0:T(8,128)(2,1)S(1)} %get-tuple-element.58), channel_id=1, source_target_pairs={{11,0},{10,1},{13,2},{12,3},{15,4},{14,5},{9,6},{8,7},{19,8},{18,9... | collective-permute-start | bytes 393224 | tf_op jit(solution)/shard_map/ppermute | solution.py:448

commit v12 on v11

--- a/solution.py
+++ b/solution.py
@@ -18,25 +18,28 @@
 VMEM = pl.BlockSpec(memory_space=pltpu.VMEM)
 
 
-def partner(index, distance, count):
-    turned_round = (index & 1) * (count // 2) if count % 4 == 0 and distance % (count // 2) == 0 else 0
-    total = index + distance + turned_round
-    return total % count if isinstance(total, int) else lax.rem(total, count)
-
-
 def offset_groups():
     seq_count = lax.axis_size("seq")
     tp_count = lax.axis_size("tp")
-    order = [(dz, dy) for dz in range(seq_count) for dy in reversed(range(tp_count))]
-    count = len(order)
-    cuts = [0, count * 3 // 8, count * 3 // 4, count]
-    return [order[a:b] for a, b in zip(cuts[:-1], cuts[1:])]
+    near = [(0, dy) for dy in reversed(range(tp_count))]
+    far = [(dz, dy) for dy in reversed(range(tp_count)) for dz in range(1, seq_count)]
+    far.sort(key=lambda o: -abs(o[0] - seq_count / 2))
+    eighth = max(1, (len(near) + len(far)) // 8)
+    short, long = far[: -2 * eighth], far[-2 * eighth :]
+    short.sort(key=lambda o: -o[1])
+    half = len(short) // 2
+    return [
+        short[:1] + near[:1] + short[1:half],
+        short[half:] + near[1:],
+        long[:eighth],
+        long[eighth:],
+    ]
 
 
 def group_at(offset):
     seq_count = lax.axis_size("seq")
     tp_count = lax.axis_size("tp")
-    z = partner(lax.axis_index("seq"), offset[0], seq_count)
+    z = lax.rem(lax.axis_index("seq") + offset[0], seq_count)
     y = lax.rem(lax.axis_index("tp") + offset[1], tp_count)
     return z * tp_count + y
 
@@ -49,7 +52,7 @@
             for y in range(tp_count):
                 source = (s * seq_count + z) * tp_count + y
                 s_to = (s + 1) % segments
-                z_to = partner(z, offset[0], seq_count)
+                z_to = (z + offset[0]) % seq_count
                 y_to = (y + offset[1]) % tp_count
                 target = (s_to * seq_count + z_to) * tp_count + y_to
                 hops.append((target, source) if back else (source, target))
@@ -294,25 +297,26 @@
         join_chunks(outs, h, rows, gk_ref, gv_ref)
 
 
-def backward_kernel(back, count, first, last, tile, *refs):
+def backward_kernel(back, counts, first, tile, *refs):
     refs = refs[back:]
-    chunks, refs = refs[:count], refs[count:]
-    low_ref, then_ref, qt_ref, gt_ref, stats_ref, grad_q_in = refs[:6]
-    refs = refs[6:]
+    groups = []
+    for count in counts:
+        groups.append((refs[:count], refs[count], refs[count + 1]))
+        refs = refs[count + 2 :]
+    qt_ref, gt_ref, stats_ref, grad_q_in = refs[:4]
     if first:
-        ready_ref, refs = refs[0], refs[1:]
-    if first or last:
-        rows_ref, refs = refs[0], refs[1:]
-    if not last:
-        grad_q_ref, refs = refs[0], refs[1:]
-    outs, refs = refs[:count], refs[count:]
-    v_ref, kt_ref, gk_ref, gv_ref = refs
-    heads, pair_rows, _ = chunks[0].shape
+        ready_ref, rows_ref, grad_q_ref, refs = refs[4], refs[5], refs[6], refs[7:]
+    else:
+        rows_ref, refs = refs[4], refs[5:]
+    outs, refs = refs[: sum(counts)], refs[sum(counts) :]
+    scratch = [refs[i : i + 4] for i in range(0, len(refs), 4)]
+    heads, pair_rows, _ = groups[0][0][0].shape
     rows = pair_rows // 2
-    for h in range(heads):
-        split_chunks(chunks, h, rows, v_ref=v_ref, kt_ref=kt_ref)
-    gk_ref[...] = jnp.zeros_like(gk_ref)
-    gv_ref[...] = jnp.zeros_like(gv_ref)
+    for (chunks, _, _), (v_ref, kt_ref, gk_ref, gv_ref) in zip(groups, scratch):
+        for h in range(heads):
+            split_chunks(chunks, h, rows, v_ref=v_ref, kt_ref=kt_ref)
+        gk_ref[...] = jnp.zeros_like(gk_ref)
+        gv_ref[...] = jnp.zeros_like(gv_ref)
 
     @tiles(qt_ref.shape[2] // tile)
     def _(j):
@@ -321,21 +325,23 @@
             columns = slice(h * HEAD, (h + 1) * HEAD)
             qt, gt = qt_ref[h, :, here], gt_ref[h, :, here]
             top, scale, row_dot = (stats_ref[h, i : i + 1, here] for i in range(3))
-            shrunk = jnp.exp2((then_ref[h, 0:1, here] - top) * EXPONENT)
-            low = low_ref[h, :, here]
-            raised = low.astype(jnp.float32)
-            grad_q = grad_q_in[h, :, here] + gradients(
-                raised, low, scale * shrunk, row_dot, qt, gt, refs, h
-            )
-            if last:
-                rows_ref[0, here, columns] = grad_q.T.astype(rows_ref.dtype)
-            else:
+            grad_q = grad_q_in[h, :, here]
+            for (_, low_ref, then_ref), own in zip(groups, scratch):
+                shrunk = jnp.exp2((then_ref[h, 0:1, here] - top) * EXPONENT)
+                low = low_ref[h, :, here]
+                raised = low.astype(jnp.float32)
+                grad_q = grad_q + gradients(
+                    raised, low, scale * shrunk, row_dot, qt, gt, own, h
+                )
+            if first:
                 grad_q_ref[h, :, here] = grad_q
-            if first:
-                rows_ref[0, here, columns] = ready_ref[h, :, here].T.astype(rows_ref.dtype)
-
-    for h in range(heads):
-        join_chunks(outs, h, rows, gk_ref, gv_ref)
+                grad_q = ready_ref[h, :, here]
+            rows_ref[0, here, columns] = grad_q.T.astype(rows_ref.dtype)
+
+    for count, (_, _, gk_ref, gv_ref) in zip(counts, scratch):
+        for h in range(heads):
+            join_chunks(outs[:count], h, rows, gk_ref, gv_ref)
+        outs = outs[count:]
 
 
 def cost(heads, rows, tokens, matmuls):
@@ -369,7 +375,6 @@
     def shapes_of(group):
         return [jax.ShapeDtypeStruct(c.shape, c.dtype) for c in group]
 
-    waits = {1: [], 0: [0]}
     state, kept = [], []
     for group in groups[:-1]:
         count = len(group)
@@ -401,31 +406,39 @@
     )(*group, qt, gt, *state)
     returned = [send_back(len(groups) - 1, grads)]
 
-    for i in reversed(range(len(groups) - 1)):
-        group, count = groups[i], len(groups[i])
-        first, last = i == len(groups) - 2, i == 0
-        back = sum((returned[k] for k in waits[i]), [])
-        operands = [*group, *kept[i], qt, gt, final, grad_q, *([context] if first else [])]
-        shapes = [rows_shape] * (first or last) + [wide_shape] * (not last)
+    for part in (list(range(len(groups) - 2, 0, -1)), [0]):
+        first = part != [0]
+        counts = [len(groups[i]) for i in part]
+        back = [] if first else returned[0]
+        operands = []
+        for i in part:
+            operands += [*groups[i], *kept[i]]
+        operands += [qt, gt, final, grad_q, *([context] if first else [])]
+        shapes = [rows_shape, wide_shape] if first else [rows_shape]
         outs = pl.pallas_call(
             functools.partial(
-                backward_kernel, len(back), count, first, last, tile_of(count * rows, tokens)
+                backward_kernel, len(back), counts, first, tile_of(max(counts) * rows, tokens)
             ),
-            out_shape=shapes + shapes_of(group),
+            out_shape=shapes + shapes_of(sum((groups[i] for i in part), [])),
             in_specs=[ANY] * len(back) + [VMEM] * len(operands),
-            out_specs=[VMEM] * (len(shapes) + count),
-            scratch_shapes=[natural(count), across(count), sums(count), sums(count)],
+            out_specs=[VMEM] * (len(shapes) + sum(counts)),
+            scratch_shapes=[
+                shape
+                for count in counts
+                for shape in (natural(count), across(count), sums(count), sums(count))
+            ],
             compiler_params=compiler_params,
-            cost_estimate=cost(heads, count * rows, tokens, 4),
+            cost_estimate=cost(heads, sum(counts) * rows, tokens, 4),
             name="backward",
         )(*back, *operands)
         if first:
-            context_rows = outs[0]
-        if last:
+            context_rows, grad_q = outs[:2]
+        else:
             grad_query = outs[0]
-        else:
-            grad_q = outs[len(shapes) - 1]
-        returned.append(send_back(i, outs[len(shapes) :]))
+        blocks = list(outs[len(shapes) :])
+        for i in part:
+            returned.append(send_back(i, blocks[: len(groups[i])]))
+            blocks = blocks[len(groups[i]) :]
     return context_rows, grad_query
 
 

time: 70.7 us -> 67.9 us (0.960)
  the two profiles are of different devices: /device:TPU:21 before, /device:TPU:0 now
where the time goes in v12:
time: 67.9 us; the launch traced here: 67.7 us
  starting transfers between devices  30.9 us (46%)
  Pallas kernels  21.1 us (31%)
  waiting for transfers between devices  13.6 us (20%)
  local copies, waits for them, and re-layouts  1.23 us (2%)
  between operations  0.91 us (1%)
    ppermute x8, starting transfers between devices, shards(): blocks.append(lax.ppermute(block, AXES, route(offset, False)))  16.9 us
    ppermute x8, starting transfers between devices, send_back(): lax.ppermute(g, AXES, route(o, True))  14 us
    pallas_call x2, Pallas kernels, attend(): pl.pallas_call(functools.partial(backward_kernel, len(back), counts, firs...  9.42 us
    ppermute x8, waiting for transfers between devices, send_back(): lax.ppermute(g, AXES, route(o, True))  7.38 us
    ppermute x8, waiting for transfers between devices, shards(): blocks.append(lax.ppermute(block, AXES, route(offset, False)))  6.22 us
    pallas_call x3, Pallas kernels, attend(): pl.pallas_call(functools.partial(forward_kernel, count, not state, tile_o...  6.12 us
    pallas_call x1, Pallas kernels, attend(): pl.pallas_call(functools.partial(turn_kernel, count, tile_of(count * rows...  2.57 us
    pallas_call x1, Pallas kernels, unpack(): pl.pallas_call(kernel, out_shape=jax.ShapeDtypeStruct((1, rows, 2, width)...  1.5 us
  transfers between devices with their start and end apart: 16, of which 6 were waited for; matrix products, arithmetic and copies ran while one was open for 0% of the time, Pallas kernels for 24%

profile of v12, /device:TPU:0, one launch (start us, length us, event | category | flops | bytes accessed | tf_op | source)
XLA Modules:
  0.0 67.7 jit_solution(12375579350733449824)
XLA Ops:
  0.6 0.0 copy-start
  0.6 1.2 %copy-done = bf16[1,128,2,2048]{3,2,1,0:T(2,128)(2,1)S(1)} copy-done((bf16[1,128,2,2048]{3,2,1,0:T(2,128)(2,1)S(1)}, bf16[1,128,2,2048]{3,2,1,0:T(2,128)(2,1)}, u32[]{:S(2)}) %copy-start) | copy-done | bytes 1048600
  1.9 0.0 copy-start.1
  1.9 0.0 copy-start.2
  1.9 0.9 %pack.1 = (bf16[2,128,2,128]{3,2,1,0:T(2,128)(2,1)S(1)}, bf16[2,128,2,128]{3,2,1,0:T(2,128)(2,1)S(1)}, bf16[2,128,2,128]{3,2,1,0:T(2,128)(2,1)S(1)}, bf16[2,128,...) custom-call(bf16[1,128,2,2048]{3,2,1,0:T(2,128)(2,1)S(1)} %copy-done), custom_call_target="tpu_custom_call" | custom-call | tf_op jit(solution)/shard_map/pack/pallas_call | solution.py:80
  2.8 3.5 %collective-permute-start.4 = (bf16[2,256,128]{2,1,0:T(8,128)(2,1)S(1)}, bf16[2,256,128]{2,1,0:T(8,128)(2,1)S(1)}, u32[]{:S(2)}, u32[]{:S(2)}) collective-permute-start(bf16[2,256,128]{2,1,0:T(8,128)(2,1)S(1)} %bitcast.31), channel_id=1, source_target_pairs={{0,11},{1,10},{2,13},{3,12},{4,15},{5,14},{6,9},{7,8},{8,19},{9,18... | collective-permute-start | bytes 393224 | tf_op jit(solution)/shard_map/ppermute | solution.py:453
  6.3 1.7 %collective-permute-start.5 = (bf16[2,256,128]{2,1,0:T(8,128)(2,1)S(1)}, bf16[2,256,128]{2,1,0:T(8,128)(2,1)S(1)}, u32[]{:S(2)}, u32[]{:S(2)}) collective-permute-start(bf16[2,256,128]{2,1,0:T(8,128)(2,1)S(1)} %bitcast.30), channel_id=1, source_target_pairs={{0,9},{1,8},{2,11},{3,10},{4,13},{5,12},{6,15},{7,14},{8,17},{9,16... | collective-permute-start | bytes 393224 | tf_op jit(solution)/shard_map/ppermute | solution.py:453
  8.0 2.6 %collective-permute-start.6 = (bf16[2,256,128]{2,1,0:T(8,128)(2,1)S(1)}, bf16[2,256,128]{2,1,0:T(8,128)(2,1)S(1)}, u32[]{:S(2)}, u32[]{:S(2)}) collective-permute-start(bf16[2,256,128]{2,1,0:T(8,128)(2,1)S(1)} %bitcast.29), channel_id=1, source_target_pairs={{0,15},{1,14},{2,9},{3,8},{4,11},{5,10},{6,13},{7,12},{8,23},{9,22... | collective-permute-start | bytes 393224 | tf_op jit(solution)/shard_map/ppermute | solution.py:453
  10.6 0.0 collective-permute-start.1
  10.7 3.5 %collective-permute-start.2 = (bf16[2,256,128]{2,1,0:T(8,128)(2,1)S(1)}, bf16[2,256,128]{2,1,0:T(8,128)(2,1)S(1)}, u32[]{:S(2)}, u32[]{:S(2)}) collective-permute-start(bf16[2,256,128]{2,1,0:T(8,128)(2,1)S(1)} %bitcast.27), channel_id=1, source_target_pairs={{0,14},{1,15},{2,8},{3,9},{4,10},{5,11},{6,12},{7,13},{8,22},{9,23... | collective-permute-start | bytes 393224 | tf_op jit(solution)/shard_map/ppermute | solution.py:453
  14.2 0.0 collective-permute-done.4.refs_0_.refs_1_
  14.2 1.6 %collective-permute-start.3 = (bf16[2,256,128]{2,1,0:T(8,128)(2,1)S(1)}, bf16[2,256,128]{2,1,0:T(8,128)(2,1)S(1)}, u32[]{:S(2)}, u32[]{:S(2)}) collective-permute-start(bf16[2,256,128]{2,1,0:T(8,128)(2,1)S(1)} %bitcast.26), channel_id=1, source_target_pairs={{0,8},{1,9},{2,10},{3,11},{4,12},{5,13},{6,14},{7,15},{8,16},{9,17... | collective-permute-start | bytes 393224 | tf_op jit(solution)/shard_map/ppermute | solution.py:453
  15.8 1.4 %collective-permute-done.5.refs_1_.refs_2_ = bf16[2,256,128]{2,1,0:T(8,128)(2,1)S(1)} collective-permute-done((bf16[2,256,128]{2,1,0:T(8,128)(2,1)S(1)}, bf16[2,256,128]{2,1,0:T(8,128)(2,1)S(1)}, u32[]{:S(2)}, u32[]{:S(2)}) %collective-permute-start.5) | collective-permute-done | bytes 131104 | tf_op jit(solution)/shard_map/ppermute | solution.py:453
  17.2 2.7 %collective-permute-start = (bf16[2,256,128]{2,1,0:T(8,128)(2,1)S(1)}, bf16[2,256,128]{2,1,0:T(8,128)(2,1)S(1)}, u32[]{:S(2)}, u32[]{:S(2)}) collective-permute-start(bf16[2,256,128]{2,1,0:T(8,128)(2,1)S(1)} %bitcast.25), channel_id=1, source_target_pairs={{0,13},{1,12},{2,15},{3,14},{4,9},{5,8},{6,11},{7,10},{8,21},{9,20... | collective-permute-start | bytes 393224 | tf_op jit(solution)/shard_map/ppermute | solution.py:453
  19.9 0.0 copy-done.1
  19.9 0.3 turned.2.refs_3_.refs_1_.refs_8_.refs_6_
  20.2 0.0 copy-done.2
  20.2 0.3 turned.3.refs_2_.refs_9_.refs_7_
  20.5 0.0 collective-permute-done.6.refs_2_.refs_3_
  20.5 1.2 %collective-permute-start.7 = (bf16[2,256,128]{2,1,0:T(8,128)(2,1)S(1)}, bf16[2,256,128]{2,1,0:T(8,128)(2,1)S(1)}, u32[]{:S(2)}, u32[]{:S(2)}) collective-permute-start(bf16[2,256,128]{2,1,0:T(8,128)(2,1)S(1)} %bitcast.24), channel_id=1, source_target_pairs={{0,12},{1,13},{2,14},{3,15},{4,8},{5,9},{6,10},{7,11},{8,20},{9,21... | collective-permute-start | bytes 393224 | tf_op jit(solution)/shard_map/ppermute | solution.py:453
  21.7 2.5 %forward.3 = (f32[2,8,1536]{2,1,0:T(8,128)S(1)}, f32[2,128,1536]{2,1,0:T(8,128)S(1)}, bf16[2,384,1536]{2,1,0:T(8,128)(2,1)S(1)}) custom-call(bf16[2,256,128]{2,1,0:T(8,128)(2,1)S(1)} %collective-permute-done.4.refs_0_.refs_1_, bf16[2,256,128]{2,1,0:T(8,128)(2,1)S(1)} %collective-permute-done.5.refs_1_.refs_2_, ...), custom_call_target="tpu_custom_call" | custom-call | flops 603979776 | bytes 3932160 | tf_op jit(solution)/shard_map/forward/pallas_call | solution.py:382
  24.3 0.0 collective-permute-done.1.refs_0_.refs_3_
  24.3 0.0 collective-permute-done.2.refs_1_.refs_4_
  24.3 0.0 collective-permute-done.3.refs_2_.refs_5_
  24.3 2.5 %forward.4 = (f32[2,8,1536]{2,1,0:T(8,128)S(1)}, f32[2,128,1536]{2,1,0:T(8,128)S(1)}, bf16[2,384,1536]{2,1,0:T(8,128)(2,1)S(1)}) custom-call(bf16[2,256,128]{2,1,0:T(8,128)(2,1)S(1)} %collective-permute-done.1.refs_0_.refs_3_, bf16[2,256,128]{2,1,0:T(8,128)(2,1)S(1)} %collective-permute-done.2.refs_1_.refs_4_, ...), custom_call_target="tpu_custom_call" | custom-call | flops 603979776 | bytes 3932160 | tf_op jit(solution)/shard_map/forward/pallas_call | solution.py:382
  26.8 4.4 %collective-permute-done.refs_0_ = bf16[2,256,128]{2,1,0:T(8,128)(2,1)S(1)} collective-permute-done((bf16[2,256,128]{2,1,0:T(8,128)(2,1)S(1)}, bf16[2,256,128]{2,1,0:T(8,128)(2,1)S(1)}, u32[]{:S(2)}, u32[]{:S(2)}) %collective-permute-start) | collective-permute-done | bytes 131104 | tf_op jit(solution)/shard_map/ppermute | solution.py:453
  31.2 1.0 %forward.5 = (f32[2,8,1536]{2,1,0:T(8,128)S(1)}, f32[2,128,1536]{2,1,0:T(8,128)S(1)}, bf16[2,128,1536]{2,1,0:T(8,128)(2,1)S(1)}) custom-call(bf16[2,256,128]{2,1,0:T(8,128)(2,1)S(1)} %collective-permute-done.refs_0_, bf16[2,128,1536]{2,1,0:T(8,128)(2,1)S(1)} %turned.2.refs_3_.refs_1_.refs_8_.refs_6_, f32[2,8,1536]{2,1,0:T(8,128)S(1)} %get-tuple-element.43.refs_2_.refs_7_, ...), custom_call_target="tpu_custom_call" | custom-call | flops 201326592 | bytes 3407872 | tf_op jit(solution)/shard_map/forward/pallas_call | solution.py:382
  32.2 0.4 collective-permute-done.7.refs_0_
  32.7 2.6 %turn.1 = (f32[2,8,1536]{2,1,0:T(8,128)S(1)}, f32[2,128,1536]{2,1,0:T(8,128)S(1)}, f32[2,128,1536]{2,1,0:T(8,128)S(1)}, bf16[2,256,128]{2,1,0:T(8,128)(2,1)S(1)}) custom-call(bf16[2,256,128]{2,1,0:T(8,128)(2,1)S(1)} %collective-permute-done.7.refs_0_, bf16[2,128,1536]{2,1,0:T(8,128)(2,1)S(1)} %turned.2.refs_3_.refs_1_.refs_8_.refs_6_, ...), custom_call_target="tpu_custom_call" | custom-call | flops 603979776 | bytes 3407872 | tf_op jit(solution)/shard_map/turn/pallas_call | solution.py:396
  35.2 0.2 collective-permute-start.8
  35.5 5.5 %backward.2 = (bf16[1,1536,256]{2,1,0:T(8,128)(2,1)}, f32[2,128,1536]{2,1,0:T(8,128)S(1)}, bf16[2,256,128]{2,1,0:T(8,128)(2,1)S(1)}, bf16[2,256,128]{2,1,0:T(8,1...) custom-call(bf16[2,256,128]{2,1,0:T(8,128)(2,1)S(1)} %collective-permute-done.refs_0_, ...), custom_call_target="tpu_custom_call" | custom-call | flops 1610612736 | bytes 4194304 | tf_op jit(solution)/shard_map/backward/pallas_call | solution.py:418
  41.0 4.8 %collective-permute-start.9 = (bf16[2,256,128]{2,1,0:T(8,128)(2,1)S(1)}, bf16[2,256,128]{2,1,0:T(8,128)(2,1)S(1)}, u32[]{:S(2)}, u32[]{:S(2)}) collective-permute-start(bf16[2,256,128]{2,1,0:T(8,128)(2,1)S(1)} %get-tuple-element.58), channel_id=1, source_target_pairs={{13,0},{12,1},{15,2},{14,3},{9,4},{8,5},{11,6},{10,7},{21,8},{20,9... | collective-permute-start | bytes 393224 | tf_op jit(solution)/shard_map/ppermute | solution.py:461
  45.7 1.7 %collective-permute-start.10 = (bf16[2,256,128]{2,1,0:T(8,128)(2,1)S(1)}, bf16[2,256,128]{2,1,0:T(8,128)(2,1)S(1)}, u32[]{:S(2)}, u32[]{:S(2)}) collective-permute-start(bf16[2,256,128]{2,1,0:T(8,128)(2,1)S(1)} %get-tuple-element.59), channel_id=1, source_target_pairs={{10,0},{11,1},{12,2},{13,3},{14,4},{15,5},{8,6},{9,7},{18,8},{19,9... | collective-permute-start | bytes 393224 | tf_op jit(solution)/shard_map/ppermute | solution.py:461
  47.4 0.1 collective-permute-start.11
  47.6 0.4 collective-permute-start.12
  48.0 0.0 collective-permute-done.8.refs_0_
  48.0 3.9 %backward.3 = (bf16[1,1536,256]{2,1,0:T(8,128)(2,1)}, bf16[2,256,128]{2,1,0:T(8,128)(2,1)S(1)}, bf16[2,256,128]{2,1,0:T(8,128)(2,1)S(1)}, bf16[2,256,128]{2,1,0:T(8,128)(2,1)S(1)}) custom-call(bf16[2,256,128]{2,1,0:T(8,128)(2,1)S(1)} %collective-permute-done.8.refs_0_, bf16[2,256,128]{2,1,0:T(8,128)(2,1)S(1)} %collective-permute-done.4.refs_0_.refs_1_, ...), custom_call_target="tpu_custom_call" | custom-call | flops 1207959552 | bytes 3932160 | tf_op jit(solution)/shard_map/backward/pallas_call | solution.py:418
  51.9 4.0 %collective-permute-start.13 = (bf16[2,256,128]{2,1,0:T(8,128)(2,1)S(1)}, bf16[2,256,128]{2,1,0:T(8,128)(2,1)S(1)}, u32[]{:S(2)}, u32[]{:S(2)}) collective-permute-start(bf16[2,256,128]{2,1,0:T(8,128)(2,1)S(1)} %get-tuple-element.62), channel_id=1, source_target_pairs={{11,0},{10,1},{13,2},{12,3},{15,4},{14,5},{9,6},{8,7},{19,8},{18,9... | collective-permute-start | bytes 393224 | tf_op jit(solution)/shard_map/ppermute | solution.py:461
  56.0 0.0 collective-permute-done.9
  56.0 1.6 %collective-permute-start.14 = (bf16[2,256,128]{2,1,0:T(8,128)(2,1)S(1)}, bf16[2,256,128]{2,1,0:T(8,128)(2,1)S(1)}, u32[]{:S(2)}, u32[]{:S(2)}) collective-permute-start(bf16[2,256,128]{2,1,0:T(8,128)(2,1)S(1)} %get-tuple-element.63), channel_id=1, source_target_pairs={{9,0},{8,1},{11,2},{10,3},{13,4},{12,5},{15,6},{14,7},{17,8},{16,9... | collective-permute-start | bytes 393224 | tf_op jit(solution)/shard_map/ppermute | solution.py:461
  57.6 0.0 collective-permute-done.10
  57.6 1.1 %collective-permute-start.15 = (bf16[2,256,128]{2,1,0:T(8,128)(2,1)S(1)}, bf16[2,256,128]{2,1,0:T(8,128)(2,1)S(1)}, u32[]{:S(2)}, u32[]{:S(2)}) collective-permute-start(bf16[2,256,128]{2,1,0:T(8,128)(2,1)S(1)} %get-tuple-element.64), channel_id=1, source_target_pairs={{15,0},{14,1},{9,2},{8,3},{11,4},{10,5},{13,6},{12,7},{23,8},{22,9... | collective-permute-start | bytes 393224 | tf_op jit(solution)/shard_map/ppermute | solution.py:461
  58.7 0.0 collective-permute-done.11
  58.7 0.0 collective-permute-done.12
  58.7 1.1 %collective-permute-done.13 = bf16[2,256,128]{2,1,0:T(8,128)(2,1)S(1)} collective-permute-done((bf16[2,256,128]{2,1,0:T(8,128)(2,1)S(1)}, bf16[2,256,128]{2,1,0:T(8,128)(2,1)S(1)}, u32[]{:S(2)}, u32[]{:S(2)}) %collective-permute-start.13) | collective-permute-done | bytes 131104 | tf_op jit(solution)/shard_map/ppermute | solution.py:461
  59.8 3.2 %collective-permute-done.14 = bf16[2,256,128]{2,1,0:T(8,128)(2,1)S(1)} collective-permute-done((bf16[2,256,128]{2,1,0:T(8,128)(2,1)S(1)}, bf16[2,256,128]{2,1,0:T(8,128)(2,1)S(1)}, u32[]{:S(2)}, u32[]{:S(2)}) %collective-permute-start.14) | collective-permute-done | bytes 131104 | tf_op jit(solution)/shard_map/ppermute | solution.py:461
  63.0 3.1 %collective-permute-done.15 = bf16[2,256,128]{2,1,0:T(8,128)(2,1)S(1)} collective-permute-done((bf16[2,256,128]{2,1,0:T(8,128)(2,1)S(1)}, bf16[2,256,128]{2,1,0:T(8,128)(2,1)S(1)}, u32[]{:S(2)}, u32[]{:S(2)}) %collective-permute-start.15) | collective-permute-done | bytes 131104 | tf_op jit(solution)/shard_map/ppermute | solution.py:461
  66.0 1.5 %unpack.1 = bf16[1,128,2,2048]{3,2,1,0:T(2,128)(2,1)} custom-call(bf16[2,128,2,128]{3,2,1,0:T(2,128)(2,1)S(1)} %bitcast.16, bf16[2,128,2,128]{3,2,1,0:T(2,128)(2,1)S(1)} %bitcast.17, bf16[2,128,2,128]{3,2,1,0:T(2,128)(2,1)S(1)} %bitcast.18, bf16[2,128,2,128]{3,2,1,0:T(2,128)(2,1)S(1)} %bitcast.19, bf16[2,128,2,128]{3,2,1,0:T(2,128)(2,1)S(1)} %bitcast.20, ...), custom_call_target="tpu_custom_call" | custom-call | tf_op jit(solution)/shard_map/unpack/pallas_call | solution.py:116
Async XLA Ops:
  0.6 1.2 %copy-start = (bf16[1,128,2,2048]{3,2,1,0:T(2,128)(2,1)S(1)}, bf16[1,128,2,2048]{3,2,1,0:T(2,128)(2,1)}, u32[]{:S(2)}) copy-start(bf16[1,128,2,2048]{3,2,1,0:T(2,128)(2,1)} %pairs_ref.1) | copy-start | bytes 3145732
  1.9 18.1 %copy-start.1 = (bf16[1,1536,256]{2,1,0:T(8,128)(2,1)S(1)}, bf16[1,1536,256]{2,1,0:T(8,128)(2,1)}, u32[]{:S(2)}) copy-start(bf16[1,1536,256]{2,1,0:T(8,128)(2,1)} %rows_ref.2) | copy-start | bytes 2359300
  1.9 18.3 %copy-start.2 = (bf16[1,1536,256]{2,1,0:T(8,128)(2,1)S(1)}, bf16[1,1536,256]{2,1,0:T(8,128)(2,1)}, u32[]{:S(2)}) copy-start(bf16[1,1536,256]{2,1,0:T(8,128)(2,1)} %rows_ref.3) | copy-start | bytes 2359300
  2.8 11.3 %collective-permute-start.4 = (bf16[2,256,128]{2,1,0:T(8,128)(2,1)S(1)}, bf16[2,256,128]{2,1,0:T(8,128)(2,1)S(1)}, u32[]{:S(2)}, u32[]{:S(2)}) collective-permute-start(bf16[2,256,128]{2,1,0:T(8,128)(2,1)S(1)} %bitcast.31), channel_id=1, source_target_pairs={{0,11},{1,10},{2,13},{3,12},{4,15},{5,14},{6,9},{7,8},{8,19},{9,18... | collective-permute-start | bytes 393224 | tf_op jit(solution)/shard_map/ppermute | solution.py:453
  6.3 10.9 %collective-permute-start.5 = (bf16[2,256,128]{2,1,0:T(8,128)(2,1)S(1)}, bf16[2,256,128]{2,1,0:T(8,128)(2,1)S(1)}, u32[]{:S(2)}, u32[]{:S(2)}) collective-permute-start(bf16[2,256,128]{2,1,0:T(8,128)(2,1)S(1)} %bitcast.30), channel_id=1, source_target_pairs={{0,9},{1,8},{2,11},{3,10},{4,13},{5,12},{6,15},{7,14},{8,17},{9,16... | collective-permute-start | bytes 393224 | tf_op jit(solution)/shard_map/ppermute | solution.py:453
  8.0 12.5 %collective-permute-start.6 = (bf16[2,256,128]{2,1,0:T(8,128)(2,1)S(1)}, bf16[2,256,128]{2,1,0:T(8,128)(2,1)S(1)}, u32[]{:S(2)}, u32[]{:S(2)}) collective-permute-start(bf16[2,256,128]{2,1,0:T(8,128)(2,1)S(1)} %bitcast.29), channel_id=1, source_target_pairs={{0,15},{1,14},{2,9},{3,8},{4,11},{5,10},{6,13},{7,12},{8,23},{9,22... | collective-permute-start | bytes 393224 | tf_op jit(solution)/shard_map/ppermute | solution.py:453
  10.6 13.6 %collective-permute-start.1 = (bf16[2,256,128]{2,1,0:T(8,128)(2,1)S(1)}, bf16[2,256,128]{2,1,0:T(8,128)(2,1)S(1)}, u32[]{:S(2)}, u32[]{:S(2)}) collective-permute-start(bf16[2,256,128]{2,1,0:T(8,128)(2,1)S(1)} %bitcast.28), channel_id=1, source_target_pairs={{0,10},{1,11},{2,12},{3,13},{4,14},{5,15},{6,8},{7,9},{8,18},{9,19... | collective-permute-start | bytes 393224 | tf_op jit(solution)/shard_map/ppermute | solution.py:453
  10.7 13.6 %collective-permute-start.2 = (bf16[2,256,128]{2,1,0:T(8,128)(2,1)S(1)}, bf16[2,256,128]{2,1,0:T(8,128)(2,1)S(1)}, u32[]{:S(2)}, u32[]{:S(2)}) collective-permute-start(bf16[2,256,128]{2,1,0:T(8,128)(2,1)S(1)} %bitcast.27), channel_id=1, source_target_pairs={{0,14},{1,15},{2,8},{3,9},{4,10},{5,11},{6,12},{7,13},{8,22},{9,23... | collective-permute-start | bytes 393224 | tf_op jit(solution)/shard_map/ppermute | solution.py:453
  14.2 10.1 %collective-permute-start.3 = (bf16[2,256,128]{2,1,0:T(8,128)(2,1)S(1)}, bf16[2,256,128]{2,1,0:T(8,128)(2,1)S(1)}, u32[]{:S(2)}, u32[]{:S(2)}) collective-permute-start(bf16[2,256,128]{2,1,0:T(8,128)(2,1)S(1)} %bitcast.26), channel_id=1, source_target_pairs={{0,8},{1,9},{2,10},{3,11},{4,12},{5,13},{6,14},{7,15},{8,16},{9,17... | collective-permute-start | bytes 393224 | tf_op jit(solution)/shard_map/ppermute | solution.py:453
  17.2 14.0 %collective-permute-start = (bf16[2,256,128]{2,1,0:T(8,128)(2,1)S(1)}, bf16[2,256,128]{2,1,0:T(8,128)(2,1)S(1)}, u32[]{:S(2)}, u32[]{:S(2)}) collective-permute-start(bf16[2,256,128]{2,1,0:T(8,128)(2,1)S(1)} %bitcast.25), channel_id=1, source_target_pairs={{0,13},{1,12},{2,15},{3,14},{4,9},{5,8},{6,11},{7,10},{8,21},{9,20... | collective-permute-start | bytes 393224 | tf_op jit(solution)/shard_map/ppermute | solution.py:453
  20.5 12.2 %collective-permute-start.7 = (bf16[2,256,128]{2,1,0:T(8,128)(2,1)S(1)}, bf16[2,256,128]{2,1,0:T(8,128)(2,1)S(1)}, u32[]{:S(2)}, u32[]{:S(2)}) collective-permute-start(bf16[2,256,128]{2,1,0:T(8,128)(2,1)S(1)} %bitcast.24), channel_id=1, source_target_pairs={{0,12},{1,13},{2,14},{3,15},{4,8},{5,9},{6,10},{7,11},{8,20},{9,21... | collective-permute-start | bytes 393224 | tf_op jit(solution)/shard_map/ppermute | solution.py:453
  35.2 12.7 %collective-permute-start.8 = (bf16[2,256,128]{2,1,0:T(8,128)(2,1)S(1)}, bf16[2,256,128]{2,1,0:T(8,128)(2,1)S(1)}, u32[]{:S(2)}, u32[]{:S(2)}) collective-permute-start(bf16[2,256,128]{2,1,0:T(8,128)(2,1)S(1)} %get-tuple-element.54), channel_id=1, source_target_pairs={{12,0},{13,1},{14,2},{15,3},{8,4},{9,5},{10,6},{11,7},{20,8},{21,9... | collective-permute-start | bytes 393224 | tf_op jit(solution)/shard_map/ppermute | solution.py:461
  41.0 15.0 %collective-permute-start.9 = (bf16[2,256,128]{2,1,0:T(8,128)(2,1)S(1)}, bf16[2,256,128]{2,1,0:T(8,128)(2,1)S(1)}, u32[]{:S(2)}, u32[]{:S(2)}) collective-permute-start(bf16[2,256,128]{2,1,0:T(8,128)(2,1)S(1)} %get-tuple-element.58), channel_id=1, source_target_pairs={{13,0},{12,1},{15,2},{14,3},{9,4},{8,5},{11,6},{10,7},{21,8},{20,9... | collective-permute-start | bytes 393224 | tf_op jit(solution)/shard_map/ppermute | solution.py:461
  45.7 11.9 %collective-permute-start.10 = (bf16[2,256,128]{2,1,0:T(8,128)(2,1)S(1)}, bf16[2,256,128]{2,1,0:T(8,128)(2,1)S(1)}, u32[]{:S(2)}, u32[]{:S(2)}) collective-permute-start(bf16[2,256,128]{2,1,0:T(8,128)(2,1)S(1)} %get-tuple-element.59), channel_id=1, source_target_pairs={{10,0},{11,1},{12,2},{13,3},{14,4},{15,5},{8,6},{9,7},{18,8},{19,9... | collective-permute-start | bytes 393224 | tf_op jit(solution)/shard_map/ppermute | solution.py:461
  47.4 11.2 %collective-permute-start.11 = (bf16[2,256,128]{2,1,0:T(8,128)(2,1)S(1)}, bf16[2,256,128]{2,1,0:T(8,128)(2,1)S(1)}, u32[]{:S(2)}, u32[]{:S(2)}) collective-permute-start(bf16[2,256,128]{2,1,0:T(8,128)(2,1)S(1)} %get-tuple-element.60), channel_id=1, source_target_pairs={{14,0},{15,1},{8,2},{9,3},{10,4},{11,5},{12,6},{13,7},{22,8},{23,9... | collective-permute-start | bytes 393224 | tf_op jit(solution)/shard_map/ppermute | solution.py:461
  47.6 11.1 %collective-permute-start.12 = (bf16[2,256,128]{2,1,0:T(8,128)(2,1)S(1)}, bf16[2,256,128]{2,1,0:T(8,128)(2,1)S(1)}, u32[]{:S(2)}, u32[]{:S(2)}) collective-permute-start(bf16[2,256,128]{2,1,0:T(8,128)(2,1)S(1)} %get-tuple-element.61), channel_id=1, source_target_pairs={{8,0},{9,1},{10,2},{11,3},{12,4},{13,5},{14,6},{15,7},{16,8},{17,9... | collective-permute-start | bytes 393224 | tf_op jit(solution)/shard_map/ppermute | solution.py:461
  51.9 7.9 %collective-permute-start.13 = (bf16[2,256,128]{2,1,0:T(8,128)(2,1)S(1)}, bf16[2,256,128]{2,1,0:T(8,128)(2,1)S(1)}, u32[]{:S(2)}, u32[]{:S(2)}) collective-permute-start(bf16[2,256,128]{2,1,0:T(8,128)(2,1)S(1)} %get-tuple-element.62), channel_id=1, source_target_pairs={{11,0},{10,1},{13,2},{12,3},{15,4},{14,5},{9,6},{8,7},{19,8},{18,9... | collective-permute-start | bytes 393224 | tf_op jit(solution)/shard_map/ppermute | solution.py:461
  56.0 7.0 %collective-permute-start.14 = (bf16[2,256,128]{2,1,0:T(8,128)(2,1)S(1)}, bf16[2,256,128]{2,1,0:T(8,128)(2,1)S(1)}, u32[]{:S(2)}, u32[]{:S(2)}) collective-permute-start(bf16[2,256,128]{2,1,0:T(8,128)(2,1)S(1)} %get-tuple-element.63), channel_id=1, source_target_pairs={{9,0},{8,1},{11,2},{10,3},{13,4},{12,5},{15,6},{14,7},{17,8},{16,9... | collective-permute-start | bytes 393224 | tf_op jit(solution)/shard_map/ppermute | solution.py:461
  57.6 8.5 %collective-permute-start.15 = (bf16[2,256,128]{2,1,0:T(8,128)(2,1)S(1)}, bf16[2,256,128]{2,1,0:T(8,128)(2,1)S(1)}, u32[]{:S(2)}, u32[]{:S(2)}) collective-permute-start(bf16[2,256,128]{2,1,0:T(8,128)(2,1)S(1)} %get-tuple-element.64), channel_id=1, source_target_pairs={{15,0},{14,1},{9,2},{8,3},{11,4},{10,5},{13,6},{12,7},{23,8},{22,9... | collective-permute-start | bytes 393224 | tf_op jit(solution)/shard_map/ppermute | solution.py:461

commit v13 on v11

--- a/solution.py
+++ b/solution.py
@@ -13,47 +13,51 @@
 EXPONENT = FACTOR * 1.4426950408889634
 MIB = 1 << 20
 NT = ((1,), (1,))
+WAITS = (False, False)
 ANY = pl.BlockSpec(memory_space=pl.ANY)
 HBM = pl.BlockSpec(memory_space=pltpu.HBM)
 VMEM = pl.BlockSpec(memory_space=pltpu.VMEM)
 
 
-def partner(index, distance, count):
-    turned_round = (index & 1) * (count // 2) if count % 4 == 0 and distance % (count // 2) == 0 else 0
-    total = index + distance + turned_round
-    return total % count if isinstance(total, int) else lax.rem(total, count)
-
-
 def offset_groups():
     seq_count = lax.axis_size("seq")
     tp_count = lax.axis_size("tp")
-    order = [(dz, dy) for dz in range(seq_count) for dy in reversed(range(tp_count))]
-    count = len(order)
-    cuts = [0, count * 3 // 8, count * 3 // 4, count]
-    return [order[a:b] for a, b in zip(cuts[:-1], cuts[1:])]
+    order = [(dz, dy) for dy in reversed(range(tp_count)) for dz in range(seq_count)]
+    order.sort(key=lambda o: (-o[1], -abs(o[0] - seq_count / 2 - 0.25)))
+    half = len(order) // 2
+    return [order[:half], order[half:]]
 
 
 def group_at(offset):
     seq_count = lax.axis_size("seq")
     tp_count = lax.axis_size("tp")
-    z = partner(lax.axis_index("seq"), offset[0], seq_count)
+    z = lax.rem(lax.axis_index("seq") + offset[0], seq_count)
     y = lax.rem(lax.axis_index("tp") + offset[1], tp_count)
     return z * tp_count + y
 
 
-def route(offset, back):
+def route(offset, parity, back):
     segments, seq_count, tp_count = (lax.axis_size(a) for a in AXES)
     hops = []
-    for s in range(segments):
+    for s in range(parity, segments, 2):
         for z in range(seq_count):
             for y in range(tp_count):
                 source = (s * seq_count + z) * tp_count + y
                 s_to = (s + 1) % segments
-                z_to = partner(z, offset[0], seq_count)
+                z_to = (z + offset[0]) % seq_count
                 y_to = (y + offset[1]) % tp_count
                 target = (s_to * seq_count + z_to) * tp_count + y_to
                 hops.append((target, source) if back else (source, target))
     return hops
+
+
+def on_parity(parity, kernel):
+    def run(*refs):
+        @pl.when(lax.rem(lax.axis_index("segment"), 2) == parity)
+        def _():
+            kernel(*refs)
+
+    return run
 
 
 def params(enc_len):
@@ -87,24 +91,29 @@
 def unpack(blocks, order, width):
     heads, rows, _, _ = blocks[0].shape
     local = heads * HEAD
+    count = len(order)
     parts = 4 if rows % 64 == 0 else 1
     size = rows // parts
 
     def kernel(*refs):
-        ins, out, held, sem = refs[: len(order)], refs[len(order)], refs[-2], refs[-1]
+        out, held, sem = refs[2 * count], refs[-2], refs[-1]
 
         def store(r):
             here = pl.ds(pl.multiple_of(r * size, size), size)
             return pltpu.make_async_copy(held.at[here], out.at[0, here], sem.at[r])
 
-        @pl.loop(0, parts)
-        def _(r):
+        def fill(r, ins):
             here = pl.ds(pl.multiple_of(r * size, size), size)
             for block, offset in zip(ins, order):
                 base = group_at(offset) * local
                 for h in range(heads):
                     column = pl.multiple_of(base + h * HEAD, HEAD)
                     held[here, :, pl.ds(column, HEAD)] = block[h, here]
+
+        @pl.loop(0, parts)
+        def _(r):
+            for parity in range(2):
+                on_parity(parity, fill)(r, refs[parity * count : (parity + 1) * count])
             store(r).start()
 
         for r in range(parts):
@@ -113,7 +122,7 @@
     return pl.pallas_call(
         kernel,
         out_shape=jax.ShapeDtypeStruct((1, rows, 2, width), blocks[0].dtype),
-        in_specs=[VMEM] * len(order),
+        in_specs=[VMEM] * (2 * count),
         out_specs=HBM,
         scratch_shapes=[
             pltpu.VMEM((rows, 2, width), blocks[0].dtype),
@@ -122,6 +131,32 @@
         compiler_params=pltpu.CompilerParams(vmem_limit_bytes=24 * MIB),
         name="unpack",
     )(*blocks)
+
+
+def turned_back(arrays, dtype):
+    heads, _, tokens = arrays[0].shape
+    tile = 256 if tokens % 256 == 0 else tokens
+
+    def kernel(*refs):
+        out = refs[2]
+
+        def turn(ref):
+            for h in range(heads):
+                for j in range(tokens // tile):
+                    here = slice(j * tile, (j + 1) * tile)
+                    out[0, here, h * HEAD : (h + 1) * HEAD] = ref[h, :, here].T.astype(dtype)
+
+        on_parity(1, turn)(refs[0])
+        on_parity(0, turn)(refs[1])
+
+    return pl.pallas_call(
+        kernel,
+        out_shape=jax.ShapeDtypeStruct((1, tokens, heads * HEAD), dtype),
+        in_specs=[VMEM] * 2,
+        out_specs=VMEM,
+        compiler_params=pltpu.CompilerParams(vmem_limit_bytes=16 * MIB),
+        name="turned_back",
+    )(*arrays)
 
 
 def turned(rows):
@@ -294,19 +329,12 @@
         join_chunks(outs, h, rows, gk_ref, gv_ref)
 
 
-def backward_kernel(back, count, first, last, tile, *refs):
+def backward_kernel(back, count, tile, *refs):
     refs = refs[back:]
     chunks, refs = refs[:count], refs[count:]
-    low_ref, then_ref, qt_ref, gt_ref, stats_ref, grad_q_in = refs[:6]
-    refs = refs[6:]
-    if first:
-        ready_ref, refs = refs[0], refs[1:]
-    if first or last:
-        rows_ref, refs = refs[0], refs[1:]
-    if not last:
-        grad_q_ref, refs = refs[0], refs[1:]
-    outs, refs = refs[:count], refs[count:]
-    v_ref, kt_ref, gk_ref, gv_ref = refs
+    low_ref, then_ref, qt_ref, gt_ref, stats_ref, grad_q_in, grad_q_ref = refs[:7]
+    outs, own = refs[7 : 7 + count], refs[7 + count :]
+    v_ref, kt_ref, gk_ref, gv_ref = own
     heads, pair_rows, _ = chunks[0].shape
     rows = pair_rows // 2
     for h in range(heads):
@@ -318,21 +346,14 @@
     def _(j):
         here = tokens_of(j, tile)
         for h in range(heads):
-            columns = slice(h * HEAD, (h + 1) * HEAD)
             qt, gt = qt_ref[h, :, here], gt_ref[h, :, here]
             top, scale, row_dot = (stats_ref[h, i : i + 1, here] for i in range(3))
             shrunk = jnp.exp2((then_ref[h, 0:1, here] - top) * EXPONENT)
             low = low_ref[h, :, here]
             raised = low.astype(jnp.float32)
-            grad_q = grad_q_in[h, :, here] + gradients(
-                raised, low, scale * shrunk, row_dot, qt, gt, refs, h
+            grad_q_ref[h, :, here] = grad_q_in[h, :, here] + gradients(
+                raised, low, scale * shrunk, row_dot, qt, gt, own, h
             )
-            if last:
-                rows_ref[0, here, columns] = grad_q.T.astype(rows_ref.dtype)
-            else:
-                grad_q_ref[h, :, here] = grad_q
-            if first:
-                rows_ref[0, here, columns] = ready_ref[h, :, here].T.astype(rows_ref.dtype)
 
     for h in range(heads):
         join_chunks(outs, h, rows, gk_ref, gv_ref)
@@ -346,15 +367,13 @@
     )
 
 
-def attend(groups, queries, upstream, send_back):
+def attend(groups, qt, gt, parity, send_back):
     heads, pair_rows, _ = groups[0][0].shape
     rows = pair_rows // 2
     enc_len = sum(len(g) for g in groups) * rows
-    tokens = queries.shape[1]
-    qt, gt = turned(queries), turned(upstream)
+    tokens = qt.shape[2]
     stats_shape = jax.ShapeDtypeStruct((heads, 8, tokens), jnp.float32)
     wide_shape = jax.ShapeDtypeStruct((heads, HEAD, tokens), jnp.float32)
-    rows_shape = jax.ShapeDtypeStruct(queries.shape, queries.dtype)
     compiler_params = params(enc_len)
 
     def natural(count):
@@ -369,27 +388,27 @@
     def shapes_of(group):
         return [jax.ShapeDtypeStruct(c.shape, c.dtype) for c in group]
 
-    waits = {1: [], 0: [0]}
-    state, kept = [], []
-    for group in groups[:-1]:
-        count = len(group)
-        low_shape = jax.ShapeDtypeStruct((heads, count * rows, tokens), jnp.bfloat16)
-        stats, context, low = pl.pallas_call(
-            functools.partial(forward_kernel, count, not state, tile_of(count * rows, tokens)),
-            out_shape=[stats_shape, wide_shape, low_shape],
-            in_specs=[VMEM] * (count + 1 + len(state)),
-            out_specs=[VMEM] * 3,
-            scratch_shapes=[natural(count), across(count, 16)],
-            compiler_params=compiler_params,
-            cost_estimate=cost(heads, count * rows, tokens, 2),
-            name="forward",
-        )(*group, qt, *state)
-        state = [stats, context]
-        kept.append((low, stats))
-
-    group, count = groups[-1], len(groups[-1])
+    def here(kernel, *static):
+        return on_parity(parity, functools.partial(kernel, *static))
+
+    group, count = groups[0], len(groups[0])
+    tile = tile_of(count * rows, tokens)
+    low_shape = jax.ShapeDtypeStruct((heads, count * rows, tokens), jnp.bfloat16)
+    stats, context, low = pl.pallas_call(
+        here(forward_kernel, count, True, tile),
+        out_shape=[stats_shape, wide_shape, low_shape],
+        in_specs=[VMEM] * (count + 1),
+        out_specs=[VMEM] * 3,
+        scratch_shapes=[natural(count), across(count, 16)],
+        compiler_params=compiler_params,
+        cost_estimate=cost(heads, count * rows, tokens, 2),
+        name="forward",
+    )(*group, qt)
+
+    group, count = groups[1], len(groups[1])
+    tile = tile_of(count * rows, tokens)
     final, context, grad_q, *grads = pl.pallas_call(
-        functools.partial(turn_kernel, count, tile_of(count * rows, tokens)),
+        here(turn_kernel, count, tile),
         out_shape=[stats_shape, wide_shape, wide_shape] + shapes_of(group),
         in_specs=[VMEM] * (count + 4),
         out_specs=[VMEM] * (count + 3),
@@ -398,35 +417,23 @@
         compiler_params=compiler_params,
         cost_estimate=cost(heads, count * rows, tokens, 6),
         name="turn",
-    )(*group, qt, gt, *state)
-    returned = [send_back(len(groups) - 1, grads)]
-
-    for i in reversed(range(len(groups) - 1)):
-        group, count = groups[i], len(groups[i])
-        first, last = i == len(groups) - 2, i == 0
-        back = sum((returned[k] for k in waits[i]), [])
-        operands = [*group, *kept[i], qt, gt, final, grad_q, *([context] if first else [])]
-        shapes = [rows_shape] * (first or last) + [wide_shape] * (not last)
-        outs = pl.pallas_call(
-            functools.partial(
-                backward_kernel, len(back), count, first, last, tile_of(count * rows, tokens)
-            ),
-            out_shape=shapes + shapes_of(group),
-            in_specs=[ANY] * len(back) + [VMEM] * len(operands),
-            out_specs=[VMEM] * (len(shapes) + count),
-            scratch_shapes=[natural(count), across(count), sums(count), sums(count)],
-            compiler_params=compiler_params,
-            cost_estimate=cost(heads, count * rows, tokens, 4),
-            name="backward",
-        )(*back, *operands)
-        if first:
-            context_rows = outs[0]
-        if last:
-            grad_query = outs[0]
-        else:
-            grad_q = outs[len(shapes) - 1]
-        returned.append(send_back(i, outs[len(shapes) :]))
-    return context_rows, grad_query
+    )(*group, qt, gt, stats, context)
+    back = send_back(1, grads)
+
+    group, count = groups[0], len(groups[0])
+    back = back if WAITS[parity] else []
+    grad_q, *grads = pl.pallas_call(
+        here(backward_kernel, len(back), count, tile_of(count * rows, tokens)),
+        out_shape=[wide_shape] + shapes_of(group),
+        in_specs=[ANY] * len(back) + [VMEM] * (count + 6),
+        out_specs=[VMEM] * (count + 1),
+        scratch_shapes=[natural(count), across(count), sums(count), sums(count)],
+        compiler_params=compiler_params,
+        cost_estimate=cost(heads, count * rows, tokens, 4),
+        name="backward",
+    )(*back, *group, low, stats, qt, gt, final, grad_q)
+    send_back(0, grads)
+    return context, grad_q
 
 
 def shards(pairs, queries, upstream):
@@ -434,24 +441,27 @@
     heads = queries.shape[2] // HEAD
     offsets = offset_groups()
     order = sum(offsets, [])
-    blocks = []
-    for offset, block in zip(order, pack(pairs, order, heads)):
-        block = block.reshape(heads, 2 * rows, HEAD)
-        blocks.append(lax.ppermute(block, AXES, route(offset, False)))
-    groups = []
-    for group in offsets:
-        groups.append(blocks[: len(group)])
-        blocks = blocks[len(group) :]
-    homes, returned = [], []
-
-    def send_back(i, grads):
-        back = [lax.ppermute(g, AXES, route(o, True)) for o, g in zip(offsets[i], grads)]
-        homes.extend(offsets[i])
-        returned.extend(b.reshape(heads, rows, 2, HEAD) for b in back)
-        return back
-
-    context, grad_query = attend(groups, queries, upstream, send_back)
-    return context, grad_query, unpack(returned, homes, width)
+    blocks = [b.reshape(heads, 2 * rows, HEAD) for b in pack(pairs, order, heads)]
+    qt, gt = turned(queries), turned(upstream)
+    arrived = []
+    for parity in range(2):
+        moved = [lax.ppermute(b, AXES, route(o, parity, False)) for o, b in zip(order, blocks)]
+        arrived.append([moved[: len(offsets[0])], moved[len(offsets[0]) :]])
+    results, returned = [], []
+    for parity in range(2):
+        parts = [None, None]
+
+        def send_back(i, grads):
+            parts[i] = [
+                lax.ppermute(g, AXES, route(o, parity, True)) for o, g in zip(offsets[i], grads)
+            ]
+            return parts[i]
+
+        results.append(attend(arrived[parity], qt, gt, 1 - parity, send_back))
+        returned += [b.reshape(heads, rows, 2, HEAD) for b in parts[0] + parts[1]]
+    context = turned_back([results[0][0], results[1][0]], queries.dtype)
+    grad_query = turned_back([results[0][1], results[1][1]], queries.dtype)
+    return context, grad_query, unpack(returned, order, width)
 
 
 def solution(mesh):

time: 70.7 us -> 107 us (1.51)
  the two profiles are of different devices: /device:TPU:21 before, /device:TPU:1 now
where the time goes in v13:
time: 107 us; the launch traced here: 106 us
  starting transfers between devices  63.8 us (60%)
  Pallas kernels  22.7 us (21%)
  waiting for transfers between devices  16.8 us (16%)
  between operations  1.3 us (1%)
  local copies, waits for them, and re-layouts  1.23 us (1%)
    ppermute x16, starting transfers between devices, send_back(): lax.ppermute(g, AXES, route(o, parity, True))  39.7 us
    ppermute x16, starting transfers between devices, shards(): lax.ppermute(b, AXES, route(o, parity, False))  24.1 us
    ppermute x16, waiting for transfers between devices, send_back(): lax.ppermute(g, AXES, route(o, parity, True))  10.6 us
    pallas_call x2, Pallas kernels, attend(): pl.pallas_call(here(turn_kernel, count, tile), out_shape=[stats_shape, wi...  8.33 us
    ppermute x16, waiting for transfers between devices, shards(): lax.ppermute(b, AXES, route(o, parity, False))  6.16 us
    pallas_call x2, Pallas kernels, attend(): pl.pallas_call(here(backward_kernel, len(back), count, tile_of(count * ro...  5.05 us
    pallas_call x2, Pallas kernels, attend(): pl.pallas_call(here(forward_kernel, count, True, tile), out_shape=[stats_...  3.88 us
    pallas_call x2, Pallas kernels, turned_back(): pl.pallas_call(kernel, out_shape=jax.ShapeDtypeStruct((1, tokens, heads *...  2.32 us
  transfers between devices with their start and end apart: 32, of which 8 were waited for; matrix products, arithmetic and copies ran while one was open for 0% of the time, Pallas kernels for 19%

profile of v13, /device:TPU:1, one launch (start us, length us, event | category | flops | bytes accessed | tf_op | source)
XLA Modules:
  0.0 105.8 jit_solution(6223312968022892532)
XLA Ops:
  0.6 1.2 %copy-done = bf16[1,128,2,2048]{3,2,1,0:T(2,128)(2,1)S(1)} copy-done((bf16[1,128,2,2048]{3,2,1,0:T(2,128)(2,1)S(1)}, bf16[1,128,2,2048]{3,2,1,0:T(2,128)(2,1)}, u32[]{:S(2)}) %copy-start) | copy-done | bytes 1048600
  1.9 1.0 pack.1
  2.8 1.3 %collective-permute-start.4 = (bf16[2,256,128]{2,1,0:T(8,128)(2,1)S(1)}, bf16[2,256,128]{2,1,0:T(8,128)(2,1)S(1)}, u32[]{:S(2)}, u32[]{:S(2)}) collective-permute-start(bf16[2,256,128]{2,1,0:T(8,128)(2,1)S(1)} %bitcast.54), channel_id=1, source_target_pairs={{0,9},{1,8},{2,11},{3,10},{4,13},{5,12},{6,15},{7,14},{16,25},{17,... | collective-permute-start | bytes 393224 | tf_op jit(solution)/shard_map/ppermute | solution.py:448
  4.1 1.3 %collective-permute-start.5 = (bf16[2,256,128]{2,1,0:T(8,128)(2,1)S(1)}, bf16[2,256,128]{2,1,0:T(8,128)(2,1)S(1)}, u32[]{:S(2)}, u32[]{:S(2)}) collective-permute-start(bf16[2,256,128]{2,1,0:T(8,128)(2,1)S(1)} %bitcast.52), channel_id=1, source_target_pairs={{0,11},{1,10},{2,13},{3,12},{4,15},{5,14},{6,9},{7,8},{16,27},{17,... | collective-permute-start | bytes 393224 | tf_op jit(solution)/shard_map/ppermute | solution.py:448
  5.4 1.3 %collective-permute-start.6 = (bf16[2,256,128]{2,1,0:T(8,128)(2,1)S(1)}, bf16[2,256,128]{2,1,0:T(8,128)(2,1)S(1)}, u32[]{:S(2)}, u32[]{:S(2)}) collective-permute-start(bf16[2,256,128]{2,1,0:T(8,128)(2,1)S(1)} %bitcast.50), channel_id=1, source_target_pairs={{0,15},{1,14},{2,9},{3,8},{4,11},{5,10},{6,13},{7,12},{16,31},{17,... | collective-permute-start | bytes 393224 | tf_op jit(solution)/shard_map/ppermute | solution.py:448
  6.7 1.3 %collective-permute-start.7 = (bf16[2,256,128]{2,1,0:T(8,128)(2,1)S(1)}, bf16[2,256,128]{2,1,0:T(8,128)(2,1)S(1)}, u32[]{:S(2)}, u32[]{:S(2)}) collective-permute-start(bf16[2,256,128]{2,1,0:T(8,128)(2,1)S(1)} %bitcast.48), channel_id=1, source_target_pairs={{0,13},{1,12},{2,15},{3,14},{4,9},{5,8},{6,11},{7,10},{16,29},{17,... | collective-permute-start | bytes 393224 | tf_op jit(solution)/shard_map/ppermute | solution.py:448
  8.0 1.3 %collective-permute-start.1 = (bf16[2,256,128]{2,1,0:T(8,128)(2,1)S(1)}, bf16[2,256,128]{2,1,0:T(8,128)(2,1)S(1)}, u32[]{:S(2)}, u32[]{:S(2)}) collective-permute-start(bf16[2,256,128]{2,1,0:T(8,128)(2,1)S(1)} %bitcast.46), channel_id=1, source_target_pairs={{0,10},{1,11},{2,12},{3,13},{4,14},{5,15},{6,8},{7,9},{16,26},{17,... | collective-permute-start | bytes 393224 | tf_op jit(solution)/shard_map/ppermute | solution.py:448
  9.3 0.1 collective-permute-done.4.refs_0_
  9.4 1.3 %collective-permute-start = (bf16[2,256,128]{2,1,0:T(8,128)(2,1)S(1)}, bf16[2,256,128]{2,1,0:T(8,128)(2,1)S(1)}, u32[]{:S(2)}, u32[]{:S(2)}) collective-permute-start(bf16[2,256,128]{2,1,0:T(8,128)(2,1)S(1)} %bitcast.44), channel_id=1, source_target_pairs={{0,8},{1,9},{2,10},{3,11},{4,12},{5,13},{6,14},{7,15},{16,24},{17,... | collective-permute-start | bytes 393224 | tf_op jit(solution)/shard_map/ppermute | solution.py:448
  10.7 3.7 %collective-permute-done.5.refs_1_ = bf16[2,256,128]{2,1,0:T(8,128)(2,1)S(1)} collective-permute-done((bf16[2,256,128]{2,1,0:T(8,128)(2,1)S(1)}, bf16[2,256,128]{2,1,0:T(8,128)(2,1)S(1)}, u32[]{:S(2)}, u32[]{:S(2)}) %collective-permute-start.5) | collective-permute-done | bytes 131104 | tf_op jit(solution)/shard_map/ppermute | solution.py:448
  14.4 1.3 %collective-permute-start.2 = (bf16[2,256,128]{2,1,0:T(8,128)(2,1)S(1)}, bf16[2,256,128]{2,1,0:T(8,128)(2,1)S(1)}, u32[]{:S(2)}, u32[]{:S(2)}) collective-permute-start(bf16[2,256,128]{2,1,0:T(8,128)(2,1)S(1)} %bitcast.42), channel_id=1, source_target_pairs={{0,14},{1,15},{2,8},{3,9},{4,10},{5,11},{6,12},{7,13},{16,30},{17,... | collective-permute-start | bytes 393224 | tf_op jit(solution)/shard_map/ppermute | solution.py:448
  15.7 0.0 collective-permute-done.6.refs_2_
  15.7 1.3 %collective-permute-start.3 = (bf16[2,256,128]{2,1,0:T(8,128)(2,1)S(1)}, bf16[2,256,128]{2,1,0:T(8,128)(2,1)S(1)}, u32[]{:S(2)}, u32[]{:S(2)}) collective-permute-start(bf16[2,256,128]{2,1,0:T(8,128)(2,1)S(1)} %bitcast.40), channel_id=1, source_target_pairs={{0,12},{1,13},{2,14},{3,15},{4,8},{5,9},{6,10},{7,11},{16,28},{17,... | collective-permute-start | bytes 393224 | tf_op jit(solution)/shard_map/ppermute | solution.py:448
  17.0 0.3 turned.2.refs_4_.refs_6_
  17.3 0.3 turned.3.refs_5_.refs_7_
  17.6 2.3 %collective-permute-done.7.refs_3_ = bf16[2,256,128]{2,1,0:T(8,128)(2,1)S(1)} collective-permute-done((bf16[2,256,128]{2,1,0:T(8,128)(2,1)S(1)}, bf16[2,256,128]{2,1,0:T(8,128)(2,1)S(1)}, u32[]{:S(2)}, u32[]{:S(2)}) %collective-permute-start.7) | collective-permute-done | bytes 131104 | tf_op jit(solution)/shard_map/ppermute | solution.py:448
  19.9 4.7 %collective-permute-start.9 = (bf16[2,256,128]{2,1,0:T(8,128)(2,1)S(1)}, bf16[2,256,128]{2,1,0:T(8,128)(2,1)S(1)}, u32[]{:S(2)}, u32[]{:S(2)}) collective-permute-start(bf16[2,256,128]{2,1,0:T(8,128)(2,1)S(1)} %bitcast.47), channel_id=1, source_target_pairs={{8,18},{9,19},{10,20},{11,21},{12,22},{13,23},{14,16},{15,17},{24,... | collective-permute-start | bytes 393224 | tf_op jit(solution)/shard_map/ppermute | solution.py:448
  24.6 3.9 %forward.2 = (f32[2,8,1536]{2,1,0:T(8,128)S(1)}, f32[2,128,1536]{2,1,0:T(8,128)S(1)}, bf16[2,512,1536]{2,1,0:T(8,128)(2,1)S(1)}) custom-call(bf16[2,256,128]{2,1,0:T(8,128)(2,1)S(1)} %collective-permute-done.4.refs_0_, bf16[2,256,128]{2,1,0:T(8,128)(2,1)S(1)} %collective-permute-done.5.refs_1_, bf16[2,256,128]{2,1,0:T(8,128)(2,1)S(1)} %collective-permute-done.6.refs_2_, ...), custom_call_target="tpu_custom_call" | custom-call | flops 805306368 | bytes 4194304 | tf_op jit(solution)/shard_map/forward/pallas_call | solution.py:397
  28.5 0.0 collective-permute-done.1.refs_1_
  28.5 1.3 %collective-permute-start.8 = (bf16[2,256,128]{2,1,0:T(8,128)(2,1)S(1)}, bf16[2,256,128]{2,1,0:T(8,128)(2,1)S(1)}, u32[]{:S(2)}, u32[]{:S(2)}) collective-permute-start(bf16[2,256,128]{2,1,0:T(8,128)(2,1)S(1)} %bitcast.45), channel_id=1, source_target_pairs={{8,16},{9,17},{10,18},{11,19},{12,20},{13,21},{14,22},{15,23},{24,... | collective-permute-start | bytes 393224 | tf_op jit(solution)/shard_map/ppermute | solution.py:448
  29.8 1.3 %collective-permute-start.12 = (bf16[2,256,128]{2,1,0:T(8,128)(2,1)S(1)}, bf16[2,256,128]{2,1,0:T(8,128)(2,1)S(1)}, u32[]{:S(2)}, u32[]{:S(2)}) collective-permute-start(bf16[2,256,128]{2,1,0:T(8,128)(2,1)S(1)} %bitcast.55), channel_id=1, source_target_pairs={{8,17},{9,16},{10,19},{11,18},{12,21},{13,20},{14,23},{15,22},{24,... | collective-permute-start | bytes 393224 | tf_op jit(solution)/shard_map/ppermute | solution.py:448
  31.1 0.0 collective-permute-done.2.refs_2_
  31.2 1.3 %collective-permute-start.13 = (bf16[2,256,128]{2,1,0:T(8,128)(2,1)S(1)}, bf16[2,256,128]{2,1,0:T(8,128)(2,1)S(1)}, u32[]{:S(2)}, u32[]{:S(2)}) collective-permute-start(bf16[2,256,128]{2,1,0:T(8,128)(2,1)S(1)} %bitcast.53), channel_id=1, source_target_pairs={{8,19},{9,18},{10,21},{11,20},{12,23},{13,22},{14,17},{15,16},{24,... | collective-permute-start | bytes 393224 | tf_op jit(solution)/shard_map/ppermute | solution.py:448
  32.5 1.3 %collective-permute-start.14 = (bf16[2,256,128]{2,1,0:T(8,128)(2,1)S(1)}, bf16[2,256,128]{2,1,0:T(8,128)(2,1)S(1)}, u32[]{:S(2)}, u32[]{:S(2)}) collective-permute-start(bf16[2,256,128]{2,1,0:T(8,128)(2,1)S(1)} %bitcast.51), channel_id=1, source_target_pairs={{8,23},{9,22},{10,17},{11,16},{12,19},{13,18},{14,21},{15,20},{24,... | collective-permute-start | bytes 393224 | tf_op jit(solution)/shard_map/ppermute | solution.py:448
  33.8 8.1 %turn.2 = (f32[2,8,1536]{2,1,0:T(8,128)S(1)}, f32[2,128,1536]{2,1,0:T(8,128)S(1)}, f32[2,128,1536]{2,1,0:T(8,128)S(1)}, bf16[2,256,128]{2,1,0:T(8,128)(2,1)S(1)}...) custom-call(bf16[2,256,128]{2,1,0:T(8,128)(2,1)S(1)} %collective-permute-done., ...), custom_call_target="tpu_custom_call" | custom-call | flops 2415919104 | bytes 4194304 | tf_op jit(solution)/shard_map/turn/pallas_call | solution.py:410
  41.9 1.3 %collective-permute-start.10 = (bf16[2,256,128]{2,1,0:T(8,128)(2,1)S(1)}, bf16[2,256,128]{2,1,0:T(8,128)(2,1)S(1)}, u32[]{:S(2)}, u32[]{:S(2)}) collective-permute-start(bf16[2,256,128]{2,1,0:T(8,128)(2,1)S(1)} %bitcast.43), channel_id=1, source_target_pairs={{8,22},{9,23},{10,16},{11,17},{12,18},{13,19},{14,20},{15,21},{24,... | collective-permute-start | bytes 393224 | tf_op jit(solution)/shard_map/ppermute | solution.py:448
  43.2 0.0 collective-permute-done.13.refs_1_
  43.2 1.3 %collective-permute-start.11 = (bf16[2,256,128]{2,1,0:T(8,128)(2,1)S(1)}, bf16[2,256,128]{2,1,0:T(8,128)(2,1)S(1)}, u32[]{:S(2)}, u32[]{:S(2)}) collective-permute-start(bf16[2,256,128]{2,1,0:T(8,128)(2,1)S(1)} %bitcast.41), channel_id=1, source_target_pairs={{8,20},{9,21},{10,22},{11,23},{12,16},{13,17},{14,18},{15,19},{24,... | collective-permute-start | bytes 393224 | tf_op jit(solution)/shard_map/ppermute | solution.py:448
  44.6 1.3 %collective-permute-start.15 = (bf16[2,256,128]{2,1,0:T(8,128)(2,1)S(1)}, bf16[2,256,128]{2,1,0:T(8,128)(2,1)S(1)}, u32[]{:S(2)}, u32[]{:S(2)}) collective-permute-start(bf16[2,256,128]{2,1,0:T(8,128)(2,1)S(1)} %bitcast.49), channel_id=1, source_target_pairs={{8,21},{9,20},{10,23},{11,22},{12,17},{13,16},{14,19},{15,18},{24,... | collective-permute-start | bytes 393224 | tf_op jit(solution)/shard_map/ppermute | solution.py:448
  45.9 5.0 %backward.2 = (f32[2,128,1536]{2,1,0:T(8,128)S(1)}, bf16[2,256,128]{2,1,0:T(8,128)(2,1)S(1)}, bf16[2,256,128]{2,1,0:T(8,128)(2,1)S(1)}, bf16[2,256,128]{2,1,0:T(8,128)(2,1)S(1)}, bf16[2,256,128]{2,1,0:T(8,128)(2,1)S(1)}) custom-call(bf16[2,256,128]{2,1,0:T(8,128)(2,1)S(1)} %collective-permute-done.4.refs_0_, ...), custom_call_target="tpu_custom_call" | custom-call | flops 1610612736 | bytes 4194304 | tf_op jit(solution)/shard_map/backward/pallas_call | solution.py:425
  50.9 3.2 %collective-permute-start.16 = (bf16[2,256,128]{2,1,0:T(8,128)(2,1)S(1)}, bf16[2,256,128]{2,1,0:T(8,128)(2,1)S(1)}, u32[]{:S(2)}, u32[]{:S(2)}) collective-permute-start(bf16[2,256,128]{2,1,0:T(8,128)(2,1)S(1)} %get-tuple-element.63), channel_id=1, source_target_pairs={{9,0},{8,1},{11,2},{10,3},{13,4},{12,5},{15,6},{14,7},{25,16},{24,... | collective-permute-start | bytes 393224 | tf_op jit(solution)/shard_map/ppermute | solution.py:456
  54.2 0.0 collective-permute-done.9.refs_1_
  54.2 8.3 %collective-permute-start.17 = (bf16[2,256,128]{2,1,0:T(8,128)(2,1)S(1)}, bf16[2,256,128]{2,1,0:T(8,128)(2,1)S(1)}, u32[]{:S(2)}, u32[]{:S(2)}) collective-permute-start(bf16[2,256,128]{2,1,0:T(8,128)(2,1)S(1)} %get-tuple-element.64), channel_id=1, source_target_pairs={{11,0},{10,1},{13,2},{12,3},{15,4},{14,5},{9,6},{8,7},{27,16},{26,... | collective-permute-start | bytes 393224 | tf_op jit(solution)/shard_map/ppermute | solution.py:456
  62.5 0.0 collective-permute-done.8.refs_0_
  62.5 1.3 %collective-permute-start.18 = (bf16[2,256,128]{2,1,0:T(8,128)(2,1)S(1)}, bf16[2,256,128]{2,1,0:T(8,128)(2,1)S(1)}, u32[]{:S(2)}, u32[]{:S(2)}) collective-permute-start(bf16[2,256,128]{2,1,0:T(8,128)(2,1)S(1)} %get-tuple-element.65), channel_id=1, source_target_pairs={{15,0},{14,1},{9,2},{8,3},{11,4},{10,5},{13,6},{12,7},{31,16},{30,... | collective-permute-start | bytes 393224 | tf_op jit(solution)/shard_map/ppermute | solution.py:456
  63.8 1.3 %collective-permute-start.19 = (bf16[2,256,128]{2,1,0:T(8,128)(2,1)S(1)}, bf16[2,256,128]{2,1,0:T(8,128)(2,1)S(1)}, u32[]{:S(2)}, u32[]{:S(2)}) collective-permute-start(bf16[2,256,128]{2,1,0:T(8,128)(2,1)S(1)} %get-tuple-element.66), channel_id=1, source_target_pairs={{13,0},{12,1},{15,2},{14,3},{9,4},{8,5},{11,6},{10,7},{29,16},{28,... | collective-permute-start | bytes 393224 | tf_op jit(solution)/shard_map/ppermute | solution.py:456
  65.1 0.0 collective-permute-done.11.refs_3_
  65.1 1.3 %collective-permute-start.20 = (bf16[2,256,128]{2,1,0:T(8,128)(2,1)S(1)}, bf16[2,256,128]{2,1,0:T(8,128)(2,1)S(1)}, u32[]{:S(2)}, u32[]{:S(2)}) collective-permute-start(bf16[2,256,128]{2,1,0:T(8,128)(2,1)S(1)} %get-tuple-element.67), channel_id=1, source_target_pairs={{8,0},{9,1},{10,2},{11,3},{12,4},{13,5},{14,6},{15,7},{24,16},{25,... | collective-permute-start | bytes 393224 | tf_op jit(solution)/shard_map/ppermute | solution.py:456
  66.4 0.2 turn.3
  66.6 9.4 %collective-permute-start.21 = (bf16[2,256,128]{2,1,0:T(8,128)(2,1)S(1)}, bf16[2,256,128]{2,1,0:T(8,128)(2,1)S(1)}, u32[]{:S(2)}, u32[]{:S(2)}) collective-permute-start(bf16[2,256,128]{2,1,0:T(8,128)(2,1)S(1)} %get-tuple-element.68), channel_id=1, source_target_pairs={{10,0},{11,1},{12,2},{13,3},{14,4},{15,5},{8,6},{9,7},{26,16},{27,... | collective-permute-start | bytes 393224 | tf_op jit(solution)/shard_map/ppermute | solution.py:456
  76.1 0.0 collective-permute-done.17
  76.1 2.2 %collective-permute-start.22 = (bf16[2,256,128]{2,1,0:T(8,128)(2,1)S(1)}, bf16[2,256,128]{2,1,0:T(8,128)(2,1)S(1)}, u32[]{:S(2)}, u32[]{:S(2)}) collective-permute-start(bf16[2,256,128]{2,1,0:T(8,128)(2,1)S(1)} %get-tuple-element.69), channel_id=1, source_target_pairs={{14,0},{15,1},{8,2},{9,3},{10,4},{11,5},{12,6},{13,7},{30,16},{31,... | collective-permute-start | bytes 393224 | tf_op jit(solution)/shard_map/ppermute | solution.py:456
  78.3 0.0 collective-permute-done.18
  78.3 2.3 %collective-permute-start.23 = (bf16[2,256,128]{2,1,0:T(8,128)(2,1)S(1)}, bf16[2,256,128]{2,1,0:T(8,128)(2,1)S(1)}, u32[]{:S(2)}, u32[]{:S(2)}) collective-permute-start(bf16[2,256,128]{2,1,0:T(8,128)(2,1)S(1)} %get-tuple-element.70), channel_id=1, source_target_pairs={{12,0},{13,1},{14,2},{15,3},{8,4},{9,5},{10,6},{11,7},{28,16},{29,... | collective-permute-start | bytes 393224 | tf_op jit(solution)/shard_map/ppermute | solution.py:456
  80.7 0.0 collective-permute-done.19
  80.7 1.3 %collective-permute-start.24 = (bf16[2,256,128]{2,1,0:T(8,128)(2,1)S(1)}, bf16[2,256,128]{2,1,0:T(8,128)(2,1)S(1)}, u32[]{:S(2)}, u32[]{:S(2)}) collective-permute-start(bf16[2,256,128]{2,1,0:T(8,128)(2,1)S(1)} %get-tuple-element.71), channel_id=1, source_target_pairs={{17,8},{16,9},{19,10},{18,11},{21,12},{20,13},{23,14},{22,15},{1,2... | collective-permute-start | bytes 393224 | tf_op jit(solution)/shard_map/ppermute | solution.py:456
  82.0 0.0 collective-permute-done.20
  82.0 1.3 %collective-permute-start.25 = (bf16[2,256,128]{2,1,0:T(8,128)(2,1)S(1)}, bf16[2,256,128]{2,1,0:T(8,128)(2,1)S(1)}, u32[]{:S(2)}, u32[]{:S(2)}) collective-permute-start(bf16[2,256,128]{2,1,0:T(8,128)(2,1)S(1)} %get-tuple-element.72), channel_id=1, source_target_pairs={{19,8},{18,9},{21,10},{20,11},{23,12},{22,13},{17,14},{16,15},{3,2... | collective-permute-start | bytes 393224 | tf_op jit(solution)/shard_map/ppermute | solution.py:456
  83.3 1.3 %collective-permute-start.26 = (bf16[2,256,128]{2,1,0:T(8,128)(2,1)S(1)}, bf16[2,256,128]{2,1,0:T(8,128)(2,1)S(1)}, u32[]{:S(2)}, u32[]{:S(2)}) collective-permute-start(bf16[2,256,128]{2,1,0:T(8,128)(2,1)S(1)} %get-tuple-element.73), channel_id=1, source_target_pairs={{23,8},{22,9},{17,10},{16,11},{19,12},{18,13},{21,14},{20,15},{7,2... | collective-permute-start | bytes 393224 | tf_op jit(solution)/shard_map/ppermute | solution.py:456
  84.6 0.0 collective-permute-done.22
  84.6 1.3 %collective-permute-start.27 = (bf16[2,256,128]{2,1,0:T(8,128)(2,1)S(1)}, bf16[2,256,128]{2,1,0:T(8,128)(2,1)S(1)}, u32[]{:S(2)}, u32[]{:S(2)}) collective-permute-start(bf16[2,256,128]{2,1,0:T(8,128)(2,1)S(1)} %get-tuple-element.74), channel_id=1, source_target_pairs={{21,8},{20,9},{23,10},{22,11},{17,12},{16,13},{19,14},{18,15},{5,2... | collective-permute-start | bytes 393224 | tf_op jit(solution)/shard_map/ppermute | solution.py:456
  85.9 0.0 collective-permute-done.23
  85.9 1.3 %collective-permute-start.28 = (bf16[2,256,128]{2,1,0:T(8,128)(2,1)S(1)}, bf16[2,256,128]{2,1,0:T(8,128)(2,1)S(1)}, u32[]{:S(2)}, u32[]{:S(2)}) collective-permute-start(bf16[2,256,128]{2,1,0:T(8,128)(2,1)S(1)} %get-tuple-element.75), channel_id=1, source_target_pairs={{16,8},{17,9},{18,10},{19,11},{20,12},{21,13},{22,14},{23,15},{0,2... | collective-permute-start | bytes 393224 | tf_op jit(solution)/shard_map/ppermute | solution.py:456
  87.2 0.6 collective-permute-done.24
  87.9 1.3 %collective-permute-start.29 = (bf16[2,256,128]{2,1,0:T(8,128)(2,1)S(1)}, bf16[2,256,128]{2,1,0:T(8,128)(2,1)S(1)}, u32[]{:S(2)}, u32[]{:S(2)}) collective-permute-start(bf16[2,256,128]{2,1,0:T(8,128)(2,1)S(1)} %get-tuple-element.76), channel_id=1, source_target_pairs={{18,8},{19,9},{20,10},{21,11},{22,12},{23,13},{16,14},{17,15},{2,2... | collective-permute-start | bytes 393224 | tf_op jit(solution)/shard_map/ppermute | solution.py:456
  89.2 3.1 %collective-permute-done.25 = bf16[2,256,128]{2,1,0:T(8,128)(2,1)S(1)} collective-permute-done((bf16[2,256,128]{2,1,0:T(8,128)(2,1)S(1)}, bf16[2,256,128]{2,1,0:T(8,128)(2,1)S(1)}, u32[]{:S(2)}, u32[]{:S(2)}) %collective-permute-start.25) | collective-permute-done | bytes 131104 | tf_op jit(solution)/shard_map/ppermute | solution.py:456
  92.3 1.3 %collective-permute-start.30 = (bf16[2,256,128]{2,1,0:T(8,128)(2,1)S(1)}, bf16[2,256,128]{2,1,0:T(8,128)(2,1)S(1)}, u32[]{:S(2)}, u32[]{:S(2)}) collective-permute-start(bf16[2,256,128]{2,1,0:T(8,128)(2,1)S(1)} %get-tuple-element.77), channel_id=1, source_target_pairs={{22,8},{23,9},{16,10},{17,11},{18,12},{19,13},{20,14},{21,15},{6,2... | collective-permute-start | bytes 393224 | tf_op jit(solution)/shard_map/ppermute | solution.py:456
  93.5 1.0 collective-permute-done.26
  94.6 1.3 %collective-permute-start.31 = (bf16[2,256,128]{2,1,0:T(8,128)(2,1)S(1)}, bf16[2,256,128]{2,1,0:T(8,128)(2,1)S(1)}, u32[]{:S(2)}, u32[]{:S(2)}) collective-permute-start(bf16[2,256,128]{2,1,0:T(8,128)(2,1)S(1)} %get-tuple-element.78), channel_id=1, source_target_pairs={{20,8},{21,9},{22,10},{23,11},{16,12},{17,13},{18,14},{19,15},{4,2... | collective-permute-start | bytes 393224 | tf_op jit(solution)/shard_map/ppermute | solution.py:456
  95.9 1.2 %turned_back.2 = bf16[1,1536,256]{2,1,0:T(8,128)(2,1)} custom-call(f32[2,128,1536]{2,1,0:T(8,128)S(1)} %get-tuple-element.51.refs_0_, f32[2,128,1536]{2,1,0:T(8,128)S(1)} %get-tuple-element.54.refs_1_), custom_call_target="tpu_custom_call" | custom-call | tf_op jit(solution)/shard_map/turned_back/pallas_call | solution.py:152
  97.0 1.2 %turned_back.3 = bf16[1,1536,256]{2,1,0:T(8,128)(2,1)} custom-call(f32[2,128,1536]{2,1,0:T(8,128)S(1)} %get-tuple-element.58.refs_0_, f32[2,128,1536]{2,1,0:T(8,128)S(1)} %get-tuple-element.62.refs_1_), custom_call_target="tpu_custom_call" | custom-call | tf_op jit(solution)/shard_map/turned_back/pallas_call | solution.py:152
  98.2 3.0 %collective-permute-done.30 = bf16[2,256,128]{2,1,0:T(8,128)(2,1)S(1)} collective-permute-done((bf16[2,256,128]{2,1,0:T(8,128)(2,1)S(1)}, bf16[2,256,128]{2,1,0:T(8,128)(2,1)S(1)}, u32[]{:S(2)}, u32[]{:S(2)}) %collective-permute-start.30) | collective-permute-done | bytes 131104 | tf_op jit(solution)/shard_map/ppermute | solution.py:456
  101.2 2.8 %collective-permute-done.31 = bf16[2,256,128]{2,1,0:T(8,128)(2,1)S(1)} collective-permute-done((bf16[2,256,128]{2,1,0:T(8,128)(2,1)S(1)}, bf16[2,256,128]{2,1,0:T(8,128)(2,1)S(1)}, u32[]{:S(2)}, u32[]{:S(2)}) %collective-permute-start.31) | collective-permute-done | bytes 131104 | tf_op jit(solution)/shard_map/ppermute | solution.py:456
  104.0 1.6 %unpack.1 = bf16[1,128,2,2048]{3,2,1,0:T(2,128)(2,1)} custom-call(bf16[2,128,2,128]{3,2,1,0:T(2,128)(2,1)S(1)} %bitcast.24, bf16[2,128,2,128]{3,2,1,0:T(2,128)(2,1)S(1)} %bitcast.25, bf16[2,128,2,128]{3,2,1,0:T(2,128)(2,1)S(1)} %bitcast.26, bf16[2,128,2,128]{3,2,1,0:T(2,128)(2,1)S(1)} %bitcast.27, bf16[2,128,2,128]{3,2,1,0:T(2,128)(2,1)S(1)} %bitcast.28, ...), custom_call_target="tpu_custom_call" | custom-call | tf_op jit(solution)/shard_map/unpack/pallas_call | solution.py:122
  (18 shorter events, 0.1 us)
Async XLA Ops:
  0.6 1.2 %copy-start = (bf16[1,128,2,2048]{3,2,1,0:T(2,128)(2,1)S(1)}, bf16[1,128,2,2048]{3,2,1,0:T(2,128)(2,1)}, u32[]{:S(2)}) copy-start(bf16[1,128,2,2048]{3,2,1,0:T(2,128)(2,1)} %pairs_ref.1) | copy-start | bytes 3145732
  1.9 15.1 %copy-start.1 = (bf16[1,1536,256]{2,1,0:T(8,128)(2,1)S(1)}, bf16[1,1536,256]{2,1,0:T(8,128)(2,1)}, u32[]{:S(2)}) copy-start(bf16[1,1536,256]{2,1,0:T(8,128)(2,1)} %rows_ref.2) | copy-start | bytes 2359300
  1.9 15.4 %copy-start.2 = (bf16[1,1536,256]{2,1,0:T(8,128)(2,1)S(1)}, bf16[1,1536,256]{2,1,0:T(8,128)(2,1)}, u32[]{:S(2)}) copy-start(bf16[1,1536,256]{2,1,0:T(8,128)(2,1)} %rows_ref.3) | copy-start | bytes 2359300
  2.8 6.6 %collective-permute-start.4 = (bf16[2,256,128]{2,1,0:T(8,128)(2,1)S(1)}, bf16[2,256,128]{2,1,0:T(8,128)(2,1)S(1)}, u32[]{:S(2)}, u32[]{:S(2)}) collective-permute-start(bf16[2,256,128]{2,1,0:T(8,128)(2,1)S(1)} %bitcast.54), channel_id=1, source_target_pairs={{0,9},{1,8},{2,11},{3,10},{4,13},{5,12},{6,15},{7,14},{16,25},{17,... | collective-permute-start | bytes 393224 | tf_op jit(solution)/shard_map/ppermute | solution.py:448
  4.1 10.3 %collective-permute-start.5 = (bf16[2,256,128]{2,1,0:T(8,128)(2,1)S(1)}, bf16[2,256,128]{2,1,0:T(8,128)(2,1)S(1)}, u32[]{:S(2)}, u32[]{:S(2)}) collective-permute-start(bf16[2,256,128]{2,1,0:T(8,128)(2,1)S(1)} %bitcast.52), channel_id=1, source_target_pairs={{0,11},{1,10},{2,13},{3,12},{4,15},{5,14},{6,9},{7,8},{16,27},{17,... | collective-permute-start | bytes 393224 | tf_op jit(solution)/shard_map/ppermute | solution.py:448
  5.4 10.3 %collective-permute-start.6 = (bf16[2,256,128]{2,1,0:T(8,128)(2,1)S(1)}, bf16[2,256,128]{2,1,0:T(8,128)(2,1)S(1)}, u32[]{:S(2)}, u32[]{:S(2)}) collective-permute-start(bf16[2,256,128]{2,1,0:T(8,128)(2,1)S(1)} %bitcast.50), channel_id=1, source_target_pairs={{0,15},{1,14},{2,9},{3,8},{4,11},{5,10},{6,13},{7,12},{16,31},{17,... | collective-permute-start | bytes 393224 | tf_op jit(solution)/shard_map/ppermute | solution.py:448
  6.7 13.2 %collective-permute-start.7 = (bf16[2,256,128]{2,1,0:T(8,128)(2,1)S(1)}, bf16[2,256,128]{2,1,0:T(8,128)(2,1)S(1)}, u32[]{:S(2)}, u32[]{:S(2)}) collective-permute-start(bf16[2,256,128]{2,1,0:T(8,128)(2,1)S(1)} %bitcast.48), channel_id=1, source_target_pairs={{0,13},{1,12},{2,15},{3,14},{4,9},{5,8},{6,11},{7,10},{16,29},{17,... | collective-permute-start | bytes 393224 | tf_op jit(solution)/shard_map/ppermute | solution.py:448
  8.0 20.5 %collective-permute-start.1 = (bf16[2,256,128]{2,1,0:T(8,128)(2,1)S(1)}, bf16[2,256,128]{2,1,0:T(8,128)(2,1)S(1)}, u32[]{:S(2)}, u32[]{:S(2)}) collective-permute-start(bf16[2,256,128]{2,1,0:T(8,128)(2,1)S(1)} %bitcast.46), channel_id=1, source_target_pairs={{0,10},{1,11},{2,12},{3,13},{4,14},{5,15},{6,8},{7,9},{16,26},{17,... | collective-permute-start | bytes 393224 | tf_op jit(solution)/shard_map/ppermute | solution.py:448
  9.4 20.4 %collective-permute-start = (bf16[2,256,128]{2,1,0:T(8,128)(2,1)S(1)}, bf16[2,256,128]{2,1,0:T(8,128)(2,1)S(1)}, u32[]{:S(2)}, u32[]{:S(2)}) collective-permute-start(bf16[2,256,128]{2,1,0:T(8,128)(2,1)S(1)} %bitcast.44), channel_id=1, source_target_pairs={{0,8},{1,9},{2,10},{3,11},{4,12},{5,13},{6,14},{7,15},{16,24},{17,... | collective-permute-start | bytes 393224 | tf_op jit(solution)/shard_map/ppermute | solution.py:448
  14.4 16.8 %collective-permute-start.2 = (bf16[2,256,128]{2,1,0:T(8,128)(2,1)S(1)}, bf16[2,256,128]{2,1,0:T(8,128)(2,1)S(1)}, u32[]{:S(2)}, u32[]{:S(2)}) collective-permute-start(bf16[2,256,128]{2,1,0:T(8,128)(2,1)S(1)} %bitcast.42), channel_id=1, source_target_pairs={{0,14},{1,15},{2,8},{3,9},{4,10},{5,11},{6,12},{7,13},{16,30},{17,... | collective-permute-start | bytes 393224 | tf_op jit(solution)/shard_map/ppermute | solution.py:448
  15.7 16.8 %collective-permute-start.3 = (bf16[2,256,128]{2,1,0:T(8,128)(2,1)S(1)}, bf16[2,256,128]{2,1,0:T(8,128)(2,1)S(1)}, u32[]{:S(2)}, u32[]{:S(2)}) collective-permute-start(bf16[2,256,128]{2,1,0:T(8,128)(2,1)S(1)} %bitcast.40), channel_id=1, source_target_pairs={{0,12},{1,13},{2,14},{3,15},{4,8},{5,9},{6,10},{7,11},{16,28},{17,... | collective-permute-start | bytes 393224 | tf_op jit(solution)/shard_map/ppermute | solution.py:448
  19.9 34.3 %collective-permute-start.9 = (bf16[2,256,128]{2,1,0:T(8,128)(2,1)S(1)}, bf16[2,256,128]{2,1,0:T(8,128)(2,1)S(1)}, u32[]{:S(2)}, u32[]{:S(2)}) collective-permute-start(bf16[2,256,128]{2,1,0:T(8,128)(2,1)S(1)} %bitcast.47), channel_id=1, source_target_pairs={{8,18},{9,19},{10,20},{11,21},{12,22},{13,23},{14,16},{15,17},{24,... | collective-permute-start | bytes 393224 | tf_op jit(solution)/shard_map/ppermute | solution.py:448
  28.5 33.9 %collective-permute-start.8 = (bf16[2,256,128]{2,1,0:T(8,128)(2,1)S(1)}, bf16[2,256,128]{2,1,0:T(8,128)(2,1)S(1)}, u32[]{:S(2)}, u32[]{:S(2)}) collective-permute-start(bf16[2,256,128]{2,1,0:T(8,128)(2,1)S(1)} %bitcast.45), channel_id=1, source_target_pairs={{8,16},{9,17},{10,18},{11,19},{12,20},{13,21},{14,22},{15,23},{24,... | collective-permute-start | bytes 393224 | tf_op jit(solution)/shard_map/ppermute | solution.py:448
  29.8 12.1 %collective-permute-start.12 = (bf16[2,256,128]{2,1,0:T(8,128)(2,1)S(1)}, bf16[2,256,128]{2,1,0:T(8,128)(2,1)S(1)}, u32[]{:S(2)}, u32[]{:S(2)}) collective-permute-start(bf16[2,256,128]{2,1,0:T(8,128)(2,1)S(1)} %bitcast.55), channel_id=1, source_target_pairs={{8,17},{9,16},{10,19},{11,18},{12,21},{13,20},{14,23},{15,22},{24,... | collective-permute-start | bytes 393224 | tf_op jit(solution)/shard_map/ppermute | solution.py:448
  31.2 12.1 %collective-permute-start.13 = (bf16[2,256,128]{2,1,0:T(8,128)(2,1)S(1)}, bf16[2,256,128]{2,1,0:T(8,128)(2,1)S(1)}, u32[]{:S(2)}, u32[]{:S(2)}) collective-permute-start(bf16[2,256,128]{2,1,0:T(8,128)(2,1)S(1)} %bitcast.53), channel_id=1, source_target_pairs={{8,19},{9,18},{10,21},{11,20},{12,23},{13,22},{14,17},{15,16},{24,... | collective-permute-start | bytes 393224 | tf_op jit(solution)/shard_map/ppermute | solution.py:448
  32.5 12.1 %collective-permute-start.14 = (bf16[2,256,128]{2,1,0:T(8,128)(2,1)S(1)}, bf16[2,256,128]{2,1,0:T(8,128)(2,1)S(1)}, u32[]{:S(2)}, u32[]{:S(2)}) collective-permute-start(bf16[2,256,128]{2,1,0:T(8,128)(2,1)S(1)} %bitcast.51), channel_id=1, source_target_pairs={{8,23},{9,22},{10,17},{11,16},{12,19},{13,18},{14,21},{15,20},{24,... | collective-permute-start | bytes 393224 | tf_op jit(solution)/shard_map/ppermute | solution.py:448
  41.9 21.9 %collective-permute-start.10 = (bf16[2,256,128]{2,1,0:T(8,128)(2,1)S(1)}, bf16[2,256,128]{2,1,0:T(8,128)(2,1)S(1)}, u32[]{:S(2)}, u32[]{:S(2)}) collective-permute-start(bf16[2,256,128]{2,1,0:T(8,128)(2,1)S(1)} %bitcast.43), channel_id=1, source_target_pairs={{8,22},{9,23},{10,16},{11,17},{12,18},{13,19},{14,20},{15,21},{24,... | collective-permute-start | bytes 393224 | tf_op jit(solution)/shard_map/ppermute | solution.py:448
  43.2 21.9 %collective-permute-start.11 = (bf16[2,256,128]{2,1,0:T(8,128)(2,1)S(1)}, bf16[2,256,128]{2,1,0:T(8,128)(2,1)S(1)}, u32[]{:S(2)}, u32[]{:S(2)}) collective-permute-start(bf16[2,256,128]{2,1,0:T(8,128)(2,1)S(1)} %bitcast.41), channel_id=1, source_target_pairs={{8,20},{9,21},{10,22},{11,23},{12,16},{13,17},{14,18},{15,19},{24,... | collective-permute-start | bytes 393224 | tf_op jit(solution)/shard_map/ppermute | solution.py:448
  44.6 6.3 %collective-permute-start.15 = (bf16[2,256,128]{2,1,0:T(8,128)(2,1)S(1)}, bf16[2,256,128]{2,1,0:T(8,128)(2,1)S(1)}, u32[]{:S(2)}, u32[]{:S(2)}) collective-permute-start(bf16[2,256,128]{2,1,0:T(8,128)(2,1)S(1)} %bitcast.49), channel_id=1, source_target_pairs={{8,21},{9,20},{10,23},{11,22},{12,17},{13,16},{14,19},{15,18},{24,... | collective-permute-start | bytes 393224 | tf_op jit(solution)/shard_map/ppermute | solution.py:448
  50.9 15.7 %collective-permute-start.16 = (bf16[2,256,128]{2,1,0:T(8,128)(2,1)S(1)}, bf16[2,256,128]{2,1,0:T(8,128)(2,1)S(1)}, u32[]{:S(2)}, u32[]{:S(2)}) collective-permute-start(bf16[2,256,128]{2,1,0:T(8,128)(2,1)S(1)} %get-tuple-element.63), channel_id=1, source_target_pairs={{9,0},{8,1},{11,2},{10,3},{13,4},{12,5},{15,6},{14,7},{25,16},{24,... | collective-permute-start | bytes 393224 | tf_op jit(solution)/shard_map/ppermute | solution.py:456
  54.2 21.9 %collective-permute-start.17 = (bf16[2,256,128]{2,1,0:T(8,128)(2,1)S(1)}, bf16[2,256,128]{2,1,0:T(8,128)(2,1)S(1)}, u32[]{:S(2)}, u32[]{:S(2)}) collective-permute-start(bf16[2,256,128]{2,1,0:T(8,128)(2,1)S(1)} %get-tuple-element.64), channel_id=1, source_target_pairs={{11,0},{10,1},{13,2},{12,3},{15,4},{14,5},{9,6},{8,7},{27,16},{26,... | collective-permute-start | bytes 393224 | tf_op jit(solution)/shard_map/ppermute | solution.py:456
  62.5 15.8 %collective-permute-start.18 = (bf16[2,256,128]{2,1,0:T(8,128)(2,1)S(1)}, bf16[2,256,128]{2,1,0:T(8,128)(2,1)S(1)}, u32[]{:S(2)}, u32[]{:S(2)}) collective-permute-start(bf16[2,256,128]{2,1,0:T(8,128)(2,1)S(1)} %get-tuple-element.65), channel_id=1, source_target_pairs={{15,0},{14,1},{9,2},{8,3},{11,4},{10,5},{13,6},{12,7},{31,16},{30,... | collective-permute-start | bytes 393224 | tf_op jit(solution)/shard_map/ppermute | solution.py:456
  63.8 16.9 %collective-permute-start.19 = (bf16[2,256,128]{2,1,0:T(8,128)(2,1)S(1)}, bf16[2,256,128]{2,1,0:T(8,128)(2,1)S(1)}, u32[]{:S(2)}, u32[]{:S(2)}) collective-permute-start(bf16[2,256,128]{2,1,0:T(8,128)(2,1)S(1)} %get-tuple-element.66), channel_id=1, source_target_pairs={{13,0},{12,1},{15,2},{14,3},{9,4},{8,5},{11,6},{10,7},{29,16},{28,... | collective-permute-start | bytes 393224 | tf_op jit(solution)/shard_map/ppermute | solution.py:456
  65.1 16.9 %collective-permute-start.20 = (bf16[2,256,128]{2,1,0:T(8,128)(2,1)S(1)}, bf16[2,256,128]{2,1,0:T(8,128)(2,1)S(1)}, u32[]{:S(2)}, u32[]{:S(2)}) collective-permute-start(bf16[2,256,128]{2,1,0:T(8,128)(2,1)S(1)} %get-tuple-element.67), channel_id=1, source_target_pairs={{8,0},{9,1},{10,2},{11,3},{12,4},{13,5},{14,6},{15,7},{24,16},{25,... | collective-permute-start | bytes 393224 | tf_op jit(solution)/shard_map/ppermute | solution.py:456
  66.6 16.7 %collective-permute-start.21 = (bf16[2,256,128]{2,1,0:T(8,128)(2,1)S(1)}, bf16[2,256,128]{2,1,0:T(8,128)(2,1)S(1)}, u32[]{:S(2)}, u32[]{:S(2)}) collective-permute-start(bf16[2,256,128]{2,1,0:T(8,128)(2,1)S(1)} %get-tuple-element.68), channel_id=1, source_target_pairs={{10,0},{11,1},{12,2},{13,3},{14,4},{15,5},{8,6},{9,7},{26,16},{27,... | collective-permute-start | bytes 393224 | tf_op jit(solution)/shard_map/ppermute | solution.py:456
  76.1 8.5 %collective-permute-start.22 = (bf16[2,256,128]{2,1,0:T(8,128)(2,1)S(1)}, bf16[2,256,128]{2,1,0:T(8,128)(2,1)S(1)}, u32[]{:S(2)}, u32[]{:S(2)}) collective-permute-start(bf16[2,256,128]{2,1,0:T(8,128)(2,1)S(1)} %get-tuple-element.69), channel_id=1, source_target_pairs={{14,0},{15,1},{8,2},{9,3},{10,4},{11,5},{12,6},{13,7},{30,16},{31,... | collective-permute-start | bytes 393224 | tf_op jit(solution)/shard_map/ppermute | solution.py:456
  78.3 7.6 %collective-permute-start.23 = (bf16[2,256,128]{2,1,0:T(8,128)(2,1)S(1)}, bf16[2,256,128]{2,1,0:T(8,128)(2,1)S(1)}, u32[]{:S(2)}, u32[]{:S(2)}) collective-permute-start(bf16[2,256,128]{2,1,0:T(8,128)(2,1)S(1)} %get-tuple-element.70), channel_id=1, source_target_pairs={{12,0},{13,1},{14,2},{15,3},{8,4},{9,5},{10,6},{11,7},{28,16},{29,... | collective-permute-start | bytes 393224 | tf_op jit(solution)/shard_map/ppermute | solution.py:456
  80.7 7.2 %collective-permute-start.24 = (bf16[2,256,128]{2,1,0:T(8,128)(2,1)S(1)}, bf16[2,256,128]{2,1,0:T(8,128)(2,1)S(1)}, u32[]{:S(2)}, u32[]{:S(2)}) collective-permute-start(bf16[2,256,128]{2,1,0:T(8,128)(2,1)S(1)} %get-tuple-element.71), channel_id=1, source_target_pairs={{17,8},{16,9},{19,10},{18,11},{21,12},{20,13},{23,14},{22,15},{1,2... | collective-permute-start | bytes 393224 | tf_op jit(solution)/shard_map/ppermute | solution.py:456
  82.0 10.3 %collective-permute-start.25 = (bf16[2,256,128]{2,1,0:T(8,128)(2,1)S(1)}, bf16[2,256,128]{2,1,0:T(8,128)(2,1)S(1)}, u32[]{:S(2)}, u32[]{:S(2)}) collective-permute-start(bf16[2,256,128]{2,1,0:T(8,128)(2,1)S(1)} %get-tuple-element.72), channel_id=1, source_target_pairs={{19,8},{18,9},{21,10},{20,11},{23,12},{22,13},{17,14},{16,15},{3,2... | collective-permute-start | bytes 393224 | tf_op jit(solution)/shard_map/ppermute | solution.py:456
  83.3 11.3 %collective-permute-start.26 = (bf16[2,256,128]{2,1,0:T(8,128)(2,1)S(1)}, bf16[2,256,128]{2,1,0:T(8,128)(2,1)S(1)}, u32[]{:S(2)}, u32[]{:S(2)}) collective-permute-start(bf16[2,256,128]{2,1,0:T(8,128)(2,1)S(1)} %get-tuple-element.73), channel_id=1, source_target_pairs={{23,8},{22,9},{17,10},{16,11},{19,12},{18,13},{21,14},{20,15},{7,2... | collective-permute-start | bytes 393224 | tf_op jit(solution)/shard_map/ppermute | solution.py:456
  84.6 13.6 %collective-permute-start.27 = (bf16[2,256,128]{2,1,0:T(8,128)(2,1)S(1)}, bf16[2,256,128]{2,1,0:T(8,128)(2,1)S(1)}, u32[]{:S(2)}, u32[]{:S(2)}) collective-permute-start(bf16[2,256,128]{2,1,0:T(8,128)(2,1)S(1)} %get-tuple-element.74), channel_id=1, source_target_pairs={{21,8},{20,9},{23,10},{22,11},{17,12},{16,13},{19,14},{18,15},{5,2... | collective-permute-start | bytes 393224 | tf_op jit(solution)/shard_map/ppermute | solution.py:456
  85.9 12.3 %collective-permute-start.28 = (bf16[2,256,128]{2,1,0:T(8,128)(2,1)S(1)}, bf16[2,256,128]{2,1,0:T(8,128)(2,1)S(1)}, u32[]{:S(2)}, u32[]{:S(2)}) collective-permute-start(bf16[2,256,128]{2,1,0:T(8,128)(2,1)S(1)} %get-tuple-element.75), channel_id=1, source_target_pairs={{16,8},{17,9},{18,10},{19,11},{20,12},{21,13},{22,14},{23,15},{0,2... | collective-permute-start | bytes 393224 | tf_op jit(solution)/shard_map/ppermute | solution.py:456
  87.9 10.3 %collective-permute-start.29 = (bf16[2,256,128]{2,1,0:T(8,128)(2,1)S(1)}, bf16[2,256,128]{2,1,0:T(8,128)(2,1)S(1)}, u32[]{:S(2)}, u32[]{:S(2)}) collective-permute-start(bf16[2,256,128]{2,1,0:T(8,128)(2,1)S(1)} %get-tuple-element.76), channel_id=1, source_target_pairs={{18,8},{19,9},{20,10},{21,11},{22,12},{23,13},{16,14},{17,15},{2,2... | collective-permute-start | bytes 393224 | tf_op jit(solution)/shard_map/ppermute | solution.py:456
  92.3 9.0 %collective-permute-start.30 = (bf16[2,256,128]{2,1,0:T(8,128)(2,1)S(1)}, bf16[2,256,128]{2,1,0:T(8,128)(2,1)S(1)}, u32[]{:S(2)}, u32[]{:S(2)}) collective-permute-start(bf16[2,256,128]{2,1,0:T(8,128)(2,1)S(1)} %get-tuple-element.77), channel_id=1, source_target_pairs={{22,8},{23,9},{16,10},{17,11},{18,12},{19,13},{20,14},{21,15},{6,2... | collective-permute-start | bytes 393224 | tf_op jit(solution)/shard_map/ppermute | solution.py:456
  94.6 9.5 %collective-permute-start.31 = (bf16[2,256,128]{2,1,0:T(8,128)(2,1)S(1)}, bf16[2,256,128]{2,1,0:T(8,128)(2,1)S(1)}, u32[]{:S(2)}, u32[]{:S(2)}) collective-permute-start(bf16[2,256,128]{2,1,0:T(8,128)(2,1)S(1)} %get-tuple-element.78), channel_id=1, source_target_pairs={{20,8},{21,9},{22,10},{23,11},{16,12},{17,13},{18,14},{19,15},{4,2... | collective-permute-start | bytes 393224 | tf_op jit(solution)/shard_map/ppermute | solution.py:456

commit v14 on v12

--- a/solution.py
+++ b/solution.py
@@ -12,7 +12,6 @@
 FACTOR = HEAD**-0.5
 EXPONENT = FACTOR * 1.4426950408889634
 MIB = 1 << 20
-NT = ((1,), (1,))
 ANY = pl.BlockSpec(memory_space=pl.ANY)
 HBM = pl.BlockSpec(memory_space=pltpu.HBM)
 VMEM = pl.BlockSpec(memory_space=pltpu.VMEM)
@@ -30,8 +29,8 @@
     half = len(short) // 2
     return [
         short[:1] + near[:1] + short[1:half],
-        short[half:] + near[1:],
-        long[:eighth],
+        short[half + eighth :] + near[1:],
+        short[half : half + eighth] + long[:eighth],
         long[eighth:],
     ]
 
@@ -205,7 +204,7 @@
     join = shuffle(rows, True)
     for i, out in enumerate(outs):
         here = slice(i * rows, (i + 1) * rows)
-        both = jnp.concatenate([gk_ref[h, here, :], gv_ref[h, here, :]], axis=0)
+        both = jnp.concatenate([gk_ref[h, here, :] * FACTOR, gv_ref[h, here, :]], axis=0)
         out[h] = dot(join, both.astype(jnp.bfloat16)).astype(jnp.bfloat16)
 
 
@@ -251,22 +250,22 @@
             context_ref[h, :, here] = context
 
 
-def gradients(raised, low, scale, row_dot, qt, gt, refs, h):
+def gradients(raised, scale, row_dot, rows, gt, refs, h):
     v_ref, kt_ref, gk_ref, gv_ref = refs
+    query_rows, grad_rows = rows
+    weights = raised * scale
     grad_weights = dot(v_ref[h], gt)
-    grad_scores = (raised * (grad_weights - row_dot)).astype(jnp.bfloat16)
-    grad_q = dot(kt_ref[h], grad_scores) * (scale * FACTOR)
-    scaled = (qt.astype(jnp.float32) * (scale * FACTOR)).astype(jnp.bfloat16)
-    gk_ref[h] += dot(grad_scores, scaled, NT)
-    gv_ref[h] += dot(low, (gt.astype(jnp.float32) * scale).astype(jnp.bfloat16), NT)
-    return grad_q
+    grad_scores = (weights * (grad_weights - row_dot)).astype(jnp.bfloat16)
+    gv_ref[h] += dot(weights.astype(jnp.bfloat16), grad_rows)
+    gk_ref[h] += dot(grad_scores, query_rows)
+    return dot(kt_ref[h], grad_scores) * FACTOR
 
 
 def turn_kernel(count, tile, *refs):
     chunks, refs = refs[:count], refs[count:]
-    qt_ref, gt_ref, stats_in, context_in = refs[:4]
-    stats_ref, context_ref, grad_q_ref = refs[4:7]
-    outs, refs = refs[7 : 7 + count], refs[7 + count :]
+    q_ref, g_ref, qt_ref, gt_ref, stats_in, context_in = refs[:6]
+    stats_ref, context_ref, grad_q_ref = refs[6:9]
+    outs, refs = refs[9 : 9 + count], refs[9 + count :]
     k_ref, vt_ref, v_ref, kt_ref, gk_ref, gv_ref = refs
     heads, pair_rows, _ = chunks[0].shape
     rows = pair_rows // 2
@@ -281,7 +280,9 @@
         for h in range(heads):
             qt, gt = qt_ref[h, :, here], gt_ref[h, :, here]
             before = (stats_in[h, 0:1, here], stats_in[h, 1:2, here], context_in[h, :, here])
-            raised, low, top, total, context = raise_scores(k_ref[h], qt, vt_ref[h], before)
+            raised, _, top, total, context = raise_scores(k_ref[h], qt, vt_ref[h], before)
+            columns = slice(h * HEAD, (h + 1) * HEAD)
+            rows_here = q_ref[0, here, columns], g_ref[0, here, columns]
             scale = 1.0 / total
             context = context * scale
             row_dot = jnp.sum(gt.astype(jnp.float32) * context, axis=0, keepdims=True)
@@ -290,7 +291,7 @@
             stats_ref[h, 1:2, here] = scale
             stats_ref[h, 2:3, here] = row_dot
             grad_q_ref[h, :, here] = gradients(
-                raised, low, scale, row_dot, qt, gt, (v_ref, kt_ref, gk_ref, gv_ref), h
+                raised, scale, row_dot, rows_here, gt, (v_ref, kt_ref, gk_ref, gv_ref), h
             )
 
     for h in range(heads):
@@ -303,11 +304,11 @@
     for count in counts:
         groups.append((refs[:count], refs[count], refs[count + 1]))
         refs = refs[count + 2 :]
-    qt_ref, gt_ref, stats_ref, grad_q_in = refs[:4]
+    q_ref, g_ref, gt_ref, stats_ref, grad_q_in = refs[:5]
     if first:
-        ready_ref, rows_ref, grad_q_ref, refs = refs[4], refs[5], refs[6], refs[7:]
+        ready_ref, rows_ref, grad_q_ref, refs = refs[5], refs[6], refs[7], refs[8:]
     else:
-        rows_ref, refs = refs[4], refs[5:]
+        rows_ref, refs = refs[5], refs[6:]
     outs, refs = refs[: sum(counts)], refs[sum(counts) :]
     scratch = [refs[i : i + 4] for i in range(0, len(refs), 4)]
     heads, pair_rows, _ = groups[0][0][0].shape
@@ -318,20 +319,20 @@
         gk_ref[...] = jnp.zeros_like(gk_ref)
         gv_ref[...] = jnp.zeros_like(gv_ref)
 
-    @tiles(qt_ref.shape[2] // tile)
+    @tiles(gt_ref.shape[2] // tile)
     def _(j):
         here = tokens_of(j, tile)
         for h in range(heads):
             columns = slice(h * HEAD, (h + 1) * HEAD)
-            qt, gt = qt_ref[h, :, here], gt_ref[h, :, here]
+            rows_here = q_ref[0, here, columns], g_ref[0, here, columns]
+            gt = gt_ref[h, :, here]
             top, scale, row_dot = (stats_ref[h, i : i + 1, here] for i in range(3))
             grad_q = grad_q_in[h, :, here]
             for (_, low_ref, then_ref), own in zip(groups, scratch):
                 shrunk = jnp.exp2((then_ref[h, 0:1, here] - top) * EXPONENT)
-                low = low_ref[h, :, here]
-                raised = low.astype(jnp.float32)
+                raised = low_ref[h, :, here].astype(jnp.float32)
                 grad_q = grad_q + gradients(
-                    raised, low, scale * shrunk, row_dot, qt, gt, own, h
+                    raised, scale * shrunk, row_dot, rows_here, gt, own, h
                 )
             if first:
                 grad_q_ref[h, :, here] = grad_q
@@ -396,24 +397,24 @@
     final, context, grad_q, *grads = pl.pallas_call(
         functools.partial(turn_kernel, count, tile_of(count * rows, tokens)),
         out_shape=[stats_shape, wide_shape, wide_shape] + shapes_of(group),
-        in_specs=[VMEM] * (count + 4),
+        in_specs=[VMEM] * (count + 6),
         out_specs=[VMEM] * (count + 3),
         scratch_shapes=[natural(count), across(count, 16), natural(count), across(count)]
         + [sums(count)] * 2,
         compiler_params=compiler_params,
         cost_estimate=cost(heads, count * rows, tokens, 6),
         name="turn",
-    )(*group, qt, gt, *state)
+    )(*group, queries, upstream, qt, gt, *state)
     returned = [send_back(len(groups) - 1, grads)]
 
-    for part in (list(range(len(groups) - 2, 0, -1)), [0]):
-        first = part != [0]
+    for part in ([len(groups) - 2], list(range(len(groups) - 3, -1, -1))):
+        first = part[-1] > 0
         counts = [len(groups[i]) for i in part]
         back = [] if first else returned[0]
         operands = []
         for i in part:
             operands += [*groups[i], *kept[i]]
-        operands += [qt, gt, final, grad_q, *([context] if first else [])]
+        operands += [queries, upstream, gt, final, grad_q, *([context] if first else [])]
         shapes = [rows_shape, wide_shape] if first else [rows_shape]
         outs = pl.pallas_call(
             functools.partial(

time: 67.9 us -> 72.3 us (1.065)
  waiting for transfers between devices: 13.6 us -> 21.3 us
  starting transfers between devices: 30.9 us -> 28.6 us
  Pallas kernels: 21.1 us -> 20.1 us
    ppermute x8, waiting for transfers between devices: 6.22 us -> 10.3 us  [shards(): blocks.append(lax.ppermute(block, AXES, route(offset, False)))]
    ppermute x8, waiting for transfers between devices: 7.38 us -> 11 us  [send_back(): lax.ppermute(g, AXES, route(o, True))]
    ppermute x8, starting transfers between devices: 16.9 us -> 13.5 us  [shards(): blocks.append(lax.ppermute(block, AXES, route(offset, False)))]
    ppermute x8, starting transfers between devices: 14 us -> 15.1 us  [send_back(): lax.ppermute(g, AXES, route(o, True))]
    pallas_call x2, Pallas kernels: 9.42 us -> 8.37 us  [attend(): pl.pallas_call(functools.partial(backward_kernel, len(back), counts, firs...]
  transfers between devices with their start and end apart: 16 -> 16, of which waited for: 6 -> 8; matrix products, arithmetic and copies ran while one was open for 0% -> 0% of each run, Pallas kernels for 24% -> 21%
where the time goes in v14:
time: 72.3 us; the launch traced here: 72.2 us
  starting transfers between devices  28.6 us (40%)
  waiting for transfers between devices  21.3 us (29%)
  Pallas kernels  20.1 us (28%)
  local copies, waits for them, and re-layouts  1.3 us (2%)
  between operations  0.9 us (1%)
    ppermute x8, starting transfers between devices, send_back(): lax.ppermute(g, AXES, route(o, True))  15.1 us
    ppermute x8, starting transfers between devices, shards(): blocks.append(lax.ppermute(block, AXES, route(offset, False)))  13.5 us
    ppermute x8, waiting for transfers between devices, send_back(): lax.ppermute(g, AXES, route(o, True))  11 us
    ppermute x8, waiting for transfers between devices, shards(): blocks.append(lax.ppermute(block, AXES, route(offset, False)))  10.3 us
    pallas_call x2, Pallas kernels, attend(): pl.pallas_call(functools.partial(backward_kernel, len(back), counts, firs...  8.37 us
    pallas_call x3, Pallas kernels, attend(): pl.pallas_call(functools.partial(forward_kernel, count, not state, tile_o...  6.24 us
    pallas_call x1, Pallas kernels, attend(): pl.pallas_call(functools.partial(turn_kernel, count, tile_of(count * rows...  2.45 us
    pallas_call x1, Pallas kernels, unpack(): pl.pallas_call(kernel, out_shape=jax.ShapeDtypeStruct((1, rows, 2, width)...  1.51 us
  transfers between devices with their start and end apart: 16, of which 8 were waited for; matrix products, arithmetic and copies ran while one was open for 0% of the time, Pallas kernels for 21%

profile of v14, /device:TPU:0, one launch (start us, length us, event | category | flops | bytes accessed | tf_op | source)
XLA Modules:
  0.0 72.2 jit_solution(3404783710393403033)
XLA Ops:
  0.6 0.0 copy-start
  0.6 0.0 copy-start.2
  0.7 1.3 %copy-done.2 = bf16[1,128,2,2048]{3,2,1,0:T(2,128)(2,1)S(1)} copy-done((bf16[1,128,2,2048]{3,2,1,0:T(2,128)(2,1)S(1)}, bf16[1,128,2,2048]{3,2,1,0:T(2,128)(2,1)}, u32[]{:S(2)}) %copy-start.2) | copy-done | bytes 1048600
  1.9 0.0 copy-start.1
  1.9 1.0 %pack.1 = (bf16[2,128,2,128]{3,2,1,0:T(2,128)(2,1)S(1)}, bf16[2,128,2,128]{3,2,1,0:T(2,128)(2,1)S(1)}, bf16[2,128,2,128]{3,2,1,0:T(2,128)(2,1)S(1)}, bf16[2,128,...) custom-call(bf16[1,128,2,2048]{3,2,1,0:T(2,128)(2,1)S(1)} %copy-done.2), custom_call_target="tpu_custom_call" | custom-call | tf_op jit(solution)/shard_map/pack/pallas_call | solution.py:79
  2.9 3.5 %collective-permute-start.4 = (bf16[2,256,128]{2,1,0:T(8,128)(2,1)S(1)}, bf16[2,256,128]{2,1,0:T(8,128)(2,1)S(1)}, u32[]{:S(2)}, u32[]{:S(2)}) collective-permute-start(bf16[2,256,128]{2,1,0:T(8,128)(2,1)S(1)} %bitcast.31), channel_id=1, source_target_pairs={{0,11},{1,10},{2,13},{3,12},{4,15},{5,14},{6,9},{7,8},{8,19},{9,18... | collective-permute-start | bytes 393224 | tf_op jit(solution)/shard_map/ppermute | solution.py:454
  6.4 1.7 %collective-permute-start.5 = (bf16[2,256,128]{2,1,0:T(8,128)(2,1)S(1)}, bf16[2,256,128]{2,1,0:T(8,128)(2,1)S(1)}, u32[]{:S(2)}, u32[]{:S(2)}) collective-permute-start(bf16[2,256,128]{2,1,0:T(8,128)(2,1)S(1)} %bitcast.30), channel_id=1, source_target_pairs={{0,9},{1,8},{2,11},{3,10},{4,13},{5,12},{6,15},{7,14},{8,17},{9,16... | collective-permute-start | bytes 393224 | tf_op jit(solution)/shard_map/ppermute | solution.py:454
  8.1 2.6 %collective-permute-start.6 = (bf16[2,256,128]{2,1,0:T(8,128)(2,1)S(1)}, bf16[2,256,128]{2,1,0:T(8,128)(2,1)S(1)}, u32[]{:S(2)}, u32[]{:S(2)}) collective-permute-start(bf16[2,256,128]{2,1,0:T(8,128)(2,1)S(1)} %bitcast.29), channel_id=1, source_target_pairs={{0,15},{1,14},{2,9},{3,8},{4,11},{5,10},{6,13},{7,12},{8,23},{9,22... | collective-permute-start | bytes 393224 | tf_op jit(solution)/shard_map/ppermute | solution.py:454
  10.7 2.1 %collective-permute-start.2 = (bf16[2,256,128]{2,1,0:T(8,128)(2,1)S(1)}, bf16[2,256,128]{2,1,0:T(8,128)(2,1)S(1)}, u32[]{:S(2)}, u32[]{:S(2)}) collective-permute-start(bf16[2,256,128]{2,1,0:T(8,128)(2,1)S(1)} %bitcast.28), channel_id=1, source_target_pairs={{0,14},{1,15},{2,8},{3,9},{4,10},{5,11},{6,12},{7,13},{8,22},{9,23... | collective-permute-start | bytes 393224 | tf_op jit(solution)/shard_map/ppermute | solution.py:454
  12.8 0.0 collective-permute-start.3
  12.8 0.7 collective-permute-done.4.refs_0_.refs_5_
  13.5 0.3 collective-permute-start.1
  13.7 3.6 %collective-permute-done.5.refs_1_.refs_6_ = bf16[2,256,128]{2,1,0:T(8,128)(2,1)S(1)} collective-permute-done((bf16[2,256,128]{2,1,0:T(8,128)(2,1)S(1)}, bf16[2,256,128]{2,1,0:T(8,128)(2,1)S(1)}, u32[]{:S(2)}, u32[]{:S(2)}) %collective-permute-start.5) | collective-permute-done | bytes 131104 | tf_op jit(solution)/shard_map/ppermute | solution.py:454
  17.3 0.7 %collective-permute-start = (bf16[2,256,128]{2,1,0:T(8,128)(2,1)S(1)}, bf16[2,256,128]{2,1,0:T(8,128)(2,1)S(1)}, u32[]{:S(2)}, u32[]{:S(2)}) collective-permute-start(bf16[2,256,128]{2,1,0:T(8,128)(2,1)S(1)} %bitcast.25), channel_id=1, source_target_pairs={{0,10},{1,11},{2,12},{3,13},{4,14},{5,15},{6,8},{7,9},{8,18},{9,19... | collective-permute-start | bytes 393224 | tf_op jit(solution)/shard_map/ppermute | solution.py:454
  18.0 0.0 copy-done
  18.0 0.3 turned.2.refs_3_.refs_2_
  18.3 0.0 copy-done.1
  18.3 0.3 turned.3.refs_4_.refs_6_.refs_12_
  18.6 0.0 collective-permute-done.6.refs_2_.refs_7_
  18.6 2.6 %collective-permute-start.7 = (bf16[2,256,128]{2,1,0:T(8,128)(2,1)S(1)}, bf16[2,256,128]{2,1,0:T(8,128)(2,1)S(1)}, u32[]{:S(2)}, u32[]{:S(2)}) collective-permute-start(bf16[2,256,128]{2,1,0:T(8,128)(2,1)S(1)} %bitcast.24), channel_id=1, source_target_pairs={{0,12},{1,13},{2,14},{3,15},{4,8},{5,9},{6,10},{7,11},{8,20},{9,21... | collective-permute-start | bytes 393224 | tf_op jit(solution)/shard_map/ppermute | solution.py:454
  21.2 2.5 %forward.3 = (f32[2,8,1536]{2,1,0:T(8,128)S(1)}, f32[2,128,1536]{2,1,0:T(8,128)S(1)}, bf16[2,384,1536]{2,1,0:T(8,128)(2,1)S(1)}) custom-call(bf16[2,256,128]{2,1,0:T(8,128)(2,1)S(1)} %collective-permute-done.4.refs_0_.refs_5_, bf16[2,256,128]{2,1,0:T(8,128)(2,1)S(1)} %collective-permute-done.5.refs_1_.refs_6_, ...), custom_call_target="tpu_custom_call" | custom-call | flops 603979776 | bytes 3932160 | tf_op jit(solution)/shard_map/forward/pallas_call | solution.py:383
  23.7 0.0 collective-permute-done.2.refs_0_.refs_1_
  23.7 0.0 collective-permute-done.3.refs_1_.refs_2_
  23.8 1.8 %forward.4 = (f32[2,8,1536]{2,1,0:T(8,128)S(1)}, f32[2,128,1536]{2,1,0:T(8,128)S(1)}, bf16[2,256,1536]{2,1,0:T(8,128)(2,1)S(1)}) custom-call(bf16[2,256,128]{2,1,0:T(8,128)(2,1)S(1)} %collective-permute-done.2.refs_0_.refs_1_, bf16[2,256,128]{2,1,0:T(8,128)(2,1)S(1)} %collective-permute-done.3.refs_1_.refs_2_, ...), custom_call_target="tpu_custom_call" | custom-call | flops 402653184 | bytes 3670016 | tf_op jit(solution)/shard_map/forward/pallas_call | solution.py:383
  25.6 4.5 %collective-permute-done.1.refs_1_ = bf16[2,256,128]{2,1,0:T(8,128)(2,1)S(1)} collective-permute-done((bf16[2,256,128]{2,1,0:T(8,128)(2,1)S(1)}, bf16[2,256,128]{2,1,0:T(8,128)(2,1)S(1)}, u32[]{:S(2)}, u32[]{:S(2)}) %collective-permute-start.1) | collective-permute-done | bytes 131104 | tf_op jit(solution)/shard_map/ppermute | solution.py:454
  30.1 0.0 collective-permute-done.refs_0_
  30.1 1.8 %forward.5 = (f32[2,8,1536]{2,1,0:T(8,128)S(1)}, f32[2,128,1536]{2,1,0:T(8,128)S(1)}, bf16[2,256,1536]{2,1,0:T(8,128)(2,1)S(1)}) custom-call(bf16[2,256,128]{2,1,0:T(8,128)(2,1)S(1)} %collective-permute-done.refs_0_, bf16[2,256,128]{2,1,0:T(8,128)(2,1)S(1)} %collective-permute-done.1.refs_1_, bf16[2,128,1536]{2,1,0:T(8,128)(2,1)S(1)} %turned.2.refs_3_.refs_2_, ...), custom_call_target="tpu_custom_call" | custom-call | flops 402653184 | bytes 3670016 | tf_op jit(solution)/shard_map/forward/pallas_call | solution.py:383
  31.9 1.6 %collective-permute-done.7.refs_0_ = bf16[2,256,128]{2,1,0:T(8,128)(2,1)S(1)} collective-permute-done((bf16[2,256,128]{2,1,0:T(8,128)(2,1)S(1)}, bf16[2,256,128]{2,1,0:T(8,128)(2,1)S(1)}, u32[]{:S(2)}, u32[]{:S(2)}) %collective-permute-start.7) | collective-permute-done | bytes 131104 | tf_op jit(solution)/shard_map/ppermute | solution.py:454
  33.5 2.4 %turn.1 = (f32[2,8,1536]{2,1,0:T(8,128)S(1)}, f32[2,128,1536]{2,1,0:T(8,128)S(1)}, f32[2,128,1536]{2,1,0:T(8,128)S(1)}, bf16[2,256,128]{2,1,0:T(8,128)(2,1)S(1)}) custom-call(bf16[2,256,128]{2,1,0:T(8,128)(2,1)S(1)} %collective-permute-done.7.refs_0_, bf16[1,1536,256]{2,1,0:T(8,128)(2,1)S(1)} %copy-done, bf16[1,1536,256]{2,1,0:T(8,128)(2,1)S(1)} %copy-done.1, ...), custom_call_target="tpu_custom_call" | custom-call | flops 603979776 | bytes 3407872 | tf_op jit(solution)/shard_map/turn/pallas_call | solution.py:397
  36.0 0.8 %collective-permute-start.8 = (bf16[2,256,128]{2,1,0:T(8,128)(2,1)S(1)}, bf16[2,256,128]{2,1,0:T(8,128)(2,1)S(1)}, u32[]{:S(2)}, u32[]{:S(2)}) collective-permute-start(bf16[2,256,128]{2,1,0:T(8,128)(2,1)S(1)} %get-tuple-element.53), channel_id=1, source_target_pairs={{12,0},{13,1},{14,2},{15,3},{8,4},{9,5},{10,6},{11,7},{20,8},{21,9... | collective-permute-start | bytes 393224 | tf_op jit(solution)/shard_map/ppermute | solution.py:462
  36.8 2.9 %backward.2 = (bf16[1,1536,256]{2,1,0:T(8,128)(2,1)}, f32[2,128,1536]{2,1,0:T(8,128)S(1)}, bf16[2,256,128]{2,1,0:T(8,128)(2,1)S(1)}, bf16[2,256,128]{2,1,0:T(8,128)(2,1)S(1)}) custom-call(bf16[2,256,128]{2,1,0:T(8,128)(2,1)S(1)} %collective-permute-done.refs_0_, bf16[2,256,128]{2,1,0:T(8,128)(2,1)S(1)} %collective-permute-done.1.refs_1_, ...), custom_call_target="tpu_custom_call" | custom-call | flops 805306368 | bytes 3670016 | tf_op jit(solution)/shard_map/backward/pallas_call | solution.py:419
  39.6 1.9 %collective-permute-start.9 = (bf16[2,256,128]{2,1,0:T(8,128)(2,1)S(1)}, bf16[2,256,128]{2,1,0:T(8,128)(2,1)S(1)}, u32[]{:S(2)}, u32[]{:S(2)}) collective-permute-start(bf16[2,256,128]{2,1,0:T(8,128)(2,1)S(1)} %get-tuple-element.58), channel_id=1, source_target_pairs={{10,0},{11,1},{12,2},{13,3},{14,4},{15,5},{8,6},{9,7},{18,8},{19,9... | collective-permute-start | bytes 393224 | tf_op jit(solution)/shard_map/ppermute | solution.py:462
  41.5 1.5 %collective-permute-start.10 = (bf16[2,256,128]{2,1,0:T(8,128)(2,1)S(1)}, bf16[2,256,128]{2,1,0:T(8,128)(2,1)S(1)}, u32[]{:S(2)}, u32[]{:S(2)}) collective-permute-start(bf16[2,256,128]{2,1,0:T(8,128)(2,1)S(1)} %get-tuple-element.59), channel_id=1, source_target_pairs={{13,0},{12,1},{15,2},{14,3},{9,4},{8,5},{11,6},{10,7},{21,8},{20,9... | collective-permute-start | bytes 393224 | tf_op jit(solution)/shard_map/ppermute | solution.py:462
  43.0 1.9 %collective-permute-done.8.refs_0_ = bf16[2,256,128]{2,1,0:T(8,128)(2,1)S(1)} collective-permute-done((bf16[2,256,128]{2,1,0:T(8,128)(2,1)S(1)}, bf16[2,256,128]{2,1,0:T(8,128)(2,1)S(1)}, u32[]{:S(2)}, u32[]{:S(2)}) %collective-permute-start.8) | collective-permute-done | bytes 131104 | tf_op jit(solution)/shard_map/ppermute | solution.py:462
  44.9 5.5 %backward.3 = (bf16[1,1536,256]{2,1,0:T(8,128)(2,1)}, bf16[2,256,128]{2,1,0:T(8,128)(2,1)S(1)}, bf16[2,256,128]{2,1,0:T(8,128)(2,1)S(1)}, bf16[2,256,128]{2,1,0:...) custom-call(bf16[2,256,128]{2,1,0:T(8,128)(2,1)S(1)} %collective-permute-done.8.refs_0_, ...), custom_call_target="tpu_custom_call" | custom-call | flops 2013265920 | bytes 4456448 | tf_op jit(solution)/shard_map/backward/pallas_call | solution.py:419
  50.4 5.5 %collective-permute-start.11 = (bf16[2,256,128]{2,1,0:T(8,128)(2,1)S(1)}, bf16[2,256,128]{2,1,0:T(8,128)(2,1)S(1)}, u32[]{:S(2)}, u32[]{:S(2)}) collective-permute-start(bf16[2,256,128]{2,1,0:T(8,128)(2,1)S(1)} %get-tuple-element.60), channel_id=1, source_target_pairs={{14,0},{15,1},{8,2},{9,3},{10,4},{11,5},{12,6},{13,7},{22,8},{23,9... | collective-permute-start | bytes 393224 | tf_op jit(solution)/shard_map/ppermute | solution.py:462
  55.8 0.6 collective-permute-start.12
  56.4 2.3 %collective-permute-start.13 = (bf16[2,256,128]{2,1,0:T(8,128)(2,1)S(1)}, bf16[2,256,128]{2,1,0:T(8,128)(2,1)S(1)}, u32[]{:S(2)}, u32[]{:S(2)}) collective-permute-start(bf16[2,256,128]{2,1,0:T(8,128)(2,1)S(1)} %get-tuple-element.62), channel_id=1, source_target_pairs={{11,0},{10,1},{13,2},{12,3},{15,4},{14,5},{9,6},{8,7},{19,8},{18,9... | collective-permute-start | bytes 393224 | tf_op jit(solution)/shard_map/ppermute | solution.py:462
  58.7 0.0 collective-permute-done.9
  58.7 2.6 %collective-permute-start.14 = (bf16[2,256,128]{2,1,0:T(8,128)(2,1)S(1)}, bf16[2,256,128]{2,1,0:T(8,128)(2,1)S(1)}, u32[]{:S(2)}, u32[]{:S(2)}) collective-permute-start(bf16[2,256,128]{2,1,0:T(8,128)(2,1)S(1)} %get-tuple-element.63), channel_id=1, source_target_pairs={{9,0},{8,1},{11,2},{10,3},{13,4},{12,5},{15,6},{14,7},{17,8},{16,9... | collective-permute-start | bytes 393224 | tf_op jit(solution)/shard_map/ppermute | solution.py:462
  61.3 0.0 collective-permute-done.10
  61.3 0.0 collective-permute-start.15
  61.3 1.4 %collective-permute-done.11 = bf16[2,256,128]{2,1,0:T(8,128)(2,1)S(1)} collective-permute-done((bf16[2,256,128]{2,1,0:T(8,128)(2,1)S(1)}, bf16[2,256,128]{2,1,0:T(8,128)(2,1)S(1)}, u32[]{:S(2)}, u32[]{:S(2)}) %collective-permute-start.11) | collective-permute-done | bytes 131104 | tf_op jit(solution)/shard_map/ppermute | solution.py:462
  62.7 0.0 collective-permute-done.12
  62.7 2.7 %collective-permute-done.13 = bf16[2,256,128]{2,1,0:T(8,128)(2,1)S(1)} collective-permute-done((bf16[2,256,128]{2,1,0:T(8,128)(2,1)S(1)}, bf16[2,256,128]{2,1,0:T(8,128)(2,1)S(1)}, u32[]{:S(2)}, u32[]{:S(2)}) %collective-permute-start.13) | collective-permute-done | bytes 131104 | tf_op jit(solution)/shard_map/ppermute | solution.py:462
  65.4 5.1 %collective-permute-done.14 = bf16[2,256,128]{2,1,0:T(8,128)(2,1)S(1)} collective-permute-done((bf16[2,256,128]{2,1,0:T(8,128)(2,1)S(1)}, bf16[2,256,128]{2,1,0:T(8,128)(2,1)S(1)}, u32[]{:S(2)}, u32[]{:S(2)}) %collective-permute-start.14) | collective-permute-done | bytes 131104 | tf_op jit(solution)/shard_map/ppermute | solution.py:462
  70.5 0.0 collective-permute-done.15
  70.5 1.5 %unpack.1 = bf16[1,128,2,2048]{3,2,1,0:T(2,128)(2,1)} custom-call(bf16[2,128,2,128]{3,2,1,0:T(2,128)(2,1)S(1)} %bitcast.16, bf16[2,128,2,128]{3,2,1,0:T(2,128)(2,1)S(1)} %bitcast.17, bf16[2,128,2,128]{3,2,1,0:T(2,128)(2,1)S(1)} %bitcast.18, bf16[2,128,2,128]{3,2,1,0:T(2,128)(2,1)S(1)} %bitcast.19, bf16[2,128,2,128]{3,2,1,0:T(2,128)(2,1)S(1)} %bitcast.20, ...), custom_call_target="tpu_custom_call" | custom-call | tf_op jit(solution)/shard_map/unpack/pallas_call | solution.py:115
Async XLA Ops:
  0.6 17.4 %copy-start = (bf16[1,1536,256]{2,1,0:T(8,128)(2,1)S(1)}, bf16[1,1536,256]{2,1,0:T(8,128)(2,1)}, u32[]{:S(2)}) copy-start(bf16[1,1536,256]{2,1,0:T(8,128)(2,1)} %refs_10_.1) | copy-start | bytes 2359300
  0.6 1.3 %copy-start.2 = (bf16[1,128,2,2048]{3,2,1,0:T(2,128)(2,1)S(1)}, bf16[1,128,2,2048]{3,2,1,0:T(2,128)(2,1)}, u32[]{:S(2)}) copy-start(bf16[1,128,2,2048]{3,2,1,0:T(2,128)(2,1)} %pairs_ref.1) | copy-start | bytes 3145732
  1.9 16.4 %copy-start.1 = (bf16[1,1536,256]{2,1,0:T(8,128)(2,1)S(1)}, bf16[1,1536,256]{2,1,0:T(8,128)(2,1)}, u32[]{:S(2)}) copy-start(bf16[1,1536,256]{2,1,0:T(8,128)(2,1)} %refs_11_.1) | copy-start | bytes 2359300
  2.9 10.6 %collective-permute-start.4 = (bf16[2,256,128]{2,1,0:T(8,128)(2,1)S(1)}, bf16[2,256,128]{2,1,0:T(8,128)(2,1)S(1)}, u32[]{:S(2)}, u32[]{:S(2)}) collective-permute-start(bf16[2,256,128]{2,1,0:T(8,128)(2,1)S(1)} %bitcast.31), channel_id=1, source_target_pairs={{0,11},{1,10},{2,13},{3,12},{4,15},{5,14},{6,9},{7,8},{8,19},{9,18... | collective-permute-start | bytes 393224 | tf_op jit(solution)/shard_map/ppermute | solution.py:454
  6.4 10.9 %collective-permute-start.5 = (bf16[2,256,128]{2,1,0:T(8,128)(2,1)S(1)}, bf16[2,256,128]{2,1,0:T(8,128)(2,1)S(1)}, u32[]{:S(2)}, u32[]{:S(2)}) collective-permute-start(bf16[2,256,128]{2,1,0:T(8,128)(2,1)S(1)} %bitcast.30), channel_id=1, source_target_pairs={{0,9},{1,8},{2,11},{3,10},{4,13},{5,12},{6,15},{7,14},{8,17},{9,16... | collective-permute-start | bytes 393224 | tf_op jit(solution)/shard_map/ppermute | solution.py:454
  8.1 10.5 %collective-permute-start.6 = (bf16[2,256,128]{2,1,0:T(8,128)(2,1)S(1)}, bf16[2,256,128]{2,1,0:T(8,128)(2,1)S(1)}, u32[]{:S(2)}, u32[]{:S(2)}) collective-permute-start(bf16[2,256,128]{2,1,0:T(8,128)(2,1)S(1)} %bitcast.29), channel_id=1, source_target_pairs={{0,15},{1,14},{2,9},{3,8},{4,11},{5,10},{6,13},{7,12},{8,23},{9,22... | collective-permute-start | bytes 393224 | tf_op jit(solution)/shard_map/ppermute | solution.py:454
  10.7 13.0 %collective-permute-start.2 = (bf16[2,256,128]{2,1,0:T(8,128)(2,1)S(1)}, bf16[2,256,128]{2,1,0:T(8,128)(2,1)S(1)}, u32[]{:S(2)}, u32[]{:S(2)}) collective-permute-start(bf16[2,256,128]{2,1,0:T(8,128)(2,1)S(1)} %bitcast.28), channel_id=1, source_target_pairs={{0,14},{1,15},{2,8},{3,9},{4,10},{5,11},{6,12},{7,13},{8,22},{9,23... | collective-permute-start | bytes 393224 | tf_op jit(solution)/shard_map/ppermute | solution.py:454
  12.8 11.0 %collective-permute-start.3 = (bf16[2,256,128]{2,1,0:T(8,128)(2,1)S(1)}, bf16[2,256,128]{2,1,0:T(8,128)(2,1)S(1)}, u32[]{:S(2)}, u32[]{:S(2)}) collective-permute-start(bf16[2,256,128]{2,1,0:T(8,128)(2,1)S(1)} %bitcast.27), channel_id=1, source_target_pairs={{0,8},{1,9},{2,10},{3,11},{4,12},{5,13},{6,14},{7,15},{8,16},{9,17... | collective-permute-start | bytes 393224 | tf_op jit(solution)/shard_map/ppermute | solution.py:454
  13.5 16.6 %collective-permute-start.1 = (bf16[2,256,128]{2,1,0:T(8,128)(2,1)S(1)}, bf16[2,256,128]{2,1,0:T(8,128)(2,1)S(1)}, u32[]{:S(2)}, u32[]{:S(2)}) collective-permute-start(bf16[2,256,128]{2,1,0:T(8,128)(2,1)S(1)} %bitcast.26), channel_id=1, source_target_pairs={{0,13},{1,12},{2,15},{3,14},{4,9},{5,8},{6,11},{7,10},{8,21},{9,20... | collective-permute-start | bytes 393224 | tf_op jit(solution)/shard_map/ppermute | solution.py:454
  17.3 12.8 %collective-permute-start = (bf16[2,256,128]{2,1,0:T(8,128)(2,1)S(1)}, bf16[2,256,128]{2,1,0:T(8,128)(2,1)S(1)}, u32[]{:S(2)}, u32[]{:S(2)}) collective-permute-start(bf16[2,256,128]{2,1,0:T(8,128)(2,1)S(1)} %bitcast.25), channel_id=1, source_target_pairs={{0,10},{1,11},{2,12},{3,13},{4,14},{5,15},{6,8},{7,9},{8,18},{9,19... | collective-permute-start | bytes 393224 | tf_op jit(solution)/shard_map/ppermute | solution.py:454
  18.6 14.9 %collective-permute-start.7 = (bf16[2,256,128]{2,1,0:T(8,128)(2,1)S(1)}, bf16[2,256,128]{2,1,0:T(8,128)(2,1)S(1)}, u32[]{:S(2)}, u32[]{:S(2)}) collective-permute-start(bf16[2,256,128]{2,1,0:T(8,128)(2,1)S(1)} %bitcast.24), channel_id=1, source_target_pairs={{0,12},{1,13},{2,14},{3,15},{4,8},{5,9},{6,10},{7,11},{8,20},{9,21... | collective-permute-start | bytes 393224 | tf_op jit(solution)/shard_map/ppermute | solution.py:454
  36.0 8.9 %collective-permute-start.8 = (bf16[2,256,128]{2,1,0:T(8,128)(2,1)S(1)}, bf16[2,256,128]{2,1,0:T(8,128)(2,1)S(1)}, u32[]{:S(2)}, u32[]{:S(2)}) collective-permute-start(bf16[2,256,128]{2,1,0:T(8,128)(2,1)S(1)} %get-tuple-element.53), channel_id=1, source_target_pairs={{12,0},{13,1},{14,2},{15,3},{8,4},{9,5},{10,6},{11,7},{20,8},{21,9... | collective-permute-start | bytes 393224 | tf_op jit(solution)/shard_map/ppermute | solution.py:462
  39.6 19.1 %collective-permute-start.9 = (bf16[2,256,128]{2,1,0:T(8,128)(2,1)S(1)}, bf16[2,256,128]{2,1,0:T(8,128)(2,1)S(1)}, u32[]{:S(2)}, u32[]{:S(2)}) collective-permute-start(bf16[2,256,128]{2,1,0:T(8,128)(2,1)S(1)} %get-tuple-element.58), channel_id=1, source_target_pairs={{10,0},{11,1},{12,2},{13,3},{14,4},{15,5},{8,6},{9,7},{18,8},{19,9... | collective-permute-start | bytes 393224 | tf_op jit(solution)/shard_map/ppermute | solution.py:462
  41.5 19.8 %collective-permute-start.10 = (bf16[2,256,128]{2,1,0:T(8,128)(2,1)S(1)}, bf16[2,256,128]{2,1,0:T(8,128)(2,1)S(1)}, u32[]{:S(2)}, u32[]{:S(2)}) collective-permute-start(bf16[2,256,128]{2,1,0:T(8,128)(2,1)S(1)} %get-tuple-element.59), channel_id=1, source_target_pairs={{13,0},{12,1},{15,2},{14,3},{9,4},{8,5},{11,6},{10,7},{21,8},{20,9... | collective-permute-start | bytes 393224 | tf_op jit(solution)/shard_map/ppermute | solution.py:462
  50.4 12.4 %collective-permute-start.11 = (bf16[2,256,128]{2,1,0:T(8,128)(2,1)S(1)}, bf16[2,256,128]{2,1,0:T(8,128)(2,1)S(1)}, u32[]{:S(2)}, u32[]{:S(2)}) collective-permute-start(bf16[2,256,128]{2,1,0:T(8,128)(2,1)S(1)} %get-tuple-element.60), channel_id=1, source_target_pairs={{14,0},{15,1},{8,2},{9,3},{10,4},{11,5},{12,6},{13,7},{22,8},{23,9... | collective-permute-start | bytes 393224 | tf_op jit(solution)/shard_map/ppermute | solution.py:462
  55.8 6.9 %collective-permute-start.12 = (bf16[2,256,128]{2,1,0:T(8,128)(2,1)S(1)}, bf16[2,256,128]{2,1,0:T(8,128)(2,1)S(1)}, u32[]{:S(2)}, u32[]{:S(2)}) collective-permute-start(bf16[2,256,128]{2,1,0:T(8,128)(2,1)S(1)} %get-tuple-element.61), channel_id=1, source_target_pairs={{8,0},{9,1},{10,2},{11,3},{12,4},{13,5},{14,6},{15,7},{16,8},{17,9... | collective-permute-start | bytes 393224 | tf_op jit(solution)/shard_map/ppermute | solution.py:462
  56.4 9.0 %collective-permute-start.13 = (bf16[2,256,128]{2,1,0:T(8,128)(2,1)S(1)}, bf16[2,256,128]{2,1,0:T(8,128)(2,1)S(1)}, u32[]{:S(2)}, u32[]{:S(2)}) collective-permute-start(bf16[2,256,128]{2,1,0:T(8,128)(2,1)S(1)} %get-tuple-element.62), channel_id=1, source_target_pairs={{11,0},{10,1},{13,2},{12,3},{15,4},{14,5},{9,6},{8,7},{19,8},{18,9... | collective-permute-start | bytes 393224 | tf_op jit(solution)/shard_map/ppermute | solution.py:462
  58.7 11.8 %collective-permute-start.14 = (bf16[2,256,128]{2,1,0:T(8,128)(2,1)S(1)}, bf16[2,256,128]{2,1,0:T(8,128)(2,1)S(1)}, u32[]{:S(2)}, u32[]{:S(2)}) collective-permute-start(bf16[2,256,128]{2,1,0:T(8,128)(2,1)S(1)} %get-tuple-element.63), channel_id=1, source_target_pairs={{9,0},{8,1},{11,2},{10,3},{13,4},{12,5},{15,6},{14,7},{17,8},{16,9... | collective-permute-start | bytes 393224 | tf_op jit(solution)/shard_map/ppermute | solution.py:462
  61.3 9.2 %collective-permute-start.15 = (bf16[2,256,128]{2,1,0:T(8,128)(2,1)S(1)}, bf16[2,256,128]{2,1,0:T(8,128)(2,1)S(1)}, u32[]{:S(2)}, u32[]{:S(2)}) collective-permute-start(bf16[2,256,128]{2,1,0:T(8,128)(2,1)S(1)} %get-tuple-element.64), channel_id=1, source_target_pairs={{15,0},{14,1},{9,2},{8,3},{11,4},{10,5},{13,6},{12,7},{23,8},{22,9... | collective-permute-start | bytes 393224 | tf_op jit(solution)/shard_map/ppermute | solution.py:462

commit v15 on v14

--- a/solution.py
+++ b/solution.py
@@ -29,8 +29,8 @@
     half = len(short) // 2
     return [
         short[:1] + near[:1] + short[1:half],
-        short[half + eighth :] + near[1:],
-        short[half : half + eighth] + long[:eighth],
+        short[half:] + near[1:],
+        long[:eighth],
         long[eighth:],
     ]
 
@@ -298,17 +298,20 @@
         join_chunks(outs, h, rows, gk_ref, gv_ref)
 
 
-def backward_kernel(back, counts, first, tile, *refs):
+def backward_kernel(back, counts, ready, last, tile, *refs):
     refs = refs[back:]
     groups = []
     for count in counts:
         groups.append((refs[:count], refs[count], refs[count + 1]))
         refs = refs[count + 2 :]
     q_ref, g_ref, gt_ref, stats_ref, grad_q_in = refs[:5]
-    if first:
-        ready_ref, rows_ref, grad_q_ref, refs = refs[5], refs[6], refs[7], refs[8:]
-    else:
-        rows_ref, refs = refs[5], refs[6:]
+    refs = refs[5:]
+    if ready:
+        ready_ref, refs = refs[0], refs[1:]
+    if ready or last:
+        rows_ref, refs = refs[0], refs[1:]
+    if not last:
+        grad_q_ref, refs = refs[0], refs[1:]
     outs, refs = refs[: sum(counts)], refs[sum(counts) :]
     scratch = [refs[i : i + 4] for i in range(0, len(refs), 4)]
     heads, pair_rows, _ = groups[0][0][0].shape
@@ -334,10 +337,12 @@
                 grad_q = grad_q + gradients(
                     raised, scale * shrunk, row_dot, rows_here, gt, own, h
                 )
-            if first:
+            if not last:
                 grad_q_ref[h, :, here] = grad_q
+            if ready:
                 grad_q = ready_ref[h, :, here]
-            rows_ref[0, here, columns] = grad_q.T.astype(rows_ref.dtype)
+            if ready or last:
+                rows_ref[0, here, columns] = grad_q.T.astype(rows_ref.dtype)
 
     for count, (_, _, gk_ref, gv_ref) in zip(counts, scratch):
         for h in range(heads):
@@ -407,20 +412,25 @@
     )(*group, queries, upstream, qt, gt, *state)
     returned = [send_back(len(groups) - 1, grads)]
 
-    for part in ([len(groups) - 2], list(range(len(groups) - 3, -1, -1))):
-        first = part[-1] > 0
-        counts = [len(groups[i]) for i in part]
-        back = [] if first else returned[0]
+    for i in reversed(range(len(groups) - 1)):
+        part, ready, last = [i], i == 1, i == 0
+        counts = [len(groups[k]) for k in part]
+        back = returned[1] + returned[0] if last else []
         operands = []
-        for i in part:
-            operands += [*groups[i], *kept[i]]
-        operands += [queries, upstream, gt, final, grad_q, *([context] if first else [])]
-        shapes = [rows_shape, wide_shape] if first else [rows_shape]
+        for k in part:
+            operands += [*groups[k], *kept[k]]
+        operands += [queries, upstream, gt, final, grad_q, *([context] if ready else [])]
+        shapes = [rows_shape] * (ready or last) + [wide_shape] * (not last)
         outs = pl.pallas_call(
             functools.partial(
-                backward_kernel, len(back), counts, first, tile_of(max(counts) * rows, tokens)
+                backward_kernel,
+                len(back),
+                counts,
+                ready,
+                last,
+                tile_of(max(counts) * rows, tokens),
             ),
-            out_shape=shapes + shapes_of(sum((groups[i] for i in part), [])),
+            out_shape=shapes + shapes_of(sum((groups[k] for k in part), [])),
             in_specs=[ANY] * len(back) + [VMEM] * len(operands),
             out_specs=[VMEM] * (len(shapes) + sum(counts)),
             scratch_shapes=[
@@ -432,14 +442,16 @@
             cost_estimate=cost(heads, sum(counts) * rows, tokens, 4),
             name="backward",
         )(*back, *operands)
-        if first:
-            context_rows, grad_q = outs[:2]
+        if ready:
+            context_rows = outs[0]
+        if last:
+            grad_query = outs[0]
         else:
-            grad_query = outs[0]
+            grad_q = outs[len(shapes) - 1]
         blocks = list(outs[len(shapes) :])
-        for i in part:
-            returned.append(send_back(i, blocks[: len(groups[i])]))
-            blocks = blocks[len(groups[i]) :]
+        for k in part:
+            returned.append(send_back(k, blocks[: len(groups[k])]))
+            blocks = blocks[len(groups[k]) :]
     return context_rows, grad_query
 
 

time: 72.3 us -> 71.9 us (level)
  starting transfers between devices: 28.6 us -> 23.9 us
  waiting for transfers between devices: 21.3 us -> 24.8 us
    ppermute x8, starting transfers between devices: 15.1 us -> 9.45 us  [send_back(): lax.ppermute(g, AXES, route(o, True))]
    ppermute x8, waiting for transfers between devices: 11 us -> 14.5 us  [send_back(): lax.ppermute(g, AXES, route(o, True))]
    ppermute x8, starting transfers between devices: 13.5 us -> 14.4 us  [shards(): blocks.append(lax.ppermute(block, AXES, route(offset, False)))]
    pallas_call x2 -> x3, Pallas kernels: 8.37 us -> 8.78 us  [attend(): pl.pallas_call(functools.partial(backward_kernel, len(back), counts, read...]
  transfers between devices with their start and end apart: 16 -> 16, of which waited for: 8 -> 9; matrix products, arithmetic and copies ran while one was open for 0% -> 0% of each run, Pallas kernels for 21% -> 20%
where the time goes in v15:
time: 71.9 us; the launch traced here: 71.3 us
  waiting for transfers between devices  24.8 us (34%)
  starting transfers between devices  23.9 us (33%)
  Pallas kernels  20.3 us (28%)
  local copies, waits for them, and re-layouts  1.3 us (2%)
  between operations  0.92 us (1%)
    ppermute x8, waiting for transfers between devices, send_back(): lax.ppermute(g, AXES, route(o, True))  14.5 us
    ppermute x8, starting transfers between devices, shards(): blocks.append(lax.ppermute(block, AXES, route(offset, False)))  14.4 us
    ppermute x8, waiting for transfers between devices, shards(): blocks.append(lax.ppermute(block, AXES, route(offset, False)))  10.3 us
    ppermute x8, starting transfers between devices, send_back(): lax.ppermute(g, AXES, route(o, True))  9.45 us
    pallas_call x3, Pallas kernels, attend(): pl.pallas_call(functools.partial(backward_kernel, len(back), counts, read...  8.78 us
    pallas_call x3, Pallas kernels, attend(): pl.pallas_call(functools.partial(forward_kernel, count, not state, tile_o...  6.11 us
    pallas_call x1, Pallas kernels, attend(): pl.pallas_call(functools.partial(turn_kernel, count, tile_of(count * rows...  2.46 us
    pallas_call x1, Pallas kernels, unpack(): pl.pallas_call(kernel, out_shape=jax.ShapeDtypeStruct((1, rows, 2, width)...  1.5 us
  transfers between devices with their start and end apart: 16, of which 9 were waited for; matrix products, arithmetic and copies ran while one was open for 0% of the time, Pallas kernels for 20%

profile of v15, /device:TPU:0, one launch (start us, length us, event | category | flops | bytes accessed | tf_op | source)
XLA Modules:
  0.0 71.3 jit_solution(4306507222868796956)
XLA Ops:
  0.6 0.0 copy-start
  0.6 0.0 copy-start.2
  0.7 1.3 %copy-done.2 = bf16[1,128,2,2048]{3,2,1,0:T(2,128)(2,1)S(1)} copy-done((bf16[1,128,2,2048]{3,2,1,0:T(2,128)(2,1)S(1)}, bf16[1,128,2,2048]{3,2,1,0:T(2,128)(2,1)}, u32[]{:S(2)}) %copy-start.2) | copy-done | bytes 1048600
  1.9 0.0 copy-start.1
  1.9 0.9 %pack.1 = (bf16[2,128,2,128]{3,2,1,0:T(2,128)(2,1)S(1)}, bf16[2,128,2,128]{3,2,1,0:T(2,128)(2,1)S(1)}, bf16[2,128,2,128]{3,2,1,0:T(2,128)(2,1)S(1)}, bf16[2,128,...) custom-call(bf16[1,128,2,2048]{3,2,1,0:T(2,128)(2,1)S(1)} %copy-done.2), custom_call_target="tpu_custom_call" | custom-call | tf_op jit(solution)/shard_map/pack/pallas_call | solution.py:79
  2.9 3.5 %collective-permute-start.3 = (bf16[2,256,128]{2,1,0:T(8,128)(2,1)S(1)}, bf16[2,256,128]{2,1,0:T(8,128)(2,1)S(1)}, u32[]{:S(2)}, u32[]{:S(2)}) collective-permute-start(bf16[2,256,128]{2,1,0:T(8,128)(2,1)S(1)} %bitcast.31), channel_id=1, source_target_pairs={{0,11},{1,10},{2,13},{3,12},{4,15},{5,14},{6,9},{7,8},{8,19},{9,18... | collective-permute-start | bytes 393224 | tf_op jit(solution)/shard_map/ppermute | solution.py:466
  6.4 1.7 %collective-permute-start.4 = (bf16[2,256,128]{2,1,0:T(8,128)(2,1)S(1)}, bf16[2,256,128]{2,1,0:T(8,128)(2,1)S(1)}, u32[]{:S(2)}, u32[]{:S(2)}) collective-permute-start(bf16[2,256,128]{2,1,0:T(8,128)(2,1)S(1)} %bitcast.30), channel_id=1, source_target_pairs={{0,9},{1,8},{2,11},{3,10},{4,13},{5,12},{6,15},{7,14},{8,17},{9,16... | collective-permute-start | bytes 393224 | tf_op jit(solution)/shard_map/ppermute | solution.py:466
  8.1 2.6 %collective-permute-start.5 = (bf16[2,256,128]{2,1,0:T(8,128)(2,1)S(1)}, bf16[2,256,128]{2,1,0:T(8,128)(2,1)S(1)}, u32[]{:S(2)}, u32[]{:S(2)}) collective-permute-start(bf16[2,256,128]{2,1,0:T(8,128)(2,1)S(1)} %bitcast.29), channel_id=1, source_target_pairs={{0,15},{1,14},{2,9},{3,8},{4,11},{5,10},{6,13},{7,12},{8,23},{9,22... | collective-permute-start | bytes 393224 | tf_op jit(solution)/shard_map/ppermute | solution.py:466
  10.7 2.1 %collective-permute-start.1 = (bf16[2,256,128]{2,1,0:T(8,128)(2,1)S(1)}, bf16[2,256,128]{2,1,0:T(8,128)(2,1)S(1)}, u32[]{:S(2)}, u32[]{:S(2)}) collective-permute-start(bf16[2,256,128]{2,1,0:T(8,128)(2,1)S(1)} %bitcast.28), channel_id=1, source_target_pairs={{0,14},{1,15},{2,8},{3,9},{4,10},{5,11},{6,12},{7,13},{8,22},{9,23... | collective-permute-start | bytes 393224 | tf_op jit(solution)/shard_map/ppermute | solution.py:466
  12.8 0.0 collective-permute-start
  12.8 0.7 collective-permute-done.3.refs_0_.refs_2_
  13.4 0.6 collective-permute-start.2
  14.0 3.2 %collective-permute-done.4.refs_1_.refs_3_ = bf16[2,256,128]{2,1,0:T(8,128)(2,1)S(1)} collective-permute-done((bf16[2,256,128]{2,1,0:T(8,128)(2,1)S(1)}, bf16[2,256,128]{2,1,0:T(8,128)(2,1)S(1)}, u32[]{:S(2)}, u32[]{:S(2)}) %collective-permute-start.4) | collective-permute-done | bytes 131104 | tf_op jit(solution)/shard_map/ppermute | solution.py:466
  17.3 2.7 %collective-permute-start.7 = (bf16[2,256,128]{2,1,0:T(8,128)(2,1)S(1)}, bf16[2,256,128]{2,1,0:T(8,128)(2,1)S(1)}, u32[]{:S(2)}, u32[]{:S(2)}) collective-permute-start(bf16[2,256,128]{2,1,0:T(8,128)(2,1)S(1)} %bitcast.25), channel_id=1, source_target_pairs={{0,13},{1,12},{2,15},{3,14},{4,9},{5,8},{6,11},{7,10},{8,21},{9,20... | collective-permute-start | bytes 393224 | tf_op jit(solution)/shard_map/ppermute | solution.py:466
  20.0 0.0 copy-done
  20.0 0.3 turned.2.refs_3_.refs_1_
  20.3 0.0 copy-done.1
  20.3 0.3 turned.3.refs_4_.refs_5_.refs_7_.refs_9_
  20.6 0.0 collective-permute-done.5.refs_2_.refs_4_
  20.6 1.2 %collective-permute-start.6 = (bf16[2,256,128]{2,1,0:T(8,128)(2,1)S(1)}, bf16[2,256,128]{2,1,0:T(8,128)(2,1)S(1)}, u32[]{:S(2)}, u32[]{:S(2)}) collective-permute-start(bf16[2,256,128]{2,1,0:T(8,128)(2,1)S(1)} %bitcast.24), channel_id=1, source_target_pairs={{0,12},{1,13},{2,14},{3,15},{4,8},{5,9},{6,10},{7,11},{8,20},{9,21... | collective-permute-start | bytes 393224 | tf_op jit(solution)/shard_map/ppermute | solution.py:466
  21.8 2.5 %forward.3 = (f32[2,8,1536]{2,1,0:T(8,128)S(1)}, f32[2,128,1536]{2,1,0:T(8,128)S(1)}, bf16[2,384,1536]{2,1,0:T(8,128)(2,1)S(1)}) custom-call(bf16[2,256,128]{2,1,0:T(8,128)(2,1)S(1)} %collective-permute-done.3.refs_0_.refs_2_, bf16[2,256,128]{2,1,0:T(8,128)(2,1)S(1)} %collective-permute-done.4.refs_1_.refs_3_, ...), custom_call_target="tpu_custom_call" | custom-call | flops 603979776 | bytes 3932160 | tf_op jit(solution)/shard_map/forward/pallas_call | solution.py:388
  24.3 0.0 collective-permute-done.1.refs_1_
  24.4 0.0 collective-permute-done.refs_0_
  24.4 0.0 collective-permute-done.2.refs_2_
  24.4 2.5 %forward.4 = (f32[2,8,1536]{2,1,0:T(8,128)S(1)}, f32[2,128,1536]{2,1,0:T(8,128)S(1)}, bf16[2,384,1536]{2,1,0:T(8,128)(2,1)S(1)}) custom-call(bf16[2,256,128]{2,1,0:T(8,128)(2,1)S(1)} %collective-permute-done.refs_0_, bf16[2,256,128]{2,1,0:T(8,128)(2,1)S(1)} %collective-permute-done.1.refs_1_, bf16[2,256,128]{2,1,0:T(8,128)(2,1)S(1)} %collective-permute-done.2.refs_2_, ...), custom_call_target="tpu_custom_call" | custom-call | flops 603979776 | bytes 3932160 | tf_op jit(solution)/shard_map/forward/pallas_call | solution.py:388
  26.9 4.3 %collective-permute-done.7.refs_0_ = bf16[2,256,128]{2,1,0:T(8,128)(2,1)S(1)} collective-permute-done((bf16[2,256,128]{2,1,0:T(8,128)(2,1)S(1)}, bf16[2,256,128]{2,1,0:T(8,128)(2,1)S(1)}, u32[]{:S(2)}, u32[]{:S(2)}) %collective-permute-start.7) | collective-permute-done | bytes 131104 | tf_op jit(solution)/shard_map/ppermute | solution.py:466
  31.2 1.0 %forward.5 = (f32[2,8,1536]{2,1,0:T(8,128)S(1)}, f32[2,128,1536]{2,1,0:T(8,128)S(1)}, bf16[2,128,1536]{2,1,0:T(8,128)(2,1)S(1)}) custom-call(bf16[2,256,128]{2,1,0:T(8,128)(2,1)S(1)} %collective-permute-done.7.refs_0_, bf16[2,128,1536]{2,1,0:T(8,128)(2,1)S(1)} %turned.2.refs_3_.refs_1_, f32[2,8,1536]{2,1,0:T(8,128)S(1)} %get-tuple-element.44.refs_2_.refs_4_, ...), custom_call_target="tpu_custom_call" | custom-call | flops 201326592 | bytes 3407872 | tf_op jit(solution)/shard_map/forward/pallas_call | solution.py:388
  32.3 2.1 %collective-permute-done.6.refs_0_ = bf16[2,256,128]{2,1,0:T(8,128)(2,1)S(1)} collective-permute-done((bf16[2,256,128]{2,1,0:T(8,128)(2,1)S(1)}, bf16[2,256,128]{2,1,0:T(8,128)(2,1)S(1)}, u32[]{:S(2)}, u32[]{:S(2)}) %collective-permute-start.6) | collective-permute-done | bytes 131104 | tf_op jit(solution)/shard_map/ppermute | solution.py:466
  34.4 2.5 %turn.1 = (f32[2,8,1536]{2,1,0:T(8,128)S(1)}, f32[2,128,1536]{2,1,0:T(8,128)S(1)}, f32[2,128,1536]{2,1,0:T(8,128)S(1)}, bf16[2,256,128]{2,1,0:T(8,128)(2,1)S(1)}) custom-call(bf16[2,256,128]{2,1,0:T(8,128)(2,1)S(1)} %collective-permute-done.6.refs_0_, bf16[1,1536,256]{2,1,0:T(8,128)(2,1)S(1)} %copy-done, bf16[1,1536,256]{2,1,0:T(8,128)(2,1)S(1)} %copy-done.1, ...), custom_call_target="tpu_custom_call" | custom-call | flops 603979776 | bytes 3407872 | tf_op jit(solution)/shard_map/turn/pallas_call | solution.py:402
  36.8 1.3 %backward.3 = (f32[2,128,1536]{2,1,0:T(8,128)S(1)}, bf16[2,256,128]{2,1,0:T(8,128)(2,1)S(1)}) custom-call(bf16[2,256,128]{2,1,0:T(8,128)(2,1)S(1)} %collective-permute-done.7.refs_0_, bf16[2,128,1536]{2,1,0:T(8,128)(2,1)S(1)} %get-tuple-element.51.refs_1_, f32[2,8,1536]{2,1,0:T(8,128)S(1)} %get-tuple-element.48.refs_5_.refs_2_, ...), custom_call_target="tpu_custom_call" | custom-call | flops 402653184 | bytes 3407872 | tf_op jit(solution)/shard_map/backward/pallas_call | solution.py:424
  38.1 0.1 collective-permute-start.8
  38.2 3.2 %collective-permute-start.9 = (bf16[2,256,128]{2,1,0:T(8,128)(2,1)S(1)}, bf16[2,256,128]{2,1,0:T(8,128)(2,1)S(1)}, u32[]{:S(2)}, u32[]{:S(2)}) collective-permute-start(bf16[2,256,128]{2,1,0:T(8,128)(2,1)S(1)} %get-tuple-element.57), channel_id=1, source_target_pairs={{12,0},{13,1},{14,2},{15,3},{8,4},{9,5},{10,6},{11,7},{20,8},{21,9... | collective-permute-start | bytes 393224 | tf_op jit(solution)/shard_map/ppermute | solution.py:474
  41.4 3.8 %backward.4 = (bf16[1,1536,256]{2,1,0:T(8,128)(2,1)}, f32[2,128,1536]{2,1,0:T(8,128)S(1)}, bf16[2,256,128]{2,1,0:T(8,128)(2,1)S(1)}, bf16[2,256,128]{2,1,0:T(8,128)(2,1)S(1)}, bf16[2,256,128]{2,1,0:T(8,128)(2,1)S(1)}) custom-call(bf16[2,256,128]{2,1,0:T(8,128)(2,1)S(1)} %collective-permute-done.refs_0_, ...), custom_call_target="tpu_custom_call" | custom-call | flops 1207959552 | bytes 3932160 | tf_op jit(solution)/shard_map/backward/pallas_call | solution.py:424
  45.1 1.7 %collective-permute-start.10 = (bf16[2,256,128]{2,1,0:T(8,128)(2,1)S(1)}, bf16[2,256,128]{2,1,0:T(8,128)(2,1)S(1)}, u32[]{:S(2)}, u32[]{:S(2)}) collective-permute-start(bf16[2,256,128]{2,1,0:T(8,128)(2,1)S(1)} %get-tuple-element.61), channel_id=1, source_target_pairs={{10,0},{11,1},{12,2},{13,3},{14,4},{15,5},{8,6},{9,7},{18,8},{19,9... | collective-permute-start | bytes 393224 | tf_op jit(solution)/shard_map/ppermute | solution.py:474
  46.8 0.1 collective-permute-start.11
  46.9 0.5 collective-permute-start.12
  47.4 2.0 %collective-permute-done.8.refs_0_ = bf16[2,256,128]{2,1,0:T(8,128)(2,1)S(1)} collective-permute-done((bf16[2,256,128]{2,1,0:T(8,128)(2,1)S(1)}, bf16[2,256,128]{2,1,0:T(8,128)(2,1)S(1)}, u32[]{:S(2)}, u32[]{:S(2)}) %collective-permute-start.8) | collective-permute-done | bytes 131104 | tf_op jit(solution)/shard_map/ppermute | solution.py:474
  49.4 5.3 %collective-permute-done.9.refs_1_ = bf16[2,256,128]{2,1,0:T(8,128)(2,1)S(1)} collective-permute-done((bf16[2,256,128]{2,1,0:T(8,128)(2,1)S(1)}, bf16[2,256,128]{2,1,0:T(8,128)(2,1)S(1)}, u32[]{:S(2)}, u32[]{:S(2)}) %collective-permute-start.9) | collective-permute-done | bytes 131104 | tf_op jit(solution)/shard_map/ppermute | solution.py:474
  54.7 3.7 %backward.5 = (bf16[1,1536,256]{2,1,0:T(8,128)(2,1)}, bf16[2,256,128]{2,1,0:T(8,128)(2,1)S(1)}, bf16[2,256,128]{2,1,0:T(8,128)(2,1)S(1)}, bf16[2,256,128]{2,1,0:T(8,128)(2,1)S(1)}) custom-call(bf16[2,256,128]{2,1,0:T(8,128)(2,1)S(1)} %collective-permute-done.8.refs_0_, bf16[2,256,128]{2,1,0:T(8,128)(2,1)S(1)} %collective-permute-done.9.refs_1_, ...), custom_call_target="tpu_custom_call" | custom-call | flops 1207959552 | bytes 3932160 | tf_op jit(solution)/shard_map/backward/pallas_call | solution.py:424
  58.4 2.5 %collective-permute-start.13 = (bf16[2,256,128]{2,1,0:T(8,128)(2,1)S(1)}, bf16[2,256,128]{2,1,0:T(8,128)(2,1)S(1)}, u32[]{:S(2)}, u32[]{:S(2)}) collective-permute-start(bf16[2,256,128]{2,1,0:T(8,128)(2,1)S(1)} %get-tuple-element.64), channel_id=1, source_target_pairs={{11,0},{10,1},{13,2},{12,3},{15,4},{14,5},{9,6},{8,7},{19,8},{18,9... | collective-permute-start | bytes 393224 | tf_op jit(solution)/shard_map/ppermute | solution.py:474
  60.9 1.1 %collective-permute-start.14 = (bf16[2,256,128]{2,1,0:T(8,128)(2,1)S(1)}, bf16[2,256,128]{2,1,0:T(8,128)(2,1)S(1)}, u32[]{:S(2)}, u32[]{:S(2)}) collective-permute-start(bf16[2,256,128]{2,1,0:T(8,128)(2,1)S(1)} %get-tuple-element.65), channel_id=1, source_target_pairs={{9,0},{8,1},{11,2},{10,3},{13,4},{12,5},{15,6},{14,7},{17,8},{16,9... | collective-permute-start | bytes 393224 | tf_op jit(solution)/shard_map/ppermute | solution.py:474
  62.0 0.0 collective-permute-done.10
  62.0 0.4 collective-permute-start.15
  62.4 0.0 collective-permute-done.11
  62.4 0.0 collective-permute-done.12
  62.4 2.5 %collective-permute-done.13 = bf16[2,256,128]{2,1,0:T(8,128)(2,1)S(1)} collective-permute-done((bf16[2,256,128]{2,1,0:T(8,128)(2,1)S(1)}, bf16[2,256,128]{2,1,0:T(8,128)(2,1)S(1)}, u32[]{:S(2)}, u32[]{:S(2)}) %collective-permute-start.13) | collective-permute-done | bytes 131104 | tf_op jit(solution)/shard_map/ppermute | solution.py:474
  64.8 2.0 %collective-permute-done.14 = bf16[2,256,128]{2,1,0:T(8,128)(2,1)S(1)} collective-permute-done((bf16[2,256,128]{2,1,0:T(8,128)(2,1)S(1)}, bf16[2,256,128]{2,1,0:T(8,128)(2,1)S(1)}, u32[]{:S(2)}, u32[]{:S(2)}) %collective-permute-start.14) | collective-permute-done | bytes 131104 | tf_op jit(solution)/shard_map/ppermute | solution.py:474
  66.9 2.7 %collective-permute-done.15 = bf16[2,256,128]{2,1,0:T(8,128)(2,1)S(1)} collective-permute-done((bf16[2,256,128]{2,1,0:T(8,128)(2,1)S(1)}, bf16[2,256,128]{2,1,0:T(8,128)(2,1)S(1)}, u32[]{:S(2)}, u32[]{:S(2)}) %collective-permute-start.15) | collective-permute-done | bytes 131104 | tf_op jit(solution)/shard_map/ppermute | solution.py:474
  69.6 1.5 %unpack.1 = bf16[1,128,2,2048]{3,2,1,0:T(2,128)(2,1)} custom-call(bf16[2,128,2,128]{3,2,1,0:T(2,128)(2,1)S(1)} %bitcast.17, bf16[2,128,2,128]{3,2,1,0:T(2,128)(2,1)S(1)} %bitcast.16, bf16[2,128,2,128]{3,2,1,0:T(2,128)(2,1)S(1)} %bitcast.18, bf16[2,128,2,128]{3,2,1,0:T(2,128)(2,1)S(1)} %bitcast.19, bf16[2,128,2,128]{3,2,1,0:T(2,128)(2,1)S(1)} %bitcast.20, ...), custom_call_target="tpu_custom_call" | custom-call | tf_op jit(solution)/shard_map/unpack/pallas_call | solution.py:115
Async XLA Ops:
  0.6 19.4 %copy-start = (bf16[1,1536,256]{2,1,0:T(8,128)(2,1)S(1)}, bf16[1,1536,256]{2,1,0:T(8,128)(2,1)}, u32[]{:S(2)}) copy-start(bf16[1,1536,256]{2,1,0:T(8,128)(2,1)} %refs_7_.1) | copy-start | bytes 2359300
  0.6 1.3 %copy-start.2 = (bf16[1,128,2,2048]{3,2,1,0:T(2,128)(2,1)S(1)}, bf16[1,128,2,2048]{3,2,1,0:T(2,128)(2,1)}, u32[]{:S(2)}) copy-start(bf16[1,128,2,2048]{3,2,1,0:T(2,128)(2,1)} %pairs_ref.1) | copy-start | bytes 3145732
  1.9 18.3 %copy-start.1 = (bf16[1,1536,256]{2,1,0:T(8,128)(2,1)S(1)}, bf16[1,1536,256]{2,1,0:T(8,128)(2,1)}, u32[]{:S(2)}) copy-start(bf16[1,1536,256]{2,1,0:T(8,128)(2,1)} %refs_8_.1) | copy-start | bytes 2359300
  2.9 10.6 %collective-permute-start.3 = (bf16[2,256,128]{2,1,0:T(8,128)(2,1)S(1)}, bf16[2,256,128]{2,1,0:T(8,128)(2,1)S(1)}, u32[]{:S(2)}, u32[]{:S(2)}) collective-permute-start(bf16[2,256,128]{2,1,0:T(8,128)(2,1)S(1)} %bitcast.31), channel_id=1, source_target_pairs={{0,11},{1,10},{2,13},{3,12},{4,15},{5,14},{6,9},{7,8},{8,19},{9,18... | collective-permute-start | bytes 393224 | tf_op jit(solution)/shard_map/ppermute | solution.py:466
  6.4 10.9 %collective-permute-start.4 = (bf16[2,256,128]{2,1,0:T(8,128)(2,1)S(1)}, bf16[2,256,128]{2,1,0:T(8,128)(2,1)S(1)}, u32[]{:S(2)}, u32[]{:S(2)}) collective-permute-start(bf16[2,256,128]{2,1,0:T(8,128)(2,1)S(1)} %bitcast.30), channel_id=1, source_target_pairs={{0,9},{1,8},{2,11},{3,10},{4,13},{5,12},{6,15},{7,14},{8,17},{9,16... | collective-permute-start | bytes 393224 | tf_op jit(solution)/shard_map/ppermute | solution.py:466
  8.1 12.5 %collective-permute-start.5 = (bf16[2,256,128]{2,1,0:T(8,128)(2,1)S(1)}, bf16[2,256,128]{2,1,0:T(8,128)(2,1)S(1)}, u32[]{:S(2)}, u32[]{:S(2)}) collective-permute-start(bf16[2,256,128]{2,1,0:T(8,128)(2,1)S(1)} %bitcast.29), channel_id=1, source_target_pairs={{0,15},{1,14},{2,9},{3,8},{4,11},{5,10},{6,13},{7,12},{8,23},{9,22... | collective-permute-start | bytes 393224 | tf_op jit(solution)/shard_map/ppermute | solution.py:466
  10.7 13.6 %collective-permute-start.1 = (bf16[2,256,128]{2,1,0:T(8,128)(2,1)S(1)}, bf16[2,256,128]{2,1,0:T(8,128)(2,1)S(1)}, u32[]{:S(2)}, u32[]{:S(2)}) collective-permute-start(bf16[2,256,128]{2,1,0:T(8,128)(2,1)S(1)} %bitcast.28), channel_id=1, source_target_pairs={{0,14},{1,15},{2,8},{3,9},{4,10},{5,11},{6,12},{7,13},{8,22},{9,23... | collective-permute-start | bytes 393224 | tf_op jit(solution)/shard_map/ppermute | solution.py:466
  12.8 11.6 %collective-permute-start = (bf16[2,256,128]{2,1,0:T(8,128)(2,1)S(1)}, bf16[2,256,128]{2,1,0:T(8,128)(2,1)S(1)}, u32[]{:S(2)}, u32[]{:S(2)}) collective-permute-start(bf16[2,256,128]{2,1,0:T(8,128)(2,1)S(1)} %bitcast.27), channel_id=1, source_target_pairs={{0,10},{1,11},{2,12},{3,13},{4,14},{5,15},{6,8},{7,9},{8,18},{9,19... | collective-permute-start | bytes 393224 | tf_op jit(solution)/shard_map/ppermute | solution.py:466
  13.4 10.9 %collective-permute-start.2 = (bf16[2,256,128]{2,1,0:T(8,128)(2,1)S(1)}, bf16[2,256,128]{2,1,0:T(8,128)(2,1)S(1)}, u32[]{:S(2)}, u32[]{:S(2)}) collective-permute-start(bf16[2,256,128]{2,1,0:T(8,128)(2,1)S(1)} %bitcast.26), channel_id=1, source_target_pairs={{0,8},{1,9},{2,10},{3,11},{4,12},{5,13},{6,14},{7,15},{8,16},{9,17... | collective-permute-start | bytes 393224 | tf_op jit(solution)/shard_map/ppermute | solution.py:466
  17.3 14.0 %collective-permute-start.7 = (bf16[2,256,128]{2,1,0:T(8,128)(2,1)S(1)}, bf16[2,256,128]{2,1,0:T(8,128)(2,1)S(1)}, u32[]{:S(2)}, u32[]{:S(2)}) collective-permute-start(bf16[2,256,128]{2,1,0:T(8,128)(2,1)S(1)} %bitcast.25), channel_id=1, source_target_pairs={{0,13},{1,12},{2,15},{3,14},{4,9},{5,8},{6,11},{7,10},{8,21},{9,20... | collective-permute-start | bytes 393224 | tf_op jit(solution)/shard_map/ppermute | solution.py:466
  20.6 13.8 %collective-permute-start.6 = (bf16[2,256,128]{2,1,0:T(8,128)(2,1)S(1)}, bf16[2,256,128]{2,1,0:T(8,128)(2,1)S(1)}, u32[]{:S(2)}, u32[]{:S(2)}) collective-permute-start(bf16[2,256,128]{2,1,0:T(8,128)(2,1)S(1)} %bitcast.24), channel_id=1, source_target_pairs={{0,12},{1,13},{2,14},{3,15},{4,8},{5,9},{6,10},{7,11},{8,20},{9,21... | collective-permute-start | bytes 393224 | tf_op jit(solution)/shard_map/ppermute | solution.py:466
  38.1 11.3 %collective-permute-start.8 = (bf16[2,256,128]{2,1,0:T(8,128)(2,1)S(1)}, bf16[2,256,128]{2,1,0:T(8,128)(2,1)S(1)}, u32[]{:S(2)}, u32[]{:S(2)}) collective-permute-start(bf16[2,256,128]{2,1,0:T(8,128)(2,1)S(1)} %get-tuple-element.56), channel_id=1, source_target_pairs={{13,0},{12,1},{15,2},{14,3},{9,4},{8,5},{11,6},{10,7},{21,8},{20,9... | collective-permute-start | bytes 393224 | tf_op jit(solution)/shard_map/ppermute | solution.py:474
  38.2 16.5 %collective-permute-start.9 = (bf16[2,256,128]{2,1,0:T(8,128)(2,1)S(1)}, bf16[2,256,128]{2,1,0:T(8,128)(2,1)S(1)}, u32[]{:S(2)}, u32[]{:S(2)}) collective-permute-start(bf16[2,256,128]{2,1,0:T(8,128)(2,1)S(1)} %get-tuple-element.57), channel_id=1, source_target_pairs={{12,0},{13,1},{14,2},{15,3},{8,4},{9,5},{10,6},{11,7},{20,8},{21,9... | collective-permute-start | bytes 393224 | tf_op jit(solution)/shard_map/ppermute | solution.py:474
  45.1 16.9 %collective-permute-start.10 = (bf16[2,256,128]{2,1,0:T(8,128)(2,1)S(1)}, bf16[2,256,128]{2,1,0:T(8,128)(2,1)S(1)}, u32[]{:S(2)}, u32[]{:S(2)}) collective-permute-start(bf16[2,256,128]{2,1,0:T(8,128)(2,1)S(1)} %get-tuple-element.61), channel_id=1, source_target_pairs={{10,0},{11,1},{12,2},{13,3},{14,4},{15,5},{8,6},{9,7},{18,8},{19,9... | collective-permute-start | bytes 393224 | tf_op jit(solution)/shard_map/ppermute | solution.py:474
  46.8 15.6 %collective-permute-start.11 = (bf16[2,256,128]{2,1,0:T(8,128)(2,1)S(1)}, bf16[2,256,128]{2,1,0:T(8,128)(2,1)S(1)}, u32[]{:S(2)}, u32[]{:S(2)}) collective-permute-start(bf16[2,256,128]{2,1,0:T(8,128)(2,1)S(1)} %get-tuple-element.62), channel_id=1, source_target_pairs={{14,0},{15,1},{8,2},{9,3},{10,4},{11,5},{12,6},{13,7},{22,8},{23,9... | collective-permute-start | bytes 393224 | tf_op jit(solution)/shard_map/ppermute | solution.py:474
  46.9 15.5 %collective-permute-start.12 = (bf16[2,256,128]{2,1,0:T(8,128)(2,1)S(1)}, bf16[2,256,128]{2,1,0:T(8,128)(2,1)S(1)}, u32[]{:S(2)}, u32[]{:S(2)}) collective-permute-start(bf16[2,256,128]{2,1,0:T(8,128)(2,1)S(1)} %get-tuple-element.63), channel_id=1, source_target_pairs={{8,0},{9,1},{10,2},{11,3},{12,4},{13,5},{14,6},{15,7},{16,8},{17,9... | collective-permute-start | bytes 393224 | tf_op jit(solution)/shard_map/ppermute | solution.py:474
  58.4 6.4 %collective-permute-start.13 = (bf16[2,256,128]{2,1,0:T(8,128)(2,1)S(1)}, bf16[2,256,128]{2,1,0:T(8,128)(2,1)S(1)}, u32[]{:S(2)}, u32[]{:S(2)}) collective-permute-start(bf16[2,256,128]{2,1,0:T(8,128)(2,1)S(1)} %get-tuple-element.64), channel_id=1, source_target_pairs={{11,0},{10,1},{13,2},{12,3},{15,4},{14,5},{9,6},{8,7},{19,8},{18,9... | collective-permute-start | bytes 393224 | tf_op jit(solution)/shard_map/ppermute | solution.py:474
  60.9 5.9 %collective-permute-start.14 = (bf16[2,256,128]{2,1,0:T(8,128)(2,1)S(1)}, bf16[2,256,128]{2,1,0:T(8,128)(2,1)S(1)}, u32[]{:S(2)}, u32[]{:S(2)}) collective-permute-start(bf16[2,256,128]{2,1,0:T(8,128)(2,1)S(1)} %get-tuple-element.65), channel_id=1, source_target_pairs={{9,0},{8,1},{11,2},{10,3},{13,4},{12,5},{15,6},{14,7},{17,8},{16,9... | collective-permute-start | bytes 393224 | tf_op jit(solution)/shard_map/ppermute | solution.py:474
  62.0 7.6 %collective-permute-start.15 = (bf16[2,256,128]{2,1,0:T(8,128)(2,1)S(1)}, bf16[2,256,128]{2,1,0:T(8,128)(2,1)S(1)}, u32[]{:S(2)}, u32[]{:S(2)}) collective-permute-start(bf16[2,256,128]{2,1,0:T(8,128)(2,1)S(1)} %get-tuple-element.66), channel_id=1, source_target_pairs={{15,0},{14,1},{9,2},{8,3},{11,4},{10,5},{13,6},{12,7},{23,8},{22,9... | collective-permute-start | bytes 393224 | tf_op jit(solution)/shard_map/ppermute | solution.py:474

commit v16 on v14

--- a/solution.py
+++ b/solution.py
@@ -29,8 +29,8 @@
     half = len(short) // 2
     return [
         short[:1] + near[:1] + short[1:half],
-        short[half + eighth :] + near[1:],
-        short[half : half + eighth] + long[:eighth],
+        short[half:] + near[1:],
+        long[:eighth],
         long[eighth:],
     ]
 
@@ -407,8 +407,8 @@
     )(*group, queries, upstream, qt, gt, *state)
     returned = [send_back(len(groups) - 1, grads)]
 
-    for part in ([len(groups) - 2], list(range(len(groups) - 3, -1, -1))):
-        first = part[-1] > 0
+    for part in (list(range(len(groups) - 2, 0, -1)), [0]):
+        first = part != [0]
         counts = [len(groups[i]) for i in part]
         back = [] if first else returned[0]
         operands = []

time: 72.3 us -> 67 us (0.927)
  waiting for transfers between devices: 21.3 us -> 13.4 us
  starting transfers between devices: 28.6 us -> 31.1 us
    ppermute x8, waiting for transfers between devices: 10.3 us -> 6.22 us  [shards(): blocks.append(lax.ppermute(block, AXES, route(offset, False)))]
    ppermute x8, waiting for transfers between devices: 11 us -> 7.19 us  [send_back(): lax.ppermute(g, AXES, route(o, True))]
    ppermute x8, starting transfers between devices: 13.5 us -> 16.9 us  [shards(): blocks.append(lax.ppermute(block, AXES, route(offset, False)))]
    ppermute x8, starting transfers between devices: 15.1 us -> 14.2 us  [send_back(): lax.ppermute(g, AXES, route(o, True))]
  transfers between devices with their start and end apart: 16 -> 16, of which waited for: 8 -> 6; matrix products, arithmetic and copies ran while one was open for 0% -> 0% of each run, Pallas kernels for 21% -> 23%
where the time goes in v16:
time: 67 us; the launch traced here: 66.9 us
  starting transfers between devices  31.1 us (46%)
  Pallas kernels  20.1 us (30%)
  waiting for transfers between devices  13.4 us (20%)
  local copies, waits for them, and re-layouts  1.3 us (2%)
  between operations  0.91 us (1%)
    ppermute x8, starting transfers between devices, shards(): blocks.append(lax.ppermute(block, AXES, route(offset, False)))  16.9 us
    ppermute x8, starting transfers between devices, send_back(): lax.ppermute(g, AXES, route(o, True))  14.2 us
    pallas_call x2, Pallas kernels, attend(): pl.pallas_call(functools.partial(backward_kernel, len(back), counts, firs...  8.59 us
    ppermute x8, waiting for transfers between devices, send_back(): lax.ppermute(g, AXES, route(o, True))  7.19 us
    ppermute x8, waiting for transfers between devices, shards(): blocks.append(lax.ppermute(block, AXES, route(offset, False)))  6.22 us
    pallas_call x3, Pallas kernels, attend(): pl.pallas_call(functools.partial(forward_kernel, count, not state, tile_o...  6.11 us
    pallas_call x1, Pallas kernels, attend(): pl.pallas_call(functools.partial(turn_kernel, count, tile_of(count * rows...  2.45 us
    pallas_call x1, Pallas kernels, unpack(): pl.pallas_call(kernel, out_shape=jax.ShapeDtypeStruct((1, rows, 2, width)...  1.5 us
  transfers between devices with their start and end apart: 16, of which 6 were waited for; matrix products, arithmetic and copies ran while one was open for 0% of the time, Pallas kernels for 23%

profile of v16, /device:TPU:0, one launch (start us, length us, event | category | flops | bytes accessed | tf_op | source)
XLA Modules:
  0.0 66.9 jit_solution(4874904103094309242)
XLA Ops:
  0.6 0.0 copy-start
  0.6 0.0 copy-start.2
  0.7 1.3 %copy-done.2 = bf16[1,128,2,2048]{3,2,1,0:T(2,128)(2,1)S(1)} copy-done((bf16[1,128,2,2048]{3,2,1,0:T(2,128)(2,1)S(1)}, bf16[1,128,2,2048]{3,2,1,0:T(2,128)(2,1)}, u32[]{:S(2)}) %copy-start.2) | copy-done | bytes 1048600
  1.9 0.0 copy-start.1
  1.9 0.9 %pack.1 = (bf16[2,128,2,128]{3,2,1,0:T(2,128)(2,1)S(1)}, bf16[2,128,2,128]{3,2,1,0:T(2,128)(2,1)S(1)}, bf16[2,128,2,128]{3,2,1,0:T(2,128)(2,1)S(1)}, bf16[2,128,...) custom-call(bf16[1,128,2,2048]{3,2,1,0:T(2,128)(2,1)S(1)} %copy-done.2), custom_call_target="tpu_custom_call" | custom-call | tf_op jit(solution)/shard_map/pack/pallas_call | solution.py:79
  2.9 3.5 %collective-permute-start.4 = (bf16[2,256,128]{2,1,0:T(8,128)(2,1)S(1)}, bf16[2,256,128]{2,1,0:T(8,128)(2,1)S(1)}, u32[]{:S(2)}, u32[]{:S(2)}) collective-permute-start(bf16[2,256,128]{2,1,0:T(8,128)(2,1)S(1)} %bitcast.31), channel_id=1, source_target_pairs={{0,11},{1,10},{2,13},{3,12},{4,15},{5,14},{6,9},{7,8},{8,19},{9,18... | collective-permute-start | bytes 393224 | tf_op jit(solution)/shard_map/ppermute | solution.py:454
  6.4 1.7 %collective-permute-start.5 = (bf16[2,256,128]{2,1,0:T(8,128)(2,1)S(1)}, bf16[2,256,128]{2,1,0:T(8,128)(2,1)S(1)}, u32[]{:S(2)}, u32[]{:S(2)}) collective-permute-start(bf16[2,256,128]{2,1,0:T(8,128)(2,1)S(1)} %bitcast.30), channel_id=1, source_target_pairs={{0,9},{1,8},{2,11},{3,10},{4,13},{5,12},{6,15},{7,14},{8,17},{9,16... | collective-permute-start | bytes 393224 | tf_op jit(solution)/shard_map/ppermute | solution.py:454
  8.1 2.6 %collective-permute-start.6 = (bf16[2,256,128]{2,1,0:T(8,128)(2,1)S(1)}, bf16[2,256,128]{2,1,0:T(8,128)(2,1)S(1)}, u32[]{:S(2)}, u32[]{:S(2)}) collective-permute-start(bf16[2,256,128]{2,1,0:T(8,128)(2,1)S(1)} %bitcast.29), channel_id=1, source_target_pairs={{0,15},{1,14},{2,9},{3,8},{4,11},{5,10},{6,13},{7,12},{8,23},{9,22... | collective-permute-start | bytes 393224 | tf_op jit(solution)/shard_map/ppermute | solution.py:454
  10.7 0.0 collective-permute-start.1
  10.8 3.5 %collective-permute-start.2 = (bf16[2,256,128]{2,1,0:T(8,128)(2,1)S(1)}, bf16[2,256,128]{2,1,0:T(8,128)(2,1)S(1)}, u32[]{:S(2)}, u32[]{:S(2)}) collective-permute-start(bf16[2,256,128]{2,1,0:T(8,128)(2,1)S(1)} %bitcast.27), channel_id=1, source_target_pairs={{0,14},{1,15},{2,8},{3,9},{4,10},{5,11},{6,12},{7,13},{8,22},{9,23... | collective-permute-start | bytes 393224 | tf_op jit(solution)/shard_map/ppermute | solution.py:454
  14.2 0.0 collective-permute-done.4.refs_0_.refs_1_
  14.2 1.6 %collective-permute-start.3 = (bf16[2,256,128]{2,1,0:T(8,128)(2,1)S(1)}, bf16[2,256,128]{2,1,0:T(8,128)(2,1)S(1)}, u32[]{:S(2)}, u32[]{:S(2)}) collective-permute-start(bf16[2,256,128]{2,1,0:T(8,128)(2,1)S(1)} %bitcast.26), channel_id=1, source_target_pairs={{0,8},{1,9},{2,10},{3,11},{4,12},{5,13},{6,14},{7,15},{8,16},{9,17... | collective-permute-start | bytes 393224 | tf_op jit(solution)/shard_map/ppermute | solution.py:454
  15.8 1.4 %collective-permute-done.5.refs_1_.refs_2_ = bf16[2,256,128]{2,1,0:T(8,128)(2,1)S(1)} collective-permute-done((bf16[2,256,128]{2,1,0:T(8,128)(2,1)S(1)}, bf16[2,256,128]{2,1,0:T(8,128)(2,1)S(1)}, u32[]{:S(2)}, u32[]{:S(2)}) %collective-permute-start.5) | collective-permute-done | bytes 131104 | tf_op jit(solution)/shard_map/ppermute | solution.py:454
  17.3 2.7 %collective-permute-start = (bf16[2,256,128]{2,1,0:T(8,128)(2,1)S(1)}, bf16[2,256,128]{2,1,0:T(8,128)(2,1)S(1)}, u32[]{:S(2)}, u32[]{:S(2)}) collective-permute-start(bf16[2,256,128]{2,1,0:T(8,128)(2,1)S(1)} %bitcast.25), channel_id=1, source_target_pairs={{0,13},{1,12},{2,15},{3,14},{4,9},{5,8},{6,11},{7,10},{8,21},{9,20... | collective-permute-start | bytes 393224 | tf_op jit(solution)/shard_map/ppermute | solution.py:454
  20.0 0.0 copy-done
  20.0 0.3 turned.2.refs_3_.refs_1_
  20.3 0.0 copy-done.1
  20.3 0.3 turned.3.refs_4_.refs_10_.refs_8_
  20.6 0.0 collective-permute-done.6.refs_2_.refs_3_
  20.6 1.2 %collective-permute-start.7 = (bf16[2,256,128]{2,1,0:T(8,128)(2,1)S(1)}, bf16[2,256,128]{2,1,0:T(8,128)(2,1)S(1)}, u32[]{:S(2)}, u32[]{:S(2)}) collective-permute-start(bf16[2,256,128]{2,1,0:T(8,128)(2,1)S(1)} %bitcast.24), channel_id=1, source_target_pairs={{0,12},{1,13},{2,14},{3,15},{4,8},{5,9},{6,10},{7,11},{8,20},{9,21... | collective-permute-start | bytes 393224 | tf_op jit(solution)/shard_map/ppermute | solution.py:454
  21.8 2.5 %forward.3 = (f32[2,8,1536]{2,1,0:T(8,128)S(1)}, f32[2,128,1536]{2,1,0:T(8,128)S(1)}, bf16[2,384,1536]{2,1,0:T(8,128)(2,1)S(1)}) custom-call(bf16[2,256,128]{2,1,0:T(8,128)(2,1)S(1)} %collective-permute-done.4.refs_0_.refs_1_, bf16[2,256,128]{2,1,0:T(8,128)(2,1)S(1)} %collective-permute-done.5.refs_1_.refs_2_, ...), custom_call_target="tpu_custom_call" | custom-call | flops 603979776 | bytes 3932160 | tf_op jit(solution)/shard_map/forward/pallas_call | solution.py:383
  24.3 0.0 collective-permute-done.1.refs_0_.refs_3_
  24.4 0.0 collective-permute-done.2.refs_1_.refs_4_
  24.4 0.0 collective-permute-done.3.refs_2_.refs_5_
  24.4 2.5 %forward.4 = (f32[2,8,1536]{2,1,0:T(8,128)S(1)}, f32[2,128,1536]{2,1,0:T(8,128)S(1)}, bf16[2,384,1536]{2,1,0:T(8,128)(2,1)S(1)}) custom-call(bf16[2,256,128]{2,1,0:T(8,128)(2,1)S(1)} %collective-permute-done.1.refs_0_.refs_3_, bf16[2,256,128]{2,1,0:T(8,128)(2,1)S(1)} %collective-permute-done.2.refs_1_.refs_4_, ...), custom_call_target="tpu_custom_call" | custom-call | flops 603979776 | bytes 3932160 | tf_op jit(solution)/shard_map/forward/pallas_call | solution.py:383
  26.9 4.4 %collective-permute-done.refs_0_ = bf16[2,256,128]{2,1,0:T(8,128)(2,1)S(1)} collective-permute-done((bf16[2,256,128]{2,1,0:T(8,128)(2,1)S(1)}, bf16[2,256,128]{2,1,0:T(8,128)(2,1)S(1)}, u32[]{:S(2)}, u32[]{:S(2)}) %collective-permute-start) | collective-permute-done | bytes 131104 | tf_op jit(solution)/shard_map/ppermute | solution.py:454
  31.3 1.0 %forward.5 = (f32[2,8,1536]{2,1,0:T(8,128)S(1)}, f32[2,128,1536]{2,1,0:T(8,128)S(1)}, bf16[2,128,1536]{2,1,0:T(8,128)(2,1)S(1)}) custom-call(bf16[2,256,128]{2,1,0:T(8,128)(2,1)S(1)} %collective-permute-done.refs_0_, bf16[2,128,1536]{2,1,0:T(8,128)(2,1)S(1)} %turned.2.refs_3_.refs_1_, f32[2,8,1536]{2,1,0:T(8,128)S(1)} %get-tuple-element.43.refs_2_.refs_7_, ...), custom_call_target="tpu_custom_call" | custom-call | flops 201326592 | bytes 3407872 | tf_op jit(solution)/shard_map/forward/pallas_call | solution.py:383
  32.3 0.4 collective-permute-done.7.refs_0_
  32.7 2.4 %turn.1 = (f32[2,8,1536]{2,1,0:T(8,128)S(1)}, f32[2,128,1536]{2,1,0:T(8,128)S(1)}, f32[2,128,1536]{2,1,0:T(8,128)S(1)}, bf16[2,256,128]{2,1,0:T(8,128)(2,1)S(1)}) custom-call(bf16[2,256,128]{2,1,0:T(8,128)(2,1)S(1)} %collective-permute-done.7.refs_0_, bf16[1,1536,256]{2,1,0:T(8,128)(2,1)S(1)} %copy-done, bf16[1,1536,256]{2,1,0:T(8,128)(2,1)S(1)} %copy-done.1, ...), custom_call_target="tpu_custom_call" | custom-call | flops 603979776 | bytes 3407872 | tf_op jit(solution)/shard_map/turn/pallas_call | solution.py:397
  35.2 0.2 collective-permute-start.8
  35.4 4.9 %backward.2 = (bf16[1,1536,256]{2,1,0:T(8,128)(2,1)}, f32[2,128,1536]{2,1,0:T(8,128)S(1)}, bf16[2,256,128]{2,1,0:T(8,128)(2,1)S(1)}, bf16[2,256,128]{2,1,0:T(8,1...) custom-call(bf16[2,256,128]{2,1,0:T(8,128)(2,1)S(1)} %collective-permute-done.refs_0_, ...), custom_call_target="tpu_custom_call" | custom-call | flops 1610612736 | bytes 4194304 | tf_op jit(solution)/shard_map/backward/pallas_call | solution.py:419
  40.3 4.8 %collective-permute-start.9 = (bf16[2,256,128]{2,1,0:T(8,128)(2,1)S(1)}, bf16[2,256,128]{2,1,0:T(8,128)(2,1)S(1)}, u32[]{:S(2)}, u32[]{:S(2)}) collective-permute-start(bf16[2,256,128]{2,1,0:T(8,128)(2,1)S(1)} %get-tuple-element.58), channel_id=1, source_target_pairs={{13,0},{12,1},{15,2},{14,3},{9,4},{8,5},{11,6},{10,7},{21,8},{20,9... | collective-permute-start | bytes 393224 | tf_op jit(solution)/shard_map/ppermute | solution.py:462
  45.1 1.7 %collective-permute-start.10 = (bf16[2,256,128]{2,1,0:T(8,128)(2,1)S(1)}, bf16[2,256,128]{2,1,0:T(8,128)(2,1)S(1)}, u32[]{:S(2)}, u32[]{:S(2)}) collective-permute-start(bf16[2,256,128]{2,1,0:T(8,128)(2,1)S(1)} %get-tuple-element.59), channel_id=1, source_target_pairs={{10,0},{11,1},{12,2},{13,3},{14,4},{15,5},{8,6},{9,7},{18,8},{19,9... | collective-permute-start | bytes 393224 | tf_op jit(solution)/shard_map/ppermute | solution.py:462
  46.8 0.1 collective-permute-start.11
  46.9 0.4 collective-permute-start.12
  47.3 0.0 collective-permute-done.8.refs_0_
  47.3 3.7 %backward.3 = (bf16[1,1536,256]{2,1,0:T(8,128)(2,1)}, bf16[2,256,128]{2,1,0:T(8,128)(2,1)S(1)}, bf16[2,256,128]{2,1,0:T(8,128)(2,1)S(1)}, bf16[2,256,128]{2,1,0:T(8,128)(2,1)S(1)}) custom-call(bf16[2,256,128]{2,1,0:T(8,128)(2,1)S(1)} %collective-permute-done.8.refs_0_, bf16[2,256,128]{2,1,0:T(8,128)(2,1)S(1)} %collective-permute-done.4.refs_0_.refs_1_, ...), custom_call_target="tpu_custom_call" | custom-call | flops 1207959552 | bytes 3932160 | tf_op jit(solution)/shard_map/backward/pallas_call | solution.py:419
  51.0 4.1 %collective-permute-start.13 = (bf16[2,256,128]{2,1,0:T(8,128)(2,1)S(1)}, bf16[2,256,128]{2,1,0:T(8,128)(2,1)S(1)}, u32[]{:S(2)}, u32[]{:S(2)}) collective-permute-start(bf16[2,256,128]{2,1,0:T(8,128)(2,1)S(1)} %get-tuple-element.62), channel_id=1, source_target_pairs={{11,0},{10,1},{13,2},{12,3},{15,4},{14,5},{9,6},{8,7},{19,8},{18,9... | collective-permute-start | bytes 393224 | tf_op jit(solution)/shard_map/ppermute | solution.py:462
  55.1 0.0 collective-permute-done.9
  55.1 1.6 %collective-permute-start.14 = (bf16[2,256,128]{2,1,0:T(8,128)(2,1)S(1)}, bf16[2,256,128]{2,1,0:T(8,128)(2,1)S(1)}, u32[]{:S(2)}, u32[]{:S(2)}) collective-permute-start(bf16[2,256,128]{2,1,0:T(8,128)(2,1)S(1)} %get-tuple-element.63), channel_id=1, source_target_pairs={{9,0},{8,1},{11,2},{10,3},{13,4},{12,5},{15,6},{14,7},{17,8},{16,9... | collective-permute-start | bytes 393224 | tf_op jit(solution)/shard_map/ppermute | solution.py:462
  56.7 0.0 collective-permute-done.10
  56.7 1.3 %collective-permute-start.15 = (bf16[2,256,128]{2,1,0:T(8,128)(2,1)S(1)}, bf16[2,256,128]{2,1,0:T(8,128)(2,1)S(1)}, u32[]{:S(2)}, u32[]{:S(2)}) collective-permute-start(bf16[2,256,128]{2,1,0:T(8,128)(2,1)S(1)} %get-tuple-element.64), channel_id=1, source_target_pairs={{15,0},{14,1},{9,2},{8,3},{11,4},{10,5},{13,6},{12,7},{23,8},{22,9... | collective-permute-start | bytes 393224 | tf_op jit(solution)/shard_map/ppermute | solution.py:462
  58.0 0.0 collective-permute-done.11
  58.0 0.0 collective-permute-done.12
  58.0 1.1 %collective-permute-done.13 = bf16[2,256,128]{2,1,0:T(8,128)(2,1)S(1)} collective-permute-done((bf16[2,256,128]{2,1,0:T(8,128)(2,1)S(1)}, bf16[2,256,128]{2,1,0:T(8,128)(2,1)S(1)}, u32[]{:S(2)}, u32[]{:S(2)}) %collective-permute-start.13) | collective-permute-done | bytes 131104 | tf_op jit(solution)/shard_map/ppermute | solution.py:462
  59.1 3.2 %collective-permute-done.14 = bf16[2,256,128]{2,1,0:T(8,128)(2,1)S(1)} collective-permute-done((bf16[2,256,128]{2,1,0:T(8,128)(2,1)S(1)}, bf16[2,256,128]{2,1,0:T(8,128)(2,1)S(1)}, u32[]{:S(2)}, u32[]{:S(2)}) %collective-permute-start.14) | collective-permute-done | bytes 131104 | tf_op jit(solution)/shard_map/ppermute | solution.py:462
  62.3 2.9 %collective-permute-done.15 = bf16[2,256,128]{2,1,0:T(8,128)(2,1)S(1)} collective-permute-done((bf16[2,256,128]{2,1,0:T(8,128)(2,1)S(1)}, bf16[2,256,128]{2,1,0:T(8,128)(2,1)S(1)}, u32[]{:S(2)}, u32[]{:S(2)}) %collective-permute-start.15) | collective-permute-done | bytes 131104 | tf_op jit(solution)/shard_map/ppermute | solution.py:462
  65.2 1.5 %unpack.1 = bf16[1,128,2,2048]{3,2,1,0:T(2,128)(2,1)} custom-call(bf16[2,128,2,128]{3,2,1,0:T(2,128)(2,1)S(1)} %bitcast.16, bf16[2,128,2,128]{3,2,1,0:T(2,128)(2,1)S(1)} %bitcast.17, bf16[2,128,2,128]{3,2,1,0:T(2,128)(2,1)S(1)} %bitcast.18, bf16[2,128,2,128]{3,2,1,0:T(2,128)(2,1)S(1)} %bitcast.19, bf16[2,128,2,128]{3,2,1,0:T(2,128)(2,1)S(1)} %bitcast.20, ...), custom_call_target="tpu_custom_call" | custom-call | tf_op jit(solution)/shard_map/unpack/pallas_call | solution.py:115
Async XLA Ops:
  0.6 19.4 %copy-start = (bf16[1,1536,256]{2,1,0:T(8,128)(2,1)S(1)}, bf16[1,1536,256]{2,1,0:T(8,128)(2,1)}, u32[]{:S(2)}) copy-start(bf16[1,1536,256]{2,1,0:T(8,128)(2,1)} %refs_6_.1) | copy-start | bytes 2359300
  0.6 1.3 %copy-start.2 = (bf16[1,128,2,2048]{3,2,1,0:T(2,128)(2,1)S(1)}, bf16[1,128,2,2048]{3,2,1,0:T(2,128)(2,1)}, u32[]{:S(2)}) copy-start(bf16[1,128,2,2048]{3,2,1,0:T(2,128)(2,1)} %pairs_ref.1) | copy-start | bytes 3145732
  1.9 18.3 %copy-start.1 = (bf16[1,1536,256]{2,1,0:T(8,128)(2,1)S(1)}, bf16[1,1536,256]{2,1,0:T(8,128)(2,1)}, u32[]{:S(2)}) copy-start(bf16[1,1536,256]{2,1,0:T(8,128)(2,1)} %refs_7_.1) | copy-start | bytes 2359300
  2.9 11.3 %collective-permute-start.4 = (bf16[2,256,128]{2,1,0:T(8,128)(2,1)S(1)}, bf16[2,256,128]{2,1,0:T(8,128)(2,1)S(1)}, u32[]{:S(2)}, u32[]{:S(2)}) collective-permute-start(bf16[2,256,128]{2,1,0:T(8,128)(2,1)S(1)} %bitcast.31), channel_id=1, source_target_pairs={{0,11},{1,10},{2,13},{3,12},{4,15},{5,14},{6,9},{7,8},{8,19},{9,18... | collective-permute-start | bytes 393224 | tf_op jit(solution)/shard_map/ppermute | solution.py:454
  6.4 10.9 %collective-permute-start.5 = (bf16[2,256,128]{2,1,0:T(8,128)(2,1)S(1)}, bf16[2,256,128]{2,1,0:T(8,128)(2,1)S(1)}, u32[]{:S(2)}, u32[]{:S(2)}) collective-permute-start(bf16[2,256,128]{2,1,0:T(8,128)(2,1)S(1)} %bitcast.30), channel_id=1, source_target_pairs={{0,9},{1,8},{2,11},{3,10},{4,13},{5,12},{6,15},{7,14},{8,17},{9,16... | collective-permute-start | bytes 393224 | tf_op jit(solution)/shard_map/ppermute | solution.py:454
  8.1 12.5 %collective-permute-start.6 = (bf16[2,256,128]{2,1,0:T(8,128)(2,1)S(1)}, bf16[2,256,128]{2,1,0:T(8,128)(2,1)S(1)}, u32[]{:S(2)}, u32[]{:S(2)}) collective-permute-start(bf16[2,256,128]{2,1,0:T(8,128)(2,1)S(1)} %bitcast.29), channel_id=1, source_target_pairs={{0,15},{1,14},{2,9},{3,8},{4,11},{5,10},{6,13},{7,12},{8,23},{9,22... | collective-permute-start | bytes 393224 | tf_op jit(solution)/shard_map/ppermute | solution.py:454
  10.7 13.6 %collective-permute-start.1 = (bf16[2,256,128]{2,1,0:T(8,128)(2,1)S(1)}, bf16[2,256,128]{2,1,0:T(8,128)(2,1)S(1)}, u32[]{:S(2)}, u32[]{:S(2)}) collective-permute-start(bf16[2,256,128]{2,1,0:T(8,128)(2,1)S(1)} %bitcast.28), channel_id=1, source_target_pairs={{0,10},{1,11},{2,12},{3,13},{4,14},{5,15},{6,8},{7,9},{8,18},{9,19... | collective-permute-start | bytes 393224 | tf_op jit(solution)/shard_map/ppermute | solution.py:454
  10.8 13.6 %collective-permute-start.2 = (bf16[2,256,128]{2,1,0:T(8,128)(2,1)S(1)}, bf16[2,256,128]{2,1,0:T(8,128)(2,1)S(1)}, u32[]{:S(2)}, u32[]{:S(2)}) collective-permute-start(bf16[2,256,128]{2,1,0:T(8,128)(2,1)S(1)} %bitcast.27), channel_id=1, source_target_pairs={{0,14},{1,15},{2,8},{3,9},{4,10},{5,11},{6,12},{7,13},{8,22},{9,23... | collective-permute-start | bytes 393224 | tf_op jit(solution)/shard_map/ppermute | solution.py:454
  14.2 10.1 %collective-permute-start.3 = (bf16[2,256,128]{2,1,0:T(8,128)(2,1)S(1)}, bf16[2,256,128]{2,1,0:T(8,128)(2,1)S(1)}, u32[]{:S(2)}, u32[]{:S(2)}) collective-permute-start(bf16[2,256,128]{2,1,0:T(8,128)(2,1)S(1)} %bitcast.26), channel_id=1, source_target_pairs={{0,8},{1,9},{2,10},{3,11},{4,12},{5,13},{6,14},{7,15},{8,16},{9,17... | collective-permute-start | bytes 393224 | tf_op jit(solution)/shard_map/ppermute | solution.py:454
  17.3 14.0 %collective-permute-start = (bf16[2,256,128]{2,1,0:T(8,128)(2,1)S(1)}, bf16[2,256,128]{2,1,0:T(8,128)(2,1)S(1)}, u32[]{:S(2)}, u32[]{:S(2)}) collective-permute-start(bf16[2,256,128]{2,1,0:T(8,128)(2,1)S(1)} %bitcast.25), channel_id=1, source_target_pairs={{0,13},{1,12},{2,15},{3,14},{4,9},{5,8},{6,11},{7,10},{8,21},{9,20... | collective-permute-start | bytes 393224 | tf_op jit(solution)/shard_map/ppermute | solution.py:454
  20.6 12.2 %collective-permute-start.7 = (bf16[2,256,128]{2,1,0:T(8,128)(2,1)S(1)}, bf16[2,256,128]{2,1,0:T(8,128)(2,1)S(1)}, u32[]{:S(2)}, u32[]{:S(2)}) collective-permute-start(bf16[2,256,128]{2,1,0:T(8,128)(2,1)S(1)} %bitcast.24), channel_id=1, source_target_pairs={{0,12},{1,13},{2,14},{3,15},{4,8},{5,9},{6,10},{7,11},{8,20},{9,21... | collective-permute-start | bytes 393224 | tf_op jit(solution)/shard_map/ppermute | solution.py:454
  35.2 12.1 %collective-permute-start.8 = (bf16[2,256,128]{2,1,0:T(8,128)(2,1)S(1)}, bf16[2,256,128]{2,1,0:T(8,128)(2,1)S(1)}, u32[]{:S(2)}, u32[]{:S(2)}) collective-permute-start(bf16[2,256,128]{2,1,0:T(8,128)(2,1)S(1)} %get-tuple-element.54), channel_id=1, source_target_pairs={{12,0},{13,1},{14,2},{15,3},{8,4},{9,5},{10,6},{11,7},{20,8},{21,9... | collective-permute-start | bytes 393224 | tf_op jit(solution)/shard_map/ppermute | solution.py:462
  40.3 14.8 %collective-permute-start.9 = (bf16[2,256,128]{2,1,0:T(8,128)(2,1)S(1)}, bf16[2,256,128]{2,1,0:T(8,128)(2,1)S(1)}, u32[]{:S(2)}, u32[]{:S(2)}) collective-permute-start(bf16[2,256,128]{2,1,0:T(8,128)(2,1)S(1)} %get-tuple-element.58), channel_id=1, source_target_pairs={{13,0},{12,1},{15,2},{14,3},{9,4},{8,5},{11,6},{10,7},{21,8},{20,9... | collective-permute-start | bytes 393224 | tf_op jit(solution)/shard_map/ppermute | solution.py:462
  45.1 11.6 %collective-permute-start.10 = (bf16[2,256,128]{2,1,0:T(8,128)(2,1)S(1)}, bf16[2,256,128]{2,1,0:T(8,128)(2,1)S(1)}, u32[]{:S(2)}, u32[]{:S(2)}) collective-permute-start(bf16[2,256,128]{2,1,0:T(8,128)(2,1)S(1)} %get-tuple-element.59), channel_id=1, source_target_pairs={{10,0},{11,1},{12,2},{13,3},{14,4},{15,5},{8,6},{9,7},{18,8},{19,9... | collective-permute-start | bytes 393224 | tf_op jit(solution)/shard_map/ppermute | solution.py:462
  46.8 11.2 %collective-permute-start.11 = (bf16[2,256,128]{2,1,0:T(8,128)(2,1)S(1)}, bf16[2,256,128]{2,1,0:T(8,128)(2,1)S(1)}, u32[]{:S(2)}, u32[]{:S(2)}) collective-permute-start(bf16[2,256,128]{2,1,0:T(8,128)(2,1)S(1)} %get-tuple-element.60), channel_id=1, source_target_pairs={{14,0},{15,1},{8,2},{9,3},{10,4},{11,5},{12,6},{13,7},{22,8},{23,9... | collective-permute-start | bytes 393224 | tf_op jit(solution)/shard_map/ppermute | solution.py:462
  46.9 11.1 %collective-permute-start.12 = (bf16[2,256,128]{2,1,0:T(8,128)(2,1)S(1)}, bf16[2,256,128]{2,1,0:T(8,128)(2,1)S(1)}, u32[]{:S(2)}, u32[]{:S(2)}) collective-permute-start(bf16[2,256,128]{2,1,0:T(8,128)(2,1)S(1)} %get-tuple-element.61), channel_id=1, source_target_pairs={{8,0},{9,1},{10,2},{11,3},{12,4},{13,5},{14,6},{15,7},{16,8},{17,9... | collective-permute-start | bytes 393224 | tf_op jit(solution)/shard_map/ppermute | solution.py:462
  51.0 8.1 %collective-permute-start.13 = (bf16[2,256,128]{2,1,0:T(8,128)(2,1)S(1)}, bf16[2,256,128]{2,1,0:T(8,128)(2,1)S(1)}, u32[]{:S(2)}, u32[]{:S(2)}) collective-permute-start(bf16[2,256,128]{2,1,0:T(8,128)(2,1)S(1)} %get-tuple-element.62), channel_id=1, source_target_pairs={{11,0},{10,1},{13,2},{12,3},{15,4},{14,5},{9,6},{8,7},{19,8},{18,9... | collective-permute-start | bytes 393224 | tf_op jit(solution)/shard_map/ppermute | solution.py:462
  55.1 7.2 %collective-permute-start.14 = (bf16[2,256,128]{2,1,0:T(8,128)(2,1)S(1)}, bf16[2,256,128]{2,1,0:T(8,128)(2,1)S(1)}, u32[]{:S(2)}, u32[]{:S(2)}) collective-permute-start(bf16[2,256,128]{2,1,0:T(8,128)(2,1)S(1)} %get-tuple-element.63), channel_id=1, source_target_pairs={{9,0},{8,1},{11,2},{10,3},{13,4},{12,5},{15,6},{14,7},{17,8},{16,9... | collective-permute-start | bytes 393224 | tf_op jit(solution)/shard_map/ppermute | solution.py:462
  56.7 8.5 %collective-permute-start.15 = (bf16[2,256,128]{2,1,0:T(8,128)(2,1)S(1)}, bf16[2,256,128]{2,1,0:T(8,128)(2,1)S(1)}, u32[]{:S(2)}, u32[]{:S(2)}) collective-permute-start(bf16[2,256,128]{2,1,0:T(8,128)(2,1)S(1)} %get-tuple-element.64), channel_id=1, source_target_pairs={{15,0},{14,1},{9,2},{8,3},{11,4},{10,5},{13,6},{12,7},{23,8},{22,9... | collective-permute-start | bytes 393224 | tf_op jit(solution)/shard_map/ppermute | solution.py:462

commit v17 on v16

--- a/solution.py
+++ b/solution.py
@@ -168,6 +168,27 @@
         if tokens % (256 * parts) == 0 and rows * (tokens // parts) * 4 <= 5 * MIB // 4:
             return tokens // parts
     return 256 if tokens % 256 == 0 else tokens
+
+
+def turned_back(columns, dtype):
+    heads, _, tokens = columns.shape
+    tile = 256 if tokens % 256 == 0 else tokens
+
+    def kernel(columns_ref, out_ref):
+        for h in range(heads):
+            for j in range(tokens // tile):
+                here = slice(j * tile, (j + 1) * tile)
+                block = columns_ref[h, :, here].T.astype(dtype)
+                out_ref[0, here, h * HEAD : (h + 1) * HEAD] = block
+
+    return pl.pallas_call(
+        kernel,
+        out_shape=jax.ShapeDtypeStruct((1, tokens, heads * HEAD), dtype),
+        in_specs=[VMEM],
+        out_specs=VMEM,
+        compiler_params=pltpu.CompilerParams(vmem_limit_bytes=16 * MIB),
+        name="turned_back",
+    )(columns)
 
 
 def dot(a, b, contract=((1,), (0,))):
@@ -298,17 +319,14 @@
         join_chunks(outs, h, rows, gk_ref, gv_ref)
 
 
-def backward_kernel(back, counts, first, tile, *refs):
+def backward_kernel(back, counts, tile, *refs):
     refs = refs[back:]
     groups = []
     for count in counts:
         groups.append((refs[:count], refs[count], refs[count + 1]))
         refs = refs[count + 2 :]
     q_ref, g_ref, gt_ref, stats_ref, grad_q_in = refs[:5]
-    if first:
-        ready_ref, rows_ref, grad_q_ref, refs = refs[5], refs[6], refs[7], refs[8:]
-    else:
-        rows_ref, refs = refs[5], refs[6:]
+    grad_q_ref, refs = refs[5], refs[6:]
     outs, refs = refs[: sum(counts)], refs[sum(counts) :]
     scratch = [refs[i : i + 4] for i in range(0, len(refs), 4)]
     heads, pair_rows, _ = groups[0][0][0].shape
@@ -334,10 +352,7 @@
                 grad_q = grad_q + gradients(
                     raised, scale * shrunk, row_dot, rows_here, gt, own, h
                 )
-            if first:
-                grad_q_ref[h, :, here] = grad_q
-                grad_q = ready_ref[h, :, here]
-            rows_ref[0, here, columns] = grad_q.T.astype(rows_ref.dtype)
+            grad_q_ref[h, :, here] = grad_q
 
     for count, (_, _, gk_ref, gv_ref) in zip(counts, scratch):
         for h in range(heads):
@@ -361,7 +376,6 @@
     qt, gt = turned(queries), turned(upstream)
     stats_shape = jax.ShapeDtypeStruct((heads, 8, tokens), jnp.float32)
     wide_shape = jax.ShapeDtypeStruct((heads, HEAD, tokens), jnp.float32)
-    rows_shape = jax.ShapeDtypeStruct(queries.shape, queries.dtype)
     compiler_params = params(enc_len)
 
     def natural(count):
@@ -414,15 +428,14 @@
         operands = []
         for i in part:
             operands += [*groups[i], *kept[i]]
-        operands += [queries, upstream, gt, final, grad_q, *([context] if first else [])]
-        shapes = [rows_shape, wide_shape] if first else [rows_shape]
+        operands += [queries, upstream, gt, final, grad_q]
         outs = pl.pallas_call(
             functools.partial(
-                backward_kernel, len(back), counts, first, tile_of(max(counts) * rows, tokens)
+                backward_kernel, len(back), counts, tile_of(max(counts) * rows, tokens)
             ),
-            out_shape=shapes + shapes_of(sum((groups[i] for i in part), [])),
+            out_shape=[wide_shape] + shapes_of(sum((groups[i] for i in part), [])),
             in_specs=[ANY] * len(back) + [VMEM] * len(operands),
-            out_specs=[VMEM] * (len(shapes) + sum(counts)),
+            out_specs=[VMEM] * (1 + sum(counts)),
             scratch_shapes=[
                 shape
                 for count in counts
@@ -432,15 +445,11 @@
             cost_estimate=cost(heads, sum(counts) * rows, tokens, 4),
             name="backward",
         )(*back, *operands)
-        if first:
-            context_rows, grad_q = outs[:2]
-        else:
-            grad_query = outs[0]
-        blocks = list(outs[len(shapes) :])
+        grad_q, blocks = outs[0], list(outs[1:])
         for i in part:
             returned.append(send_back(i, blocks[: len(groups[i])]))
             blocks = blocks[len(groups[i]) :]
-    return context_rows, grad_query
+    return turned_back(context, queries.dtype), turned_back(grad_q, queries.dtype)
 
 
 def shards(pairs, queries, upstream):
@@ -449,7 +458,9 @@
     offsets = offset_groups()
     order = sum(offsets, [])
     blocks = []
-    for offset, block in zip(order, pack(pairs, order, heads)):
+    first = len(offsets[0])
+    packed = pack(pairs, order[:first], heads) + pack(pairs, order[first:], heads)
+    for offset, block in zip(order, packed):
         block = block.reshape(heads, 2 * rows, HEAD)
         blocks.append(lax.ppermute(block, AXES, route(offset, False)))
     groups = []

time: 67 us -> 64.9 us (0.969)
  starting transfers between devices: 31.1 us -> 29.1 us
  waiting for transfers between devices: 13.4 us -> 12.4 us
  Pallas kernels: 20.1 us -> 20.8 us
    ppermute x8, waiting for transfers between devices: 7.19 us -> 3.15 us  [send_back(): lax.ppermute(g, AXES, route(o, True))]
    ppermute x8, waiting for transfers between devices: 6.22 us -> 9.23 us  [shards(): blocks.append(lax.ppermute(block, AXES, route(offset, False)))]
    ppermute x8, starting transfers between devices: 16.9 us -> 14.3 us  [shards(): blocks.append(lax.ppermute(block, AXES, route(offset, False)))]
    pallas_call x2 -> x4, Pallas kernels: 8.59 us -> 9.13 us  [the longest x2 6.83 us: attend(): pl.pallas_call(functools.partial(backward_kernel, len(back), counts, tile...]
  transfers between devices with their start and end apart: 16 -> 16, of which waited for: 6 -> 5; matrix products, arithmetic and copies ran while one was open for 0% -> 0% of each run, Pallas kernels for 23% -> 25%
where the time goes in v17:
time: 64.9 us; the launch traced here: 64.6 us
  starting transfers between devices  29.1 us (45%)
  Pallas kernels  20.8 us (32%)
  waiting for transfers between devices  12.4 us (19%)
  local copies, waits for them, and re-layouts  1.3 us (2%)
  between operations  0.94 us (1%)
    ppermute x8, starting transfers between devices, send_back(): lax.ppermute(g, AXES, route(o, True))  14.8 us
    ppermute x8, starting transfers between devices, shards(): blocks.append(lax.ppermute(block, AXES, route(offset, False)))  14.3 us
    ppermute x8, waiting for transfers between devices, shards(): blocks.append(lax.ppermute(block, AXES, route(offset, False)))  9.23 us
    pallas_call x2, Pallas kernels, attend(): pl.pallas_call(functools.partial(backward_kernel, len(back), counts, tile...  6.83 us
    pallas_call x3, Pallas kernels, attend(): pl.pallas_call(functools.partial(forward_kernel, count, not state, tile_o...  6.12 us
    ppermute x8, waiting for transfers between devices, send_back(): lax.ppermute(g, AXES, route(o, True))  3.15 us
    pallas_call x1, Pallas kernels, attend(): pl.pallas_call(functools.partial(turn_kernel, count, tile_of(count * rows...  2.44 us
    pallas_call x2, Pallas kernels, turned_back(): pl.pallas_call(kernel, out_shape=jax.ShapeDtypeStruct((1, tokens, heads *...  2.3 us
  transfers between devices with their start and end apart: 16, of which 5 were waited for; matrix products, arithmetic and copies ran while one was open for 0% of the time, Pallas kernels for 25%

profile of v17, /device:TPU:0, one launch (start us, length us, event | category | flops | bytes accessed | tf_op | source)
XLA Modules:
  0.0 64.6 jit_solution(5627429154902814804)
XLA Ops:
  0.6 0.0 copy-start
  0.6 0.0 copy-start.2
  0.6 1.3 %copy-done.2 = bf16[1,128,2,2048]{3,2,1,0:T(2,128)(2,1)S(1)} copy-done((bf16[1,128,2,2048]{3,2,1,0:T(2,128)(2,1)S(1)}, bf16[1,128,2,2048]{3,2,1,0:T(2,128)(2,1)}, u32[]{:S(2)}) %copy-start.2) | copy-done | bytes 1048600
  1.9 0.4 pack.3
  2.4 0.0 copy-start.1
  2.4 2.5 %collective-permute-start.6 = (bf16[2,256,128]{2,1,0:T(8,128)(2,1)S(1)}, bf16[2,256,128]{2,1,0:T(8,128)(2,1)S(1)}, u32[]{:S(2)}, u32[]{:S(2)}) collective-permute-start(bf16[2,256,128]{2,1,0:T(8,128)(2,1)S(1)} %bitcast.31), channel_id=1, source_target_pairs={{0,9},{1,8},{2,11},{3,10},{4,13},{5,12},{6,15},{7,14},{8,17},{9,16... | collective-permute-start | bytes 393224 | tf_op jit(solution)/shard_map/ppermute | solution.py:465
  4.9 2.7 %collective-permute-start.5 = (bf16[2,256,128]{2,1,0:T(8,128)(2,1)S(1)}, bf16[2,256,128]{2,1,0:T(8,128)(2,1)S(1)}, u32[]{:S(2)}, u32[]{:S(2)}) collective-permute-start(bf16[2,256,128]{2,1,0:T(8,128)(2,1)S(1)} %bitcast.30), channel_id=1, source_target_pairs={{0,11},{1,10},{2,13},{3,12},{4,15},{5,14},{6,9},{7,8},{8,19},{9,18... | collective-permute-start | bytes 393224 | tf_op jit(solution)/shard_map/ppermute | solution.py:465
  7.6 2.6 %collective-permute-start.7 = (bf16[2,256,128]{2,1,0:T(8,128)(2,1)S(1)}, bf16[2,256,128]{2,1,0:T(8,128)(2,1)S(1)}, u32[]{:S(2)}, u32[]{:S(2)}) collective-permute-start(bf16[2,256,128]{2,1,0:T(8,128)(2,1)S(1)} %bitcast.28), channel_id=1, source_target_pairs={{0,15},{1,14},{2,9},{3,8},{4,11},{5,10},{6,13},{7,12},{8,23},{9,22... | collective-permute-start | bytes 393224 | tf_op jit(solution)/shard_map/ppermute | solution.py:465
  10.2 0.7 %pack.2 = (bf16[2,128,2,128]{3,2,1,0:T(2,128)(2,1)S(1)}, bf16[2,128,2,128]{3,2,1,0:T(2,128)(2,1)S(1)}, bf16[2,128,2,128]{3,2,1,0:T(2,128)(2,1)S(1)}, bf16[2,128,...) custom-call(bf16[1,128,2,2048]{3,2,1,0:T(2,128)(2,1)S(1)} %copy-done.2), custom_call_target="tpu_custom_call" | custom-call | tf_op jit(solution)/shard_map/pack/pallas_call | solution.py:79
  10.9 0.1 collective-permute-start.2
  11.0 3.5 %collective-permute-start.3 = (bf16[2,256,128]{2,1,0:T(8,128)(2,1)S(1)}, bf16[2,256,128]{2,1,0:T(8,128)(2,1)S(1)}, u32[]{:S(2)}, u32[]{:S(2)}) collective-permute-start(bf16[2,256,128]{2,1,0:T(8,128)(2,1)S(1)} %bitcast.27), channel_id=1, source_target_pairs={{0,14},{1,15},{2,8},{3,9},{4,10},{5,11},{6,12},{7,13},{8,22},{9,23... | collective-permute-start | bytes 393224 | tf_op jit(solution)/shard_map/ppermute | solution.py:465
  14.5 0.0 collective-permute-done.6.refs_1_.refs_2_
  14.5 1.6 %collective-permute-start.4 = (bf16[2,256,128]{2,1,0:T(8,128)(2,1)S(1)}, bf16[2,256,128]{2,1,0:T(8,128)(2,1)S(1)}, u32[]{:S(2)}, u32[]{:S(2)}) collective-permute-start(bf16[2,256,128]{2,1,0:T(8,128)(2,1)S(1)} %bitcast.26), channel_id=1, source_target_pairs={{0,8},{1,9},{2,10},{3,11},{4,12},{5,13},{6,14},{7,15},{8,16},{9,17... | collective-permute-start | bytes 393224 | tf_op jit(solution)/shard_map/ppermute | solution.py:465
  16.1 0.0 collective-permute-done.5.refs_0_.refs_1_
  16.1 1.3 %collective-permute-start.1 = (bf16[2,256,128]{2,1,0:T(8,128)(2,1)S(1)}, bf16[2,256,128]{2,1,0:T(8,128)(2,1)S(1)}, u32[]{:S(2)}, u32[]{:S(2)}) collective-permute-start(bf16[2,256,128]{2,1,0:T(8,128)(2,1)S(1)} %bitcast.25), channel_id=1, source_target_pairs={{0,13},{1,12},{2,15},{3,14},{4,9},{5,8},{6,11},{7,10},{8,21},{9,20... | collective-permute-start | bytes 393224 | tf_op jit(solution)/shard_map/ppermute | solution.py:465
  17.4 0.0 copy-done
  17.4 0.3 turned.2.refs_3_.refs_1_
  17.7 0.0 copy-done.1
  17.7 0.3 turned.3.refs_4_.refs_10_.refs_8_
  18.0 2.1 %collective-permute-done.7.refs_2_.refs_3_ = bf16[2,256,128]{2,1,0:T(8,128)(2,1)S(1)} collective-permute-done((bf16[2,256,128]{2,1,0:T(8,128)(2,1)S(1)}, bf16[2,256,128]{2,1,0:T(8,128)(2,1)S(1)}, u32[]{:S(2)}, u32[]{:S(2)}) %collective-permute-start.7) | collective-permute-done | bytes 131104 | tf_op jit(solution)/shard_map/ppermute | solution.py:465
  20.1 0.0 collective-permute-start
  20.1 2.5 %forward.3 = (f32[2,8,1536]{2,1,0:T(8,128)S(1)}, f32[2,128,1536]{2,1,0:T(8,128)S(1)}, bf16[2,384,1536]{2,1,0:T(8,128)(2,1)S(1)}) custom-call(bf16[2,256,128]{2,1,0:T(8,128)(2,1)S(1)} %collective-permute-done.5.refs_0_.refs_1_, bf16[2,256,128]{2,1,0:T(8,128)(2,1)S(1)} %collective-permute-done.6.refs_1_.refs_2_, ...), custom_call_target="tpu_custom_call" | custom-call | flops 603979776 | bytes 3932160 | tf_op jit(solution)/shard_map/forward/pallas_call | solution.py:397
  22.7 0.0 collective-permute-done.2.refs_0_.refs_3_
  22.7 0.0 collective-permute-done.3.refs_1_.refs_4_
  22.7 0.0 collective-permute-done.4.refs_2_.refs_5_
  22.7 2.5 %forward.4 = (f32[2,8,1536]{2,1,0:T(8,128)S(1)}, f32[2,128,1536]{2,1,0:T(8,128)S(1)}, bf16[2,384,1536]{2,1,0:T(8,128)(2,1)S(1)}) custom-call(bf16[2,256,128]{2,1,0:T(8,128)(2,1)S(1)} %collective-permute-done.2.refs_0_.refs_3_, bf16[2,256,128]{2,1,0:T(8,128)(2,1)S(1)} %collective-permute-done.3.refs_1_.refs_4_, ...), custom_call_target="tpu_custom_call" | custom-call | flops 603979776 | bytes 3932160 | tf_op jit(solution)/shard_map/forward/pallas_call | solution.py:397
  25.3 5.9 %collective-permute-done.1.refs_0_ = bf16[2,256,128]{2,1,0:T(8,128)(2,1)S(1)} collective-permute-done((bf16[2,256,128]{2,1,0:T(8,128)(2,1)S(1)}, bf16[2,256,128]{2,1,0:T(8,128)(2,1)S(1)}, u32[]{:S(2)}, u32[]{:S(2)}) %collective-permute-start.1) | collective-permute-done | bytes 131104 | tf_op jit(solution)/shard_map/ppermute | solution.py:465
  31.2 1.0 %forward.5 = (f32[2,8,1536]{2,1,0:T(8,128)S(1)}, f32[2,128,1536]{2,1,0:T(8,128)S(1)}, bf16[2,128,1536]{2,1,0:T(8,128)(2,1)S(1)}) custom-call(bf16[2,256,128]{2,1,0:T(8,128)(2,1)S(1)} %collective-permute-done.1.refs_0_, bf16[2,128,1536]{2,1,0:T(8,128)(2,1)S(1)} %turned.2.refs_3_.refs_1_, f32[2,8,1536]{2,1,0:T(8,128)S(1)} %get-tuple-element.43.refs_2_.refs_7_, ...), custom_call_target="tpu_custom_call" | custom-call | flops 201326592 | bytes 3407872 | tf_op jit(solution)/shard_map/forward/pallas_call | solution.py:397
  32.2 1.2 %collective-permute-done.refs_0_ = bf16[2,256,128]{2,1,0:T(8,128)(2,1)S(1)} collective-permute-done((bf16[2,256,128]{2,1,0:T(8,128)(2,1)S(1)}, bf16[2,256,128]{2,1,0:T(8,128)(2,1)S(1)}, u32[]{:S(2)}, u32[]{:S(2)}) %collective-permute-start) | collective-permute-done | bytes 131104 | tf_op jit(solution)/shard_map/ppermute | solution.py:465
  33.4 2.4 %turn.1 = (f32[2,8,1536]{2,1,0:T(8,128)S(1)}, f32[2,128,1536]{2,1,0:T(8,128)S(1)}, f32[2,128,1536]{2,1,0:T(8,128)S(1)}, bf16[2,256,128]{2,1,0:T(8,128)(2,1)S(1)}) custom-call(bf16[2,256,128]{2,1,0:T(8,128)(2,1)S(1)} %collective-permute-done.refs_0_, bf16[1,1536,256]{2,1,0:T(8,128)(2,1)S(1)} %copy-done, bf16[1,1536,256]{2,1,0:T(8,128)(2,1)S(1)} %copy-done.1, ...), custom_call_target="tpu_custom_call" | custom-call | flops 603979776 | bytes 3407872 | tf_op jit(solution)/shard_map/turn/pallas_call | solution.py:411
  35.8 0.2 collective-permute-start.8
  36.0 4.0 %backward.2 = (f32[2,128,1536]{2,1,0:T(8,128)S(1)}, bf16[2,256,128]{2,1,0:T(8,128)(2,1)S(1)}, bf16[2,256,128]{2,1,0:T(8,128)(2,1)S(1)}, bf16[2,256,128]{2,1,0:T(8,128)(2,1)S(1)}, bf16[2,256,128]{2,1,0:T(8,128)(2,1)S(1)}) custom-call(bf16[2,256,128]{2,1,0:T(8,128)(2,1)S(1)} %collective-permute-done.1.refs_0_, ...), custom_call_target="tpu_custom_call" | custom-call | flops 1610612736 | bytes 4194304 | tf_op jit(solution)/shard_map/backward/pallas_call | solution.py:432
  40.0 4.1 %collective-permute-start.9 = (bf16[2,256,128]{2,1,0:T(8,128)(2,1)S(1)}, bf16[2,256,128]{2,1,0:T(8,128)(2,1)S(1)}, u32[]{:S(2)}, u32[]{:S(2)}) collective-permute-start(bf16[2,256,128]{2,1,0:T(8,128)(2,1)S(1)} %get-tuple-element.56), channel_id=1, source_target_pairs={{13,0},{12,1},{15,2},{14,3},{9,4},{8,5},{11,6},{10,7},{21,8},{20,9... | collective-permute-start | bytes 393224 | tf_op jit(solution)/shard_map/ppermute | solution.py:473
  44.1 1.4 %collective-permute-start.10 = (bf16[2,256,128]{2,1,0:T(8,128)(2,1)S(1)}, bf16[2,256,128]{2,1,0:T(8,128)(2,1)S(1)}, u32[]{:S(2)}, u32[]{:S(2)}) collective-permute-start(bf16[2,256,128]{2,1,0:T(8,128)(2,1)S(1)} %get-tuple-element.57), channel_id=1, source_target_pairs={{10,0},{11,1},{12,2},{13,3},{14,4},{15,5},{8,6},{9,7},{18,8},{19,9... | collective-permute-start | bytes 393224 | tf_op jit(solution)/shard_map/ppermute | solution.py:473
  45.5 0.5 collective-permute-start.11
  45.9 0.2 collective-permute-start.12
  46.1 0.0 collective-permute-done.8.refs_0_
  46.1 2.9 %backward.3 = (f32[2,128,1536]{2,1,0:T(8,128)S(1)}, bf16[2,256,128]{2,1,0:T(8,128)(2,1)S(1)}, bf16[2,256,128]{2,1,0:T(8,128)(2,1)S(1)}, bf16[2,256,128]{2,1,0:T(8,128)(2,1)S(1)}) custom-call(bf16[2,256,128]{2,1,0:T(8,128)(2,1)S(1)} %collective-permute-done.8.refs_0_, bf16[2,256,128]{2,1,0:T(8,128)(2,1)S(1)} %collective-permute-done.5.refs_0_.refs_1_, ...), custom_call_target="tpu_custom_call" | custom-call | flops 1207959552 | bytes 3932160 | tf_op jit(solution)/shard_map/backward/pallas_call | solution.py:432
  49.0 4.9 %collective-permute-start.13 = (bf16[2,256,128]{2,1,0:T(8,128)(2,1)S(1)}, bf16[2,256,128]{2,1,0:T(8,128)(2,1)S(1)}, u32[]{:S(2)}, u32[]{:S(2)}) collective-permute-start(bf16[2,256,128]{2,1,0:T(8,128)(2,1)S(1)} %get-tuple-element.60), channel_id=1, source_target_pairs={{11,0},{10,1},{13,2},{12,3},{15,4},{14,5},{9,6},{8,7},{19,8},{18,9... | collective-permute-start | bytes 393224 | tf_op jit(solution)/shard_map/ppermute | solution.py:473
  53.9 0.0 collective-permute-done.9
  53.9 0.7 %collective-permute-start.14 = (bf16[2,256,128]{2,1,0:T(8,128)(2,1)S(1)}, bf16[2,256,128]{2,1,0:T(8,128)(2,1)S(1)}, u32[]{:S(2)}, u32[]{:S(2)}) collective-permute-start(bf16[2,256,128]{2,1,0:T(8,128)(2,1)S(1)} %get-tuple-element.61), channel_id=1, source_target_pairs={{9,0},{8,1},{11,2},{10,3},{13,4},{12,5},{15,6},{14,7},{17,8},{16,9... | collective-permute-start | bytes 393224 | tf_op jit(solution)/shard_map/ppermute | solution.py:473
  54.6 0.0 collective-permute-done.10
  54.6 2.9 %collective-permute-start.15 = (bf16[2,256,128]{2,1,0:T(8,128)(2,1)S(1)}, bf16[2,256,128]{2,1,0:T(8,128)(2,1)S(1)}, u32[]{:S(2)}, u32[]{:S(2)}) collective-permute-start(bf16[2,256,128]{2,1,0:T(8,128)(2,1)S(1)} %get-tuple-element.62), channel_id=1, source_target_pairs={{15,0},{14,1},{9,2},{8,3},{11,4},{10,5},{13,6},{12,7},{23,8},{22,9... | collective-permute-start | bytes 393224 | tf_op jit(solution)/shard_map/ppermute | solution.py:473
  57.5 1.2 %turned_back.2 = bf16[1,1536,256]{2,1,0:T(8,128)(2,1)} custom-call(f32[2,128,1536]{2,1,0:T(8,128)S(1)} %get-tuple-element.47.columns_ref), custom_call_target="tpu_custom_call" | custom-call | tf_op jit(solution)/shard_map/turned_back/pallas_call | solution.py:184
  58.6 1.2 %turned_back.3 = bf16[1,1536,256]{2,1,0:T(8,128)(2,1)} custom-call(f32[2,128,1536]{2,1,0:T(8,128)S(1)} %get-tuple-element.55.columns_ref), custom_call_target="tpu_custom_call" | custom-call | tf_op jit(solution)/shard_map/turned_back/pallas_call | solution.py:184
  59.8 0.0 collective-permute-done.11
  59.8 0.0 collective-permute-done.12
  59.8 0.0 collective-permute-done.13
  59.8 1.8 %collective-permute-done.14 = bf16[2,256,128]{2,1,0:T(8,128)(2,1)S(1)} collective-permute-done((bf16[2,256,128]{2,1,0:T(8,128)(2,1)S(1)}, bf16[2,256,128]{2,1,0:T(8,128)(2,1)S(1)}, u32[]{:S(2)}, u32[]{:S(2)}) %collective-permute-start.14) | collective-permute-done | bytes 131104 | tf_op jit(solution)/shard_map/ppermute | solution.py:473
  61.6 1.4 %collective-permute-done.15 = bf16[2,256,128]{2,1,0:T(8,128)(2,1)S(1)} collective-permute-done((bf16[2,256,128]{2,1,0:T(8,128)(2,1)S(1)}, bf16[2,256,128]{2,1,0:T(8,128)(2,1)S(1)}, u32[]{:S(2)}, u32[]{:S(2)}) %collective-permute-start.15) | collective-permute-done | bytes 131104 | tf_op jit(solution)/shard_map/ppermute | solution.py:473
  62.9 1.5 %unpack.1 = bf16[1,128,2,2048]{3,2,1,0:T(2,128)(2,1)} custom-call(bf16[2,128,2,128]{3,2,1,0:T(2,128)(2,1)S(1)} %bitcast.16, bf16[2,128,2,128]{3,2,1,0:T(2,128)(2,1)S(1)} %bitcast.17, bf16[2,128,2,128]{3,2,1,0:T(2,128)(2,1)S(1)} %bitcast.18, bf16[2,128,2,128]{3,2,1,0:T(2,128)(2,1)S(1)} %bitcast.19, bf16[2,128,2,128]{3,2,1,0:T(2,128)(2,1)S(1)} %bitcast.20, ...), custom_call_target="tpu_custom_call" | custom-call | tf_op jit(solution)/shard_map/unpack/pallas_call | solution.py:115
Async XLA Ops:
  0.6 16.8 %copy-start = (bf16[1,1536,256]{2,1,0:T(8,128)(2,1)S(1)}, bf16[1,1536,256]{2,1,0:T(8,128)(2,1)}, u32[]{:S(2)}) copy-start(bf16[1,1536,256]{2,1,0:T(8,128)(2,1)} %refs_6_.1) | copy-start | bytes 2359300
  0.6 1.3 %copy-start.2 = (bf16[1,128,2,2048]{3,2,1,0:T(2,128)(2,1)S(1)}, bf16[1,128,2,2048]{3,2,1,0:T(2,128)(2,1)}, u32[]{:S(2)}) copy-start(bf16[1,128,2,2048]{3,2,1,0:T(2,128)(2,1)} %pairs_ref.3) | copy-start | bytes 3145732
  2.4 15.3 %copy-start.1 = (bf16[1,1536,256]{2,1,0:T(8,128)(2,1)S(1)}, bf16[1,1536,256]{2,1,0:T(8,128)(2,1)}, u32[]{:S(2)}) copy-start(bf16[1,1536,256]{2,1,0:T(8,128)(2,1)} %refs_7_.1) | copy-start | bytes 2359300
  2.4 12.1 %collective-permute-start.6 = (bf16[2,256,128]{2,1,0:T(8,128)(2,1)S(1)}, bf16[2,256,128]{2,1,0:T(8,128)(2,1)S(1)}, u32[]{:S(2)}, u32[]{:S(2)}) collective-permute-start(bf16[2,256,128]{2,1,0:T(8,128)(2,1)S(1)} %bitcast.31), channel_id=1, source_target_pairs={{0,9},{1,8},{2,11},{3,10},{4,13},{5,12},{6,15},{7,14},{8,17},{9,16... | collective-permute-start | bytes 393224 | tf_op jit(solution)/shard_map/ppermute | solution.py:465
  4.9 11.2 %collective-permute-start.5 = (bf16[2,256,128]{2,1,0:T(8,128)(2,1)S(1)}, bf16[2,256,128]{2,1,0:T(8,128)(2,1)S(1)}, u32[]{:S(2)}, u32[]{:S(2)}) collective-permute-start(bf16[2,256,128]{2,1,0:T(8,128)(2,1)S(1)} %bitcast.30), channel_id=1, source_target_pairs={{0,11},{1,10},{2,13},{3,12},{4,15},{5,14},{6,9},{7,8},{8,19},{9,18... | collective-permute-start | bytes 393224 | tf_op jit(solution)/shard_map/ppermute | solution.py:465
  7.6 12.5 %collective-permute-start.7 = (bf16[2,256,128]{2,1,0:T(8,128)(2,1)S(1)}, bf16[2,256,128]{2,1,0:T(8,128)(2,1)S(1)}, u32[]{:S(2)}, u32[]{:S(2)}) collective-permute-start(bf16[2,256,128]{2,1,0:T(8,128)(2,1)S(1)} %bitcast.28), channel_id=1, source_target_pairs={{0,15},{1,14},{2,9},{3,8},{4,11},{5,10},{6,13},{7,12},{8,23},{9,22... | collective-permute-start | bytes 393224 | tf_op jit(solution)/shard_map/ppermute | solution.py:465
  10.9 11.8 %collective-permute-start.2 = (bf16[2,256,128]{2,1,0:T(8,128)(2,1)S(1)}, bf16[2,256,128]{2,1,0:T(8,128)(2,1)S(1)}, u32[]{:S(2)}, u32[]{:S(2)}) collective-permute-start(bf16[2,256,128]{2,1,0:T(8,128)(2,1)S(1)} %bitcast.29), channel_id=1, source_target_pairs={{0,10},{1,11},{2,12},{3,13},{4,14},{5,15},{6,8},{7,9},{8,18},{9,19... | collective-permute-start | bytes 393224 | tf_op jit(solution)/shard_map/ppermute | solution.py:465
  11.0 11.7 %collective-permute-start.3 = (bf16[2,256,128]{2,1,0:T(8,128)(2,1)S(1)}, bf16[2,256,128]{2,1,0:T(8,128)(2,1)S(1)}, u32[]{:S(2)}, u32[]{:S(2)}) collective-permute-start(bf16[2,256,128]{2,1,0:T(8,128)(2,1)S(1)} %bitcast.27), channel_id=1, source_target_pairs={{0,14},{1,15},{2,8},{3,9},{4,10},{5,11},{6,12},{7,13},{8,22},{9,23... | collective-permute-start | bytes 393224 | tf_op jit(solution)/shard_map/ppermute | solution.py:465
  14.5 8.2 %collective-permute-start.4 = (bf16[2,256,128]{2,1,0:T(8,128)(2,1)S(1)}, bf16[2,256,128]{2,1,0:T(8,128)(2,1)S(1)}, u32[]{:S(2)}, u32[]{:S(2)}) collective-permute-start(bf16[2,256,128]{2,1,0:T(8,128)(2,1)S(1)} %bitcast.26), channel_id=1, source_target_pairs={{0,8},{1,9},{2,10},{3,11},{4,12},{5,13},{6,14},{7,15},{8,16},{9,17... | collective-permute-start | bytes 393224 | tf_op jit(solution)/shard_map/ppermute | solution.py:465
  16.1 15.1 %collective-permute-start.1 = (bf16[2,256,128]{2,1,0:T(8,128)(2,1)S(1)}, bf16[2,256,128]{2,1,0:T(8,128)(2,1)S(1)}, u32[]{:S(2)}, u32[]{:S(2)}) collective-permute-start(bf16[2,256,128]{2,1,0:T(8,128)(2,1)S(1)} %bitcast.25), channel_id=1, source_target_pairs={{0,13},{1,12},{2,15},{3,14},{4,9},{5,8},{6,11},{7,10},{8,21},{9,20... | collective-permute-start | bytes 393224 | tf_op jit(solution)/shard_map/ppermute | solution.py:465
  20.1 13.2 %collective-permute-start = (bf16[2,256,128]{2,1,0:T(8,128)(2,1)S(1)}, bf16[2,256,128]{2,1,0:T(8,128)(2,1)S(1)}, u32[]{:S(2)}, u32[]{:S(2)}) collective-permute-start(bf16[2,256,128]{2,1,0:T(8,128)(2,1)S(1)} %bitcast.24), channel_id=1, source_target_pairs={{0,12},{1,13},{2,14},{3,15},{4,8},{5,9},{6,10},{7,11},{8,20},{9,21... | collective-permute-start | bytes 393224 | tf_op jit(solution)/shard_map/ppermute | solution.py:465
  35.8 10.3 %collective-permute-start.8 = (bf16[2,256,128]{2,1,0:T(8,128)(2,1)S(1)}, bf16[2,256,128]{2,1,0:T(8,128)(2,1)S(1)}, u32[]{:S(2)}, u32[]{:S(2)}) collective-permute-start(bf16[2,256,128]{2,1,0:T(8,128)(2,1)S(1)} %get-tuple-element.48), channel_id=1, source_target_pairs={{12,0},{13,1},{14,2},{15,3},{8,4},{9,5},{10,6},{11,7},{20,8},{21,9... | collective-permute-start | bytes 393224 | tf_op jit(solution)/shard_map/ppermute | solution.py:473
  40.0 13.9 %collective-permute-start.9 = (bf16[2,256,128]{2,1,0:T(8,128)(2,1)S(1)}, bf16[2,256,128]{2,1,0:T(8,128)(2,1)S(1)}, u32[]{:S(2)}, u32[]{:S(2)}) collective-permute-start(bf16[2,256,128]{2,1,0:T(8,128)(2,1)S(1)} %get-tuple-element.56), channel_id=1, source_target_pairs={{13,0},{12,1},{15,2},{14,3},{9,4},{8,5},{11,6},{10,7},{21,8},{20,9... | collective-permute-start | bytes 393224 | tf_op jit(solution)/shard_map/ppermute | solution.py:473
  44.1 10.5 %collective-permute-start.10 = (bf16[2,256,128]{2,1,0:T(8,128)(2,1)S(1)}, bf16[2,256,128]{2,1,0:T(8,128)(2,1)S(1)}, u32[]{:S(2)}, u32[]{:S(2)}) collective-permute-start(bf16[2,256,128]{2,1,0:T(8,128)(2,1)S(1)} %get-tuple-element.57), channel_id=1, source_target_pairs={{10,0},{11,1},{12,2},{13,3},{14,4},{15,5},{8,6},{9,7},{18,8},{19,9... | collective-permute-start | bytes 393224 | tf_op jit(solution)/shard_map/ppermute | solution.py:473
  45.5 14.3 %collective-permute-start.11 = (bf16[2,256,128]{2,1,0:T(8,128)(2,1)S(1)}, bf16[2,256,128]{2,1,0:T(8,128)(2,1)S(1)}, u32[]{:S(2)}, u32[]{:S(2)}) collective-permute-start(bf16[2,256,128]{2,1,0:T(8,128)(2,1)S(1)} %get-tuple-element.58), channel_id=1, source_target_pairs={{14,0},{15,1},{8,2},{9,3},{10,4},{11,5},{12,6},{13,7},{22,8},{23,9... | collective-permute-start | bytes 393224 | tf_op jit(solution)/shard_map/ppermute | solution.py:473
  45.9 13.9 %collective-permute-start.12 = (bf16[2,256,128]{2,1,0:T(8,128)(2,1)S(1)}, bf16[2,256,128]{2,1,0:T(8,128)(2,1)S(1)}, u32[]{:S(2)}, u32[]{:S(2)}) collective-permute-start(bf16[2,256,128]{2,1,0:T(8,128)(2,1)S(1)} %get-tuple-element.59), channel_id=1, source_target_pairs={{8,0},{9,1},{10,2},{11,3},{12,4},{13,5},{14,6},{15,7},{16,8},{17,9... | collective-permute-start | bytes 393224 | tf_op jit(solution)/shard_map/ppermute | solution.py:473
  49.0 10.8 %collective-permute-start.13 = (bf16[2,256,128]{2,1,0:T(8,128)(2,1)S(1)}, bf16[2,256,128]{2,1,0:T(8,128)(2,1)S(1)}, u32[]{:S(2)}, u32[]{:S(2)}) collective-permute-start(bf16[2,256,128]{2,1,0:T(8,128)(2,1)S(1)} %get-tuple-element.60), channel_id=1, source_target_pairs={{11,0},{10,1},{13,2},{12,3},{15,4},{14,5},{9,6},{8,7},{19,8},{18,9... | collective-permute-start | bytes 393224 | tf_op jit(solution)/shard_map/ppermute | solution.py:473
  53.9 7.7 %collective-permute-start.14 = (bf16[2,256,128]{2,1,0:T(8,128)(2,1)S(1)}, bf16[2,256,128]{2,1,0:T(8,128)(2,1)S(1)}, u32[]{:S(2)}, u32[]{:S(2)}) collective-permute-start(bf16[2,256,128]{2,1,0:T(8,128)(2,1)S(1)} %get-tuple-element.61), channel_id=1, source_target_pairs={{9,0},{8,1},{11,2},{10,3},{13,4},{12,5},{15,6},{14,7},{17,8},{16,9... | collective-permute-start | bytes 393224 | tf_op jit(solution)/shard_map/ppermute | solution.py:473
  54.6 8.4 %collective-permute-start.15 = (bf16[2,256,128]{2,1,0:T(8,128)(2,1)S(1)}, bf16[2,256,128]{2,1,0:T(8,128)(2,1)S(1)}, u32[]{:S(2)}, u32[]{:S(2)}) collective-permute-start(bf16[2,256,128]{2,1,0:T(8,128)(2,1)S(1)} %get-tuple-element.62), channel_id=1, source_target_pairs={{15,0},{14,1},{9,2},{8,3},{11,4},{10,5},{13,6},{12,7},{23,8},{22,9... | collective-permute-start | bytes 393224 | tf_op jit(solution)/shard_map/ppermute | solution.py:473

commit v18 on v17

--- a/solution.py
+++ b/solution.py
@@ -28,7 +28,7 @@
     short.sort(key=lambda o: -o[1])
     half = len(short) // 2
     return [
-        short[:1] + near[:1] + short[1:half],
+        short[1:half] + short[:1] + near[:1],
         short[half:] + near[1:],
         long[:eighth],
         long[eighth:],
@@ -470,8 +470,9 @@
     homes, returned = [], []
 
     def send_back(i, grads):
-        back = [lax.ppermute(g, AXES, route(o, True)) for o, g in zip(offsets[i], grads)]
-        homes.extend(offsets[i])
+        sent = sorted(zip(offsets[i], grads), key=lambda s: (s[0][0] > 0) == (i == 1))
+        back = [lax.ppermute(g, AXES, route(o, True)) for o, g in sent]
+        homes.extend(o for o, _ in sent)
         returned.extend(b.reshape(heads, rows, 2, HEAD) for b in back)
         return back
 

time: 64.9 us -> 64.8 us (level)
  waiting for transfers between devices: 12.4 us -> 11.6 us
  starting transfers between devices: 29.1 us -> 29.9 us
    ppermute x8, waiting for transfers between devices: 9.23 us -> 5.96 us  [shards(): blocks.append(lax.ppermute(block, AXES, route(offset, False)))]
    ppermute x8, starting transfers between devices: 14.3 us -> 17.2 us  [shards(): blocks.append(lax.ppermute(block, AXES, route(offset, False)))]
    ppermute x8, waiting for transfers between devices: 3.15 us -> 5.66 us  [send_back(): back = [lax.ppermute(g, AXES, route(o, True)) for o, g in sent]]
    ppermute x8, starting transfers between devices: 14.8 us -> 12.7 us  [send_back(): back = [lax.ppermute(g, AXES, route(o, True)) for o, g in sent]]
  transfers between devices with their start and end apart: 16 -> 16, of which waited for: 5 -> 6; matrix products, arithmetic and copies ran while one was open for 0% -> 0% of each run, Pallas kernels for 25% -> 25%
where the time goes in v18:
time: 64.8 us; the launch traced here: 64.6 us
  starting transfers between devices  29.9 us (46%)
  Pallas kernels  20.9 us (32%)
  waiting for transfers between devices  11.6 us (18%)
  local copies, waits for them, and re-layouts  1.3 us (2%)
  between operations  0.94 us (1%)
    ppermute x8, starting transfers between devices, shards(): blocks.append(lax.ppermute(block, AXES, route(offset, False)))  17.2 us
    ppermute x8, starting transfers between devices, send_back(): back = [lax.ppermute(g, AXES, route(o, True)) for o, g in sent]  12.7 us
    pallas_call x2, Pallas kernels, attend(): pl.pallas_call(functools.partial(backward_kernel, len(back), counts, tile...  6.83 us
    pallas_call x3, Pallas kernels, attend(): pl.pallas_call(functools.partial(forward_kernel, count, not state, tile_o...  6.12 us
    ppermute x8, waiting for transfers between devices, shards(): blocks.append(lax.ppermute(block, AXES, route(offset, False)))  5.96 us
    ppermute x8, waiting for transfers between devices, send_back(): back = [lax.ppermute(g, AXES, route(o, True)) for o, g in sent]  5.66 us
    pallas_call x1, Pallas kernels, attend(): pl.pallas_call(functools.partial(turn_kernel, count, tile_of(count * rows...  2.46 us
    pallas_call x2, Pallas kernels, turned_back(): pl.pallas_call(kernel, out_shape=jax.ShapeDtypeStruct((1, tokens, heads *...  2.3 us
  transfers between devices with their start and end apart: 16, of which 6 were waited for; matrix products, arithmetic and copies ran while one was open for 0% of the time, Pallas kernels for 25%

profile of v18, /device:TPU:0, one launch (start us, length us, event | category | flops | bytes accessed | tf_op | source)
XLA Modules:
  0.0 64.6 jit_solution(9574839188031010964)
XLA Ops:
  0.6 0.0 copy-start
  0.6 0.0 copy-start.2
  0.6 1.3 %copy-done.2 = bf16[1,128,2,2048]{3,2,1,0:T(2,128)(2,1)S(1)} copy-done((bf16[1,128,2,2048]{3,2,1,0:T(2,128)(2,1)S(1)}, bf16[1,128,2,2048]{3,2,1,0:T(2,128)(2,1)}, u32[]{:S(2)}) %copy-start.2) | copy-done | bytes 1048600
  1.9 0.4 pack.3
  2.4 0.0 copy-start.1
  2.4 3.5 %collective-permute-start.6 = (bf16[2,256,128]{2,1,0:T(8,128)(2,1)S(1)}, bf16[2,256,128]{2,1,0:T(8,128)(2,1)S(1)}, u32[]{:S(2)}, u32[]{:S(2)}) collective-permute-start(bf16[2,256,128]{2,1,0:T(8,128)(2,1)S(1)} %bitcast.31), channel_id=1, source_target_pairs={{0,11},{1,10},{2,13},{3,12},{4,15},{5,14},{6,9},{7,8},{8,19},{9,18... | collective-permute-start | bytes 393224 | tf_op jit(solution)/shard_map/ppermute | solution.py:465
  5.9 3.4 %collective-permute-start.5 = (bf16[2,256,128]{2,1,0:T(8,128)(2,1)S(1)}, bf16[2,256,128]{2,1,0:T(8,128)(2,1)S(1)}, u32[]{:S(2)}, u32[]{:S(2)}) collective-permute-start(bf16[2,256,128]{2,1,0:T(8,128)(2,1)S(1)} %bitcast.30), channel_id=1, source_target_pairs={{0,15},{1,14},{2,9},{3,8},{4,11},{5,10},{6,13},{7,12},{8,23},{9,22... | collective-permute-start | bytes 393224 | tf_op jit(solution)/shard_map/ppermute | solution.py:465
  9.3 1.0 %collective-permute-start.7 = (bf16[2,256,128]{2,1,0:T(8,128)(2,1)S(1)}, bf16[2,256,128]{2,1,0:T(8,128)(2,1)S(1)}, u32[]{:S(2)}, u32[]{:S(2)}) collective-permute-start(bf16[2,256,128]{2,1,0:T(8,128)(2,1)S(1)} %bitcast.28), channel_id=1, source_target_pairs={{0,9},{1,8},{2,11},{3,10},{4,13},{5,12},{6,15},{7,14},{8,17},{9,16... | collective-permute-start | bytes 393224 | tf_op jit(solution)/shard_map/ppermute | solution.py:465
  10.2 0.7 %pack.2 = (bf16[2,128,2,128]{3,2,1,0:T(2,128)(2,1)S(1)}, bf16[2,128,2,128]{3,2,1,0:T(2,128)(2,1)S(1)}, bf16[2,128,2,128]{3,2,1,0:T(2,128)(2,1)S(1)}, bf16[2,128,...) custom-call(bf16[1,128,2,2048]{3,2,1,0:T(2,128)(2,1)S(1)} %copy-done.2), custom_call_target="tpu_custom_call" | custom-call | tf_op jit(solution)/shard_map/pack/pallas_call | solution.py:79
  10.9 0.1 collective-permute-start.2
  11.0 3.5 %collective-permute-start.3 = (bf16[2,256,128]{2,1,0:T(8,128)(2,1)S(1)}, bf16[2,256,128]{2,1,0:T(8,128)(2,1)S(1)}, u32[]{:S(2)}, u32[]{:S(2)}) collective-permute-start(bf16[2,256,128]{2,1,0:T(8,128)(2,1)S(1)} %bitcast.27), channel_id=1, source_target_pairs={{0,14},{1,15},{2,8},{3,9},{4,10},{5,11},{6,12},{7,13},{8,22},{9,23... | collective-permute-start | bytes 393224 | tf_op jit(solution)/shard_map/ppermute | solution.py:465
  14.5 0.0 collective-permute-done.6.refs_1_.refs_2_
  14.5 1.6 %collective-permute-start.4 = (bf16[2,256,128]{2,1,0:T(8,128)(2,1)S(1)}, bf16[2,256,128]{2,1,0:T(8,128)(2,1)S(1)}, u32[]{:S(2)}, u32[]{:S(2)}) collective-permute-start(bf16[2,256,128]{2,1,0:T(8,128)(2,1)S(1)} %bitcast.26), channel_id=1, source_target_pairs={{0,8},{1,9},{2,10},{3,11},{4,12},{5,13},{6,14},{7,15},{8,16},{9,17... | collective-permute-start | bytes 393224 | tf_op jit(solution)/shard_map/ppermute | solution.py:465
  16.1 0.3 collective-permute-done.5.refs_0_.refs_1_
  16.4 0.6 collective-permute-start.1
  17.0 0.0 copy-done
  17.0 0.3 turned.2.refs_3_.refs_1_
  17.3 0.0 copy-done.1
  17.3 0.3 turned.3.refs_4_.refs_10_.refs_8_
  17.5 0.0 collective-permute-done.7.refs_2_.refs_3_
  17.6 3.6 %collective-permute-start = (bf16[2,256,128]{2,1,0:T(8,128)(2,1)S(1)}, bf16[2,256,128]{2,1,0:T(8,128)(2,1)S(1)}, u32[]{:S(2)}, u32[]{:S(2)}) collective-permute-start(bf16[2,256,128]{2,1,0:T(8,128)(2,1)S(1)} %bitcast.24), channel_id=1, source_target_pairs={{0,12},{1,13},{2,14},{3,15},{4,8},{5,9},{6,10},{7,11},{8,20},{9,21... | collective-permute-start | bytes 393224 | tf_op jit(solution)/shard_map/ppermute | solution.py:465
  21.2 2.5 %forward.3 = (f32[2,8,1536]{2,1,0:T(8,128)S(1)}, f32[2,128,1536]{2,1,0:T(8,128)S(1)}, bf16[2,384,1536]{2,1,0:T(8,128)(2,1)S(1)}) custom-call(bf16[2,256,128]{2,1,0:T(8,128)(2,1)S(1)} %collective-permute-done.5.refs_0_.refs_1_, bf16[2,256,128]{2,1,0:T(8,128)(2,1)S(1)} %collective-permute-done.6.refs_1_.refs_2_, ...), custom_call_target="tpu_custom_call" | custom-call | flops 603979776 | bytes 3932160 | tf_op jit(solution)/shard_map/forward/pallas_call | solution.py:397
  23.7 0.0 collective-permute-done.2.refs_0_.refs_3_
  23.7 0.0 collective-permute-done.3.refs_1_.refs_4_
  23.7 0.0 collective-permute-done.4.refs_2_.refs_5_
  23.7 2.5 %forward.4 = (f32[2,8,1536]{2,1,0:T(8,128)S(1)}, f32[2,128,1536]{2,1,0:T(8,128)S(1)}, bf16[2,384,1536]{2,1,0:T(8,128)(2,1)S(1)}) custom-call(bf16[2,256,128]{2,1,0:T(8,128)(2,1)S(1)} %collective-permute-done.2.refs_0_.refs_3_, bf16[2,256,128]{2,1,0:T(8,128)(2,1)S(1)} %collective-permute-done.3.refs_1_.refs_4_, ...), custom_call_target="tpu_custom_call" | custom-call | flops 603979776 | bytes 3932160 | tf_op jit(solution)/shard_map/forward/pallas_call | solution.py:397
  26.3 4.1 %collective-permute-done.1.refs_0_ = bf16[2,256,128]{2,1,0:T(8,128)(2,1)S(1)} collective-permute-done((bf16[2,256,128]{2,1,0:T(8,128)(2,1)S(1)}, bf16[2,256,128]{2,1,0:T(8,128)(2,1)S(1)}, u32[]{:S(2)}, u32[]{:S(2)}) %collective-permute-start.1) | collective-permute-done | bytes 131104 | tf_op jit(solution)/shard_map/ppermute | solution.py:465
  30.4 1.0 %forward.5 = (f32[2,8,1536]{2,1,0:T(8,128)S(1)}, f32[2,128,1536]{2,1,0:T(8,128)S(1)}, bf16[2,128,1536]{2,1,0:T(8,128)(2,1)S(1)}) custom-call(bf16[2,256,128]{2,1,0:T(8,128)(2,1)S(1)} %collective-permute-done.1.refs_0_, bf16[2,128,1536]{2,1,0:T(8,128)(2,1)S(1)} %turned.2.refs_3_.refs_1_, f32[2,8,1536]{2,1,0:T(8,128)S(1)} %get-tuple-element.43.refs_2_.refs_7_, ...), custom_call_target="tpu_custom_call" | custom-call | flops 201326592 | bytes 3407872 | tf_op jit(solution)/shard_map/forward/pallas_call | solution.py:397
  31.5 1.5 %collective-permute-done.refs_0_ = bf16[2,256,128]{2,1,0:T(8,128)(2,1)S(1)} collective-permute-done((bf16[2,256,128]{2,1,0:T(8,128)(2,1)S(1)}, bf16[2,256,128]{2,1,0:T(8,128)(2,1)S(1)}, u32[]{:S(2)}, u32[]{:S(2)}) %collective-permute-start) | collective-permute-done | bytes 131104 | tf_op jit(solution)/shard_map/ppermute | solution.py:465
  32.9 2.5 %turn.1 = (f32[2,8,1536]{2,1,0:T(8,128)S(1)}, f32[2,128,1536]{2,1,0:T(8,128)S(1)}, f32[2,128,1536]{2,1,0:T(8,128)S(1)}, bf16[2,256,128]{2,1,0:T(8,128)(2,1)S(1)}) custom-call(bf16[2,256,128]{2,1,0:T(8,128)(2,1)S(1)} %collective-permute-done.refs_0_, bf16[1,1536,256]{2,1,0:T(8,128)(2,1)S(1)} %copy-done, bf16[1,1536,256]{2,1,0:T(8,128)(2,1)S(1)} %copy-done.1, ...), custom_call_target="tpu_custom_call" | custom-call | flops 603979776 | bytes 3407872 | tf_op jit(solution)/shard_map/turn/pallas_call | solution.py:411
  35.4 0.2 collective-permute-start.8
  35.7 4.0 %backward.2 = (f32[2,128,1536]{2,1,0:T(8,128)S(1)}, bf16[2,256,128]{2,1,0:T(8,128)(2,1)S(1)}, bf16[2,256,128]{2,1,0:T(8,128)(2,1)S(1)}, bf16[2,256,128]{2,1,0:T(8,128)(2,1)S(1)}, bf16[2,256,128]{2,1,0:T(8,128)(2,1)S(1)}) custom-call(bf16[2,256,128]{2,1,0:T(8,128)(2,1)S(1)} %collective-permute-done.1.refs_0_, ...), custom_call_target="tpu_custom_call" | custom-call | flops 1610612736 | bytes 4194304 | tf_op jit(solution)/shard_map/backward/pallas_call | solution.py:432
  39.6 3.1 %collective-permute-start.9 = (bf16[2,256,128]{2,1,0:T(8,128)(2,1)S(1)}, bf16[2,256,128]{2,1,0:T(8,128)(2,1)S(1)}, u32[]{:S(2)}, u32[]{:S(2)}) collective-permute-start(bf16[2,256,128]{2,1,0:T(8,128)(2,1)S(1)} %get-tuple-element.56), channel_id=1, source_target_pairs={{13,0},{12,1},{15,2},{14,3},{9,4},{8,5},{11,6},{10,7},{21,8},{20,9... | collective-permute-start | bytes 393224 | tf_op jit(solution)/shard_map/ppermute | solution.py:474
  42.8 0.0 collective-permute-start.10
  42.8 2.2 %collective-permute-start.11 = (bf16[2,256,128]{2,1,0:T(8,128)(2,1)S(1)}, bf16[2,256,128]{2,1,0:T(8,128)(2,1)S(1)}, u32[]{:S(2)}, u32[]{:S(2)}) collective-permute-start(bf16[2,256,128]{2,1,0:T(8,128)(2,1)S(1)} %get-tuple-element.58), channel_id=1, source_target_pairs={{10,0},{11,1},{12,2},{13,3},{14,4},{15,5},{8,6},{9,7},{18,8},{19,9... | collective-permute-start | bytes 393224 | tf_op jit(solution)/shard_map/ppermute | solution.py:474
  45.0 0.0 collective-permute-start.12
  45.0 0.0 collective-permute-done.8.refs_0_
  45.0 2.9 %backward.3 = (f32[2,128,1536]{2,1,0:T(8,128)S(1)}, bf16[2,256,128]{2,1,0:T(8,128)(2,1)S(1)}, bf16[2,256,128]{2,1,0:T(8,128)(2,1)S(1)}, bf16[2,256,128]{2,1,0:T(8,128)(2,1)S(1)}) custom-call(bf16[2,256,128]{2,1,0:T(8,128)(2,1)S(1)} %collective-permute-done.8.refs_0_, bf16[2,256,128]{2,1,0:T(8,128)(2,1)S(1)} %collective-permute-done.5.refs_0_.refs_1_, ...), custom_call_target="tpu_custom_call" | custom-call | flops 1207959552 | bytes 3932160 | tf_op jit(solution)/shard_map/backward/pallas_call | solution.py:432
  47.9 1.3 %collective-permute-start.13 = (bf16[2,256,128]{2,1,0:T(8,128)(2,1)S(1)}, bf16[2,256,128]{2,1,0:T(8,128)(2,1)S(1)}, u32[]{:S(2)}, u32[]{:S(2)}) collective-permute-start(bf16[2,256,128]{2,1,0:T(8,128)(2,1)S(1)} %get-tuple-element.60), channel_id=1, source_target_pairs={{15,0},{14,1},{9,2},{8,3},{11,4},{10,5},{13,6},{12,7},{23,8},{22,9... | collective-permute-start | bytes 393224 | tf_op jit(solution)/shard_map/ppermute | solution.py:474
  49.1 0.8 %collective-permute-done.9 = bf16[2,256,128]{2,1,0:T(8,128)(2,1)S(1)} collective-permute-done((bf16[2,256,128]{2,1,0:T(8,128)(2,1)S(1)}, bf16[2,256,128]{2,1,0:T(8,128)(2,1)S(1)}, u32[]{:S(2)}, u32[]{:S(2)}) %collective-permute-start.9) | collective-permute-done | bytes 131104 | tf_op jit(solution)/shard_map/ppermute | solution.py:474
  49.9 5.3 %collective-permute-start.14 = (bf16[2,256,128]{2,1,0:T(8,128)(2,1)S(1)}, bf16[2,256,128]{2,1,0:T(8,128)(2,1)S(1)}, u32[]{:S(2)}, u32[]{:S(2)}) collective-permute-start(bf16[2,256,128]{2,1,0:T(8,128)(2,1)S(1)} %get-tuple-element.61), channel_id=1, source_target_pairs={{11,0},{10,1},{13,2},{12,3},{15,4},{14,5},{9,6},{8,7},{19,8},{18,9... | collective-permute-start | bytes 393224 | tf_op jit(solution)/shard_map/ppermute | solution.py:474
  55.3 0.0 collective-permute-done.10
  55.3 0.5 collective-permute-start.15
  55.8 1.2 %turned_back.2 = bf16[1,1536,256]{2,1,0:T(8,128)(2,1)} custom-call(f32[2,128,1536]{2,1,0:T(8,128)S(1)} %get-tuple-element.47.columns_ref), custom_call_target="tpu_custom_call" | custom-call | tf_op jit(solution)/shard_map/turned_back/pallas_call | solution.py:184
  56.9 1.2 %turned_back.3 = bf16[1,1536,256]{2,1,0:T(8,128)(2,1)} custom-call(f32[2,128,1536]{2,1,0:T(8,128)S(1)} %get-tuple-element.55.columns_ref), custom_call_target="tpu_custom_call" | custom-call | tf_op jit(solution)/shard_map/turned_back/pallas_call | solution.py:184
  58.1 0.0 collective-permute-done.11
  58.1 0.0 collective-permute-done.12
  58.1 0.0 collective-permute-done.13
  58.1 2.6 %collective-permute-done.14 = bf16[2,256,128]{2,1,0:T(8,128)(2,1)S(1)} collective-permute-done((bf16[2,256,128]{2,1,0:T(8,128)(2,1)S(1)}, bf16[2,256,128]{2,1,0:T(8,128)(2,1)S(1)}, u32[]{:S(2)}, u32[]{:S(2)}) %collective-permute-start.14) | collective-permute-done | bytes 131104 | tf_op jit(solution)/shard_map/ppermute | solution.py:474
  60.7 2.2 %collective-permute-done.15 = bf16[2,256,128]{2,1,0:T(8,128)(2,1)S(1)} collective-permute-done((bf16[2,256,128]{2,1,0:T(8,128)(2,1)S(1)}, bf16[2,256,128]{2,1,0:T(8,128)(2,1)S(1)}, u32[]{:S(2)}, u32[]{:S(2)}) %collective-permute-start.15) | collective-permute-done | bytes 131104 | tf_op jit(solution)/shard_map/ppermute | solution.py:474
  63.0 1.5 %unpack.1 = bf16[1,128,2,2048]{3,2,1,0:T(2,128)(2,1)} custom-call(bf16[2,128,2,128]{3,2,1,0:T(2,128)(2,1)S(1)} %bitcast.16, bf16[2,128,2,128]{3,2,1,0:T(2,128)(2,1)S(1)} %bitcast.17, bf16[2,128,2,128]{3,2,1,0:T(2,128)(2,1)S(1)} %bitcast.18, bf16[2,128,2,128]{3,2,1,0:T(2,128)(2,1)S(1)} %bitcast.19, bf16[2,128,2,128]{3,2,1,0:T(2,128)(2,1)S(1)} %bitcast.20, ...), custom_call_target="tpu_custom_call" | custom-call | tf_op jit(solution)/shard_map/unpack/pallas_call | solution.py:115
Async XLA Ops:
  0.6 16.3 %copy-start = (bf16[1,1536,256]{2,1,0:T(8,128)(2,1)S(1)}, bf16[1,1536,256]{2,1,0:T(8,128)(2,1)}, u32[]{:S(2)}) copy-start(bf16[1,1536,256]{2,1,0:T(8,128)(2,1)} %refs_6_.1) | copy-start | bytes 2359300
  0.6 1.3 %copy-start.2 = (bf16[1,128,2,2048]{3,2,1,0:T(2,128)(2,1)S(1)}, bf16[1,128,2,2048]{3,2,1,0:T(2,128)(2,1)}, u32[]{:S(2)}) copy-start(bf16[1,128,2,2048]{3,2,1,0:T(2,128)(2,1)} %pairs_ref.3) | copy-start | bytes 3145732
  2.4 14.9 %copy-start.1 = (bf16[1,1536,256]{2,1,0:T(8,128)(2,1)S(1)}, bf16[1,1536,256]{2,1,0:T(8,128)(2,1)}, u32[]{:S(2)}) copy-start(bf16[1,1536,256]{2,1,0:T(8,128)(2,1)} %refs_7_.1) | copy-start | bytes 2359300
  2.4 12.1 %collective-permute-start.6 = (bf16[2,256,128]{2,1,0:T(8,128)(2,1)S(1)}, bf16[2,256,128]{2,1,0:T(8,128)(2,1)S(1)}, u32[]{:S(2)}, u32[]{:S(2)}) collective-permute-start(bf16[2,256,128]{2,1,0:T(8,128)(2,1)S(1)} %bitcast.31), channel_id=1, source_target_pairs={{0,11},{1,10},{2,13},{3,12},{4,15},{5,14},{6,9},{7,8},{8,19},{9,18... | collective-permute-start | bytes 393224 | tf_op jit(solution)/shard_map/ppermute | solution.py:465
  5.9 10.5 %collective-permute-start.5 = (bf16[2,256,128]{2,1,0:T(8,128)(2,1)S(1)}, bf16[2,256,128]{2,1,0:T(8,128)(2,1)S(1)}, u32[]{:S(2)}, u32[]{:S(2)}) collective-permute-start(bf16[2,256,128]{2,1,0:T(8,128)(2,1)S(1)} %bitcast.30), channel_id=1, source_target_pairs={{0,15},{1,14},{2,9},{3,8},{4,11},{5,10},{6,13},{7,12},{8,23},{9,22... | collective-permute-start | bytes 393224 | tf_op jit(solution)/shard_map/ppermute | solution.py:465
  9.3 8.3 %collective-permute-start.7 = (bf16[2,256,128]{2,1,0:T(8,128)(2,1)S(1)}, bf16[2,256,128]{2,1,0:T(8,128)(2,1)S(1)}, u32[]{:S(2)}, u32[]{:S(2)}) collective-permute-start(bf16[2,256,128]{2,1,0:T(8,128)(2,1)S(1)} %bitcast.28), channel_id=1, source_target_pairs={{0,9},{1,8},{2,11},{3,10},{4,13},{5,12},{6,15},{7,14},{8,17},{9,16... | collective-permute-start | bytes 393224 | tf_op jit(solution)/shard_map/ppermute | solution.py:465
  10.9 12.8 %collective-permute-start.2 = (bf16[2,256,128]{2,1,0:T(8,128)(2,1)S(1)}, bf16[2,256,128]{2,1,0:T(8,128)(2,1)S(1)}, u32[]{:S(2)}, u32[]{:S(2)}) collective-permute-start(bf16[2,256,128]{2,1,0:T(8,128)(2,1)S(1)} %bitcast.29), channel_id=1, source_target_pairs={{0,10},{1,11},{2,12},{3,13},{4,14},{5,15},{6,8},{7,9},{8,18},{9,19... | collective-permute-start | bytes 393224 | tf_op jit(solution)/shard_map/ppermute | solution.py:465
  11.0 12.7 %collective-permute-start.3 = (bf16[2,256,128]{2,1,0:T(8,128)(2,1)S(1)}, bf16[2,256,128]{2,1,0:T(8,128)(2,1)S(1)}, u32[]{:S(2)}, u32[]{:S(2)}) collective-permute-start(bf16[2,256,128]{2,1,0:T(8,128)(2,1)S(1)} %bitcast.27), channel_id=1, source_target_pairs={{0,14},{1,15},{2,8},{3,9},{4,10},{5,11},{6,12},{7,13},{8,22},{9,23... | collective-permute-start | bytes 393224 | tf_op jit(solution)/shard_map/ppermute | solution.py:465
  14.5 9.3 %collective-permute-start.4 = (bf16[2,256,128]{2,1,0:T(8,128)(2,1)S(1)}, bf16[2,256,128]{2,1,0:T(8,128)(2,1)S(1)}, u32[]{:S(2)}, u32[]{:S(2)}) collective-permute-start(bf16[2,256,128]{2,1,0:T(8,128)(2,1)S(1)} %bitcast.26), channel_id=1, source_target_pairs={{0,8},{1,9},{2,10},{3,11},{4,12},{5,13},{6,14},{7,15},{8,16},{9,17... | collective-permute-start | bytes 393224 | tf_op jit(solution)/shard_map/ppermute | solution.py:465
  16.4 14.0 %collective-permute-start.1 = (bf16[2,256,128]{2,1,0:T(8,128)(2,1)S(1)}, bf16[2,256,128]{2,1,0:T(8,128)(2,1)S(1)}, u32[]{:S(2)}, u32[]{:S(2)}) collective-permute-start(bf16[2,256,128]{2,1,0:T(8,128)(2,1)S(1)} %bitcast.25), channel_id=1, source_target_pairs={{0,13},{1,12},{2,15},{3,14},{4,9},{5,8},{6,11},{7,10},{8,21},{9,20... | collective-permute-start | bytes 393224 | tf_op jit(solution)/shard_map/ppermute | solution.py:465
  17.6 15.4 %collective-permute-start = (bf16[2,256,128]{2,1,0:T(8,128)(2,1)S(1)}, bf16[2,256,128]{2,1,0:T(8,128)(2,1)S(1)}, u32[]{:S(2)}, u32[]{:S(2)}) collective-permute-start(bf16[2,256,128]{2,1,0:T(8,128)(2,1)S(1)} %bitcast.24), channel_id=1, source_target_pairs={{0,12},{1,13},{2,14},{3,15},{4,8},{5,9},{6,10},{7,11},{8,20},{9,21... | collective-permute-start | bytes 393224 | tf_op jit(solution)/shard_map/ppermute | solution.py:465
  35.4 9.6 %collective-permute-start.8 = (bf16[2,256,128]{2,1,0:T(8,128)(2,1)S(1)}, bf16[2,256,128]{2,1,0:T(8,128)(2,1)S(1)}, u32[]{:S(2)}, u32[]{:S(2)}) collective-permute-start(bf16[2,256,128]{2,1,0:T(8,128)(2,1)S(1)} %get-tuple-element.48), channel_id=1, source_target_pairs={{12,0},{13,1},{14,2},{15,3},{8,4},{9,5},{10,6},{11,7},{20,8},{21,9... | collective-permute-start | bytes 393224 | tf_op jit(solution)/shard_map/ppermute | solution.py:474
  39.6 10.3 %collective-permute-start.9 = (bf16[2,256,128]{2,1,0:T(8,128)(2,1)S(1)}, bf16[2,256,128]{2,1,0:T(8,128)(2,1)S(1)}, u32[]{:S(2)}, u32[]{:S(2)}) collective-permute-start(bf16[2,256,128]{2,1,0:T(8,128)(2,1)S(1)} %get-tuple-element.56), channel_id=1, source_target_pairs={{13,0},{12,1},{15,2},{14,3},{9,4},{8,5},{11,6},{10,7},{21,8},{20,9... | collective-permute-start | bytes 393224 | tf_op jit(solution)/shard_map/ppermute | solution.py:474
  42.8 12.5 %collective-permute-start.10 = (bf16[2,256,128]{2,1,0:T(8,128)(2,1)S(1)}, bf16[2,256,128]{2,1,0:T(8,128)(2,1)S(1)}, u32[]{:S(2)}, u32[]{:S(2)}) collective-permute-start(bf16[2,256,128]{2,1,0:T(8,128)(2,1)S(1)} %get-tuple-element.57), channel_id=1, source_target_pairs={{8,0},{9,1},{10,2},{11,3},{12,4},{13,5},{14,6},{15,7},{16,8},{17,9... | collective-permute-start | bytes 393224 | tf_op jit(solution)/shard_map/ppermute | solution.py:474
  42.8 15.3 %collective-permute-start.11 = (bf16[2,256,128]{2,1,0:T(8,128)(2,1)S(1)}, bf16[2,256,128]{2,1,0:T(8,128)(2,1)S(1)}, u32[]{:S(2)}, u32[]{:S(2)}) collective-permute-start(bf16[2,256,128]{2,1,0:T(8,128)(2,1)S(1)} %get-tuple-element.58), channel_id=1, source_target_pairs={{10,0},{11,1},{12,2},{13,3},{14,4},{15,5},{8,6},{9,7},{18,8},{19,9... | collective-permute-start | bytes 393224 | tf_op jit(solution)/shard_map/ppermute | solution.py:474
  45.0 13.1 %collective-permute-start.12 = (bf16[2,256,128]{2,1,0:T(8,128)(2,1)S(1)}, bf16[2,256,128]{2,1,0:T(8,128)(2,1)S(1)}, u32[]{:S(2)}, u32[]{:S(2)}) collective-permute-start(bf16[2,256,128]{2,1,0:T(8,128)(2,1)S(1)} %get-tuple-element.59), channel_id=1, source_target_pairs={{14,0},{15,1},{8,2},{9,3},{10,4},{11,5},{12,6},{13,7},{22,8},{23,9... | collective-permute-start | bytes 393224 | tf_op jit(solution)/shard_map/ppermute | solution.py:474
  47.9 10.2 %collective-permute-start.13 = (bf16[2,256,128]{2,1,0:T(8,128)(2,1)S(1)}, bf16[2,256,128]{2,1,0:T(8,128)(2,1)S(1)}, u32[]{:S(2)}, u32[]{:S(2)}) collective-permute-start(bf16[2,256,128]{2,1,0:T(8,128)(2,1)S(1)} %get-tuple-element.60), channel_id=1, source_target_pairs={{15,0},{14,1},{9,2},{8,3},{11,4},{10,5},{13,6},{12,7},{23,8},{22,9... | collective-permute-start | bytes 393224 | tf_op jit(solution)/shard_map/ppermute | solution.py:474
  49.9 10.8 %collective-permute-start.14 = (bf16[2,256,128]{2,1,0:T(8,128)(2,1)S(1)}, bf16[2,256,128]{2,1,0:T(8,128)(2,1)S(1)}, u32[]{:S(2)}, u32[]{:S(2)}) collective-permute-start(bf16[2,256,128]{2,1,0:T(8,128)(2,1)S(1)} %get-tuple-element.61), channel_id=1, source_target_pairs={{11,0},{10,1},{13,2},{12,3},{15,4},{14,5},{9,6},{8,7},{19,8},{18,9... | collective-permute-start | bytes 393224 | tf_op jit(solution)/shard_map/ppermute | solution.py:474
  55.3 7.7 %collective-permute-start.15 = (bf16[2,256,128]{2,1,0:T(8,128)(2,1)S(1)}, bf16[2,256,128]{2,1,0:T(8,128)(2,1)S(1)}, u32[]{:S(2)}, u32[]{:S(2)}) collective-permute-start(bf16[2,256,128]{2,1,0:T(8,128)(2,1)S(1)} %get-tuple-element.62), channel_id=1, source_target_pairs={{9,0},{8,1},{11,2},{10,3},{13,4},{12,5},{15,6},{14,7},{17,8},{16,9... | collective-permute-start | bytes 393224 | tf_op jit(solution)/shard_map/ppermute | solution.py:474

commit v19 on v18

--- a/solution.py
+++ b/solution.py
@@ -202,31 +202,47 @@
     return jnp.where(source == wanted, 1.0, 0.0).astype(jnp.bfloat16)
 
 
-def split_chunks(chunks, h, rows, k_ref=None, v_ref=None, kt_ref=None, vt_ref=None):
-    split = shuffle(rows, False)
+def reordered(blocks, join):
+    heads, pair_rows, _ = blocks[0].shape
+
+    def kernel(*refs):
+        order = shuffle(pair_rows // 2, join)
+        for block, out in zip(refs[: len(blocks)], refs[len(blocks) :]):
+            for h in range(heads):
+                out[h] = dot(order, block[h]).astype(out.dtype)
+
+    return pl.pallas_call(
+        kernel,
+        out_shape=[jax.ShapeDtypeStruct(b.shape, b.dtype) for b in blocks],
+        in_specs=[VMEM] * len(blocks),
+        out_specs=[VMEM] * len(blocks),
+        compiler_params=pltpu.CompilerParams(vmem_limit_bytes=24 * MIB),
+        name="reordered",
+    )(*blocks)
+
+
+def split_chunks(chunks, h, rows, refs, done):
+    k_ref, v_ref, kt_ref, vt_ref = refs
+    split = None if done else shuffle(rows, False)
     for i, chunk in enumerate(chunks):
-        both = dot(split, chunk[h])
+        both = chunk[h].astype(jnp.float32) if done else dot(split, chunk[h])
         here = slice(i * rows, (i + 1) * rows)
         keys, values = both[:rows], both[rows:]
-        if k_ref is not None:
-            k_ref[h, here, :] = keys.astype(jnp.bfloat16)
-        if v_ref is not None:
-            v_ref[h, here, :] = values.astype(jnp.bfloat16)
-        if kt_ref is not None:
-            kt_ref[h, :, here] = keys.T.astype(jnp.bfloat16)
-        if vt_ref is not None:
-            vt_ref[h, :HEAD, here] = values.T.astype(jnp.bfloat16)
-    if vt_ref is not None:
-        tail = (vt_ref.shape[1] - HEAD, vt_ref.shape[2])
-        vt_ref[h, HEAD:, :] = jnp.ones(tail, jnp.bfloat16)
-
-
-def join_chunks(outs, h, rows, gk_ref, gv_ref):
-    join = shuffle(rows, True)
+        k_ref[h, here, :] = keys.astype(jnp.bfloat16)
+        v_ref[h, here, :] = values.astype(jnp.bfloat16)
+        kt_ref[h, :, here] = keys.T.astype(jnp.bfloat16)
+        vt_ref[h, :HEAD, here] = values.T.astype(jnp.bfloat16)
+    tail = (vt_ref.shape[1] - HEAD, vt_ref.shape[2])
+    vt_ref[h, HEAD:, :] = jnp.ones(tail, jnp.bfloat16)
+
+
+def store_chunks(outs, h, rows, gk_ref, gv_ref, join):
+    order = shuffle(rows, True) if join else None
     for i, out in enumerate(outs):
         here = slice(i * rows, (i + 1) * rows)
         both = jnp.concatenate([gk_ref[h, here, :] * FACTOR, gv_ref[h, here, :]], axis=0)
-        out[h] = dot(join, both.astype(jnp.bfloat16)).astype(jnp.bfloat16)
+        both = both.astype(jnp.bfloat16)
+        out[h] = dot(order, both).astype(jnp.bfloat16) if join else both
 
 
 def raise_scores(keys, qt, values_t, before):
@@ -250,10 +266,10 @@
     qt_ref, refs = refs[0], refs[1:]
     if not first:
         stats_in, context_in, refs = refs[0], refs[1], refs[2:]
-    stats_ref, context_ref, low_ref, k_ref, vt_ref = refs
+    stats_ref, context_ref, low_ref, v_ref, kt_ref, k_ref, vt_ref = refs
     heads, pair_rows, _ = chunks[0].shape
     for h in range(heads):
-        split_chunks(chunks, h, pair_rows // 2, k_ref=k_ref, vt_ref=vt_ref)
+        split_chunks(chunks, h, pair_rows // 2, (k_ref, v_ref, kt_ref, vt_ref), False)
 
     @tiles(qt_ref.shape[2] // tile)
     def _(j):
@@ -291,7 +307,7 @@
     heads, pair_rows, _ = chunks[0].shape
     rows = pair_rows // 2
     for h in range(heads):
-        split_chunks(chunks, h, rows, k_ref, v_ref, kt_ref, vt_ref)
+        split_chunks(chunks, h, rows, (k_ref, v_ref, kt_ref, vt_ref), True)
     gk_ref[...] = jnp.zeros_like(gk_ref)
     gv_ref[...] = jnp.zeros_like(gv_ref)
 
@@ -316,26 +332,19 @@
             )
 
     for h in range(heads):
-        join_chunks(outs, h, rows, gk_ref, gv_ref)
-
-
-def backward_kernel(back, counts, tile, *refs):
+        store_chunks(outs, h, rows, gk_ref, gv_ref, False)
+
+
+def backward_kernel(back, counts, join, tile, *refs):
     refs = refs[back:]
-    groups = []
-    for count in counts:
-        groups.append((refs[:count], refs[count], refs[count + 1]))
-        refs = refs[count + 2 :]
-    q_ref, g_ref, gt_ref, stats_ref, grad_q_in = refs[:5]
-    grad_q_ref, refs = refs[5], refs[6:]
-    outs, refs = refs[: sum(counts)], refs[sum(counts) :]
-    scratch = [refs[i : i + 4] for i in range(0, len(refs), 4)]
-    heads, pair_rows, _ = groups[0][0][0].shape
-    rows = pair_rows // 2
-    for (chunks, _, _), (v_ref, kt_ref, gk_ref, gv_ref) in zip(groups, scratch):
-        for h in range(heads):
-            split_chunks(chunks, h, rows, v_ref=v_ref, kt_ref=kt_ref)
-        gk_ref[...] = jnp.zeros_like(gk_ref)
-        gv_ref[...] = jnp.zeros_like(gv_ref)
+    groups = [refs[4 * i : 4 * i + 4] for i in range(len(counts))]
+    refs = refs[4 * len(counts) :]
+    q_ref, g_ref, gt_ref, stats_ref, grad_q_in, grad_q_ref = refs[:6]
+    outs, refs = refs[6 : 6 + sum(counts)], refs[6 + sum(counts) :]
+    sums = [refs[i : i + 2] for i in range(0, len(refs), 2)]
+    heads, pair_rows, _ = outs[0].shape
+    for ref in refs:
+        ref[...] = jnp.zeros_like(ref)
 
     @tiles(gt_ref.shape[2] // tile)
     def _(j):
@@ -346,17 +355,17 @@
             gt = gt_ref[h, :, here]
             top, scale, row_dot = (stats_ref[h, i : i + 1, here] for i in range(3))
             grad_q = grad_q_in[h, :, here]
-            for (_, low_ref, then_ref), own in zip(groups, scratch):
+            for (low_ref, then_ref, v_ref, kt_ref), own in zip(groups, sums):
                 shrunk = jnp.exp2((then_ref[h, 0:1, here] - top) * EXPONENT)
                 raised = low_ref[h, :, here].astype(jnp.float32)
                 grad_q = grad_q + gradients(
-                    raised, scale * shrunk, row_dot, rows_here, gt, own, h
+                    raised, scale * shrunk, row_dot, rows_here, gt, (v_ref, kt_ref, *own), h
                 )
             grad_q_ref[h, :, here] = grad_q
 
-    for count, (_, _, gk_ref, gv_ref) in zip(counts, scratch):
+    for count, (gk_ref, gv_ref) in zip(counts, sums):
         for h in range(heads):
-            join_chunks(outs[:count], h, rows, gk_ref, gv_ref)
+            store_chunks(outs[:count], h, pair_rows // 2, gk_ref, gv_ref, join)
         outs = outs[count:]
 
 
@@ -394,18 +403,20 @@
     for group in groups[:-1]:
         count = len(group)
         low_shape = jax.ShapeDtypeStruct((heads, count * rows, tokens), jnp.bfloat16)
-        stats, context, low = pl.pallas_call(
+        v_shape = jax.ShapeDtypeStruct((heads, count * rows, HEAD), jnp.bfloat16)
+        kt_shape = jax.ShapeDtypeStruct((heads, HEAD, count * rows), jnp.bfloat16)
+        stats, context, *saved = pl.pallas_call(
             functools.partial(forward_kernel, count, not state, tile_of(count * rows, tokens)),
-            out_shape=[stats_shape, wide_shape, low_shape],
+            out_shape=[stats_shape, wide_shape, low_shape, v_shape, kt_shape],
             in_specs=[VMEM] * (count + 1 + len(state)),
-            out_specs=[VMEM] * 3,
+            out_specs=[VMEM] * 5,
             scratch_shapes=[natural(count), across(count, 16)],
             compiler_params=compiler_params,
             cost_estimate=cost(heads, count * rows, tokens, 2),
             name="forward",
         )(*group, qt, *state)
         state = [stats, context]
-        kept.append((low, stats))
+        kept.append((saved[0], stats, *saved[1:]))
 
     group, count = groups[-1], len(groups[-1])
     final, context, grad_q, *grads = pl.pallas_call(
@@ -427,20 +438,16 @@
         back = [] if first else returned[0]
         operands = []
         for i in part:
-            operands += [*groups[i], *kept[i]]
+            operands += kept[i]
         operands += [queries, upstream, gt, final, grad_q]
         outs = pl.pallas_call(
             functools.partial(
-                backward_kernel, len(back), counts, tile_of(max(counts) * rows, tokens)
+                backward_kernel, len(back), counts, not first, tile_of(max(counts) * rows, tokens)
             ),
             out_shape=[wide_shape] + shapes_of(sum((groups[i] for i in part), [])),
             in_specs=[ANY] * len(back) + [VMEM] * len(operands),
             out_specs=[VMEM] * (1 + sum(counts)),
-            scratch_shapes=[
-                shape
-                for count in counts
-                for shape in (natural(count), across(count), sums(count), sums(count))
-            ],
+            scratch_shapes=[sums(count) for count in counts for _ in range(2)],
             compiler_params=compiler_params,
             cost_estimate=cost(heads, sum(counts) * rows, tokens, 4),
             name="backward",
@@ -460,8 +467,10 @@
     blocks = []
     first = len(offsets[0])
     packed = pack(pairs, order[:first], heads) + pack(pairs, order[first:], heads)
+    packed = [block.reshape(heads, 2 * rows, HEAD) for block in packed]
+    final = len(offsets[-1])
+    packed[-final:] = reordered(packed[-final:], False)
     for offset, block in zip(order, packed):
-        block = block.reshape(heads, 2 * rows, HEAD)
         blocks.append(lax.ppermute(block, AXES, route(offset, False)))
     groups = []
     for group in offsets:
@@ -473,10 +482,12 @@
         sent = sorted(zip(offsets[i], grads), key=lambda s: (s[0][0] > 0) == (i == 1))
         back = [lax.ppermute(g, AXES, route(o, True)) for o, g in sent]
         homes.extend(o for o, _ in sent)
-        returned.extend(b.reshape(heads, rows, 2, HEAD) for b in back)
+        returned.append(back)
         return back
 
     context, grad_query = attend(groups, queries, upstream, send_back)
+    early = reordered(sum(returned[:-1], []), True)
+    returned = [b.reshape(heads, rows, 2, HEAD) for b in list(early) + returned[-1]]
     return context, grad_query, unpack(returned, homes, width)
 
 

time: 64.8 us -> 64 us (0.988)
    pallas_call x2 -> x4, Pallas kernels: 6.83 us -> 6.77 us  [the longest x2 6.06 us: attend(): pl.pallas_call(functools.partial(backward_kernel, len(back), counts, not...]
  transfers between devices with their start and end apart: 16 -> 16, of which waited for: 6 -> 6; matrix products, arithmetic and copies ran while one was open for 0% -> 0% of each run, Pallas kernels for 25% -> 26%
where the time goes in v19:
time: 64 us; the launch traced here: 63.9 us
  starting transfers between devices  29.9 us (47%)
  Pallas kernels  20.6 us (32%)
  waiting for transfers between devices  11.1 us (17%)
  local copies, waits for them, and re-layouts  1.3 us (2%)
  between operations  0.97 us (2%)
    ppermute x8, starting transfers between devices, shards(): blocks.append(lax.ppermute(block, AXES, route(offset, False)))  17.2 us
    ppermute x8, starting transfers between devices, send_back(): back = [lax.ppermute(g, AXES, route(o, True)) for o, g in sent]  12.7 us
    pallas_call x2, Pallas kernels, attend(): pl.pallas_call(functools.partial(backward_kernel, len(back), counts, not...  6.06 us
    pallas_call x3, Pallas kernels, attend(): pl.pallas_call(functools.partial(forward_kernel, count, not state, tile_o...  6.03 us
    ppermute x8, waiting for transfers between devices, shards(): blocks.append(lax.ppermute(block, AXES, route(offset, False)))  5.81 us
    ppermute x8, waiting for transfers between devices, send_back(): back = [lax.ppermute(g, AXES, route(o, True)) for o, g in sent]  5.33 us
    pallas_call x2, Pallas kernels, turned_back(): pl.pallas_call(kernel, out_shape=jax.ShapeDtypeStruct((1, tokens, heads *...  2.3 us
    pallas_call x1, Pallas kernels, attend(): pl.pallas_call(functools.partial(turn_kernel, count, tile_of(count * rows...  2.29 us
  transfers between devices with their start and end apart: 16, of which 6 were waited for; matrix products, arithmetic and copies ran while one was open for 0% of the time, Pallas kernels for 26%

profile of v19, /device:TPU:0, one launch (start us, length us, event | category | flops | bytes accessed | tf_op | source)
XLA Modules:
  0.0 63.9 jit_solution(15739414255827647941)
XLA Ops:
  0.6 0.0 copy-start
  0.6 0.0 copy-start.2
  0.6 1.3 %copy-done.2 = bf16[1,128,2,2048]{3,2,1,0:T(2,128)(2,1)S(1)} copy-done((bf16[1,128,2,2048]{3,2,1,0:T(2,128)(2,1)S(1)}, bf16[1,128,2,2048]{3,2,1,0:T(2,128)(2,1)}, u32[]{:S(2)}) %copy-start.2) | copy-done | bytes 1048600
  1.9 0.4 pack.3
  2.4 0.0 copy-start.1
  2.4 3.5 %collective-permute-start.6 = (bf16[2,256,128]{2,1,0:T(8,128)(2,1)S(1)}, bf16[2,256,128]{2,1,0:T(8,128)(2,1)S(1)}, u32[]{:S(2)}, u32[]{:S(2)}) collective-permute-start(bf16[2,256,128]{2,1,0:T(8,128)(2,1)S(1)} %bitcast.31), channel_id=1, source_target_pairs={{0,11},{1,10},{2,13},{3,12},{4,15},{5,14},{6,9},{7,8},{8,19},{9,18... | collective-permute-start | bytes 393224 | tf_op jit(solution)/shard_map/ppermute | solution.py:474
  5.9 3.4 %collective-permute-start.5 = (bf16[2,256,128]{2,1,0:T(8,128)(2,1)S(1)}, bf16[2,256,128]{2,1,0:T(8,128)(2,1)S(1)}, u32[]{:S(2)}, u32[]{:S(2)}) collective-permute-start(bf16[2,256,128]{2,1,0:T(8,128)(2,1)S(1)} %bitcast.30), channel_id=1, source_target_pairs={{0,15},{1,14},{2,9},{3,8},{4,11},{5,10},{6,13},{7,12},{8,23},{9,22... | collective-permute-start | bytes 393224 | tf_op jit(solution)/shard_map/ppermute | solution.py:474
  9.3 1.0 %collective-permute-start.7 = (bf16[2,256,128]{2,1,0:T(8,128)(2,1)S(1)}, bf16[2,256,128]{2,1,0:T(8,128)(2,1)S(1)}, u32[]{:S(2)}, u32[]{:S(2)}) collective-permute-start(bf16[2,256,128]{2,1,0:T(8,128)(2,1)S(1)} %bitcast.29), channel_id=1, source_target_pairs={{0,9},{1,8},{2,11},{3,10},{4,13},{5,12},{6,15},{7,14},{8,17},{9,16... | collective-permute-start | bytes 393224 | tf_op jit(solution)/shard_map/ppermute | solution.py:474
  10.2 0.7 %pack.2 = (bf16[2,128,2,128]{3,2,1,0:T(2,128)(2,1)S(1)}, bf16[2,128,2,128]{3,2,1,0:T(2,128)(2,1)S(1)}, bf16[2,128,2,128]{3,2,1,0:T(2,128)(2,1)S(1)}, bf16[2,128,...) custom-call(bf16[1,128,2,2048]{3,2,1,0:T(2,128)(2,1)S(1)} %copy-done.2), custom_call_target="tpu_custom_call" | custom-call | tf_op jit(solution)/shard_map/pack/pallas_call | solution.py:79
  10.9 0.1 collective-permute-start.2
  11.0 3.5 %collective-permute-start.3 = (bf16[2,256,128]{2,1,0:T(8,128)(2,1)S(1)}, bf16[2,256,128]{2,1,0:T(8,128)(2,1)S(1)}, u32[]{:S(2)}, u32[]{:S(2)}) collective-permute-start(bf16[2,256,128]{2,1,0:T(8,128)(2,1)S(1)} %bitcast.27), channel_id=1, source_target_pairs={{0,14},{1,15},{2,8},{3,9},{4,10},{5,11},{6,12},{7,13},{8,22},{9,23... | collective-permute-start | bytes 393224 | tf_op jit(solution)/shard_map/ppermute | solution.py:474
  14.5 0.0 collective-permute-done.6.refs_1_
  14.5 1.6 %collective-permute-start.4 = (bf16[2,256,128]{2,1,0:T(8,128)(2,1)S(1)}, bf16[2,256,128]{2,1,0:T(8,128)(2,1)S(1)}, u32[]{:S(2)}, u32[]{:S(2)}) collective-permute-start(bf16[2,256,128]{2,1,0:T(8,128)(2,1)S(1)} %bitcast.26), channel_id=1, source_target_pairs={{0,8},{1,9},{2,10},{3,11},{4,12},{5,13},{6,14},{7,15},{8,16},{9,17... | collective-permute-start | bytes 393224 | tf_op jit(solution)/shard_map/ppermute | solution.py:474
  16.1 0.3 collective-permute-done.5.refs_0_
  16.4 0.6 collective-permute-start.1
  17.0 0.2 reordered.2
  17.2 0.0 copy-done
  17.2 0.3 turned.2.refs_3_.refs_1_
  17.5 0.0 copy-done.1
  17.5 0.3 turned.3.refs_4_.refs_10_.refs_7_
  17.8 0.0 collective-permute-done.7.refs_2_
  17.8 3.6 %collective-permute-start = (bf16[2,256,128]{2,1,0:T(8,128)(2,1)S(1)}, bf16[2,256,128]{2,1,0:T(8,128)(2,1)S(1)}, u32[]{:S(2)}, u32[]{:S(2)}) collective-permute-start(bf16[2,256,128]{2,1,0:T(8,128)(2,1)S(1)} %reordered.2), channel_id=1, source_target_pairs={{0,12},{1,13},{2,14},{3,15},{4,8},{5,9},{6,10},{7,11},{8,20},{9,21... | collective-permute-start | bytes 393224 | tf_op jit(solution)/shard_map/ppermute | solution.py:474
  21.4 2.5 %forward.3 = (f32[2,8,1536]{2,1,0:T(8,128)S(1)}, f32[2,128,1536]{2,1,0:T(8,128)S(1)}, bf16[2,384,1536]{2,1,0:T(8,128)(2,1)S(1)}, bf16[2,384,128]{2,1,0:T(8,128)(2,1)S(1)}, bf16[2,128,384]{2,1,0:T(8,128)(2,1)S(1)}) custom-call(bf16[2,256,128]{2,1,0:T(8,128)(2,1)S(1)} %collective-permute-done.5.refs_0_, ...), custom_call_target="tpu_custom_call" | custom-call | flops 603979776 | bytes 3932160 | tf_op jit(solution)/shard_map/forward/pallas_call | solution.py:408
  23.9 0.0 collective-permute-done.2.refs_0_
  23.9 0.0 collective-permute-done.3.refs_1_
  23.9 0.0 collective-permute-done.4.refs_2_
  23.9 2.5 %forward.4 = (f32[2,8,1536]{2,1,0:T(8,128)S(1)}, f32[2,128,1536]{2,1,0:T(8,128)S(1)}, bf16[2,384,1536]{2,1,0:T(8,128)(2,1)S(1)}, bf16[2,384,128]{2,1,0:T(8,128)(2,1)S(1)}, bf16[2,128,384]{2,1,0:T(8,128)(2,1)S(1)}) custom-call(bf16[2,256,128]{2,1,0:T(8,128)(2,1)S(1)} %collective-permute-done.2.refs_0_, ...), custom_call_target="tpu_custom_call" | custom-call | flops 603979776 | bytes 3932160 | tf_op jit(solution)/shard_map/forward/pallas_call | solution.py:408
  26.4 4.0 %collective-permute-done.1.refs_0_ = bf16[2,256,128]{2,1,0:T(8,128)(2,1)S(1)} collective-permute-done((bf16[2,256,128]{2,1,0:T(8,128)(2,1)S(1)}, bf16[2,256,128]{2,1,0:T(8,128)(2,1)S(1)}, u32[]{:S(2)}, u32[]{:S(2)}) %collective-permute-start.1) | collective-permute-done | bytes 131104 | tf_op jit(solution)/shard_map/ppermute | solution.py:474
  30.4 1.0 %forward.5 = (f32[2,8,1536]{2,1,0:T(8,128)S(1)}, f32[2,128,1536]{2,1,0:T(8,128)S(1)}, bf16[2,128,1536]{2,1,0:T(8,128)(2,1)S(1)}, bf16[2,128,128]{2,1,0:T(8,128)(2,1)S(1)}, bf16[2,128,128]{2,1,0:T(8,128)(2,1)S(1)}) custom-call(bf16[2,256,128]{2,1,0:T(8,128)(2,1)S(1)} %collective-permute-done.1.refs_0_, bf16[2,128,1536]{2,1,0:T(8,128)(2,1)S(1)} %turned.2.refs_3_.refs_1_, ...), custom_call_target="tpu_custom_call" | custom-call | flops 201326592 | bytes 3407872 | tf_op jit(solution)/shard_map/forward/pallas_call | solution.py:408
  31.5 1.5 %collective-permute-done.refs_0_ = bf16[2,256,128]{2,1,0:T(8,128)(2,1)S(1)} collective-permute-done((bf16[2,256,128]{2,1,0:T(8,128)(2,1)S(1)}, bf16[2,256,128]{2,1,0:T(8,128)(2,1)S(1)}, u32[]{:S(2)}, u32[]{:S(2)}) %collective-permute-start) | collective-permute-done | bytes 131104 | tf_op jit(solution)/shard_map/ppermute | solution.py:474
  32.9 2.3 %turn.1 = (f32[2,8,1536]{2,1,0:T(8,128)S(1)}, f32[2,128,1536]{2,1,0:T(8,128)S(1)}, f32[2,128,1536]{2,1,0:T(8,128)S(1)}, bf16[2,256,128]{2,1,0:T(8,128)(2,1)S(1)}) custom-call(bf16[2,256,128]{2,1,0:T(8,128)(2,1)S(1)} %collective-permute-done.refs_0_, bf16[1,1536,256]{2,1,0:T(8,128)(2,1)S(1)} %copy-done, bf16[1,1536,256]{2,1,0:T(8,128)(2,1)S(1)} %copy-done.1, ...), custom_call_target="tpu_custom_call" | custom-call | flops 603979776 | bytes 3407872 | tf_op jit(solution)/shard_map/turn/pallas_call | solution.py:422
  35.2 0.2 collective-permute-start.8
  35.5 3.4 %backward.2 = (f32[2,128,1536]{2,1,0:T(8,128)S(1)}, bf16[2,256,128]{2,1,0:T(8,128)(2,1)S(1)}, bf16[2,256,128]{2,1,0:T(8,128)(2,1)S(1)}, bf16[2,256,128]{2,1,0:T(8,128)(2,1)S(1)}, bf16[2,256,128]{2,1,0:T(8,128)(2,1)S(1)}) custom-call(bf16[2,128,1536]{2,1,0:T(8,128)(2,1)S(1)} %get-tuple-element.64.refs_0_, ...), custom_call_target="tpu_custom_call" | custom-call | flops 1610612736 | bytes 4194304 | tf_op jit(solution)/shard_map/backward/pallas_call | solution.py:443
  38.9 3.1 %collective-permute-start.9 = (bf16[2,256,128]{2,1,0:T(8,128)(2,1)S(1)}, bf16[2,256,128]{2,1,0:T(8,128)(2,1)S(1)}, u32[]{:S(2)}, u32[]{:S(2)}) collective-permute-start(bf16[2,256,128]{2,1,0:T(8,128)(2,1)S(1)} %get-tuple-element.73), channel_id=1, source_target_pairs={{13,0},{12,1},{15,2},{14,3},{9,4},{8,5},{11,6},{10,7},{21,8},{20,9... | collective-permute-start | bytes 393224 | tf_op jit(solution)/shard_map/ppermute | solution.py:483
  42.0 0.0 collective-permute-start.10
  42.0 2.2 %collective-permute-start.11 = (bf16[2,256,128]{2,1,0:T(8,128)(2,1)S(1)}, bf16[2,256,128]{2,1,0:T(8,128)(2,1)S(1)}, u32[]{:S(2)}, u32[]{:S(2)}) collective-permute-start(bf16[2,256,128]{2,1,0:T(8,128)(2,1)S(1)} %get-tuple-element.75), channel_id=1, source_target_pairs={{10,0},{11,1},{12,2},{13,3},{14,4},{15,5},{8,6},{9,7},{18,8},{19,9... | collective-permute-start | bytes 393224 | tf_op jit(solution)/shard_map/ppermute | solution.py:483
  44.2 0.0 collective-permute-start.12
  44.2 0.0 collective-permute-done.8.refs_0_
  44.2 2.7 %backward.3 = (f32[2,128,1536]{2,1,0:T(8,128)S(1)}, bf16[2,256,128]{2,1,0:T(8,128)(2,1)S(1)}, bf16[2,256,128]{2,1,0:T(8,128)(2,1)S(1)}, bf16[2,256,128]{2,1,0:T(8,128)(2,1)S(1)}) custom-call(bf16[2,256,128]{2,1,0:T(8,128)(2,1)S(1)} %collective-permute-done.8.refs_0_, bf16[2,384,1536]{2,1,0:T(8,128)(2,1)S(1)} %get-tuple-element.60.refs_1_, ...), custom_call_target="tpu_custom_call" | custom-call | flops 1207959552 | bytes 3932160 | tf_op jit(solution)/shard_map/backward/pallas_call | solution.py:443
  46.9 1.3 %collective-permute-start.13 = (bf16[2,256,128]{2,1,0:T(8,128)(2,1)S(1)}, bf16[2,256,128]{2,1,0:T(8,128)(2,1)S(1)}, u32[]{:S(2)}, u32[]{:S(2)}) collective-permute-start(bf16[2,256,128]{2,1,0:T(8,128)(2,1)S(1)} %get-tuple-element.82), channel_id=1, source_target_pairs={{15,0},{14,1},{9,2},{8,3},{11,4},{10,5},{13,6},{12,7},{23,8},{22,9... | collective-permute-start | bytes 393224 | tf_op jit(solution)/shard_map/ppermute | solution.py:483
  48.2 1.0 %collective-permute-done.9.refs_1_ = bf16[2,256,128]{2,1,0:T(8,128)(2,1)S(1)} collective-permute-done((bf16[2,256,128]{2,1,0:T(8,128)(2,1)S(1)}, bf16[2,256,128]{2,1,0:T(8,128)(2,1)S(1)}, u32[]{:S(2)}, u32[]{:S(2)}) %collective-permute-start.9) | collective-permute-done | bytes 131104 | tf_op jit(solution)/shard_map/ppermute | solution.py:483
  49.2 5.6 %collective-permute-start.14 = (bf16[2,256,128]{2,1,0:T(8,128)(2,1)S(1)}, bf16[2,256,128]{2,1,0:T(8,128)(2,1)S(1)}, u32[]{:S(2)}, u32[]{:S(2)}) collective-permute-start(bf16[2,256,128]{2,1,0:T(8,128)(2,1)S(1)} %get-tuple-element.83), channel_id=1, source_target_pairs={{11,0},{10,1},{13,2},{12,3},{15,4},{14,5},{9,6},{8,7},{19,8},{18,9... | collective-permute-start | bytes 393224 | tf_op jit(solution)/shard_map/ppermute | solution.py:483
  54.8 0.0 collective-permute-done.10.refs_2_
  54.8 0.2 collective-permute-start.15
  55.1 1.2 %turned_back.2 = bf16[1,1536,256]{2,1,0:T(8,128)(2,1)} custom-call(f32[2,128,1536]{2,1,0:T(8,128)S(1)} %get-tuple-element.58.columns_ref), custom_call_target="tpu_custom_call" | custom-call | tf_op jit(solution)/shard_map/turned_back/pallas_call | solution.py:184
  56.2 1.2 %turned_back.3 = bf16[1,1536,256]{2,1,0:T(8,128)(2,1)} custom-call(f32[2,128,1536]{2,1,0:T(8,128)S(1)} %get-tuple-element.72.columns_ref), custom_call_target="tpu_custom_call" | custom-call | tf_op jit(solution)/shard_map/turned_back/pallas_call | solution.py:184
  57.4 0.0 collective-permute-done.11.refs_3_
  57.4 0.0 collective-permute-done.12.refs_4_
  57.4 0.5 reordered.3
  57.9 0.0 collective-permute-done.13
  57.9 1.9 %collective-permute-done.14 = bf16[2,256,128]{2,1,0:T(8,128)(2,1)S(1)} collective-permute-done((bf16[2,256,128]{2,1,0:T(8,128)(2,1)S(1)}, bf16[2,256,128]{2,1,0:T(8,128)(2,1)S(1)}, u32[]{:S(2)}, u32[]{:S(2)}) %collective-permute-start.14) | collective-permute-done | bytes 131104 | tf_op jit(solution)/shard_map/ppermute | solution.py:483
  59.8 2.4 %collective-permute-done.15 = bf16[2,256,128]{2,1,0:T(8,128)(2,1)S(1)} collective-permute-done((bf16[2,256,128]{2,1,0:T(8,128)(2,1)S(1)}, bf16[2,256,128]{2,1,0:T(8,128)(2,1)S(1)}, u32[]{:S(2)}, u32[]{:S(2)}) %collective-permute-start.15) | collective-permute-done | bytes 131104 | tf_op jit(solution)/shard_map/ppermute | solution.py:483
  62.2 1.5 %unpack.1 = bf16[1,128,2,2048]{3,2,1,0:T(2,128)(2,1)} custom-call(bf16[2,128,2,128]{3,2,1,0:T(2,128)(2,1)S(1)} %bitcast.19, bf16[2,128,2,128]{3,2,1,0:T(2,128)(2,1)S(1)} %bitcast.20, bf16[2,128,2,128]{3,2,1,0:T(2,128)(2,1)S(1)} %bitcast.21, bf16[2,128,2,128]{3,2,1,0:T(2,128)(2,1)S(1)} %bitcast.22, bf16[2,128,2,128]{3,2,1,0:T(2,128)(2,1)S(1)} %bitcast.23, ...), custom_call_target="tpu_custom_call" | custom-call | tf_op jit(solution)/shard_map/unpack/pallas_call | solution.py:115
Async XLA Ops:
  0.6 16.6 %copy-start = (bf16[1,1536,256]{2,1,0:T(8,128)(2,1)S(1)}, bf16[1,1536,256]{2,1,0:T(8,128)(2,1)}, u32[]{:S(2)}) copy-start(bf16[1,1536,256]{2,1,0:T(8,128)(2,1)} %refs_5_.1) | copy-start | bytes 2359300
  0.6 1.3 %copy-start.2 = (bf16[1,128,2,2048]{3,2,1,0:T(2,128)(2,1)S(1)}, bf16[1,128,2,2048]{3,2,1,0:T(2,128)(2,1)}, u32[]{:S(2)}) copy-start(bf16[1,128,2,2048]{3,2,1,0:T(2,128)(2,1)} %pairs_ref.3) | copy-start | bytes 3145732
  2.4 15.1 %copy-start.1 = (bf16[1,1536,256]{2,1,0:T(8,128)(2,1)S(1)}, bf16[1,1536,256]{2,1,0:T(8,128)(2,1)}, u32[]{:S(2)}) copy-start(bf16[1,1536,256]{2,1,0:T(8,128)(2,1)} %refs_6_.1) | copy-start | bytes 2359300
  2.4 12.1 %collective-permute-start.6 = (bf16[2,256,128]{2,1,0:T(8,128)(2,1)S(1)}, bf16[2,256,128]{2,1,0:T(8,128)(2,1)S(1)}, u32[]{:S(2)}, u32[]{:S(2)}) collective-permute-start(bf16[2,256,128]{2,1,0:T(8,128)(2,1)S(1)} %bitcast.31), channel_id=1, source_target_pairs={{0,11},{1,10},{2,13},{3,12},{4,15},{5,14},{6,9},{7,8},{8,19},{9,18... | collective-permute-start | bytes 393224 | tf_op jit(solution)/shard_map/ppermute | solution.py:474
  5.9 10.5 %collective-permute-start.5 = (bf16[2,256,128]{2,1,0:T(8,128)(2,1)S(1)}, bf16[2,256,128]{2,1,0:T(8,128)(2,1)S(1)}, u32[]{:S(2)}, u32[]{:S(2)}) collective-permute-start(bf16[2,256,128]{2,1,0:T(8,128)(2,1)S(1)} %bitcast.30), channel_id=1, source_target_pairs={{0,15},{1,14},{2,9},{3,8},{4,11},{5,10},{6,13},{7,12},{8,23},{9,22... | collective-permute-start | bytes 393224 | tf_op jit(solution)/shard_map/ppermute | solution.py:474
  9.3 8.5 %collective-permute-start.7 = (bf16[2,256,128]{2,1,0:T(8,128)(2,1)S(1)}, bf16[2,256,128]{2,1,0:T(8,128)(2,1)S(1)}, u32[]{:S(2)}, u32[]{:S(2)}) collective-permute-start(bf16[2,256,128]{2,1,0:T(8,128)(2,1)S(1)} %bitcast.29), channel_id=1, source_target_pairs={{0,9},{1,8},{2,11},{3,10},{4,13},{5,12},{6,15},{7,14},{8,17},{9,16... | collective-permute-start | bytes 393224 | tf_op jit(solution)/shard_map/ppermute | solution.py:474
  10.9 13.0 %collective-permute-start.2 = (bf16[2,256,128]{2,1,0:T(8,128)(2,1)S(1)}, bf16[2,256,128]{2,1,0:T(8,128)(2,1)S(1)}, u32[]{:S(2)}, u32[]{:S(2)}) collective-permute-start(bf16[2,256,128]{2,1,0:T(8,128)(2,1)S(1)} %bitcast.28), channel_id=1, source_target_pairs={{0,10},{1,11},{2,12},{3,13},{4,14},{5,15},{6,8},{7,9},{8,18},{9,19... | collective-permute-start | bytes 393224 | tf_op jit(solution)/shard_map/ppermute | solution.py:474
  11.0 12.9 %collective-permute-start.3 = (bf16[2,256,128]{2,1,0:T(8,128)(2,1)S(1)}, bf16[2,256,128]{2,1,0:T(8,128)(2,1)S(1)}, u32[]{:S(2)}, u32[]{:S(2)}) collective-permute-start(bf16[2,256,128]{2,1,0:T(8,128)(2,1)S(1)} %bitcast.27), channel_id=1, source_target_pairs={{0,14},{1,15},{2,8},{3,9},{4,10},{5,11},{6,12},{7,13},{8,22},{9,23... | collective-permute-start | bytes 393224 | tf_op jit(solution)/shard_map/ppermute | solution.py:474
  14.5 9.4 %collective-permute-start.4 = (bf16[2,256,128]{2,1,0:T(8,128)(2,1)S(1)}, bf16[2,256,128]{2,1,0:T(8,128)(2,1)S(1)}, u32[]{:S(2)}, u32[]{:S(2)}) collective-permute-start(bf16[2,256,128]{2,1,0:T(8,128)(2,1)S(1)} %bitcast.26), channel_id=1, source_target_pairs={{0,8},{1,9},{2,10},{3,11},{4,12},{5,13},{6,14},{7,15},{8,16},{9,17... | collective-permute-start | bytes 393224 | tf_op jit(solution)/shard_map/ppermute | solution.py:474
  16.4 14.0 %collective-permute-start.1 = (bf16[2,256,128]{2,1,0:T(8,128)(2,1)S(1)}, bf16[2,256,128]{2,1,0:T(8,128)(2,1)S(1)}, u32[]{:S(2)}, u32[]{:S(2)}) collective-permute-start(bf16[2,256,128]{2,1,0:T(8,128)(2,1)S(1)} %bitcast.25), channel_id=1, source_target_pairs={{0,13},{1,12},{2,15},{3,14},{4,9},{5,8},{6,11},{7,10},{8,21},{9,20... | collective-permute-start | bytes 393224 | tf_op jit(solution)/shard_map/ppermute | solution.py:474
  17.8 15.2 %collective-permute-start = (bf16[2,256,128]{2,1,0:T(8,128)(2,1)S(1)}, bf16[2,256,128]{2,1,0:T(8,128)(2,1)S(1)}, u32[]{:S(2)}, u32[]{:S(2)}) collective-permute-start(bf16[2,256,128]{2,1,0:T(8,128)(2,1)S(1)} %reordered.2), channel_id=1, source_target_pairs={{0,12},{1,13},{2,14},{3,15},{4,8},{5,9},{6,10},{7,11},{8,20},{9,21... | collective-permute-start | bytes 393224 | tf_op jit(solution)/shard_map/ppermute | solution.py:474
  35.2 9.0 %collective-permute-start.8 = (bf16[2,256,128]{2,1,0:T(8,128)(2,1)S(1)}, bf16[2,256,128]{2,1,0:T(8,128)(2,1)S(1)}, u32[]{:S(2)}, u32[]{:S(2)}) collective-permute-start(bf16[2,256,128]{2,1,0:T(8,128)(2,1)S(1)} %get-tuple-element.59), channel_id=1, source_target_pairs={{12,0},{13,1},{14,2},{15,3},{8,4},{9,5},{10,6},{11,7},{20,8},{21,9... | collective-permute-start | bytes 393224 | tf_op jit(solution)/shard_map/ppermute | solution.py:483
  38.9 10.3 %collective-permute-start.9 = (bf16[2,256,128]{2,1,0:T(8,128)(2,1)S(1)}, bf16[2,256,128]{2,1,0:T(8,128)(2,1)S(1)}, u32[]{:S(2)}, u32[]{:S(2)}) collective-permute-start(bf16[2,256,128]{2,1,0:T(8,128)(2,1)S(1)} %get-tuple-element.73), channel_id=1, source_target_pairs={{13,0},{12,1},{15,2},{14,3},{9,4},{8,5},{11,6},{10,7},{21,8},{20,9... | collective-permute-start | bytes 393224 | tf_op jit(solution)/shard_map/ppermute | solution.py:483
  42.0 12.8 %collective-permute-start.10 = (bf16[2,256,128]{2,1,0:T(8,128)(2,1)S(1)}, bf16[2,256,128]{2,1,0:T(8,128)(2,1)S(1)}, u32[]{:S(2)}, u32[]{:S(2)}) collective-permute-start(bf16[2,256,128]{2,1,0:T(8,128)(2,1)S(1)} %get-tuple-element.74), channel_id=1, source_target_pairs={{8,0},{9,1},{10,2},{11,3},{12,4},{13,5},{14,6},{15,7},{16,8},{17,9... | collective-permute-start | bytes 393224 | tf_op jit(solution)/shard_map/ppermute | solution.py:483
  42.0 15.4 %collective-permute-start.11 = (bf16[2,256,128]{2,1,0:T(8,128)(2,1)S(1)}, bf16[2,256,128]{2,1,0:T(8,128)(2,1)S(1)}, u32[]{:S(2)}, u32[]{:S(2)}) collective-permute-start(bf16[2,256,128]{2,1,0:T(8,128)(2,1)S(1)} %get-tuple-element.75), channel_id=1, source_target_pairs={{10,0},{11,1},{12,2},{13,3},{14,4},{15,5},{8,6},{9,7},{18,8},{19,9... | collective-permute-start | bytes 393224 | tf_op jit(solution)/shard_map/ppermute | solution.py:483
  44.2 13.1 %collective-permute-start.12 = (bf16[2,256,128]{2,1,0:T(8,128)(2,1)S(1)}, bf16[2,256,128]{2,1,0:T(8,128)(2,1)S(1)}, u32[]{:S(2)}, u32[]{:S(2)}) collective-permute-start(bf16[2,256,128]{2,1,0:T(8,128)(2,1)S(1)} %get-tuple-element.76), channel_id=1, source_target_pairs={{14,0},{15,1},{8,2},{9,3},{10,4},{11,5},{12,6},{13,7},{22,8},{23,9... | collective-permute-start | bytes 393224 | tf_op jit(solution)/shard_map/ppermute | solution.py:483
  46.9 10.9 %collective-permute-start.13 = (bf16[2,256,128]{2,1,0:T(8,128)(2,1)S(1)}, bf16[2,256,128]{2,1,0:T(8,128)(2,1)S(1)}, u32[]{:S(2)}, u32[]{:S(2)}) collective-permute-start(bf16[2,256,128]{2,1,0:T(8,128)(2,1)S(1)} %get-tuple-element.82), channel_id=1, source_target_pairs={{15,0},{14,1},{9,2},{8,3},{11,4},{10,5},{13,6},{12,7},{23,8},{22,9... | collective-permute-start | bytes 393224 | tf_op jit(solution)/shard_map/ppermute | solution.py:483
  49.2 10.6 %collective-permute-start.14 = (bf16[2,256,128]{2,1,0:T(8,128)(2,1)S(1)}, bf16[2,256,128]{2,1,0:T(8,128)(2,1)S(1)}, u32[]{:S(2)}, u32[]{:S(2)}) collective-permute-start(bf16[2,256,128]{2,1,0:T(8,128)(2,1)S(1)} %get-tuple-element.83), channel_id=1, source_target_pairs={{11,0},{10,1},{13,2},{12,3},{15,4},{14,5},{9,6},{8,7},{19,8},{18,9... | collective-permute-start | bytes 393224 | tf_op jit(solution)/shard_map/ppermute | solution.py:483
  54.8 7.4 %collective-permute-start.15 = (bf16[2,256,128]{2,1,0:T(8,128)(2,1)S(1)}, bf16[2,256,128]{2,1,0:T(8,128)(2,1)S(1)}, u32[]{:S(2)}, u32[]{:S(2)}) collective-permute-start(bf16[2,256,128]{2,1,0:T(8,128)(2,1)S(1)} %get-tuple-element.84), channel_id=1, source_target_pairs={{9,0},{8,1},{11,2},{10,3},{13,4},{12,5},{15,6},{14,7},{17,8},{16,9... | collective-permute-start | bytes 393224 | tf_op jit(solution)/shard_map/ppermute | solution.py:483

commit v20 on v19

--- a/solution.py
+++ b/solution.py
@@ -170,25 +170,27 @@
     return 256 if tokens % 256 == 0 else tokens
 
 
-def turned_back(columns, dtype):
-    heads, _, tokens = columns.shape
+def turned_back(parts, dtype):
+    tokens = parts[0].shape[2]
+    heads = sum(p.shape[0] for p in parts)
     tile = 256 if tokens % 256 == 0 else tokens
 
-    def kernel(columns_ref, out_ref):
-        for h in range(heads):
+    def kernel(*refs):
+        out_ref = refs[-1]
+        sources = [(ref, k) for ref in refs[:-1] for k in range(ref.shape[0])]
+        for h, (ref, k) in enumerate(sources):
             for j in range(tokens // tile):
                 here = slice(j * tile, (j + 1) * tile)
-                block = columns_ref[h, :, here].T.astype(dtype)
-                out_ref[0, here, h * HEAD : (h + 1) * HEAD] = block
+                out_ref[0, here, h * HEAD : (h + 1) * HEAD] = ref[k, :, here].T.astype(dtype)
 
     return pl.pallas_call(
         kernel,
         out_shape=jax.ShapeDtypeStruct((1, tokens, heads * HEAD), dtype),
-        in_specs=[VMEM],
+        in_specs=[VMEM] * len(parts),
         out_specs=VMEM,
         compiler_params=pltpu.CompilerParams(vmem_limit_bytes=16 * MIB),
         name="turned_back",
-    )(columns)
+    )(*parts)
 
 
 def dot(a, b, contract=((1,), (0,))):
@@ -202,23 +204,33 @@
     return jnp.where(source == wanted, 1.0, 0.0).astype(jnp.bfloat16)
 
 
-def reordered(blocks, join):
-    heads, pair_rows, _ = blocks[0].shape
+def reordered(parts, join, apart=False):
+    pair_rows = parts[0][0].shape[1]
+    heads = sum(b.shape[0] for b in parts[0])
+    sizes = [1] * heads if apart else [heads]
 
     def kernel(*refs):
         order = shuffle(pair_rows // 2, join)
-        for block, out in zip(refs[: len(blocks)], refs[len(blocks) :]):
-            for h in range(heads):
-                out[h] = dot(order, block[h]).astype(out.dtype)
+        ins, outs = refs[: sum(map(len, parts))], refs[sum(map(len, parts)) :]
+        for part in parts:
+            sources = [(ref, h) for ref in ins[: len(part)] for h in range(ref.shape[0])]
+            targets = [(ref, h) for ref in outs[: len(sizes)] for h in range(ref.shape[0])]
+            for (source, h), (target, k) in zip(sources, targets):
+                target[k] = dot(order, source[h]).astype(target.dtype)
+            ins, outs = ins[len(part) :], outs[len(sizes) :]
 
     return pl.pallas_call(
         kernel,
-        out_shape=[jax.ShapeDtypeStruct(b.shape, b.dtype) for b in blocks],
-        in_specs=[VMEM] * len(blocks),
-        out_specs=[VMEM] * len(blocks),
+        out_shape=[
+            jax.ShapeDtypeStruct((size, pair_rows, HEAD), part[0].dtype)
+            for part in parts
+            for size in sizes
+        ],
+        in_specs=[VMEM] * sum(map(len, parts)),
+        out_specs=[VMEM] * (len(parts) * len(sizes)),
         compiler_params=pltpu.CompilerParams(vmem_limit_bytes=24 * MIB),
         name="reordered",
-    )(*blocks)
+    )(*sum(parts, []))
 
 
 def split_chunks(chunks, h, rows, refs, done):
@@ -298,51 +310,57 @@
     return dot(kt_ref[h], grad_scores) * FACTOR
 
 
-def turn_kernel(count, tile, *refs):
+def turn_kernel(count, head, tile, *refs):
     chunks, refs = refs[:count], refs[count:]
     q_ref, g_ref, qt_ref, gt_ref, stats_in, context_in = refs[:6]
     stats_ref, context_ref, grad_q_ref = refs[6:9]
     outs, refs = refs[9 : 9 + count], refs[9 + count :]
     k_ref, vt_ref, v_ref, kt_ref, gk_ref, gv_ref = refs
-    heads, pair_rows, _ = chunks[0].shape
-    rows = pair_rows // 2
-    for h in range(heads):
-        split_chunks(chunks, h, rows, (k_ref, v_ref, kt_ref, vt_ref), True)
+    rows = chunks[0].shape[1] // 2
+    columns = slice(head * HEAD, (head + 1) * HEAD)
+    split_chunks(chunks, 0, rows, (k_ref, v_ref, kt_ref, vt_ref), True)
     gk_ref[...] = jnp.zeros_like(gk_ref)
     gv_ref[...] = jnp.zeros_like(gv_ref)
 
     @tiles(qt_ref.shape[2] // tile)
     def _(j):
         here = tokens_of(j, tile)
-        for h in range(heads):
-            qt, gt = qt_ref[h, :, here], gt_ref[h, :, here]
-            before = (stats_in[h, 0:1, here], stats_in[h, 1:2, here], context_in[h, :, here])
-            raised, _, top, total, context = raise_scores(k_ref[h], qt, vt_ref[h], before)
-            columns = slice(h * HEAD, (h + 1) * HEAD)
-            rows_here = q_ref[0, here, columns], g_ref[0, here, columns]
-            scale = 1.0 / total
-            context = context * scale
-            row_dot = jnp.sum(gt.astype(jnp.float32) * context, axis=0, keepdims=True)
-            context_ref[h, :, here] = context
-            stats_ref[h, 0:1, here] = top
-            stats_ref[h, 1:2, here] = scale
-            stats_ref[h, 2:3, here] = row_dot
-            grad_q_ref[h, :, here] = gradients(
-                raised, scale, row_dot, rows_here, gt, (v_ref, kt_ref, gk_ref, gv_ref), h
-            )
-
-    for h in range(heads):
-        store_chunks(outs, h, rows, gk_ref, gv_ref, False)
-
-
-def backward_kernel(back, counts, join, tile, *refs):
+        qt, gt = qt_ref[head, :, here], gt_ref[head, :, here]
+        before = (
+            stats_in[head, 0:1, here],
+            stats_in[head, 1:2, here],
+            context_in[head, :, here],
+        )
+        raised, _, top, total, context = raise_scores(k_ref[0], qt, vt_ref[0], before)
+        rows_here = q_ref[0, here, columns], g_ref[0, here, columns]
+        scale = 1.0 / total
+        context = context * scale
+        row_dot = jnp.sum(gt.astype(jnp.float32) * context, axis=0, keepdims=True)
+        context_ref[0, :, here] = context
+        stats_ref[0, 0:1, here] = top
+        stats_ref[0, 1:2, here] = scale
+        stats_ref[0, 2:3, here] = row_dot
+        grad_q_ref[0, :, here] = gradients(
+            raised, scale, row_dot, rows_here, gt, (v_ref, kt_ref, gk_ref, gv_ref), 0
+        )
+
+    store_chunks(outs, 0, rows, gk_ref, gv_ref, False)
+
+
+def backward_kernel(back, counts, heads, joined, join, tile, *refs):
     refs = refs[back:]
     groups = [refs[4 * i : 4 * i + 4] for i in range(len(counts))]
     refs = refs[4 * len(counts) :]
-    q_ref, g_ref, gt_ref, stats_ref, grad_q_in, grad_q_ref = refs[:6]
-    outs, refs = refs[6 : 6 + sum(counts)], refs[6 + sum(counts) :]
+    q_ref, g_ref, gt_ref, refs = refs[0], refs[1], refs[2], refs[3:]
+    stats, refs = refs[:heads], refs[heads:]
+    if joined:
+        grads_in, refs = [refs[0].at[h : h + 1] for h in range(heads)], refs[1:]
+    else:
+        grads_in, refs = refs[:heads], refs[heads:]
+    grad_q_ref, refs = refs[0], refs[1:]
+    outs, refs = refs[: sum(counts)], refs[sum(counts) :]
     sums = [refs[i : i + 2] for i in range(0, len(refs), 2)]
-    heads, pair_rows, _ = outs[0].shape
+    pair_rows = outs[0].shape[1]
     for ref in refs:
         ref[...] = jnp.zeros_like(ref)
 
@@ -353,8 +371,8 @@
             columns = slice(h * HEAD, (h + 1) * HEAD)
             rows_here = q_ref[0, here, columns], g_ref[0, here, columns]
             gt = gt_ref[h, :, here]
-            top, scale, row_dot = (stats_ref[h, i : i + 1, here] for i in range(3))
-            grad_q = grad_q_in[h, :, here]
+            top, scale, row_dot = (stats[h][0, i : i + 1, here] for i in range(3))
+            grad_q = grads_in[h][0, :, here]
             for (low_ref, then_ref, v_ref, kt_ref), own in zip(groups, sums):
                 shrunk = jnp.exp2((then_ref[h, 0:1, here] - top) * EXPONENT)
                 raised = low_ref[h, :, here].astype(jnp.float32)
@@ -377,10 +395,10 @@
     )
 
 
-def attend(groups, queries, upstream, send_back):
+def attend(groups, final_blocks, queries, upstream, send_back):
     heads, pair_rows, _ = groups[0][0].shape
     rows = pair_rows // 2
-    enc_len = sum(len(g) for g in groups) * rows
+    enc_len = (sum(len(g) for g in groups) + len(final_blocks[0])) * rows
     tokens = queries.shape[1]
     qt, gt = turned(queries), turned(upstream)
     stats_shape = jax.ShapeDtypeStruct((heads, 8, tokens), jnp.float32)
@@ -400,7 +418,7 @@
         return [jax.ShapeDtypeStruct(c.shape, c.dtype) for c in group]
 
     state, kept = [], []
-    for group in groups[:-1]:
+    for group in groups:
         count = len(group)
         low_shape = jax.ShapeDtypeStruct((heads, count * rows, tokens), jnp.bfloat16)
         v_shape = jax.ShapeDtypeStruct((heads, count * rows, HEAD), jnp.bfloat16)
@@ -418,45 +436,64 @@
         state = [stats, context]
         kept.append((saved[0], stats, *saved[1:]))
 
-    group, count = groups[-1], len(groups[-1])
-    final, context, grad_q, *grads = pl.pallas_call(
-        functools.partial(turn_kernel, count, tile_of(count * rows, tokens)),
-        out_shape=[stats_shape, wide_shape, wide_shape] + shapes_of(group),
-        in_specs=[VMEM] * (count + 6),
-        out_specs=[VMEM] * (count + 3),
-        scratch_shapes=[natural(count), across(count, 16), natural(count), across(count)]
-        + [sums(count)] * 2,
-        compiler_params=compiler_params,
-        cost_estimate=cost(heads, count * rows, tokens, 6),
-        name="turn",
-    )(*group, queries, upstream, qt, gt, *state)
-    returned = [send_back(len(groups) - 1, grads)]
-
-    for part in (list(range(len(groups) - 2, 0, -1)), [0]):
+    stats_one = jax.ShapeDtypeStruct((1, 8, tokens), jnp.float32)
+    wide_one = jax.ShapeDtypeStruct((1, HEAD, tokens), jnp.float32)
+    final, contexts, grads_q, back = [], [], [], []
+    for h, group in enumerate(final_blocks):
+        count = len(group)
+        stats, context, grad_q, *grads = pl.pallas_call(
+            functools.partial(turn_kernel, count, h, tile_of(count * rows, tokens)),
+            out_shape=[stats_one, wide_one, wide_one] + shapes_of(group),
+            in_specs=[VMEM] * (count + 6),
+            out_specs=[VMEM] * (count + 3),
+            scratch_shapes=[
+                pltpu.VMEM((1, count * rows, HEAD), jnp.bfloat16),
+                pltpu.VMEM((1, HEAD + 16, count * rows), jnp.bfloat16),
+                pltpu.VMEM((1, count * rows, HEAD), jnp.bfloat16),
+                pltpu.VMEM((1, HEAD, count * rows), jnp.bfloat16),
+                pltpu.VMEM((1, count * rows, HEAD), jnp.float32),
+                pltpu.VMEM((1, count * rows, HEAD), jnp.float32),
+            ],
+            compiler_params=compiler_params,
+            cost_estimate=cost(1, count * rows, tokens, 6),
+            name="turn",
+        )(*group, queries, upstream, qt, gt, *state)
+        final.append(stats)
+        contexts.append(context)
+        grads_q.append(grad_q)
+        back += send_back(len(groups), grads)
+
+    for part in (list(range(len(groups) - 1, 0, -1)), [0]):
         first = part != [0]
         counts = [len(groups[i]) for i in part]
-        back = [] if first else returned[0]
+        waits = [] if first else back
         operands = []
         for i in part:
             operands += kept[i]
-        operands += [queries, upstream, gt, final, grad_q]
+        operands += [queries, upstream, gt, *final, *grads_q]
         outs = pl.pallas_call(
             functools.partial(
-                backward_kernel, len(back), counts, not first, tile_of(max(counts) * rows, tokens)
+                backward_kernel,
+                len(waits),
+                counts,
+                heads,
+                not first,
+                not first,
+                tile_of(max(counts) * rows, tokens),
             ),
             out_shape=[wide_shape] + shapes_of(sum((groups[i] for i in part), [])),
-            in_specs=[ANY] * len(back) + [VMEM] * len(operands),
+            in_specs=[ANY] * len(waits) + [VMEM] * len(operands),
             out_specs=[VMEM] * (1 + sum(counts)),
             scratch_shapes=[sums(count) for count in counts for _ in range(2)],
             compiler_params=compiler_params,
             cost_estimate=cost(heads, sum(counts) * rows, tokens, 4),
             name="backward",
-        )(*back, *operands)
-        grad_q, blocks = outs[0], list(outs[1:])
+        )(*waits, *operands)
+        grads_q, blocks = [outs[0]], list(outs[1:])
         for i in part:
-            returned.append(send_back(i, blocks[: len(groups[i])]))
+            send_back(i, blocks[: len(groups[i])])
             blocks = blocks[len(groups[i]) :]
-    return turned_back(context, queries.dtype), turned_back(grad_q, queries.dtype)
+    return turned_back(contexts, queries.dtype), turned_back(grads_q, queries.dtype)
 
 
 def shards(pairs, queries, upstream):
@@ -464,31 +501,38 @@
     heads = queries.shape[2] // HEAD
     offsets = offset_groups()
     order = sum(offsets, [])
-    blocks = []
-    first = len(offsets[0])
+    first, final = len(offsets[0]), len(offsets[-1])
     packed = pack(pairs, order[:first], heads) + pack(pairs, order[first:], heads)
     packed = [block.reshape(heads, 2 * rows, HEAD) for block in packed]
-    final = len(offsets[-1])
-    packed[-final:] = reordered(packed[-final:], False)
-    for offset, block in zip(order, packed):
-        blocks.append(lax.ppermute(block, AXES, route(offset, False)))
+
+    def send(block, offset, back):
+        return lax.ppermute(block, AXES, route(offset, back))
+
+    blocks = [send(b, o, False) for b, o in zip(packed[:-final], order)]
     groups = []
-    for group in offsets:
+    for group in offsets[:-1]:
         groups.append(blocks[: len(group)])
         blocks = blocks[len(group) :]
-    homes, returned = [], []
+    apart = reordered([[b] for b in packed[-final:]], False, apart=True)
+    final_blocks = [
+        [send(b, o, False) for b, o in zip(apart[h::heads], offsets[-1])] for h in range(heads)
+    ]
+    homes, returned = [], [[] for _ in offsets]
 
     def send_back(i, grads):
         sent = sorted(zip(offsets[i], grads), key=lambda s: (s[0][0] > 0) == (i == 1))
-        back = [lax.ppermute(g, AXES, route(o, True)) for o, g in sent]
-        homes.extend(o for o, _ in sent)
-        returned.append(back)
+        back = [send(g, o, True) for o, g in sent]
+        returned[i].append(back)
+        if len(returned[i]) == 1:
+            homes.extend(o for o, _ in sent)
         return back
 
-    context, grad_query = attend(groups, queries, upstream, send_back)
-    early = reordered(sum(returned[:-1], []), True)
-    returned = [b.reshape(heads, rows, 2, HEAD) for b in list(early) + returned[-1]]
-    return context, grad_query, unpack(returned, homes, width)
+    context, grad_query = attend(groups, final_blocks, queries, upstream, send_back)
+    parts = [list(by_head) for by_head in zip(*returned[-1])]
+    parts += [[b] for i in range(len(groups) - 1, 0, -1) for b in returned[i][0]]
+    joined = reordered(parts, True)
+    joined = [b.reshape(heads, rows, 2, HEAD) for b in list(joined) + returned[0][0]]
+    return context, grad_query, unpack(joined, homes, width)
 
 
 def solution(mesh):

time: 64 us -> 65.6 us (1.025)
  starting transfers between devices: 29.9 us -> 32.4 us
  waiting for transfers between devices: 11.1 us -> 10.1 us
    ppermute x16 -> x18, starting transfers between devices: 29.9 us -> 32.4 us  [send(): return lax.ppermute(block, AXES, route(offset, back))]
    ppermute x16 -> x18, waiting for transfers between devices: 11.1 us -> 10.1 us  [send(): return lax.ppermute(block, AXES, route(offset, back))]
    pallas_call x5 -> x6, Pallas kernels: 9.06 us -> 9.22 us  [the longest x2 6.05 us: attend(): pl.pallas_call(functools.partial(backward_kernel, len(waits), counts, hea...]
  transfers between devices with their start and end apart: 16 -> 18, of which waited for: 6 -> 6; matrix products, arithmetic and copies ran while one was open for 0% -> 0% of each run, Pallas kernels for 26% -> 29%
where the time goes in v20:
time: 65.6 us; the launch traced here: 65.5 us
  starting transfers between devices  32.4 us (49%)
  Pallas kernels  20.7 us (32%)
  waiting for transfers between devices  10.1 us (15%)
  local copies, waits for them, and re-layouts  1.3 us (2%)
  between operations  0.98 us (1%)
    ppermute x18, starting transfers between devices, send(): return lax.ppermute(block, AXES, route(offset, back))  32.4 us
    ppermute x18, waiting for transfers between devices, send(): return lax.ppermute(block, AXES, route(offset, back))  10.1 us
    pallas_call x2, Pallas kernels, attend(): pl.pallas_call(functools.partial(backward_kernel, len(waits), counts, hea...  6.05 us
    pallas_call x3, Pallas kernels, attend(): pl.pallas_call(functools.partial(forward_kernel, count, not state, tile_o...  6.03 us
    pallas_call x2, Pallas kernels, attend(): pl.pallas_call(functools.partial(turn_kernel, count, h, tile_of(count * r...  2.47 us
    pallas_call x2, Pallas kernels, turned_back(): pl.pallas_call(kernel, out_shape=jax.ShapeDtypeStruct((1, tokens, heads *...  2.3 us
    pallas_call x1, Pallas kernels, unpack(): pl.pallas_call(kernel, out_shape=jax.ShapeDtypeStruct((1, rows, 2, width)...  1.51 us
  transfers between devices with their start and end apart: 18, of which 6 were waited for; matrix products, arithmetic and copies ran while one was open for 0% of the time, Pallas kernels for 29%

profile of v20, /device:TPU:0, one launch (start us, length us, event | category | flops | bytes accessed | tf_op | source)
XLA Modules:
  0.0 65.5 jit_solution(6314238611622992661)
XLA Ops:
  0.6 0.0 copy-start
  0.6 0.0 copy-start.2
  0.6 1.3 %copy-done.2 = bf16[1,128,2,2048]{3,2,1,0:T(2,128)(2,1)S(1)} copy-done((bf16[1,128,2,2048]{3,2,1,0:T(2,128)(2,1)S(1)}, bf16[1,128,2,2048]{3,2,1,0:T(2,128)(2,1)}, u32[]{:S(2)}) %copy-start.2) | copy-done | bytes 1048600
  1.9 0.4 pack.3
  2.4 0.0 copy-start.1
  2.4 3.5 %collective-permute-start.6 = (bf16[2,256,128]{2,1,0:T(8,128)(2,1)S(1)}, bf16[2,256,128]{2,1,0:T(8,128)(2,1)S(1)}, u32[]{:S(2)}, u32[]{:S(2)}) collective-permute-start(bf16[2,256,128]{2,1,0:T(8,128)(2,1)S(1)} %bitcast.31), channel_id=1, source_target_pairs={{0,11},{1,10},{2,13},{3,12},{4,15},{5,14},{6,9},{7,8},{8,19},{9,18... | collective-permute-start | bytes 393224 | tf_op jit(solution)/shard_map/ppermute | solution.py:509
  5.9 3.4 %collective-permute-start.5 = (bf16[2,256,128]{2,1,0:T(8,128)(2,1)S(1)}, bf16[2,256,128]{2,1,0:T(8,128)(2,1)S(1)}, u32[]{:S(2)}, u32[]{:S(2)}) collective-permute-start(bf16[2,256,128]{2,1,0:T(8,128)(2,1)S(1)} %bitcast.30), channel_id=1, source_target_pairs={{0,15},{1,14},{2,9},{3,8},{4,11},{5,10},{6,13},{7,12},{8,23},{9,22... | collective-permute-start | bytes 393224 | tf_op jit(solution)/shard_map/ppermute | solution.py:509
  9.3 1.0 %collective-permute-start.7 = (bf16[2,256,128]{2,1,0:T(8,128)(2,1)S(1)}, bf16[2,256,128]{2,1,0:T(8,128)(2,1)S(1)}, u32[]{:S(2)}, u32[]{:S(2)}) collective-permute-start(bf16[2,256,128]{2,1,0:T(8,128)(2,1)S(1)} %bitcast.29), channel_id=1, source_target_pairs={{0,9},{1,8},{2,11},{3,10},{4,13},{5,12},{6,15},{7,14},{8,17},{9,16... | collective-permute-start | bytes 393224 | tf_op jit(solution)/shard_map/ppermute | solution.py:509
  10.2 0.7 %pack.2 = (bf16[2,128,2,128]{3,2,1,0:T(2,128)(2,1)S(1)}, bf16[2,128,2,128]{3,2,1,0:T(2,128)(2,1)S(1)}, bf16[2,128,2,128]{3,2,1,0:T(2,128)(2,1)S(1)}, bf16[2,128,...) custom-call(bf16[1,128,2,2048]{3,2,1,0:T(2,128)(2,1)S(1)} %copy-done.2), custom_call_target="tpu_custom_call" | custom-call | tf_op jit(solution)/shard_map/pack/pallas_call | solution.py:79
  10.9 0.1 collective-permute-start.2
  11.0 3.5 %collective-permute-start.3 = (bf16[2,256,128]{2,1,0:T(8,128)(2,1)S(1)}, bf16[2,256,128]{2,1,0:T(8,128)(2,1)S(1)}, u32[]{:S(2)}, u32[]{:S(2)}) collective-permute-start(bf16[2,256,128]{2,1,0:T(8,128)(2,1)S(1)} %bitcast.27), channel_id=1, source_target_pairs={{0,14},{1,15},{2,8},{3,9},{4,10},{5,11},{6,12},{7,13},{8,22},{9,23... | collective-permute-start | bytes 393224 | tf_op jit(solution)/shard_map/ppermute | solution.py:509
  14.5 0.0 collective-permute-done.6.refs_1_
  14.5 1.6 %collective-permute-start.4 = (bf16[2,256,128]{2,1,0:T(8,128)(2,1)S(1)}, bf16[2,256,128]{2,1,0:T(8,128)(2,1)S(1)}, u32[]{:S(2)}, u32[]{:S(2)}) collective-permute-start(bf16[2,256,128]{2,1,0:T(8,128)(2,1)S(1)} %bitcast.26), channel_id=1, source_target_pairs={{0,8},{1,9},{2,10},{3,11},{4,12},{5,13},{6,14},{7,15},{8,16},{9,17... | collective-permute-start | bytes 393224 | tf_op jit(solution)/shard_map/ppermute | solution.py:509
  16.1 0.3 collective-permute-done.5.refs_0_
  16.4 0.6 collective-permute-start.1
  17.0 0.2 reordered.2
  17.2 0.0 copy-done
  17.2 0.3 turned.2.refs_3_.refs_1_
  17.5 0.0 copy-done.1
  17.5 0.3 turned.3.refs_4_.refs_10_.refs_8_
  17.8 0.0 collective-permute-done.7.refs_2_
  17.8 3.6 %collective-permute-start = (bf16[1,256,128]{2,1,0:T(8,128)(2,1)S(1)}, bf16[1,256,128]{2,1,0:T(8,128)(2,1)S(1)}, u32[]{:S(2)}, u32[]{:S(2)}) collective-permute-start(bf16[1,256,128]{2,1,0:T(8,128)(2,1)S(1)} %get-tuple-element.51), channel_id=1, source_target_pairs={{0,12},{1,13},{2,14},{3,15},{4,8},{5,9},{6,10},{7,11},{8,20},{9,21... | collective-permute-start | bytes 196616 | tf_op jit(solution)/shard_map/ppermute | solution.py:509
  21.4 2.5 %forward.3 = (f32[2,8,1536]{2,1,0:T(8,128)S(1)}, f32[2,128,1536]{2,1,0:T(8,128)S(1)}, bf16[2,384,1536]{2,1,0:T(8,128)(2,1)S(1)}, bf16[2,384,128]{2,1,0:T(8,128)(2,1)S(1)}, bf16[2,128,384]{2,1,0:T(8,128)(2,1)S(1)}) custom-call(bf16[2,256,128]{2,1,0:T(8,128)(2,1)S(1)} %collective-permute-done.5.refs_0_, ...), custom_call_target="tpu_custom_call" | custom-call | flops 603979776 | bytes 3932160 | tf_op jit(solution)/shard_map/forward/pallas_call | solution.py:426
  23.9 0.0 collective-permute-done.2.refs_0_
  23.9 0.4 collective-permute-start.8
  24.4 0.0 collective-permute-done.3.refs_1_
  24.4 0.0 collective-permute-done.4.refs_2_
  24.4 2.5 %forward.4 = (f32[2,8,1536]{2,1,0:T(8,128)S(1)}, f32[2,128,1536]{2,1,0:T(8,128)S(1)}, bf16[2,384,1536]{2,1,0:T(8,128)(2,1)S(1)}, bf16[2,384,128]{2,1,0:T(8,128)(2,1)S(1)}, bf16[2,128,384]{2,1,0:T(8,128)(2,1)S(1)}) custom-call(bf16[2,256,128]{2,1,0:T(8,128)(2,1)S(1)} %collective-permute-done.2.refs_0_, ...), custom_call_target="tpu_custom_call" | custom-call | flops 603979776 | bytes 3932160 | tf_op jit(solution)/shard_map/forward/pallas_call | solution.py:426
  26.9 3.6 %collective-permute-done.1.refs_0_ = bf16[2,256,128]{2,1,0:T(8,128)(2,1)S(1)} collective-permute-done((bf16[2,256,128]{2,1,0:T(8,128)(2,1)S(1)}, bf16[2,256,128]{2,1,0:T(8,128)(2,1)S(1)}, u32[]{:S(2)}, u32[]{:S(2)}) %collective-permute-start.1) | collective-permute-done | bytes 131104 | tf_op jit(solution)/shard_map/ppermute | solution.py:509
  30.4 1.0 %forward.5 = (f32[2,8,1536]{2,1,0:T(8,128)S(1)}, f32[2,128,1536]{2,1,0:T(8,128)S(1)}, bf16[2,128,1536]{2,1,0:T(8,128)(2,1)S(1)}, bf16[2,128,128]{2,1,0:T(8,128)(2,1)S(1)}, bf16[2,128,128]{2,1,0:T(8,128)(2,1)S(1)}) custom-call(bf16[2,256,128]{2,1,0:T(8,128)(2,1)S(1)} %collective-permute-done.1.refs_0_, bf16[2,128,1536]{2,1,0:T(8,128)(2,1)S(1)} %turned.2.refs_3_.refs_1_, ...), custom_call_target="tpu_custom_call" | custom-call | flops 201326592 | bytes 3407872 | tf_op jit(solution)/shard_map/forward/pallas_call | solution.py:426
  31.5 1.5 %collective-permute-done.8.refs_0_ = bf16[1,256,128]{2,1,0:T(8,128)(2,1)S(1)} collective-permute-done((bf16[1,256,128]{2,1,0:T(8,128)(2,1)S(1)}, bf16[1,256,128]{2,1,0:T(8,128)(2,1)S(1)}, u32[]{:S(2)}, u32[]{:S(2)}) %collective-permute-start.8) | collective-permute-done | bytes 65568 | tf_op jit(solution)/shard_map/ppermute | solution.py:509
  32.9 1.2 %turn.3 = (f32[1,8,1536]{2,1,0:T(8,128)S(1)}, f32[1,128,1536]{2,1,0:T(8,128)S(1)}, f32[1,128,1536]{2,1,0:T(8,128)S(1)}, bf16[1,256,128]{2,1,0:T(8,128)(2,1)S(1)}) custom-call(bf16[1,256,128]{2,1,0:T(8,128)(2,1)S(1)} %collective-permute-done.8.refs_0_, bf16[1,1536,256]{2,1,0:T(8,128)(2,1)S(1)} %copy-done, bf16[1,1536,256]{2,1,0:T(8,128)(2,1)S(1)} %copy-done.1, ...), custom_call_target="tpu_custom_call" | custom-call | flops 301989888 | bytes 1703936 | tf_op jit(solution)/shard_map/turn/pallas_call | solution.py:444
  34.2 0.1 collective-permute-start.10
  34.3 0.0 collective-permute-done.refs_0_
  34.3 1.2 %turn.2 = (f32[1,8,1536]{2,1,0:T(8,128)S(1)}, f32[1,128,1536]{2,1,0:T(8,128)S(1)}, f32[1,128,1536]{2,1,0:T(8,128)S(1)}, bf16[1,256,128]{2,1,0:T(8,128)(2,1)S(1)}) custom-call(bf16[1,256,128]{2,1,0:T(8,128)(2,1)S(1)} %collective-permute-done.refs_0_, bf16[1,1536,256]{2,1,0:T(8,128)(2,1)S(1)} %copy-done, bf16[1,1536,256]{2,1,0:T(8,128)(2,1)S(1)} %copy-done.1, ...), custom_call_target="tpu_custom_call" | custom-call | flops 301989888 | bytes 1703936 | tf_op jit(solution)/shard_map/turn/pallas_call | solution.py:444
  35.5 2.9 %collective-permute-start.9 = (bf16[1,256,128]{2,1,0:T(8,128)(2,1)S(1)}, bf16[1,256,128]{2,1,0:T(8,128)(2,1)S(1)}, u32[]{:S(2)}, u32[]{:S(2)}) collective-permute-start(bf16[1,256,128]{2,1,0:T(8,128)(2,1)S(1)} %get-tuple-element.68), channel_id=1, source_target_pairs={{12,0},{13,1},{14,2},{15,3},{8,4},{9,5},{10,6},{11,7},{20,8},{21,9... | collective-permute-start | bytes 196616 | tf_op jit(solution)/shard_map/ppermute | solution.py:509
  38.4 3.4 %backward.2 = (f32[2,128,1536]{2,1,0:T(8,128)S(1)}, bf16[2,256,128]{2,1,0:T(8,128)(2,1)S(1)}, bf16[2,256,128]{2,1,0:T(8,128)(2,1)S(1)}, bf16[2,256,128]{2,1,0:T(8,128)(2,1)S(1)}, bf16[2,256,128]{2,1,0:T(8,128)(2,1)S(1)}) custom-call(bf16[2,128,1536]{2,1,0:T(8,128)(2,1)S(1)} %get-tuple-element.75.refs_0_, ...), custom_call_target="tpu_custom_call" | custom-call | flops 1610612736 | bytes 4194304 | tf_op jit(solution)/shard_map/backward/pallas_call | solution.py:474
  41.8 0.5 collective-permute-start.11
  42.2 0.0 collective-permute-start.12
  42.2 2.3 %collective-permute-start.13 = (bf16[2,256,128]{2,1,0:T(8,128)(2,1)S(1)}, bf16[2,256,128]{2,1,0:T(8,128)(2,1)S(1)}, u32[]{:S(2)}, u32[]{:S(2)}) collective-permute-start(bf16[2,256,128]{2,1,0:T(8,128)(2,1)S(1)} %get-tuple-element.87), channel_id=1, source_target_pairs={{10,0},{11,1},{12,2},{13,3},{14,4},{15,5},{8,6},{9,7},{18,8},{19,9... | collective-permute-start | bytes 393224 | tf_op jit(solution)/shard_map/ppermute | solution.py:509
  44.6 0.0 collective-permute-done.10.refs_1_
  44.6 0.3 collective-permute-start.14
  44.9 0.0 collective-permute-done.9.refs_0_
  44.9 2.7 %backward.3 = (f32[2,128,1536]{2,1,0:T(8,128)S(1)}, bf16[2,256,128]{2,1,0:T(8,128)(2,1)S(1)}, bf16[2,256,128]{2,1,0:T(8,128)(2,1)S(1)}, bf16[2,256,128]{2,1,0:T(8,128)(2,1)S(1)}) custom-call(bf16[1,256,128]{2,1,0:T(8,128)(2,1)S(1)} %collective-permute-done.9.refs_0_, bf16[1,256,128]{2,1,0:T(8,128)(2,1)S(1)} %collective-permute-done.10.refs_1_, ...), custom_call_target="tpu_custom_call" | custom-call | flops 1207959552 | bytes 3932160 | tf_op jit(solution)/shard_map/backward/pallas_call | solution.py:474
  47.5 2.7 %collective-permute-start.15 = (bf16[2,256,128]{2,1,0:T(8,128)(2,1)S(1)}, bf16[2,256,128]{2,1,0:T(8,128)(2,1)S(1)}, u32[]{:S(2)}, u32[]{:S(2)}) collective-permute-start(bf16[2,256,128]{2,1,0:T(8,128)(2,1)S(1)} %get-tuple-element.94), channel_id=1, source_target_pairs={{15,0},{14,1},{9,2},{8,3},{11,4},{10,5},{13,6},{12,7},{23,8},{22,9... | collective-permute-start | bytes 393224 | tf_op jit(solution)/shard_map/ppermute | solution.py:509
  50.2 1.0 %collective-permute-done.11.refs_2_ = bf16[2,256,128]{2,1,0:T(8,128)(2,1)S(1)} collective-permute-done((bf16[2,256,128]{2,1,0:T(8,128)(2,1)S(1)}, bf16[2,256,128]{2,1,0:T(8,128)(2,1)S(1)}, u32[]{:S(2)}, u32[]{:S(2)}) %collective-permute-start.11) | collective-permute-done | bytes 131104 | tf_op jit(solution)/shard_map/ppermute | solution.py:509
  51.2 5.2 %collective-permute-start.16 = (bf16[2,256,128]{2,1,0:T(8,128)(2,1)S(1)}, bf16[2,256,128]{2,1,0:T(8,128)(2,1)S(1)}, u32[]{:S(2)}, u32[]{:S(2)}) collective-permute-start(bf16[2,256,128]{2,1,0:T(8,128)(2,1)S(1)} %get-tuple-element.95), channel_id=1, source_target_pairs={{11,0},{10,1},{13,2},{12,3},{15,4},{14,5},{9,6},{8,7},{19,8},{18,9... | collective-permute-start | bytes 393224 | tf_op jit(solution)/shard_map/ppermute | solution.py:509
  56.4 0.0 collective-permute-done.12.refs_3_
  56.4 0.9 %collective-permute-start.17 = (bf16[2,256,128]{2,1,0:T(8,128)(2,1)S(1)}, bf16[2,256,128]{2,1,0:T(8,128)(2,1)S(1)}, u32[]{:S(2)}, u32[]{:S(2)}) collective-permute-start(bf16[2,256,128]{2,1,0:T(8,128)(2,1)S(1)} %get-tuple-element.96), channel_id=1, source_target_pairs={{9,0},{8,1},{11,2},{10,3},{13,4},{12,5},{15,6},{14,7},{17,8},{16,9... | collective-permute-start | bytes 393224 | tf_op jit(solution)/shard_map/ppermute | solution.py:509
  57.3 1.2 %turned_back.2 = bf16[1,1536,256]{2,1,0:T(8,128)(2,1)} custom-call(f32[1,128,1536]{2,1,0:T(8,128)S(1)} %get-tuple-element.65.refs_0_, f32[1,128,1536]{2,1,0:T(8,128)S(1)} %get-tuple-element.67.refs_1_), custom_call_target="tpu_custom_call" | custom-call | tf_op jit(solution)/shard_map/turned_back/pallas_call | solution.py:186
  58.4 1.2 %turned_back.3 = bf16[1,1536,256]{2,1,0:T(8,128)(2,1)} custom-call(f32[2,128,1536]{2,1,0:T(8,128)S(1)} %get-tuple-element.84.refs_0_), custom_call_target="tpu_custom_call" | custom-call | tf_op jit(solution)/shard_map/turned_back/pallas_call | solution.py:186
  59.6 0.0 collective-permute-done.13.refs_4_
  59.6 0.0 collective-permute-done.14.refs_5_
  59.6 0.5 reordered.3
  60.1 0.0 collective-permute-done.15
  60.1 0.6 collective-permute-done.16
  60.7 3.1 %collective-permute-done.17 = bf16[2,256,128]{2,1,0:T(8,128)(2,1)S(1)} collective-permute-done((bf16[2,256,128]{2,1,0:T(8,128)(2,1)S(1)}, bf16[2,256,128]{2,1,0:T(8,128)(2,1)S(1)}, u32[]{:S(2)}, u32[]{:S(2)}) %collective-permute-start.17) | collective-permute-done | bytes 131104 | tf_op jit(solution)/shard_map/ppermute | solution.py:509
  63.8 1.5 %unpack.1 = bf16[1,128,2,2048]{3,2,1,0:T(2,128)(2,1)} custom-call(bf16[2,128,2,128]{3,2,1,0:T(2,128)(2,1)S(1)} %bitcast.19, bf16[2,128,2,128]{3,2,1,0:T(2,128)(2,1)S(1)} %bitcast.20, bf16[2,128,2,128]{3,2,1,0:T(2,128)(2,1)S(1)} %bitcast.21, bf16[2,128,2,128]{3,2,1,0:T(2,128)(2,1)S(1)} %bitcast.22, bf16[2,128,2,128]{3,2,1,0:T(2,128)(2,1)S(1)} %bitcast.23, ...), custom_call_target="tpu_custom_call" | custom-call | tf_op jit(solution)/shard_map/unpack/pallas_call | solution.py:115
Async XLA Ops:
  0.6 16.6 %copy-start = (bf16[1,1536,256]{2,1,0:T(8,128)(2,1)S(1)}, bf16[1,1536,256]{2,1,0:T(8,128)(2,1)}, u32[]{:S(2)}) copy-start(bf16[1,1536,256]{2,1,0:T(8,128)(2,1)} %refs_6_.1) | copy-start | bytes 2359300
  0.6 1.3 %copy-start.2 = (bf16[1,128,2,2048]{3,2,1,0:T(2,128)(2,1)S(1)}, bf16[1,128,2,2048]{3,2,1,0:T(2,128)(2,1)}, u32[]{:S(2)}) copy-start(bf16[1,128,2,2048]{3,2,1,0:T(2,128)(2,1)} %pairs_ref.3) | copy-start | bytes 3145732
  2.4 15.1 %copy-start.1 = (bf16[1,1536,256]{2,1,0:T(8,128)(2,1)S(1)}, bf16[1,1536,256]{2,1,0:T(8,128)(2,1)}, u32[]{:S(2)}) copy-start(bf16[1,1536,256]{2,1,0:T(8,128)(2,1)} %refs_7_.1) | copy-start | bytes 2359300
  2.4 12.1 %collective-permute-start.6 = (bf16[2,256,128]{2,1,0:T(8,128)(2,1)S(1)}, bf16[2,256,128]{2,1,0:T(8,128)(2,1)S(1)}, u32[]{:S(2)}, u32[]{:S(2)}) collective-permute-start(bf16[2,256,128]{2,1,0:T(8,128)(2,1)S(1)} %bitcast.31), channel_id=1, source_target_pairs={{0,11},{1,10},{2,13},{3,12},{4,15},{5,14},{6,9},{7,8},{8,19},{9,18... | collective-permute-start | bytes 393224 | tf_op jit(solution)/shard_map/ppermute | solution.py:509
  5.9 10.5 %collective-permute-start.5 = (bf16[2,256,128]{2,1,0:T(8,128)(2,1)S(1)}, bf16[2,256,128]{2,1,0:T(8,128)(2,1)S(1)}, u32[]{:S(2)}, u32[]{:S(2)}) collective-permute-start(bf16[2,256,128]{2,1,0:T(8,128)(2,1)S(1)} %bitcast.30), channel_id=1, source_target_pairs={{0,15},{1,14},{2,9},{3,8},{4,11},{5,10},{6,13},{7,12},{8,23},{9,22... | collective-permute-start | bytes 393224 | tf_op jit(solution)/shard_map/ppermute | solution.py:509
  9.3 8.5 %collective-permute-start.7 = (bf16[2,256,128]{2,1,0:T(8,128)(2,1)S(1)}, bf16[2,256,128]{2,1,0:T(8,128)(2,1)S(1)}, u32[]{:S(2)}, u32[]{:S(2)}) collective-permute-start(bf16[2,256,128]{2,1,0:T(8,128)(2,1)S(1)} %bitcast.29), channel_id=1, source_target_pairs={{0,9},{1,8},{2,11},{3,10},{4,13},{5,12},{6,15},{7,14},{8,17},{9,16... | collective-permute-start | bytes 393224 | tf_op jit(solution)/shard_map/ppermute | solution.py:509
  10.9 13.0 %collective-permute-start.2 = (bf16[2,256,128]{2,1,0:T(8,128)(2,1)S(1)}, bf16[2,256,128]{2,1,0:T(8,128)(2,1)S(1)}, u32[]{:S(2)}, u32[]{:S(2)}) collective-permute-start(bf16[2,256,128]{2,1,0:T(8,128)(2,1)S(1)} %bitcast.28), channel_id=1, source_target_pairs={{0,10},{1,11},{2,12},{3,13},{4,14},{5,15},{6,8},{7,9},{8,18},{9,19... | collective-permute-start | bytes 393224 | tf_op jit(solution)/shard_map/ppermute | solution.py:509
  11.0 13.4 %collective-permute-start.3 = (bf16[2,256,128]{2,1,0:T(8,128)(2,1)S(1)}, bf16[2,256,128]{2,1,0:T(8,128)(2,1)S(1)}, u32[]{:S(2)}, u32[]{:S(2)}) collective-permute-start(bf16[2,256,128]{2,1,0:T(8,128)(2,1)S(1)} %bitcast.27), channel_id=1, source_target_pairs={{0,14},{1,15},{2,8},{3,9},{4,10},{5,11},{6,12},{7,13},{8,22},{9,23... | collective-permute-start | bytes 393224 | tf_op jit(solution)/shard_map/ppermute | solution.py:509
  14.5 9.9 %collective-permute-start.4 = (bf16[2,256,128]{2,1,0:T(8,128)(2,1)S(1)}, bf16[2,256,128]{2,1,0:T(8,128)(2,1)S(1)}, u32[]{:S(2)}, u32[]{:S(2)}) collective-permute-start(bf16[2,256,128]{2,1,0:T(8,128)(2,1)S(1)} %bitcast.26), channel_id=1, source_target_pairs={{0,8},{1,9},{2,10},{3,11},{4,12},{5,13},{6,14},{7,15},{8,16},{9,17... | collective-permute-start | bytes 393224 | tf_op jit(solution)/shard_map/ppermute | solution.py:509
  16.4 14.0 %collective-permute-start.1 = (bf16[2,256,128]{2,1,0:T(8,128)(2,1)S(1)}, bf16[2,256,128]{2,1,0:T(8,128)(2,1)S(1)}, u32[]{:S(2)}, u32[]{:S(2)}) collective-permute-start(bf16[2,256,128]{2,1,0:T(8,128)(2,1)S(1)} %bitcast.25), channel_id=1, source_target_pairs={{0,13},{1,12},{2,15},{3,14},{4,9},{5,8},{6,11},{7,10},{8,21},{9,20... | collective-permute-start | bytes 393224 | tf_op jit(solution)/shard_map/ppermute | solution.py:509
  17.8 16.5 %collective-permute-start = (bf16[1,256,128]{2,1,0:T(8,128)(2,1)S(1)}, bf16[1,256,128]{2,1,0:T(8,128)(2,1)S(1)}, u32[]{:S(2)}, u32[]{:S(2)}) collective-permute-start(bf16[1,256,128]{2,1,0:T(8,128)(2,1)S(1)} %get-tuple-element.51), channel_id=1, source_target_pairs={{0,12},{1,13},{2,14},{3,15},{4,8},{5,9},{6,10},{7,11},{8,20},{9,21... | collective-permute-start | bytes 196616 | tf_op jit(solution)/shard_map/ppermute | solution.py:509
  23.9 9.0 %collective-permute-start.8 = (bf16[1,256,128]{2,1,0:T(8,128)(2,1)S(1)}, bf16[1,256,128]{2,1,0:T(8,128)(2,1)S(1)}, u32[]{:S(2)}, u32[]{:S(2)}) collective-permute-start(bf16[1,256,128]{2,1,0:T(8,128)(2,1)S(1)} %get-tuple-element.66), channel_id=1, source_target_pairs={{0,12},{1,13},{2,14},{3,15},{4,8},{5,9},{6,10},{7,11},{8,20},{9,21... | collective-permute-start | bytes 196616 | tf_op jit(solution)/shard_map/ppermute | solution.py:509
  34.2 10.4 %collective-permute-start.10 = (bf16[1,256,128]{2,1,0:T(8,128)(2,1)S(1)}, bf16[1,256,128]{2,1,0:T(8,128)(2,1)S(1)}, u32[]{:S(2)}, u32[]{:S(2)}) collective-permute-start(bf16[1,256,128]{2,1,0:T(8,128)(2,1)S(1)} %get-tuple-element.69), channel_id=1, source_target_pairs={{12,0},{13,1},{14,2},{15,3},{8,4},{9,5},{10,6},{11,7},{20,8},{21,9... | collective-permute-start | bytes 196616 | tf_op jit(solution)/shard_map/ppermute | solution.py:509
  35.5 9.3 %collective-permute-start.9 = (bf16[1,256,128]{2,1,0:T(8,128)(2,1)S(1)}, bf16[1,256,128]{2,1,0:T(8,128)(2,1)S(1)}, u32[]{:S(2)}, u32[]{:S(2)}) collective-permute-start(bf16[1,256,128]{2,1,0:T(8,128)(2,1)S(1)} %get-tuple-element.68), channel_id=1, source_target_pairs={{12,0},{13,1},{14,2},{15,3},{8,4},{9,5},{10,6},{11,7},{20,8},{21,9... | collective-permute-start | bytes 196616 | tf_op jit(solution)/shard_map/ppermute | solution.py:509
  41.8 9.4 %collective-permute-start.11 = (bf16[2,256,128]{2,1,0:T(8,128)(2,1)S(1)}, bf16[2,256,128]{2,1,0:T(8,128)(2,1)S(1)}, u32[]{:S(2)}, u32[]{:S(2)}) collective-permute-start(bf16[2,256,128]{2,1,0:T(8,128)(2,1)S(1)} %get-tuple-element.85), channel_id=1, source_target_pairs={{13,0},{12,1},{15,2},{14,3},{9,4},{8,5},{11,6},{10,7},{21,8},{20,9... | collective-permute-start | bytes 393224 | tf_op jit(solution)/shard_map/ppermute | solution.py:509
  42.2 14.2 %collective-permute-start.12 = (bf16[2,256,128]{2,1,0:T(8,128)(2,1)S(1)}, bf16[2,256,128]{2,1,0:T(8,128)(2,1)S(1)}, u32[]{:S(2)}, u32[]{:S(2)}) collective-permute-start(bf16[2,256,128]{2,1,0:T(8,128)(2,1)S(1)} %get-tuple-element.86), channel_id=1, source_target_pairs={{8,0},{9,1},{10,2},{11,3},{12,4},{13,5},{14,6},{15,7},{16,8},{17,9... | collective-permute-start | bytes 393224 | tf_op jit(solution)/shard_map/ppermute | solution.py:509
  42.2 17.3 %collective-permute-start.13 = (bf16[2,256,128]{2,1,0:T(8,128)(2,1)S(1)}, bf16[2,256,128]{2,1,0:T(8,128)(2,1)S(1)}, u32[]{:S(2)}, u32[]{:S(2)}) collective-permute-start(bf16[2,256,128]{2,1,0:T(8,128)(2,1)S(1)} %get-tuple-element.87), channel_id=1, source_target_pairs={{10,0},{11,1},{12,2},{13,3},{14,4},{15,5},{8,6},{9,7},{18,8},{19,9... | collective-permute-start | bytes 393224 | tf_op jit(solution)/shard_map/ppermute | solution.py:509
  44.6 15.0 %collective-permute-start.14 = (bf16[2,256,128]{2,1,0:T(8,128)(2,1)S(1)}, bf16[2,256,128]{2,1,0:T(8,128)(2,1)S(1)}, u32[]{:S(2)}, u32[]{:S(2)}) collective-permute-start(bf16[2,256,128]{2,1,0:T(8,128)(2,1)S(1)} %get-tuple-element.88), channel_id=1, source_target_pairs={{14,0},{15,1},{8,2},{9,3},{10,4},{11,5},{12,6},{13,7},{22,8},{23,9... | collective-permute-start | bytes 393224 | tf_op jit(solution)/shard_map/ppermute | solution.py:509
  47.5 12.5 %collective-permute-start.15 = (bf16[2,256,128]{2,1,0:T(8,128)(2,1)S(1)}, bf16[2,256,128]{2,1,0:T(8,128)(2,1)S(1)}, u32[]{:S(2)}, u32[]{:S(2)}) collective-permute-start(bf16[2,256,128]{2,1,0:T(8,128)(2,1)S(1)} %get-tuple-element.94), channel_id=1, source_target_pairs={{15,0},{14,1},{9,2},{8,3},{11,4},{10,5},{13,6},{12,7},{23,8},{22,9... | collective-permute-start | bytes 393224 | tf_op jit(solution)/shard_map/ppermute | solution.py:509
  51.2 9.5 %collective-permute-start.16 = (bf16[2,256,128]{2,1,0:T(8,128)(2,1)S(1)}, bf16[2,256,128]{2,1,0:T(8,128)(2,1)S(1)}, u32[]{:S(2)}, u32[]{:S(2)}) collective-permute-start(bf16[2,256,128]{2,1,0:T(8,128)(2,1)S(1)} %get-tuple-element.95), channel_id=1, source_target_pairs={{11,0},{10,1},{13,2},{12,3},{15,4},{14,5},{9,6},{8,7},{19,8},{18,9... | collective-permute-start | bytes 393224 | tf_op jit(solution)/shard_map/ppermute | solution.py:509
  56.4 7.4 %collective-permute-start.17 = (bf16[2,256,128]{2,1,0:T(8,128)(2,1)S(1)}, bf16[2,256,128]{2,1,0:T(8,128)(2,1)S(1)}, u32[]{:S(2)}, u32[]{:S(2)}) collective-permute-start(bf16[2,256,128]{2,1,0:T(8,128)(2,1)S(1)} %get-tuple-element.96), channel_id=1, source_target_pairs={{9,0},{8,1},{11,2},{10,3},{13,4},{12,5},{15,6},{14,7},{17,8},{16,9... | collective-permute-start | bytes 393224 | tf_op jit(solution)/shard_map/ppermute | solution.py:509

commit v21 on v19

--- a/solution.py
+++ b/solution.py
@@ -25,20 +25,21 @@
     far.sort(key=lambda o: -abs(o[0] - seq_count / 2))
     eighth = max(1, (len(near) + len(far)) // 8)
     short, long = far[: -2 * eighth], far[-2 * eighth :]
-    short.sort(key=lambda o: -o[1])
+    short = [((d, d), dy) for d, dy in sorted(short, key=lambda o: -o[1]) if d != 1]
+    long = [((d, d), dy) for d, dy in long]
     half = len(short) // 2
-    return [
-        short[1:half] + short[:1] + near[:1],
-        short[half:] + near[1:],
-        long[:eighth],
-        long[eighth:],
-    ]
+    mixed = []
+    for part, (_, dy) in zip((short[:half], short[half:]), near):
+        mixed.append(part[:1] + [((1, 0), dy)] + part[1:] + [((0, 1), dy)])
+    return [mixed[0], mixed[1], long[:eighth], long[eighth:]]
 
 
 def group_at(offset):
     seq_count = lax.axis_size("seq")
     tp_count = lax.axis_size("tp")
-    z = lax.rem(lax.axis_index("seq") + offset[0], seq_count)
+    even, odd = offset[0]
+    dz = even + (odd - even) * lax.rem(lax.axis_index("segment"), 2)
+    z = lax.rem(lax.axis_index("seq") + dz, seq_count)
     y = lax.rem(lax.axis_index("tp") + offset[1], tp_count)
     return z * tp_count + y
 
@@ -51,7 +52,7 @@
             for y in range(tp_count):
                 source = (s * seq_count + z) * tp_count + y
                 s_to = (s + 1) % segments
-                z_to = (z + offset[0]) % seq_count
+                z_to = (z + offset[0][s % 2]) % seq_count
                 y_to = (y + offset[1]) % tp_count
                 target = (s_to * seq_count + z_to) * tp_count + y_to
                 hops.append((target, source) if back else (source, target))
@@ -479,9 +480,8 @@
     homes, returned = [], []
 
     def send_back(i, grads):
-        sent = sorted(zip(offsets[i], grads), key=lambda s: (s[0][0] > 0) == (i == 1))
-        back = [lax.ppermute(g, AXES, route(o, True)) for o, g in sent]
-        homes.extend(o for o, _ in sent)
+        back = [lax.ppermute(g, AXES, route(o, True)) for o, g in zip(offsets[i], grads)]
+        homes.extend(offsets[i])
         returned.append(back)
         return back
 

time: 64 us -> 66.2 us (1.034)
  waiting for transfers between devices: 11.1 us -> 18.2 us
  starting transfers between devices: 29.9 us -> 25 us
    ppermute x8, waiting for transfers between devices: 5.33 us -> 9.8 us  [send_back(): lax.ppermute(g, AXES, route(o, True))]
    ppermute x8, starting transfers between devices: 12.7 us -> 9.66 us  [send_back(): lax.ppermute(g, AXES, route(o, True))]
    ppermute x8, waiting for transfers between devices: 5.81 us -> 8.41 us  [shards(): blocks.append(lax.ppermute(block, AXES, route(offset, False)))]
    ppermute x8, starting transfers between devices: 17.2 us -> 15.3 us  [shards(): blocks.append(lax.ppermute(block, AXES, route(offset, False)))]
  transfers between devices with their start and end apart: 16 -> 16, of which waited for: 6 -> 8; matrix products, arithmetic and copies ran while one was open for 0% -> 0% of each run, Pallas kernels for 26% -> 25%
where the time goes in v21:
time: 66.2 us; the launch traced here: 66 us
  starting transfers between devices  25 us (38%)
  Pallas kernels  20.6 us (31%)
  waiting for transfers between devices  18.2 us (27%)
  local copies, waits for them, and re-layouts  1.3 us (2%)
  between operations  0.96 us (1%)
    ppermute x8, starting transfers between devices, shards(): blocks.append(lax.ppermute(block, AXES, route(offset, False)))  15.3 us
    ppermute x8, waiting for transfers between devices, send_back(): lax.ppermute(g, AXES, route(o, True))  9.8 us
    ppermute x8, starting transfers between devices, send_back(): lax.ppermute(g, AXES, route(o, True))  9.66 us
    ppermute x8, waiting for transfers between devices, shards(): blocks.append(lax.ppermute(block, AXES, route(offset, False)))  8.41 us
    pallas_call x2, Pallas kernels, attend(): pl.pallas_call(functools.partial(backward_kernel, len(back), counts, not...  6.06 us
    pallas_call x3, Pallas kernels, attend(): pl.pallas_call(functools.partial(forward_kernel, count, not state, tile_o...  6.04 us
    pallas_call x2, Pallas kernels, turned_back(): pl.pallas_call(kernel, out_shape=jax.ShapeDtypeStruct((1, tokens, heads *...  2.3 us
    pallas_call x1, Pallas kernels, attend(): pl.pallas_call(functools.partial(turn_kernel, count, tile_of(count * rows...  2.28 us
  transfers between devices with their start and end apart: 16, of which 8 were waited for; matrix products, arithmetic and copies ran while one was open for 0% of the time, Pallas kernels for 25%

profile of v21, /device:TPU:0, one launch (start us, length us, event | category | flops | bytes accessed | tf_op | source)
XLA Modules:
  0.0 66.0 jit_solution(95060993097780484)
XLA Ops:
  0.6 0.0 copy-start
  0.6 0.0 copy-start.2
  0.6 1.3 %copy-done.2 = bf16[1,128,2,2048]{3,2,1,0:T(2,128)(2,1)S(1)} copy-done((bf16[1,128,2,2048]{3,2,1,0:T(2,128)(2,1)S(1)}, bf16[1,128,2,2048]{3,2,1,0:T(2,128)(2,1)}, u32[]{:S(2)}) %copy-start.2) | copy-done | bytes 1048600
  1.9 0.5 pack.3
  2.4 0.0 copy-start.1
  2.4 3.5 %collective-permute-start.6 = (bf16[2,256,128]{2,1,0:T(8,128)(2,1)S(1)}, bf16[2,256,128]{2,1,0:T(8,128)(2,1)S(1)}, u32[]{:S(2)}, u32[]{:S(2)}) collective-permute-start(bf16[2,256,128]{2,1,0:T(8,128)(2,1)S(1)} %bitcast.31), channel_id=1, source_target_pairs={{0,11},{1,10},{2,13},{3,12},{4,15},{5,14},{6,9},{7,8},{8,17},{9,16... | collective-permute-start | bytes 393224 | tf_op jit(solution)/shard_map/ppermute | solution.py:475
  5.9 3.7 %collective-permute-start.5 = (bf16[2,256,128]{2,1,0:T(8,128)(2,1)S(1)}, bf16[2,256,128]{2,1,0:T(8,128)(2,1)S(1)}, u32[]{:S(2)}, u32[]{:S(2)}) collective-permute-start(bf16[2,256,128]{2,1,0:T(8,128)(2,1)S(1)} %bitcast.30), channel_id=1, source_target_pairs={{0,15},{1,14},{2,9},{3,8},{4,11},{5,10},{6,13},{7,12},{8,23},{9,22... | collective-permute-start | bytes 393224 | tf_op jit(solution)/shard_map/ppermute | solution.py:475
  9.7 0.6 collective-permute-start.7
  10.3 0.7 %pack.2 = (bf16[2,128,2,128]{3,2,1,0:T(2,128)(2,1)S(1)}, bf16[2,128,2,128]{3,2,1,0:T(2,128)(2,1)S(1)}, bf16[2,128,2,128]{3,2,1,0:T(2,128)(2,1)S(1)}, bf16[2,128,...) custom-call(bf16[1,128,2,2048]{3,2,1,0:T(2,128)(2,1)S(1)} %copy-done.2), custom_call_target="tpu_custom_call" | custom-call | tf_op jit(solution)/shard_map/pack/pallas_call | solution.py:80
  11.0 3.9 %collective-permute-start.2 = (bf16[2,256,128]{2,1,0:T(8,128)(2,1)S(1)}, bf16[2,256,128]{2,1,0:T(8,128)(2,1)S(1)}, u32[]{:S(2)}, u32[]{:S(2)}) collective-permute-start(bf16[2,256,128]{2,1,0:T(8,128)(2,1)S(1)} %bitcast.28), channel_id=1, source_target_pairs={{0,14},{1,15},{2,8},{3,9},{4,10},{5,11},{6,12},{7,13},{8,22},{9,23... | collective-permute-start | bytes 393224 | tf_op jit(solution)/shard_map/ppermute | solution.py:475
  14.9 0.0 collective-permute-start.3
  14.9 0.0 collective-permute-done.6.refs_1_
  14.9 1.6 %collective-permute-start.4 = (bf16[2,256,128]{2,1,0:T(8,128)(2,1)S(1)}, bf16[2,256,128]{2,1,0:T(8,128)(2,1)S(1)}, u32[]{:S(2)}, u32[]{:S(2)}) collective-permute-start(bf16[2,256,128]{2,1,0:T(8,128)(2,1)S(1)} %bitcast.26), channel_id=1, source_target_pairs={{0,8},{1,9},{2,10},{3,11},{4,12},{5,13},{6,14},{7,15},{8,18},{9,19... | collective-permute-start | bytes 393224 | tf_op jit(solution)/shard_map/ppermute | solution.py:475
  16.5 0.0 collective-permute-done.5.refs_0_
  16.5 1.0 %collective-permute-start.1 = (bf16[2,256,128]{2,1,0:T(8,128)(2,1)S(1)}, bf16[2,256,128]{2,1,0:T(8,128)(2,1)S(1)}, u32[]{:S(2)}, u32[]{:S(2)}) collective-permute-start(bf16[2,256,128]{2,1,0:T(8,128)(2,1)S(1)} %bitcast.25), channel_id=1, source_target_pairs={{0,13},{1,12},{2,15},{3,14},{4,9},{5,8},{6,11},{7,10},{8,21},{9,20... | collective-permute-start | bytes 393224 | tf_op jit(solution)/shard_map/ppermute | solution.py:475
  17.5 0.2 reordered.2
  17.7 0.0 copy-done
  17.7 0.3 turned.2.refs_3_.refs_1_
  18.0 0.0 copy-done.1
  18.0 0.3 turned.3.refs_4_.refs_10_.refs_7_
  18.3 0.6 collective-permute-done.7.refs_2_
  18.9 1.0 %collective-permute-start = (bf16[2,256,128]{2,1,0:T(8,128)(2,1)S(1)}, bf16[2,256,128]{2,1,0:T(8,128)(2,1)S(1)}, u32[]{:S(2)}, u32[]{:S(2)}) collective-permute-start(bf16[2,256,128]{2,1,0:T(8,128)(2,1)S(1)} %reordered.2), channel_id=1, source_target_pairs={{0,12},{1,13},{2,14},{3,15},{4,8},{5,9},{6,10},{7,11},{8,20},{9,21... | collective-permute-start | bytes 393224 | tf_op jit(solution)/shard_map/ppermute | solution.py:475
  19.9 2.5 %forward.3 = (f32[2,8,1536]{2,1,0:T(8,128)S(1)}, f32[2,128,1536]{2,1,0:T(8,128)S(1)}, bf16[2,384,1536]{2,1,0:T(8,128)(2,1)S(1)}, bf16[2,384,128]{2,1,0:T(8,128)(2,1)S(1)}, bf16[2,128,384]{2,1,0:T(8,128)(2,1)S(1)}) custom-call(bf16[2,256,128]{2,1,0:T(8,128)(2,1)S(1)} %collective-permute-done.5.refs_0_, ...), custom_call_target="tpu_custom_call" | custom-call | flops 603979776 | bytes 3932160 | tf_op jit(solution)/shard_map/forward/pallas_call | solution.py:409
  22.4 0.0 collective-permute-done.2.refs_0_
  22.4 0.0 collective-permute-done.3.refs_1_
  22.4 1.9 %collective-permute-done.4.refs_2_ = bf16[2,256,128]{2,1,0:T(8,128)(2,1)S(1)} collective-permute-done((bf16[2,256,128]{2,1,0:T(8,128)(2,1)S(1)}, bf16[2,256,128]{2,1,0:T(8,128)(2,1)S(1)}, u32[]{:S(2)}, u32[]{:S(2)}) %collective-permute-start.4) | collective-permute-done | bytes 131104 | tf_op jit(solution)/shard_map/ppermute | solution.py:475
  24.3 2.5 %forward.4 = (f32[2,8,1536]{2,1,0:T(8,128)S(1)}, f32[2,128,1536]{2,1,0:T(8,128)S(1)}, bf16[2,384,1536]{2,1,0:T(8,128)(2,1)S(1)}, bf16[2,384,128]{2,1,0:T(8,128)(2,1)S(1)}, bf16[2,128,384]{2,1,0:T(8,128)(2,1)S(1)}) custom-call(bf16[2,256,128]{2,1,0:T(8,128)(2,1)S(1)} %collective-permute-done.2.refs_0_, ...), custom_call_target="tpu_custom_call" | custom-call | flops 603979776 | bytes 3932160 | tf_op jit(solution)/shard_map/forward/pallas_call | solution.py:409
  26.9 4.5 %collective-permute-done.1.refs_0_ = bf16[2,256,128]{2,1,0:T(8,128)(2,1)S(1)} collective-permute-done((bf16[2,256,128]{2,1,0:T(8,128)(2,1)S(1)}, bf16[2,256,128]{2,1,0:T(8,128)(2,1)S(1)}, u32[]{:S(2)}, u32[]{:S(2)}) %collective-permute-start.1) | collective-permute-done | bytes 131104 | tf_op jit(solution)/shard_map/ppermute | solution.py:475
  31.4 1.0 %forward.5 = (f32[2,8,1536]{2,1,0:T(8,128)S(1)}, f32[2,128,1536]{2,1,0:T(8,128)S(1)}, bf16[2,128,1536]{2,1,0:T(8,128)(2,1)S(1)}, bf16[2,128,128]{2,1,0:T(8,128)(2,1)S(1)}, bf16[2,128,128]{2,1,0:T(8,128)(2,1)S(1)}) custom-call(bf16[2,256,128]{2,1,0:T(8,128)(2,1)S(1)} %collective-permute-done.1.refs_0_, bf16[2,128,1536]{2,1,0:T(8,128)(2,1)S(1)} %turned.2.refs_3_.refs_1_, ...), custom_call_target="tpu_custom_call" | custom-call | flops 201326592 | bytes 3407872 | tf_op jit(solution)/shard_map/forward/pallas_call | solution.py:409
  32.4 1.3 %collective-permute-done.refs_0_ = bf16[2,256,128]{2,1,0:T(8,128)(2,1)S(1)} collective-permute-done((bf16[2,256,128]{2,1,0:T(8,128)(2,1)S(1)}, bf16[2,256,128]{2,1,0:T(8,128)(2,1)S(1)}, u32[]{:S(2)}, u32[]{:S(2)}) %collective-permute-start) | collective-permute-done | bytes 131104 | tf_op jit(solution)/shard_map/ppermute | solution.py:475
  33.7 2.3 %turn.1 = (f32[2,8,1536]{2,1,0:T(8,128)S(1)}, f32[2,128,1536]{2,1,0:T(8,128)S(1)}, f32[2,128,1536]{2,1,0:T(8,128)S(1)}, bf16[2,256,128]{2,1,0:T(8,128)(2,1)S(1)}) custom-call(bf16[2,256,128]{2,1,0:T(8,128)(2,1)S(1)} %collective-permute-done.refs_0_, bf16[1,1536,256]{2,1,0:T(8,128)(2,1)S(1)} %copy-done, bf16[1,1536,256]{2,1,0:T(8,128)(2,1)S(1)} %copy-done.1, ...), custom_call_target="tpu_custom_call" | custom-call | flops 603979776 | bytes 3407872 | tf_op jit(solution)/shard_map/turn/pallas_call | solution.py:423
  36.0 0.2 collective-permute-start.8
  36.3 3.4 %backward.2 = (f32[2,128,1536]{2,1,0:T(8,128)S(1)}, bf16[2,256,128]{2,1,0:T(8,128)(2,1)S(1)}, bf16[2,256,128]{2,1,0:T(8,128)(2,1)S(1)}, bf16[2,256,128]{2,1,0:T(8,128)(2,1)S(1)}, bf16[2,256,128]{2,1,0:T(8,128)(2,1)S(1)}) custom-call(bf16[2,128,1536]{2,1,0:T(8,128)(2,1)S(1)} %get-tuple-element.64.refs_0_, ...), custom_call_target="tpu_custom_call" | custom-call | flops 1610612736 | bytes 4194304 | tf_op jit(solution)/shard_map/backward/pallas_call | solution.py:444
  39.7 3.5 %collective-permute-start.9 = (bf16[2,256,128]{2,1,0:T(8,128)(2,1)S(1)}, bf16[2,256,128]{2,1,0:T(8,128)(2,1)S(1)}, u32[]{:S(2)}, u32[]{:S(2)}) collective-permute-start(bf16[2,256,128]{2,1,0:T(8,128)(2,1)S(1)} %get-tuple-element.73), channel_id=1, source_target_pairs={{13,0},{12,1},{15,2},{14,3},{9,4},{8,5},{11,6},{10,7},{21,8},{20,9... | collective-permute-start | bytes 393224 | tf_op jit(solution)/shard_map/ppermute | solution.py:483
  43.2 0.0 collective-permute-start.10
  43.2 0.3 collective-permute-start.11
  43.4 3.8 %collective-permute-start.12 = (bf16[2,256,128]{2,1,0:T(8,128)(2,1)S(1)}, bf16[2,256,128]{2,1,0:T(8,128)(2,1)S(1)}, u32[]{:S(2)}, u32[]{:S(2)}) collective-permute-start(bf16[2,256,128]{2,1,0:T(8,128)(2,1)S(1)} %get-tuple-element.76), channel_id=1, source_target_pairs={{8,0},{9,1},{10,2},{11,3},{12,4},{13,5},{14,6},{15,7},{18,8},{19,9... | collective-permute-start | bytes 393224 | tf_op jit(solution)/shard_map/ppermute | solution.py:483
  47.2 0.0 collective-permute-done.8.refs_0_
  47.2 2.7 %backward.3 = (f32[2,128,1536]{2,1,0:T(8,128)S(1)}, bf16[2,256,128]{2,1,0:T(8,128)(2,1)S(1)}, bf16[2,256,128]{2,1,0:T(8,128)(2,1)S(1)}, bf16[2,256,128]{2,1,0:T(8,128)(2,1)S(1)}) custom-call(bf16[2,256,128]{2,1,0:T(8,128)(2,1)S(1)} %collective-permute-done.8.refs_0_, bf16[2,384,1536]{2,1,0:T(8,128)(2,1)S(1)} %get-tuple-element.60.refs_1_, ...), custom_call_target="tpu_custom_call" | custom-call | flops 1207959552 | bytes 3932160 | tf_op jit(solution)/shard_map/backward/pallas_call | solution.py:444
  49.9 0.1 collective-permute-start.13
  50.0 3.1 %collective-permute-done.9.refs_1_ = bf16[2,256,128]{2,1,0:T(8,128)(2,1)S(1)} collective-permute-done((bf16[2,256,128]{2,1,0:T(8,128)(2,1)S(1)}, bf16[2,256,128]{2,1,0:T(8,128)(2,1)S(1)}, u32[]{:S(2)}, u32[]{:S(2)}) %collective-permute-start.9) | collective-permute-done | bytes 131104 | tf_op jit(solution)/shard_map/ppermute | solution.py:483
  53.1 1.6 %collective-permute-start.14 = (bf16[2,256,128]{2,1,0:T(8,128)(2,1)S(1)}, bf16[2,256,128]{2,1,0:T(8,128)(2,1)S(1)}, u32[]{:S(2)}, u32[]{:S(2)}) collective-permute-start(bf16[2,256,128]{2,1,0:T(8,128)(2,1)S(1)} %get-tuple-element.83), channel_id=1, source_target_pairs={{11,0},{10,1},{13,2},{12,3},{15,4},{14,5},{9,6},{8,7},{17,8},{16,9... | collective-permute-start | bytes 393224 | tf_op jit(solution)/shard_map/ppermute | solution.py:483
  54.7 0.0 collective-permute-done.10.refs_2_
  54.7 0.2 collective-permute-start.15
  54.9 1.2 %turned_back.2 = bf16[1,1536,256]{2,1,0:T(8,128)(2,1)} custom-call(f32[2,128,1536]{2,1,0:T(8,128)S(1)} %get-tuple-element.58.columns_ref), custom_call_target="tpu_custom_call" | custom-call | tf_op jit(solution)/shard_map/turned_back/pallas_call | solution.py:185
  56.0 1.2 %turned_back.3 = bf16[1,1536,256]{2,1,0:T(8,128)(2,1)} custom-call(f32[2,128,1536]{2,1,0:T(8,128)S(1)} %get-tuple-element.72.columns_ref), custom_call_target="tpu_custom_call" | custom-call | tf_op jit(solution)/shard_map/turned_back/pallas_call | solution.py:185
  57.2 0.0 collective-permute-done.11.refs_3_
  57.2 0.0 collective-permute-done.12.refs_4_
  57.2 0.5 reordered.3
  57.7 1.3 %collective-permute-done.13 = bf16[2,256,128]{2,1,0:T(8,128)(2,1)S(1)} collective-permute-done((bf16[2,256,128]{2,1,0:T(8,128)(2,1)S(1)}, bf16[2,256,128]{2,1,0:T(8,128)(2,1)S(1)}, u32[]{:S(2)}, u32[]{:S(2)}) %collective-permute-start.13) | collective-permute-done | bytes 131104 | tf_op jit(solution)/shard_map/ppermute | solution.py:483
  58.9 2.9 %collective-permute-done.14 = bf16[2,256,128]{2,1,0:T(8,128)(2,1)S(1)} collective-permute-done((bf16[2,256,128]{2,1,0:T(8,128)(2,1)S(1)}, bf16[2,256,128]{2,1,0:T(8,128)(2,1)S(1)}, u32[]{:S(2)}, u32[]{:S(2)}) %collective-permute-start.14) | collective-permute-done | bytes 131104 | tf_op jit(solution)/shard_map/ppermute | solution.py:483
  61.8 2.5 %collective-permute-done.15 = bf16[2,256,128]{2,1,0:T(8,128)(2,1)S(1)} collective-permute-done((bf16[2,256,128]{2,1,0:T(8,128)(2,1)S(1)}, bf16[2,256,128]{2,1,0:T(8,128)(2,1)S(1)}, u32[]{:S(2)}, u32[]{:S(2)}) %collective-permute-start.15) | collective-permute-done | bytes 131104 | tf_op jit(solution)/shard_map/ppermute | solution.py:483
  64.4 1.5 %unpack.1 = bf16[1,128,2,2048]{3,2,1,0:T(2,128)(2,1)} custom-call(bf16[2,128,2,128]{3,2,1,0:T(2,128)(2,1)S(1)} %bitcast.19, bf16[2,128,2,128]{3,2,1,0:T(2,128)(2,1)S(1)} %bitcast.20, bf16[2,128,2,128]{3,2,1,0:T(2,128)(2,1)S(1)} %bitcast.21, bf16[2,128,2,128]{3,2,1,0:T(2,128)(2,1)S(1)} %bitcast.22, bf16[2,128,2,128]{3,2,1,0:T(2,128)(2,1)S(1)} %bitcast.23, ...), custom_call_target="tpu_custom_call" | custom-call | tf_op jit(solution)/shard_map/unpack/pallas_call | solution.py:116
Async XLA Ops:
  0.6 17.1 %copy-start = (bf16[1,1536,256]{2,1,0:T(8,128)(2,1)S(1)}, bf16[1,1536,256]{2,1,0:T(8,128)(2,1)}, u32[]{:S(2)}) copy-start(bf16[1,1536,256]{2,1,0:T(8,128)(2,1)} %refs_5_.1) | copy-start | bytes 2359300
  0.6 1.3 %copy-start.2 = (bf16[1,128,2,2048]{3,2,1,0:T(2,128)(2,1)S(1)}, bf16[1,128,2,2048]{3,2,1,0:T(2,128)(2,1)}, u32[]{:S(2)}) copy-start(bf16[1,128,2,2048]{3,2,1,0:T(2,128)(2,1)} %pairs_ref.3) | copy-start | bytes 3145732
  2.4 15.6 %copy-start.1 = (bf16[1,1536,256]{2,1,0:T(8,128)(2,1)S(1)}, bf16[1,1536,256]{2,1,0:T(8,128)(2,1)}, u32[]{:S(2)}) copy-start(bf16[1,1536,256]{2,1,0:T(8,128)(2,1)} %refs_6_.1) | copy-start | bytes 2359300
  2.4 12.4 %collective-permute-start.6 = (bf16[2,256,128]{2,1,0:T(8,128)(2,1)S(1)}, bf16[2,256,128]{2,1,0:T(8,128)(2,1)S(1)}, u32[]{:S(2)}, u32[]{:S(2)}) collective-permute-start(bf16[2,256,128]{2,1,0:T(8,128)(2,1)S(1)} %bitcast.31), channel_id=1, source_target_pairs={{0,11},{1,10},{2,13},{3,12},{4,15},{5,14},{6,9},{7,8},{8,17},{9,16... | collective-permute-start | bytes 393224 | tf_op jit(solution)/shard_map/ppermute | solution.py:475
  5.9 10.6 %collective-permute-start.5 = (bf16[2,256,128]{2,1,0:T(8,128)(2,1)S(1)}, bf16[2,256,128]{2,1,0:T(8,128)(2,1)S(1)}, u32[]{:S(2)}, u32[]{:S(2)}) collective-permute-start(bf16[2,256,128]{2,1,0:T(8,128)(2,1)S(1)} %bitcast.30), channel_id=1, source_target_pairs={{0,15},{1,14},{2,9},{3,8},{4,11},{5,10},{6,13},{7,12},{8,23},{9,22... | collective-permute-start | bytes 393224 | tf_op jit(solution)/shard_map/ppermute | solution.py:475
  9.7 9.3 %collective-permute-start.7 = (bf16[2,256,128]{2,1,0:T(8,128)(2,1)S(1)}, bf16[2,256,128]{2,1,0:T(8,128)(2,1)S(1)}, u32[]{:S(2)}, u32[]{:S(2)}) collective-permute-start(bf16[2,256,128]{2,1,0:T(8,128)(2,1)S(1)} %bitcast.29), channel_id=1, source_target_pairs={{0,9},{1,8},{2,11},{3,10},{4,13},{5,12},{6,15},{7,14},{8,19},{9,18... | collective-permute-start | bytes 393224 | tf_op jit(solution)/shard_map/ppermute | solution.py:475
  11.0 11.5 %collective-permute-start.2 = (bf16[2,256,128]{2,1,0:T(8,128)(2,1)S(1)}, bf16[2,256,128]{2,1,0:T(8,128)(2,1)S(1)}, u32[]{:S(2)}, u32[]{:S(2)}) collective-permute-start(bf16[2,256,128]{2,1,0:T(8,128)(2,1)S(1)} %bitcast.28), channel_id=1, source_target_pairs={{0,14},{1,15},{2,8},{3,9},{4,10},{5,11},{6,12},{7,13},{8,22},{9,23... | collective-permute-start | bytes 393224 | tf_op jit(solution)/shard_map/ppermute | solution.py:475
  14.9 7.6 %collective-permute-start.3 = (bf16[2,256,128]{2,1,0:T(8,128)(2,1)S(1)}, bf16[2,256,128]{2,1,0:T(8,128)(2,1)S(1)}, u32[]{:S(2)}, u32[]{:S(2)}) collective-permute-start(bf16[2,256,128]{2,1,0:T(8,128)(2,1)S(1)} %bitcast.27), channel_id=1, source_target_pairs={{0,10},{1,11},{2,12},{3,13},{4,14},{5,15},{6,8},{7,9},{8,16},{9,17... | collective-permute-start | bytes 393224 | tf_op jit(solution)/shard_map/ppermute | solution.py:475
  14.9 9.5 %collective-permute-start.4 = (bf16[2,256,128]{2,1,0:T(8,128)(2,1)S(1)}, bf16[2,256,128]{2,1,0:T(8,128)(2,1)S(1)}, u32[]{:S(2)}, u32[]{:S(2)}) collective-permute-start(bf16[2,256,128]{2,1,0:T(8,128)(2,1)S(1)} %bitcast.26), channel_id=1, source_target_pairs={{0,8},{1,9},{2,10},{3,11},{4,12},{5,13},{6,14},{7,15},{8,18},{9,19... | collective-permute-start | bytes 393224 | tf_op jit(solution)/shard_map/ppermute | solution.py:475
  16.5 14.9 %collective-permute-start.1 = (bf16[2,256,128]{2,1,0:T(8,128)(2,1)S(1)}, bf16[2,256,128]{2,1,0:T(8,128)(2,1)S(1)}, u32[]{:S(2)}, u32[]{:S(2)}) collective-permute-start(bf16[2,256,128]{2,1,0:T(8,128)(2,1)S(1)} %bitcast.25), channel_id=1, source_target_pairs={{0,13},{1,12},{2,15},{3,14},{4,9},{5,8},{6,11},{7,10},{8,21},{9,20... | collective-permute-start | bytes 393224 | tf_op jit(solution)/shard_map/ppermute | solution.py:475
  18.9 14.8 %collective-permute-start = (bf16[2,256,128]{2,1,0:T(8,128)(2,1)S(1)}, bf16[2,256,128]{2,1,0:T(8,128)(2,1)S(1)}, u32[]{:S(2)}, u32[]{:S(2)}) collective-permute-start(bf16[2,256,128]{2,1,0:T(8,128)(2,1)S(1)} %reordered.2), channel_id=1, source_target_pairs={{0,12},{1,13},{2,14},{3,15},{4,8},{5,9},{6,10},{7,11},{8,20},{9,21... | collective-permute-start | bytes 393224 | tf_op jit(solution)/shard_map/ppermute | solution.py:475
  36.0 11.2 %collective-permute-start.8 = (bf16[2,256,128]{2,1,0:T(8,128)(2,1)S(1)}, bf16[2,256,128]{2,1,0:T(8,128)(2,1)S(1)}, u32[]{:S(2)}, u32[]{:S(2)}) collective-permute-start(bf16[2,256,128]{2,1,0:T(8,128)(2,1)S(1)} %get-tuple-element.59), channel_id=1, source_target_pairs={{12,0},{13,1},{14,2},{15,3},{8,4},{9,5},{10,6},{11,7},{20,8},{21,9... | collective-permute-start | bytes 393224 | tf_op jit(solution)/shard_map/ppermute | solution.py:483
  39.7 13.4 %collective-permute-start.9 = (bf16[2,256,128]{2,1,0:T(8,128)(2,1)S(1)}, bf16[2,256,128]{2,1,0:T(8,128)(2,1)S(1)}, u32[]{:S(2)}, u32[]{:S(2)}) collective-permute-start(bf16[2,256,128]{2,1,0:T(8,128)(2,1)S(1)} %get-tuple-element.73), channel_id=1, source_target_pairs={{13,0},{12,1},{15,2},{14,3},{9,4},{8,5},{11,6},{10,7},{21,8},{20,9... | collective-permute-start | bytes 393224 | tf_op jit(solution)/shard_map/ppermute | solution.py:483
  43.2 11.5 %collective-permute-start.10 = (bf16[2,256,128]{2,1,0:T(8,128)(2,1)S(1)}, bf16[2,256,128]{2,1,0:T(8,128)(2,1)S(1)}, u32[]{:S(2)}, u32[]{:S(2)}) collective-permute-start(bf16[2,256,128]{2,1,0:T(8,128)(2,1)S(1)} %get-tuple-element.74), channel_id=1, source_target_pairs={{14,0},{15,1},{8,2},{9,3},{10,4},{11,5},{12,6},{13,7},{22,8},{23,9... | collective-permute-start | bytes 393224 | tf_op jit(solution)/shard_map/ppermute | solution.py:483
  43.2 14.0 %collective-permute-start.11 = (bf16[2,256,128]{2,1,0:T(8,128)(2,1)S(1)}, bf16[2,256,128]{2,1,0:T(8,128)(2,1)S(1)}, u32[]{:S(2)}, u32[]{:S(2)}) collective-permute-start(bf16[2,256,128]{2,1,0:T(8,128)(2,1)S(1)} %get-tuple-element.75), channel_id=1, source_target_pairs={{10,0},{11,1},{12,2},{13,3},{14,4},{15,5},{8,6},{9,7},{16,8},{17,9... | collective-permute-start | bytes 393224 | tf_op jit(solution)/shard_map/ppermute | solution.py:483
  43.4 13.7 %collective-permute-start.12 = (bf16[2,256,128]{2,1,0:T(8,128)(2,1)S(1)}, bf16[2,256,128]{2,1,0:T(8,128)(2,1)S(1)}, u32[]{:S(2)}, u32[]{:S(2)}) collective-permute-start(bf16[2,256,128]{2,1,0:T(8,128)(2,1)S(1)} %get-tuple-element.76), channel_id=1, source_target_pairs={{8,0},{9,1},{10,2},{11,3},{12,4},{13,5},{14,6},{15,7},{18,8},{19,9... | collective-permute-start | bytes 393224 | tf_op jit(solution)/shard_map/ppermute | solution.py:483
  49.9 9.0 %collective-permute-start.13 = (bf16[2,256,128]{2,1,0:T(8,128)(2,1)S(1)}, bf16[2,256,128]{2,1,0:T(8,128)(2,1)S(1)}, u32[]{:S(2)}, u32[]{:S(2)}) collective-permute-start(bf16[2,256,128]{2,1,0:T(8,128)(2,1)S(1)} %get-tuple-element.82), channel_id=1, source_target_pairs={{15,0},{14,1},{9,2},{8,3},{11,4},{10,5},{13,6},{12,7},{23,8},{22,9... | collective-permute-start | bytes 393224 | tf_op jit(solution)/shard_map/ppermute | solution.py:483
  53.1 8.8 %collective-permute-start.14 = (bf16[2,256,128]{2,1,0:T(8,128)(2,1)S(1)}, bf16[2,256,128]{2,1,0:T(8,128)(2,1)S(1)}, u32[]{:S(2)}, u32[]{:S(2)}) collective-permute-start(bf16[2,256,128]{2,1,0:T(8,128)(2,1)S(1)} %get-tuple-element.83), channel_id=1, source_target_pairs={{11,0},{10,1},{13,2},{12,3},{15,4},{14,5},{9,6},{8,7},{17,8},{16,9... | collective-permute-start | bytes 393224 | tf_op jit(solution)/shard_map/ppermute | solution.py:483
  54.7 9.7 %collective-permute-start.15 = (bf16[2,256,128]{2,1,0:T(8,128)(2,1)S(1)}, bf16[2,256,128]{2,1,0:T(8,128)(2,1)S(1)}, u32[]{:S(2)}, u32[]{:S(2)}) collective-permute-start(bf16[2,256,128]{2,1,0:T(8,128)(2,1)S(1)} %get-tuple-element.84), channel_id=1, source_target_pairs={{9,0},{8,1},{11,2},{10,3},{13,4},{12,5},{15,6},{14,7},{19,8},{18,9... | collective-permute-start | bytes 393224 | tf_op jit(solution)/shard_map/ppermute | solution.py:483

commit v22 on v19

--- a/solution.py
+++ b/solution.py
@@ -479,7 +479,7 @@
     homes, returned = [], []
 
     def send_back(i, grads):
-        sent = sorted(zip(offsets[i], grads), key=lambda s: (s[0][0] > 0) == (i == 1))
+        sent = sorted(zip(offsets[i], grads), key=lambda s: s[0][0] > 0)
         back = [lax.ppermute(g, AXES, route(o, True)) for o, g in sent]
         homes.extend(o for o, _ in sent)
         returned.append(back)

time: 64 us -> 62 us (0.969); the launches traced: 63.9 us -> 61.1 us
  waiting for transfers between devices: 11.1 us -> 8.12 us
    ppermute x8, waiting for transfers between devices: 5.33 us -> 2.31 us  [send_back(): back = [lax.ppermute(g, AXES, route(o, True)) for o, g in sent]]
  transfers between devices with their start and end apart: 16 -> 16, of which waited for: 6 -> 5; matrix products, arithmetic and copies ran while one was open for 0% -> 0% of each run, Pallas kernels for 26% -> 27%
where the time goes in v22:
time: 62 us; the launch traced here: 61.1 us
  starting transfers between devices  30.1 us (49%)
  Pallas kernels  20.6 us (33%)
  waiting for transfers between devices  8.12 us (13%)
  local copies, waits for them, and re-layouts  1.3 us (2%)
  between operations  0.97 us (2%)
    ppermute x8, starting transfers between devices, shards(): blocks.append(lax.ppermute(block, AXES, route(offset, False)))  17.2 us
    ppermute x8, starting transfers between devices, send_back(): back = [lax.ppermute(g, AXES, route(o, True)) for o, g in sent]  13 us
    pallas_call x2, Pallas kernels, attend(): pl.pallas_call(functools.partial(backward_kernel, len(back), counts, not...  6.06 us
    pallas_call x3, Pallas kernels, attend(): pl.pallas_call(functools.partial(forward_kernel, count, not state, tile_o...  6.03 us
    ppermute x8, waiting for transfers between devices, shards(): blocks.append(lax.ppermute(block, AXES, route(offset, False)))  5.81 us
    ppermute x8, waiting for transfers between devices, send_back(): back = [lax.ppermute(g, AXES, route(o, True)) for o, g in sent]  2.31 us
    pallas_call x2, Pallas kernels, turned_back(): pl.pallas_call(kernel, out_shape=jax.ShapeDtypeStruct((1, tokens, heads *...  2.3 us
    pallas_call x1, Pallas kernels, attend(): pl.pallas_call(functools.partial(turn_kernel, count, tile_of(count * rows...  2.29 us
  transfers between devices with their start and end apart: 16, of which 5 were waited for; matrix products, arithmetic and copies ran while one was open for 0% of the time, Pallas kernels for 27%

profile of v22, /device:TPU:0, one launch (start us, length us, event | category | flops | bytes accessed | tf_op | source)
XLA Modules:
  0.0 61.1 jit_solution(7455468691957332183)
XLA Ops:
  0.6 0.0 copy-start
  0.6 0.0 copy-start.2
  0.6 1.3 %copy-done.2 = bf16[1,128,2,2048]{3,2,1,0:T(2,128)(2,1)S(1)} copy-done((bf16[1,128,2,2048]{3,2,1,0:T(2,128)(2,1)S(1)}, bf16[1,128,2,2048]{3,2,1,0:T(2,128)(2,1)}, u32[]{:S(2)}) %copy-start.2) | copy-done | bytes 1048600
  1.9 0.4 pack.3
  2.4 0.0 copy-start.1
  2.4 3.5 %collective-permute-start.6 = (bf16[2,256,128]{2,1,0:T(8,128)(2,1)S(1)}, bf16[2,256,128]{2,1,0:T(8,128)(2,1)S(1)}, u32[]{:S(2)}, u32[]{:S(2)}) collective-permute-start(bf16[2,256,128]{2,1,0:T(8,128)(2,1)S(1)} %bitcast.31), channel_id=1, source_target_pairs={{0,11},{1,10},{2,13},{3,12},{4,15},{5,14},{6,9},{7,8},{8,19},{9,18... | collective-permute-start | bytes 393224 | tf_op jit(solution)/shard_map/ppermute | solution.py:474
  5.9 3.4 %collective-permute-start.5 = (bf16[2,256,128]{2,1,0:T(8,128)(2,1)S(1)}, bf16[2,256,128]{2,1,0:T(8,128)(2,1)S(1)}, u32[]{:S(2)}, u32[]{:S(2)}) collective-permute-start(bf16[2,256,128]{2,1,0:T(8,128)(2,1)S(1)} %bitcast.30), channel_id=1, source_target_pairs={{0,15},{1,14},{2,9},{3,8},{4,11},{5,10},{6,13},{7,12},{8,23},{9,22... | collective-permute-start | bytes 393224 | tf_op jit(solution)/shard_map/ppermute | solution.py:474
  9.3 1.0 %collective-permute-start.7 = (bf16[2,256,128]{2,1,0:T(8,128)(2,1)S(1)}, bf16[2,256,128]{2,1,0:T(8,128)(2,1)S(1)}, u32[]{:S(2)}, u32[]{:S(2)}) collective-permute-start(bf16[2,256,128]{2,1,0:T(8,128)(2,1)S(1)} %bitcast.29), channel_id=1, source_target_pairs={{0,9},{1,8},{2,11},{3,10},{4,13},{5,12},{6,15},{7,14},{8,17},{9,16... | collective-permute-start | bytes 393224 | tf_op jit(solution)/shard_map/ppermute | solution.py:474
  10.2 0.7 %pack.2 = (bf16[2,128,2,128]{3,2,1,0:T(2,128)(2,1)S(1)}, bf16[2,128,2,128]{3,2,1,0:T(2,128)(2,1)S(1)}, bf16[2,128,2,128]{3,2,1,0:T(2,128)(2,1)S(1)}, bf16[2,128,...) custom-call(bf16[1,128,2,2048]{3,2,1,0:T(2,128)(2,1)S(1)} %copy-done.2), custom_call_target="tpu_custom_call" | custom-call | tf_op jit(solution)/shard_map/pack/pallas_call | solution.py:79
  10.9 0.1 collective-permute-start.2
  11.0 3.5 %collective-permute-start.3 = (bf16[2,256,128]{2,1,0:T(8,128)(2,1)S(1)}, bf16[2,256,128]{2,1,0:T(8,128)(2,1)S(1)}, u32[]{:S(2)}, u32[]{:S(2)}) collective-permute-start(bf16[2,256,128]{2,1,0:T(8,128)(2,1)S(1)} %bitcast.27), channel_id=1, source_target_pairs={{0,14},{1,15},{2,8},{3,9},{4,10},{5,11},{6,12},{7,13},{8,22},{9,23... | collective-permute-start | bytes 393224 | tf_op jit(solution)/shard_map/ppermute | solution.py:474
  14.5 0.0 collective-permute-done.6.refs_1_
  14.5 1.6 %collective-permute-start.4 = (bf16[2,256,128]{2,1,0:T(8,128)(2,1)S(1)}, bf16[2,256,128]{2,1,0:T(8,128)(2,1)S(1)}, u32[]{:S(2)}, u32[]{:S(2)}) collective-permute-start(bf16[2,256,128]{2,1,0:T(8,128)(2,1)S(1)} %bitcast.26), channel_id=1, source_target_pairs={{0,8},{1,9},{2,10},{3,11},{4,12},{5,13},{6,14},{7,15},{8,16},{9,17... | collective-permute-start | bytes 393224 | tf_op jit(solution)/shard_map/ppermute | solution.py:474
  16.1 0.3 collective-permute-done.5.refs_0_
  16.4 0.6 collective-permute-start.1
  17.0 0.2 reordered.2
  17.2 0.0 copy-done
  17.2 0.3 turned.2.refs_3_.refs_1_
  17.5 0.0 copy-done.1
  17.5 0.3 turned.3.refs_4_.refs_10_.refs_7_
  17.8 0.0 collective-permute-done.7.refs_2_
  17.8 3.6 %collective-permute-start = (bf16[2,256,128]{2,1,0:T(8,128)(2,1)S(1)}, bf16[2,256,128]{2,1,0:T(8,128)(2,1)S(1)}, u32[]{:S(2)}, u32[]{:S(2)}) collective-permute-start(bf16[2,256,128]{2,1,0:T(8,128)(2,1)S(1)} %reordered.2), channel_id=1, source_target_pairs={{0,12},{1,13},{2,14},{3,15},{4,8},{5,9},{6,10},{7,11},{8,20},{9,21... | collective-permute-start | bytes 393224 | tf_op jit(solution)/shard_map/ppermute | solution.py:474
  21.4 2.5 %forward.3 = (f32[2,8,1536]{2,1,0:T(8,128)S(1)}, f32[2,128,1536]{2,1,0:T(8,128)S(1)}, bf16[2,384,1536]{2,1,0:T(8,128)(2,1)S(1)}, bf16[2,384,128]{2,1,0:T(8,128)(2,1)S(1)}, bf16[2,128,384]{2,1,0:T(8,128)(2,1)S(1)}) custom-call(bf16[2,256,128]{2,1,0:T(8,128)(2,1)S(1)} %collective-permute-done.5.refs_0_, ...), custom_call_target="tpu_custom_call" | custom-call | flops 603979776 | bytes 3932160 | tf_op jit(solution)/shard_map/forward/pallas_call | solution.py:408
  23.9 0.0 collective-permute-done.2.refs_0_
  23.9 0.0 collective-permute-done.3.refs_1_
  23.9 0.0 collective-permute-done.4.refs_2_
  23.9 2.5 %forward.4 = (f32[2,8,1536]{2,1,0:T(8,128)S(1)}, f32[2,128,1536]{2,1,0:T(8,128)S(1)}, bf16[2,384,1536]{2,1,0:T(8,128)(2,1)S(1)}, bf16[2,384,128]{2,1,0:T(8,128)(2,1)S(1)}, bf16[2,128,384]{2,1,0:T(8,128)(2,1)S(1)}) custom-call(bf16[2,256,128]{2,1,0:T(8,128)(2,1)S(1)} %collective-permute-done.2.refs_0_, ...), custom_call_target="tpu_custom_call" | custom-call | flops 603979776 | bytes 3932160 | tf_op jit(solution)/shard_map/forward/pallas_call | solution.py:408
  26.4 4.0 %collective-permute-done.1.refs_0_ = bf16[2,256,128]{2,1,0:T(8,128)(2,1)S(1)} collective-permute-done((bf16[2,256,128]{2,1,0:T(8,128)(2,1)S(1)}, bf16[2,256,128]{2,1,0:T(8,128)(2,1)S(1)}, u32[]{:S(2)}, u32[]{:S(2)}) %collective-permute-start.1) | collective-permute-done | bytes 131104 | tf_op jit(solution)/shard_map/ppermute | solution.py:474
  30.4 1.0 %forward.5 = (f32[2,8,1536]{2,1,0:T(8,128)S(1)}, f32[2,128,1536]{2,1,0:T(8,128)S(1)}, bf16[2,128,1536]{2,1,0:T(8,128)(2,1)S(1)}, bf16[2,128,128]{2,1,0:T(8,128)(2,1)S(1)}, bf16[2,128,128]{2,1,0:T(8,128)(2,1)S(1)}) custom-call(bf16[2,256,128]{2,1,0:T(8,128)(2,1)S(1)} %collective-permute-done.1.refs_0_, bf16[2,128,1536]{2,1,0:T(8,128)(2,1)S(1)} %turned.2.refs_3_.refs_1_, ...), custom_call_target="tpu_custom_call" | custom-call | flops 201326592 | bytes 3407872 | tf_op jit(solution)/shard_map/forward/pallas_call | solution.py:408
  31.5 1.5 %collective-permute-done.refs_0_ = bf16[2,256,128]{2,1,0:T(8,128)(2,1)S(1)} collective-permute-done((bf16[2,256,128]{2,1,0:T(8,128)(2,1)S(1)}, bf16[2,256,128]{2,1,0:T(8,128)(2,1)S(1)}, u32[]{:S(2)}, u32[]{:S(2)}) %collective-permute-start) | collective-permute-done | bytes 131104 | tf_op jit(solution)/shard_map/ppermute | solution.py:474
  32.9 2.3 %turn.1 = (f32[2,8,1536]{2,1,0:T(8,128)S(1)}, f32[2,128,1536]{2,1,0:T(8,128)S(1)}, f32[2,128,1536]{2,1,0:T(8,128)S(1)}, bf16[2,256,128]{2,1,0:T(8,128)(2,1)S(1)}) custom-call(bf16[2,256,128]{2,1,0:T(8,128)(2,1)S(1)} %collective-permute-done.refs_0_, bf16[1,1536,256]{2,1,0:T(8,128)(2,1)S(1)} %copy-done, bf16[1,1536,256]{2,1,0:T(8,128)(2,1)S(1)} %copy-done.1, ...), custom_call_target="tpu_custom_call" | custom-call | flops 603979776 | bytes 3407872 | tf_op jit(solution)/shard_map/turn/pallas_call | solution.py:422
  35.2 0.2 collective-permute-start.8
  35.5 3.4 %backward.2 = (f32[2,128,1536]{2,1,0:T(8,128)S(1)}, bf16[2,256,128]{2,1,0:T(8,128)(2,1)S(1)}, bf16[2,256,128]{2,1,0:T(8,128)(2,1)S(1)}, bf16[2,256,128]{2,1,0:T(8,128)(2,1)S(1)}, bf16[2,256,128]{2,1,0:T(8,128)(2,1)S(1)}) custom-call(bf16[2,128,1536]{2,1,0:T(8,128)(2,1)S(1)} %get-tuple-element.64.refs_0_, ...), custom_call_target="tpu_custom_call" | custom-call | flops 1610612736 | bytes 4194304 | tf_op jit(solution)/shard_map/backward/pallas_call | solution.py:443
  38.9 3.1 %collective-permute-start.9 = (bf16[2,256,128]{2,1,0:T(8,128)(2,1)S(1)}, bf16[2,256,128]{2,1,0:T(8,128)(2,1)S(1)}, u32[]{:S(2)}, u32[]{:S(2)}) collective-permute-start(bf16[2,256,128]{2,1,0:T(8,128)(2,1)S(1)} %get-tuple-element.73), channel_id=1, source_target_pairs={{13,0},{12,1},{15,2},{14,3},{9,4},{8,5},{11,6},{10,7},{21,8},{20,9... | collective-permute-start | bytes 393224 | tf_op jit(solution)/shard_map/ppermute | solution.py:483
  42.0 0.0 collective-permute-start.10
  42.0 2.2 %collective-permute-start.11 = (bf16[2,256,128]{2,1,0:T(8,128)(2,1)S(1)}, bf16[2,256,128]{2,1,0:T(8,128)(2,1)S(1)}, u32[]{:S(2)}, u32[]{:S(2)}) collective-permute-start(bf16[2,256,128]{2,1,0:T(8,128)(2,1)S(1)} %get-tuple-element.75), channel_id=1, source_target_pairs={{10,0},{11,1},{12,2},{13,3},{14,4},{15,5},{8,6},{9,7},{18,8},{19,9... | collective-permute-start | bytes 393224 | tf_op jit(solution)/shard_map/ppermute | solution.py:483
  44.2 0.0 collective-permute-start.12
  44.2 0.0 collective-permute-done.8.refs_0_
  44.2 2.7 %backward.3 = (f32[2,128,1536]{2,1,0:T(8,128)S(1)}, bf16[2,256,128]{2,1,0:T(8,128)(2,1)S(1)}, bf16[2,256,128]{2,1,0:T(8,128)(2,1)S(1)}, bf16[2,256,128]{2,1,0:T(8,128)(2,1)S(1)}) custom-call(bf16[2,256,128]{2,1,0:T(8,128)(2,1)S(1)} %collective-permute-done.8.refs_0_, bf16[2,384,1536]{2,1,0:T(8,128)(2,1)S(1)} %get-tuple-element.60.refs_1_, ...), custom_call_target="tpu_custom_call" | custom-call | flops 1207959552 | bytes 3932160 | tf_op jit(solution)/shard_map/backward/pallas_call | solution.py:443
  46.9 1.7 %collective-permute-start.13 = (bf16[2,256,128]{2,1,0:T(8,128)(2,1)S(1)}, bf16[2,256,128]{2,1,0:T(8,128)(2,1)S(1)}, u32[]{:S(2)}, u32[]{:S(2)}) collective-permute-start(bf16[2,256,128]{2,1,0:T(8,128)(2,1)S(1)} %get-tuple-element.82), channel_id=1, source_target_pairs={{9,0},{8,1},{11,2},{10,3},{13,4},{12,5},{15,6},{14,7},{17,8},{16,9... | collective-permute-start | bytes 393224 | tf_op jit(solution)/shard_map/ppermute | solution.py:483
  48.6 0.6 collective-permute-done.9.refs_1_
  49.2 1.4 %collective-permute-start.14 = (bf16[2,256,128]{2,1,0:T(8,128)(2,1)S(1)}, bf16[2,256,128]{2,1,0:T(8,128)(2,1)S(1)}, u32[]{:S(2)}, u32[]{:S(2)}) collective-permute-start(bf16[2,256,128]{2,1,0:T(8,128)(2,1)S(1)} %get-tuple-element.83), channel_id=1, source_target_pairs={{15,0},{14,1},{9,2},{8,3},{11,4},{10,5},{13,6},{12,7},{23,8},{22,9... | collective-permute-start | bytes 393224 | tf_op jit(solution)/shard_map/ppermute | solution.py:483
  50.6 0.0 collective-permute-done.10.refs_2_
  50.6 4.3 %collective-permute-start.15 = (bf16[2,256,128]{2,1,0:T(8,128)(2,1)S(1)}, bf16[2,256,128]{2,1,0:T(8,128)(2,1)S(1)}, u32[]{:S(2)}, u32[]{:S(2)}) collective-permute-start(bf16[2,256,128]{2,1,0:T(8,128)(2,1)S(1)} %get-tuple-element.84), channel_id=1, source_target_pairs={{11,0},{10,1},{13,2},{12,3},{15,4},{14,5},{9,6},{8,7},{19,8},{18,9... | collective-permute-start | bytes 393224 | tf_op jit(solution)/shard_map/ppermute | solution.py:483
  54.9 1.2 %turned_back.2 = bf16[1,1536,256]{2,1,0:T(8,128)(2,1)} custom-call(f32[2,128,1536]{2,1,0:T(8,128)S(1)} %get-tuple-element.58.columns_ref), custom_call_target="tpu_custom_call" | custom-call | tf_op jit(solution)/shard_map/turned_back/pallas_call | solution.py:184
  56.0 1.2 %turned_back.3 = bf16[1,1536,256]{2,1,0:T(8,128)(2,1)} custom-call(f32[2,128,1536]{2,1,0:T(8,128)S(1)} %get-tuple-element.72.columns_ref), custom_call_target="tpu_custom_call" | custom-call | tf_op jit(solution)/shard_map/turned_back/pallas_call | solution.py:184
  57.2 0.0 collective-permute-done.11.refs_3_
  57.2 0.0 collective-permute-done.12.refs_4_
  57.2 0.5 reordered.3
  57.7 0.0 collective-permute-done.13
  57.7 1.7 %collective-permute-done.14 = bf16[2,256,128]{2,1,0:T(8,128)(2,1)S(1)} collective-permute-done((bf16[2,256,128]{2,1,0:T(8,128)(2,1)S(1)}, bf16[2,256,128]{2,1,0:T(8,128)(2,1)S(1)}, u32[]{:S(2)}, u32[]{:S(2)}) %collective-permute-start.14) | collective-permute-done | bytes 131104 | tf_op jit(solution)/shard_map/ppermute | solution.py:483
  59.4 0.0 collective-permute-done.15
  59.4 1.5 %unpack.1 = bf16[1,128,2,2048]{3,2,1,0:T(2,128)(2,1)} custom-call(bf16[2,128,2,128]{3,2,1,0:T(2,128)(2,1)S(1)} %bitcast.19, bf16[2,128,2,128]{3,2,1,0:T(2,128)(2,1)S(1)} %bitcast.20, bf16[2,128,2,128]{3,2,1,0:T(2,128)(2,1)S(1)} %bitcast.21, bf16[2,128,2,128]{3,2,1,0:T(2,128)(2,1)S(1)} %bitcast.22, bf16[2,128,2,128]{3,2,1,0:T(2,128)(2,1)S(1)} %bitcast.23, ...), custom_call_target="tpu_custom_call" | custom-call | tf_op jit(solution)/shard_map/unpack/pallas_call | solution.py:115
Async XLA Ops:
  0.6 16.6 %copy-start = (bf16[1,1536,256]{2,1,0:T(8,128)(2,1)S(1)}, bf16[1,1536,256]{2,1,0:T(8,128)(2,1)}, u32[]{:S(2)}) copy-start(bf16[1,1536,256]{2,1,0:T(8,128)(2,1)} %refs_5_.1) | copy-start | bytes 2359300
  0.6 1.3 %copy-start.2 = (bf16[1,128,2,2048]{3,2,1,0:T(2,128)(2,1)S(1)}, bf16[1,128,2,2048]{3,2,1,0:T(2,128)(2,1)}, u32[]{:S(2)}) copy-start(bf16[1,128,2,2048]{3,2,1,0:T(2,128)(2,1)} %pairs_ref.3) | copy-start | bytes 3145732
  2.4 15.1 %copy-start.1 = (bf16[1,1536,256]{2,1,0:T(8,128)(2,1)S(1)}, bf16[1,1536,256]{2,1,0:T(8,128)(2,1)}, u32[]{:S(2)}) copy-start(bf16[1,1536,256]{2,1,0:T(8,128)(2,1)} %refs_6_.1) | copy-start | bytes 2359300
  2.4 12.1 %collective-permute-start.6 = (bf16[2,256,128]{2,1,0:T(8,128)(2,1)S(1)}, bf16[2,256,128]{2,1,0:T(8,128)(2,1)S(1)}, u32[]{:S(2)}, u32[]{:S(2)}) collective-permute-start(bf16[2,256,128]{2,1,0:T(8,128)(2,1)S(1)} %bitcast.31), channel_id=1, source_target_pairs={{0,11},{1,10},{2,13},{3,12},{4,15},{5,14},{6,9},{7,8},{8,19},{9,18... | collective-permute-start | bytes 393224 | tf_op jit(solution)/shard_map/ppermute | solution.py:474
  5.9 10.5 %collective-permute-start.5 = (bf16[2,256,128]{2,1,0:T(8,128)(2,1)S(1)}, bf16[2,256,128]{2,1,0:T(8,128)(2,1)S(1)}, u32[]{:S(2)}, u32[]{:S(2)}) collective-permute-start(bf16[2,256,128]{2,1,0:T(8,128)(2,1)S(1)} %bitcast.30), channel_id=1, source_target_pairs={{0,15},{1,14},{2,9},{3,8},{4,11},{5,10},{6,13},{7,12},{8,23},{9,22... | collective-permute-start | bytes 393224 | tf_op jit(solution)/shard_map/ppermute | solution.py:474
  9.3 8.5 %collective-permute-start.7 = (bf16[2,256,128]{2,1,0:T(8,128)(2,1)S(1)}, bf16[2,256,128]{2,1,0:T(8,128)(2,1)S(1)}, u32[]{:S(2)}, u32[]{:S(2)}) collective-permute-start(bf16[2,256,128]{2,1,0:T(8,128)(2,1)S(1)} %bitcast.29), channel_id=1, source_target_pairs={{0,9},{1,8},{2,11},{3,10},{4,13},{5,12},{6,15},{7,14},{8,17},{9,16... | collective-permute-start | bytes 393224 | tf_op jit(solution)/shard_map/ppermute | solution.py:474
  10.9 13.0 %collective-permute-start.2 = (bf16[2,256,128]{2,1,0:T(8,128)(2,1)S(1)}, bf16[2,256,128]{2,1,0:T(8,128)(2,1)S(1)}, u32[]{:S(2)}, u32[]{:S(2)}) collective-permute-start(bf16[2,256,128]{2,1,0:T(8,128)(2,1)S(1)} %bitcast.28), channel_id=1, source_target_pairs={{0,10},{1,11},{2,12},{3,13},{4,14},{5,15},{6,8},{7,9},{8,18},{9,19... | collective-permute-start | bytes 393224 | tf_op jit(solution)/shard_map/ppermute | solution.py:474
  11.0 12.9 %collective-permute-start.3 = (bf16[2,256,128]{2,1,0:T(8,128)(2,1)S(1)}, bf16[2,256,128]{2,1,0:T(8,128)(2,1)S(1)}, u32[]{:S(2)}, u32[]{:S(2)}) collective-permute-start(bf16[2,256,128]{2,1,0:T(8,128)(2,1)S(1)} %bitcast.27), channel_id=1, source_target_pairs={{0,14},{1,15},{2,8},{3,9},{4,10},{5,11},{6,12},{7,13},{8,22},{9,23... | collective-permute-start | bytes 393224 | tf_op jit(solution)/shard_map/ppermute | solution.py:474
  14.5 9.4 %collective-permute-start.4 = (bf16[2,256,128]{2,1,0:T(8,128)(2,1)S(1)}, bf16[2,256,128]{2,1,0:T(8,128)(2,1)S(1)}, u32[]{:S(2)}, u32[]{:S(2)}) collective-permute-start(bf16[2,256,128]{2,1,0:T(8,128)(2,1)S(1)} %bitcast.26), channel_id=1, source_target_pairs={{0,8},{1,9},{2,10},{3,11},{4,12},{5,13},{6,14},{7,15},{8,16},{9,17... | collective-permute-start | bytes 393224 | tf_op jit(solution)/shard_map/ppermute | solution.py:474
  16.4 14.0 %collective-permute-start.1 = (bf16[2,256,128]{2,1,0:T(8,128)(2,1)S(1)}, bf16[2,256,128]{2,1,0:T(8,128)(2,1)S(1)}, u32[]{:S(2)}, u32[]{:S(2)}) collective-permute-start(bf16[2,256,128]{2,1,0:T(8,128)(2,1)S(1)} %bitcast.25), channel_id=1, source_target_pairs={{0,13},{1,12},{2,15},{3,14},{4,9},{5,8},{6,11},{7,10},{8,21},{9,20... | collective-permute-start | bytes 393224 | tf_op jit(solution)/shard_map/ppermute | solution.py:474
  17.8 15.2 %collective-permute-start = (bf16[2,256,128]{2,1,0:T(8,128)(2,1)S(1)}, bf16[2,256,128]{2,1,0:T(8,128)(2,1)S(1)}, u32[]{:S(2)}, u32[]{:S(2)}) collective-permute-start(bf16[2,256,128]{2,1,0:T(8,128)(2,1)S(1)} %reordered.2), channel_id=1, source_target_pairs={{0,12},{1,13},{2,14},{3,15},{4,8},{5,9},{6,10},{7,11},{8,20},{9,21... | collective-permute-start | bytes 393224 | tf_op jit(solution)/shard_map/ppermute | solution.py:474
  35.2 9.0 %collective-permute-start.8 = (bf16[2,256,128]{2,1,0:T(8,128)(2,1)S(1)}, bf16[2,256,128]{2,1,0:T(8,128)(2,1)S(1)}, u32[]{:S(2)}, u32[]{:S(2)}) collective-permute-start(bf16[2,256,128]{2,1,0:T(8,128)(2,1)S(1)} %get-tuple-element.59), channel_id=1, source_target_pairs={{12,0},{13,1},{14,2},{15,3},{8,4},{9,5},{10,6},{11,7},{20,8},{21,9... | collective-permute-start | bytes 393224 | tf_op jit(solution)/shard_map/ppermute | solution.py:483
  38.9 10.3 %collective-permute-start.9 = (bf16[2,256,128]{2,1,0:T(8,128)(2,1)S(1)}, bf16[2,256,128]{2,1,0:T(8,128)(2,1)S(1)}, u32[]{:S(2)}, u32[]{:S(2)}) collective-permute-start(bf16[2,256,128]{2,1,0:T(8,128)(2,1)S(1)} %get-tuple-element.73), channel_id=1, source_target_pairs={{13,0},{12,1},{15,2},{14,3},{9,4},{8,5},{11,6},{10,7},{21,8},{20,9... | collective-permute-start | bytes 393224 | tf_op jit(solution)/shard_map/ppermute | solution.py:483
  42.0 8.6 %collective-permute-start.10 = (bf16[2,256,128]{2,1,0:T(8,128)(2,1)S(1)}, bf16[2,256,128]{2,1,0:T(8,128)(2,1)S(1)}, u32[]{:S(2)}, u32[]{:S(2)}) collective-permute-start(bf16[2,256,128]{2,1,0:T(8,128)(2,1)S(1)} %get-tuple-element.74), channel_id=1, source_target_pairs={{8,0},{9,1},{10,2},{11,3},{12,4},{13,5},{14,6},{15,7},{16,8},{17,9... | collective-permute-start | bytes 393224 | tf_op jit(solution)/shard_map/ppermute | solution.py:483
  42.0 15.2 %collective-permute-start.11 = (bf16[2,256,128]{2,1,0:T(8,128)(2,1)S(1)}, bf16[2,256,128]{2,1,0:T(8,128)(2,1)S(1)}, u32[]{:S(2)}, u32[]{:S(2)}) collective-permute-start(bf16[2,256,128]{2,1,0:T(8,128)(2,1)S(1)} %get-tuple-element.75), channel_id=1, source_target_pairs={{10,0},{11,1},{12,2},{13,3},{14,4},{15,5},{8,6},{9,7},{18,8},{19,9... | collective-permute-start | bytes 393224 | tf_op jit(solution)/shard_map/ppermute | solution.py:483
  44.2 13.0 %collective-permute-start.12 = (bf16[2,256,128]{2,1,0:T(8,128)(2,1)S(1)}, bf16[2,256,128]{2,1,0:T(8,128)(2,1)S(1)}, u32[]{:S(2)}, u32[]{:S(2)}) collective-permute-start(bf16[2,256,128]{2,1,0:T(8,128)(2,1)S(1)} %get-tuple-element.76), channel_id=1, source_target_pairs={{14,0},{15,1},{8,2},{9,3},{10,4},{11,5},{12,6},{13,7},{22,8},{23,9... | collective-permute-start | bytes 393224 | tf_op jit(solution)/shard_map/ppermute | solution.py:483
  46.9 10.8 %collective-permute-start.13 = (bf16[2,256,128]{2,1,0:T(8,128)(2,1)S(1)}, bf16[2,256,128]{2,1,0:T(8,128)(2,1)S(1)}, u32[]{:S(2)}, u32[]{:S(2)}) collective-permute-start(bf16[2,256,128]{2,1,0:T(8,128)(2,1)S(1)} %get-tuple-element.82), channel_id=1, source_target_pairs={{9,0},{8,1},{11,2},{10,3},{13,4},{12,5},{15,6},{14,7},{17,8},{16,9... | collective-permute-start | bytes 393224 | tf_op jit(solution)/shard_map/ppermute | solution.py:483
  49.2 10.2 %collective-permute-start.14 = (bf16[2,256,128]{2,1,0:T(8,128)(2,1)S(1)}, bf16[2,256,128]{2,1,0:T(8,128)(2,1)S(1)}, u32[]{:S(2)}, u32[]{:S(2)}) collective-permute-start(bf16[2,256,128]{2,1,0:T(8,128)(2,1)S(1)} %get-tuple-element.83), channel_id=1, source_target_pairs={{15,0},{14,1},{9,2},{8,3},{11,4},{10,5},{13,6},{12,7},{23,8},{22,9... | collective-permute-start | bytes 393224 | tf_op jit(solution)/shard_map/ppermute | solution.py:483
  50.6 8.8 %collective-permute-start.15 = (bf16[2,256,128]{2,1,0:T(8,128)(2,1)S(1)}, bf16[2,256,128]{2,1,0:T(8,128)(2,1)S(1)}, u32[]{:S(2)}, u32[]{:S(2)}) collective-permute-start(bf16[2,256,128]{2,1,0:T(8,128)(2,1)S(1)} %get-tuple-element.84), channel_id=1, source_target_pairs={{11,0},{10,1},{13,2},{12,3},{15,4},{14,5},{9,6},{8,7},{19,8},{18,9... | collective-permute-start | bytes 393224 | tf_op jit(solution)/shard_map/ppermute | solution.py:483
